TPU v7x, 32 devices: a whole 2x2x4 slice. The times are simulated.
32 devices in a mesh: parts: 2 (over y), gx: 4 (over z), gy: 2 (over x), gz: 2 (over core).
Axes of the slice: x: 2, y: 2, z: 4, core: 2. Of those that a mesh axis runs over, the one named last changes fastest.
Arguments:
- adjoint_rhs: float32 [2, 20, 64, 1024], P(None, None, ('parts', 'gx'), ('gy', 'gz')), parts along dimension 2, may hold values from -40 to 40
- viscosity: float32 [20, 64, 1024], P(None, ('parts', 'gx'), ('gy', 'gz')), parts along dimension 1, may hold values from 0.03 to 0.3
- friction: float32 [64, 1024], P(('parts', 'gx'), ('gy', 'gz')), parts along dimension 0, may hold values from 0.05 to 1
- ice_mask: int32 [64, 1024], P(('parts', 'gx'), ('gy', 'gz')), parts along dimension 0, may hold values 0 or 1
- grounded: int32 [64, 1024], P(('parts', 'gx'), ('gy', 'gz')), parts along dimension 0, may hold values 0 or 1
- basal_velocity: float32 [2, 64, 1024], P(None, ('parts', 'gx'), ('gy', 'gz')), parts along dimension 1, may hold values from -6 to 6
Outputs:
- adjoint_solution: float32 [2, 20, 64, 1024], P(None, None, ('parts', 'gx'), ('gy', 'gz')), parts along dimension 2
- adjoint_residual: float32 [2, 20, 64, 1024], P(None, None, ('parts', 'gx'), ('gy', 'gz')), parts along dimension 2
- hessian_action: float32 [64, 1024], P(('parts', 'gx'), ('gy', 'gz')), parts along dimension 0
There are 2 independent parts, one for each index of `parts`. A program takes and returns all parts, laid end to end along the dimension named above; each array names one. Nothing has to cross between parts.
All inputs are finite; a program needn't handle non-finite values. No bound on the sum of `ice_mask` or of `grounded` on one device may be relied on, other than what follows from the above.
Results may differ from a plain program's by a relative error of at most 0.00015.
Values sent between devices are 32-bit elements; how exact they have to be, the bound alone decides.
No kernel may reach another device: no remote copies, remote signals or barrier semaphores. Data moves between devices by JAX's collectives and lax.ppermute only.
A program may use at most 64 MiB of HBM per device.

v0:
```python
import jax
import jax.numpy as jnp
from jax import lax
from jax.sharding import PartitionSpec as P

ITERS = 2


vertical_weight = 2.0


def padded(cells, sides, width):
    for axis, dim in sides:
        count = lax.axis_size(axis)
        ends = count - 1
        head = lax.slice_in_dim(cells, 0, width, axis=dim)
        tail = lax.slice_in_dim(cells, cells.shape[dim] - width, cells.shape[dim], axis=dim)
        cells = jnp.concatenate(
            [
                lax.ppermute(tail, axis, [(i, (i + 1) % count) for i in range(ends)]),
                cells,
                lax.ppermute(head, axis, [((i + 1) % count, i) for i in range(ends)]),
            ],
            axis=dim,
        )
    return cells


def extend(masked):
    return padded(masked, (("gx", 2), (("gy", "gz"), 3)), 1)


def stencil(extended, eta_rim, viscosity, basal_drag):
    masked = extended[:, :, 1:-1, 1:-1]
    eta_next_row = 0.5 * (viscosity + eta_rim[:, 2:, 1:-1])
    eta_prev_row = 0.5 * (viscosity + eta_rim[:, :-2, 1:-1])
    eta_next_col = 0.5 * (viscosity + eta_rim[:, 1:-1, 2:])
    eta_prev_col = 0.5 * (viscosity + eta_rim[:, 1:-1, :-2])
    across_rows = eta_next_row * (masked - extended[:, :, 2:, 1:-1]) + eta_prev_row * (
        masked - extended[:, :, :-2, 1:-1]
    )
    across_columns = eta_next_col * (masked - extended[:, :, 1:-1, 2:]) + eta_prev_col * (
        masked - extended[:, :, 1:-1, :-2]
    )
    layer_eta = 0.5 * (viscosity[1:] + viscosity[:-1])
    layer_flux = layer_eta * (masked[:, 1:] - masked[:, :-1])
    vertical = jnp.pad(-layer_flux, ((0, 0), (0, 1), (0, 0), (0, 0))) + jnp.pad(
        layer_flux, ((0, 0), (1, 0), (0, 0), (0, 0))
    )
    bed_term = jnp.pad(
        (basal_drag * masked[:, 0])[:, None], ((0, 0), (0, masked.shape[1] - 1), (0, 0), (0, 0))
    )
    cross_first = eta_rim[:, :, 1:-1] * (0.5 * (extended[1, :, :, 2:] - extended[1, :, :, :-2]))
    mixed_first = -(cross_first[:, 2:] - cross_first[:, :-2])
    cross_second = eta_rim[:, 1:-1, :] * (0.5 * (extended[0, :, 2:, :] - extended[0, :, :-2, :]))
    mixed_second = -(cross_second[:, :, 2:] - cross_second[:, :, :-2])
    row_gain = jnp.array([4.0, 1.0], jnp.float32).reshape(2, 1, 1, 1)
    column_gain = jnp.array([1.0, 4.0], jnp.float32).reshape(2, 1, 1, 1)
    return (
        row_gain * across_rows
        + column_gain * across_columns
        + vertical_weight * vertical
        + bed_term
        + jnp.stack([mixed_first, mixed_second])
    )


def body(adjoint_rhs, viscosity, friction, ice_mask, grounded, basal_velocity):
    eta_rim = padded(viscosity, (("gx", 1), (("gy", "gz"), 2)), 1)
    ice_cover = ice_mask.astype(jnp.float32)
    basal_drag = friction * grounded.astype(jnp.float32)

    def apply_op(vector_in):
        extended = extend(vector_in * ice_cover)
        return (
            ice_cover * stencil(extended, eta_rim, viscosity, basal_drag)
            + (1.0 - ice_cover) * vector_in
        )

    quasi = adjoint_rhs
    search = adjoint_rhs
    applied = apply_op(search)
    carried = applied
    update = jnp.zeros_like(adjoint_rhs)
    iterate = jnp.zeros_like(adjoint_rhs)
    rho_now = lax.psum(jnp.sum(adjoint_rhs * adjoint_rhs), ("gx", "gy", "gz"))
    tau_now = jnp.sqrt(rho_now)
    width_sq = rho_now
    theta_now = jnp.zeros((), jnp.float32)
    eta_now = jnp.zeros((), jnp.float32)
    alpha_step = jnp.ones((), jnp.float32)
    search_next = search
    rho_next = rho_now
    for half_step in range(2 * ITERS):
        if half_step % 2 == 0:
            sigma_now = lax.psum(jnp.sum(carried * adjoint_rhs), ("gx", "gy", "gz"))
            alpha_step = rho_now / sigma_now
            quasi = quasi - alpha_step * applied
            width_sq = lax.psum(jnp.sum(quasi * quasi), ("gx", "gy", "gz"))
            search_next = search - alpha_step * carried
        else:
            quasi = quasi - alpha_step * applied
            width_sq, rho_next = lax.psum(
                (jnp.sum(quasi * quasi), jnp.sum(quasi * adjoint_rhs)), ("gx", "gy", "gz")
            )
        update = search + theta_now * theta_now / alpha_step * eta_now * update
        theta_now = jnp.sqrt(width_sq) / tau_now
        cosine = 1.0 / jnp.sqrt(1.0 + theta_now * theta_now)
        tau_now = tau_now * theta_now * cosine
        eta_now = cosine * cosine * alpha_step
        iterate = iterate + eta_now * update
        if half_step % 2 == 0:
            search = search_next
            applied = apply_op(search)
        elif half_step < 2 * ITERS - 1:
            beta_step = rho_next / rho_now
            search_new = quasi + beta_step * search
            applied_new = apply_op(search_new)
            carried = applied_new + beta_step * (applied + beta_step * carried)
            search = search_new
            applied = applied_new
            rho_now = rho_next
    residual_out = adjoint_rhs - apply_op(iterate)
    hessian_out = (
        ice_cover
        * basal_drag
        * (basal_velocity[0] * iterate[0, 0] + basal_velocity[1] * iterate[1, 0])
    )
    return (iterate, residual_out, hessian_out)


def solution(mesh):
    in_specs = (
        P(None, None, ("parts", "gx"), ("gy", "gz")),
        P(None, ("parts", "gx"), ("gy", "gz")),
        P(("parts", "gx"), ("gy", "gz")),
        P(("parts", "gx"), ("gy", "gz")),
        P(("parts", "gx"), ("gy", "gz")),
        P(None, ("parts", "gx"), ("gy", "gz")),
    )
    out_specs = (
        P(None, None, ("parts", "gx"), ("gy", "gz")),
        P(None, None, ("parts", "gx"), ("gy", "gz")),
        P(("parts", "gx"), ("gy", "gz")),
    )
    return jax.shard_map(body, mesh=mesh, in_specs=in_specs, out_specs=out_specs, check_vma=False)
```

profile of v0, /device:TPU:0, one launch (start us, length us, event | category | flops | bytes accessed | tf_op | source)
XLA Modules:
  0.0 250.2 jit_solution(11331215624023212765)
XLA Ops:
  3.7 5.6 %collective-permute-start.3 = (f32[2,20,1,256]{3,2,1,0:T(1,128)S(1)}, f32[2,20,1,256]{3,2,1,0:T(1,128)S(1)}, u32[]{:S(2)}, u32[]{:S(2)}) collective-permute-start(f32[2,20,1,256]{3,2,1,0:T(1,128)S(1)} %get-tuple-element.58), channel_id=1, source_target_pairs={{0,4},{4,8},{8,12},{1,5},{5,9},{9,13},{2,6},{6,10},{10,14},{3,7},{... | collective-permute-start | bytes 122888 | tf_op jit(solution)/shard_map/ppermute | solution.py:20
  10.6 4.5 %collective-permute-start.2 = (f32[20,1,256]{2,1,0:T(1,128)S(1)}, f32[20,1,256]{2,1,0:T(1,128)S(1)}, u32[]{:S(2)}, u32[]{:S(2)}) collective-permute-start(f32[20,1,256]{2,1,0:T(1,128)S(1)} %get-tuple-element.66), channel_id=1, source_target_pairs={{0,4},{4,8},{8,12},{1,5},{5,9},{9,13},{2,6},{6,10},{10,14},{3,7},{... | collective-permute-start | bytes 61448 | tf_op jit(solution)/shard_map/ppermute | solution.py:20
  17.5 3.1 %collective-permute-start.7 = (f32[2,20,10,1]{3,2,1,0:T(8,128)S(1)}, f32[2,20,10,1]{3,2,1,0:T(8,128)S(1)}, u32[]{:S(2)}, u32[]{:S(2)}) collective-permute-start(f32[2,20,10,1]{3,2,1,0:T(8,128)S(1)} %get-tuple-element.46), channel_id=1, source_target_pairs={{0,1},{1,2},{2,3},{4,5},{5,6},{6,7},{8,9},{9,10},{10,11},{12,13},{... | collective-permute-start | bytes 4808 | tf_op jit(solution)/shard_map/ppermute | solution.py:20
  22.4 1.3 collective-permute-start.4
  23.7 6.8 %collective-permute-start.6 = (f32[20,10,1]{2,1,0:T(8,128)S(1)}, f32[20,10,1]{2,1,0:T(8,128)S(1)}, u32[]{:S(2)}, u32[]{:S(2)}) collective-permute-start(f32[20,10,1]{2,1,0:T(8,128)S(1)} %get-tuple-element.56), channel_id=1, source_target_pairs={{0,1},{1,2},{2,3},{4,5},{5,6},{6,7},{8,9},{9,10},{10,11},{12,13},{... | collective-permute-start | bytes 2408 | tf_op jit(solution)/shard_map/ppermute | solution.py:20
  34.5 33.9 %all-reduce.16 = (f32[]{:T(128)}, f32[]{:T(128)}) all-reduce(f32[]{:T(128)} %get-tuple-element.6, f32[]{:T(128)} %get-tuple-element.5), channel_id=1, replica_groups=mesh['parts'=2,'gx'=4,'gy'=2,'gz'=2] {'gx','gy','gz'}, use_global_device_ids=true, to_apply=%region_1.2 | all-reduce | flops 2 | bytes 16 | tf_op jit(solution)/shard_map/psum | solution.py:86
  71.8 4.5 %collective-permute-start.9 = (f32[2,20,1,256]{3,2,1,0:T(1,128)S(1)}, f32[2,20,1,256]{3,2,1,0:T(1,128)S(1)}, u32[]{:S(2)}, u32[]{:S(2)}) collective-permute-start(f32[2,20,1,256]{3,2,1,0:T(1,128)S(1)} %get-tuple-element.54), channel_id=1, source_target_pairs={{0,4},{4,8},{8,12},{1,5},{5,9},{9,13},{2,6},{6,10},{10,14},{3,7},{... | collective-permute-start | bytes 122888 | tf_op jit(solution)/shard_map/ppermute | solution.py:20
  80.8 3.0 %collective-permute-start.11 = (f32[2,20,10,1]{3,2,1,0:T(8,128)}, f32[2,20,10,1]{3,2,1,0:T(8,128)S(1)}, u32[]{:S(2)}, u32[]{:S(2)}) collective-permute-start(f32[2,20,10,1]{3,2,1,0:T(8,128)} %get-tuple-element.44), channel_id=1, source_target_pairs={{0,1},{1,2},{2,3},{4,5},{5,6},{6,7},{8,9},{9,10},{10,11},{12,13},{... | collective-permute-start | bytes 4808 | tf_op jit(solution)/shard_map/ppermute | solution.py:20
  86.5 1.3 fusion.67
  89.4 1.9 multiply_reduce_fusion.2
  91.3 31.7 %psum.60 = f32[]{:T(128)} all-reduce(f32[]{:T(128)} %get-tuple-element.28), channel_id=1, replica_groups=mesh['parts'=2,'gx'=4,'gy'=2,'gz'=2] {'gx','gy','gz'}, use_global_device_ids=true, to_apply=%region_9.10 | all-reduce | flops 1 | bytes 8 | tf_op jit(solution)/shard_map/psum | solution.py:103
  126.5 4.5 %collective-permute-start.13 = (f32[2,20,1,256]{3,2,1,0:T(1,128)S(1)}, f32[2,20,1,256]{3,2,1,0:T(1,128)S(1)}, u32[]{:S(2)}, u32[]{:S(2)}) collective-permute-start(f32[2,20,1,256]{3,2,1,0:T(1,128)S(1)} %get-tuple-element.52), channel_id=1, source_target_pairs={{0,4},{4,8},{8,12},{1,5},{5,9},{9,13},{2,6},{6,10},{10,14},{3,7},{... | collective-permute-start | bytes 122888 | tf_op jit(solution)/shard_map/ppermute | solution.py:20
  131.1 1.6 collective-permute-done.13
  134.3 3.1 %collective-permute-start.15 = (f32[2,20,10,1]{3,2,1,0:T(8,128)S(1)}, f32[2,20,10,1]{3,2,1,0:T(8,128)S(1)}, u32[]{:S(2)}, u32[]{:S(2)}) collective-permute-start(f32[2,20,10,1]{3,2,1,0:T(8,128)S(1)} %get-tuple-element.42), channel_id=1, source_target_pairs={{0,1},{1,2},{2,3},{4,5},{5,6},{6,7},{8,9},{9,10},{10,11},{12,13},{... | collective-permute-start | bytes 4808 | tf_op jit(solution)/shard_map/ppermute | solution.py:20
  141.8 32.9 %psum.61 = f32[]{:T(128)} all-reduce(f32[]{:T(128)} %get-tuple-element.21), channel_id=1, replica_groups=mesh['parts'=2,'gx'=4,'gy'=2,'gz'=2] {'gx','gy','gz'}, use_global_device_ids=true, to_apply=%region_11.12 | all-reduce | flops 1 | bytes 8 | tf_op jit(solution)/shard_map/psum | solution.py:96
  178.2 4.5 %collective-permute-start.17 = (f32[2,20,1,256]{3,2,1,0:T(1,128)S(1)}, f32[2,20,1,256]{3,2,1,0:T(1,128)S(1)}, u32[]{:S(2)}, u32[]{:S(2)}) collective-permute-start(f32[2,20,1,256]{3,2,1,0:T(1,128)S(1)} %get-tuple-element.50), channel_id=1, source_target_pairs={{0,4},{4,8},{8,12},{1,5},{5,9},{9,13},{2,6},{6,10},{10,14},{3,7},{... | collective-permute-start | bytes 122888 | tf_op jit(solution)/shard_map/ppermute | solution.py:20
  182.8 1.6 collective-permute-done.17
  186.0 3.1 %collective-permute-start.19 = (f32[2,20,10,1]{3,2,1,0:T(8,128)S(1)}, f32[2,20,10,1]{3,2,1,0:T(8,128)S(1)}, u32[]{:S(2)}, u32[]{:S(2)}) collective-permute-start(f32[2,20,10,1]{3,2,1,0:T(8,128)S(1)} %get-tuple-element.40), channel_id=1, source_target_pairs={{0,1},{1,2},{2,3},{4,5},{5,6},{6,7},{8,9},{9,10},{10,11},{12,13},{... | collective-permute-start | bytes 4808 | tf_op jit(solution)/shard_map/ppermute | solution.py:20
  192.1 1.4 fusion.104
  193.5 33.0 %all-reduce.15 = (f32[]{:T(128)}, f32[]{:T(128)}, f32[]{:T(128)}, f32[]{:T(128)}) all-reduce(f32[]{:T(128)} %get-tuple-element.4, f32[]{:T(128)} %get-tuple-element.19, f32[]{:T(128)} %get-tuple-element.3, f32[]{:T(128)} %fusion.104), channel_id=1, replica_groups=mesh['parts'=2,'gx'=4,'gy'=2,'gz'=2] {'gx','gy','gz'}, use_global_device_ids=true, to_apply=%region_13.14 | all-reduce | flops 4 | bytes 32 | tf_op jit(solution)/shard_map/psum | solution.py:99
  235.0 4.5 %collective-permute-start.21 = (f32[2,20,1,256]{3,2,1,0:T(1,128)S(1)}, f32[2,20,1,256]{3,2,1,0:T(1,128)S(1)}, u32[]{:S(2)}, u32[]{:S(2)}) collective-permute-start(f32[2,20,1,256]{3,2,1,0:T(1,128)S(1)} %get-tuple-element.48), channel_id=1, source_target_pairs={{0,4},{4,8},{8,12},{1,5},{5,9},{9,13},{2,6},{6,10},{10,14},{3,7},{... | collective-permute-start | bytes 122888 | tf_op jit(solution)/shard_map/ppermute | solution.py:20
  239.6 1.6 collective-permute-done.21
  242.8 3.1 %collective-permute-start.23 = (f32[2,20,10,1]{3,2,1,0:T(8,128)S(1)}, f32[2,20,10,1]{3,2,1,0:T(8,128)S(1)}, u32[]{:S(2)}, u32[]{:S(2)}) collective-permute-start(f32[2,20,10,1]{3,2,1,0:T(8,128)S(1)} %get-tuple-element.39), channel_id=1, source_target_pairs={{0,1},{1,2},{2,3},{4,5},{5,6},{6,7},{8,9},{9,10},{10,11},{12,13},{... | collective-permute-start | bytes 4808 | tf_op jit(solution)/shard_map/ppermute | solution.py:20
  248.9 1.3 fusion.13
  (172 shorter events, 41.7 us)
Async XLA Ops:
  2.4 13.5 %collective-permute-start.1 = (f32[2,20,1,256]{3,2,1,0:T(1,128)S(1)}, f32[2,20,1,256]{3,2,1,0:T(1,128)S(1)}, u32[]{:S(2)}, u32[]{:S(2)}) collective-permute-start(f32[2,20,1,256]{3,2,1,0:T(1,128)S(1)} %get-tuple-element.59), channel_id=1, source_target_pairs={{4,0},{8,4},{12,8},{5,1},{9,5},{13,9},{6,2},{10,6},{14,10},{7,3},{... | collective-permute-start | bytes 122888 | tf_op jit(solution)/shard_map/ppermute | solution.py:22
  3.7 12.2 %collective-permute-start.3 = (f32[2,20,1,256]{3,2,1,0:T(1,128)S(1)}, f32[2,20,1,256]{3,2,1,0:T(1,128)S(1)}, u32[]{:S(2)}, u32[]{:S(2)}) collective-permute-start(f32[2,20,1,256]{3,2,1,0:T(1,128)S(1)} %get-tuple-element.58), channel_id=1, source_target_pairs={{0,4},{4,8},{8,12},{1,5},{5,9},{9,13},{2,6},{6,10},{10,14},{3,7},{... | collective-permute-start | bytes 122888 | tf_op jit(solution)/shard_map/ppermute | solution.py:20
  9.3 11.3 %collective-permute-start = (f32[20,1,256]{2,1,0:T(1,128)S(1)}, f32[20,1,256]{2,1,0:T(1,128)S(1)}, u32[]{:S(2)}, u32[]{:S(2)}) collective-permute-start(f32[20,1,256]{2,1,0:T(1,128)S(1)} %get-tuple-element.67), channel_id=1, source_target_pairs={{4,0},{8,4},{12,8},{5,1},{9,5},{13,9},{6,2},{10,6},{14,10},{7,3},{... | collective-permute-start | bytes 61448 | tf_op jit(solution)/shard_map/ppermute | solution.py:22
  10.6 10.0 %collective-permute-start.2 = (f32[20,1,256]{2,1,0:T(1,128)S(1)}, f32[20,1,256]{2,1,0:T(1,128)S(1)}, u32[]{:S(2)}, u32[]{:S(2)}) collective-permute-start(f32[20,1,256]{2,1,0:T(1,128)S(1)} %get-tuple-element.66), channel_id=1, source_target_pairs={{0,4},{4,8},{8,12},{1,5},{5,9},{9,13},{2,6},{6,10},{10,14},{3,7},{... | collective-permute-start | bytes 61448 | tf_op jit(solution)/shard_map/ppermute | solution.py:20
  16.2 4.4 %collective-permute-start.5 = (f32[2,20,10,1]{3,2,1,0:T(8,128)S(1)}, f32[2,20,10,1]{3,2,1,0:T(8,128)S(1)}, u32[]{:S(2)}, u32[]{:S(2)}) collective-permute-start(f32[2,20,10,1]{3,2,1,0:T(8,128)S(1)} %get-tuple-element.47), channel_id=1, source_target_pairs={{1,0},{2,1},{3,2},{5,4},{6,5},{7,6},{9,8},{10,9},{11,10},{13,12},{... | collective-permute-start | bytes 4808 | tf_op jit(solution)/shard_map/ppermute | solution.py:22
  17.5 4.3 %collective-permute-start.7 = (f32[2,20,10,1]{3,2,1,0:T(8,128)S(1)}, f32[2,20,10,1]{3,2,1,0:T(8,128)S(1)}, u32[]{:S(2)}, u32[]{:S(2)}) collective-permute-start(f32[2,20,10,1]{3,2,1,0:T(8,128)S(1)} %get-tuple-element.46), channel_id=1, source_target_pairs={{0,1},{1,2},{2,3},{4,5},{5,6},{6,7},{8,9},{9,10},{10,11},{12,13},{... | collective-permute-start | bytes 4808 | tf_op jit(solution)/shard_map/ppermute | solution.py:20
  22.4 8.2 %collective-permute-start.4 = (f32[20,10,1]{2,1,0:T(8,128)S(1)}, f32[20,10,1]{2,1,0:T(8,128)S(1)}, u32[]{:S(2)}, u32[]{:S(2)}) collective-permute-start(f32[20,10,1]{2,1,0:T(8,128)S(1)} %get-tuple-element.57), channel_id=1, source_target_pairs={{1,0},{2,1},{3,2},{5,4},{6,5},{7,6},{9,8},{10,9},{11,10},{13,12},{... | collective-permute-start | bytes 2408 | tf_op jit(solution)/shard_map/ppermute | solution.py:22
  23.7 7.9 %collective-permute-start.6 = (f32[20,10,1]{2,1,0:T(8,128)S(1)}, f32[20,10,1]{2,1,0:T(8,128)S(1)}, u32[]{:S(2)}, u32[]{:S(2)}) collective-permute-start(f32[20,10,1]{2,1,0:T(8,128)S(1)} %get-tuple-element.56), channel_id=1, source_target_pairs={{0,1},{1,2},{2,3},{4,5},{5,6},{6,7},{8,9},{9,10},{10,11},{12,13},{... | collective-permute-start | bytes 2408 | tf_op jit(solution)/shard_map/ppermute | solution.py:20
  70.5 6.8 %collective-permute-start.8 = (f32[2,20,1,256]{3,2,1,0:T(1,128)S(1)}, f32[2,20,1,256]{3,2,1,0:T(1,128)S(1)}, u32[]{:S(2)}, u32[]{:S(2)}) collective-permute-start(f32[2,20,1,256]{3,2,1,0:T(1,128)S(1)} %get-tuple-element.55), channel_id=1, source_target_pairs={{4,0},{8,4},{12,8},{5,1},{9,5},{13,9},{6,2},{10,6},{14,10},{7,3},{... | collective-permute-start | bytes 122888 | tf_op jit(solution)/shard_map/ppermute | solution.py:22
  71.8 6.2 %collective-permute-start.9 = (f32[2,20,1,256]{3,2,1,0:T(1,128)S(1)}, f32[2,20,1,256]{3,2,1,0:T(1,128)S(1)}, u32[]{:S(2)}, u32[]{:S(2)}) collective-permute-start(f32[2,20,1,256]{3,2,1,0:T(1,128)S(1)} %get-tuple-element.54), channel_id=1, source_target_pairs={{0,4},{4,8},{8,12},{1,5},{5,9},{9,13},{2,6},{6,10},{10,14},{3,7},{... | collective-permute-start | bytes 122888 | tf_op jit(solution)/shard_map/ppermute | solution.py:20
  79.5 7.0 %collective-permute-start.10 = (f32[2,20,10,1]{3,2,1,0:T(8,128)}, f32[2,20,10,1]{3,2,1,0:T(8,128)S(1)}, u32[]{:S(2)}, u32[]{:S(2)}) collective-permute-start(f32[2,20,10,1]{3,2,1,0:T(8,128)} %get-tuple-element.45), channel_id=1, source_target_pairs={{1,0},{2,1},{3,2},{5,4},{6,5},{7,6},{9,8},{10,9},{11,10},{13,12},{... | collective-permute-start | bytes 4808 | tf_op jit(solution)/shard_map/ppermute | solution.py:22
  80.8 5.7 %collective-permute-start.11 = (f32[2,20,10,1]{3,2,1,0:T(8,128)}, f32[2,20,10,1]{3,2,1,0:T(8,128)S(1)}, u32[]{:S(2)}, u32[]{:S(2)}) collective-permute-start(f32[2,20,10,1]{3,2,1,0:T(8,128)} %get-tuple-element.44), channel_id=1, source_target_pairs={{0,1},{1,2},{2,3},{4,5},{5,6},{6,7},{8,9},{9,10},{10,11},{12,13},{... | collective-permute-start | bytes 4808 | tf_op jit(solution)/shard_map/ppermute | solution.py:20
  125.2 5.9 %collective-permute-start.12 = (f32[2,20,1,256]{3,2,1,0:T(1,128)S(1)}, f32[2,20,1,256]{3,2,1,0:T(1,128)S(1)}, u32[]{:S(2)}, u32[]{:S(2)}) collective-permute-start(f32[2,20,1,256]{3,2,1,0:T(1,128)S(1)} %get-tuple-element.53), channel_id=1, source_target_pairs={{4,0},{8,4},{12,8},{5,1},{9,5},{13,9},{6,2},{10,6},{14,10},{7,3},{... | collective-permute-start | bytes 122888 | tf_op jit(solution)/shard_map/ppermute | solution.py:22
  126.5 6.2 %collective-permute-start.13 = (f32[2,20,1,256]{3,2,1,0:T(1,128)S(1)}, f32[2,20,1,256]{3,2,1,0:T(1,128)S(1)}, u32[]{:S(2)}, u32[]{:S(2)}) collective-permute-start(f32[2,20,1,256]{3,2,1,0:T(1,128)S(1)} %get-tuple-element.52), channel_id=1, source_target_pairs={{0,4},{4,8},{8,12},{1,5},{5,9},{9,13},{2,6},{6,10},{10,14},{3,7},{... | collective-permute-start | bytes 122888 | tf_op jit(solution)/shard_map/ppermute | solution.py:20
  133.0 4.4 %collective-permute-start.14 = (f32[2,20,10,1]{3,2,1,0:T(8,128)S(1)}, f32[2,20,10,1]{3,2,1,0:T(8,128)S(1)}, u32[]{:S(2)}, u32[]{:S(2)}) collective-permute-start(f32[2,20,10,1]{3,2,1,0:T(8,128)S(1)} %get-tuple-element.43), channel_id=1, source_target_pairs={{1,0},{2,1},{3,2},{5,4},{6,5},{7,6},{9,8},{10,9},{11,10},{13,12},{... | collective-permute-start | bytes 4808 | tf_op jit(solution)/shard_map/ppermute | solution.py:22
  134.3 4.3 %collective-permute-start.15 = (f32[2,20,10,1]{3,2,1,0:T(8,128)S(1)}, f32[2,20,10,1]{3,2,1,0:T(8,128)S(1)}, u32[]{:S(2)}, u32[]{:S(2)}) collective-permute-start(f32[2,20,10,1]{3,2,1,0:T(8,128)S(1)} %get-tuple-element.42), channel_id=1, source_target_pairs={{0,1},{1,2},{2,3},{4,5},{5,6},{6,7},{8,9},{9,10},{10,11},{12,13},{... | collective-permute-start | bytes 4808 | tf_op jit(solution)/shard_map/ppermute | solution.py:20
  176.9 5.9 %collective-permute-start.16 = (f32[2,20,1,256]{3,2,1,0:T(1,128)S(1)}, f32[2,20,1,256]{3,2,1,0:T(1,128)S(1)}, u32[]{:S(2)}, u32[]{:S(2)}) collective-permute-start(f32[2,20,1,256]{3,2,1,0:T(1,128)S(1)} %get-tuple-element.51), channel_id=1, source_target_pairs={{4,0},{8,4},{12,8},{5,1},{9,5},{13,9},{6,2},{10,6},{14,10},{7,3},{... | collective-permute-start | bytes 122888 | tf_op jit(solution)/shard_map/ppermute | solution.py:22
  178.2 6.2 %collective-permute-start.17 = (f32[2,20,1,256]{3,2,1,0:T(1,128)S(1)}, f32[2,20,1,256]{3,2,1,0:T(1,128)S(1)}, u32[]{:S(2)}, u32[]{:S(2)}) collective-permute-start(f32[2,20,1,256]{3,2,1,0:T(1,128)S(1)} %get-tuple-element.50), channel_id=1, source_target_pairs={{0,4},{4,8},{8,12},{1,5},{5,9},{9,13},{2,6},{6,10},{10,14},{3,7},{... | collective-permute-start | bytes 122888 | tf_op jit(solution)/shard_map/ppermute | solution.py:20
  184.7 5.1 %collective-permute-start.18 = (f32[2,20,10,1]{3,2,1,0:T(8,128)S(1)}, f32[2,20,10,1]{3,2,1,0:T(8,128)S(1)}, u32[]{:S(2)}, u32[]{:S(2)}) collective-permute-start(f32[2,20,10,1]{3,2,1,0:T(8,128)S(1)} %get-tuple-element.41), channel_id=1, source_target_pairs={{1,0},{2,1},{3,2},{5,4},{6,5},{7,6},{9,8},{10,9},{11,10},{13,12},{... | collective-permute-start | bytes 4808 | tf_op jit(solution)/shard_map/ppermute | solution.py:22
  186.0 4.3 %collective-permute-start.19 = (f32[2,20,10,1]{3,2,1,0:T(8,128)S(1)}, f32[2,20,10,1]{3,2,1,0:T(8,128)S(1)}, u32[]{:S(2)}, u32[]{:S(2)}) collective-permute-start(f32[2,20,10,1]{3,2,1,0:T(8,128)S(1)} %get-tuple-element.40), channel_id=1, source_target_pairs={{0,1},{1,2},{2,3},{4,5},{5,6},{6,7},{8,9},{9,10},{10,11},{12,13},{... | collective-permute-start | bytes 4808 | tf_op jit(solution)/shard_map/ppermute | solution.py:20
  233.7 5.9 %collective-permute-start.20 = (f32[2,20,1,256]{3,2,1,0:T(1,128)S(1)}, f32[2,20,1,256]{3,2,1,0:T(1,128)S(1)}, u32[]{:S(2)}, u32[]{:S(2)}) collective-permute-start(f32[2,20,1,256]{3,2,1,0:T(1,128)S(1)} %get-tuple-element.49), channel_id=1, source_target_pairs={{4,0},{8,4},{12,8},{5,1},{9,5},{13,9},{6,2},{10,6},{14,10},{7,3},{... | collective-permute-start | bytes 122888 | tf_op jit(solution)/shard_map/ppermute | solution.py:22
  235.0 6.2 %collective-permute-start.21 = (f32[2,20,1,256]{3,2,1,0:T(1,128)S(1)}, f32[2,20,1,256]{3,2,1,0:T(1,128)S(1)}, u32[]{:S(2)}, u32[]{:S(2)}) collective-permute-start(f32[2,20,1,256]{3,2,1,0:T(1,128)S(1)} %get-tuple-element.48), channel_id=1, source_target_pairs={{0,4},{4,8},{8,12},{1,5},{5,9},{9,13},{2,6},{6,10},{10,14},{3,7},{... | collective-permute-start | bytes 122888 | tf_op jit(solution)/shard_map/ppermute | solution.py:20
  241.5 5.0 %collective-permute-start.22 = (f32[2,20,10,1]{3,2,1,0:T(8,128)S(1)}, f32[2,20,10,1]{3,2,1,0:T(8,128)S(1)}, u32[]{:S(2)}, u32[]{:S(2)}) collective-permute-start(f32[2,20,10,1]{3,2,1,0:T(8,128)S(1)} %get-tuple-element.38), channel_id=1, source_target_pairs={{1,0},{2,1},{3,2},{5,4},{6,5},{7,6},{9,8},{10,9},{11,10},{13,12},{... | collective-permute-start | bytes 4808 | tf_op jit(solution)/shard_map/ppermute | solution.py:22
  242.8 4.3 %collective-permute-start.23 = (f32[2,20,10,1]{3,2,1,0:T(8,128)S(1)}, f32[2,20,10,1]{3,2,1,0:T(8,128)S(1)}, u32[]{:S(2)}, u32[]{:S(2)}) collective-permute-start(f32[2,20,10,1]{3,2,1,0:T(8,128)S(1)} %get-tuple-element.39), channel_id=1, source_target_pairs={{0,1},{1,2},{2,3},{4,5},{5,6},{6,7},{8,9},{9,10},{10,11},{12,13},{... | collective-permute-start | bytes 4808 | tf_op jit(solution)/shard_map/ppermute | solution.py:20
  (40 other events, 225.4 us)
where the time goes:
time: 255 us; the launch traced here: 250 us
  blocking collectives  131 us (51%)
  starting transfers between devices  65.9 us (26%)
  other arithmetic  21.5 us (8%)
  between operations  14.5 us (6%)
  waiting for transfers between devices  9.97 us (4%)
  local copies, waits for them, and re-layouts  6.83 us (3%)
    ppermute x12, starting transfers between devices, padded(): lax.ppermute(tail, axis, [(i, (i + 1) % count) for i in range(ends)])  50.4 us
    psum x1, blocking collectives, body(): rho_now = lax.psum(jnp.sum(adjoint_rhs * adjoint_rhs), ('gx', 'gy', 'gz'))  33.9 us
    psum x1, blocking collectives, body(): width_sq = lax.psum(jnp.sum(quasi * quasi), ('gx', 'gy', 'gz'))  33 us
    psum x1, blocking collectives, body(): sigma_now = lax.psum(jnp.sum(carried * adjoint_rhs), ('gx', 'gy', 'gz'))  32.9 us
    psum x1, blocking collectives, body(): lax.psum((jnp.sum(quasi * quasi), jnp.sum(quasi * adjoint_rhs)), ('gx', '...  31.7 us
    ppermute x12, starting transfers between devices, padded(): lax.ppermute(head, axis, [((i + 1) % count, i) for i in range(ends)])  15.5 us
    ppermute x12, waiting for transfers between devices, padded(): lax.ppermute(tail, axis, [(i, (i + 1) % count) for i in range(ends)])  9.91 us
  transfers between devices with their start and end apart: 24, of which 9 were waited for; matrix products, arithmetic and copies ran while one was open for 1% of the time, Pallas kernels for 0%

commit v1 on v0

v1 whole, which is shorter than its diff:
```python
import functools

import jax
import jax.numpy as jnp
from jax import lax
from jax.experimental import pallas as pl
from jax.experimental.pallas import tpu as pltpu
from jax.sharding import PartitionSpec as P

STEPS = 4
HALO = 4
ROWS = 8
LANES = 128
VMEM = pltpu.CompilerParams(vmem_limit_bytes=40 * 1024 * 1024)


def call(kernel, outs, scratch=()):
    return pl.pallas_call(
        kernel,
        out_shape=[jax.ShapeDtypeStruct(s, jnp.float32) for s in outs],
        scratch_shapes=[pltpu.VMEM(s, jnp.float32) for s in scratch],
        compiler_params=VMEM,
    )


def own_planes(rhs, eta, friction, ice, grounded):
    layers = eta.shape[0]
    cover = ice[...].astype(jnp.float32)
    drag = friction[...] * grounded[...].astype(jnp.float32)

    def plane(p):
        if p < 2 * layers:
            return rhs[p // layers, p % layers] * cover
        if p < 3 * layers:
            return eta[p - 2 * layers]
        return cover if p == 3 * layers else drag

    return plane


def pair_of(q, layers):
    if q < layers:
        return q, q + layers
    if q < layers + layers // 2:
        return q + layers, q + layers + layers // 2
    return 3 * layers, 3 * layers + 1


def pack_kernel(rhs, eta, friction, ice, grounded, to_left, to_right, to_prev, to_next):
    layers = eta.shape[0]
    plane = own_planes(rhs, eta, friction, ice, grounded)
    lane = lax.broadcasted_iota(jnp.int32, (ROWS, LANES), 1)
    row = lax.broadcasted_iota(jnp.int32, (ROWS, LANES), 0)
    upper = row < HALO
    width = to_prev.shape[0]
    left = [jnp.zeros((ROWS, LANES), jnp.float32) for _ in range(2)]
    right = [jnp.zeros((ROWS, LANES), jnp.float32) for _ in range(2)]
    for q in range(width // 2):
        first, second = pair_of(q, layers)
        x, y = plane(first), plane(second)
        for half in range(2):
            xs = x[:, half * LANES : (half + 1) * LANES]
            ys = y[:, half * LANES : (half + 1) * LANES]
            to_prev[2 * q + half] = jnp.where(upper, xs, pltpu.roll(ys, HALO, 0))
            to_next[2 * q + half] = jnp.where(upper, pltpu.roll(ys, HALO, 0), xs)
        for p, v in ((first, x), (second, y)):
            group, place = p // 32, HALO * (p % 32)
            mine = (lane >= place) & (lane < place + HALO)
            head, tail = v[:, :LANES], v[:, LANES:]
            shift = (place + HALO) % LANES
            left[group] = jnp.where(mine, pltpu.roll(head, place, 1) if place else head, left[group])
            right[group] = jnp.where(mine, pltpu.roll(tail, shift, 1) if shift else tail, right[group])
    for group in range(2):
        to_left[group] = left[group]
        to_right[group] = right[group]


def two_sum(a, b):
    s = a + b
    t = s - a
    return s, (a - (s - t)) + (b - t)


def join(x, y):
    s, e = two_sum(x[0], y[0])
    e = e + (x[1] + y[1])
    h = s + e
    return h, e - (h - s)


def times(scalar, x):
    def cut(v):
        t = v * 4097.0
        h = t - (t - v)
        return h, v - h

    p = scalar * x[0]
    sh, sl = cut(scalar)
    xh, xl = cut(x[0])
    e = ((sh * xh - p) + sh * xl + sl * xh) + sl * xl
    return p, e + scalar * x[1]


def power_kernel(
    rhs, eta, friction, ice, grounded, from_next, from_prev, columns,
    powers, moments,
    field_a, field_b, eta_row, eta_col, eta_half, eta_up, cover, drag,
):
    layers = eta.shape[0]
    plane = own_planes(rhs, eta, friction, ice, grounded)
    lane = lax.broadcasted_iota(jnp.int32, (ROWS, LANES), 1)
    row = lax.broadcasted_iota(jnp.int32, (ROWS, LANES), 0)
    upper = row < HALO
    strips = from_next.shape[0] - 4
    corner = [jnp.where(upper, from_next[strips + t], from_prev[strips + t]) for t in range(4)]
    beside = [columns[t] for t in range(4)]

    def side(tiles, p):
        group, place = p // 32, HALO * (p % 32)
        a, b = (LANES - place) % LANES, LANES - place - HALO
        right = pltpu.roll(tiles[group], a, 1) if a else tiles[group]
        left = pltpu.roll(tiles[2 + group], b, 1) if b else tiles[2 + group]
        return jnp.where(lane < HALO, right, jnp.where(lane >= LANES - HALO, left, 0.0))

    def fill(p, dst):
        dst[0:ROWS, 0 : 2 * LANES] = plane(p)
        dst[0:ROWS, 2 * LANES :] = side(beside, p)
        dst[ROWS:, 2 * LANES :] = side(corner, p)

    def target(p):
        if p < 2 * layers:
            return field_a.at[p // layers, p % layers]
        if p < 3 * layers:
            return eta_half.at[p - 2 * layers]
        return cover if p == 3 * layers else drag

    for q in range(strips // 2):
        first, second = pair_of(q, layers)
        for half in range(2):
            below, above = from_next[2 * q + half], from_prev[2 * q + half]
            cut = slice(half * LANES, (half + 1) * LANES)
            target(first)[ROWS:, cut] = jnp.where(upper, below, above)
            target(second)[ROWS:, cut] = pltpu.roll(jnp.where(upper, above, below), HALO, 0)
        fill(first, target(first))
        fill(second, target(second))

    def row_next(v):
        return pltpu.roll(v, 2 * ROWS - 1, 0)

    def row_prev(v):
        return pltpu.roll(v, 1, 0)

    def col_next(v):
        return pltpu.roll(v, 3 * LANES - 1, 1)

    def col_prev(v):
        return pltpu.roll(v, 1, 1)

    for k in range(layers):
        e = eta_half[k]
        eta_row[k] = 2.0 * (e + row_next(e))
        eta_col[k] = 0.5 * (e + col_next(e))
        eta_up[k] = e + eta_half[k + 1] if k + 1 < layers else jnp.zeros_like(e)
        if k:
            eta_half[k - 1] = 0.5 * eta_half[k - 1]
    eta_half[layers - 1] = 0.5 * eta_half[layers - 1]

    own = (slice(0, ROWS), slice(0, 2 * LANES))
    bare = 1.0 - ice[...].astype(jnp.float32)

    def apply(t, src, dst):
        def layer(k, carry):
            below0, below1, odd, even = carry
            g0, g1 = src[0, k], src[1, k]
            after = jnp.minimum(k + 1, layers - 1)
            e_row, e_col, e_half, e_up = eta_row[k], eta_col[k], eta_half[k], eta_up[k]
            up0 = e_up * (g0 - src[0, after])
            up1 = e_up * (g1 - src[1, after])
            g0n, g1n = row_next(g0), col_next(g1)
            f = e_half * (g1n - col_prev(g1))
            h = e_half * (g0n - row_prev(g0))
            flux = e_row * (g0 - g0n)
            out0 = flux - row_next(f) - row_prev(flux - f)
            flux = e_col * (g0 - col_next(g0))
            out0 = out0 + (flux - col_prev(flux)) + (up0 - below0)
            flux = (4.0 * e_col) * (g1 - g1n)
            out1 = flux - col_next(h) - col_prev(flux - h)
            flux = (0.25 * e_row) * (g1 - row_next(g1))
            out1 = out1 + (flux - row_prev(flux)) + (up1 - below1)
            m = cover[...]
            out0, out1 = m * out0, m * out1
            if t < STEPS:
                dst[0, k], dst[1, k] = out0, out1
            for c, g, out in ((0, g0, out0), (1, g1, out1)):
                outside = rhs[c, k] * bare
                before = g[own] + outside
                now = out[own] + outside
                powers[t - 1, c, k] = now
                odd = odd + before * now
                even = even + now * now
            return up0, up1, odd, even

        zero = jnp.zeros((ROWS, 2 * LANES), jnp.float32)
        d = drag[...]
        start = (-d * src[0, 0], -d * src[1, 0], zero, zero)
        return lax.fori_loop(0, layers, layer, start)[2:]

    square = jnp.zeros((ROWS, 2 * LANES), jnp.float32)
    for c in range(2):
        for k in range(layers):
            square = square + rhs[c, k] * rhs[c, k]
    sums = [square]
    src, dst = field_a, field_b
    for t in range(1, STEPS + 1):
        sums.extend(apply(t, src, dst))
        src, dst = dst, src

    tall = lax.broadcasted_iota(jnp.int32, (2 * ROWS, LANES), 0)
    high = jnp.zeros((2 * ROWS, LANES), jnp.float32)
    low = jnp.zeros((2 * ROWS, LANES), jnp.float32)
    for j, total in enumerate(sums):
        pair = two_sum(total[:, :LANES], total[:, LANES:])
        for step in (4, 2, 1):
            pair = join(pair, tuple(pltpu.roll(v, step, 0) for v in pair))
        high = jnp.where(tall == j, jnp.concatenate([pair[0]] * 2, 0), high)
        low = jnp.where(tall == j, jnp.concatenate([pair[1]] * 2, 0), low)
    moments[0] = high
    moments[1] = low


def add_kernel(*refs):
    *ins, out = refs
    total = (ins[0][0], ins[0][1])
    for x in ins[1:]:
        total = join(total, (x[0], x[1]))
    out[0], out[1] = total


def solve(total):
    for step in (64, 32, 16, 8, 4, 2, 1):
        total = join(total, tuple(pltpu.roll(v, step, 1) for v in total))

    def spread(v, j):
        return jnp.broadcast_to(v[j : j + 1], (ROWS, LANES))

    centre = spread(total[0], 1) / spread(total[0], 0)
    wide = jnp.concatenate([centre, centre], 0)
    mu = [spread(total[0], 0)]
    for _ in range(2 * STEPS):
        step = times(wide, total)
        total = join(tuple(pltpu.roll(v, 2 * ROWS - 1, 0) for v in total), (-step[0], -step[1]))
        mu.append(spread(total[0], 0))

    def plus(a, b):
        n = max(len(a), len(b))
        return [a[i] + b[i] if i < min(len(a), len(b)) else (a[i] if i < len(a) else b[i]) for i in range(n)]

    def scaled(s, a):
        return [s * x for x in a]

    def operator(a):
        return plus([centre * x for x in a], [jnp.zeros_like(centre)] + a)

    def dot(a, b):
        square = [None] * (len(a) + len(b) - 1)
        for i, x in enumerate(a):
            for j, y in enumerate(b):
                z = x * y
                square[i + j] = z if square[i + j] is None else square[i + j] + z
        value = square[0] * mu[0]
        for n in range(1, len(square)):
            value = value + square[n] * mu[n]
        return value

    one = jnp.ones_like(centre)
    right = [one]
    quasi, search, update, iterate = right, right, [], []
    applied = operator(search)
    carried = applied
    rho = mu[0]
    tau_sq = rho
    alpha = theta_sq = eta = None
    for half in range(STEPS):
        if half % 2 == 0:
            alpha = rho / dot(carried, right)
            search_next = plus(search, scaled(-alpha, carried))
        quasi = plus(quasi, scaled(-alpha, applied))
        if half:
            update = plus(search, scaled(theta_sq / alpha * eta, update))
        else:
            update = search
        theta_sq = dot(quasi, quasi) / tau_sq
        cosine_sq = 1.0 / (1.0 + theta_sq)
        tau_sq = tau_sq * theta_sq * cosine_sq
        eta = cosine_sq * alpha
        iterate = plus(iterate, scaled(eta, update))
        if half % 2 == 0:
            search = search_next
            applied = operator(search)
        elif half < STEPS - 1:
            rho_next = dot(quasi, right)
            beta = rho_next / rho
            search = plus(quasi, scaled(beta, search))
            applied_next = operator(search)
            carried = plus(applied_next, scaled(beta, plus(applied, scaled(beta, carried))))
            applied, rho = applied_next, rho_next
    powers = [iterate[-1]]
    for c in iterate[-2::-1]:
        powers = plus([c] + powers, scaled(-centre, powers))
    return powers


def final_kernel(rhs, powers, friction, ice, grounded, speed, *rest):
    *parts, iterate, residual, hessian = rest
    layers = rhs.shape[1]
    total = (parts[0][0], parts[0][1])
    for x in parts[1:]:
        total = join(total, (x[0], x[1]))
    factors = [jnp.concatenate([c, c], 1) for c in solve(total)]
    for c in range(2):
        for k in range(layers):
            r = rhs[c, k]
            vectors = [r] + [powers[t, c, k] for t in range(STEPS)]
            x = factors[0] * vectors[0]
            y = factors[0] * vectors[1]
            for t in range(1, STEPS):
                x = x + factors[t] * vectors[t]
                y = y + factors[t] * vectors[t + 1]
            iterate[c, k] = x
            residual[c, k] = r - y
    weight = ice[...].astype(jnp.float32) * (friction[...] * grounded[...].astype(jnp.float32))
    hessian[...] = weight * (speed[0] * iterate[0, 0] + speed[1] * iterate[1, 0])


def shifted(x, axis, step):
    count = lax.axis_size(axis)
    pairs = [(i, i + step) for i in range(count) if 0 <= i + step < count]
    return lax.ppermute(x, axis, pairs)


def exchange(x, axis):
    count = lax.axis_size(axis)
    stride = 1
    rounds = []
    while stride < count:
        size = 4 if (count // stride) % 4 == 0 else 2
        rounds.append((stride, size))
        stride *= size
    for at, (stride, size) in enumerate(rounds):
        parts = [x]
        for turn in range(1, size):
            pairs = []
            for i in range(count):
                place = (i // stride) % size
                pairs.append((i, i + ((place + turn) % size - place) * stride))
            parts.append(lax.ppermute(x, axis, pairs))
        if at == len(rounds) - 1:
            return parts
        x = call(add_kernel, [x.shape])(*parts)[0]
    return [x]


def body(adjoint_rhs, viscosity, friction, ice_mask, grounded, basal_velocity):
    layers = viscosity.shape[0]
    fields = (adjoint_rhs, viscosity, friction, ice_mask, grounded)
    tile = (ROWS, LANES)
    strips = (2 * (layers + layers // 2 + 1),) + tile
    to_left, to_right, to_prev, to_next = call(pack_kernel, [(2,) + tile, (2,) + tile, strips, strips])(*fields)
    columns = jnp.concatenate(
        [shifted(to_left, ("gy", "gz"), -1), shifted(to_right, ("gy", "gz"), 1)], axis=0
    )
    from_next = shifted(jnp.concatenate([to_prev, columns], axis=0), "gx", -1)
    from_prev = shifted(jnp.concatenate([to_next, columns], axis=0), "gx", 1)
    block = (layers, 2 * ROWS, 3 * LANES)
    powers, sums = call(
        power_kernel,
        [(STEPS,) + adjoint_rhs.shape, (2, 2 * ROWS, LANES)],
        [(2,) + block] * 2 + [block] * 4 + [block[1:]] * 2,
    )(*fields, from_next, from_prev, columns)
    parts = exchange(sums, ("gy", "gz"))
    if len(parts) > 1:
        sums = call(add_kernel, [sums.shape])(*parts)[0]
    parts = exchange(sums, "gx")
    return tuple(
        call(final_kernel, [adjoint_rhs.shape, adjoint_rhs.shape, friction.shape])(
            adjoint_rhs, powers, friction, ice_mask, grounded, basal_velocity, *parts
        )
    )


def solution(mesh):
    in_specs = (
        P(None, None, ("parts", "gx"), ("gy", "gz")),
        P(None, ("parts", "gx"), ("gy", "gz")),
        P(("parts", "gx"), ("gy", "gz")),
        P(("parts", "gx"), ("gy", "gz")),
        P(("parts", "gx"), ("gy", "gz")),
        P(None, ("parts", "gx"), ("gy", "gz")),
    )
    out_specs = (
        P(None, None, ("parts", "gx"), ("gy", "gz")),
        P(None, None, ("parts", "gx"), ("gy", "gz")),
        P(("parts", "gx"), ("gy", "gz")),
    )
    return jax.shard_map(body, mesh=mesh, in_specs=in_specs, out_specs=out_specs, check_vma=False)
```

time: 255 us -> 55.1 us (0.22); the launches traced: 250 us -> 54.7 us
  blocking collectives: 131 us -> 0 us
  starting transfers between devices: 65.9 us -> 16.8 us
  other arithmetic: 21.5 us -> 0.04 us
  Pallas kernels: 0 us -> 15.5 us
  between operations: 14.5 us -> 0.72 us
  waiting for transfers between devices: 9.97 us -> 17.7 us
  local copies, waits for them, and re-layouts: 6.83 us -> 3.98 us
    psum x4 -> x0, blocking collectives: 131 us -> none  [the longest x1 33.9 us: body(): rho_now = lax.psum(jnp.sum(adjoint_rhs * adjoint_rhs), ('gx', 'gy', 'gz'))]
    ppermute x24 -> x10, starting transfers between devices: 65.9 us -> 16.8 us  [the longest x4 10.6 us: shifted(): return lax.ppermute(x, axis, pairs)]
    pallas_call x0 -> x4, Pallas kernels: none -> 15.5 us  [the longest x1 13.7 us: body(): call(power_kernel, [(STEPS,) + adjoint_rhs.shape, (2, 2 * ROWS, LANES)],...]
    mul x24 -> x0, other arithmetic: 9.79 us -> none  [the longest x5 3.13 us: stencil(): eta_rim[:, :, 1:-1]]
    ppermute x24 -> x10, waiting for transfers between devices: 9.97 us -> 17.7 us  [the longest x4 10.6 us: shifted(): return lax.ppermute(x, axis, pairs)]
    reduce_sum x6 -> x0, other arithmetic: 7.37 us -> none  [the longest x2 2.54 us: body(): sigma_now = lax.psum(jnp.sum(carried * adjoint_rhs), ('gx', 'gy', 'gz'))]
  transfers between devices with their start and end apart: 24 -> 10, of which waited for: 9 -> 7; matrix products, arithmetic and copies ran while one was open for 1% -> 0% of each run, Pallas kernels for 0% -> 0%
where the time goes in v1:
time: 55.1 us; the launch traced here: 54.7 us
  waiting for transfers between devices  17.7 us (32%)
  starting transfers between devices  16.8 us (30%)
  Pallas kernels  15.5 us (28%)
  local copies, waits for them, and re-layouts  3.98 us (7%)
  between operations  0.72 us (1%)
    pallas_call x1, Pallas kernels, body(): call(power_kernel, [(STEPS,) + adjoint_rhs.shape, (2, 2 * ROWS, LANES)],...  13.7 us
    ppermute x4, waiting for transfers between devices, shifted(): return lax.ppermute(x, axis, pairs)  10.6 us
    ppermute x4, starting transfers between devices, shifted(): return lax.ppermute(x, axis, pairs)  10.6 us
    ppermute x6, waiting for transfers between devices, exchange(): parts.append(lax.ppermute(x, axis, pairs))  7.12 us
    ppermute x6, starting transfers between devices, exchange(): parts.append(lax.ppermute(x, axis, pairs))  6.26 us
    unnamed x14, local copies, waits for them, and re-layouts  3.98 us
    pallas_call x1, Pallas kernels, body(): call(final_kernel, [adjoint_rhs.shape, adjoint_rhs.shape, friction.shape])  1.6 us
  transfers between devices with their start and end apart: 10, of which 7 were waited for; matrix products, arithmetic and copies ran while one was open for 0% of the time, Pallas kernels for 0%

profile of v1, /device:TPU:0, one launch (start us, length us, event | category | flops | bytes accessed | tf_op | source)
XLA Modules:
  0.0 54.7 jit_solution(13661550707837764136)
XLA Ops:
  0.6 1.0 %copy-done = f32[2,20,8,256]{3,2,1,0:T(8,128)S(1)} copy-done((f32[2,20,8,256]{3,2,1,0:T(8,128)S(1)}, f32[2,20,8,256]{3,2,1,0:T(8,128)}, u32[]{:S(2)}) %copy-start) | copy-done | bytes 327704
  1.6 0.9 %copy-done.2 = f32[20,8,256]{2,1,0:T(8,128)S(1)} copy-done((f32[20,8,256]{2,1,0:T(8,128)S(1)}, f32[20,8,256]{2,1,0:T(8,128)}, u32[]{:S(2)}) %copy-start.2) | copy-done | bytes 163864
  2.5 0.7 %copy-done.3 = f32[8,256]{1,0:T(8,128)S(1)} copy-done((f32[8,256]{1,0:T(8,128)S(1)}, f32[8,256]{1,0:T(8,128)}, u32[]{:S(2)}) %copy-start.3) | copy-done | bytes 8216
  3.2 0.7 %copy-done.4 = s32[8,256]{1,0:T(8,128)S(1)} copy-done((s32[8,256]{1,0:T(8,128)S(1)}, s32[8,256]{1,0:T(8,128)}, u32[]{:S(2)}) %copy-start.4) | copy-done | bytes 8216
  3.9 0.7 %copy-done.5 = s32[8,256]{1,0:T(8,128)S(1)} copy-done((s32[8,256]{1,0:T(8,128)S(1)}, s32[8,256]{1,0:T(8,128)}, u32[]{:S(2)}) %copy-start.5) | copy-done | bytes 8216
  4.6 0.2 shard_map.85
  4.8 1.3 %collective-permute-start = (f32[2,8,128]{2,1,0:T(8,128)S(1)}, f32[2,8,128]{2,1,0:T(8,128)S(1)}, u32[]{:S(2)}, u32[]{:S(2)}) collective-permute-start(f32[2,8,128]{2,1,0:T(8,128)S(1)} %get-tuple-element.10), channel_id=1, source_target_pairs={{1,0},{2,1},{3,2},{5,4},{6,5},{7,6},{9,8},{10,9},{11,10},{13,12},{... | collective-permute-start | bytes 24584 | tf_op jit(solution)/shard_map/ppermute | solution.py:338
  6.1 3.0 %collective-permute-start.1 = (f32[2,8,128]{2,1,0:T(8,128)S(1)}, f32[2,8,128]{2,1,0:T(8,128)S(1)}, u32[]{:S(2)}, u32[]{:S(2)}) collective-permute-start(f32[2,8,128]{2,1,0:T(8,128)S(1)} %get-tuple-element.11), channel_id=1, source_target_pairs={{0,1},{1,2},{2,3},{4,5},{5,6},{6,7},{8,9},{9,10},{10,11},{12,13},{... | collective-permute-start | bytes 24584 | tf_op jit(solution)/shard_map/ppermute | solution.py:338
  9.2 0.8 %collective-permute-done.1 = f32[2,8,128]{2,1,0:T(8,128)S(1)} collective-permute-done((f32[2,8,128]{2,1,0:T(8,128)S(1)}, f32[2,8,128]{2,1,0:T(8,128)S(1)}, u32[]{:S(2)}, u32[]{:S(2)}) %collective-permute-start.1) | collective-permute-done | bytes 8224 | tf_op jit(solution)/shard_map/ppermute | solution.py:338
  10.0 4.9 %collective-permute-start.3 = (f32[66,8,128]{2,1,0:T(8,128)S(1)}, f32[66,8,128]{2,1,0:T(8,128)S(1)}, u32[]{:S(2)}, u32[]{:S(2)}) collective-permute-start(f32[66,8,128]{2,1,0:T(8,128)S(1)} %get-tuple-element.15), channel_id=1, source_target_pairs={{0,4},{4,8},{8,12},{1,5},{5,9},{9,13},{2,6},{6,10},{10,14},{3,7},{... | collective-permute-start | bytes 811016 | tf_op jit(solution)/shard_map/ppermute | solution.py:338
  15.0 1.3 %collective-permute-start.2 = (f32[66,8,128]{2,1,0:T(8,128)S(1)}, f32[66,8,128]{2,1,0:T(8,128)S(1)}, u32[]{:S(2)}, u32[]{:S(2)}) collective-permute-start(f32[66,8,128]{2,1,0:T(8,128)S(1)} %get-tuple-element.16), channel_id=1, source_target_pairs={{4,0},{8,4},{12,8},{5,1},{9,5},{13,9},{6,2},{10,6},{14,10},{7,3},{... | collective-permute-start | bytes 811016 | tf_op jit(solution)/shard_map/ppermute | solution.py:338
  16.3 5.4 %collective-permute-done.3.from_prev = f32[66,8,128]{2,1,0:T(8,128)S(1)} collective-permute-done((f32[66,8,128]{2,1,0:T(8,128)S(1)}, f32[66,8,128]{2,1,0:T(8,128)S(1)}, u32[]{:S(2)}, u32[]{:S(2)}) %collective-permute-start.3) | collective-permute-done | bytes 270368 | tf_op jit(solution)/shard_map/ppermute | solution.py:338
  21.7 4.3 %collective-permute-done.2.from_next = f32[66,8,128]{2,1,0:T(8,128)S(1)} collective-permute-done((f32[66,8,128]{2,1,0:T(8,128)S(1)}, f32[66,8,128]{2,1,0:T(8,128)S(1)}, u32[]{:S(2)}, u32[]{:S(2)}) %collective-permute-start.2) | collective-permute-done | bytes 270368 | tf_op jit(solution)/shard_map/ppermute | solution.py:338
  26.0 13.7 %shard_map.86 = (f32[4,2,20,8,256]{4,3,2,1,0:T(8,128)S(1)}, f32[2,16,128]{2,1,0:T(8,128)S(1)}) custom-call(f32[2,20,8,256]{3,2,1,0:T(8,128)S(1)} %copy-done, f32[20,8,256]{2,1,0:T(8,128)S(1)} %copy-done.2, f32[8,256]{1,0:T(8,128)S(1)} %copy-done.3, s32[8,256]{1,0:T(8,128)S(1)} %copy-done.4, s32[8,256]{1,0:T(8,128)S(1)} %copy-done.5, ...), custom_call_target="tpu_custom_call" | custom-call | tf_op jit(solution)/shard_map/pallas_call | solution.py:375
  39.7 0.1 collective-permute-start.6
  39.8 1.6 %collective-permute-start.5 = (f32[2,16,128]{2,1,0:T(8,128)S(1)}, f32[2,16,128]{2,1,0:T(8,128)S(1)}, u32[]{:S(2)}, u32[]{:S(2)}) collective-permute-start(f32[2,16,128]{2,1,0:T(8,128)S(1)} %get-tuple-element.14.refs_0_), channel_id=1, source_target_pairs={{0,2},{1,3},{2,0},{3,1},{4,6},{5,7},{6,4},{7,5},{8,10},{9,11},{10,... | collective-permute-start | bytes 49160 | tf_op jit(solution)/shard_map/ppermute | solution.py:356
  41.3 2.2 %collective-permute-done.5.refs_2_ = f32[2,16,128]{2,1,0:T(8,128)S(1)} collective-permute-done((f32[2,16,128]{2,1,0:T(8,128)S(1)}, f32[2,16,128]{2,1,0:T(8,128)S(1)}, u32[]{:S(2)}, u32[]{:S(2)}) %collective-permute-start.5) | collective-permute-done | bytes 16416 | tf_op jit(solution)/shard_map/ppermute | solution.py:356
  43.6 0.9 %collective-permute-done.4.refs_1_ = f32[2,16,128]{2,1,0:T(8,128)S(1)} collective-permute-done((f32[2,16,128]{2,1,0:T(8,128)S(1)}, f32[2,16,128]{2,1,0:T(8,128)S(1)}, u32[]{:S(2)}, u32[]{:S(2)}) %collective-permute-start.4) | collective-permute-done | bytes 16416 | tf_op jit(solution)/shard_map/ppermute | solution.py:356
  44.5 1.6 %collective-permute-start.9 = (f32[2,16,128]{2,1,0:T(8,128)S(1)}, f32[2,16,128]{2,1,0:T(8,128)S(1)}, u32[]{:S(2)}, u32[]{:S(2)}) collective-permute-start(f32[2,16,128]{2,1,0:T(8,128)S(1)} %shard_map.87.rest_0_), channel_id=1, source_target_pairs={{0,12},{4,0},{8,4},{12,8},{1,13},{5,1},{9,5},{13,9},{2,14},{6,2},{... | collective-permute-start | bytes 49160 | tf_op jit(solution)/shard_map/ppermute | solution.py:356
  46.1 1.5 %collective-permute-start.8 = (f32[2,16,128]{2,1,0:T(8,128)S(1)}, f32[2,16,128]{2,1,0:T(8,128)S(1)}, u32[]{:S(2)}, u32[]{:S(2)}) collective-permute-start(f32[2,16,128]{2,1,0:T(8,128)S(1)} %shard_map.87.rest_0_), channel_id=1, source_target_pairs={{0,8},{4,12},{8,0},{12,4},{1,9},{5,13},{9,1},{13,5},{2,10},{6,14},... | collective-permute-start | bytes 49160 | tf_op jit(solution)/shard_map/ppermute | solution.py:356
  47.6 1.6 %collective-permute-start.7 = (f32[2,16,128]{2,1,0:T(8,128)S(1)}, f32[2,16,128]{2,1,0:T(8,128)S(1)}, u32[]{:S(2)}, u32[]{:S(2)}) collective-permute-start(f32[2,16,128]{2,1,0:T(8,128)S(1)} %shard_map.87.rest_0_), channel_id=1, source_target_pairs={{0,4},{4,8},{8,12},{12,0},{1,5},{5,9},{9,13},{13,1},{2,6},{6,10},{... | collective-permute-start | bytes 49160 | tf_op jit(solution)/shard_map/ppermute | solution.py:356
  49.2 1.7 %collective-permute-done.8.rest_2_ = f32[2,16,128]{2,1,0:T(8,128)S(1)} collective-permute-done((f32[2,16,128]{2,1,0:T(8,128)S(1)}, f32[2,16,128]{2,1,0:T(8,128)S(1)}, u32[]{:S(2)}, u32[]{:S(2)}) %collective-permute-start.8) | collective-permute-done | bytes 16416 | tf_op jit(solution)/shard_map/ppermute | solution.py:356
  50.8 2.3 %collective-permute-done.7.rest_1_ = f32[2,16,128]{2,1,0:T(8,128)S(1)} collective-permute-done((f32[2,16,128]{2,1,0:T(8,128)S(1)}, f32[2,16,128]{2,1,0:T(8,128)S(1)}, u32[]{:S(2)}, u32[]{:S(2)}) %collective-permute-start.7) | collective-permute-done | bytes 16416 | tf_op jit(solution)/shard_map/ppermute | solution.py:356
  53.1 1.6 %shard_map.88 = (f32[2,20,8,256]{3,2,1,0:T(8,128)}, f32[2,20,8,256]{3,2,1,0:T(8,128)}, f32[8,256]{1,0:T(8,128)}) custom-call(f32[2,20,8,256]{3,2,1,0:T(8,128)S(1)} %copy-done.1, f32[4,2,20,8,256]{4,3,2,1,0:T(8,128)S(1)} %get-tuple-element.13.powers, f32[8,256]{1,0:T(8,128)S(1)} %copy-done.3, s32[8,256]{1,0:T(8,128)S(1)} %copy-done.4, ...), custom_call_target="tpu_custom_call" | custom-call | tf_op jit(solution)/shard_map/pallas_call | solution.py:385
  (16 shorter events, 0.1 us)
Async XLA Ops:
  0.6 1.0 %copy-start = (f32[2,20,8,256]{3,2,1,0:T(8,128)S(1)}, f32[2,20,8,256]{3,2,1,0:T(8,128)}, u32[]{:S(2)}) copy-start(f32[2,20,8,256]{3,2,1,0:T(8,128)} %rhs.5) | copy-start | bytes 983044
  1.6 0.9 %copy-start.2 = (f32[20,8,256]{2,1,0:T(8,128)S(1)}, f32[20,8,256]{2,1,0:T(8,128)}, u32[]{:S(2)}) copy-start(f32[20,8,256]{2,1,0:T(8,128)} %eta.3) | copy-start | bytes 491524
  2.5 0.7 %copy-start.3 = (f32[8,256]{1,0:T(8,128)S(1)}, f32[8,256]{1,0:T(8,128)}, u32[]{:S(2)}) copy-start(f32[8,256]{1,0:T(8,128)} %friction.5) | copy-start | bytes 24580
  3.2 0.7 %copy-start.4 = (s32[8,256]{1,0:T(8,128)S(1)}, s32[8,256]{1,0:T(8,128)}, u32[]{:S(2)}) copy-start(s32[8,256]{1,0:T(8,128)} %ice.5) | copy-start | bytes 24580
  3.9 0.7 %copy-start.5 = (s32[8,256]{1,0:T(8,128)S(1)}, s32[8,256]{1,0:T(8,128)}, u32[]{:S(2)}) copy-start(s32[8,256]{1,0:T(8,128)} %grounded.5) | copy-start | bytes 24580
  4.6 48.5 %copy-start.1 = (f32[2,20,8,256]{3,2,1,0:T(8,128)S(1)}, f32[2,20,8,256]{3,2,1,0:T(8,128)}, u32[]{:S(2)}) copy-start(f32[2,20,8,256]{3,2,1,0:T(8,128)} %rhs.5) | copy-start | bytes 983044
  4.6 48.5 %copy-start.6 = (f32[2,8,256]{2,1,0:T(8,128)S(1)}, f32[2,8,256]{2,1,0:T(8,128)}, u32[]{:S(2)}) copy-start(f32[2,8,256]{2,1,0:T(8,128)} %speed.1) | copy-start | bytes 49156
  4.8 4.3 %collective-permute-start = (f32[2,8,128]{2,1,0:T(8,128)S(1)}, f32[2,8,128]{2,1,0:T(8,128)S(1)}, u32[]{:S(2)}, u32[]{:S(2)}) collective-permute-start(f32[2,8,128]{2,1,0:T(8,128)S(1)} %get-tuple-element.10), channel_id=1, source_target_pairs={{1,0},{2,1},{3,2},{5,4},{6,5},{7,6},{9,8},{10,9},{11,10},{13,12},{... | collective-permute-start | bytes 24584 | tf_op jit(solution)/shard_map/ppermute | solution.py:338
  6.1 3.8 %collective-permute-start.1 = (f32[2,8,128]{2,1,0:T(8,128)S(1)}, f32[2,8,128]{2,1,0:T(8,128)S(1)}, u32[]{:S(2)}, u32[]{:S(2)}) collective-permute-start(f32[2,8,128]{2,1,0:T(8,128)S(1)} %get-tuple-element.11), channel_id=1, source_target_pairs={{0,1},{1,2},{2,3},{4,5},{5,6},{6,7},{8,9},{9,10},{10,11},{12,13},{... | collective-permute-start | bytes 24584 | tf_op jit(solution)/shard_map/ppermute | solution.py:338
  10.0 11.7 %collective-permute-start.3 = (f32[66,8,128]{2,1,0:T(8,128)S(1)}, f32[66,8,128]{2,1,0:T(8,128)S(1)}, u32[]{:S(2)}, u32[]{:S(2)}) collective-permute-start(f32[66,8,128]{2,1,0:T(8,128)S(1)} %get-tuple-element.15), channel_id=1, source_target_pairs={{0,4},{4,8},{8,12},{1,5},{5,9},{9,13},{2,6},{6,10},{10,14},{3,7},{... | collective-permute-start | bytes 811016 | tf_op jit(solution)/shard_map/ppermute | solution.py:338
  15.0 11.1 %collective-permute-start.2 = (f32[66,8,128]{2,1,0:T(8,128)S(1)}, f32[66,8,128]{2,1,0:T(8,128)S(1)}, u32[]{:S(2)}, u32[]{:S(2)}) collective-permute-start(f32[66,8,128]{2,1,0:T(8,128)S(1)} %get-tuple-element.16), channel_id=1, source_target_pairs={{4,0},{8,4},{12,8},{5,1},{9,5},{13,9},{6,2},{10,6},{14,10},{7,3},{... | collective-permute-start | bytes 811016 | tf_op jit(solution)/shard_map/ppermute | solution.py:338
  39.7 1.6 %collective-permute-start.6 = (f32[2,16,128]{2,1,0:T(8,128)S(1)}, f32[2,16,128]{2,1,0:T(8,128)S(1)}, u32[]{:S(2)}, u32[]{:S(2)}) collective-permute-start(f32[2,16,128]{2,1,0:T(8,128)S(1)} %get-tuple-element.14.refs_0_), channel_id=1, source_target_pairs={{0,3},{1,0},{2,1},{3,2},{4,7},{5,4},{6,5},{7,6},{8,11},{9,8},{10,9... | collective-permute-start | bytes 49160 | tf_op jit(solution)/shard_map/ppermute | solution.py:356
  39.8 3.8 %collective-permute-start.5 = (f32[2,16,128]{2,1,0:T(8,128)S(1)}, f32[2,16,128]{2,1,0:T(8,128)S(1)}, u32[]{:S(2)}, u32[]{:S(2)}) collective-permute-start(f32[2,16,128]{2,1,0:T(8,128)S(1)} %get-tuple-element.14.refs_0_), channel_id=1, source_target_pairs={{0,2},{1,3},{2,0},{3,1},{4,6},{5,7},{6,4},{7,5},{8,10},{9,11},{10,... | collective-permute-start | bytes 49160 | tf_op jit(solution)/shard_map/ppermute | solution.py:356
  41.3 3.2 %collective-permute-start.4 = (f32[2,16,128]{2,1,0:T(8,128)S(1)}, f32[2,16,128]{2,1,0:T(8,128)S(1)}, u32[]{:S(2)}, u32[]{:S(2)}) collective-permute-start(f32[2,16,128]{2,1,0:T(8,128)S(1)} %get-tuple-element.14.refs_0_), channel_id=1, source_target_pairs={{0,1},{1,2},{2,3},{3,0},{4,5},{5,6},{6,7},{7,4},{8,9},{9,10},{10,1... | collective-permute-start | bytes 49160 | tf_op jit(solution)/shard_map/ppermute | solution.py:356
  44.5 4.7 %collective-permute-start.9 = (f32[2,16,128]{2,1,0:T(8,128)S(1)}, f32[2,16,128]{2,1,0:T(8,128)S(1)}, u32[]{:S(2)}, u32[]{:S(2)}) collective-permute-start(f32[2,16,128]{2,1,0:T(8,128)S(1)} %shard_map.87.rest_0_), channel_id=1, source_target_pairs={{0,12},{4,0},{8,4},{12,8},{1,13},{5,1},{9,5},{13,9},{2,14},{6,2},{... | collective-permute-start | bytes 49160 | tf_op jit(solution)/shard_map/ppermute | solution.py:356
  46.1 4.7 %collective-permute-start.8 = (f32[2,16,128]{2,1,0:T(8,128)S(1)}, f32[2,16,128]{2,1,0:T(8,128)S(1)}, u32[]{:S(2)}, u32[]{:S(2)}) collective-permute-start(f32[2,16,128]{2,1,0:T(8,128)S(1)} %shard_map.87.rest_0_), channel_id=1, source_target_pairs={{0,8},{4,12},{8,0},{12,4},{1,9},{5,13},{9,1},{13,5},{2,10},{6,14},... | collective-permute-start | bytes 49160 | tf_op jit(solution)/shard_map/ppermute | solution.py:356
  47.6 5.5 %collective-permute-start.7 = (f32[2,16,128]{2,1,0:T(8,128)S(1)}, f32[2,16,128]{2,1,0:T(8,128)S(1)}, u32[]{:S(2)}, u32[]{:S(2)}) collective-permute-start(f32[2,16,128]{2,1,0:T(8,128)S(1)} %shard_map.87.rest_0_), channel_id=1, source_target_pairs={{0,4},{4,8},{8,12},{12,0},{1,5},{5,9},{9,13},{13,1},{2,6},{6,10},{... | collective-permute-start | bytes 49160 | tf_op jit(solution)/shard_map/ppermute | solution.py:356

commit v2 on v1

--- a/solution.py
+++ b/solution.py
@@ -11,15 +11,17 @@
 HALO = 4
 ROWS = 8
 LANES = 128
+UNROLL = 4
 VMEM = pltpu.CompilerParams(vmem_limit_bytes=40 * 1024 * 1024)
 
 
-def call(kernel, outs, scratch=()):
+def call(kernel, outs, scratch=(), **more):
     return pl.pallas_call(
         kernel,
-        out_shape=[jax.ShapeDtypeStruct(s, jnp.float32) for s in outs],
-        scratch_shapes=[pltpu.VMEM(s, jnp.float32) for s in scratch],
+        out_shape=[jax.ShapeDtypeStruct(s, jnp.float32) if isinstance(s, tuple) else s for s in outs],
+        scratch_shapes=[pltpu.VMEM(s, jnp.float32) if isinstance(s, tuple) else s for s in scratch],
         compiler_params=VMEM,
+        **more,
     )
 
 
@@ -46,7 +48,14 @@
     return 3 * layers, 3 * layers + 1
 
 
-def pack_kernel(rhs, eta, friction, ice, grounded, to_left, to_right, to_prev, to_next):
+def pack_kernel(*refs):
+    sources, held, (to_left, to_right, to_prev, to_next, arrived) = refs[:6], refs[6:12], refs[12:]
+    copies = [pltpu.make_async_copy(a, b, arrived.at[i]) for i, (a, b) in enumerate(zip(sources, held))]
+    for copy in copies:
+        copy.start()
+    for copy in copies:
+        copy.wait()
+    rhs, eta, friction, ice, grounded, _ = held
     layers = eta.shape[0]
     plane = own_planes(rhs, eta, friction, ice, grounded)
     lane = lax.broadcasted_iota(jnp.int32, (ROWS, LANES), 1)
@@ -102,7 +111,7 @@
 
 
 def power_kernel(
-    rhs, eta, friction, ice, grounded, from_next, from_prev, columns,
+    rhs, eta, friction, ice, grounded, from_next, from_prev, columns, next_columns, prev_columns,
     powers, moments,
     field_a, field_b, eta_row, eta_col, eta_half, eta_up, cover, drag,
 ):
@@ -111,8 +120,8 @@
     lane = lax.broadcasted_iota(jnp.int32, (ROWS, LANES), 1)
     row = lax.broadcasted_iota(jnp.int32, (ROWS, LANES), 0)
     upper = row < HALO
-    strips = from_next.shape[0] - 4
-    corner = [jnp.where(upper, from_next[strips + t], from_prev[strips + t]) for t in range(4)]
+    strips = from_next.shape[0]
+    corner = [jnp.where(upper, next_columns[t], prev_columns[t]) for t in range(4)]
     beside = [columns[t] for t in range(4)]
 
     def side(tiles, p):
@@ -203,7 +212,13 @@
         zero = jnp.zeros((ROWS, 2 * LANES), jnp.float32)
         d = drag[...]
         start = (-d * src[0, 0], -d * src[1, 0], zero, zero)
-        return lax.fori_loop(0, layers, layer, start)[2:]
+
+        def block(b, carry):
+            for i in range(UNROLL):
+                carry = layer(b * UNROLL + i, carry)
+            return carry
+
+        return lax.fori_loop(0, layers // UNROLL, block, start)[2:]
 
     square = jnp.zeros((ROWS, 2 * LANES), jnp.float32)
     for c in range(2):
@@ -362,28 +377,36 @@
 
 def body(adjoint_rhs, viscosity, friction, ice_mask, grounded, basal_velocity):
     layers = viscosity.shape[0]
-    fields = (adjoint_rhs, viscosity, friction, ice_mask, grounded)
+    inputs = (adjoint_rhs, viscosity, friction, ice_mask, grounded, basal_velocity)
     tile = (ROWS, LANES)
     strips = (2 * (layers + layers // 2 + 1),) + tile
-    to_left, to_right, to_prev, to_next = call(pack_kernel, [(2,) + tile, (2,) + tile, strips, strips])(*fields)
+    *held, to_left, to_right, to_prev, to_next = call(
+        pack_kernel,
+        [jax.ShapeDtypeStruct(x.shape, x.dtype) for x in inputs] + [(2,) + tile, (2,) + tile, strips, strips],
+        [pltpu.SemaphoreType.DMA((len(inputs),))],
+        in_specs=[pl.BlockSpec(memory_space=pltpu.HBM)] * len(inputs),
+    )(*inputs)
+    rhs, eta, friction, ice_mask, grounded, speed = held
+    from_next = shifted(to_prev, "gx", -1)
+    from_prev = shifted(to_next, "gx", 1)
     columns = jnp.concatenate(
         [shifted(to_left, ("gy", "gz"), -1), shifted(to_right, ("gy", "gz"), 1)], axis=0
     )
-    from_next = shifted(jnp.concatenate([to_prev, columns], axis=0), "gx", -1)
-    from_prev = shifted(jnp.concatenate([to_next, columns], axis=0), "gx", 1)
+    next_columns = shifted(columns, "gx", -1)
+    prev_columns = shifted(columns, "gx", 1)
     block = (layers, 2 * ROWS, 3 * LANES)
     powers, sums = call(
         power_kernel,
         [(STEPS,) + adjoint_rhs.shape, (2, 2 * ROWS, LANES)],
         [(2,) + block] * 2 + [block] * 4 + [block[1:]] * 2,
-    )(*fields, from_next, from_prev, columns)
+    )(*held[:5], from_next, from_prev, columns, next_columns, prev_columns)
     parts = exchange(sums, ("gy", "gz"))
     if len(parts) > 1:
         sums = call(add_kernel, [sums.shape])(*parts)[0]
     parts = exchange(sums, "gx")
     return tuple(
         call(final_kernel, [adjoint_rhs.shape, adjoint_rhs.shape, friction.shape])(
-            adjoint_rhs, powers, friction, ice_mask, grounded, basal_velocity, *parts
+            rhs, powers, friction, ice_mask, grounded, speed, *parts
         )
     )
 

time: 55.1 us -> 51.3 us (0.931)
  Pallas kernels: 15.5 us -> 8.68 us
  starting transfers between devices: 16.8 us -> 23 us
  waiting for transfers between devices: 17.7 us -> 13.6 us
  local copies, waits for them, and re-layouts: 3.98 us -> 4.69 us
    pallas_call x1, Pallas kernels: 13.7 us -> 6.43 us  [body(): call(power_kernel, [(STEPS,) + adjoint_rhs.shape, (2, 2 * ROWS, LANES)],...]
    ppermute x4 -> x6, starting transfers between devices: 10.6 us -> 16.4 us  [shifted(): return lax.ppermute(x, axis, pairs)]
    ppermute x4 -> x6, waiting for transfers between devices: 10.6 us -> 5.13 us  [shifted(): return lax.ppermute(x, axis, pairs)]
    ppermute x6, waiting for transfers between devices: 7.12 us -> 8.52 us  [exchange(): parts.append(lax.ppermute(x, axis, pairs))]
    unnamed x14 -> x13, local copies, waits for them, and re-layouts: 3.98 us -> 4.69 us
  transfers between devices with their start and end apart: 10 -> 12, of which waited for: 7 -> 8; matrix products, arithmetic and copies ran while one was open for 0% -> 0% of each run, Pallas kernels for 0% -> 0%
where the time goes in v2:
time: 51.3 us; the launch traced here: 50.8 us
  starting transfers between devices  23 us (45%)
  waiting for transfers between devices  13.6 us (27%)
  Pallas kernels  8.68 us (17%)
  local copies, waits for them, and re-layouts  4.69 us (9%)
  between operations  0.74 us (1%)
    ppermute x6, starting transfers between devices, shifted(): return lax.ppermute(x, axis, pairs)  16.4 us
    ppermute x6, waiting for transfers between devices, exchange(): parts.append(lax.ppermute(x, axis, pairs))  8.52 us
    ppermute x6, starting transfers between devices, exchange(): parts.append(lax.ppermute(x, axis, pairs))  6.64 us
    pallas_call x1, Pallas kernels, body(): call(power_kernel, [(STEPS,) + adjoint_rhs.shape, (2, 2 * ROWS, LANES)],...  6.43 us
    ppermute x6, waiting for transfers between devices, shifted(): return lax.ppermute(x, axis, pairs)  5.13 us
    unnamed x13, local copies, waits for them, and re-layouts  4.69 us
    pallas_call x1, Pallas kernels, body(): call(final_kernel, [adjoint_rhs.shape, adjoint_rhs.shape, friction.shape])  1.6 us
  transfers between devices with their start and end apart: 12, of which 8 were waited for; matrix products, arithmetic and copies ran while one was open for 0% of the time, Pallas kernels for 0%

profile of v2, /device:TPU:0, one launch (start us, length us, event | category | flops | bytes accessed | tf_op | source)
XLA Modules:
  0.0 50.8 jit_solution(12723018818613003693)
XLA Ops:
  0.6 1.0 %copy-done = f32[2,20,8,256]{3,2,1,0:T(8,128)S(1)} copy-done((f32[2,20,8,256]{3,2,1,0:T(8,128)S(1)}, f32[2,20,8,256]{3,2,1,0:T(8,128)}, u32[]{:S(2)}) %copy-start) | copy-done | bytes 327704
  1.6 0.9 %copy-done.1 = f32[20,8,256]{2,1,0:T(8,128)S(1)} copy-done((f32[20,8,256]{2,1,0:T(8,128)S(1)}, f32[20,8,256]{2,1,0:T(8,128)}, u32[]{:S(2)}) %copy-start.1) | copy-done | bytes 163864
  2.5 0.7 %copy-done.2 = f32[2,8,256]{2,1,0:T(8,128)S(1)} copy-done((f32[2,8,256]{2,1,0:T(8,128)S(1)}, f32[2,8,256]{2,1,0:T(8,128)}, u32[]{:S(2)}) %copy-start.2) | copy-done | bytes 16408
  3.2 0.7 %copy-done.3 = f32[8,256]{1,0:T(8,128)S(1)} copy-done((f32[8,256]{1,0:T(8,128)S(1)}, f32[8,256]{1,0:T(8,128)}, u32[]{:S(2)}) %copy-start.3) | copy-done | bytes 8216
  3.9 0.7 %copy-done.4 = s32[8,256]{1,0:T(8,128)S(1)} copy-done((s32[8,256]{1,0:T(8,128)S(1)}, s32[8,256]{1,0:T(8,128)}, u32[]{:S(2)}) %copy-start.4) | copy-done | bytes 8216
  4.6 0.7 %copy-done.5 = s32[8,256]{1,0:T(8,128)S(1)} copy-done((s32[8,256]{1,0:T(8,128)S(1)}, s32[8,256]{1,0:T(8,128)}, u32[]{:S(2)}) %copy-start.5) | copy-done | bytes 8216
  5.3 0.6 %shard_map.85 = (f32[2,20,8,256]{3,2,1,0:T(8,128)S(1)}, f32[20,8,256]{2,1,0:T(8,128)S(1)}, f32[8,256]{1,0:T(8,128)S(1)}, s32[8,256]{1,0:T(8,128)S(1)}, s32[8,256...) custom-call(f32[2,20,8,256]{3,2,1,0:T(8,128)S(1)} %copy-done, ...), custom_call_target="tpu_custom_call" | custom-call | tf_op jit(solution)/shard_map/pallas_call | solution.py:383
  6.0 1.3 %collective-permute-start = (f32[62,8,128]{2,1,0:T(8,128)S(1)}, f32[62,8,128]{2,1,0:T(8,128)S(1)}, u32[]{:S(2)}, u32[]{:S(2)}) collective-permute-start(f32[62,8,128]{2,1,0:T(8,128)S(1)} %get-tuple-element.20), channel_id=1, source_target_pairs={{4,0},{8,4},{12,8},{5,1},{9,5},{13,9},{6,2},{10,6},{14,10},{7,3},{... | collective-permute-start | bytes 761864 | tf_op jit(solution)/shard_map/ppermute | solution.py:353
  7.3 5.6 %collective-permute-start.1 = (f32[62,8,128]{2,1,0:T(8,128)S(1)}, f32[62,8,128]{2,1,0:T(8,128)S(1)}, u32[]{:S(2)}, u32[]{:S(2)}) collective-permute-start(f32[62,8,128]{2,1,0:T(8,128)S(1)} %get-tuple-element.21), channel_id=1, source_target_pairs={{0,4},{4,8},{8,12},{1,5},{5,9},{9,13},{2,6},{6,10},{10,14},{3,7},{... | collective-permute-start | bytes 761864 | tf_op jit(solution)/shard_map/ppermute | solution.py:353
  12.8 1.3 %collective-permute-start.2 = (f32[2,8,128]{2,1,0:T(8,128)S(1)}, f32[2,8,128]{2,1,0:T(8,128)S(1)}, u32[]{:S(2)}, u32[]{:S(2)}) collective-permute-start(f32[2,8,128]{2,1,0:T(8,128)S(1)} %get-tuple-element.22), channel_id=1, source_target_pairs={{1,0},{2,1},{3,2},{5,4},{6,5},{7,6},{9,8},{10,9},{11,10},{13,12},{... | collective-permute-start | bytes 24584 | tf_op jit(solution)/shard_map/ppermute | solution.py:353
  14.1 3.0 %collective-permute-start.3 = (f32[2,8,128]{2,1,0:T(8,128)S(1)}, f32[2,8,128]{2,1,0:T(8,128)S(1)}, u32[]{:S(2)}, u32[]{:S(2)}) collective-permute-start(f32[2,8,128]{2,1,0:T(8,128)S(1)} %get-tuple-element.23), channel_id=1, source_target_pairs={{0,1},{1,2},{2,3},{4,5},{5,6},{6,7},{8,9},{9,10},{10,11},{12,13},{... | collective-permute-start | bytes 24584 | tf_op jit(solution)/shard_map/ppermute | solution.py:353
  17.2 0.8 %collective-permute-done.3 = f32[2,8,128]{2,1,0:T(8,128)S(1)} collective-permute-done((f32[2,8,128]{2,1,0:T(8,128)S(1)}, f32[2,8,128]{2,1,0:T(8,128)S(1)}, u32[]{:S(2)}, u32[]{:S(2)}) %collective-permute-start.3) | collective-permute-done | bytes 8224 | tf_op jit(solution)/shard_map/ppermute | solution.py:353
  18.0 3.9 %collective-permute-start.5 = (f32[4,8,128]{2,1,0:T(8,128)S(1)}, f32[4,8,128]{2,1,0:T(8,128)S(1)}, u32[]{:S(2)}, u32[]{:S(2)}) collective-permute-start(f32[4,8,128]{2,1,0:T(8,128)S(1)} %constant_dynamic-update-slice_fusion.columns), channel_id=1, source_target_pairs={{0,4},{4,8},{8,12},{1,5},{5,9},{9,13},{2,6},{6,10},{10,14},{3,7},{... | collective-permute-start | bytes 49160 | tf_op jit(solution)/shard_map/ppermute | solution.py:353
  21.9 1.3 %collective-permute-start.4 = (f32[4,8,128]{2,1,0:T(8,128)S(1)}, f32[4,8,128]{2,1,0:T(8,128)S(1)}, u32[]{:S(2)}, u32[]{:S(2)}) collective-permute-start(f32[4,8,128]{2,1,0:T(8,128)S(1)} %constant_dynamic-update-slice_fusion.columns), channel_id=1, source_target_pairs={{4,0},{8,4},{12,8},{5,1},{9,5},{13,9},{6,2},{10,6},{14,10},{7,3},{... | collective-permute-start | bytes 49160 | tf_op jit(solution)/shard_map/ppermute | solution.py:353
  23.3 4.2 %collective-permute-done.4.next_columns = f32[4,8,128]{2,1,0:T(8,128)S(1)} collective-permute-done((f32[4,8,128]{2,1,0:T(8,128)S(1)}, f32[4,8,128]{2,1,0:T(8,128)S(1)}, u32[]{:S(2)}, u32[]{:S(2)}) %collective-permute-start.4) | collective-permute-done | bytes 16416 | tf_op jit(solution)/shard_map/ppermute | solution.py:353
  27.5 6.4 %shard_map.86 = (f32[4,2,20,8,256]{4,3,2,1,0:T(8,128)S(1)}, f32[2,16,128]{2,1,0:T(8,128)S(1)}) custom-call(f32[2,20,8,256]{3,2,1,0:T(8,128)S(1)} %get-tuple-element.15.rhs, f32[20,8,256]{2,1,0:T(8,128)S(1)} %get-tuple-element.16.eta, f32[8,256]{1,0:T(8,128)S(1)} %get-tuple-element.17.friction, s32[8,256]{1,0:T(8,128)S(1)} %get-tuple-element.18.ice, ...), custom_call_target="tpu_custom_call" | custom-call | tf_op jit(solution)/shard_map/pallas_call | solution.py:398
  34.0 3.3 %collective-permute-start.7 = (f32[2,16,128]{2,1,0:T(8,128)S(1)}, f32[2,16,128]{2,1,0:T(8,128)S(1)}, u32[]{:S(2)}, u32[]{:S(2)}) collective-permute-start(f32[2,16,128]{2,1,0:T(8,128)S(1)} %get-tuple-element.26.refs_0_), channel_id=1, source_target_pairs={{0,2},{1,3},{2,0},{3,1},{4,6},{5,7},{6,4},{7,5},{8,10},{9,11},{10,... | collective-permute-start | bytes 49160 | tf_op jit(solution)/shard_map/ppermute | solution.py:371
  37.5 1.6 %collective-permute-done.7.refs_2_ = f32[2,16,128]{2,1,0:T(8,128)S(1)} collective-permute-done((f32[2,16,128]{2,1,0:T(8,128)S(1)}, f32[2,16,128]{2,1,0:T(8,128)S(1)}, u32[]{:S(2)}, u32[]{:S(2)}) %collective-permute-start.7) | collective-permute-done | bytes 16416 | tf_op jit(solution)/shard_map/ppermute | solution.py:371
  39.2 1.3 %collective-permute-done.6.refs_1_ = f32[2,16,128]{2,1,0:T(8,128)S(1)} collective-permute-done((f32[2,16,128]{2,1,0:T(8,128)S(1)}, f32[2,16,128]{2,1,0:T(8,128)S(1)}, u32[]{:S(2)}, u32[]{:S(2)}) %collective-permute-start.6) | collective-permute-done | bytes 16416 | tf_op jit(solution)/shard_map/ppermute | solution.py:371
  40.8 2.8 %collective-permute-start.10 = (f32[2,16,128]{2,1,0:T(8,128)S(1)}, f32[2,16,128]{2,1,0:T(8,128)S(1)}, u32[]{:S(2)}, u32[]{:S(2)}) collective-permute-start(f32[2,16,128]{2,1,0:T(8,128)S(1)} %shard_map.87.rest_0_), channel_id=1, source_target_pairs={{0,8},{4,12},{8,0},{12,4},{1,9},{5,13},{9,1},{13,5},{2,10},{6,14},... | collective-permute-start | bytes 49160 | tf_op jit(solution)/shard_map/ppermute | solution.py:371
  43.6 0.7 %collective-permute-done.11.rest_3_ = f32[2,16,128]{2,1,0:T(8,128)S(1)} collective-permute-done((f32[2,16,128]{2,1,0:T(8,128)S(1)}, f32[2,16,128]{2,1,0:T(8,128)S(1)}, u32[]{:S(2)}, u32[]{:S(2)}) %collective-permute-start.11) | collective-permute-done | bytes 16416 | tf_op jit(solution)/shard_map/ppermute | solution.py:371
  44.3 1.2 %collective-permute-done.10.rest_2_ = f32[2,16,128]{2,1,0:T(8,128)S(1)} collective-permute-done((f32[2,16,128]{2,1,0:T(8,128)S(1)}, f32[2,16,128]{2,1,0:T(8,128)S(1)}, u32[]{:S(2)}, u32[]{:S(2)}) %collective-permute-start.10) | collective-permute-done | bytes 16416 | tf_op jit(solution)/shard_map/ppermute | solution.py:371
  45.5 3.6 %collective-permute-done.9.rest_1_ = f32[2,16,128]{2,1,0:T(8,128)S(1)} collective-permute-done((f32[2,16,128]{2,1,0:T(8,128)S(1)}, f32[2,16,128]{2,1,0:T(8,128)S(1)}, u32[]{:S(2)}, u32[]{:S(2)}) %collective-permute-start.9) | collective-permute-done | bytes 16416 | tf_op jit(solution)/shard_map/ppermute | solution.py:371
  49.2 1.6 %shard_map.88 = (f32[2,20,8,256]{3,2,1,0:T(8,128)}, f32[2,20,8,256]{3,2,1,0:T(8,128)}, f32[8,256]{1,0:T(8,128)}) custom-call(f32[2,20,8,256]{3,2,1,0:T(8,128)S(1)} %get-tuple-element.15.rhs, f32[4,2,20,8,256]{4,3,2,1,0:T(8,128)S(1)} %get-tuple-element.24.powers, f32[8,256]{1,0:T(8,128)S(1)} %get-tuple-element.17.friction, ...), custom_call_target="tpu_custom_call" | custom-call | tf_op jit(solution)/shard_map/pallas_call | solution.py:408
  (18 shorter events, 0.7 us)
Async XLA Ops:
  0.6 1.0 %copy-start = (f32[2,20,8,256]{3,2,1,0:T(8,128)S(1)}, f32[2,20,8,256]{3,2,1,0:T(8,128)}, u32[]{:S(2)}) copy-start(f32[2,20,8,256]{3,2,1,0:T(8,128)} %refs_0_.1) | copy-start | bytes 983044
  1.6 0.9 %copy-start.1 = (f32[20,8,256]{2,1,0:T(8,128)S(1)}, f32[20,8,256]{2,1,0:T(8,128)}, u32[]{:S(2)}) copy-start(f32[20,8,256]{2,1,0:T(8,128)} %refs_1_.1) | copy-start | bytes 491524
  2.5 0.7 %copy-start.2 = (f32[2,8,256]{2,1,0:T(8,128)S(1)}, f32[2,8,256]{2,1,0:T(8,128)}, u32[]{:S(2)}) copy-start(f32[2,8,256]{2,1,0:T(8,128)} %refs_5_.1) | copy-start | bytes 49156
  3.2 0.7 %copy-start.3 = (f32[8,256]{1,0:T(8,128)S(1)}, f32[8,256]{1,0:T(8,128)}, u32[]{:S(2)}) copy-start(f32[8,256]{1,0:T(8,128)} %refs_2_.1) | copy-start | bytes 24580
  3.9 0.7 %copy-start.4 = (s32[8,256]{1,0:T(8,128)S(1)}, s32[8,256]{1,0:T(8,128)}, u32[]{:S(2)}) copy-start(s32[8,256]{1,0:T(8,128)} %refs_3_.1) | copy-start | bytes 24580
  4.6 0.7 %copy-start.5 = (s32[8,256]{1,0:T(8,128)S(1)}, s32[8,256]{1,0:T(8,128)}, u32[]{:S(2)}) copy-start(s32[8,256]{1,0:T(8,128)} %refs_4_.1) | copy-start | bytes 24580
  6.0 21.6 %collective-permute-start = (f32[62,8,128]{2,1,0:T(8,128)S(1)}, f32[62,8,128]{2,1,0:T(8,128)S(1)}, u32[]{:S(2)}, u32[]{:S(2)}) collective-permute-start(f32[62,8,128]{2,1,0:T(8,128)S(1)} %get-tuple-element.20), channel_id=1, source_target_pairs={{4,0},{8,4},{12,8},{5,1},{9,5},{13,9},{6,2},{10,6},{14,10},{7,3},{... | collective-permute-start | bytes 761864 | tf_op jit(solution)/shard_map/ppermute | solution.py:353
  7.3 20.3 %collective-permute-start.1 = (f32[62,8,128]{2,1,0:T(8,128)S(1)}, f32[62,8,128]{2,1,0:T(8,128)S(1)}, u32[]{:S(2)}, u32[]{:S(2)}) collective-permute-start(f32[62,8,128]{2,1,0:T(8,128)S(1)} %get-tuple-element.21), channel_id=1, source_target_pairs={{0,4},{4,8},{8,12},{1,5},{5,9},{9,13},{2,6},{6,10},{10,14},{3,7},{... | collective-permute-start | bytes 761864 | tf_op jit(solution)/shard_map/ppermute | solution.py:353
  12.8 4.3 %collective-permute-start.2 = (f32[2,8,128]{2,1,0:T(8,128)S(1)}, f32[2,8,128]{2,1,0:T(8,128)S(1)}, u32[]{:S(2)}, u32[]{:S(2)}) collective-permute-start(f32[2,8,128]{2,1,0:T(8,128)S(1)} %get-tuple-element.22), channel_id=1, source_target_pairs={{1,0},{2,1},{3,2},{5,4},{6,5},{7,6},{9,8},{10,9},{11,10},{13,12},{... | collective-permute-start | bytes 24584 | tf_op jit(solution)/shard_map/ppermute | solution.py:353
  14.1 3.8 %collective-permute-start.3 = (f32[2,8,128]{2,1,0:T(8,128)S(1)}, f32[2,8,128]{2,1,0:T(8,128)S(1)}, u32[]{:S(2)}, u32[]{:S(2)}) collective-permute-start(f32[2,8,128]{2,1,0:T(8,128)S(1)} %get-tuple-element.23), channel_id=1, source_target_pairs={{0,1},{1,2},{2,3},{4,5},{5,6},{6,7},{8,9},{9,10},{10,11},{12,13},{... | collective-permute-start | bytes 24584 | tf_op jit(solution)/shard_map/ppermute | solution.py:353
  18.0 5.3 %collective-permute-start.5 = (f32[4,8,128]{2,1,0:T(8,128)S(1)}, f32[4,8,128]{2,1,0:T(8,128)S(1)}, u32[]{:S(2)}, u32[]{:S(2)}) collective-permute-start(f32[4,8,128]{2,1,0:T(8,128)S(1)} %constant_dynamic-update-slice_fusion.columns), channel_id=1, source_target_pairs={{0,4},{4,8},{8,12},{1,5},{5,9},{9,13},{2,6},{6,10},{10,14},{3,7},{... | collective-permute-start | bytes 49160 | tf_op jit(solution)/shard_map/ppermute | solution.py:353
  21.9 5.6 %collective-permute-start.4 = (f32[4,8,128]{2,1,0:T(8,128)S(1)}, f32[4,8,128]{2,1,0:T(8,128)S(1)}, u32[]{:S(2)}, u32[]{:S(2)}) collective-permute-start(f32[4,8,128]{2,1,0:T(8,128)S(1)} %constant_dynamic-update-slice_fusion.columns), channel_id=1, source_target_pairs={{4,0},{8,4},{12,8},{5,1},{9,5},{13,9},{6,2},{10,6},{14,10},{7,3},{... | collective-permute-start | bytes 49160 | tf_op jit(solution)/shard_map/ppermute | solution.py:353
  34.0 3.5 %collective-permute-start.8 = (f32[2,16,128]{2,1,0:T(8,128)S(1)}, f32[2,16,128]{2,1,0:T(8,128)S(1)}, u32[]{:S(2)}, u32[]{:S(2)}) collective-permute-start(f32[2,16,128]{2,1,0:T(8,128)S(1)} %get-tuple-element.26.refs_0_), channel_id=1, source_target_pairs={{0,3},{1,0},{2,1},{3,2},{4,7},{5,4},{6,5},{7,6},{8,11},{9,8},{10,9... | collective-permute-start | bytes 49160 | tf_op jit(solution)/shard_map/ppermute | solution.py:371
  34.0 5.1 %collective-permute-start.7 = (f32[2,16,128]{2,1,0:T(8,128)S(1)}, f32[2,16,128]{2,1,0:T(8,128)S(1)}, u32[]{:S(2)}, u32[]{:S(2)}) collective-permute-start(f32[2,16,128]{2,1,0:T(8,128)S(1)} %get-tuple-element.26.refs_0_), channel_id=1, source_target_pairs={{0,2},{1,3},{2,0},{3,1},{4,6},{5,7},{6,4},{7,5},{8,10},{9,11},{10,... | collective-permute-start | bytes 49160 | tf_op jit(solution)/shard_map/ppermute | solution.py:371
  37.3 3.2 %collective-permute-start.6 = (f32[2,16,128]{2,1,0:T(8,128)S(1)}, f32[2,16,128]{2,1,0:T(8,128)S(1)}, u32[]{:S(2)}, u32[]{:S(2)}) collective-permute-start(f32[2,16,128]{2,1,0:T(8,128)S(1)} %get-tuple-element.26.refs_0_), channel_id=1, source_target_pairs={{0,1},{1,2},{2,3},{3,0},{4,5},{5,6},{6,7},{7,4},{8,9},{9,10},{10,1... | collective-permute-start | bytes 49160 | tf_op jit(solution)/shard_map/ppermute | solution.py:371
  40.5 3.8 %collective-permute-start.11 = (f32[2,16,128]{2,1,0:T(8,128)S(1)}, f32[2,16,128]{2,1,0:T(8,128)S(1)}, u32[]{:S(2)}, u32[]{:S(2)}) collective-permute-start(f32[2,16,128]{2,1,0:T(8,128)S(1)} %shard_map.87.rest_0_), channel_id=1, source_target_pairs={{0,12},{4,0},{8,4},{12,8},{1,13},{5,1},{9,5},{13,9},{2,14},{6,2},{... | collective-permute-start | bytes 49160 | tf_op jit(solution)/shard_map/ppermute | solution.py:371
  40.8 4.7 %collective-permute-start.10 = (f32[2,16,128]{2,1,0:T(8,128)S(1)}, f32[2,16,128]{2,1,0:T(8,128)S(1)}, u32[]{:S(2)}, u32[]{:S(2)}) collective-permute-start(f32[2,16,128]{2,1,0:T(8,128)S(1)} %shard_map.87.rest_0_), channel_id=1, source_target_pairs={{0,8},{4,12},{8,0},{12,4},{1,9},{5,13},{9,1},{13,5},{2,10},{6,14},... | collective-permute-start | bytes 49160 | tf_op jit(solution)/shard_map/ppermute | solution.py:371
  43.6 5.5 %collective-permute-start.9 = (f32[2,16,128]{2,1,0:T(8,128)S(1)}, f32[2,16,128]{2,1,0:T(8,128)S(1)}, u32[]{:S(2)}, u32[]{:S(2)}) collective-permute-start(f32[2,16,128]{2,1,0:T(8,128)S(1)} %shard_map.87.rest_0_), channel_id=1, source_target_pairs={{0,4},{4,8},{8,12},{12,0},{1,5},{5,9},{9,13},{13,1},{2,6},{6,10},{... | collective-permute-start | bytes 49160 | tf_op jit(solution)/shard_map/ppermute | solution.py:371

commit v3 on v2

--- a/solution.py
+++ b/solution.py
@@ -12,7 +12,6 @@
 ROWS = 8
 LANES = 128
 UNROLL = 4
-VMEM = pltpu.CompilerParams(vmem_limit_bytes=40 * 1024 * 1024)
 
 
 def call(kernel, outs, scratch=(), **more):
@@ -20,7 +19,7 @@
         kernel,
         out_shape=[jax.ShapeDtypeStruct(s, jnp.float32) if isinstance(s, tuple) else s for s in outs],
         scratch_shapes=[pltpu.VMEM(s, jnp.float32) if isinstance(s, tuple) else s for s in scratch],
-        compiler_params=VMEM,
+        compiler_params=pltpu.CompilerParams(vmem_limit_bytes=40 * 1024 * 1024),
         **more,
     )
 
@@ -385,8 +384,7 @@
         [jax.ShapeDtypeStruct(x.shape, x.dtype) for x in inputs] + [(2,) + tile, (2,) + tile, strips, strips],
         [pltpu.SemaphoreType.DMA((len(inputs),))],
         in_specs=[pl.BlockSpec(memory_space=pltpu.HBM)] * len(inputs),
-    )(*inputs)
-    rhs, eta, friction, ice_mask, grounded, speed = held
+    )(*[pltpu.with_memory_space_constraint(x, pltpu.HBM) for x in inputs])
     from_next = shifted(to_prev, "gx", -1)
     from_prev = shifted(to_next, "gx", 1)
     columns = jnp.concatenate(
@@ -404,6 +402,7 @@
     if len(parts) > 1:
         sums = call(add_kernel, [sums.shape])(*parts)[0]
     parts = exchange(sums, "gx")
+    rhs, _, friction, ice_mask, grounded, speed = held
     return tuple(
         call(final_kernel, [adjoint_rhs.shape, adjoint_rhs.shape, friction.shape])(
             rhs, powers, friction, ice_mask, grounded, speed, *parts

time: 51.3 us -> 47 us (0.916)
  local copies, waits for them, and re-layouts: 4.69 us -> 0.01 us
  Pallas kernels: 8.68 us -> 9.33 us
    unnamed x13 -> x1, local copies, waits for them, and re-layouts: 4.69 us -> 0.01 us
    pallas_call x1, Pallas kernels: 0.62 us -> 1.28 us  [body(): call(pack_kernel, [jax.ShapeDtypeStruct(x.shape, x.dtype) for x in inputs...]
where the time goes in v3:
time: 47 us; the launch traced here: 46.7 us
  starting transfers between devices  23 us (49%)
  waiting for transfers between devices  13.6 us (29%)
  Pallas kernels  9.33 us (20%)
  between operations  0.73 us (2%)
    ppermute x6, starting transfers between devices, shifted(): return lax.ppermute(x, axis, pairs)  16.4 us
    ppermute x6, waiting for transfers between devices, exchange(): parts.append(lax.ppermute(x, axis, pairs))  8.52 us
    ppermute x6, starting transfers between devices, exchange(): parts.append(lax.ppermute(x, axis, pairs))  6.64 us
    pallas_call x1, Pallas kernels, body(): call(power_kernel, [(STEPS,) + adjoint_rhs.shape, (2, 2 * ROWS, LANES)],...  6.43 us
    ppermute x6, waiting for transfers between devices, shifted(): return lax.ppermute(x, axis, pairs)  5.13 us
    pallas_call x1, Pallas kernels, body(): call(final_kernel, [adjoint_rhs.shape, adjoint_rhs.shape, friction.shape])  1.6 us
    pallas_call x1, Pallas kernels, body(): call(pack_kernel, [jax.ShapeDtypeStruct(x.shape, x.dtype) for x in inputs...  1.28 us
  transfers between devices with their start and end apart: 12, of which 8 were waited for; matrix products, arithmetic and copies ran while one was open for 0% of the time, Pallas kernels for 0%

profile of v3, /device:TPU:0, one launch (start us, length us, event | category | flops | bytes accessed | tf_op | source)
XLA Modules:
  0.0 46.7 jit_solution(306158159085286372)
XLA Ops:
  0.6 1.3 %shard_map.85 = (f32[2,20,8,256]{3,2,1,0:T(8,128)S(1)}, f32[20,8,256]{2,1,0:T(8,128)S(1)}, f32[8,256]{1,0:T(8,128)S(1)}, s32[8,256]{1,0:T(8,128)S(1)}, s32[8,256...) custom-call(f32[2,20,8,256]{3,2,1,0:T(8,128)} %refs_0_.1, ...), custom_call_target="tpu_custom_call" | custom-call | tf_op jit(solution)/shard_map/pallas_call | solution.py:382
  1.9 1.3 %collective-permute-start = (f32[62,8,128]{2,1,0:T(8,128)S(1)}, f32[62,8,128]{2,1,0:T(8,128)S(1)}, u32[]{:S(2)}, u32[]{:S(2)}) collective-permute-start(f32[62,8,128]{2,1,0:T(8,128)S(1)} %get-tuple-element.20), channel_id=1, source_target_pairs={{4,0},{8,4},{12,8},{5,1},{9,5},{13,9},{6,2},{10,6},{14,10},{7,3},{... | collective-permute-start | bytes 761864 | tf_op jit(solution)/shard_map/ppermute | solution.py:352
  3.2 5.6 %collective-permute-start.1 = (f32[62,8,128]{2,1,0:T(8,128)S(1)}, f32[62,8,128]{2,1,0:T(8,128)S(1)}, u32[]{:S(2)}, u32[]{:S(2)}) collective-permute-start(f32[62,8,128]{2,1,0:T(8,128)S(1)} %get-tuple-element.21), channel_id=1, source_target_pairs={{0,4},{4,8},{8,12},{1,5},{5,9},{9,13},{2,6},{6,10},{10,14},{3,7},{... | collective-permute-start | bytes 761864 | tf_op jit(solution)/shard_map/ppermute | solution.py:352
  8.8 1.3 %collective-permute-start.2 = (f32[2,8,128]{2,1,0:T(8,128)S(1)}, f32[2,8,128]{2,1,0:T(8,128)S(1)}, u32[]{:S(2)}, u32[]{:S(2)}) collective-permute-start(f32[2,8,128]{2,1,0:T(8,128)S(1)} %get-tuple-element.22), channel_id=1, source_target_pairs={{1,0},{2,1},{3,2},{5,4},{6,5},{7,6},{9,8},{10,9},{11,10},{13,12},{... | collective-permute-start | bytes 24584 | tf_op jit(solution)/shard_map/ppermute | solution.py:352
  10.1 3.0 %collective-permute-start.3 = (f32[2,8,128]{2,1,0:T(8,128)S(1)}, f32[2,8,128]{2,1,0:T(8,128)S(1)}, u32[]{:S(2)}, u32[]{:S(2)}) collective-permute-start(f32[2,8,128]{2,1,0:T(8,128)S(1)} %get-tuple-element.23), channel_id=1, source_target_pairs={{0,1},{1,2},{2,3},{4,5},{5,6},{6,7},{8,9},{9,10},{10,11},{12,13},{... | collective-permute-start | bytes 24584 | tf_op jit(solution)/shard_map/ppermute | solution.py:352
  13.2 0.8 %collective-permute-done.3 = f32[2,8,128]{2,1,0:T(8,128)S(1)} collective-permute-done((f32[2,8,128]{2,1,0:T(8,128)S(1)}, f32[2,8,128]{2,1,0:T(8,128)S(1)}, u32[]{:S(2)}, u32[]{:S(2)}) %collective-permute-start.3) | collective-permute-done | bytes 8224 | tf_op jit(solution)/shard_map/ppermute | solution.py:352
  13.9 3.9 %collective-permute-start.5 = (f32[4,8,128]{2,1,0:T(8,128)S(1)}, f32[4,8,128]{2,1,0:T(8,128)S(1)}, u32[]{:S(2)}, u32[]{:S(2)}) collective-permute-start(f32[4,8,128]{2,1,0:T(8,128)S(1)} %constant_dynamic-update-slice_fusion.columns), channel_id=1, source_target_pairs={{0,4},{4,8},{8,12},{1,5},{5,9},{9,13},{2,6},{6,10},{10,14},{3,7},{... | collective-permute-start | bytes 49160 | tf_op jit(solution)/shard_map/ppermute | solution.py:352
  17.8 1.3 %collective-permute-start.4 = (f32[4,8,128]{2,1,0:T(8,128)S(1)}, f32[4,8,128]{2,1,0:T(8,128)S(1)}, u32[]{:S(2)}, u32[]{:S(2)}) collective-permute-start(f32[4,8,128]{2,1,0:T(8,128)S(1)} %constant_dynamic-update-slice_fusion.columns), channel_id=1, source_target_pairs={{4,0},{8,4},{12,8},{5,1},{9,5},{13,9},{6,2},{10,6},{14,10},{7,3},{... | collective-permute-start | bytes 49160 | tf_op jit(solution)/shard_map/ppermute | solution.py:352
  19.1 0.1 collective-permute-done.5.prev_columns
  19.3 4.2 %collective-permute-done.4.next_columns = f32[4,8,128]{2,1,0:T(8,128)S(1)} collective-permute-done((f32[4,8,128]{2,1,0:T(8,128)S(1)}, f32[4,8,128]{2,1,0:T(8,128)S(1)}, u32[]{:S(2)}, u32[]{:S(2)}) %collective-permute-start.4) | collective-permute-done | bytes 16416 | tf_op jit(solution)/shard_map/ppermute | solution.py:352
  23.5 0.0 collective-permute-done.1.from_prev
  23.5 6.4 %shard_map.86 = (f32[4,2,20,8,256]{4,3,2,1,0:T(8,128)S(1)}, f32[2,16,128]{2,1,0:T(8,128)S(1)}) custom-call(f32[2,20,8,256]{3,2,1,0:T(8,128)S(1)} %get-tuple-element.15.rhs, f32[20,8,256]{2,1,0:T(8,128)S(1)} %get-tuple-element.16.eta, f32[8,256]{1,0:T(8,128)S(1)} %get-tuple-element.17.friction, s32[8,256]{1,0:T(8,128)S(1)} %get-tuple-element.18.ice, ...), custom_call_target="tpu_custom_call" | custom-call | tf_op jit(solution)/shard_map/pallas_call | solution.py:396
  29.9 0.1 collective-permute-start.8
  30.0 3.3 %collective-permute-start.7 = (f32[2,16,128]{2,1,0:T(8,128)S(1)}, f32[2,16,128]{2,1,0:T(8,128)S(1)}, u32[]{:S(2)}, u32[]{:S(2)}) collective-permute-start(f32[2,16,128]{2,1,0:T(8,128)S(1)} %get-tuple-element.26.refs_0_), channel_id=1, source_target_pairs={{0,2},{1,3},{2,0},{3,1},{4,6},{5,7},{6,4},{7,5},{8,10},{9,11},{10,... | collective-permute-start | bytes 49160 | tf_op jit(solution)/shard_map/ppermute | solution.py:370
  33.3 0.2 collective-permute-start.6
  33.5 1.6 %collective-permute-done.7.refs_2_ = f32[2,16,128]{2,1,0:T(8,128)S(1)} collective-permute-done((f32[2,16,128]{2,1,0:T(8,128)S(1)}, f32[2,16,128]{2,1,0:T(8,128)S(1)}, u32[]{:S(2)}, u32[]{:S(2)}) %collective-permute-start.7) | collective-permute-done | bytes 16416 | tf_op jit(solution)/shard_map/ppermute | solution.py:370
  35.1 1.3 %collective-permute-done.6.refs_1_ = f32[2,16,128]{2,1,0:T(8,128)S(1)} collective-permute-done((f32[2,16,128]{2,1,0:T(8,128)S(1)}, f32[2,16,128]{2,1,0:T(8,128)S(1)}, u32[]{:S(2)}, u32[]{:S(2)}) %collective-permute-start.6) | collective-permute-done | bytes 16416 | tf_op jit(solution)/shard_map/ppermute | solution.py:370
  36.5 0.3 collective-permute-start.11
  36.7 2.8 %collective-permute-start.10 = (f32[2,16,128]{2,1,0:T(8,128)S(1)}, f32[2,16,128]{2,1,0:T(8,128)S(1)}, u32[]{:S(2)}, u32[]{:S(2)}) collective-permute-start(f32[2,16,128]{2,1,0:T(8,128)S(1)} %shard_map.87.rest_0_), channel_id=1, source_target_pairs={{0,8},{4,12},{8,0},{12,4},{1,9},{5,13},{9,1},{13,5},{2,10},{6,14},... | collective-permute-start | bytes 49160 | tf_op jit(solution)/shard_map/ppermute | solution.py:370
  39.6 0.0 collective-permute-start.9
  39.6 0.7 %collective-permute-done.11.rest_3_ = f32[2,16,128]{2,1,0:T(8,128)S(1)} collective-permute-done((f32[2,16,128]{2,1,0:T(8,128)S(1)}, f32[2,16,128]{2,1,0:T(8,128)S(1)}, u32[]{:S(2)}, u32[]{:S(2)}) %collective-permute-start.11) | collective-permute-done | bytes 16416 | tf_op jit(solution)/shard_map/ppermute | solution.py:370
  40.3 1.2 %collective-permute-done.10.rest_2_ = f32[2,16,128]{2,1,0:T(8,128)S(1)} collective-permute-done((f32[2,16,128]{2,1,0:T(8,128)S(1)}, f32[2,16,128]{2,1,0:T(8,128)S(1)}, u32[]{:S(2)}, u32[]{:S(2)}) %collective-permute-start.10) | collective-permute-done | bytes 16416 | tf_op jit(solution)/shard_map/ppermute | solution.py:370
  41.5 3.6 %collective-permute-done.9.rest_1_ = f32[2,16,128]{2,1,0:T(8,128)S(1)} collective-permute-done((f32[2,16,128]{2,1,0:T(8,128)S(1)}, f32[2,16,128]{2,1,0:T(8,128)S(1)}, u32[]{:S(2)}, u32[]{:S(2)}) %collective-permute-start.9) | collective-permute-done | bytes 16416 | tf_op jit(solution)/shard_map/ppermute | solution.py:370
  45.1 1.6 %shard_map.88 = (f32[2,20,8,256]{3,2,1,0:T(8,128)}, f32[2,20,8,256]{3,2,1,0:T(8,128)}, f32[8,256]{1,0:T(8,128)}) custom-call(f32[2,20,8,256]{3,2,1,0:T(8,128)S(1)} %get-tuple-element.15.rhs, f32[4,2,20,8,256]{4,3,2,1,0:T(8,128)S(1)} %get-tuple-element.24.powers, f32[8,256]{1,0:T(8,128)S(1)} %get-tuple-element.17.friction, ...), custom_call_target="tpu_custom_call" | custom-call | tf_op jit(solution)/shard_map/pallas_call | solution.py:407
  (6 shorter events, 0.0 us)
Async XLA Ops:
  1.9 21.6 %collective-permute-start = (f32[62,8,128]{2,1,0:T(8,128)S(1)}, f32[62,8,128]{2,1,0:T(8,128)S(1)}, u32[]{:S(2)}, u32[]{:S(2)}) collective-permute-start(f32[62,8,128]{2,1,0:T(8,128)S(1)} %get-tuple-element.20), channel_id=1, source_target_pairs={{4,0},{8,4},{12,8},{5,1},{9,5},{13,9},{6,2},{10,6},{14,10},{7,3},{... | collective-permute-start | bytes 761864 | tf_op jit(solution)/shard_map/ppermute | solution.py:352
  3.2 20.3 %collective-permute-start.1 = (f32[62,8,128]{2,1,0:T(8,128)S(1)}, f32[62,8,128]{2,1,0:T(8,128)S(1)}, u32[]{:S(2)}, u32[]{:S(2)}) collective-permute-start(f32[62,8,128]{2,1,0:T(8,128)S(1)} %get-tuple-element.21), channel_id=1, source_target_pairs={{0,4},{4,8},{8,12},{1,5},{5,9},{9,13},{2,6},{6,10},{10,14},{3,7},{... | collective-permute-start | bytes 761864 | tf_op jit(solution)/shard_map/ppermute | solution.py:352
  8.8 4.3 %collective-permute-start.2 = (f32[2,8,128]{2,1,0:T(8,128)S(1)}, f32[2,8,128]{2,1,0:T(8,128)S(1)}, u32[]{:S(2)}, u32[]{:S(2)}) collective-permute-start(f32[2,8,128]{2,1,0:T(8,128)S(1)} %get-tuple-element.22), channel_id=1, source_target_pairs={{1,0},{2,1},{3,2},{5,4},{6,5},{7,6},{9,8},{10,9},{11,10},{13,12},{... | collective-permute-start | bytes 24584 | tf_op jit(solution)/shard_map/ppermute | solution.py:352
  10.1 3.8 %collective-permute-start.3 = (f32[2,8,128]{2,1,0:T(8,128)S(1)}, f32[2,8,128]{2,1,0:T(8,128)S(1)}, u32[]{:S(2)}, u32[]{:S(2)}) collective-permute-start(f32[2,8,128]{2,1,0:T(8,128)S(1)} %get-tuple-element.23), channel_id=1, source_target_pairs={{0,1},{1,2},{2,3},{4,5},{5,6},{6,7},{8,9},{9,10},{10,11},{12,13},{... | collective-permute-start | bytes 24584 | tf_op jit(solution)/shard_map/ppermute | solution.py:352
  13.9 5.3 %collective-permute-start.5 = (f32[4,8,128]{2,1,0:T(8,128)S(1)}, f32[4,8,128]{2,1,0:T(8,128)S(1)}, u32[]{:S(2)}, u32[]{:S(2)}) collective-permute-start(f32[4,8,128]{2,1,0:T(8,128)S(1)} %constant_dynamic-update-slice_fusion.columns), channel_id=1, source_target_pairs={{0,4},{4,8},{8,12},{1,5},{5,9},{9,13},{2,6},{6,10},{10,14},{3,7},{... | collective-permute-start | bytes 49160 | tf_op jit(solution)/shard_map/ppermute | solution.py:352
  17.8 5.6 %collective-permute-start.4 = (f32[4,8,128]{2,1,0:T(8,128)S(1)}, f32[4,8,128]{2,1,0:T(8,128)S(1)}, u32[]{:S(2)}, u32[]{:S(2)}) collective-permute-start(f32[4,8,128]{2,1,0:T(8,128)S(1)} %constant_dynamic-update-slice_fusion.columns), channel_id=1, source_target_pairs={{4,0},{8,4},{12,8},{5,1},{9,5},{13,9},{6,2},{10,6},{14,10},{7,3},{... | collective-permute-start | bytes 49160 | tf_op jit(solution)/shard_map/ppermute | solution.py:352
  29.9 3.5 %collective-permute-start.8 = (f32[2,16,128]{2,1,0:T(8,128)S(1)}, f32[2,16,128]{2,1,0:T(8,128)S(1)}, u32[]{:S(2)}, u32[]{:S(2)}) collective-permute-start(f32[2,16,128]{2,1,0:T(8,128)S(1)} %get-tuple-element.26.refs_0_), channel_id=1, source_target_pairs={{0,3},{1,0},{2,1},{3,2},{4,7},{5,4},{6,5},{7,6},{8,11},{9,8},{10,9... | collective-permute-start | bytes 49160 | tf_op jit(solution)/shard_map/ppermute | solution.py:370
  30.0 5.1 %collective-permute-start.7 = (f32[2,16,128]{2,1,0:T(8,128)S(1)}, f32[2,16,128]{2,1,0:T(8,128)S(1)}, u32[]{:S(2)}, u32[]{:S(2)}) collective-permute-start(f32[2,16,128]{2,1,0:T(8,128)S(1)} %get-tuple-element.26.refs_0_), channel_id=1, source_target_pairs={{0,2},{1,3},{2,0},{3,1},{4,6},{5,7},{6,4},{7,5},{8,10},{9,11},{10,... | collective-permute-start | bytes 49160 | tf_op jit(solution)/shard_map/ppermute | solution.py:370
  33.3 3.2 %collective-permute-start.6 = (f32[2,16,128]{2,1,0:T(8,128)S(1)}, f32[2,16,128]{2,1,0:T(8,128)S(1)}, u32[]{:S(2)}, u32[]{:S(2)}) collective-permute-start(f32[2,16,128]{2,1,0:T(8,128)S(1)} %get-tuple-element.26.refs_0_), channel_id=1, source_target_pairs={{0,1},{1,2},{2,3},{3,0},{4,5},{5,6},{6,7},{7,4},{8,9},{9,10},{10,1... | collective-permute-start | bytes 49160 | tf_op jit(solution)/shard_map/ppermute | solution.py:370
  36.5 3.8 %collective-permute-start.11 = (f32[2,16,128]{2,1,0:T(8,128)S(1)}, f32[2,16,128]{2,1,0:T(8,128)S(1)}, u32[]{:S(2)}, u32[]{:S(2)}) collective-permute-start(f32[2,16,128]{2,1,0:T(8,128)S(1)} %shard_map.87.rest_0_), channel_id=1, source_target_pairs={{0,12},{4,0},{8,4},{12,8},{1,13},{5,1},{9,5},{13,9},{2,14},{6,2},{... | collective-permute-start | bytes 49160 | tf_op jit(solution)/shard_map/ppermute | solution.py:370
  36.7 4.7 %collective-permute-start.10 = (f32[2,16,128]{2,1,0:T(8,128)S(1)}, f32[2,16,128]{2,1,0:T(8,128)S(1)}, u32[]{:S(2)}, u32[]{:S(2)}) collective-permute-start(f32[2,16,128]{2,1,0:T(8,128)S(1)} %shard_map.87.rest_0_), channel_id=1, source_target_pairs={{0,8},{4,12},{8,0},{12,4},{1,9},{5,13},{9,1},{13,5},{2,10},{6,14},... | collective-permute-start | bytes 49160 | tf_op jit(solution)/shard_map/ppermute | solution.py:370
  39.6 5.5 %collective-permute-start.9 = (f32[2,16,128]{2,1,0:T(8,128)S(1)}, f32[2,16,128]{2,1,0:T(8,128)S(1)}, u32[]{:S(2)}, u32[]{:S(2)}) collective-permute-start(f32[2,16,128]{2,1,0:T(8,128)S(1)} %shard_map.87.rest_0_), channel_id=1, source_target_pairs={{0,4},{4,8},{8,12},{12,0},{1,5},{5,9},{9,13},{13,1},{2,6},{6,10},{... | collective-permute-start | bytes 49160 | tf_op jit(solution)/shard_map/ppermute | solution.py:370

commit v4 on v3

--- a/solution.py
+++ b/solution.py
@@ -24,6 +24,23 @@
     )
 
 
+def place_of(axis):
+    place, count = lax.axis_index(axis), lax.axis_size(axis)
+    even = place % 2 == 0
+    has_a = jnp.logical_or(jnp.logical_not(even), place < count - 1)
+    has_b = jnp.where(even, place > 0, place < count - 1)
+    return even, has_a, has_b
+
+
+def swapped(x, axis, first):
+    count = lax.axis_size(axis)
+    pairs = []
+    for i in range(count):
+        other = i + 1 if (i - first) % 2 == 0 else i - 1
+        pairs.append((i, other if 0 <= other < count else i))
+    return lax.ppermute(x, axis, pairs)
+
+
 def own_planes(rhs, eta, friction, ice, grounded):
     layers = eta.shape[0]
     cover = ice[...].astype(jnp.float32)
@@ -48,7 +65,7 @@
 
 
 def pack_kernel(*refs):
-    sources, held, (to_left, to_right, to_prev, to_next, arrived) = refs[:6], refs[6:12], refs[12:]
+    sources, held, (column_a, column_b, strip_a, strip_b, arrived) = refs[:6], refs[6:12], refs[12:]
     copies = [pltpu.make_async_copy(a, b, arrived.at[i]) for i, (a, b) in enumerate(zip(sources, held))]
     for copy in copies:
         copy.start()
@@ -59,8 +76,10 @@
     plane = own_planes(rhs, eta, friction, ice, grounded)
     lane = lax.broadcasted_iota(jnp.int32, (ROWS, LANES), 1)
     row = lax.broadcasted_iota(jnp.int32, (ROWS, LANES), 0)
-    upper = row < HALO
-    width = to_prev.shape[0]
+    rows_even, _, _ = place_of("gx")
+    columns_even, _, _ = place_of(("gy", "gz"))
+    upper_a = (row < HALO) != rows_even
+    width = strip_a.shape[0]
     left = [jnp.zeros((ROWS, LANES), jnp.float32) for _ in range(2)]
     right = [jnp.zeros((ROWS, LANES), jnp.float32) for _ in range(2)]
     for q in range(width // 2):
@@ -69,8 +88,9 @@
         for half in range(2):
             xs = x[:, half * LANES : (half + 1) * LANES]
             ys = y[:, half * LANES : (half + 1) * LANES]
-            to_prev[2 * q + half] = jnp.where(upper, xs, pltpu.roll(ys, HALO, 0))
-            to_next[2 * q + half] = jnp.where(upper, pltpu.roll(ys, HALO, 0), xs)
+            ys = pltpu.roll(ys, HALO, 0)
+            strip_a[2 * q + half] = jnp.where(upper_a, xs, ys)
+            strip_b[2 * q + half] = jnp.where(upper_a, ys, xs)
         for p, v in ((first, x), (second, y)):
             group, place = p // 32, HALO * (p % 32)
             mine = (lane >= place) & (lane < place + HALO)
@@ -79,8 +99,8 @@
             left[group] = jnp.where(mine, pltpu.roll(head, place, 1) if place else head, left[group])
             right[group] = jnp.where(mine, pltpu.roll(tail, shift, 1) if shift else tail, right[group])
     for group in range(2):
-        to_left[group] = left[group]
-        to_right[group] = right[group]
+        column_a[group] = jnp.where(columns_even, right[group], left[group])
+        column_b[group] = jnp.where(columns_even, left[group], right[group])
 
 
 def two_sum(a, b):
@@ -110,7 +130,7 @@
 
 
 def power_kernel(
-    rhs, eta, friction, ice, grounded, from_next, from_prev, columns, next_columns, prev_columns,
+    rhs, eta, friction, ice, grounded, strip_a, strip_b, columns, columns_a, columns_b,
     powers, moments,
     field_a, field_b, eta_row, eta_col, eta_half, eta_up, cover, drag,
 ):
@@ -118,10 +138,27 @@
     plane = own_planes(rhs, eta, friction, ice, grounded)
     lane = lax.broadcasted_iota(jnp.int32, (ROWS, LANES), 1)
     row = lax.broadcasted_iota(jnp.int32, (ROWS, LANES), 0)
-    upper = row < HALO
-    strips = from_next.shape[0]
-    corner = [jnp.where(upper, next_columns[t], prev_columns[t]) for t in range(4)]
-    beside = [columns[t] for t in range(4)]
+    strips = strip_a.shape[0]
+    even, has_a, has_b = place_of("gx")
+    upper_a = (row < HALO) == even
+
+    def below_and_above(from_a, from_b):
+        return jnp.where(upper_a, jnp.where(has_a, from_a, 0.0), jnp.where(has_b, from_b, 0.0))
+
+    def above_and_below(from_a, from_b):
+        return jnp.where(upper_a, jnp.where(has_b, from_b, 0.0), jnp.where(has_a, from_a, 0.0))
+
+    even, came_a, came_b = place_of(("gy", "gz"))
+
+    def right_and_left(tiles):
+        from_a = [jnp.where(came_a, tiles[t], 0.0) for t in (0, 1)]
+        from_b = [jnp.where(came_b, tiles[t], 0.0) for t in (2, 3)]
+        right = [jnp.where(even, x, y) for x, y in zip(from_a, from_b)]
+        left = [jnp.where(even, y, x) for x, y in zip(from_a, from_b)]
+        return right + left
+
+    corner = right_and_left([below_and_above(columns_a[t], columns_b[t]) for t in range(4)])
+    beside = right_and_left([columns[t] for t in range(4)])
 
     def side(tiles, p):
         group, place = p // 32, HALO * (p % 32)
@@ -145,10 +182,10 @@
     for q in range(strips // 2):
         first, second = pair_of(q, layers)
         for half in range(2):
-            below, above = from_next[2 * q + half], from_prev[2 * q + half]
+            from_a, from_b = strip_a[2 * q + half], strip_b[2 * q + half]
             cut = slice(half * LANES, (half + 1) * LANES)
-            target(first)[ROWS:, cut] = jnp.where(upper, below, above)
-            target(second)[ROWS:, cut] = pltpu.roll(jnp.where(upper, above, below), HALO, 0)
+            target(first)[ROWS:, cut] = below_and_above(from_a, from_b)
+            target(second)[ROWS:, cut] = pltpu.roll(above_and_below(from_a, from_b), HALO, 0)
         fill(first, target(first))
         fill(second, target(second))
 
@@ -346,12 +383,6 @@
     hessian[...] = weight * (speed[0] * iterate[0, 0] + speed[1] * iterate[1, 0])
 
 
-def shifted(x, axis, step):
-    count = lax.axis_size(axis)
-    pairs = [(i, i + step) for i in range(count) if 0 <= i + step < count]
-    return lax.ppermute(x, axis, pairs)
-
-
 def exchange(x, axis):
     count = lax.axis_size(axis)
     stride = 1
@@ -366,7 +397,7 @@
             pairs = []
             for i in range(count):
                 place = (i // stride) % size
-                pairs.append((i, i + ((place + turn) % size - place) * stride))
+                pairs.append((i, i + ((place ^ turn) - place) * stride))
             parts.append(lax.ppermute(x, axis, pairs))
         if at == len(rounds) - 1:
             return parts
@@ -379,25 +410,22 @@
     inputs = (adjoint_rhs, viscosity, friction, ice_mask, grounded, basal_velocity)
     tile = (ROWS, LANES)
     strips = (2 * (layers + layers // 2 + 1),) + tile
-    *held, to_left, to_right, to_prev, to_next = call(
+    *held, column_a, column_b, strip_a, strip_b = call(
         pack_kernel,
         [jax.ShapeDtypeStruct(x.shape, x.dtype) for x in inputs] + [(2,) + tile, (2,) + tile, strips, strips],
         [pltpu.SemaphoreType.DMA((len(inputs),))],
         in_specs=[pl.BlockSpec(memory_space=pltpu.HBM)] * len(inputs),
     )(*[pltpu.with_memory_space_constraint(x, pltpu.HBM) for x in inputs])
-    from_next = shifted(to_prev, "gx", -1)
-    from_prev = shifted(to_next, "gx", 1)
-    columns = jnp.concatenate(
-        [shifted(to_left, ("gy", "gz"), -1), shifted(to_right, ("gy", "gz"), 1)], axis=0
-    )
-    next_columns = shifted(columns, "gx", -1)
-    prev_columns = shifted(columns, "gx", 1)
+    strip_a, strip_b = swapped(strip_a, "gx", 0), swapped(strip_b, "gx", 1)
+    beside = ("gy", "gz")
+    columns = jnp.concatenate([swapped(column_a, beside, 0), swapped(column_b, beside, 1)], axis=0)
+    columns_a, columns_b = swapped(columns, "gx", 0), swapped(columns, "gx", 1)
     block = (layers, 2 * ROWS, 3 * LANES)
     powers, sums = call(
         power_kernel,
         [(STEPS,) + adjoint_rhs.shape, (2, 2 * ROWS, LANES)],
         [(2,) + block] * 2 + [block] * 4 + [block[1:]] * 2,
-    )(*held[:5], from_next, from_prev, columns, next_columns, prev_columns)
+    )(*held[:5], strip_a, strip_b, columns, columns_a, columns_b)
     parts = exchange(sums, ("gy", "gz"))
     if len(parts) > 1:
         sums = call(add_kernel, [sums.shape])(*parts)[0]

time: 47 us -> 38.2 us (0.81)
  waiting for transfers between devices: 13.6 us -> 7.17 us
  starting transfers between devices: 23 us -> 20.8 us
    ppermute x6, starting transfers between devices: 16.4 us -> 10.9 us  [swapped(): return lax.ppermute(x, axis, pairs)]
    ppermute x6, waiting for transfers between devices: 8.52 us -> 4.95 us  [exchange(): parts.append(lax.ppermute(x, axis, pairs))]
    ppermute x6, starting transfers between devices: 6.64 us -> 9.92 us  [exchange(): parts.append(lax.ppermute(x, axis, pairs))]
    ppermute x6, waiting for transfers between devices: 5.13 us -> 2.22 us  [swapped(): return lax.ppermute(x, axis, pairs)]
  transfers between devices with their start and end apart: 12 -> 12, of which waited for: 8 -> 5; matrix products, arithmetic and copies ran while one was open for 0% -> 0% of each run, Pallas kernels for 0% -> 0%
where the time goes in v4:
time: 38.2 us; the launch traced here: 38 us
  starting transfers between devices  20.8 us (54%)
  Pallas kernels  9.35 us (24%)
  waiting for transfers between devices  7.17 us (19%)
  between operations  0.69 us (2%)
    ppermute x6, starting transfers between devices, swapped(): return lax.ppermute(x, axis, pairs)  10.9 us
    ppermute x6, starting transfers between devices, exchange(): parts.append(lax.ppermute(x, axis, pairs))  9.92 us
    pallas_call x1, Pallas kernels, body(): call(power_kernel, [(STEPS,) + adjoint_rhs.shape, (2, 2 * ROWS, LANES)],...  6.44 us
    ppermute x6, waiting for transfers between devices, exchange(): parts.append(lax.ppermute(x, axis, pairs))  4.95 us
    ppermute x6, waiting for transfers between devices, swapped(): return lax.ppermute(x, axis, pairs)  2.22 us
    pallas_call x1, Pallas kernels, body(): call(final_kernel, [adjoint_rhs.shape, adjoint_rhs.shape, friction.shape])  1.6 us
    pallas_call x1, Pallas kernels, body(): call(pack_kernel, [jax.ShapeDtypeStruct(x.shape, x.dtype) for x in inputs...  1.28 us
  transfers between devices with their start and end apart: 12, of which 5 were waited for; matrix products, arithmetic and copies ran while one was open for 0% of the time, Pallas kernels for 0%

profile of v4, /device:TPU:0, one launch (start us, length us, event | category | flops | bytes accessed | tf_op | source)
XLA Modules:
  0.0 38.0 jit_solution(16799443104099609479)
XLA Ops:
  0.6 1.3 %shard_map.85 = (f32[2,20,8,256]{3,2,1,0:T(8,128)S(1)}, f32[20,8,256]{2,1,0:T(8,128)S(1)}, f32[8,256]{1,0:T(8,128)S(1)}, s32[8,256]{1,0:T(8,128)S(1)}, s32[8,256...) custom-call(f32[2,20,8,256]{3,2,1,0:T(8,128)} %refs_0_.1, ...), custom_call_target="tpu_custom_call" | custom-call | tf_op jit(solution)/shard_map/pallas_call | solution.py:413
  1.9 3.1 %collective-permute-start = (f32[62,8,128]{2,1,0:T(8,128)S(1)}, f32[62,8,128]{2,1,0:T(8,128)S(1)}, u32[]{:S(2)}, u32[]{:S(2)}) collective-permute-start(f32[62,8,128]{2,1,0:T(8,128)S(1)} %get-tuple-element.20), channel_id=1, source_target_pairs={{0,4},{4,0},{8,12},{12,8},{1,5},{5,1},{9,13},{13,9},{2,6},{6,2},{1... | collective-permute-start | bytes 761864 | tf_op jit(solution)/shard_map/ppermute | solution.py:41
  5.0 0.7 %collective-permute-start.1 = (f32[62,8,128]{2,1,0:T(8,128)S(1)}, f32[62,8,128]{2,1,0:T(8,128)S(1)}, u32[]{:S(2)}, u32[]{:S(2)}) collective-permute-start(f32[62,8,128]{2,1,0:T(8,128)S(1)} %get-tuple-element.21), channel_id=1, source_target_pairs={{0,0},{4,8},{8,4},{12,12},{1,1},{5,9},{9,5},{13,13},{2,2},{6,10},{... | collective-permute-start | bytes 761864 | tf_op jit(solution)/shard_map/ppermute | solution.py:41
  5.7 0.1 collective-permute-start.2
  5.8 0.7 %collective-permute-start.3 = (f32[2,8,128]{2,1,0:T(8,128)S(1)}, f32[2,8,128]{2,1,0:T(8,128)S(1)}, u32[]{:S(2)}, u32[]{:S(2)}) collective-permute-start(f32[2,8,128]{2,1,0:T(8,128)S(1)} %get-tuple-element.23), channel_id=1, source_target_pairs={{0,0},{1,2},{2,1},{3,3},{4,4},{5,6},{6,5},{7,7},{8,8},{9,10},{10,9... | collective-permute-start | bytes 24584 | tf_op jit(solution)/shard_map/ppermute | solution.py:41
  6.4 0.5 %collective-permute-done.2 = f32[2,8,128]{2,1,0:T(8,128)S(1)} collective-permute-done((f32[2,8,128]{2,1,0:T(8,128)S(1)}, f32[2,8,128]{2,1,0:T(8,128)S(1)}, u32[]{:S(2)}, u32[]{:S(2)}) %collective-permute-start.2) | collective-permute-done | bytes 8224 | tf_op jit(solution)/shard_map/ppermute | solution.py:41
  6.9 0.0 collective-permute-done.3
  6.9 0.7 %collective-permute-start.5 = (f32[4,8,128]{2,1,0:T(8,128)S(1)}, f32[4,8,128]{2,1,0:T(8,128)S(1)}, u32[]{:S(2)}, u32[]{:S(2)}) collective-permute-start(f32[4,8,128]{2,1,0:T(8,128)S(1)} %constant_dynamic-update-slice_fusion.columns), channel_id=1, source_target_pairs={{0,0},{4,8},{8,4},{12,12},{1,1},{5,9},{9,5},{13,13},{2,2},{6,10},{... | collective-permute-start | bytes 49160 | tf_op jit(solution)/shard_map/ppermute | solution.py:41
  7.6 5.7 %collective-permute-start.4 = (f32[4,8,128]{2,1,0:T(8,128)S(1)}, f32[4,8,128]{2,1,0:T(8,128)S(1)}, u32[]{:S(2)}, u32[]{:S(2)}) collective-permute-start(f32[4,8,128]{2,1,0:T(8,128)S(1)} %constant_dynamic-update-slice_fusion.columns), channel_id=1, source_target_pairs={{0,4},{4,0},{8,12},{12,8},{1,5},{5,1},{9,13},{13,9},{2,6},{6,2},{1... | collective-permute-start | bytes 49160 | tf_op jit(solution)/shard_map/ppermute | solution.py:41
  13.3 0.0 collective-permute-done.5.columns_b
  13.3 1.7 %collective-permute-done.4.columns_a = f32[4,8,128]{2,1,0:T(8,128)S(1)} collective-permute-done((f32[4,8,128]{2,1,0:T(8,128)S(1)}, f32[4,8,128]{2,1,0:T(8,128)S(1)}, u32[]{:S(2)}, u32[]{:S(2)}) %collective-permute-start.4) | collective-permute-done | bytes 16416 | tf_op jit(solution)/shard_map/ppermute | solution.py:41
  15.0 0.0 collective-permute-done.strip_a
  15.0 6.4 %shard_map.86 = (f32[4,2,20,8,256]{4,3,2,1,0:T(8,128)S(1)}, f32[2,16,128]{2,1,0:T(8,128)S(1)}) custom-call(f32[2,20,8,256]{3,2,1,0:T(8,128)S(1)} %get-tuple-element.15.rhs, f32[20,8,256]{2,1,0:T(8,128)S(1)} %get-tuple-element.16.eta, f32[8,256]{1,0:T(8,128)S(1)} %get-tuple-element.17.friction, s32[8,256]{1,0:T(8,128)S(1)} %get-tuple-element.18.ice, ...), custom_call_target="tpu_custom_call" | custom-call | tf_op jit(solution)/shard_map/pallas_call | solution.py:424
  21.5 0.5 %collective-permute-start.8 = (f32[2,16,128]{2,1,0:T(8,128)S(1)}, f32[2,16,128]{2,1,0:T(8,128)S(1)}, u32[]{:S(2)}, u32[]{:S(2)}) collective-permute-start(f32[2,16,128]{2,1,0:T(8,128)S(1)} %get-tuple-element.26.refs_0_), channel_id=1, source_target_pairs={{0,3},{1,2},{2,1},{3,0},{4,7},{5,6},{6,5},{7,4},{8,11},{9,10},{10,... | collective-permute-start | bytes 49160 | tf_op jit(solution)/shard_map/ppermute | solution.py:401
  21.9 5.0 %collective-permute-start.7 = (f32[2,16,128]{2,1,0:T(8,128)S(1)}, f32[2,16,128]{2,1,0:T(8,128)S(1)}, u32[]{:S(2)}, u32[]{:S(2)}) collective-permute-start(f32[2,16,128]{2,1,0:T(8,128)S(1)} %get-tuple-element.26.refs_0_), channel_id=1, source_target_pairs={{0,2},{1,3},{2,0},{3,1},{4,6},{5,7},{6,4},{7,5},{8,10},{9,11},{10,... | collective-permute-start | bytes 49160 | tf_op jit(solution)/shard_map/ppermute | solution.py:401
  26.9 0.0 collective-permute-start.6
  27.0 1.8 %collective-permute-done.7.refs_2_ = f32[2,16,128]{2,1,0:T(8,128)S(1)} collective-permute-done((f32[2,16,128]{2,1,0:T(8,128)S(1)}, f32[2,16,128]{2,1,0:T(8,128)S(1)}, u32[]{:S(2)}, u32[]{:S(2)}) %collective-permute-start.7) | collective-permute-done | bytes 16416 | tf_op jit(solution)/shard_map/ppermute | solution.py:401
  28.8 0.0 collective-permute-done.6.refs_1_
  28.8 2.9 %collective-permute-start.11 = (f32[2,16,128]{2,1,0:T(8,128)S(1)}, f32[2,16,128]{2,1,0:T(8,128)S(1)}, u32[]{:S(2)}, u32[]{:S(2)}) collective-permute-start(f32[2,16,128]{2,1,0:T(8,128)S(1)} %shard_map.87.rest_0_), channel_id=1, source_target_pairs={{0,12},{4,8},{8,4},{12,0},{1,13},{5,9},{9,5},{13,1},{2,14},{6,10},... | collective-permute-start | bytes 49160 | tf_op jit(solution)/shard_map/ppermute | solution.py:401
  31.7 0.6 %collective-permute-start.10 = (f32[2,16,128]{2,1,0:T(8,128)S(1)}, f32[2,16,128]{2,1,0:T(8,128)S(1)}, u32[]{:S(2)}, u32[]{:S(2)}) collective-permute-start(f32[2,16,128]{2,1,0:T(8,128)S(1)} %shard_map.87.rest_0_), channel_id=1, source_target_pairs={{0,8},{4,12},{8,0},{12,4},{1,9},{5,13},{9,1},{13,5},{2,10},{6,14},... | collective-permute-start | bytes 49160 | tf_op jit(solution)/shard_map/ppermute | solution.py:401
  32.4 0.9 %collective-permute-start.9 = (f32[2,16,128]{2,1,0:T(8,128)S(1)}, f32[2,16,128]{2,1,0:T(8,128)S(1)}, u32[]{:S(2)}, u32[]{:S(2)}) collective-permute-start(f32[2,16,128]{2,1,0:T(8,128)S(1)} %shard_map.87.rest_0_), channel_id=1, source_target_pairs={{0,4},{4,0},{8,12},{12,8},{1,5},{5,1},{9,13},{13,9},{2,6},{6,2},{1... | collective-permute-start | bytes 49160 | tf_op jit(solution)/shard_map/ppermute | solution.py:401
  33.2 1.2 %collective-permute-done.11.rest_3_ = f32[2,16,128]{2,1,0:T(8,128)S(1)} collective-permute-done((f32[2,16,128]{2,1,0:T(8,128)S(1)}, f32[2,16,128]{2,1,0:T(8,128)S(1)}, u32[]{:S(2)}, u32[]{:S(2)}) %collective-permute-start.11) | collective-permute-done | bytes 16416 | tf_op jit(solution)/shard_map/ppermute | solution.py:401
  34.5 1.9 %collective-permute-done.10.rest_2_ = f32[2,16,128]{2,1,0:T(8,128)S(1)} collective-permute-done((f32[2,16,128]{2,1,0:T(8,128)S(1)}, f32[2,16,128]{2,1,0:T(8,128)S(1)}, u32[]{:S(2)}, u32[]{:S(2)}) %collective-permute-start.10) | collective-permute-done | bytes 16416 | tf_op jit(solution)/shard_map/ppermute | solution.py:401
  36.4 1.6 %shard_map.88 = (f32[2,20,8,256]{3,2,1,0:T(8,128)}, f32[2,20,8,256]{3,2,1,0:T(8,128)}, f32[8,256]{1,0:T(8,128)}) custom-call(f32[2,20,8,256]{3,2,1,0:T(8,128)S(1)} %get-tuple-element.15.rhs, f32[4,2,20,8,256]{4,3,2,1,0:T(8,128)S(1)} %get-tuple-element.24.powers, f32[8,256]{1,0:T(8,128)S(1)} %get-tuple-element.17.friction, ...), custom_call_target="tpu_custom_call" | custom-call | tf_op jit(solution)/shard_map/pallas_call | solution.py:435
  (6 shorter events, 0.0 us)
Async XLA Ops:
  1.9 13.1 %collective-permute-start = (f32[62,8,128]{2,1,0:T(8,128)S(1)}, f32[62,8,128]{2,1,0:T(8,128)S(1)}, u32[]{:S(2)}, u32[]{:S(2)}) collective-permute-start(f32[62,8,128]{2,1,0:T(8,128)S(1)} %get-tuple-element.20), channel_id=1, source_target_pairs={{0,4},{4,0},{8,12},{12,8},{1,5},{5,1},{9,13},{13,9},{2,6},{6,2},{1... | collective-permute-start | bytes 761864 | tf_op jit(solution)/shard_map/ppermute | solution.py:41
  5.0 10.0 %collective-permute-start.1 = (f32[62,8,128]{2,1,0:T(8,128)S(1)}, f32[62,8,128]{2,1,0:T(8,128)S(1)}, u32[]{:S(2)}, u32[]{:S(2)}) collective-permute-start(f32[62,8,128]{2,1,0:T(8,128)S(1)} %get-tuple-element.21), channel_id=1, source_target_pairs={{0,0},{4,8},{8,4},{12,12},{1,1},{5,9},{9,5},{13,13},{2,2},{6,10},{... | collective-permute-start | bytes 761864 | tf_op jit(solution)/shard_map/ppermute | solution.py:41
  5.7 1.2 %collective-permute-start.2 = (f32[2,8,128]{2,1,0:T(8,128)S(1)}, f32[2,8,128]{2,1,0:T(8,128)S(1)}, u32[]{:S(2)}, u32[]{:S(2)}) collective-permute-start(f32[2,8,128]{2,1,0:T(8,128)S(1)} %get-tuple-element.22), channel_id=1, source_target_pairs={{0,1},{1,0},{2,3},{3,2},{4,5},{5,4},{6,7},{7,6},{8,9},{9,8},{10,11... | collective-permute-start | bytes 24584 | tf_op jit(solution)/shard_map/ppermute | solution.py:41
  5.8 1.2 %collective-permute-start.3 = (f32[2,8,128]{2,1,0:T(8,128)S(1)}, f32[2,8,128]{2,1,0:T(8,128)S(1)}, u32[]{:S(2)}, u32[]{:S(2)}) collective-permute-start(f32[2,8,128]{2,1,0:T(8,128)S(1)} %get-tuple-element.23), channel_id=1, source_target_pairs={{0,0},{1,2},{2,1},{3,3},{4,4},{5,6},{6,5},{7,7},{8,8},{9,10},{10,9... | collective-permute-start | bytes 24584 | tf_op jit(solution)/shard_map/ppermute | solution.py:41
  6.9 6.4 %collective-permute-start.5 = (f32[4,8,128]{2,1,0:T(8,128)S(1)}, f32[4,8,128]{2,1,0:T(8,128)S(1)}, u32[]{:S(2)}, u32[]{:S(2)}) collective-permute-start(f32[4,8,128]{2,1,0:T(8,128)S(1)} %constant_dynamic-update-slice_fusion.columns), channel_id=1, source_target_pairs={{0,0},{4,8},{8,4},{12,12},{1,1},{5,9},{9,5},{13,13},{2,2},{6,10},{... | collective-permute-start | bytes 49160 | tf_op jit(solution)/shard_map/ppermute | solution.py:41
  7.6 7.4 %collective-permute-start.4 = (f32[4,8,128]{2,1,0:T(8,128)S(1)}, f32[4,8,128]{2,1,0:T(8,128)S(1)}, u32[]{:S(2)}, u32[]{:S(2)}) collective-permute-start(f32[4,8,128]{2,1,0:T(8,128)S(1)} %constant_dynamic-update-slice_fusion.columns), channel_id=1, source_target_pairs={{0,4},{4,0},{8,12},{12,8},{1,5},{5,1},{9,13},{13,9},{2,6},{6,2},{1... | collective-permute-start | bytes 49160 | tf_op jit(solution)/shard_map/ppermute | solution.py:41
  21.5 5.5 %collective-permute-start.8 = (f32[2,16,128]{2,1,0:T(8,128)S(1)}, f32[2,16,128]{2,1,0:T(8,128)S(1)}, u32[]{:S(2)}, u32[]{:S(2)}) collective-permute-start(f32[2,16,128]{2,1,0:T(8,128)S(1)} %get-tuple-element.26.refs_0_), channel_id=1, source_target_pairs={{0,3},{1,2},{2,1},{3,0},{4,7},{5,6},{6,5},{7,4},{8,11},{9,10},{10,... | collective-permute-start | bytes 49160 | tf_op jit(solution)/shard_map/ppermute | solution.py:401
  21.9 6.8 %collective-permute-start.7 = (f32[2,16,128]{2,1,0:T(8,128)S(1)}, f32[2,16,128]{2,1,0:T(8,128)S(1)}, u32[]{:S(2)}, u32[]{:S(2)}) collective-permute-start(f32[2,16,128]{2,1,0:T(8,128)S(1)} %get-tuple-element.26.refs_0_), channel_id=1, source_target_pairs={{0,2},{1,3},{2,0},{3,1},{4,6},{5,7},{6,4},{7,5},{8,10},{9,11},{10,... | collective-permute-start | bytes 49160 | tf_op jit(solution)/shard_map/ppermute | solution.py:401
  26.9 1.9 %collective-permute-start.6 = (f32[2,16,128]{2,1,0:T(8,128)S(1)}, f32[2,16,128]{2,1,0:T(8,128)S(1)}, u32[]{:S(2)}, u32[]{:S(2)}) collective-permute-start(f32[2,16,128]{2,1,0:T(8,128)S(1)} %get-tuple-element.26.refs_0_), channel_id=1, source_target_pairs={{0,1},{1,0},{2,3},{3,2},{4,5},{5,4},{6,7},{7,6},{8,9},{9,8},{10,11... | collective-permute-start | bytes 49160 | tf_op jit(solution)/shard_map/ppermute | solution.py:401
  28.8 5.7 %collective-permute-start.11 = (f32[2,16,128]{2,1,0:T(8,128)S(1)}, f32[2,16,128]{2,1,0:T(8,128)S(1)}, u32[]{:S(2)}, u32[]{:S(2)}) collective-permute-start(f32[2,16,128]{2,1,0:T(8,128)S(1)} %shard_map.87.rest_0_), channel_id=1, source_target_pairs={{0,12},{4,8},{8,4},{12,0},{1,13},{5,9},{9,5},{13,1},{2,14},{6,10},... | collective-permute-start | bytes 49160 | tf_op jit(solution)/shard_map/ppermute | solution.py:401
  31.7 4.6 %collective-permute-start.10 = (f32[2,16,128]{2,1,0:T(8,128)S(1)}, f32[2,16,128]{2,1,0:T(8,128)S(1)}, u32[]{:S(2)}, u32[]{:S(2)}) collective-permute-start(f32[2,16,128]{2,1,0:T(8,128)S(1)} %shard_map.87.rest_0_), channel_id=1, source_target_pairs={{0,8},{4,12},{8,0},{12,4},{1,9},{5,13},{9,1},{13,5},{2,10},{6,14},... | collective-permute-start | bytes 49160 | tf_op jit(solution)/shard_map/ppermute | solution.py:401
  32.4 4.0 %collective-permute-start.9 = (f32[2,16,128]{2,1,0:T(8,128)S(1)}, f32[2,16,128]{2,1,0:T(8,128)S(1)}, u32[]{:S(2)}, u32[]{:S(2)}) collective-permute-start(f32[2,16,128]{2,1,0:T(8,128)S(1)} %shard_map.87.rest_0_), channel_id=1, source_target_pairs={{0,4},{4,0},{8,12},{12,8},{1,5},{5,1},{9,13},{13,9},{2,6},{6,2},{1... | collective-permute-start | bytes 49160 | tf_op jit(solution)/shard_map/ppermute | solution.py:401

commit v5 on v4

--- a/solution.py
+++ b/solution.py
@@ -12,6 +12,7 @@
 ROWS = 8
 LANES = 128
 UNROLL = 4
+GROUP = ("gx", "gy", "gz")
 
 
 def call(kernel, outs, scratch=(), **more):
@@ -275,16 +276,9 @@
             pair = join(pair, tuple(pltpu.roll(v, step, 0) for v in pair))
         high = jnp.where(tall == j, jnp.concatenate([pair[0]] * 2, 0), high)
         low = jnp.where(tall == j, jnp.concatenate([pair[1]] * 2, 0), low)
-    moments[0] = high
-    moments[1] = low
-
-
-def add_kernel(*refs):
-    *ins, out = refs
-    total = (ins[0][0], ins[0][1])
-    for x in ins[1:]:
-        total = join(total, (x[0], x[1]))
-    out[0], out[1] = total
+    for copy in range(moments.shape[0]):
+        moments[copy, 0] = high
+        moments[copy, 1] = low
 
 
 def solve(total):
@@ -361,12 +355,13 @@
     return powers
 
 
-def final_kernel(rhs, powers, friction, ice, grounded, speed, *rest):
-    *parts, iterate, residual, hessian = rest
+def final_kernel(rhs, powers, friction, ice, grounded, speed, parts, iterate, residual, hessian):
     layers = rhs.shape[1]
-    total = (parts[0][0], parts[0][1])
-    for x in parts[1:]:
-        total = join(total, (x[0], x[1]))
+    terms = [(parts[i, 0], parts[i, 1]) for i in range(parts.shape[0])]
+    while len(terms) > 1:
+        pairs = [join(x, y) for x, y in zip(terms[::2], terms[1::2])]
+        terms = pairs + terms[2 * len(pairs) :]
+    (total,) = terms
     factors = [jnp.concatenate([c, c], 1) for c in solve(total)]
     for c in range(2):
         for k in range(layers):
@@ -381,28 +376,6 @@
             residual[c, k] = r - y
     weight = ice[...].astype(jnp.float32) * (friction[...] * grounded[...].astype(jnp.float32))
     hessian[...] = weight * (speed[0] * iterate[0, 0] + speed[1] * iterate[1, 0])
-
-
-def exchange(x, axis):
-    count = lax.axis_size(axis)
-    stride = 1
-    rounds = []
-    while stride < count:
-        size = 4 if (count // stride) % 4 == 0 else 2
-        rounds.append((stride, size))
-        stride *= size
-    for at, (stride, size) in enumerate(rounds):
-        parts = [x]
-        for turn in range(1, size):
-            pairs = []
-            for i in range(count):
-                place = (i // stride) % size
-                pairs.append((i, i + ((place ^ turn) - place) * stride))
-            parts.append(lax.ppermute(x, axis, pairs))
-        if at == len(rounds) - 1:
-            return parts
-        x = call(add_kernel, [x.shape])(*parts)[0]
-    return [x]
 
 
 def body(adjoint_rhs, viscosity, friction, ice_mask, grounded, basal_velocity):
@@ -423,17 +396,14 @@
     block = (layers, 2 * ROWS, 3 * LANES)
     powers, sums = call(
         power_kernel,
-        [(STEPS,) + adjoint_rhs.shape, (2, 2 * ROWS, LANES)],
+        [(STEPS,) + adjoint_rhs.shape, (lax.axis_size(GROUP), 2, 2 * ROWS, LANES)],
         [(2,) + block] * 2 + [block] * 4 + [block[1:]] * 2,
     )(*held[:5], strip_a, strip_b, columns, columns_a, columns_b)
-    parts = exchange(sums, ("gy", "gz"))
-    if len(parts) > 1:
-        sums = call(add_kernel, [sums.shape])(*parts)[0]
-    parts = exchange(sums, "gx")
+    parts = lax.all_to_all(sums, GROUP, 0, 0)
     rhs, _, friction, ice_mask, grounded, speed = held
     return tuple(
         call(final_kernel, [adjoint_rhs.shape, adjoint_rhs.shape, friction.shape])(
-            rhs, powers, friction, ice_mask, grounded, speed, *parts
+            rhs, powers, friction, ice_mask, grounded, speed, parts
         )
     )
 

time: 38.2 us -> 42.8 us (1.12)
  blocking collectives: 0 us -> 19.4 us
  starting transfers between devices: 20.8 us -> 10.9 us
  waiting for transfers between devices: 7.17 us -> 2.22 us
    all_to_all x0 -> x1, blocking collectives: none -> 19.4 us  [body(): parts = lax.all_to_all(sums, GROUP, 0, 0)]
    ppermute x6 -> x0, starting transfers between devices: 9.92 us -> none  [exchange(): parts.append(lax.ppermute(x, axis, pairs))]
    ppermute x6 -> x0, waiting for transfers between devices: 4.95 us -> none  [exchange(): parts.append(lax.ppermute(x, axis, pairs))]
    pallas_call x2 -> x1, Pallas kernels: 6.47 us -> 6.45 us  [body(): call(power_kernel, [(STEPS,) + adjoint_rhs.shape, (lax.axis_size(GROUP),...]
  transfers between devices with their start and end apart: 12 -> 6, of which waited for: 5 -> 2; matrix products, arithmetic and copies ran while one was open for 0% -> 0% of each run, Pallas kernels for 0% -> 0%
where the time goes in v5:
time: 42.8 us; the launch traced here: 42.5 us
  blocking collectives  19.4 us (45%)
  starting transfers between devices  10.9 us (25%)
  Pallas kernels  9.36 us (22%)
  waiting for transfers between devices  2.22 us (5%)
  between operations  0.69 us (2%)
    all_to_all x1, blocking collectives, body(): parts = lax.all_to_all(sums, GROUP, 0, 0)  19.4 us
    ppermute x6, starting transfers between devices, swapped(): return lax.ppermute(x, axis, pairs)  10.9 us
    pallas_call x1, Pallas kernels, body(): call(power_kernel, [(STEPS,) + adjoint_rhs.shape, (lax.axis_size(GROUP),...  6.45 us
    ppermute x6, waiting for transfers between devices, swapped(): return lax.ppermute(x, axis, pairs)  2.22 us
    pallas_call x1, Pallas kernels, body(): call(final_kernel, [adjoint_rhs.shape, adjoint_rhs.shape, friction.shape])  1.63 us
    pallas_call x1, Pallas kernels, body(): call(pack_kernel, [jax.ShapeDtypeStruct(x.shape, x.dtype) for x in inputs...  1.28 us
  transfers between devices with their start and end apart: 6, of which 2 were waited for; matrix products, arithmetic and copies ran while one was open for 0% of the time, Pallas kernels for 0%

profile of v5, /device:TPU:0, one launch (start us, length us, event | category | flops | bytes accessed | tf_op | source)
XLA Modules:
  0.0 42.5 jit_solution(14128292468502788662)
XLA Ops:
  0.6 1.3 %shard_map.85 = (f32[2,20,8,256]{3,2,1,0:T(8,128)S(1)}, f32[20,8,256]{2,1,0:T(8,128)S(1)}, f32[8,256]{1,0:T(8,128)S(1)}, s32[8,256]{1,0:T(8,128)S(1)}, s32[8,256...) custom-call(f32[2,20,8,256]{3,2,1,0:T(8,128)} %refs_0_.1, ...), custom_call_target="tpu_custom_call" | custom-call | tf_op jit(solution)/shard_map/pallas_call | solution.py:386
  1.9 3.1 %collective-permute-start = (f32[62,8,128]{2,1,0:T(8,128)S(1)}, f32[62,8,128]{2,1,0:T(8,128)S(1)}, u32[]{:S(2)}, u32[]{:S(2)}) collective-permute-start(f32[62,8,128]{2,1,0:T(8,128)S(1)} %get-tuple-element.20), channel_id=1, source_target_pairs={{0,4},{4,0},{8,12},{12,8},{1,5},{5,1},{9,13},{13,9},{2,6},{6,2},{1... | collective-permute-start | bytes 761864 | tf_op jit(solution)/shard_map/ppermute | solution.py:42
  5.0 0.7 %collective-permute-start.1 = (f32[62,8,128]{2,1,0:T(8,128)S(1)}, f32[62,8,128]{2,1,0:T(8,128)S(1)}, u32[]{:S(2)}, u32[]{:S(2)}) collective-permute-start(f32[62,8,128]{2,1,0:T(8,128)S(1)} %get-tuple-element.21), channel_id=1, source_target_pairs={{0,0},{4,8},{8,4},{12,12},{1,1},{5,9},{9,5},{13,13},{2,2},{6,10},{... | collective-permute-start | bytes 761864 | tf_op jit(solution)/shard_map/ppermute | solution.py:42
  5.7 0.1 collective-permute-start.2
  5.8 0.7 %collective-permute-start.3 = (f32[2,8,128]{2,1,0:T(8,128)S(1)}, f32[2,8,128]{2,1,0:T(8,128)S(1)}, u32[]{:S(2)}, u32[]{:S(2)}) collective-permute-start(f32[2,8,128]{2,1,0:T(8,128)S(1)} %get-tuple-element.23), channel_id=1, source_target_pairs={{0,0},{1,2},{2,1},{3,3},{4,4},{5,6},{6,5},{7,7},{8,8},{9,10},{10,9... | collective-permute-start | bytes 24584 | tf_op jit(solution)/shard_map/ppermute | solution.py:42
  6.4 0.5 %collective-permute-done.2 = f32[2,8,128]{2,1,0:T(8,128)S(1)} collective-permute-done((f32[2,8,128]{2,1,0:T(8,128)S(1)}, f32[2,8,128]{2,1,0:T(8,128)S(1)}, u32[]{:S(2)}, u32[]{:S(2)}) %collective-permute-start.2) | collective-permute-done | bytes 8224 | tf_op jit(solution)/shard_map/ppermute | solution.py:42
  6.9 0.0 collective-permute-done.3
  6.9 0.7 %collective-permute-start.5 = (f32[4,8,128]{2,1,0:T(8,128)S(1)}, f32[4,8,128]{2,1,0:T(8,128)S(1)}, u32[]{:S(2)}, u32[]{:S(2)}) collective-permute-start(f32[4,8,128]{2,1,0:T(8,128)S(1)} %constant_dynamic-update-slice_fusion.columns), channel_id=1, source_target_pairs={{0,0},{4,8},{8,4},{12,12},{1,1},{5,9},{9,5},{13,13},{2,2},{6,10},{... | collective-permute-start | bytes 49160 | tf_op jit(solution)/shard_map/ppermute | solution.py:42
  7.6 5.7 %collective-permute-start.4 = (f32[4,8,128]{2,1,0:T(8,128)S(1)}, f32[4,8,128]{2,1,0:T(8,128)S(1)}, u32[]{:S(2)}, u32[]{:S(2)}) collective-permute-start(f32[4,8,128]{2,1,0:T(8,128)S(1)} %constant_dynamic-update-slice_fusion.columns), channel_id=1, source_target_pairs={{0,4},{4,0},{8,12},{12,8},{1,5},{5,1},{9,13},{13,9},{2,6},{6,2},{1... | collective-permute-start | bytes 49160 | tf_op jit(solution)/shard_map/ppermute | solution.py:42
  13.3 0.0 collective-permute-done.5.columns_b
  13.3 1.7 %collective-permute-done.4.columns_a = f32[4,8,128]{2,1,0:T(8,128)S(1)} collective-permute-done((f32[4,8,128]{2,1,0:T(8,128)S(1)}, f32[4,8,128]{2,1,0:T(8,128)S(1)}, u32[]{:S(2)}, u32[]{:S(2)}) %collective-permute-start.4) | collective-permute-done | bytes 16416 | tf_op jit(solution)/shard_map/ppermute | solution.py:42
  15.0 0.0 collective-permute-done.strip_a
  15.0 0.0 collective-permute-done.1.strip_b
  15.0 6.5 %shard_map.86 = (f32[4,2,20,8,256]{4,3,2,1,0:T(8,128)S(1)}, f32[16,2,16,128]{3,2,1,0:T(8,128)S(1)}) custom-call(f32[2,20,8,256]{3,2,1,0:T(8,128)S(1)} %get-tuple-element.15.rhs, f32[20,8,256]{2,1,0:T(8,128)S(1)} %get-tuple-element.16.eta, f32[8,256]{1,0:T(8,128)S(1)} %get-tuple-element.17.friction, s32[8,256]{1,0:T(8,128)S(1)} %get-tuple-element.18.ice, ...), custom_call_target="tpu_custom_call" | custom-call | tf_op jit(solution)/shard_map/pallas_call | solution.py:397
  21.5 19.4 %all_to_all.5.parts = f32[16,2,16,128]{3,2,1,0:T(8,128)S(1)} all-to-all(f32[16,2,16,128]{3,2,1,0:T(8,128)S(1)} %get-tuple-element.26), channel_id=1, replica_groups=mesh['parts'=2,'gx'=4,'gy'=2,'gz'=2] {'gx','gy','gz'}, dimensions={0} | all-to-all | bytes 524288 | tf_op jit(solution)/shard_map/all_to_all | solution.py:402
  40.9 1.6 %shard_map.87 = (f32[2,20,8,256]{3,2,1,0:T(8,128)}, f32[2,20,8,256]{3,2,1,0:T(8,128)}, f32[8,256]{1,0:T(8,128)}) custom-call(f32[2,20,8,256]{3,2,1,0:T(8,128)S(1)} %get-tuple-element.15.rhs, f32[4,2,20,8,256]{4,3,2,1,0:T(8,128)S(1)} %get-tuple-element.24.powers, f32[8,256]{1,0:T(8,128)S(1)} %get-tuple-element.17.friction, ...), custom_call_target="tpu_custom_call" | custom-call | tf_op jit(solution)/shard_map/pallas_call | solution.py:405
  (2 shorter events, 0.0 us)
Async XLA Ops:
  1.9 13.1 %collective-permute-start = (f32[62,8,128]{2,1,0:T(8,128)S(1)}, f32[62,8,128]{2,1,0:T(8,128)S(1)}, u32[]{:S(2)}, u32[]{:S(2)}) collective-permute-start(f32[62,8,128]{2,1,0:T(8,128)S(1)} %get-tuple-element.20), channel_id=1, source_target_pairs={{0,4},{4,0},{8,12},{12,8},{1,5},{5,1},{9,13},{13,9},{2,6},{6,2},{1... | collective-permute-start | bytes 761864 | tf_op jit(solution)/shard_map/ppermute | solution.py:42
  5.0 10.0 %collective-permute-start.1 = (f32[62,8,128]{2,1,0:T(8,128)S(1)}, f32[62,8,128]{2,1,0:T(8,128)S(1)}, u32[]{:S(2)}, u32[]{:S(2)}) collective-permute-start(f32[62,8,128]{2,1,0:T(8,128)S(1)} %get-tuple-element.21), channel_id=1, source_target_pairs={{0,0},{4,8},{8,4},{12,12},{1,1},{5,9},{9,5},{13,13},{2,2},{6,10},{... | collective-permute-start | bytes 761864 | tf_op jit(solution)/shard_map/ppermute | solution.py:42
  5.7 1.2 %collective-permute-start.2 = (f32[2,8,128]{2,1,0:T(8,128)S(1)}, f32[2,8,128]{2,1,0:T(8,128)S(1)}, u32[]{:S(2)}, u32[]{:S(2)}) collective-permute-start(f32[2,8,128]{2,1,0:T(8,128)S(1)} %get-tuple-element.22), channel_id=1, source_target_pairs={{0,1},{1,0},{2,3},{3,2},{4,5},{5,4},{6,7},{7,6},{8,9},{9,8},{10,11... | collective-permute-start | bytes 24584 | tf_op jit(solution)/shard_map/ppermute | solution.py:42
  5.8 1.2 %collective-permute-start.3 = (f32[2,8,128]{2,1,0:T(8,128)S(1)}, f32[2,8,128]{2,1,0:T(8,128)S(1)}, u32[]{:S(2)}, u32[]{:S(2)}) collective-permute-start(f32[2,8,128]{2,1,0:T(8,128)S(1)} %get-tuple-element.23), channel_id=1, source_target_pairs={{0,0},{1,2},{2,1},{3,3},{4,4},{5,6},{6,5},{7,7},{8,8},{9,10},{10,9... | collective-permute-start | bytes 24584 | tf_op jit(solution)/shard_map/ppermute | solution.py:42
  6.9 6.4 %collective-permute-start.5 = (f32[4,8,128]{2,1,0:T(8,128)S(1)}, f32[4,8,128]{2,1,0:T(8,128)S(1)}, u32[]{:S(2)}, u32[]{:S(2)}) collective-permute-start(f32[4,8,128]{2,1,0:T(8,128)S(1)} %constant_dynamic-update-slice_fusion.columns), channel_id=1, source_target_pairs={{0,0},{4,8},{8,4},{12,12},{1,1},{5,9},{9,5},{13,13},{2,2},{6,10},{... | collective-permute-start | bytes 49160 | tf_op jit(solution)/shard_map/ppermute | solution.py:42
  7.6 7.4 %collective-permute-start.4 = (f32[4,8,128]{2,1,0:T(8,128)S(1)}, f32[4,8,128]{2,1,0:T(8,128)S(1)}, u32[]{:S(2)}, u32[]{:S(2)}) collective-permute-start(f32[4,8,128]{2,1,0:T(8,128)S(1)} %constant_dynamic-update-slice_fusion.columns), channel_id=1, source_target_pairs={{0,4},{4,0},{8,12},{12,8},{1,5},{5,1},{9,13},{13,9},{2,6},{6,2},{1... | collective-permute-start | bytes 49160 | tf_op jit(solution)/shard_map/ppermute | solution.py:42

commit v6 on v5

--- a/solution.py
+++ b/solution.py
@@ -276,9 +276,8 @@
             pair = join(pair, tuple(pltpu.roll(v, step, 0) for v in pair))
         high = jnp.where(tall == j, jnp.concatenate([pair[0]] * 2, 0), high)
         low = jnp.where(tall == j, jnp.concatenate([pair[1]] * 2, 0), low)
-    for copy in range(moments.shape[0]):
-        moments[copy, 0] = high
-        moments[copy, 1] = low
+    moments[0] = high
+    moments[1] = low
 
 
 def solve(total):
@@ -396,10 +395,10 @@
     block = (layers, 2 * ROWS, 3 * LANES)
     powers, sums = call(
         power_kernel,
-        [(STEPS,) + adjoint_rhs.shape, (lax.axis_size(GROUP), 2, 2 * ROWS, LANES)],
+        [(STEPS,) + adjoint_rhs.shape, (2, 2 * ROWS, LANES)],
         [(2,) + block] * 2 + [block] * 4 + [block[1:]] * 2,
     )(*held[:5], strip_a, strip_b, columns, columns_a, columns_b)
-    parts = lax.all_to_all(sums, GROUP, 0, 0)
+    parts = lax.all_gather(sums, GROUP)
     rhs, _, friction, ice_mask, grounded, speed = held
     return tuple(
         call(final_kernel, [adjoint_rhs.shape, adjoint_rhs.shape, friction.shape])(

time: 42.8 us -> 48.8 us (1.14)
  blocking collectives: 19.4 us -> 25.4 us
    all_gather x0 -> x1, blocking collectives: none -> 25.4 us  [body(): parts = lax.all_gather(sums, GROUP)]
    all_to_all x1 -> x0, blocking collectives: 19.4 us -> none  [body(): parts = lax.all_to_all(sums, GROUP, 0, 0)]
where the time goes in v6:
time: 48.8 us; the launch traced here: 48.5 us
  blocking collectives  25.4 us (52%)
  starting transfers between devices  10.9 us (22%)
  Pallas kernels  9.35 us (19%)
  waiting for transfers between devices  2.22 us (5%)
  between operations  0.68 us (1%)
    all_gather x1, blocking collectives, body(): parts = lax.all_gather(sums, GROUP)  25.4 us
    ppermute x6, starting transfers between devices, swapped(): return lax.ppermute(x, axis, pairs)  10.9 us
    pallas_call x1, Pallas kernels, body(): call(power_kernel, [(STEPS,) + adjoint_rhs.shape, (2, 2 * ROWS, LANES)],...  6.44 us
    ppermute x6, waiting for transfers between devices, swapped(): return lax.ppermute(x, axis, pairs)  2.22 us
    pallas_call x1, Pallas kernels, body(): call(final_kernel, [adjoint_rhs.shape, adjoint_rhs.shape, friction.shape])  1.63 us
    pallas_call x1, Pallas kernels, body(): call(pack_kernel, [jax.ShapeDtypeStruct(x.shape, x.dtype) for x in inputs...  1.28 us
  transfers between devices with their start and end apart: 6, of which 2 were waited for; matrix products, arithmetic and copies ran while one was open for 0% of the time, Pallas kernels for 0%

profile of v6, /device:TPU:0, one launch (start us, length us, event | category | flops | bytes accessed | tf_op | source)
XLA Modules:
  0.0 48.5 jit_solution(11998446849323175389)
XLA Ops:
  0.6 1.3 %shard_map.85 = (f32[2,20,8,256]{3,2,1,0:T(8,128)S(1)}, f32[20,8,256]{2,1,0:T(8,128)S(1)}, f32[8,256]{1,0:T(8,128)S(1)}, s32[8,256]{1,0:T(8,128)S(1)}, s32[8,256...) custom-call(f32[2,20,8,256]{3,2,1,0:T(8,128)} %refs_0_.1, ...), custom_call_target="tpu_custom_call" | custom-call | tf_op jit(solution)/shard_map/pallas_call | solution.py:385
  1.9 3.1 %collective-permute-start = (f32[62,8,128]{2,1,0:T(8,128)S(1)}, f32[62,8,128]{2,1,0:T(8,128)S(1)}, u32[]{:S(2)}, u32[]{:S(2)}) collective-permute-start(f32[62,8,128]{2,1,0:T(8,128)S(1)} %get-tuple-element.20), channel_id=1, source_target_pairs={{0,4},{4,0},{8,12},{12,8},{1,5},{5,1},{9,13},{13,9},{2,6},{6,2},{1... | collective-permute-start | bytes 761864 | tf_op jit(solution)/shard_map/ppermute | solution.py:42
  5.0 0.7 %collective-permute-start.1 = (f32[62,8,128]{2,1,0:T(8,128)S(1)}, f32[62,8,128]{2,1,0:T(8,128)S(1)}, u32[]{:S(2)}, u32[]{:S(2)}) collective-permute-start(f32[62,8,128]{2,1,0:T(8,128)S(1)} %get-tuple-element.21), channel_id=1, source_target_pairs={{0,0},{4,8},{8,4},{12,12},{1,1},{5,9},{9,5},{13,13},{2,2},{6,10},{... | collective-permute-start | bytes 761864 | tf_op jit(solution)/shard_map/ppermute | solution.py:42
  5.7 0.1 collective-permute-start.2
  5.8 0.7 %collective-permute-start.3 = (f32[2,8,128]{2,1,0:T(8,128)S(1)}, f32[2,8,128]{2,1,0:T(8,128)S(1)}, u32[]{:S(2)}, u32[]{:S(2)}) collective-permute-start(f32[2,8,128]{2,1,0:T(8,128)S(1)} %get-tuple-element.23), channel_id=1, source_target_pairs={{0,0},{1,2},{2,1},{3,3},{4,4},{5,6},{6,5},{7,7},{8,8},{9,10},{10,9... | collective-permute-start | bytes 24584 | tf_op jit(solution)/shard_map/ppermute | solution.py:42
  6.4 0.5 %collective-permute-done.2 = f32[2,8,128]{2,1,0:T(8,128)S(1)} collective-permute-done((f32[2,8,128]{2,1,0:T(8,128)S(1)}, f32[2,8,128]{2,1,0:T(8,128)S(1)}, u32[]{:S(2)}, u32[]{:S(2)}) %collective-permute-start.2) | collective-permute-done | bytes 8224 | tf_op jit(solution)/shard_map/ppermute | solution.py:42
  6.9 0.0 collective-permute-done.3
  6.9 0.7 %collective-permute-start.5 = (f32[4,8,128]{2,1,0:T(8,128)S(1)}, f32[4,8,128]{2,1,0:T(8,128)S(1)}, u32[]{:S(2)}, u32[]{:S(2)}) collective-permute-start(f32[4,8,128]{2,1,0:T(8,128)S(1)} %constant_dynamic-update-slice_fusion.columns), channel_id=1, source_target_pairs={{0,0},{4,8},{8,4},{12,12},{1,1},{5,9},{9,5},{13,13},{2,2},{6,10},{... | collective-permute-start | bytes 49160 | tf_op jit(solution)/shard_map/ppermute | solution.py:42
  7.6 5.7 %collective-permute-start.4 = (f32[4,8,128]{2,1,0:T(8,128)S(1)}, f32[4,8,128]{2,1,0:T(8,128)S(1)}, u32[]{:S(2)}, u32[]{:S(2)}) collective-permute-start(f32[4,8,128]{2,1,0:T(8,128)S(1)} %constant_dynamic-update-slice_fusion.columns), channel_id=1, source_target_pairs={{0,4},{4,0},{8,12},{12,8},{1,5},{5,1},{9,13},{13,9},{2,6},{6,2},{1... | collective-permute-start | bytes 49160 | tf_op jit(solution)/shard_map/ppermute | solution.py:42
  13.3 0.0 collective-permute-done.5.columns_b
  13.3 1.7 %collective-permute-done.4.columns_a = f32[4,8,128]{2,1,0:T(8,128)S(1)} collective-permute-done((f32[4,8,128]{2,1,0:T(8,128)S(1)}, f32[4,8,128]{2,1,0:T(8,128)S(1)}, u32[]{:S(2)}, u32[]{:S(2)}) %collective-permute-start.4) | collective-permute-done | bytes 16416 | tf_op jit(solution)/shard_map/ppermute | solution.py:42
  15.0 0.0 collective-permute-done.strip_a
  15.0 0.0 collective-permute-done.1.strip_b
  15.0 6.4 %shard_map.86 = (f32[4,2,20,8,256]{4,3,2,1,0:T(8,128)S(1)}, f32[2,16,128]{2,1,0:T(8,128)S(1)}) custom-call(f32[2,20,8,256]{3,2,1,0:T(8,128)S(1)} %get-tuple-element.15.rhs, f32[20,8,256]{2,1,0:T(8,128)S(1)} %get-tuple-element.16.eta, f32[8,256]{1,0:T(8,128)S(1)} %get-tuple-element.17.friction, s32[8,256]{1,0:T(8,128)S(1)} %get-tuple-element.18.ice, ...), custom_call_target="tpu_custom_call" | custom-call | tf_op jit(solution)/shard_map/pallas_call | solution.py:396
  21.5 25.4 %all-gather = f32[32,16,128]{2,1,0:T(8,128)S(1)} all-gather(f32[2,16,128]{2,1,0:T(8,128)S(1)} %get-tuple-element.26), channel_id=2, replica_groups=mesh['parts'=2,'gx'=4,'gy'=2,'gz'=2] {'gx','gy','gz'}, dimensions={0}, use_global_device_ids=true | all-gather | bytes 278528 | tf_op jit(solution)/shard_map/all_gather | solution.py:401
  46.9 1.6 %shard_map.87 = (f32[2,20,8,256]{3,2,1,0:T(8,128)}, f32[2,20,8,256]{3,2,1,0:T(8,128)}, f32[8,256]{1,0:T(8,128)}) custom-call(f32[2,20,8,256]{3,2,1,0:T(8,128)S(1)} %get-tuple-element.15.rhs, f32[4,2,20,8,256]{4,3,2,1,0:T(8,128)S(1)} %get-tuple-element.24.powers, f32[8,256]{1,0:T(8,128)S(1)} %get-tuple-element.17.friction, ...), custom_call_target="tpu_custom_call" | custom-call | tf_op jit(solution)/shard_map/pallas_call | solution.py:404
  (2 shorter events, 0.0 us)
Async XLA Ops:
  1.9 13.1 %collective-permute-start = (f32[62,8,128]{2,1,0:T(8,128)S(1)}, f32[62,8,128]{2,1,0:T(8,128)S(1)}, u32[]{:S(2)}, u32[]{:S(2)}) collective-permute-start(f32[62,8,128]{2,1,0:T(8,128)S(1)} %get-tuple-element.20), channel_id=1, source_target_pairs={{0,4},{4,0},{8,12},{12,8},{1,5},{5,1},{9,13},{13,9},{2,6},{6,2},{1... | collective-permute-start | bytes 761864 | tf_op jit(solution)/shard_map/ppermute | solution.py:42
  5.0 10.0 %collective-permute-start.1 = (f32[62,8,128]{2,1,0:T(8,128)S(1)}, f32[62,8,128]{2,1,0:T(8,128)S(1)}, u32[]{:S(2)}, u32[]{:S(2)}) collective-permute-start(f32[62,8,128]{2,1,0:T(8,128)S(1)} %get-tuple-element.21), channel_id=1, source_target_pairs={{0,0},{4,8},{8,4},{12,12},{1,1},{5,9},{9,5},{13,13},{2,2},{6,10},{... | collective-permute-start | bytes 761864 | tf_op jit(solution)/shard_map/ppermute | solution.py:42
  5.7 1.2 %collective-permute-start.2 = (f32[2,8,128]{2,1,0:T(8,128)S(1)}, f32[2,8,128]{2,1,0:T(8,128)S(1)}, u32[]{:S(2)}, u32[]{:S(2)}) collective-permute-start(f32[2,8,128]{2,1,0:T(8,128)S(1)} %get-tuple-element.22), channel_id=1, source_target_pairs={{0,1},{1,0},{2,3},{3,2},{4,5},{5,4},{6,7},{7,6},{8,9},{9,8},{10,11... | collective-permute-start | bytes 24584 | tf_op jit(solution)/shard_map/ppermute | solution.py:42
  5.8 1.2 %collective-permute-start.3 = (f32[2,8,128]{2,1,0:T(8,128)S(1)}, f32[2,8,128]{2,1,0:T(8,128)S(1)}, u32[]{:S(2)}, u32[]{:S(2)}) collective-permute-start(f32[2,8,128]{2,1,0:T(8,128)S(1)} %get-tuple-element.23), channel_id=1, source_target_pairs={{0,0},{1,2},{2,1},{3,3},{4,4},{5,6},{6,5},{7,7},{8,8},{9,10},{10,9... | collective-permute-start | bytes 24584 | tf_op jit(solution)/shard_map/ppermute | solution.py:42
  6.9 6.4 %collective-permute-start.5 = (f32[4,8,128]{2,1,0:T(8,128)S(1)}, f32[4,8,128]{2,1,0:T(8,128)S(1)}, u32[]{:S(2)}, u32[]{:S(2)}) collective-permute-start(f32[4,8,128]{2,1,0:T(8,128)S(1)} %constant_dynamic-update-slice_fusion.columns), channel_id=1, source_target_pairs={{0,0},{4,8},{8,4},{12,12},{1,1},{5,9},{9,5},{13,13},{2,2},{6,10},{... | collective-permute-start | bytes 49160 | tf_op jit(solution)/shard_map/ppermute | solution.py:42
  7.6 7.4 %collective-permute-start.4 = (f32[4,8,128]{2,1,0:T(8,128)S(1)}, f32[4,8,128]{2,1,0:T(8,128)S(1)}, u32[]{:S(2)}, u32[]{:S(2)}) collective-permute-start(f32[4,8,128]{2,1,0:T(8,128)S(1)} %constant_dynamic-update-slice_fusion.columns), channel_id=1, source_target_pairs={{0,4},{4,0},{8,12},{12,8},{1,5},{5,1},{9,13},{13,9},{2,6},{6,2},{1... | collective-permute-start | bytes 49160 | tf_op jit(solution)/shard_map/ppermute | solution.py:42

commit v7 on v4

--- a/solution.py
+++ b/solution.py
@@ -11,7 +11,8 @@
 HALO = 4
 ROWS = 8
 LANES = 128
-UNROLL = 4
+UNROLL = 5
+SLOT = 32
 
 
 def call(kernel, outs, scratch=(), **more):
@@ -62,6 +63,27 @@
     if q < layers + layers // 2:
         return q + layers, q + layers + layers // 2
     return 3 * layers, 3 * layers + 1
+
+
+def ribbon_places(p, layers):
+    tiles = layers // 4
+    if p < 3 * layers:
+        k = p % layers
+        return p // layers * tiles + k % tiles, (k // tiles,)
+    return (3 * tiles, (0, 1, 2, 3)) if p == 3 * layers else (3 * tiles + 1, (0,))
+
+
+def ribbon_tiles(layers):
+    return 3 * (layers // 4) + 2
+
+
+def between(lane, first, width):
+    return (lane >= first) & (lane < first + width)
+
+
+def turned(v, shift):
+    shift = shift % LANES
+    return pltpu.roll(v, shift, 1) if shift else v
 
 
 def pack_kernel(*refs):
@@ -79,10 +101,10 @@
     rows_even, _, _ = place_of("gx")
     columns_even, _, _ = place_of(("gy", "gz"))
     upper_a = (row < HALO) != rows_even
-    width = strip_a.shape[0]
-    left = [jnp.zeros((ROWS, LANES), jnp.float32) for _ in range(2)]
-    right = [jnp.zeros((ROWS, LANES), jnp.float32) for _ in range(2)]
-    for q in range(width // 2):
+    count = column_a.shape[0]
+    left = [jnp.zeros((ROWS, LANES), jnp.float32) for _ in range(count)]
+    right = [jnp.zeros((ROWS, LANES), jnp.float32) for _ in range(count)]
+    for q in range(strip_a.shape[0] // 2):
         first, second = pair_of(q, layers)
         x, y = plane(first), plane(second)
         for half in range(2):
@@ -92,15 +114,20 @@
             strip_a[2 * q + half] = jnp.where(upper_a, xs, ys)
             strip_b[2 * q + half] = jnp.where(upper_a, ys, xs)
         for p, v in ((first, x), (second, y)):
-            group, place = p // 32, HALO * (p % 32)
-            mine = (lane >= place) & (lane < place + HALO)
-            head, tail = v[:, :LANES], v[:, LANES:]
-            shift = (place + HALO) % LANES
-            left[group] = jnp.where(mine, pltpu.roll(head, place, 1) if place else head, left[group])
-            right[group] = jnp.where(mine, pltpu.roll(tail, shift, 1) if shift else tail, right[group])
-    for group in range(2):
-        column_a[group] = jnp.where(columns_even, right[group], left[group])
-        column_b[group] = jnp.where(columns_even, left[group], right[group])
+            tile, slots = ribbon_places(p, layers)
+            for slot in slots:
+                at = slot * SLOT
+                left[tile] = jnp.where(between(lane, at + 8, 4), turned(v[:, :LANES], at + 8), left[tile])
+                right[tile] = jnp.where(between(lane, at + 16, 4), turned(v[:, LANES:], at + 20), right[tile])
+    for tile in range(count):
+        column_a[tile] = jnp.where(columns_even, right[tile], left[tile])
+        column_b[tile] = jnp.where(columns_even, left[tile], right[tile])
+
+
+def beside_kernel(from_a, from_b, columns):
+    _, has_a, has_b = place_of(("gy", "gz"))
+    for tile in range(columns.shape[0]):
+        columns[tile] = jnp.where(has_a, from_a[tile], 0.0) + jnp.where(has_b, from_b[tile], 0.0)
 
 
 def two_sum(a, b):
@@ -129,48 +156,59 @@
     return p, e + scalar * x[1]
 
 
-def power_kernel(
-    rhs, eta, friction, ice, grounded, strip_a, strip_b, columns, columns_a, columns_b,
-    powers, moments,
+def beyond():
+    even, has_a, has_b = place_of("gx")
+    upper_a = (lax.broadcasted_iota(jnp.int32, (ROWS, LANES), 0) < HALO) == even
+
+    def below_and_above(from_a, from_b):
+        return jnp.where(upper_a, jnp.where(has_a, from_a, 0.0), jnp.where(has_b, from_b, 0.0))
+
+    def above_and_below(from_a, from_b):
+        return jnp.where(upper_a, jnp.where(has_b, from_b, 0.0), jnp.where(has_a, from_a, 0.0))
+
+    return below_and_above, above_and_below
+
+
+def row_next(v):
+    return pltpu.roll(v, 2 * ROWS - 1, 0)
+
+
+def row_prev(v):
+    return pltpu.roll(v, 1, 0)
+
+
+def col_next(v):
+    return pltpu.roll(v, v.shape[1] - 1, 1)
+
+
+def col_prev(v):
+    return pltpu.roll(v, 1, 1)
+
+
+def horizontal(g0, g1, e_row, e_col, e_half):
+    g0n, g1n = row_next(g0), col_next(g1)
+    f = e_half * (g1n - col_prev(g1))
+    h = e_half * (g0n - row_prev(g0))
+    flux = e_row * (g0 - g0n)
+    out0 = flux - row_next(f) - row_prev(flux - f)
+    flux = e_col * (g0 - col_next(g0))
+    out0 = out0 + (flux - col_prev(flux))
+    flux = (4.0 * e_col) * (g1 - g1n)
+    out1 = flux - col_next(h) - col_prev(flux - h)
+    flux = (0.25 * e_row) * (g1 - row_next(g1))
+    out1 = out1 + (flux - row_prev(flux))
+    return out0, out1
+
+
+def main_kernel(
+    rhs, eta, friction, ice, grounded, strip_a, strip_b,
+    powers, sums, ribbon,
     field_a, field_b, eta_row, eta_col, eta_half, eta_up, cover, drag,
 ):
     layers = eta.shape[0]
     plane = own_planes(rhs, eta, friction, ice, grounded)
-    lane = lax.broadcasted_iota(jnp.int32, (ROWS, LANES), 1)
-    row = lax.broadcasted_iota(jnp.int32, (ROWS, LANES), 0)
-    strips = strip_a.shape[0]
-    even, has_a, has_b = place_of("gx")
-    upper_a = (row < HALO) == even
-
-    def below_and_above(from_a, from_b):
-        return jnp.where(upper_a, jnp.where(has_a, from_a, 0.0), jnp.where(has_b, from_b, 0.0))
-
-    def above_and_below(from_a, from_b):
-        return jnp.where(upper_a, jnp.where(has_b, from_b, 0.0), jnp.where(has_a, from_a, 0.0))
-
-    even, came_a, came_b = place_of(("gy", "gz"))
-
-    def right_and_left(tiles):
-        from_a = [jnp.where(came_a, tiles[t], 0.0) for t in (0, 1)]
-        from_b = [jnp.where(came_b, tiles[t], 0.0) for t in (2, 3)]
-        right = [jnp.where(even, x, y) for x, y in zip(from_a, from_b)]
-        left = [jnp.where(even, y, x) for x, y in zip(from_a, from_b)]
-        return right + left
-
-    corner = right_and_left([below_and_above(columns_a[t], columns_b[t]) for t in range(4)])
-    beside = right_and_left([columns[t] for t in range(4)])
-
-    def side(tiles, p):
-        group, place = p // 32, HALO * (p % 32)
-        a, b = (LANES - place) % LANES, LANES - place - HALO
-        right = pltpu.roll(tiles[group], a, 1) if a else tiles[group]
-        left = pltpu.roll(tiles[2 + group], b, 1) if b else tiles[2 + group]
-        return jnp.where(lane < HALO, right, jnp.where(lane >= LANES - HALO, left, 0.0))
-
-    def fill(p, dst):
-        dst[0:ROWS, 0 : 2 * LANES] = plane(p)
-        dst[0:ROWS, 2 * LANES :] = side(beside, p)
-        dst[ROWS:, 2 * LANES :] = side(corner, p)
+    below_and_above, above_and_below = beyond()
+    lane = lax.broadcasted_iota(jnp.int32, (2 * ROWS, LANES), 1)
 
     def target(p):
         if p < 2 * layers:
@@ -179,27 +217,28 @@
             return eta_half.at[p - 2 * layers]
         return cover if p == 3 * layers else drag
 
-    for q in range(strips // 2):
+    strips = [jnp.zeros((2 * ROWS, LANES), jnp.float32) for _ in range(ribbon.shape[0])]
+    for q in range(strip_a.shape[0] // 2):
         first, second = pair_of(q, layers)
+        halves = ([], [])
         for half in range(2):
             from_a, from_b = strip_a[2 * q + half], strip_b[2 * q + half]
-            cut = slice(half * LANES, (half + 1) * LANES)
-            target(first)[ROWS:, cut] = below_and_above(from_a, from_b)
-            target(second)[ROWS:, cut] = pltpu.roll(above_and_below(from_a, from_b), HALO, 0)
-        fill(first, target(first))
-        fill(second, target(second))
-
-    def row_next(v):
-        return pltpu.roll(v, 2 * ROWS - 1, 0)
-
-    def row_prev(v):
-        return pltpu.roll(v, 1, 0)
-
-    def col_next(v):
-        return pltpu.roll(v, 3 * LANES - 1, 1)
-
-    def col_prev(v):
-        return pltpu.roll(v, 1, 1)
+            halves[0].append(below_and_above(from_a, from_b))
+            halves[1].append(pltpu.roll(above_and_below(from_a, from_b), HALO, 0))
+        for p, halo in zip((first, second), halves):
+            v = plane(p)
+            dst = target(p)
+            dst[0:ROWS, :] = v
+            dst[ROWS:, 0:LANES], dst[ROWS:, LANES:] = halo
+            head = jnp.concatenate([v[:, :LANES], halo[0]], 0)
+            tail = jnp.concatenate([v[:, LANES:], halo[1]], 0)
+            tile, slots = ribbon_places(p, layers)
+            for slot in slots:
+                at = slot * SLOT
+                strips[tile] = jnp.where(between(lane, at, 8), turned(tail, at + 8), strips[tile])
+                strips[tile] = jnp.where(between(lane, at + 20, 8), turned(head, at + 20), strips[tile])
+    for tile, v in enumerate(strips):
+        ribbon[tile] = v
 
     for k in range(layers):
         e = eta_half[k]
@@ -210,67 +249,104 @@
             eta_half[k - 1] = 0.5 * eta_half[k - 1]
     eta_half[layers - 1] = 0.5 * eta_half[layers - 1]
 
-    own = (slice(0, ROWS), slice(0, 2 * LANES))
-    bare = 1.0 - ice[...].astype(jnp.float32)
-
     def apply(t, src, dst):
         def layer(k, carry):
             below0, below1, odd, even = carry
             g0, g1 = src[0, k], src[1, k]
             after = jnp.minimum(k + 1, layers - 1)
-            e_row, e_col, e_half, e_up = eta_row[k], eta_col[k], eta_half[k], eta_up[k]
+            e_up = eta_up[k]
             up0 = e_up * (g0 - src[0, after])
             up1 = e_up * (g1 - src[1, after])
-            g0n, g1n = row_next(g0), col_next(g1)
-            f = e_half * (g1n - col_prev(g1))
-            h = e_half * (g0n - row_prev(g0))
-            flux = e_row * (g0 - g0n)
-            out0 = flux - row_next(f) - row_prev(flux - f)
-            flux = e_col * (g0 - col_next(g0))
-            out0 = out0 + (flux - col_prev(flux)) + (up0 - below0)
-            flux = (4.0 * e_col) * (g1 - g1n)
-            out1 = flux - col_next(h) - col_prev(flux - h)
-            flux = (0.25 * e_row) * (g1 - row_next(g1))
-            out1 = out1 + (flux - row_prev(flux)) + (up1 - below1)
+            out0, out1 = horizontal(g0, g1, eta_row[k], eta_col[k], eta_half[k])
             m = cover[...]
-            out0, out1 = m * out0, m * out1
+            out0, out1 = m * (out0 + (up0 - below0)), m * (out1 + (up1 - below1))
             if t < STEPS:
                 dst[0, k], dst[1, k] = out0, out1
             for c, g, out in ((0, g0, out0), (1, g1, out1)):
-                outside = rhs[c, k] * bare
-                before = g[own] + outside
-                now = out[own] + outside
+                now = out[:ROWS]
                 powers[t - 1, c, k] = now
-                odd = odd + before * now
+                odd = odd + g[:ROWS] * now
                 even = even + now * now
             return up0, up1, odd, even
-
-        zero = jnp.zeros((ROWS, 2 * LANES), jnp.float32)
-        d = drag[...]
-        start = (-d * src[0, 0], -d * src[1, 0], zero, zero)
 
         def block(b, carry):
             for i in range(UNROLL):
                 carry = layer(b * UNROLL + i, carry)
             return carry
 
+        zero = jnp.zeros((ROWS, 2 * LANES), jnp.float32)
+        d = drag[...]
+        start = (-d * src[0, 0], -d * src[1, 0], zero, zero)
         return lax.fori_loop(0, layers // UNROLL, block, start)[2:]
 
-    square = jnp.zeros((ROWS, 2 * LANES), jnp.float32)
+    bare = 1.0 - ice[...].astype(jnp.float32)
+    whole = jnp.zeros((ROWS, 2 * LANES), jnp.float32)
+    outside = jnp.zeros((ROWS, 2 * LANES), jnp.float32)
     for c in range(2):
         for k in range(layers):
-            square = square + rhs[c, k] * rhs[c, k]
-    sums = [square]
+            square = rhs[c, k] * rhs[c, k]
+            whole = whole + square
+            outside = outside + bare * square
+    sums[0] = whole
+    wide = lax.broadcasted_iota(jnp.int32, (ROWS, 2 * LANES), 1)
+    inner = between(wide, HALO, 2 * LANES - 2 * HALO)
     src, dst = field_a, field_b
     for t in range(1, STEPS + 1):
-        sums.extend(apply(t, src, dst))
+        odd, even = apply(t, src, dst)
+        sums[2 * t - 1] = jnp.where(inner, odd, 0.0) + outside
+        sums[2 * t] = jnp.where(inner, even, 0.0) + outside
         src, dst = dst, src
+
+
+def ribbon_kernel(ribbon, columns, columns_a, columns_b, sums, edges, moments):
+    tiles = edges.shape[2]
+    below_and_above, _ = beyond()
+    lane = lax.broadcasted_iota(jnp.int32, (2 * ROWS, LANES), 1)
+
+    def whole(tile):
+        side = jnp.concatenate([columns[tile], below_and_above(columns_a[tile], columns_b[tile])], 0)
+        return ribbon[tile] + side
+
+    field = [[whole(c * tiles + n) for n in range(tiles)] for c in range(2)]
+    eta = [whole(2 * tiles + n) for n in range(tiles)]
+    cover, drag = whole(3 * tiles), whole(3 * tiles + 1)
+
+    def after(v):
+        return v[1:] + [turned(v[0], -SLOT)]
+
+    eta_row = [2.0 * (e + row_next(e)) for e in eta]
+    eta_col = [0.5 * (e + col_next(e)) for e in eta]
+    eta_half = [0.5 * e for e in eta]
+    eta_up = [e + n for e, n in zip(eta, after(eta))]
+    eta_up[-1] = jnp.where(lane < LANES - SLOT, eta_up[-1], 0.0)
+    place = lax.broadcasted_iota(jnp.int32, (ROWS, LANES), 1) % SLOT
+    edge = between(place, 4, HALO) | between(place, 20, HALO)
+    extra = [None]
+    for t in range(1, STEPS + 1):
+        ups = [[u * (g - n) for u, g, n in zip(eta_up, field[c], after(field[c]))] for c in range(2)]
+        result = ([], [])
+        odd = even = jnp.zeros((ROWS, LANES), jnp.float32)
+        for n in range(tiles):
+            outs = horizontal(field[0][n], field[1][n], eta_row[n], eta_col[n], eta_half[n])
+            for c in range(2):
+                below = ups[c][n - 1] if n else turned(ups[c][-1], SLOT) - drag * field[c][0]
+                out = cover * (outs[c] + (ups[c][n] - below))
+                result[c].append(out)
+                now = out[:ROWS]
+                edges[t - 1, c, n] = now
+                odd = odd + field[c][n][:ROWS] * now
+                even = even + now * now
+        field = result
+        extra.extend([jnp.where(edge, odd, 0.0), jnp.where(edge, even, 0.0)])
 
     tall = lax.broadcasted_iota(jnp.int32, (2 * ROWS, LANES), 0)
     high = jnp.zeros((2 * ROWS, LANES), jnp.float32)
     low = jnp.zeros((2 * ROWS, LANES), jnp.float32)
-    for j, total in enumerate(sums):
+    for j, more in enumerate(extra):
+        total = sums[j]
         pair = two_sum(total[:, :LANES], total[:, LANES:])
+        if more is not None:
+            pair = join(pair, (more, jnp.zeros_like(more)))
         for step in (4, 2, 1):
             pair = join(pair, tuple(pltpu.roll(v, step, 0) for v in pair))
         high = jnp.where(tall == j, jnp.concatenate([pair[0]] * 2, 0), high)
@@ -361,25 +437,42 @@
     return powers
 
 
-def final_kernel(rhs, powers, friction, ice, grounded, speed, *rest):
+def final_kernel(rhs, powers, edges, friction, ice, grounded, speed, *rest):
     *parts, iterate, residual, hessian = rest
-    layers = rhs.shape[1]
+    layers, tiles = rhs.shape[1], edges.shape[2]
     total = (parts[0][0], parts[0][1])
     for x in parts[1:]:
         total = join(total, (x[0], x[1]))
-    factors = [jnp.concatenate([c, c], 1) for c in solve(total)]
+    factors = solve(total)
+    wide = [jnp.concatenate([c, c], 1) for c in factors]
+    rest = sum(wide[1:], wide[0])
+    cover = ice[...].astype(jnp.float32)
+    lane = lax.broadcasted_iota(jnp.int32, (ROWS, LANES), 1)
+
+    def combined(vectors, weights):
+        x = weights[1] * vectors[0]
+        y = weights[0] * vectors[0]
+        for t in range(1, STEPS):
+            if t + 1 < STEPS:
+                x = x + weights[t + 1] * vectors[t]
+            y = y + weights[t] * vectors[t]
+        return x, y
+
     for c in range(2):
+        side = [combined([edges[t, c, n] for t in range(STEPS)], factors) for n in range(tiles)]
         for k in range(layers):
+            at = k // tiles * SLOT
+            inner = combined([powers[t, c, k] for t in range(STEPS)], wide)
+            patched = []
+            for v, e in zip(inner, side[k % tiles]):
+                head = jnp.where(lane < HALO, turned(e, -at - 20), v[:, :LANES])
+                tail = jnp.where(lane >= LANES - HALO, turned(e, 120 - at), v[:, LANES:])
+                patched.append(jnp.concatenate([head, tail], 1))
             r = rhs[c, k]
-            vectors = [r] + [powers[t, c, k] for t in range(STEPS)]
-            x = factors[0] * vectors[0]
-            y = factors[0] * vectors[1]
-            for t in range(1, STEPS):
-                x = x + factors[t] * vectors[t]
-                y = y + factors[t] * vectors[t + 1]
-            iterate[c, k] = x
-            residual[c, k] = r - y
-    weight = ice[...].astype(jnp.float32) * (friction[...] * grounded[...].astype(jnp.float32))
+            x, y = patched
+            iterate[c, k] = jnp.where(cover > 0.0, wide[0] * r + x, rest * r)
+            residual[c, k] = r - jnp.where(cover > 0.0, y, rest * r)
+    weight = cover * (friction[...] * grounded[...].astype(jnp.float32))
     hessian[...] = weight * (speed[0] * iterate[0, 0] + speed[1] * iterate[1, 0])
 
 
@@ -410,22 +503,28 @@
     inputs = (adjoint_rhs, viscosity, friction, ice_mask, grounded, basal_velocity)
     tile = (ROWS, LANES)
     strips = (2 * (layers + layers // 2 + 1),) + tile
+    ribbons = (ribbon_tiles(layers),) + tile
     *held, column_a, column_b, strip_a, strip_b = call(
         pack_kernel,
-        [jax.ShapeDtypeStruct(x.shape, x.dtype) for x in inputs] + [(2,) + tile, (2,) + tile, strips, strips],
+        [jax.ShapeDtypeStruct(x.shape, x.dtype) for x in inputs] + [ribbons, ribbons, strips, strips],
         [pltpu.SemaphoreType.DMA((len(inputs),))],
         in_specs=[pl.BlockSpec(memory_space=pltpu.HBM)] * len(inputs),
     )(*[pltpu.with_memory_space_constraint(x, pltpu.HBM) for x in inputs])
     strip_a, strip_b = swapped(strip_a, "gx", 0), swapped(strip_b, "gx", 1)
     beside = ("gy", "gz")
-    columns = jnp.concatenate([swapped(column_a, beside, 0), swapped(column_b, beside, 1)], axis=0)
+    (columns,) = call(beside_kernel, [ribbons])(swapped(column_a, beside, 0), swapped(column_b, beside, 1))
     columns_a, columns_b = swapped(columns, "gx", 0), swapped(columns, "gx", 1)
-    block = (layers, 2 * ROWS, 3 * LANES)
-    powers, sums = call(
-        power_kernel,
-        [(STEPS,) + adjoint_rhs.shape, (2, 2 * ROWS, LANES)],
+    block = (layers, 2 * ROWS, 2 * LANES)
+    powers, sums, ribbon = call(
+        main_kernel,
+        [(STEPS,) + adjoint_rhs.shape, (2 * STEPS + 1, ROWS, 2 * LANES), (ribbons[0], 2 * ROWS, LANES)],
         [(2,) + block] * 2 + [block] * 4 + [block[1:]] * 2,
-    )(*held[:5], strip_a, strip_b, columns, columns_a, columns_b)
+        cost_estimate=pl.CostEstimate(flops=200_000_000, bytes_accessed=8_000_000, transcendentals=0),
+    )(*held[:5], strip_a, strip_b)
+    edges, sums = call(
+        ribbon_kernel,
+        [(STEPS, 2, layers // 4) + tile, (2, 2 * ROWS, LANES)],
+    )(ribbon, columns, columns_a, columns_b, sums)
     parts = exchange(sums, ("gy", "gz"))
     if len(parts) > 1:
         sums = call(add_kernel, [sums.shape])(*parts)[0]
@@ -433,7 +532,7 @@
     rhs, _, friction, ice_mask, grounded, speed = held
     return tuple(
         call(final_kernel, [adjoint_rhs.shape, adjoint_rhs.shape, friction.shape])(
-            rhs, powers, friction, ice_mask, grounded, speed, *parts
+            rhs, powers, edges, friction, ice_mask, grounded, speed, *parts
         )
     )
 

time: 38.2 us -> 36.6 us (0.958)
  starting transfers between devices: 20.8 us -> 19.4 us
  Pallas kernels: 9.35 us -> 8.02 us
  waiting for transfers between devices: 7.17 us -> 8.3 us
    ppermute x6, waiting for transfers between devices: 4.95 us -> 7.71 us  [exchange(): parts.append(lax.ppermute(x, axis, pairs))]
    ppermute x6, waiting for transfers between devices: 2.22 us -> 0.59 us  [swapped(): return lax.ppermute(x, axis, pairs)]
    pallas_call x1 -> x3, Pallas kernels: 6.44 us -> 4.89 us  [the longest x1 4.22 us: body(): call(main_kernel, [(STEPS,) + adjoint_rhs.shape, (2 * STEPS + 1, ROWS, 2...]
    ppermute x6, starting transfers between devices: 10.9 us -> 9.59 us  [swapped(): return lax.ppermute(x, axis, pairs)]
  transfers between devices with their start and end apart: 12 -> 12, of which waited for: 5 -> 5; matrix products, arithmetic and copies ran while one was open for 0% -> 0% of each run, Pallas kernels for 0% -> 12%
where the time goes in v7:
time: 36.6 us; the launch traced here: 36.4 us
  starting transfers between devices  19.4 us (53%)
  waiting for transfers between devices  8.3 us (23%)
  Pallas kernels  8.02 us (22%)
  between operations  0.73 us (2%)
    ppermute x6, starting transfers between devices, exchange(): parts.append(lax.ppermute(x, axis, pairs))  9.8 us
    ppermute x6, starting transfers between devices, swapped(): return lax.ppermute(x, axis, pairs)  9.59 us
    ppermute x6, waiting for transfers between devices, exchange(): parts.append(lax.ppermute(x, axis, pairs))  7.71 us
    pallas_call x1, Pallas kernels, body(): call(main_kernel, [(STEPS,) + adjoint_rhs.shape, (2 * STEPS + 1, ROWS, 2...  4.22 us
    pallas_call x1, Pallas kernels, body(): call(final_kernel, [adjoint_rhs.shape, adjoint_rhs.shape, friction.shape])  1.82 us
    pallas_call x1, Pallas kernels, body(): call(pack_kernel, [jax.ShapeDtypeStruct(x.shape, x.dtype) for x in inputs...  1.29 us
  transfers between devices with their start and end apart: 12, of which 5 were waited for; matrix products, arithmetic and copies ran while one was open for 0% of the time, Pallas kernels for 12%

profile of v7, /device:TPU:0, one launch (start us, length us, event | category | flops | bytes accessed | tf_op | source)
XLA Modules:
  0.0 36.4 jit_solution(10355477864804544970)
XLA Ops:
  0.6 1.3 %shard_map.85 = (f32[2,20,8,256]{3,2,1,0:T(8,128)S(1)}, f32[20,8,256]{2,1,0:T(8,128)S(1)}, f32[8,256]{1,0:T(8,128)S(1)}, s32[8,256]{1,0:T(8,128)S(1)}, s32[8,256...) custom-call(f32[2,20,8,256]{3,2,1,0:T(8,128)} %refs_0_.1, ...), custom_call_target="tpu_custom_call" | custom-call | tf_op jit(solution)/shard_map/pallas_call | solution.py:507
  1.9 3.1 %collective-permute-start = (f32[62,8,128]{2,1,0:T(8,128)S(1)}, f32[62,8,128]{2,1,0:T(8,128)S(1)}, u32[]{:S(2)}, u32[]{:S(2)}) collective-permute-start(f32[62,8,128]{2,1,0:T(8,128)S(1)} %get-tuple-element.23), channel_id=1, source_target_pairs={{0,4},{4,0},{8,12},{12,8},{1,5},{5,1},{9,13},{13,9},{2,6},{6,2},{1... | collective-permute-start | bytes 761864 | tf_op jit(solution)/shard_map/ppermute | solution.py:42
  5.0 0.7 %collective-permute-start.1 = (f32[62,8,128]{2,1,0:T(8,128)S(1)}, f32[62,8,128]{2,1,0:T(8,128)S(1)}, u32[]{:S(2)}, u32[]{:S(2)}) collective-permute-start(f32[62,8,128]{2,1,0:T(8,128)S(1)} %get-tuple-element.24), channel_id=1, source_target_pairs={{0,0},{4,8},{8,4},{12,12},{1,1},{5,9},{9,5},{13,13},{2,2},{6,10},{... | collective-permute-start | bytes 761864 | tf_op jit(solution)/shard_map/ppermute | solution.py:42
  5.7 0.1 collective-permute-start.2
  5.8 0.7 %collective-permute-start.3 = (f32[17,8,128]{2,1,0:T(8,128)S(1)}, f32[17,8,128]{2,1,0:T(8,128)S(1)}, u32[]{:S(2)}, u32[]{:S(2)}) collective-permute-start(f32[17,8,128]{2,1,0:T(8,128)S(1)} %get-tuple-element.28), channel_id=1, source_target_pairs={{0,0},{1,2},{2,1},{3,3},{4,4},{5,6},{6,5},{7,7},{8,8},{9,10},{10,9... | collective-permute-start | bytes 208904 | tf_op jit(solution)/shard_map/ppermute | solution.py:42
  6.4 0.6 %collective-permute-done.2.from_a = f32[17,8,128]{2,1,0:T(8,128)S(1)} collective-permute-done((f32[17,8,128]{2,1,0:T(8,128)S(1)}, f32[17,8,128]{2,1,0:T(8,128)S(1)}, u32[]{:S(2)}, u32[]{:S(2)}) %collective-permute-start.2) | collective-permute-done | bytes 69664 | tf_op jit(solution)/shard_map/ppermute | solution.py:42
  7.0 4.4 %collective-permute-start.4 = (f32[17,8,128]{2,1,0:T(8,128)S(1)}, f32[17,8,128]{2,1,0:T(8,128)S(1)}, u32[]{:S(2)}, u32[]{:S(2)}) collective-permute-start(f32[17,8,128]{2,1,0:T(8,128)S(1)} %shard_map.87.columns), channel_id=1, source_target_pairs={{0,4},{4,0},{8,12},{12,8},{1,5},{5,1},{9,13},{13,9},{2,6},{6,2},{1... | collective-permute-start | bytes 208904 | tf_op jit(solution)/shard_map/ppermute | solution.py:42
  11.5 0.7 %collective-permute-start.5 = (f32[17,8,128]{2,1,0:T(8,128)S(1)}, f32[17,8,128]{2,1,0:T(8,128)S(1)}, u32[]{:S(2)}, u32[]{:S(2)}) collective-permute-start(f32[17,8,128]{2,1,0:T(8,128)S(1)} %shard_map.87.columns), channel_id=1, source_target_pairs={{0,0},{4,8},{8,4},{12,12},{1,1},{5,9},{9,5},{13,13},{2,2},{6,10},{... | collective-permute-start | bytes 208904 | tf_op jit(solution)/shard_map/ppermute | solution.py:42
  12.2 0.0 collective-permute-done.1.strip_b
  12.2 4.2 %shard_map.86 = (f32[4,2,20,8,256]{4,3,2,1,0:T(8,128)S(1)}, f32[9,8,256]{2,1,0:T(8,128)S(1)}, f32[17,16,128]{2,1,0:T(8,128)S(1)}) custom-call(f32[2,20,8,256]{3,2,1,0:T(8,128)S(1)} %get-tuple-element.18.rhs, f32[20,8,256]{2,1,0:T(8,128)S(1)} %get-tuple-element.19.eta, f32[8,256]{1,0:T(8,128)S(1)} %get-tuple-element.20.friction, ...), custom_call_target="tpu_custom_call" | custom-call | flops 200000000 | bytes 8000000 | tf_op jit(solution)/shard_map/pallas_call | solution.py:518
  16.4 0.0 collective-permute-done.4.columns_a
  16.4 0.7 %shard_map.88 = (f32[4,2,5,8,128]{4,3,2,1,0:T(8,128)S(1)}, f32[2,16,128]{2,1,0:T(8,128)S(1)}) custom-call(f32[17,16,128]{2,1,0:T(8,128)S(1)} %get-tuple-element.26.ribbon, f32[17,8,128]{2,1,0:T(8,128)S(1)} %shard_map.87.columns, f32[17,8,128]{2,1,0:T(8,128)S(1)} %collective-permute-done.4.columns_a, f32[17,8,128]{2,1,0:T(8,128)S(1)} %collective-permute-done.5.columns_b, ...), custom_call_target="tpu_custom_call" | custom-call | tf_op jit(solution)/shard_map/pallas_call | solution.py:524
  17.1 4.6 %collective-permute-start.6 = (f32[2,16,128]{2,1,0:T(8,128)S(1)}, f32[2,16,128]{2,1,0:T(8,128)S(1)}, u32[]{:S(2)}, u32[]{:S(2)}) collective-permute-start(f32[2,16,128]{2,1,0:T(8,128)S(1)} %get-tuple-element.32.refs_0_), channel_id=1, source_target_pairs={{0,1},{1,0},{2,3},{3,2},{4,5},{5,4},{6,7},{7,6},{8,9},{9,8},{10,11... | collective-permute-start | bytes 49160 | tf_op jit(solution)/shard_map/ppermute | solution.py:494
  21.7 1.4 %collective-permute-start.7 = (f32[2,16,128]{2,1,0:T(8,128)S(1)}, f32[2,16,128]{2,1,0:T(8,128)S(1)}, u32[]{:S(2)}, u32[]{:S(2)}) collective-permute-start(f32[2,16,128]{2,1,0:T(8,128)S(1)} %get-tuple-element.32.refs_0_), channel_id=1, source_target_pairs={{0,2},{1,3},{2,0},{3,1},{4,6},{5,7},{6,4},{7,5},{8,10},{9,11},{10,... | collective-permute-start | bytes 49160 | tf_op jit(solution)/shard_map/ppermute | solution.py:494
  23.1 0.1 collective-permute-start.8
  23.2 0.0 collective-permute-done.6.refs_1_
  23.2 2.3 %collective-permute-done.7.refs_2_ = f32[2,16,128]{2,1,0:T(8,128)S(1)} collective-permute-done((f32[2,16,128]{2,1,0:T(8,128)S(1)}, f32[2,16,128]{2,1,0:T(8,128)S(1)}, u32[]{:S(2)}, u32[]{:S(2)}) %collective-permute-start.7) | collective-permute-done | bytes 16416 | tf_op jit(solution)/shard_map/ppermute | solution.py:494
  25.5 0.8 %collective-permute-done.8.refs_3_ = f32[2,16,128]{2,1,0:T(8,128)S(1)} collective-permute-done((f32[2,16,128]{2,1,0:T(8,128)S(1)}, f32[2,16,128]{2,1,0:T(8,128)S(1)}, u32[]{:S(2)}, u32[]{:S(2)}) %collective-permute-start.8) | collective-permute-done | bytes 16416 | tf_op jit(solution)/shard_map/ppermute | solution.py:494
  26.3 2.8 %collective-permute-start.10 = (f32[2,16,128]{2,1,0:T(8,128)S(1)}, f32[2,16,128]{2,1,0:T(8,128)S(1)}, u32[]{:S(2)}, u32[]{:S(2)}) collective-permute-start(f32[2,16,128]{2,1,0:T(8,128)S(1)} %shard_map.89.rest_0_), channel_id=1, source_target_pairs={{0,8},{4,12},{8,0},{12,4},{1,9},{5,13},{9,1},{13,5},{2,10},{6,14},... | collective-permute-start | bytes 49160 | tf_op jit(solution)/shard_map/ppermute | solution.py:494
  29.1 0.9 %collective-permute-start.11 = (f32[2,16,128]{2,1,0:T(8,128)S(1)}, f32[2,16,128]{2,1,0:T(8,128)S(1)}, u32[]{:S(2)}, u32[]{:S(2)}) collective-permute-start(f32[2,16,128]{2,1,0:T(8,128)S(1)} %shard_map.89.rest_0_), channel_id=1, source_target_pairs={{0,12},{4,8},{8,4},{12,0},{1,13},{5,9},{9,5},{13,1},{2,14},{6,10},... | collective-permute-start | bytes 49160 | tf_op jit(solution)/shard_map/ppermute | solution.py:494
  30.0 0.0 collective-permute-start.9
  30.0 1.1 %collective-permute-done.10.rest_2_ = f32[2,16,128]{2,1,0:T(8,128)S(1)} collective-permute-done((f32[2,16,128]{2,1,0:T(8,128)S(1)}, f32[2,16,128]{2,1,0:T(8,128)S(1)}, u32[]{:S(2)}, u32[]{:S(2)}) %collective-permute-start.10) | collective-permute-done | bytes 16416 | tf_op jit(solution)/shard_map/ppermute | solution.py:494
  31.1 3.5 %collective-permute-done.11.rest_3_ = f32[2,16,128]{2,1,0:T(8,128)S(1)} collective-permute-done((f32[2,16,128]{2,1,0:T(8,128)S(1)}, f32[2,16,128]{2,1,0:T(8,128)S(1)}, u32[]{:S(2)}, u32[]{:S(2)}) %collective-permute-start.11) | collective-permute-done | bytes 16416 | tf_op jit(solution)/shard_map/ppermute | solution.py:494
  34.6 1.8 %shard_map.90 = (f32[2,20,8,256]{3,2,1,0:T(8,128)}, f32[2,20,8,256]{3,2,1,0:T(8,128)}, f32[8,256]{1,0:T(8,128)}) custom-call(f32[2,20,8,256]{3,2,1,0:T(8,128)S(1)} %get-tuple-element.18.rhs, f32[4,2,20,8,256]{4,3,2,1,0:T(8,128)S(1)} %get-tuple-element.25.powers, f32[4,2,5,8,128]{4,3,2,1,0:T(8,128)S(1)} %get-tuple-element.30.edges, ...), custom_call_target="tpu_custom_call" | custom-call | tf_op jit(solution)/shard_map/pallas_call | solution.py:534
  (6 shorter events, 0.1 us)
Async XLA Ops:
  1.9 10.2 %collective-permute-start = (f32[62,8,128]{2,1,0:T(8,128)S(1)}, f32[62,8,128]{2,1,0:T(8,128)S(1)}, u32[]{:S(2)}, u32[]{:S(2)}) collective-permute-start(f32[62,8,128]{2,1,0:T(8,128)S(1)} %get-tuple-element.23), channel_id=1, source_target_pairs={{0,4},{4,0},{8,12},{12,8},{1,5},{5,1},{9,13},{13,9},{2,6},{6,2},{1... | collective-permute-start | bytes 761864 | tf_op jit(solution)/shard_map/ppermute | solution.py:42
  5.0 7.1 %collective-permute-start.1 = (f32[62,8,128]{2,1,0:T(8,128)S(1)}, f32[62,8,128]{2,1,0:T(8,128)S(1)}, u32[]{:S(2)}, u32[]{:S(2)}) collective-permute-start(f32[62,8,128]{2,1,0:T(8,128)S(1)} %get-tuple-element.24), channel_id=1, source_target_pairs={{0,0},{4,8},{8,4},{12,12},{1,1},{5,9},{9,5},{13,13},{2,2},{6,10},{... | collective-permute-start | bytes 761864 | tf_op jit(solution)/shard_map/ppermute | solution.py:42
  5.7 1.3 %collective-permute-start.2 = (f32[17,8,128]{2,1,0:T(8,128)S(1)}, f32[17,8,128]{2,1,0:T(8,128)S(1)}, u32[]{:S(2)}, u32[]{:S(2)}) collective-permute-start(f32[17,8,128]{2,1,0:T(8,128)S(1)} %get-tuple-element.27), channel_id=1, source_target_pairs={{0,1},{1,0},{2,3},{3,2},{4,5},{5,4},{6,7},{7,6},{8,9},{9,8},{10,11... | collective-permute-start | bytes 208904 | tf_op jit(solution)/shard_map/ppermute | solution.py:42
  5.8 1.2 %collective-permute-start.3 = (f32[17,8,128]{2,1,0:T(8,128)S(1)}, f32[17,8,128]{2,1,0:T(8,128)S(1)}, u32[]{:S(2)}, u32[]{:S(2)}) collective-permute-start(f32[17,8,128]{2,1,0:T(8,128)S(1)} %get-tuple-element.28), channel_id=1, source_target_pairs={{0,0},{1,2},{2,1},{3,3},{4,4},{5,6},{6,5},{7,7},{8,8},{9,10},{10,9... | collective-permute-start | bytes 208904 | tf_op jit(solution)/shard_map/ppermute | solution.py:42
  7.0 9.4 %collective-permute-start.4 = (f32[17,8,128]{2,1,0:T(8,128)S(1)}, f32[17,8,128]{2,1,0:T(8,128)S(1)}, u32[]{:S(2)}, u32[]{:S(2)}) collective-permute-start(f32[17,8,128]{2,1,0:T(8,128)S(1)} %shard_map.87.columns), channel_id=1, source_target_pairs={{0,4},{4,0},{8,12},{12,8},{1,5},{5,1},{9,13},{13,9},{2,6},{6,2},{1... | collective-permute-start | bytes 208904 | tf_op jit(solution)/shard_map/ppermute | solution.py:42
  11.5 4.9 %collective-permute-start.5 = (f32[17,8,128]{2,1,0:T(8,128)S(1)}, f32[17,8,128]{2,1,0:T(8,128)S(1)}, u32[]{:S(2)}, u32[]{:S(2)}) collective-permute-start(f32[17,8,128]{2,1,0:T(8,128)S(1)} %shard_map.87.columns), channel_id=1, source_target_pairs={{0,0},{4,8},{8,4},{12,12},{1,1},{5,9},{9,5},{13,13},{2,2},{6,10},{... | collective-permute-start | bytes 208904 | tf_op jit(solution)/shard_map/ppermute | solution.py:42
  17.1 6.1 %collective-permute-start.6 = (f32[2,16,128]{2,1,0:T(8,128)S(1)}, f32[2,16,128]{2,1,0:T(8,128)S(1)}, u32[]{:S(2)}, u32[]{:S(2)}) collective-permute-start(f32[2,16,128]{2,1,0:T(8,128)S(1)} %get-tuple-element.32.refs_0_), channel_id=1, source_target_pairs={{0,1},{1,0},{2,3},{3,2},{4,5},{5,4},{6,7},{7,6},{8,9},{9,8},{10,11... | collective-permute-start | bytes 49160 | tf_op jit(solution)/shard_map/ppermute | solution.py:494
  21.7 3.7 %collective-permute-start.7 = (f32[2,16,128]{2,1,0:T(8,128)S(1)}, f32[2,16,128]{2,1,0:T(8,128)S(1)}, u32[]{:S(2)}, u32[]{:S(2)}) collective-permute-start(f32[2,16,128]{2,1,0:T(8,128)S(1)} %get-tuple-element.32.refs_0_), channel_id=1, source_target_pairs={{0,2},{1,3},{2,0},{3,1},{4,6},{5,7},{6,4},{7,5},{8,10},{9,11},{10,... | collective-permute-start | bytes 49160 | tf_op jit(solution)/shard_map/ppermute | solution.py:494
  23.1 3.2 %collective-permute-start.8 = (f32[2,16,128]{2,1,0:T(8,128)S(1)}, f32[2,16,128]{2,1,0:T(8,128)S(1)}, u32[]{:S(2)}, u32[]{:S(2)}) collective-permute-start(f32[2,16,128]{2,1,0:T(8,128)S(1)} %get-tuple-element.32.refs_0_), channel_id=1, source_target_pairs={{0,3},{1,2},{2,1},{3,0},{4,7},{5,6},{6,5},{7,4},{8,11},{9,10},{10,... | collective-permute-start | bytes 49160 | tf_op jit(solution)/shard_map/ppermute | solution.py:494
  26.3 4.8 %collective-permute-start.10 = (f32[2,16,128]{2,1,0:T(8,128)S(1)}, f32[2,16,128]{2,1,0:T(8,128)S(1)}, u32[]{:S(2)}, u32[]{:S(2)}) collective-permute-start(f32[2,16,128]{2,1,0:T(8,128)S(1)} %shard_map.89.rest_0_), channel_id=1, source_target_pairs={{0,8},{4,12},{8,0},{12,4},{1,9},{5,13},{9,1},{13,5},{2,10},{6,14},... | collective-permute-start | bytes 49160 | tf_op jit(solution)/shard_map/ppermute | solution.py:494
  29.1 5.5 %collective-permute-start.11 = (f32[2,16,128]{2,1,0:T(8,128)S(1)}, f32[2,16,128]{2,1,0:T(8,128)S(1)}, u32[]{:S(2)}, u32[]{:S(2)}) collective-permute-start(f32[2,16,128]{2,1,0:T(8,128)S(1)} %shard_map.89.rest_0_), channel_id=1, source_target_pairs={{0,12},{4,8},{8,4},{12,0},{1,13},{5,9},{9,5},{13,1},{2,14},{6,10},... | collective-permute-start | bytes 49160 | tf_op jit(solution)/shard_map/ppermute | solution.py:494
  30.0 4.6 %collective-permute-start.9 = (f32[2,16,128]{2,1,0:T(8,128)S(1)}, f32[2,16,128]{2,1,0:T(8,128)S(1)}, u32[]{:S(2)}, u32[]{:S(2)}) collective-permute-start(f32[2,16,128]{2,1,0:T(8,128)S(1)} %shard_map.89.rest_0_), channel_id=1, source_target_pairs={{0,4},{4,0},{8,12},{12,8},{1,5},{5,1},{9,13},{13,9},{2,6},{6,2},{1... | collective-permute-start | bytes 49160 | tf_op jit(solution)/shard_map/ppermute | solution.py:494

commit v8 on v7

--- a/solution.py
+++ b/solution.py
@@ -11,7 +11,7 @@
 HALO = 4
 ROWS = 8
 LANES = 128
-UNROLL = 5
+UNROLL = 10
 SLOT = 32
 
 
@@ -87,7 +87,7 @@
 
 
 def pack_kernel(*refs):
-    sources, held, (column_a, column_b, strip_a, strip_b, arrived) = refs[:6], refs[6:12], refs[12:]
+    sources, held, (strip_a, strip_b, arrived) = refs[:6], refs[6:12], refs[12:]
     copies = [pltpu.make_async_copy(a, b, arrived.at[i]) for i, (a, b) in enumerate(zip(sources, held))]
     for copy in copies:
         copy.start()
@@ -96,14 +96,9 @@
     rhs, eta, friction, ice, grounded, _ = held
     layers = eta.shape[0]
     plane = own_planes(rhs, eta, friction, ice, grounded)
-    lane = lax.broadcasted_iota(jnp.int32, (ROWS, LANES), 1)
     row = lax.broadcasted_iota(jnp.int32, (ROWS, LANES), 0)
     rows_even, _, _ = place_of("gx")
-    columns_even, _, _ = place_of(("gy", "gz"))
     upper_a = (row < HALO) != rows_even
-    count = column_a.shape[0]
-    left = [jnp.zeros((ROWS, LANES), jnp.float32) for _ in range(count)]
-    right = [jnp.zeros((ROWS, LANES), jnp.float32) for _ in range(count)]
     for q in range(strip_a.shape[0] // 2):
         first, second = pair_of(q, layers)
         x, y = plane(first), plane(second)
@@ -113,21 +108,49 @@
             ys = pltpu.roll(ys, HALO, 0)
             strip_a[2 * q + half] = jnp.where(upper_a, xs, ys)
             strip_b[2 * q + half] = jnp.where(upper_a, ys, xs)
-        for p, v in ((first, x), (second, y)):
+
+
+def beyond(strip_a, strip_b):
+    even, has_a, has_b = place_of("gx")
+    upper_a = (lax.broadcasted_iota(jnp.int32, (ROWS, LANES), 0) < HALO) == even
+
+    def halos(q):
+        first, second = [], []
+        for half in range(2):
+            from_a = jnp.where(has_a, strip_a[2 * q + half], 0.0)
+            from_b = jnp.where(has_b, strip_b[2 * q + half], 0.0)
+            first.append(jnp.where(upper_a, from_a, from_b))
+            second.append(pltpu.roll(jnp.where(upper_a, from_b, from_a), HALO, 0))
+        return first, second
+
+    return halos
+
+
+def edge_kernel(rhs, eta, friction, ice, grounded, strip_a, strip_b, ribbon, column_a, column_b):
+    layers = eta.shape[0]
+    plane = own_planes(rhs, eta, friction, ice, grounded)
+    halos = beyond(strip_a, strip_b)
+    lane = lax.broadcasted_iota(jnp.int32, (2 * ROWS, LANES), 1)
+    even, _, _ = place_of(("gy", "gz"))
+    zero = jnp.zeros((2 * ROWS, LANES), jnp.float32)
+    own = [zero] * ribbon.shape[0]
+    left, right = list(own), list(own)
+    for q in range(strip_a.shape[0] // 2):
+        for p, halo in zip(pair_of(q, layers), halos(q)):
+            v = plane(p)
+            head = jnp.concatenate([v[:, :LANES], halo[0]], 0)
+            tail = jnp.concatenate([v[:, LANES:], halo[1]], 0)
             tile, slots = ribbon_places(p, layers)
             for slot in slots:
                 at = slot * SLOT
-                left[tile] = jnp.where(between(lane, at + 8, 4), turned(v[:, :LANES], at + 8), left[tile])
-                right[tile] = jnp.where(between(lane, at + 16, 4), turned(v[:, LANES:], at + 20), right[tile])
-    for tile in range(count):
-        column_a[tile] = jnp.where(columns_even, right[tile], left[tile])
-        column_b[tile] = jnp.where(columns_even, left[tile], right[tile])
-
-
-def beside_kernel(from_a, from_b, columns):
-    _, has_a, has_b = place_of(("gy", "gz"))
-    for tile in range(columns.shape[0]):
-        columns[tile] = jnp.where(has_a, from_a[tile], 0.0) + jnp.where(has_b, from_b[tile], 0.0)
+                own[tile] = jnp.where(between(lane, at, 8), turned(tail, at + 8), own[tile])
+                own[tile] = jnp.where(between(lane, at + 20, 8), turned(head, at + 20), own[tile])
+                left[tile] = jnp.where(between(lane, at + 8, 4), turned(head, at + 8), left[tile])
+                right[tile] = jnp.where(between(lane, at + 16, 4), turned(tail, at + 20), right[tile])
+    for tile in range(ribbon.shape[0]):
+        ribbon[tile] = own[tile]
+        column_a[tile] = jnp.where(even, right[tile], left[tile])
+        column_b[tile] = jnp.where(even, left[tile], right[tile])
 
 
 def two_sum(a, b):
@@ -154,19 +177,6 @@
     xh, xl = cut(x[0])
     e = ((sh * xh - p) + sh * xl + sl * xh) + sl * xl
     return p, e + scalar * x[1]
-
-
-def beyond():
-    even, has_a, has_b = place_of("gx")
-    upper_a = (lax.broadcasted_iota(jnp.int32, (ROWS, LANES), 0) < HALO) == even
-
-    def below_and_above(from_a, from_b):
-        return jnp.where(upper_a, jnp.where(has_a, from_a, 0.0), jnp.where(has_b, from_b, 0.0))
-
-    def above_and_below(from_a, from_b):
-        return jnp.where(upper_a, jnp.where(has_b, from_b, 0.0), jnp.where(has_a, from_a, 0.0))
-
-    return below_and_above, above_and_below
 
 
 def row_next(v):
@@ -202,13 +212,12 @@
 
 def main_kernel(
     rhs, eta, friction, ice, grounded, strip_a, strip_b,
-    powers, sums, ribbon,
+    powers, sums,
     field_a, field_b, eta_row, eta_col, eta_half, eta_up, cover, drag,
 ):
     layers = eta.shape[0]
     plane = own_planes(rhs, eta, friction, ice, grounded)
-    below_and_above, above_and_below = beyond()
-    lane = lax.broadcasted_iota(jnp.int32, (2 * ROWS, LANES), 1)
+    halos = beyond(strip_a, strip_b)
 
     def target(p):
         if p < 2 * layers:
@@ -217,28 +226,11 @@
             return eta_half.at[p - 2 * layers]
         return cover if p == 3 * layers else drag
 
-    strips = [jnp.zeros((2 * ROWS, LANES), jnp.float32) for _ in range(ribbon.shape[0])]
     for q in range(strip_a.shape[0] // 2):
-        first, second = pair_of(q, layers)
-        halves = ([], [])
-        for half in range(2):
-            from_a, from_b = strip_a[2 * q + half], strip_b[2 * q + half]
-            halves[0].append(below_and_above(from_a, from_b))
-            halves[1].append(pltpu.roll(above_and_below(from_a, from_b), HALO, 0))
-        for p, halo in zip((first, second), halves):
-            v = plane(p)
+        for p, halo in zip(pair_of(q, layers), halos(q)):
             dst = target(p)
-            dst[0:ROWS, :] = v
+            dst[0:ROWS, :] = plane(p)
             dst[ROWS:, 0:LANES], dst[ROWS:, LANES:] = halo
-            head = jnp.concatenate([v[:, :LANES], halo[0]], 0)
-            tail = jnp.concatenate([v[:, LANES:], halo[1]], 0)
-            tile, slots = ribbon_places(p, layers)
-            for slot in slots:
-                at = slot * SLOT
-                strips[tile] = jnp.where(between(lane, at, 8), turned(tail, at + 8), strips[tile])
-                strips[tile] = jnp.where(between(lane, at + 20, 8), turned(head, at + 20), strips[tile])
-    for tile, v in enumerate(strips):
-        ribbon[tile] = v
 
     for k in range(layers):
         e = eta_half[k]
@@ -298,14 +290,13 @@
         src, dst = dst, src
 
 
-def ribbon_kernel(ribbon, columns, columns_a, columns_b, sums, edges, moments):
+def ribbon_kernel(ribbon, column_a, column_b, sums, edges, moments):
     tiles = edges.shape[2]
-    below_and_above, _ = beyond()
+    _, has_a, has_b = place_of(("gy", "gz"))
     lane = lax.broadcasted_iota(jnp.int32, (2 * ROWS, LANES), 1)
 
     def whole(tile):
-        side = jnp.concatenate([columns[tile], below_and_above(columns_a[tile], columns_b[tile])], 0)
-        return ribbon[tile] + side
+        return ribbon[tile] + jnp.where(has_a, column_a[tile], 0.0) + jnp.where(has_b, column_b[tile], 0.0)
 
     field = [[whole(c * tiles + n) for n in range(tiles)] for c in range(2)]
     eta = [whole(2 * tiles + n) for n in range(tiles)]
@@ -503,28 +494,28 @@
     inputs = (adjoint_rhs, viscosity, friction, ice_mask, grounded, basal_velocity)
     tile = (ROWS, LANES)
     strips = (2 * (layers + layers // 2 + 1),) + tile
-    ribbons = (ribbon_tiles(layers),) + tile
-    *held, column_a, column_b, strip_a, strip_b = call(
+    ribbons = (ribbon_tiles(layers), 2 * ROWS, LANES)
+    *held, strip_a, strip_b = call(
         pack_kernel,
-        [jax.ShapeDtypeStruct(x.shape, x.dtype) for x in inputs] + [ribbons, ribbons, strips, strips],
+        [jax.ShapeDtypeStruct(x.shape, x.dtype) for x in inputs] + [strips, strips],
         [pltpu.SemaphoreType.DMA((len(inputs),))],
         in_specs=[pl.BlockSpec(memory_space=pltpu.HBM)] * len(inputs),
     )(*[pltpu.with_memory_space_constraint(x, pltpu.HBM) for x in inputs])
     strip_a, strip_b = swapped(strip_a, "gx", 0), swapped(strip_b, "gx", 1)
-    beside = ("gy", "gz")
-    (columns,) = call(beside_kernel, [ribbons])(swapped(column_a, beside, 0), swapped(column_b, beside, 1))
-    columns_a, columns_b = swapped(columns, "gx", 0), swapped(columns, "gx", 1)
+    fields = (*held[:5], strip_a, strip_b)
+    ribbon, column_a, column_b = call(edge_kernel, [ribbons] * 3)(*fields)
+    column_a, column_b = swapped(column_a, ("gy", "gz"), 0), swapped(column_b, ("gy", "gz"), 1)
     block = (layers, 2 * ROWS, 2 * LANES)
-    powers, sums, ribbon = call(
+    powers, sums = call(
         main_kernel,
-        [(STEPS,) + adjoint_rhs.shape, (2 * STEPS + 1, ROWS, 2 * LANES), (ribbons[0], 2 * ROWS, LANES)],
+        [(STEPS,) + adjoint_rhs.shape, (2 * STEPS + 1, ROWS, 2 * LANES)],
         [(2,) + block] * 2 + [block] * 4 + [block[1:]] * 2,
         cost_estimate=pl.CostEstimate(flops=200_000_000, bytes_accessed=8_000_000, transcendentals=0),
-    )(*held[:5], strip_a, strip_b)
+    )(*fields)
     edges, sums = call(
         ribbon_kernel,
         [(STEPS, 2, layers // 4) + tile, (2, 2 * ROWS, LANES)],
-    )(ribbon, columns, columns_a, columns_b, sums)
+    )(ribbon, column_a, column_b, sums)
     parts = exchange(sums, ("gy", "gz"))
     if len(parts) > 1:
         sums = call(add_kernel, [sums.shape])(*parts)[0]

time: 36.6 us -> 37 us (1.011)
  starting transfers between devices: 19.4 us -> 15.7 us
  waiting for transfers between devices: 8.3 us -> 10.9 us
  Pallas kernels: 8.02 us -> 9.47 us
    ppermute x6 -> x4, starting transfers between devices: 9.59 us -> 4.49 us  [swapped(): return lax.ppermute(x, axis, pairs)]
    ppermute x6 -> x4, waiting for transfers between devices: 0.59 us -> 5.47 us  [swapped(): return lax.ppermute(x, axis, pairs)]
    ppermute x6, waiting for transfers between devices: 7.71 us -> 5.41 us  [exchange(): parts.append(lax.ppermute(x, axis, pairs))]
    ppermute x6, starting transfers between devices: 9.8 us -> 11.2 us  [exchange(): parts.append(lax.ppermute(x, axis, pairs))]
    pallas_call x1, Pallas kernels: 4.22 us -> 5.21 us  [body(): call(main_kernel, [(STEPS,) + adjoint_rhs.shape, (2 * STEPS + 1, ROWS, 2...]
    pallas_call x1, Pallas kernels: 0.01 us -> 0.63 us  [body(): ribbon, column_a, column_b = call(edge_kernel, [ribbons] * 3)(*fields)]
  transfers between devices with their start and end apart: 12 -> 10, of which waited for: 5 -> 4; matrix products, arithmetic and copies ran while one was open for 0% -> 0% of each run, Pallas kernels for 12% -> 14%
where the time goes in v8:
time: 37 us; the launch traced here: 36.8 us
  starting transfers between devices  15.7 us (42%)
  waiting for transfers between devices  10.9 us (29%)
  Pallas kernels  9.47 us (26%)
  between operations  0.7 us (2%)
    ppermute x6, starting transfers between devices, exchange(): parts.append(lax.ppermute(x, axis, pairs))  11.2 us
    ppermute x4, waiting for transfers between devices, swapped(): return lax.ppermute(x, axis, pairs)  5.47 us
    ppermute x6, waiting for transfers between devices, exchange(): parts.append(lax.ppermute(x, axis, pairs))  5.41 us
    pallas_call x1, Pallas kernels, body(): call(main_kernel, [(STEPS,) + adjoint_rhs.shape, (2 * STEPS + 1, ROWS, 2...  5.21 us
    ppermute x4, starting transfers between devices, swapped(): return lax.ppermute(x, axis, pairs)  4.49 us
    pallas_call x1, Pallas kernels, body(): call(final_kernel, [adjoint_rhs.shape, adjoint_rhs.shape, friction.shape])  1.77 us
    pallas_call x1, Pallas kernels, body(): call(pack_kernel, [jax.ShapeDtypeStruct(x.shape, x.dtype) for x in inputs...  1.13 us
  transfers between devices with their start and end apart: 10, of which 4 were waited for; matrix products, arithmetic and copies ran while one was open for 0% of the time, Pallas kernels for 14%

profile of v8, /device:TPU:0, one launch (start us, length us, event | category | flops | bytes accessed | tf_op | source)
XLA Modules:
  0.0 36.8 jit_solution(5747622782859943863)
XLA Ops:
  0.6 1.1 %shard_map.85 = (f32[2,20,8,256]{3,2,1,0:T(8,128)S(1)}, f32[20,8,256]{2,1,0:T(8,128)S(1)}, f32[8,256]{1,0:T(8,128)S(1)}, s32[8,256]{1,0:T(8,128)S(1)}, s32[8,256...) custom-call(f32[2,20,8,256]{3,2,1,0:T(8,128)} %refs_0_.1, ...), custom_call_target="tpu_custom_call" | custom-call | tf_op jit(solution)/shard_map/pallas_call | solution.py:498
  1.8 3.1 %collective-permute-start = (f32[62,8,128]{2,1,0:T(8,128)S(1)}, f32[62,8,128]{2,1,0:T(8,128)S(1)}, u32[]{:S(2)}, u32[]{:S(2)}) collective-permute-start(f32[62,8,128]{2,1,0:T(8,128)S(1)} %get-tuple-element.23), channel_id=1, source_target_pairs={{0,4},{4,0},{8,12},{12,8},{1,5},{5,1},{9,13},{13,9},{2,6},{6,2},{1... | collective-permute-start | bytes 761864 | tf_op jit(solution)/shard_map/ppermute | solution.py:42
  4.9 0.7 %collective-permute-start.1 = (f32[62,8,128]{2,1,0:T(8,128)S(1)}, f32[62,8,128]{2,1,0:T(8,128)S(1)}, u32[]{:S(2)}, u32[]{:S(2)}) collective-permute-start(f32[62,8,128]{2,1,0:T(8,128)S(1)} %get-tuple-element.24), channel_id=1, source_target_pairs={{0,0},{4,8},{8,4},{12,12},{1,1},{5,9},{9,5},{13,13},{2,2},{6,10},{... | collective-permute-start | bytes 761864 | tf_op jit(solution)/shard_map/ppermute | solution.py:42
  5.5 5.5 %collective-permute-done.strip_a = f32[62,8,128]{2,1,0:T(8,128)S(1)} collective-permute-done((f32[62,8,128]{2,1,0:T(8,128)S(1)}, f32[62,8,128]{2,1,0:T(8,128)S(1)}, u32[]{:S(2)}, u32[]{:S(2)}) %collective-permute-start) | collective-permute-done | bytes 253984 | tf_op jit(solution)/shard_map/ppermute | solution.py:42
  11.0 0.0 collective-permute-done.1.strip_b
  11.0 0.6 %shard_map.87 = (f32[17,16,128]{2,1,0:T(8,128)S(1)}, f32[17,16,128]{2,1,0:T(8,128)S(1)}, f32[17,16,128]{2,1,0:T(8,128)S(1)}) custom-call(f32[2,20,8,256]{3,2,1,0:T(8,128)S(1)} %get-tuple-element.18.rhs, f32[20,8,256]{2,1,0:T(8,128)S(1)} %get-tuple-element.19.eta, f32[8,256]{1,0:T(8,128)S(1)} %get-tuple-element.20.friction, ...), custom_call_target="tpu_custom_call" | custom-call | tf_op jit(solution)/shard_map/pallas_call | solution.py:506
  11.6 0.1 collective-permute-start.2
  11.7 0.7 %collective-permute-start.3 = (f32[17,16,128]{2,1,0:T(8,128)S(1)}, f32[17,16,128]{2,1,0:T(8,128)S(1)}, u32[]{:S(2)}, u32[]{:S(2)}) collective-permute-start(f32[17,16,128]{2,1,0:T(8,128)S(1)} %get-tuple-element.28), channel_id=1, source_target_pairs={{0,0},{1,2},{2,1},{3,3},{4,4},{5,6},{6,5},{7,7},{8,8},{9,10},{10,9... | collective-permute-start | bytes 417800 | tf_op jit(solution)/shard_map/ppermute | solution.py:42
  12.4 5.2 %shard_map.86 = (f32[4,2,20,8,256]{4,3,2,1,0:T(8,128)S(1)}, f32[9,8,256]{2,1,0:T(8,128)S(1)}) custom-call(f32[2,20,8,256]{3,2,1,0:T(8,128)S(1)} %get-tuple-element.18.rhs, f32[20,8,256]{2,1,0:T(8,128)S(1)} %get-tuple-element.19.eta, f32[8,256]{1,0:T(8,128)S(1)} %get-tuple-element.20.friction, s32[8,256]{1,0:T(8,128)S(1)} %get-tuple-element.21.ice, ...), custom_call_target="tpu_custom_call" | custom-call | flops 200000000 | bytes 8000000 | tf_op jit(solution)/shard_map/pallas_call | solution.py:509
  17.6 0.0 collective-permute-done.3.column_b
  17.6 0.7 %shard_map.88 = (f32[4,2,5,8,128]{4,3,2,1,0:T(8,128)S(1)}, f32[2,16,128]{2,1,0:T(8,128)S(1)}) custom-call(f32[17,16,128]{2,1,0:T(8,128)S(1)} %get-tuple-element.26.ribbon, f32[17,16,128]{2,1,0:T(8,128)S(1)} %collective-permute-done.2.column_a, f32[17,16,128]{2,1,0:T(8,128)S(1)} %collective-permute-done.3.column_b, f32[9,8,256]{2,1,0:T(8,128)S(1)} %get-tuple-element.29.sums), custom_call_target="tpu_custom_call" | custom-call | tf_op jit(solution)/shard_map/pallas_call | solution.py:515
  18.3 1.8 %collective-permute-start.6 = (f32[2,16,128]{2,1,0:T(8,128)S(1)}, f32[2,16,128]{2,1,0:T(8,128)S(1)}, u32[]{:S(2)}, u32[]{:S(2)}) collective-permute-start(f32[2,16,128]{2,1,0:T(8,128)S(1)} %get-tuple-element.32.refs_0_), channel_id=1, source_target_pairs={{0,3},{1,2},{2,1},{3,0},{4,7},{5,6},{6,5},{7,4},{8,11},{9,10},{10,... | collective-permute-start | bytes 49160 | tf_op jit(solution)/shard_map/ppermute | solution.py:485
  20.1 2.9 %collective-permute-start.5 = (f32[2,16,128]{2,1,0:T(8,128)S(1)}, f32[2,16,128]{2,1,0:T(8,128)S(1)}, u32[]{:S(2)}, u32[]{:S(2)}) collective-permute-start(f32[2,16,128]{2,1,0:T(8,128)S(1)} %get-tuple-element.32.refs_0_), channel_id=1, source_target_pairs={{0,2},{1,3},{2,0},{3,1},{4,6},{5,7},{6,4},{7,5},{8,10},{9,11},{10,... | collective-permute-start | bytes 49160 | tf_op jit(solution)/shard_map/ppermute | solution.py:485
  23.0 0.0 collective-permute-start.4
  23.0 0.0 collective-permute-done.6.refs_3_
  23.0 1.9 %collective-permute-done.5.refs_2_ = f32[2,16,128]{2,1,0:T(8,128)S(1)} collective-permute-done((f32[2,16,128]{2,1,0:T(8,128)S(1)}, f32[2,16,128]{2,1,0:T(8,128)S(1)}, u32[]{:S(2)}, u32[]{:S(2)}) %collective-permute-start.5) | collective-permute-done | bytes 16416 | tf_op jit(solution)/shard_map/ppermute | solution.py:485
  25.0 0.0 collective-permute-done.4.refs_1_
  25.0 3.8 %collective-permute-start.9 = (f32[2,16,128]{2,1,0:T(8,128)S(1)}, f32[2,16,128]{2,1,0:T(8,128)S(1)}, u32[]{:S(2)}, u32[]{:S(2)}) collective-permute-start(f32[2,16,128]{2,1,0:T(8,128)S(1)} %shard_map.89.rest_0_), channel_id=1, source_target_pairs={{0,12},{4,8},{8,4},{12,0},{1,13},{5,9},{9,5},{13,1},{2,14},{6,10},... | collective-permute-start | bytes 49160 | tf_op jit(solution)/shard_map/ppermute | solution.py:485
  28.8 2.5 %collective-permute-start.8 = (f32[2,16,128]{2,1,0:T(8,128)S(1)}, f32[2,16,128]{2,1,0:T(8,128)S(1)}, u32[]{:S(2)}, u32[]{:S(2)}) collective-permute-start(f32[2,16,128]{2,1,0:T(8,128)S(1)} %shard_map.89.rest_0_), channel_id=1, source_target_pairs={{0,8},{4,12},{8,0},{12,4},{1,9},{5,13},{9,1},{13,5},{2,10},{6,14},... | collective-permute-start | bytes 49160 | tf_op jit(solution)/shard_map/ppermute | solution.py:485
  31.3 0.3 collective-permute-start.7
  31.5 0.0 collective-permute-done.9.rest_3_
  31.5 1.9 %collective-permute-done.8.rest_2_ = f32[2,16,128]{2,1,0:T(8,128)S(1)} collective-permute-done((f32[2,16,128]{2,1,0:T(8,128)S(1)}, f32[2,16,128]{2,1,0:T(8,128)S(1)}, u32[]{:S(2)}, u32[]{:S(2)}) %collective-permute-start.8) | collective-permute-done | bytes 16416 | tf_op jit(solution)/shard_map/ppermute | solution.py:485
  33.4 1.6 %collective-permute-done.7.rest_1_ = f32[2,16,128]{2,1,0:T(8,128)S(1)} collective-permute-done((f32[2,16,128]{2,1,0:T(8,128)S(1)}, f32[2,16,128]{2,1,0:T(8,128)S(1)}, u32[]{:S(2)}, u32[]{:S(2)}) %collective-permute-start.7) | collective-permute-done | bytes 16416 | tf_op jit(solution)/shard_map/ppermute | solution.py:485
  35.0 1.8 %shard_map.90 = (f32[2,20,8,256]{3,2,1,0:T(8,128)}, f32[2,20,8,256]{3,2,1,0:T(8,128)}, f32[8,256]{1,0:T(8,128)}) custom-call(f32[2,20,8,256]{3,2,1,0:T(8,128)S(1)} %get-tuple-element.18.rhs, f32[4,2,20,8,256]{4,3,2,1,0:T(8,128)S(1)} %get-tuple-element.25.powers, f32[4,2,5,8,128]{4,3,2,1,0:T(8,128)S(1)} %get-tuple-element.30.edges, ...), custom_call_target="tpu_custom_call" | custom-call | tf_op jit(solution)/shard_map/pallas_call | solution.py:525
  (2 shorter events, 0.0 us)
Async XLA Ops:
  1.8 9.2 %collective-permute-start = (f32[62,8,128]{2,1,0:T(8,128)S(1)}, f32[62,8,128]{2,1,0:T(8,128)S(1)}, u32[]{:S(2)}, u32[]{:S(2)}) collective-permute-start(f32[62,8,128]{2,1,0:T(8,128)S(1)} %get-tuple-element.23), channel_id=1, source_target_pairs={{0,4},{4,0},{8,12},{12,8},{1,5},{5,1},{9,13},{13,9},{2,6},{6,2},{1... | collective-permute-start | bytes 761864 | tf_op jit(solution)/shard_map/ppermute | solution.py:42
  4.9 6.1 %collective-permute-start.1 = (f32[62,8,128]{2,1,0:T(8,128)S(1)}, f32[62,8,128]{2,1,0:T(8,128)S(1)}, u32[]{:S(2)}, u32[]{:S(2)}) collective-permute-start(f32[62,8,128]{2,1,0:T(8,128)S(1)} %get-tuple-element.24), channel_id=1, source_target_pairs={{0,0},{4,8},{8,4},{12,12},{1,1},{5,9},{9,5},{13,13},{2,2},{6,10},{... | collective-permute-start | bytes 761864 | tf_op jit(solution)/shard_map/ppermute | solution.py:42
  11.6 6.0 %collective-permute-start.2 = (f32[17,16,128]{2,1,0:T(8,128)S(1)}, f32[17,16,128]{2,1,0:T(8,128)S(1)}, u32[]{:S(2)}, u32[]{:S(2)}) collective-permute-start(f32[17,16,128]{2,1,0:T(8,128)S(1)} %get-tuple-element.27), channel_id=1, source_target_pairs={{0,1},{1,0},{2,3},{3,2},{4,5},{5,4},{6,7},{7,6},{8,9},{9,8},{10,11... | collective-permute-start | bytes 417800 | tf_op jit(solution)/shard_map/ppermute | solution.py:42
  11.7 5.9 %collective-permute-start.3 = (f32[17,16,128]{2,1,0:T(8,128)S(1)}, f32[17,16,128]{2,1,0:T(8,128)S(1)}, u32[]{:S(2)}, u32[]{:S(2)}) collective-permute-start(f32[17,16,128]{2,1,0:T(8,128)S(1)} %get-tuple-element.28), channel_id=1, source_target_pairs={{0,0},{1,2},{2,1},{3,3},{4,4},{5,6},{6,5},{7,7},{8,8},{9,10},{10,9... | collective-permute-start | bytes 417800 | tf_op jit(solution)/shard_map/ppermute | solution.py:42
  18.3 4.7 %collective-permute-start.6 = (f32[2,16,128]{2,1,0:T(8,128)S(1)}, f32[2,16,128]{2,1,0:T(8,128)S(1)}, u32[]{:S(2)}, u32[]{:S(2)}) collective-permute-start(f32[2,16,128]{2,1,0:T(8,128)S(1)} %get-tuple-element.32.refs_0_), channel_id=1, source_target_pairs={{0,3},{1,2},{2,1},{3,0},{4,7},{5,6},{6,5},{7,4},{8,11},{9,10},{10,... | collective-permute-start | bytes 49160 | tf_op jit(solution)/shard_map/ppermute | solution.py:485
  20.1 4.8 %collective-permute-start.5 = (f32[2,16,128]{2,1,0:T(8,128)S(1)}, f32[2,16,128]{2,1,0:T(8,128)S(1)}, u32[]{:S(2)}, u32[]{:S(2)}) collective-permute-start(f32[2,16,128]{2,1,0:T(8,128)S(1)} %get-tuple-element.32.refs_0_), channel_id=1, source_target_pairs={{0,2},{1,3},{2,0},{3,1},{4,6},{5,7},{6,4},{7,5},{8,10},{9,11},{10,... | collective-permute-start | bytes 49160 | tf_op jit(solution)/shard_map/ppermute | solution.py:485
  23.0 2.0 %collective-permute-start.4 = (f32[2,16,128]{2,1,0:T(8,128)S(1)}, f32[2,16,128]{2,1,0:T(8,128)S(1)}, u32[]{:S(2)}, u32[]{:S(2)}) collective-permute-start(f32[2,16,128]{2,1,0:T(8,128)S(1)} %get-tuple-element.32.refs_0_), channel_id=1, source_target_pairs={{0,1},{1,0},{2,3},{3,2},{4,5},{5,4},{6,7},{7,6},{8,9},{9,8},{10,11... | collective-permute-start | bytes 49160 | tf_op jit(solution)/shard_map/ppermute | solution.py:485
  25.0 6.5 %collective-permute-start.9 = (f32[2,16,128]{2,1,0:T(8,128)S(1)}, f32[2,16,128]{2,1,0:T(8,128)S(1)}, u32[]{:S(2)}, u32[]{:S(2)}) collective-permute-start(f32[2,16,128]{2,1,0:T(8,128)S(1)} %shard_map.89.rest_0_), channel_id=1, source_target_pairs={{0,12},{4,8},{8,4},{12,0},{1,13},{5,9},{9,5},{13,1},{2,14},{6,10},... | collective-permute-start | bytes 49160 | tf_op jit(solution)/shard_map/ppermute | solution.py:485
  28.8 4.6 %collective-permute-start.8 = (f32[2,16,128]{2,1,0:T(8,128)S(1)}, f32[2,16,128]{2,1,0:T(8,128)S(1)}, u32[]{:S(2)}, u32[]{:S(2)}) collective-permute-start(f32[2,16,128]{2,1,0:T(8,128)S(1)} %shard_map.89.rest_0_), channel_id=1, source_target_pairs={{0,8},{4,12},{8,0},{12,4},{1,9},{5,13},{9,1},{13,5},{2,10},{6,14},... | collective-permute-start | bytes 49160 | tf_op jit(solution)/shard_map/ppermute | solution.py:485
  31.3 3.7 %collective-permute-start.7 = (f32[2,16,128]{2,1,0:T(8,128)S(1)}, f32[2,16,128]{2,1,0:T(8,128)S(1)}, u32[]{:S(2)}, u32[]{:S(2)}) collective-permute-start(f32[2,16,128]{2,1,0:T(8,128)S(1)} %shard_map.89.rest_0_), channel_id=1, source_target_pairs={{0,4},{4,0},{8,12},{12,8},{1,5},{5,1},{9,13},{13,9},{2,6},{6,2},{1... | collective-permute-start | bytes 49160 | tf_op jit(solution)/shard_map/ppermute | solution.py:485

commit v9 on v7

--- a/solution.py
+++ b/solution.py
@@ -203,7 +203,7 @@
 def main_kernel(
     rhs, eta, friction, ice, grounded, strip_a, strip_b,
     powers, sums, ribbon,
-    field_a, field_b, eta_row, eta_col, eta_half, eta_up, cover, drag,
+    fields, eta_row, eta_col, eta_half, eta_up, cover, drag,
 ):
     layers = eta.shape[0]
     plane = own_planes(rhs, eta, friction, ice, grounded)
@@ -212,7 +212,7 @@
 
     def target(p):
         if p < 2 * layers:
-            return field_a.at[p // layers, p % layers]
+            return fields.at[0, p // layers, p % layers]
         if p < 3 * layers:
             return eta_half.at[p - 2 * layers]
         return cover if p == 3 * layers else drag
@@ -249,7 +249,9 @@
             eta_half[k - 1] = 0.5 * eta_half[k - 1]
     eta_half[layers - 1] = 0.5 * eta_half[layers - 1]
 
-    def apply(t, src, dst):
+    def apply(t, carry):
+        src, dst = fields.at[t % 2], fields.at[1 - t % 2]
+
         def layer(k, carry):
             below0, below1, odd, even = carry
             g0, g1 = src[0, k], src[1, k]
@@ -260,11 +262,10 @@
             out0, out1 = horizontal(g0, g1, eta_row[k], eta_col[k], eta_half[k])
             m = cover[...]
             out0, out1 = m * (out0 + (up0 - below0)), m * (out1 + (up1 - below1))
-            if t < STEPS:
-                dst[0, k], dst[1, k] = out0, out1
+            dst[0, k], dst[1, k] = out0, out1
             for c, g, out in ((0, g0, out0), (1, g1, out1)):
                 now = out[:ROWS]
-                powers[t - 1, c, k] = now
+                powers[t, c, k] = now
                 odd = odd + g[:ROWS] * now
                 even = even + now * now
             return up0, up1, odd, even
@@ -277,7 +278,10 @@
         zero = jnp.zeros((ROWS, 2 * LANES), jnp.float32)
         d = drag[...]
         start = (-d * src[0, 0], -d * src[1, 0], zero, zero)
-        return lax.fori_loop(0, layers // UNROLL, block, start)[2:]
+        _, _, odd, even = lax.fori_loop(0, layers // UNROLL, block, start)
+        sums[2 * t + 1] = jnp.where(inner, odd, 0.0) + outside
+        sums[2 * t + 2] = jnp.where(inner, even, 0.0) + outside
+        return carry
 
     bare = 1.0 - ice[...].astype(jnp.float32)
     whole = jnp.zeros((ROWS, 2 * LANES), jnp.float32)
@@ -290,12 +294,7 @@
     sums[0] = whole
     wide = lax.broadcasted_iota(jnp.int32, (ROWS, 2 * LANES), 1)
     inner = between(wide, HALO, 2 * LANES - 2 * HALO)
-    src, dst = field_a, field_b
-    for t in range(1, STEPS + 1):
-        odd, even = apply(t, src, dst)
-        sums[2 * t - 1] = jnp.where(inner, odd, 0.0) + outside
-        sums[2 * t] = jnp.where(inner, even, 0.0) + outside
-        src, dst = dst, src
+    lax.fori_loop(0, STEPS, apply, 0)
 
 
 def ribbon_kernel(ribbon, columns, columns_a, columns_b, sums, edges, moments):
@@ -510,15 +509,20 @@
         [pltpu.SemaphoreType.DMA((len(inputs),))],
         in_specs=[pl.BlockSpec(memory_space=pltpu.HBM)] * len(inputs),
     )(*[pltpu.with_memory_space_constraint(x, pltpu.HBM) for x in inputs])
+    beside = ("gy", "gz")
+    column_a, column_b = swapped(column_a, beside, 0), swapped(column_b, beside, 1)
     strip_a, strip_b = swapped(strip_a, "gx", 0), swapped(strip_b, "gx", 1)
-    beside = ("gy", "gz")
-    (columns,) = call(beside_kernel, [ribbons])(swapped(column_a, beside, 0), swapped(column_b, beside, 1))
+    (columns,) = call(
+        beside_kernel,
+        [ribbons],
+        cost_estimate=pl.CostEstimate(flops=3_000_000_000, bytes_accessed=200_000, transcendentals=0),
+    )(column_a, column_b)
     columns_a, columns_b = swapped(columns, "gx", 0), swapped(columns, "gx", 1)
     block = (layers, 2 * ROWS, 2 * LANES)
     powers, sums, ribbon = call(
         main_kernel,
         [(STEPS,) + adjoint_rhs.shape, (2 * STEPS + 1, ROWS, 2 * LANES), (ribbons[0], 2 * ROWS, LANES)],
-        [(2,) + block] * 2 + [block] * 4 + [block[1:]] * 2,
+        [(2, 2) + block] + [block] * 4 + [block[1:]] * 2,
         cost_estimate=pl.CostEstimate(flops=200_000_000, bytes_accessed=8_000_000, transcendentals=0),
     )(*held[:5], strip_a, strip_b)
     edges, sums = call(

time: 36.6 us -> 45.6 us (1.25)
  Pallas kernels: 8.02 us -> 17 us
  waiting for transfers between devices: 8.3 us -> 7.45 us
  starting transfers between devices: 19.4 us -> 20.1 us
    pallas_call x1, Pallas kernels: 4.22 us -> 13.2 us  [body(): call(main_kernel, [(STEPS,) + adjoint_rhs.shape, (2 * STEPS + 1, ROWS, 2...]
    ppermute x6, starting transfers between devices: 9.8 us -> 10.5 us  [exchange(): parts.append(lax.ppermute(x, axis, pairs))]
    ppermute x6, waiting for transfers between devices: 0.59 us -> 0.02 us  [swapped(): return lax.ppermute(x, axis, pairs)]
  transfers between devices with their start and end apart: 12 -> 12, of which waited for: 5 -> 4; matrix products, arithmetic and copies ran while one was open for 0% -> 0% of each run, Pallas kernels for 12% -> 29%
where the time goes in v9:
time: 45.6 us; the launch traced here: 45.3 us
  starting transfers between devices  20.1 us (44%)
  Pallas kernels  17 us (37%)
  waiting for transfers between devices  7.45 us (16%)
  between operations  0.74 us (2%)
    pallas_call x1, Pallas kernels, body(): call(main_kernel, [(STEPS,) + adjoint_rhs.shape, (2 * STEPS + 1, ROWS, 2...  13.2 us
    ppermute x6, starting transfers between devices, exchange(): parts.append(lax.ppermute(x, axis, pairs))  10.5 us
    ppermute x6, starting transfers between devices, swapped(): return lax.ppermute(x, axis, pairs)  9.6 us
    ppermute x6, waiting for transfers between devices, exchange(): parts.append(lax.ppermute(x, axis, pairs))  7.44 us
    pallas_call x1, Pallas kernels, body(): call(final_kernel, [adjoint_rhs.shape, adjoint_rhs.shape, friction.shape])  1.82 us
    pallas_call x1, Pallas kernels, body(): call(pack_kernel, [jax.ShapeDtypeStruct(x.shape, x.dtype) for x in inputs...  1.29 us
  transfers between devices with their start and end apart: 12, of which 4 were waited for; matrix products, arithmetic and copies ran while one was open for 0% of the time, Pallas kernels for 29%

profile of v9, /device:TPU:0, one launch (start us, length us, event | category | flops | bytes accessed | tf_op | source)
XLA Modules:
  0.0 45.3 jit_solution(103003652453976313)
XLA Ops:
  0.6 1.3 %shard_map.85 = (f32[2,20,8,256]{3,2,1,0:T(8,128)S(1)}, f32[20,8,256]{2,1,0:T(8,128)S(1)}, f32[8,256]{1,0:T(8,128)S(1)}, s32[8,256]{1,0:T(8,128)S(1)}, s32[8,256...) custom-call(f32[2,20,8,256]{3,2,1,0:T(8,128)} %refs_0_.1, ...), custom_call_target="tpu_custom_call" | custom-call | tf_op jit(solution)/shard_map/pallas_call | solution.py:506
  1.9 0.5 %collective-permute-start.2 = (f32[17,8,128]{2,1,0:T(8,128)S(1)}, f32[17,8,128]{2,1,0:T(8,128)S(1)}, u32[]{:S(2)}, u32[]{:S(2)}) collective-permute-start(f32[17,8,128]{2,1,0:T(8,128)S(1)} %get-tuple-element.27), channel_id=1, source_target_pairs={{0,1},{1,0},{2,3},{3,2},{4,5},{5,4},{6,7},{7,6},{8,9},{9,8},{10,11... | collective-permute-start | bytes 208904 | tf_op jit(solution)/shard_map/ppermute | solution.py:42
  2.4 0.7 %collective-permute-start.3 = (f32[17,8,128]{2,1,0:T(8,128)S(1)}, f32[17,8,128]{2,1,0:T(8,128)S(1)}, u32[]{:S(2)}, u32[]{:S(2)}) collective-permute-start(f32[17,8,128]{2,1,0:T(8,128)S(1)} %get-tuple-element.28), channel_id=1, source_target_pairs={{0,0},{1,2},{2,1},{3,3},{4,4},{5,6},{6,5},{7,7},{8,8},{9,10},{10,9... | collective-permute-start | bytes 208904 | tf_op jit(solution)/shard_map/ppermute | solution.py:42
  3.1 2.7 %collective-permute-start = (f32[62,8,128]{2,1,0:T(8,128)S(1)}, f32[62,8,128]{2,1,0:T(8,128)S(1)}, u32[]{:S(2)}, u32[]{:S(2)}) collective-permute-start(f32[62,8,128]{2,1,0:T(8,128)S(1)} %get-tuple-element.23), channel_id=1, source_target_pairs={{0,4},{4,0},{8,12},{12,8},{1,5},{5,1},{9,13},{13,9},{2,6},{6,2},{1... | collective-permute-start | bytes 761864 | tf_op jit(solution)/shard_map/ppermute | solution.py:42
  5.8 0.7 %collective-permute-start.1 = (f32[62,8,128]{2,1,0:T(8,128)S(1)}, f32[62,8,128]{2,1,0:T(8,128)S(1)}, u32[]{:S(2)}, u32[]{:S(2)}) collective-permute-start(f32[62,8,128]{2,1,0:T(8,128)S(1)} %get-tuple-element.24), channel_id=1, source_target_pairs={{0,0},{4,8},{8,4},{12,12},{1,1},{5,9},{9,5},{13,13},{2,2},{6,10},{... | collective-permute-start | bytes 761864 | tf_op jit(solution)/shard_map/ppermute | solution.py:42
  6.5 0.0 collective-permute-done.3.from_b
  6.5 4.4 %collective-permute-start.4 = (f32[17,8,128]{2,1,0:T(8,128)S(1)}, f32[17,8,128]{2,1,0:T(8,128)S(1)}, u32[]{:S(2)}, u32[]{:S(2)}) collective-permute-start(f32[17,8,128]{2,1,0:T(8,128)S(1)} %shard_map.87.columns), channel_id=1, source_target_pairs={{0,4},{4,0},{8,12},{12,8},{1,5},{5,1},{9,13},{13,9},{2,6},{6,2},{1... | collective-permute-start | bytes 208904 | tf_op jit(solution)/shard_map/ppermute | solution.py:42
  11.0 0.7 %collective-permute-start.5 = (f32[17,8,128]{2,1,0:T(8,128)S(1)}, f32[17,8,128]{2,1,0:T(8,128)S(1)}, u32[]{:S(2)}, u32[]{:S(2)}) collective-permute-start(f32[17,8,128]{2,1,0:T(8,128)S(1)} %shard_map.87.columns), channel_id=1, source_target_pairs={{0,0},{4,8},{8,4},{12,12},{1,1},{5,9},{9,5},{13,13},{2,2},{6,10},{... | collective-permute-start | bytes 208904 | tf_op jit(solution)/shard_map/ppermute | solution.py:42
  11.6 0.0 collective-permute-done.strip_a
  11.6 0.0 collective-permute-done.1.strip_b
  11.6 13.2 %shard_map.86 = (f32[4,2,20,8,256]{4,3,2,1,0:T(8,128)S(1)}, f32[9,8,256]{2,1,0:T(8,128)S(1)}, f32[17,16,128]{2,1,0:T(8,128)S(1)}) custom-call(f32[2,20,8,256]{3,2,1,0:T(8,128)S(1)} %get-tuple-element.18.rhs, f32[20,8,256]{2,1,0:T(8,128)S(1)} %get-tuple-element.19.eta, f32[8,256]{1,0:T(8,128)S(1)} %get-tuple-element.20.friction, ...), custom_call_target="tpu_custom_call" | custom-call | flops 200000000 | bytes 8000000 | tf_op jit(solution)/shard_map/pallas_call | solution.py:522
  24.8 0.0 collective-permute-done.4.columns_a
  24.8 0.0 collective-permute-done.5.columns_b
  24.9 0.7 %shard_map.88 = (f32[4,2,5,8,128]{4,3,2,1,0:T(8,128)S(1)}, f32[2,16,128]{2,1,0:T(8,128)S(1)}) custom-call(f32[17,16,128]{2,1,0:T(8,128)S(1)} %get-tuple-element.26.ribbon, f32[17,8,128]{2,1,0:T(8,128)S(1)} %shard_map.87.columns, f32[17,8,128]{2,1,0:T(8,128)S(1)} %collective-permute-done.4.columns_a, f32[17,8,128]{2,1,0:T(8,128)S(1)} %collective-permute-done.5.columns_b, ...), custom_call_target="tpu_custom_call" | custom-call | tf_op jit(solution)/shard_map/pallas_call | solution.py:528
  25.5 2.1 %collective-permute-start.6 = (f32[2,16,128]{2,1,0:T(8,128)S(1)}, f32[2,16,128]{2,1,0:T(8,128)S(1)}, u32[]{:S(2)}, u32[]{:S(2)}) collective-permute-start(f32[2,16,128]{2,1,0:T(8,128)S(1)} %get-tuple-element.32.refs_0_), channel_id=1, source_target_pairs={{0,1},{1,0},{2,3},{3,2},{4,5},{5,4},{6,7},{7,6},{8,9},{9,8},{10,11... | collective-permute-start | bytes 49160 | tf_op jit(solution)/shard_map/ppermute | solution.py:493
  27.6 1.4 %collective-permute-start.7 = (f32[2,16,128]{2,1,0:T(8,128)S(1)}, f32[2,16,128]{2,1,0:T(8,128)S(1)}, u32[]{:S(2)}, u32[]{:S(2)}) collective-permute-start(f32[2,16,128]{2,1,0:T(8,128)S(1)} %get-tuple-element.32.refs_0_), channel_id=1, source_target_pairs={{0,2},{1,3},{2,0},{3,1},{4,6},{5,7},{6,4},{7,5},{8,10},{9,11},{10,... | collective-permute-start | bytes 49160 | tf_op jit(solution)/shard_map/ppermute | solution.py:493
  29.0 0.1 collective-permute-start.8
  29.1 2.2 %collective-permute-done.7.refs_2_ = f32[2,16,128]{2,1,0:T(8,128)S(1)} collective-permute-done((f32[2,16,128]{2,1,0:T(8,128)S(1)}, f32[2,16,128]{2,1,0:T(8,128)S(1)}, u32[]{:S(2)}, u32[]{:S(2)}) %collective-permute-start.7) | collective-permute-done | bytes 16416 | tf_op jit(solution)/shard_map/ppermute | solution.py:493
  31.3 0.9 %collective-permute-done.8.refs_3_ = f32[2,16,128]{2,1,0:T(8,128)S(1)} collective-permute-done((f32[2,16,128]{2,1,0:T(8,128)S(1)}, f32[2,16,128]{2,1,0:T(8,128)S(1)}, u32[]{:S(2)}, u32[]{:S(2)}) %collective-permute-start.8) | collective-permute-done | bytes 16416 | tf_op jit(solution)/shard_map/ppermute | solution.py:493
  32.2 5.8 %collective-permute-start.10 = (f32[2,16,128]{2,1,0:T(8,128)S(1)}, f32[2,16,128]{2,1,0:T(8,128)S(1)}, u32[]{:S(2)}, u32[]{:S(2)}) collective-permute-start(f32[2,16,128]{2,1,0:T(8,128)S(1)} %shard_map.89.rest_0_), channel_id=1, source_target_pairs={{0,8},{4,12},{8,0},{12,4},{1,9},{5,13},{9,1},{13,5},{2,10},{6,14},... | collective-permute-start | bytes 49160 | tf_op jit(solution)/shard_map/ppermute | solution.py:493
  38.0 1.2 %collective-permute-start.11 = (f32[2,16,128]{2,1,0:T(8,128)S(1)}, f32[2,16,128]{2,1,0:T(8,128)S(1)}, u32[]{:S(2)}, u32[]{:S(2)}) collective-permute-start(f32[2,16,128]{2,1,0:T(8,128)S(1)} %shard_map.89.rest_0_), channel_id=1, source_target_pairs={{0,12},{4,8},{8,4},{12,0},{1,13},{5,9},{9,5},{13,1},{2,14},{6,10},... | collective-permute-start | bytes 49160 | tf_op jit(solution)/shard_map/ppermute | solution.py:493
  39.2 0.5 %collective-permute-done.10.rest_2_ = f32[2,16,128]{2,1,0:T(8,128)S(1)} collective-permute-done((f32[2,16,128]{2,1,0:T(8,128)S(1)}, f32[2,16,128]{2,1,0:T(8,128)S(1)}, u32[]{:S(2)}, u32[]{:S(2)}) %collective-permute-start.10) | collective-permute-done | bytes 16416 | tf_op jit(solution)/shard_map/ppermute | solution.py:493
  39.7 3.8 %collective-permute-done.11.rest_3_ = f32[2,16,128]{2,1,0:T(8,128)S(1)} collective-permute-done((f32[2,16,128]{2,1,0:T(8,128)S(1)}, f32[2,16,128]{2,1,0:T(8,128)S(1)}, u32[]{:S(2)}, u32[]{:S(2)}) %collective-permute-start.11) | collective-permute-done | bytes 16416 | tf_op jit(solution)/shard_map/ppermute | solution.py:493
  43.5 1.8 %shard_map.90 = (f32[2,20,8,256]{3,2,1,0:T(8,128)}, f32[2,20,8,256]{3,2,1,0:T(8,128)}, f32[8,256]{1,0:T(8,128)}) custom-call(f32[2,20,8,256]{3,2,1,0:T(8,128)S(1)} %get-tuple-element.18.rhs, f32[4,2,20,8,256]{4,3,2,1,0:T(8,128)S(1)} %get-tuple-element.25.powers, f32[4,2,5,8,128]{4,3,2,1,0:T(8,128)S(1)} %get-tuple-element.30.edges, ...), custom_call_target="tpu_custom_call" | custom-call | tf_op jit(solution)/shard_map/pallas_call | solution.py:538
  (6 shorter events, 0.1 us)
Async XLA Ops:
  1.9 4.5 %collective-permute-start.2 = (f32[17,8,128]{2,1,0:T(8,128)S(1)}, f32[17,8,128]{2,1,0:T(8,128)S(1)}, u32[]{:S(2)}, u32[]{:S(2)}) collective-permute-start(f32[17,8,128]{2,1,0:T(8,128)S(1)} %get-tuple-element.27), channel_id=1, source_target_pairs={{0,1},{1,0},{2,3},{3,2},{4,5},{5,4},{6,7},{7,6},{8,9},{9,8},{10,11... | collective-permute-start | bytes 208904 | tf_op jit(solution)/shard_map/ppermute | solution.py:42
  2.4 4.0 %collective-permute-start.3 = (f32[17,8,128]{2,1,0:T(8,128)S(1)}, f32[17,8,128]{2,1,0:T(8,128)S(1)}, u32[]{:S(2)}, u32[]{:S(2)}) collective-permute-start(f32[17,8,128]{2,1,0:T(8,128)S(1)} %get-tuple-element.28), channel_id=1, source_target_pairs={{0,0},{1,2},{2,1},{3,3},{4,4},{5,6},{6,5},{7,7},{8,8},{9,10},{10,9... | collective-permute-start | bytes 208904 | tf_op jit(solution)/shard_map/ppermute | solution.py:42
  3.1 8.5 %collective-permute-start = (f32[62,8,128]{2,1,0:T(8,128)S(1)}, f32[62,8,128]{2,1,0:T(8,128)S(1)}, u32[]{:S(2)}, u32[]{:S(2)}) collective-permute-start(f32[62,8,128]{2,1,0:T(8,128)S(1)} %get-tuple-element.23), channel_id=1, source_target_pairs={{0,4},{4,0},{8,12},{12,8},{1,5},{5,1},{9,13},{13,9},{2,6},{6,2},{1... | collective-permute-start | bytes 761864 | tf_op jit(solution)/shard_map/ppermute | solution.py:42
  5.8 5.9 %collective-permute-start.1 = (f32[62,8,128]{2,1,0:T(8,128)S(1)}, f32[62,8,128]{2,1,0:T(8,128)S(1)}, u32[]{:S(2)}, u32[]{:S(2)}) collective-permute-start(f32[62,8,128]{2,1,0:T(8,128)S(1)} %get-tuple-element.24), channel_id=1, source_target_pairs={{0,0},{4,8},{8,4},{12,12},{1,1},{5,9},{9,5},{13,13},{2,2},{6,10},{... | collective-permute-start | bytes 761864 | tf_op jit(solution)/shard_map/ppermute | solution.py:42
  6.5 18.3 %collective-permute-start.4 = (f32[17,8,128]{2,1,0:T(8,128)S(1)}, f32[17,8,128]{2,1,0:T(8,128)S(1)}, u32[]{:S(2)}, u32[]{:S(2)}) collective-permute-start(f32[17,8,128]{2,1,0:T(8,128)S(1)} %shard_map.87.columns), channel_id=1, source_target_pairs={{0,4},{4,0},{8,12},{12,8},{1,5},{5,1},{9,13},{13,9},{2,6},{6,2},{1... | collective-permute-start | bytes 208904 | tf_op jit(solution)/shard_map/ppermute | solution.py:42
  11.0 13.9 %collective-permute-start.5 = (f32[17,8,128]{2,1,0:T(8,128)S(1)}, f32[17,8,128]{2,1,0:T(8,128)S(1)}, u32[]{:S(2)}, u32[]{:S(2)}) collective-permute-start(f32[17,8,128]{2,1,0:T(8,128)S(1)} %shard_map.87.columns), channel_id=1, source_target_pairs={{0,0},{4,8},{8,4},{12,12},{1,1},{5,9},{9,5},{13,13},{2,2},{6,10},{... | collective-permute-start | bytes 208904 | tf_op jit(solution)/shard_map/ppermute | solution.py:42
  25.5 3.6 %collective-permute-start.6 = (f32[2,16,128]{2,1,0:T(8,128)S(1)}, f32[2,16,128]{2,1,0:T(8,128)S(1)}, u32[]{:S(2)}, u32[]{:S(2)}) collective-permute-start(f32[2,16,128]{2,1,0:T(8,128)S(1)} %get-tuple-element.32.refs_0_), channel_id=1, source_target_pairs={{0,1},{1,0},{2,3},{3,2},{4,5},{5,4},{6,7},{7,6},{8,9},{9,8},{10,11... | collective-permute-start | bytes 49160 | tf_op jit(solution)/shard_map/ppermute | solution.py:493
  27.6 3.7 %collective-permute-start.7 = (f32[2,16,128]{2,1,0:T(8,128)S(1)}, f32[2,16,128]{2,1,0:T(8,128)S(1)}, u32[]{:S(2)}, u32[]{:S(2)}) collective-permute-start(f32[2,16,128]{2,1,0:T(8,128)S(1)} %get-tuple-element.32.refs_0_), channel_id=1, source_target_pairs={{0,2},{1,3},{2,0},{3,1},{4,6},{5,7},{6,4},{7,5},{8,10},{9,11},{10,... | collective-permute-start | bytes 49160 | tf_op jit(solution)/shard_map/ppermute | solution.py:493
  29.0 3.2 %collective-permute-start.8 = (f32[2,16,128]{2,1,0:T(8,128)S(1)}, f32[2,16,128]{2,1,0:T(8,128)S(1)}, u32[]{:S(2)}, u32[]{:S(2)}) collective-permute-start(f32[2,16,128]{2,1,0:T(8,128)S(1)} %get-tuple-element.32.refs_0_), channel_id=1, source_target_pairs={{0,3},{1,2},{2,1},{3,0},{4,7},{5,6},{6,5},{7,4},{8,11},{9,10},{10,... | collective-permute-start | bytes 49160 | tf_op jit(solution)/shard_map/ppermute | solution.py:493
  32.2 7.5 %collective-permute-start.10 = (f32[2,16,128]{2,1,0:T(8,128)S(1)}, f32[2,16,128]{2,1,0:T(8,128)S(1)}, u32[]{:S(2)}, u32[]{:S(2)}) collective-permute-start(f32[2,16,128]{2,1,0:T(8,128)S(1)} %shard_map.89.rest_0_), channel_id=1, source_target_pairs={{0,8},{4,12},{8,0},{12,4},{1,9},{5,13},{9,1},{13,5},{2,10},{6,14},... | collective-permute-start | bytes 49160 | tf_op jit(solution)/shard_map/ppermute | solution.py:493
  38.0 5.5 %collective-permute-start.11 = (f32[2,16,128]{2,1,0:T(8,128)S(1)}, f32[2,16,128]{2,1,0:T(8,128)S(1)}, u32[]{:S(2)}, u32[]{:S(2)}) collective-permute-start(f32[2,16,128]{2,1,0:T(8,128)S(1)} %shard_map.89.rest_0_), channel_id=1, source_target_pairs={{0,12},{4,8},{8,4},{12,0},{1,13},{5,9},{9,5},{13,1},{2,14},{6,10},... | collective-permute-start | bytes 49160 | tf_op jit(solution)/shard_map/ppermute | solution.py:493
  39.2 4.3 %collective-permute-start.9 = (f32[2,16,128]{2,1,0:T(8,128)S(1)}, f32[2,16,128]{2,1,0:T(8,128)S(1)}, u32[]{:S(2)}, u32[]{:S(2)}) collective-permute-start(f32[2,16,128]{2,1,0:T(8,128)S(1)} %shard_map.89.rest_0_), channel_id=1, source_target_pairs={{0,4},{4,0},{8,12},{12,8},{1,5},{5,1},{9,13},{13,9},{2,6},{6,2},{1... | collective-permute-start | bytes 49160 | tf_op jit(solution)/shard_map/ppermute | solution.py:493

commit v10 on v7

--- a/solution.py
+++ b/solution.py
@@ -12,6 +12,7 @@
 ROWS = 8
 LANES = 128
 UNROLL = 5
+PIECES = 2
 SLOT = 32
 
 
@@ -75,6 +76,10 @@
 
 def ribbon_tiles(layers):
     return 3 * (layers // 4) + 2
+
+
+def packed_place(tile):
+    return tile // 8, HALO * (tile % 8)
 
 
 def between(lane, first, width):
@@ -101,9 +106,9 @@
     rows_even, _, _ = place_of("gx")
     columns_even, _, _ = place_of(("gy", "gz"))
     upper_a = (row < HALO) != rows_even
-    count = column_a.shape[0]
-    left = [jnp.zeros((ROWS, LANES), jnp.float32) for _ in range(count)]
-    right = [jnp.zeros((ROWS, LANES), jnp.float32) for _ in range(count)]
+    count = ribbon_tiles(layers)
+    zero = jnp.zeros((ROWS, LANES), jnp.float32)
+    left, right = [zero] * count, [zero] * count
     for q in range(strip_a.shape[0] // 2):
         first, second = pair_of(q, layers)
         x, y = plane(first), plane(second)
@@ -119,15 +124,25 @@
                 at = slot * SLOT
                 left[tile] = jnp.where(between(lane, at + 8, 4), turned(v[:, :LANES], at + 8), left[tile])
                 right[tile] = jnp.where(between(lane, at + 16, 4), turned(v[:, LANES:], at + 20), right[tile])
+    to_left, to_right = [zero] * column_a.shape[0], [zero] * column_a.shape[0]
     for tile in range(count):
-        column_a[tile] = jnp.where(columns_even, right[tile], left[tile])
-        column_b[tile] = jnp.where(columns_even, left[tile], right[tile])
+        group, at = packed_place(tile)
+        here = between(lane % SLOT, at, HALO)
+        to_left[group] = jnp.where(here, turned(left[tile], at - 8), to_left[group])
+        to_right[group] = jnp.where(here, turned(right[tile], at - 16), to_right[group])
+    for group in range(column_a.shape[0]):
+        column_a[group] = jnp.where(columns_even, to_right[group], to_left[group])
+        column_b[group] = jnp.where(columns_even, to_left[group], to_right[group])
 
 
 def beside_kernel(from_a, from_b, columns):
-    _, has_a, has_b = place_of(("gy", "gz"))
-    for tile in range(columns.shape[0]):
-        columns[tile] = jnp.where(has_a, from_a[tile], 0.0) + jnp.where(has_b, from_b[tile], 0.0)
+    even, has_a, has_b = place_of(("gy", "gz"))
+    count = from_a.shape[0]
+    for group in range(count):
+        a = jnp.where(has_a, from_a[group], 0.0)
+        b = jnp.where(has_b, from_b[group], 0.0)
+        columns[group] = jnp.where(even, a, b)
+        columns[count + group] = jnp.where(even, b, a)
 
 
 def two_sum(a, b):
@@ -185,7 +200,77 @@
     return pltpu.roll(v, 1, 1)
 
 
-def horizontal(g0, g1, e_row, e_col, e_half):
+class Tiles:
+    def __init__(self, tiles):
+        self.tiles = tiles
+
+    @staticmethod
+    def load(ref):
+        return Tiles([ref[r : r + ROWS, c : c + LANES] for r in (0, ROWS) for c in (0, LANES)])
+
+    def store(self, ref):
+        for v, (r, c) in zip(self.tiles, ((0, 0), (0, LANES), (ROWS, 0), (ROWS, LANES))):
+            ref[r : r + ROWS, c : c + LANES] = v
+
+    def both(self, other, op):
+        if isinstance(other, Tiles):
+            return Tiles([op(x, y) for x, y in zip(self.tiles, other.tiles)])
+        return Tiles([op(x, other) for x in self.tiles])
+
+    def __add__(self, other):
+        return self.both(other, lambda x, y: x + y)
+
+    def __sub__(self, other):
+        return self.both(other, lambda x, y: x - y)
+
+    def __mul__(self, other):
+        return self.both(other, lambda x, y: x * y)
+
+    __rmul__ = __mul__
+
+
+class Moves:
+    def __init__(self):
+        row = lax.broadcasted_iota(jnp.int32, (ROWS, LANES), 0)
+        lane = lax.broadcasted_iota(jnp.int32, (ROWS, LANES), 1)
+        self.first_row, self.last_row = row == 0, row == ROWS - 1
+        self.first_lane, self.last_lane = lane == 0, lane == LANES - 1
+
+    def rows(self, v, shift, edge):
+        own0, own1, halo0, halo1 = [pltpu.roll(x, shift, 0) for x in v.tiles]
+        return Tiles(
+            [
+                jnp.where(edge, halo0, own0),
+                jnp.where(edge, halo1, own1),
+                jnp.where(edge, own0, halo0),
+                jnp.where(edge, own1, halo1),
+            ]
+        )
+
+    def row_next(self, v):
+        return self.rows(v, ROWS - 1, self.last_row)
+
+    def row_prev(self, v):
+        return self.rows(v, 1, self.first_row)
+
+    def col_next(self, v):
+        own0, own1, halo0, halo1 = [pltpu.roll(x, LANES - 1, 1) for x in v.tiles]
+        return Tiles([jnp.where(self.last_lane, own1, own0), own1, jnp.where(self.last_lane, halo1, halo0), halo1])
+
+    def col_prev(self, v):
+        own0, own1, halo0, halo1 = [pltpu.roll(x, 1, 1) for x in v.tiles]
+        return Tiles([own0, jnp.where(self.first_lane, own0, own1), halo0, jnp.where(self.first_lane, halo0, halo1)])
+
+
+class Turns:
+    row_next = staticmethod(row_next)
+    row_prev = staticmethod(row_prev)
+    col_next = staticmethod(col_next)
+    col_prev = staticmethod(col_prev)
+
+
+def horizontal(g0, g1, e_row, e_col, e_half, moves):
+    row_next, row_prev, col_next, col_prev = moves.row_next, moves.row_prev, moves.col_next, moves.col_prev
     g0n, g1n = row_next(g0), col_next(g1)
     f = e_half * (g1n - col_prev(g1))
     h = e_half * (g0n - row_prev(g0))
@@ -240,11 +325,13 @@
     for tile, v in enumerate(strips):
         ribbon[tile] = v
 
+    moves = Moves()
+    load = Tiles.load
     for k in range(layers):
-        e = eta_half[k]
-        eta_row[k] = 2.0 * (e + row_next(e))
-        eta_col[k] = 0.5 * (e + col_next(e))
-        eta_up[k] = e + eta_half[k + 1] if k + 1 < layers else jnp.zeros_like(e)
+        e = load(eta_half.at[k])
+        (2.0 * (e + moves.row_next(e))).store(eta_row.at[k])
+        (0.5 * (e + moves.col_next(e))).store(eta_col.at[k])
+        eta_up[k] = eta_half[k] + eta_half[k + 1] if k + 1 < layers else jnp.zeros_like(eta_up[k])
         if k:
             eta_half[k - 1] = 0.5 * eta_half[k - 1]
     eta_half[layers - 1] = 0.5 * eta_half[layers - 1]
@@ -252,32 +339,36 @@
     def apply(t, src, dst):
         def layer(k, carry):
             below0, below1, odd, even = carry
-            g0, g1 = src[0, k], src[1, k]
+            g0, g1 = load(src.at[0, k]), load(src.at[1, k])
             after = jnp.minimum(k + 1, layers - 1)
-            e_up = eta_up[k]
-            up0 = e_up * (g0 - src[0, after])
-            up1 = e_up * (g1 - src[1, after])
-            out0, out1 = horizontal(g0, g1, eta_row[k], eta_col[k], eta_half[k])
-            m = cover[...]
-            out0, out1 = m * (out0 + (up0 - below0)), m * (out1 + (up1 - below1))
+            e_up = load(eta_up.at[k])
+            up0 = e_up * (g0 - load(src.at[0, after]))
+            up1 = e_up * (g1 - load(src.at[1, after]))
+            out0, out1 = horizontal(g0, g1, load(eta_row.at[k]), load(eta_col.at[k]), load(eta_half.at[k]), moves)
+            m = load(cover)
+            out0, out1 = m * (out0 + (up0 - Tiles(below0))), m * (out1 + (up1 - Tiles(below1)))
             if t < STEPS:
-                dst[0, k], dst[1, k] = out0, out1
+                out0.store(dst.at[0, k])
+                out1.store(dst.at[1, k])
+            odd, even = list(odd), list(even)
             for c, g, out in ((0, g0, out0), (1, g1, out1)):
-                now = out[:ROWS]
-                powers[t - 1, c, k] = now
-                odd = odd + g[:ROWS] * now
-                even = even + now * now
-            return up0, up1, odd, even
+                for half in range(2):
+                    now = out.tiles[half]
+                    powers[t - 1, c, k, :, half * LANES : (half + 1) * LANES] = now
+                    odd[half] = odd[half] + g.tiles[half] * now
+                    even[half] = even[half] + now * now
+            return up0.tiles, up1.tiles, odd, even
 
         def block(b, carry):
             for i in range(UNROLL):
                 carry = layer(b * UNROLL + i, carry)
             return carry
 
-        zero = jnp.zeros((ROWS, 2 * LANES), jnp.float32)
-        d = drag[...]
-        start = (-d * src[0, 0], -d * src[1, 0], zero, zero)
-        return lax.fori_loop(0, layers // UNROLL, block, start)[2:]
+        zero = [jnp.zeros((ROWS, LANES), jnp.float32)] * 2
+        d = -1.0 * load(drag)
+        start = ((d * load(src.at[0, 0])).tiles, (d * load(src.at[1, 0])).tiles, zero, zero)
+        ends = lax.fori_loop(0, layers // UNROLL, block, start)[2:]
+        return [jnp.concatenate(v, 1) for v in ends]
 
     bare = 1.0 - ice[...].astype(jnp.float32)
     whole = jnp.zeros((ROWS, 2 * LANES), jnp.float32)
@@ -303,9 +394,16 @@
     below_and_above, _ = beyond()
     lane = lax.broadcasted_iota(jnp.int32, (2 * ROWS, LANES), 1)
 
+    count = columns.shape[0] // 2
+    beside = [
+        jnp.concatenate([columns[i], below_and_above(columns_a[i], columns_b[i])], 0) for i in range(2 * count)
+    ]
+    spot = lane % SLOT
+
     def whole(tile):
-        side = jnp.concatenate([columns[tile], below_and_above(columns_a[tile], columns_b[tile])], 0)
-        return ribbon[tile] + side
+        group, at = packed_place(tile)
+        right = jnp.where(between(spot, 8, HALO), turned(beside[group], 8 - at), ribbon[tile])
+        return jnp.where(between(spot, 16, HALO), turned(beside[count + group], 16 - at), right)
 
     field = [[whole(c * tiles + n) for n in range(tiles)] for c in range(2)]
     eta = [whole(2 * tiles + n) for n in range(tiles)]
@@ -327,7 +425,7 @@
         result = ([], [])
         odd = even = jnp.zeros((ROWS, LANES), jnp.float32)
         for n in range(tiles):
-            outs = horizontal(field[0][n], field[1][n], eta_row[n], eta_col[n], eta_half[n])
+            outs = horizontal(field[0][n], field[1][n], eta_row[n], eta_col[n], eta_half[n], Turns)
             for c in range(2):
                 below = ups[c][n - 1] if n else turned(ups[c][-1], SLOT) - drag * field[c][0]
                 out = cover * (outs[c] + (ups[c][n] - below))
@@ -438,7 +536,7 @@
 
 
 def final_kernel(rhs, powers, edges, friction, ice, grounded, speed, *rest):
-    *parts, iterate, residual, hessian = rest
+    *parts, iterate_out, residual_out, hessian, iterate, residual, gone = rest
     layers, tiles = rhs.shape[1], edges.shape[2]
     total = (parts[0][0], parts[0][1])
     for x in parts[1:]:
@@ -458,6 +556,8 @@
             y = y + weights[t] * vectors[t]
         return x, y
 
+    piece = layers // PIECES
+    copies = []
     for c in range(2):
         side = [combined([edges[t, c, n] for t in range(STEPS)], factors) for n in range(tiles)]
         for k in range(layers):
@@ -472,8 +572,15 @@
             x, y = patched
             iterate[c, k] = jnp.where(cover > 0.0, wide[0] * r + x, rest * r)
             residual[c, k] = r - jnp.where(cover > 0.0, y, rest * r)
+            if (k + 1) % piece == 0:
+                for i, (src, dst) in enumerate(((iterate, iterate_out), (residual, residual_out))):
+                    part = (c, pl.ds(k + 1 - piece, piece))
+                    copies.append(pltpu.make_async_copy(src.at[part], dst.at[part], gone.at[len(copies)]))
+                    copies[-1].start()
     weight = cover * (friction[...] * grounded[...].astype(jnp.float32))
     hessian[...] = weight * (speed[0] * iterate[0, 0] + speed[1] * iterate[1, 0])
+    for copy in copies:
+        copy.wait()
 
 
 def exchange(x, axis):
@@ -503,21 +610,23 @@
     inputs = (adjoint_rhs, viscosity, friction, ice_mask, grounded, basal_velocity)
     tile = (ROWS, LANES)
     strips = (2 * (layers + layers // 2 + 1),) + tile
-    ribbons = (ribbon_tiles(layers),) + tile
+    ribbons = ribbon_tiles(layers)
+    packed = ((ribbons + 7) // 8,) + tile
+    both = (2 * packed[0],) + tile
     *held, column_a, column_b, strip_a, strip_b = call(
         pack_kernel,
-        [jax.ShapeDtypeStruct(x.shape, x.dtype) for x in inputs] + [ribbons, ribbons, strips, strips],
+        [jax.ShapeDtypeStruct(x.shape, x.dtype) for x in inputs] + [packed, packed, strips, strips],
         [pltpu.SemaphoreType.DMA((len(inputs),))],
         in_specs=[pl.BlockSpec(memory_space=pltpu.HBM)] * len(inputs),
     )(*[pltpu.with_memory_space_constraint(x, pltpu.HBM) for x in inputs])
     strip_a, strip_b = swapped(strip_a, "gx", 0), swapped(strip_b, "gx", 1)
     beside = ("gy", "gz")
-    (columns,) = call(beside_kernel, [ribbons])(swapped(column_a, beside, 0), swapped(column_b, beside, 1))
+    (columns,) = call(beside_kernel, [both])(swapped(column_a, beside, 0), swapped(column_b, beside, 1))
     columns_a, columns_b = swapped(columns, "gx", 0), swapped(columns, "gx", 1)
     block = (layers, 2 * ROWS, 2 * LANES)
     powers, sums, ribbon = call(
         main_kernel,
-        [(STEPS,) + adjoint_rhs.shape, (2 * STEPS + 1, ROWS, 2 * LANES), (ribbons[0], 2 * ROWS, LANES)],
+        [(STEPS,) + adjoint_rhs.shape, (2 * STEPS + 1, ROWS, 2 * LANES), (ribbons, 2 * ROWS, LANES)],
         [(2,) + block] * 2 + [block] * 4 + [block[1:]] * 2,
         cost_estimate=pl.CostEstimate(flops=200_000_000, bytes_accessed=8_000_000, transcendentals=0),
     )(*held[:5], strip_a, strip_b)
@@ -531,7 +640,12 @@
     parts = exchange(sums, "gx")
     rhs, _, friction, ice_mask, grounded, speed = held
     return tuple(
-        call(final_kernel, [adjoint_rhs.shape, adjoint_rhs.shape, friction.shape])(
+        call(
+            final_kernel,
+            [adjoint_rhs.shape, adjoint_rhs.shape, friction.shape],
+            [adjoint_rhs.shape] * 2 + [pltpu.SemaphoreType.DMA((4 * PIECES,))],
+            out_specs=[pl.BlockSpec(memory_space=pltpu.HBM)] * 2 + [pl.BlockSpec(memory_space=pltpu.VMEM)],
+        )(
             rhs, powers, edges, friction, ice_mask, grounded, speed, *parts
         )
     )

time: 36.6 us -> 36.6 us (level)
  Pallas kernels: 8.02 us -> 8.68 us
    pallas_call x2, Pallas kernels: 1.83 us -> 2.37 us  [the longest x1 2.37 us: body(): call(final_kernel, [adjoint_rhs.shape, adjoint_rhs.shape, friction.shape]...]
where the time goes in v10:
time: 36.6 us; the launch traced here: 36.4 us
  starting transfers between devices  19.1 us (52%)
  Pallas kernels  8.68 us (24%)
  waiting for transfers between devices  7.94 us (22%)
  between operations  0.73 us (2%)
    ppermute x6, starting transfers between devices, swapped(): return lax.ppermute(x, axis, pairs)  9.59 us
    ppermute x6, starting transfers between devices, exchange(): parts.append(lax.ppermute(x, axis, pairs))  9.48 us
    ppermute x6, waiting for transfers between devices, exchange(): parts.append(lax.ppermute(x, axis, pairs))  7.43 us
    pallas_call x1, Pallas kernels, body(): call(main_kernel, [(STEPS,) + adjoint_rhs.shape, (2 * STEPS + 1, ROWS, 2...  4.2 us
    pallas_call x1, Pallas kernels, body(): call(final_kernel, [adjoint_rhs.shape, adjoint_rhs.shape, friction.shape]...  2.37 us
    pallas_call x1, Pallas kernels, body(): call(pack_kernel, [jax.ShapeDtypeStruct(x.shape, x.dtype) for x in inputs...  1.35 us
    pallas_call x1, Pallas kernels, body(): call(ribbon_kernel, [(STEPS, 2, layers // 4) + tile, (2, 2 * ROWS, LANES)])  0.74 us
  transfers between devices with their start and end apart: 12, of which 5 were waited for; matrix products, arithmetic and copies ran while one was open for 0% of the time, Pallas kernels for 12%

profile of v10, /device:TPU:0, one launch (start us, length us, event | category | flops | bytes accessed | tf_op | source)
XLA Modules:
  0.0 36.4 jit_solution(15003135586229274029)
XLA Ops:
  0.6 1.3 %shard_map.85 = (f32[2,20,8,256]{3,2,1,0:T(8,128)S(1)}, f32[20,8,256]{2,1,0:T(8,128)S(1)}, f32[8,256]{1,0:T(8,128)S(1)}, s32[8,256]{1,0:T(8,128)S(1)}, s32[8,256...) custom-call(f32[2,20,8,256]{3,2,1,0:T(8,128)} %refs_0_.1, ...), custom_call_target="tpu_custom_call" | custom-call | tf_op jit(solution)/shard_map/pallas_call | solution.py:616
  2.0 3.1 %collective-permute-start = (f32[62,8,128]{2,1,0:T(8,128)S(1)}, f32[62,8,128]{2,1,0:T(8,128)S(1)}, u32[]{:S(2)}, u32[]{:S(2)}) collective-permute-start(f32[62,8,128]{2,1,0:T(8,128)S(1)} %get-tuple-element.23), channel_id=1, source_target_pairs={{0,4},{4,0},{8,12},{12,8},{1,5},{5,1},{9,13},{13,9},{2,6},{6,2},{1... | collective-permute-start | bytes 761864 | tf_op jit(solution)/shard_map/ppermute | solution.py:43
  5.1 0.7 %collective-permute-start.1 = (f32[62,8,128]{2,1,0:T(8,128)S(1)}, f32[62,8,128]{2,1,0:T(8,128)S(1)}, u32[]{:S(2)}, u32[]{:S(2)}) collective-permute-start(f32[62,8,128]{2,1,0:T(8,128)S(1)} %get-tuple-element.24), channel_id=1, source_target_pairs={{0,0},{4,8},{8,4},{12,12},{1,1},{5,9},{9,5},{13,13},{2,2},{6,10},{... | collective-permute-start | bytes 761864 | tf_op jit(solution)/shard_map/ppermute | solution.py:43
  5.8 0.1 collective-permute-start.2
  5.8 0.7 %collective-permute-start.3 = (f32[3,8,128]{2,1,0:T(8,128)S(1)}, f32[3,8,128]{2,1,0:T(8,128)S(1)}, u32[]{:S(2)}, u32[]{:S(2)}) collective-permute-start(f32[3,8,128]{2,1,0:T(8,128)S(1)} %get-tuple-element.28), channel_id=1, source_target_pairs={{0,0},{1,2},{2,1},{3,3},{4,4},{5,6},{6,5},{7,7},{8,8},{9,10},{10,9... | collective-permute-start | bytes 36872 | tf_op jit(solution)/shard_map/ppermute | solution.py:43
  6.5 0.5 %collective-permute-done.2.from_a = f32[3,8,128]{2,1,0:T(8,128)S(1)} collective-permute-done((f32[3,8,128]{2,1,0:T(8,128)S(1)}, f32[3,8,128]{2,1,0:T(8,128)S(1)}, u32[]{:S(2)}, u32[]{:S(2)}) %collective-permute-start.2) | collective-permute-done | bytes 12320 | tf_op jit(solution)/shard_map/ppermute | solution.py:43
  7.0 0.0 collective-permute-done.3.from_b
  7.0 4.4 %collective-permute-start.4 = (f32[6,8,128]{2,1,0:T(8,128)S(1)}, f32[6,8,128]{2,1,0:T(8,128)S(1)}, u32[]{:S(2)}, u32[]{:S(2)}) collective-permute-start(f32[6,8,128]{2,1,0:T(8,128)S(1)} %shard_map.87.columns), channel_id=1, source_target_pairs={{0,4},{4,0},{8,12},{12,8},{1,5},{5,1},{9,13},{13,9},{2,6},{6,2},{1... | collective-permute-start | bytes 73736 | tf_op jit(solution)/shard_map/ppermute | solution.py:43
  11.5 0.7 %collective-permute-start.5 = (f32[6,8,128]{2,1,0:T(8,128)S(1)}, f32[6,8,128]{2,1,0:T(8,128)S(1)}, u32[]{:S(2)}, u32[]{:S(2)}) collective-permute-start(f32[6,8,128]{2,1,0:T(8,128)S(1)} %shard_map.87.columns), channel_id=1, source_target_pairs={{0,0},{4,8},{8,4},{12,12},{1,1},{5,9},{9,5},{13,13},{2,2},{6,10},{... | collective-permute-start | bytes 73736 | tf_op jit(solution)/shard_map/ppermute | solution.py:43
  12.1 0.0 collective-permute-done.1.strip_b
  12.1 4.2 %shard_map.86 = (f32[4,2,20,8,256]{4,3,2,1,0:T(8,128)S(1)}, f32[9,8,256]{2,1,0:T(8,128)S(1)}, f32[17,16,128]{2,1,0:T(8,128)S(1)}) custom-call(f32[2,20,8,256]{3,2,1,0:T(8,128)S(1)} %get-tuple-element.18.rhs, f32[20,8,256]{2,1,0:T(8,128)S(1)} %get-tuple-element.19.eta, f32[8,256]{1,0:T(8,128)S(1)} %get-tuple-element.20.friction, ...), custom_call_target="tpu_custom_call" | custom-call | flops 200000000 | bytes 8000000 | tf_op jit(solution)/shard_map/pallas_call | solution.py:627
  16.3 0.0 collective-permute-done.5.columns_b
  16.4 0.7 %shard_map.88 = (f32[4,2,5,8,128]{4,3,2,1,0:T(8,128)S(1)}, f32[2,16,128]{2,1,0:T(8,128)S(1)}) custom-call(f32[17,16,128]{2,1,0:T(8,128)S(1)} %get-tuple-element.26.ribbon, f32[6,8,128]{2,1,0:T(8,128)S(1)} %shard_map.87.columns, f32[6,8,128]{2,1,0:T(8,128)S(1)} %collective-permute-done.4.columns_a, f32[6,8,128]{2,1,0:T(8,128)S(1)} %collective-permute-done.5.columns_b, ...), custom_call_target="tpu_custom_call" | custom-call | tf_op jit(solution)/shard_map/pallas_call | solution.py:633
  17.1 4.3 %collective-permute-start.6 = (f32[2,16,128]{2,1,0:T(8,128)S(1)}, f32[2,16,128]{2,1,0:T(8,128)S(1)}, u32[]{:S(2)}, u32[]{:S(2)}) collective-permute-start(f32[2,16,128]{2,1,0:T(8,128)S(1)} %get-tuple-element.32.refs_0_), channel_id=1, source_target_pairs={{0,1},{1,0},{2,3},{3,2},{4,5},{5,4},{6,7},{7,6},{8,9},{9,8},{10,11... | collective-permute-start | bytes 49160 | tf_op jit(solution)/shard_map/ppermute | solution.py:601
  21.4 1.1 %collective-permute-start.7 = (f32[2,16,128]{2,1,0:T(8,128)S(1)}, f32[2,16,128]{2,1,0:T(8,128)S(1)}, u32[]{:S(2)}, u32[]{:S(2)}) collective-permute-start(f32[2,16,128]{2,1,0:T(8,128)S(1)} %get-tuple-element.32.refs_0_), channel_id=1, source_target_pairs={{0,2},{1,3},{2,0},{3,1},{4,6},{5,7},{6,4},{7,5},{8,10},{9,11},{10,... | collective-permute-start | bytes 49160 | tf_op jit(solution)/shard_map/ppermute | solution.py:601
  22.5 0.4 collective-permute-start.8
  22.9 0.0 collective-permute-done.6.refs_1_
  22.9 2.3 %collective-permute-done.7.refs_2_ = f32[2,16,128]{2,1,0:T(8,128)S(1)} collective-permute-done((f32[2,16,128]{2,1,0:T(8,128)S(1)}, f32[2,16,128]{2,1,0:T(8,128)S(1)}, u32[]{:S(2)}, u32[]{:S(2)}) %collective-permute-start.7) | collective-permute-done | bytes 16416 | tf_op jit(solution)/shard_map/ppermute | solution.py:601
  25.2 0.5 %collective-permute-done.8.refs_3_ = f32[2,16,128]{2,1,0:T(8,128)S(1)} collective-permute-done((f32[2,16,128]{2,1,0:T(8,128)S(1)}, f32[2,16,128]{2,1,0:T(8,128)S(1)}, u32[]{:S(2)}, u32[]{:S(2)}) %collective-permute-start.8) | collective-permute-done | bytes 16416 | tf_op jit(solution)/shard_map/ppermute | solution.py:601
  25.7 2.8 %collective-permute-start.10 = (f32[2,16,128]{2,1,0:T(8,128)S(1)}, f32[2,16,128]{2,1,0:T(8,128)S(1)}, u32[]{:S(2)}, u32[]{:S(2)}) collective-permute-start(f32[2,16,128]{2,1,0:T(8,128)S(1)} %shard_map.89.rest_0_), channel_id=1, source_target_pairs={{0,8},{4,12},{8,0},{12,4},{1,9},{5,13},{9,1},{13,5},{2,10},{6,14},... | collective-permute-start | bytes 49160 | tf_op jit(solution)/shard_map/ppermute | solution.py:601
  28.5 0.9 %collective-permute-start.11 = (f32[2,16,128]{2,1,0:T(8,128)S(1)}, f32[2,16,128]{2,1,0:T(8,128)S(1)}, u32[]{:S(2)}, u32[]{:S(2)}) collective-permute-start(f32[2,16,128]{2,1,0:T(8,128)S(1)} %shard_map.89.rest_0_), channel_id=1, source_target_pairs={{0,12},{4,8},{8,4},{12,0},{1,13},{5,9},{9,5},{13,1},{2,14},{6,10},... | collective-permute-start | bytes 49160 | tf_op jit(solution)/shard_map/ppermute | solution.py:601
  29.4 1.1 %collective-permute-done.10.rest_2_ = f32[2,16,128]{2,1,0:T(8,128)S(1)} collective-permute-done((f32[2,16,128]{2,1,0:T(8,128)S(1)}, f32[2,16,128]{2,1,0:T(8,128)S(1)}, u32[]{:S(2)}, u32[]{:S(2)}) %collective-permute-start.10) | collective-permute-done | bytes 16416 | tf_op jit(solution)/shard_map/ppermute | solution.py:601
  30.5 3.5 %collective-permute-done.11.rest_3_ = f32[2,16,128]{2,1,0:T(8,128)S(1)} collective-permute-done((f32[2,16,128]{2,1,0:T(8,128)S(1)}, f32[2,16,128]{2,1,0:T(8,128)S(1)}, u32[]{:S(2)}, u32[]{:S(2)}) %collective-permute-start.11) | collective-permute-done | bytes 16416 | tf_op jit(solution)/shard_map/ppermute | solution.py:601
  34.0 2.4 %shard_map.90 = (f32[2,20,8,256]{3,2,1,0:T(8,128)}, f32[2,20,8,256]{3,2,1,0:T(8,128)}, f32[8,256]{1,0:T(8,128)}) custom-call(f32[2,20,8,256]{3,2,1,0:T(8,128)S(1)} %get-tuple-element.18.rhs, f32[4,2,20,8,256]{4,3,2,1,0:T(8,128)S(1)} %get-tuple-element.25.powers, f32[4,2,5,8,128]{4,3,2,1,0:T(8,128)S(1)} %get-tuple-element.30.edges, ...), custom_call_target="tpu_custom_call" | custom-call | tf_op jit(solution)/shard_map/pallas_call | solution.py:643
  (6 shorter events, 0.0 us)
Async XLA Ops:
  2.0 10.1 %collective-permute-start = (f32[62,8,128]{2,1,0:T(8,128)S(1)}, f32[62,8,128]{2,1,0:T(8,128)S(1)}, u32[]{:S(2)}, u32[]{:S(2)}) collective-permute-start(f32[62,8,128]{2,1,0:T(8,128)S(1)} %get-tuple-element.23), channel_id=1, source_target_pairs={{0,4},{4,0},{8,12},{12,8},{1,5},{5,1},{9,13},{13,9},{2,6},{6,2},{1... | collective-permute-start | bytes 761864 | tf_op jit(solution)/shard_map/ppermute | solution.py:43
  5.1 7.0 %collective-permute-start.1 = (f32[62,8,128]{2,1,0:T(8,128)S(1)}, f32[62,8,128]{2,1,0:T(8,128)S(1)}, u32[]{:S(2)}, u32[]{:S(2)}) collective-permute-start(f32[62,8,128]{2,1,0:T(8,128)S(1)} %get-tuple-element.24), channel_id=1, source_target_pairs={{0,0},{4,8},{8,4},{12,12},{1,1},{5,9},{9,5},{13,13},{2,2},{6,10},{... | collective-permute-start | bytes 761864 | tf_op jit(solution)/shard_map/ppermute | solution.py:43
  5.8 1.2 %collective-permute-start.2 = (f32[3,8,128]{2,1,0:T(8,128)S(1)}, f32[3,8,128]{2,1,0:T(8,128)S(1)}, u32[]{:S(2)}, u32[]{:S(2)}) collective-permute-start(f32[3,8,128]{2,1,0:T(8,128)S(1)} %get-tuple-element.27), channel_id=1, source_target_pairs={{0,1},{1,0},{2,3},{3,2},{4,5},{5,4},{6,7},{7,6},{8,9},{9,8},{10,11... | collective-permute-start | bytes 36872 | tf_op jit(solution)/shard_map/ppermute | solution.py:43
  5.8 1.2 %collective-permute-start.3 = (f32[3,8,128]{2,1,0:T(8,128)S(1)}, f32[3,8,128]{2,1,0:T(8,128)S(1)}, u32[]{:S(2)}, u32[]{:S(2)}) collective-permute-start(f32[3,8,128]{2,1,0:T(8,128)S(1)} %get-tuple-element.28), channel_id=1, source_target_pairs={{0,0},{1,2},{2,1},{3,3},{4,4},{5,6},{6,5},{7,7},{8,8},{9,10},{10,9... | collective-permute-start | bytes 36872 | tf_op jit(solution)/shard_map/ppermute | solution.py:43
  7.0 9.3 %collective-permute-start.4 = (f32[6,8,128]{2,1,0:T(8,128)S(1)}, f32[6,8,128]{2,1,0:T(8,128)S(1)}, u32[]{:S(2)}, u32[]{:S(2)}) collective-permute-start(f32[6,8,128]{2,1,0:T(8,128)S(1)} %shard_map.87.columns), channel_id=1, source_target_pairs={{0,4},{4,0},{8,12},{12,8},{1,5},{5,1},{9,13},{13,9},{2,6},{6,2},{1... | collective-permute-start | bytes 73736 | tf_op jit(solution)/shard_map/ppermute | solution.py:43
  11.5 4.9 %collective-permute-start.5 = (f32[6,8,128]{2,1,0:T(8,128)S(1)}, f32[6,8,128]{2,1,0:T(8,128)S(1)}, u32[]{:S(2)}, u32[]{:S(2)}) collective-permute-start(f32[6,8,128]{2,1,0:T(8,128)S(1)} %shard_map.87.columns), channel_id=1, source_target_pairs={{0,0},{4,8},{8,4},{12,12},{1,1},{5,9},{9,5},{13,13},{2,2},{6,10},{... | collective-permute-start | bytes 73736 | tf_op jit(solution)/shard_map/ppermute | solution.py:43
  17.1 5.8 %collective-permute-start.6 = (f32[2,16,128]{2,1,0:T(8,128)S(1)}, f32[2,16,128]{2,1,0:T(8,128)S(1)}, u32[]{:S(2)}, u32[]{:S(2)}) collective-permute-start(f32[2,16,128]{2,1,0:T(8,128)S(1)} %get-tuple-element.32.refs_0_), channel_id=1, source_target_pairs={{0,1},{1,0},{2,3},{3,2},{4,5},{5,4},{6,7},{7,6},{8,9},{9,8},{10,11... | collective-permute-start | bytes 49160 | tf_op jit(solution)/shard_map/ppermute | solution.py:601
  21.4 3.7 %collective-permute-start.7 = (f32[2,16,128]{2,1,0:T(8,128)S(1)}, f32[2,16,128]{2,1,0:T(8,128)S(1)}, u32[]{:S(2)}, u32[]{:S(2)}) collective-permute-start(f32[2,16,128]{2,1,0:T(8,128)S(1)} %get-tuple-element.32.refs_0_), channel_id=1, source_target_pairs={{0,2},{1,3},{2,0},{3,1},{4,6},{5,7},{6,4},{7,5},{8,10},{9,11},{10,... | collective-permute-start | bytes 49160 | tf_op jit(solution)/shard_map/ppermute | solution.py:601
  22.5 3.2 %collective-permute-start.8 = (f32[2,16,128]{2,1,0:T(8,128)S(1)}, f32[2,16,128]{2,1,0:T(8,128)S(1)}, u32[]{:S(2)}, u32[]{:S(2)}) collective-permute-start(f32[2,16,128]{2,1,0:T(8,128)S(1)} %get-tuple-element.32.refs_0_), channel_id=1, source_target_pairs={{0,3},{1,2},{2,1},{3,0},{4,7},{5,6},{6,5},{7,4},{8,11},{9,10},{10,... | collective-permute-start | bytes 49160 | tf_op jit(solution)/shard_map/ppermute | solution.py:601
  25.7 4.8 %collective-permute-start.10 = (f32[2,16,128]{2,1,0:T(8,128)S(1)}, f32[2,16,128]{2,1,0:T(8,128)S(1)}, u32[]{:S(2)}, u32[]{:S(2)}) collective-permute-start(f32[2,16,128]{2,1,0:T(8,128)S(1)} %shard_map.89.rest_0_), channel_id=1, source_target_pairs={{0,8},{4,12},{8,0},{12,4},{1,9},{5,13},{9,1},{13,5},{2,10},{6,14},... | collective-permute-start | bytes 49160 | tf_op jit(solution)/shard_map/ppermute | solution.py:601
  28.5 5.5 %collective-permute-start.11 = (f32[2,16,128]{2,1,0:T(8,128)S(1)}, f32[2,16,128]{2,1,0:T(8,128)S(1)}, u32[]{:S(2)}, u32[]{:S(2)}) collective-permute-start(f32[2,16,128]{2,1,0:T(8,128)S(1)} %shard_map.89.rest_0_), channel_id=1, source_target_pairs={{0,12},{4,8},{8,4},{12,0},{1,13},{5,9},{9,5},{13,1},{2,14},{6,10},... | collective-permute-start | bytes 49160 | tf_op jit(solution)/shard_map/ppermute | solution.py:601
  29.4 4.6 %collective-permute-start.9 = (f32[2,16,128]{2,1,0:T(8,128)S(1)}, f32[2,16,128]{2,1,0:T(8,128)S(1)}, u32[]{:S(2)}, u32[]{:S(2)}) collective-permute-start(f32[2,16,128]{2,1,0:T(8,128)S(1)} %shard_map.89.rest_0_), channel_id=1, source_target_pairs={{0,4},{4,0},{8,12},{12,8},{1,5},{5,1},{9,13},{13,9},{2,6},{6,2},{1... | collective-permute-start | bytes 49160 | tf_op jit(solution)/shard_map/ppermute | solution.py:601

commit v11 on v10

--- a/solution.py
+++ b/solution.py
@@ -12,7 +12,7 @@
 ROWS = 8
 LANES = 128
 UNROLL = 5
-PIECES = 2
+FIRST = 4
 SLOT = 32
 
 
@@ -205,12 +205,13 @@
         self.tiles = tiles
 
     @staticmethod
-    def load(ref):
-        return Tiles([ref[r : r + ROWS, c : c + LANES] for r in (0, ROWS) for c in (0, LANES)])
-
-    def store(self, ref):
-        for v, (r, c) in zip(self.tiles, ((0, 0), (0, LANES), (ROWS, 0), (ROWS, LANES))):
-            ref[r : r + ROWS, c : c + LANES] = v
+    def load(ref, *place, shift=0):
+        at = FIRST + shift
+        return Tiles([ref[(half, *place, pl.ds(at + r, ROWS))] for r in (0, ROWS) for half in (0, 1)])
+
+    def store(self, ref, *place):
+        for i, v in enumerate(self.tiles):
+            ref[(i % 2, *place, pl.ds(FIRST + i // 2 * ROWS, ROWS))] = v
 
     def both(self, other, op):
         if isinstance(other, Tiles):
@@ -236,22 +237,13 @@
         self.first_row, self.last_row = row == 0, row == ROWS - 1
         self.first_lane, self.last_lane = lane == 0, lane == LANES - 1
 
-    def rows(self, v, shift, edge):
-        own0, own1, halo0, halo1 = [pltpu.roll(x, shift, 0) for x in v.tiles]
-        return Tiles(
-            [
-                jnp.where(edge, halo0, own0),
-                jnp.where(edge, halo1, own1),
-                jnp.where(edge, own0, halo0),
-                jnp.where(edge, own1, halo1),
-            ]
-        )
-
     def row_next(self, v):
-        return self.rows(v, ROWS - 1, self.last_row)
+        top0, top1, low0, low1 = [pltpu.roll(x, ROWS - 1, 0) for x in v.tiles]
+        return Tiles([jnp.where(self.last_row, low0, top0), jnp.where(self.last_row, low1, top1), low0, low1])
 
     def row_prev(self, v):
-        return self.rows(v, 1, self.first_row)
+        top0, top1, low0, low1 = [pltpu.roll(x, 1, 0) for x in v.tiles]
+        return Tiles([top0, top1, jnp.where(self.first_row, top0, low0), jnp.where(self.first_row, top1, low1)])
 
     def col_next(self, v):
         own0, own1, halo0, halo1 = [pltpu.roll(x, LANES - 1, 1) for x in v.tiles]
@@ -269,26 +261,25 @@
     col_prev = staticmethod(col_prev)
 
 
-def horizontal(g0, g1, e_row, e_col, e_half, moves):
+def horizontal(g0, g1, e_row, e_row_prev, e_col, e_half, moves, rows=None):
     row_next, row_prev, col_next, col_prev = moves.row_next, moves.row_prev, moves.col_next, moves.col_prev
-    g0n, g1n = row_next(g0), col_next(g1)
-    f = e_half * (g1n - col_prev(g1))
-    h = e_half * (g0n - row_prev(g0))
-    flux = e_row * (g0 - g0n)
-    out0 = flux - row_next(f) - row_prev(flux - f)
+    g0n, g0p, g1n, g1p = rows or (row_next(g0), row_prev(g0), row_next(g1), row_prev(g1))
+    g1c = col_next(g1)
+    f = e_half * (g1c - col_prev(g1))
+    h = e_half * (g0n - g0p)
+    out0 = e_row * (g0 - g0n) + e_row_prev * (g0 - g0p) - row_next(f) + row_prev(f)
     flux = e_col * (g0 - col_next(g0))
     out0 = out0 + (flux - col_prev(flux))
-    flux = (4.0 * e_col) * (g1 - g1n)
+    flux = (4.0 * e_col) * (g1 - g1c)
     out1 = flux - col_next(h) - col_prev(flux - h)
-    flux = (0.25 * e_row) * (g1 - row_next(g1))
-    out1 = out1 + (flux - row_prev(flux))
+    out1 = out1 + 0.25 * (e_row * (g1 - g1n) + e_row_prev * (g1 - g1p))
     return out0, out1
 
 
 def main_kernel(
     rhs, eta, friction, ice, grounded, strip_a, strip_b,
-    powers, sums, ribbon,
-    field_a, field_b, eta_row, eta_col, eta_half, eta_up, cover, drag,
+    power_1, power_2, power_3, power_4, sums, ribbon,
+    masked, eta_row, eta_col, eta_half, eta_up, cover, drag,
 ):
     layers = eta.shape[0]
     plane = own_planes(rhs, eta, friction, ice, grounded)
@@ -297,10 +288,10 @@
 
     def target(p):
         if p < 2 * layers:
-            return field_a.at[p // layers, p % layers]
+            return masked, (p // layers, p % layers)
         if p < 3 * layers:
-            return eta_half.at[p - 2 * layers]
-        return cover if p == 3 * layers else drag
+            return eta_half, (p - 2 * layers,)
+        return (cover if p == 3 * layers else drag), ()
 
     strips = [jnp.zeros((2 * ROWS, LANES), jnp.float32) for _ in range(ribbon.shape[0])]
     for q in range(strip_a.shape[0] // 2):
@@ -312,9 +303,11 @@
             halves[1].append(pltpu.roll(above_and_below(from_a, from_b), HALO, 0))
         for p, halo in zip((first, second), halves):
             v = plane(p)
-            dst = target(p)
-            dst[0:ROWS, :] = v
-            dst[ROWS:, 0:LANES], dst[ROWS:, LANES:] = halo
+            ref, at = target(p)
+            for half in range(2):
+                ref[(half, *at, pl.ds(FIRST + HALO, ROWS))] = v[:, half * LANES : (half + 1) * LANES]
+                ref[(half, *at, pl.ds(FIRST, HALO))] = halo[half][HALO:]
+                ref[(half, *at, pl.ds(FIRST + HALO + ROWS, HALO))] = halo[half][:HALO]
             head = jnp.concatenate([v[:, :LANES], halo[0]], 0)
             tail = jnp.concatenate([v[:, LANES:], halo[1]], 0)
             tile, slots = ribbon_places(p, layers)
@@ -327,48 +320,48 @@
 
     moves = Moves()
     load = Tiles.load
+    before = None
     for k in range(layers):
-        e = load(eta_half.at[k])
-        (2.0 * (e + moves.row_next(e))).store(eta_row.at[k])
-        (0.5 * (e + moves.col_next(e))).store(eta_col.at[k])
-        eta_up[k] = eta_half[k] + eta_half[k + 1] if k + 1 < layers else jnp.zeros_like(eta_up[k])
+        e = load(eta_half, k)
+        (2.0 * (e + load(eta_half, k, shift=1))).store(eta_row, k)
+        (0.5 * (e + moves.col_next(e))).store(eta_col, k)
         if k:
-            eta_half[k - 1] = 0.5 * eta_half[k - 1]
-    eta_half[layers - 1] = 0.5 * eta_half[layers - 1]
-
-    def apply(t, src, dst):
+            (before + e).store(eta_up, k - 1)
+        before = e
+    (0.0 * before).store(eta_up, layers - 1)
+    for k in range(layers):
+        (0.5 * load(eta_half, k)).store(eta_half, k)
+
+    def apply(src, dst):
         def layer(k, carry):
             below0, below1, odd, even = carry
-            g0, g1 = load(src.at[0, k]), load(src.at[1, k])
+            g0, g1 = load(src, 0, k), load(src, 1, k)
             after = jnp.minimum(k + 1, layers - 1)
-            e_up = load(eta_up.at[k])
-            up0 = e_up * (g0 - load(src.at[0, after]))
-            up1 = e_up * (g1 - load(src.at[1, after]))
-            out0, out1 = horizontal(g0, g1, load(eta_row.at[k]), load(eta_col.at[k]), load(eta_half.at[k]), moves)
+            e_up = load(eta_up, k)
+            up0 = e_up * (g0 - load(src, 0, after))
+            up1 = e_up * (g1 - load(src, 1, after))
+            rows = [load(src, c, k, shift=d) for c in (0, 1) for d in (1, -1)]
+            coefficients = (load(eta_row, k), load(eta_row, k, shift=-1), load(eta_col, k), load(eta_half, k))
+            out0, out1 = horizontal(g0, g1, *coefficients, moves, rows)
             m = load(cover)
             out0, out1 = m * (out0 + (up0 - Tiles(below0))), m * (out1 + (up1 - Tiles(below1)))
-            if t < STEPS:
-                out0.store(dst.at[0, k])
-                out1.store(dst.at[1, k])
-            odd, even = list(odd), list(even)
-            for c, g, out in ((0, g0, out0), (1, g1, out1)):
-                for half in range(2):
-                    now = out.tiles[half]
-                    powers[t - 1, c, k, :, half * LANES : (half + 1) * LANES] = now
-                    odd[half] = odd[half] + g.tiles[half] * now
-                    even[half] = even[half] + now * now
-            return up0.tiles, up1.tiles, odd, even
+            out0.store(dst, 0, k)
+            out1.store(dst, 1, k)
+            odd = Tiles(odd) + (g0 * out0 + g1 * out1)
+            even = Tiles(even) + (out0 * out0 + out1 * out1)
+            return up0.tiles, up1.tiles, odd.tiles, even.tiles
 
         def block(b, carry):
             for i in range(UNROLL):
                 carry = layer(b * UNROLL + i, carry)
             return carry
 
-        zero = [jnp.zeros((ROWS, LANES), jnp.float32)] * 2
+        zero = [jnp.zeros((ROWS, LANES), jnp.float32)] * 4
         d = -1.0 * load(drag)
-        start = ((d * load(src.at[0, 0])).tiles, (d * load(src.at[1, 0])).tiles, zero, zero)
+        start = ((d * load(src, 0, 0)).tiles, (d * load(src, 1, 0)).tiles, zero, zero)
         ends = lax.fori_loop(0, layers // UNROLL, block, start)[2:]
-        return [jnp.concatenate(v, 1) for v in ends]
+        halo = lax.broadcasted_iota(jnp.int32, (ROWS, LANES), 0) < HALO
+        return [jnp.concatenate([jnp.where(halo, v[2 + i], v[i]) for i in (0, 1)], 1) for v in ends]
 
     bare = 1.0 - ice[...].astype(jnp.float32)
     whole = jnp.zeros((ROWS, 2 * LANES), jnp.float32)
@@ -381,12 +374,11 @@
     sums[0] = whole
     wide = lax.broadcasted_iota(jnp.int32, (ROWS, 2 * LANES), 1)
     inner = between(wide, HALO, 2 * LANES - 2 * HALO)
-    src, dst = field_a, field_b
+    fields = (masked, power_1, power_2, power_3, power_4)
     for t in range(1, STEPS + 1):
-        odd, even = apply(t, src, dst)
+        odd, even = apply(fields[t - 1], fields[t])
         sums[2 * t - 1] = jnp.where(inner, odd, 0.0) + outside
         sums[2 * t] = jnp.where(inner, even, 0.0) + outside
-        src, dst = dst, src
 
 
 def ribbon_kernel(ribbon, columns, columns_a, columns_b, sums, edges, moments):
@@ -413,6 +405,7 @@
         return v[1:] + [turned(v[0], -SLOT)]
 
     eta_row = [2.0 * (e + row_next(e)) for e in eta]
+    eta_row_prev = [row_prev(e) for e in eta_row]
     eta_col = [0.5 * (e + col_next(e)) for e in eta]
     eta_half = [0.5 * e for e in eta]
     eta_up = [e + n for e, n in zip(eta, after(eta))]
@@ -425,7 +418,8 @@
         result = ([], [])
         odd = even = jnp.zeros((ROWS, LANES), jnp.float32)
         for n in range(tiles):
-            outs = horizontal(field[0][n], field[1][n], eta_row[n], eta_col[n], eta_half[n], Turns)
+            coefficients = (eta_row[n], eta_row_prev[n], eta_col[n], eta_half[n])
+            outs = horizontal(field[0][n], field[1][n], *coefficients, Turns)
             for c in range(2):
                 below = ups[c][n - 1] if n else turned(ups[c][-1], SLOT) - drag * field[c][0]
                 out = cover * (outs[c] + (ups[c][n] - below))
@@ -535,13 +529,14 @@
     return powers
 
 
-def final_kernel(rhs, powers, edges, friction, ice, grounded, speed, *rest):
-    *parts, iterate_out, residual_out, hessian, iterate, residual, gone = rest
+def final_kernel(rhs, power_1, power_2, power_3, power_4, edges, friction, ice, grounded, speed, *rest):
+    *parts, iterate, residual, hessian = rest
     layers, tiles = rhs.shape[1], edges.shape[2]
     total = (parts[0][0], parts[0][1])
     for x in parts[1:]:
         total = join(total, (x[0], x[1]))
     factors = solve(total)
+    powers = (power_1, power_2, power_3, power_4)
     wide = [jnp.concatenate([c, c], 1) for c in factors]
     rest = sum(wide[1:], wide[0])
     cover = ice[...].astype(jnp.float32)
@@ -556,31 +551,26 @@
             y = y + weights[t] * vectors[t]
         return x, y
 
-    piece = layers // PIECES
-    copies = []
     for c in range(2):
         side = [combined([edges[t, c, n] for t in range(STEPS)], factors) for n in range(tiles)]
         for k in range(layers):
             at = k // tiles * SLOT
-            inner = combined([powers[t, c, k] for t in range(STEPS)], wide)
+            halves = [
+                combined([p[half, c, k, FIRST + HALO : FIRST + HALO + ROWS] for p in powers], factors)
+                for half in (0, 1)
+            ]
+            inner = zip(*halves)
             patched = []
-            for v, e in zip(inner, side[k % tiles]):
-                head = jnp.where(lane < HALO, turned(e, -at - 20), v[:, :LANES])
-                tail = jnp.where(lane >= LANES - HALO, turned(e, 120 - at), v[:, LANES:])
+            for (head, tail), e in zip(inner, side[k % tiles]):
+                head = jnp.where(lane < HALO, turned(e, -at - 20), head)
+                tail = jnp.where(lane >= LANES - HALO, turned(e, 120 - at), tail)
                 patched.append(jnp.concatenate([head, tail], 1))
             r = rhs[c, k]
             x, y = patched
             iterate[c, k] = jnp.where(cover > 0.0, wide[0] * r + x, rest * r)
             residual[c, k] = r - jnp.where(cover > 0.0, y, rest * r)
-            if (k + 1) % piece == 0:
-                for i, (src, dst) in enumerate(((iterate, iterate_out), (residual, residual_out))):
-                    part = (c, pl.ds(k + 1 - piece, piece))
-                    copies.append(pltpu.make_async_copy(src.at[part], dst.at[part], gone.at[len(copies)]))
-                    copies[-1].start()
     weight = cover * (friction[...] * grounded[...].astype(jnp.float32))
     hessian[...] = weight * (speed[0] * iterate[0, 0] + speed[1] * iterate[1, 0])
-    for copy in copies:
-        copy.wait()
 
 
 def exchange(x, axis):
@@ -623,11 +613,11 @@
     beside = ("gy", "gz")
     (columns,) = call(beside_kernel, [both])(swapped(column_a, beside, 0), swapped(column_b, beside, 1))
     columns_a, columns_b = swapped(columns, "gx", 0), swapped(columns, "gx", 1)
-    block = (layers, 2 * ROWS, 2 * LANES)
-    powers, sums, ribbon = call(
+    block = (layers, 3 * ROWS, LANES)
+    *powers, sums, ribbon = call(
         main_kernel,
-        [(STEPS,) + adjoint_rhs.shape, (2 * STEPS + 1, ROWS, 2 * LANES), (ribbons, 2 * ROWS, LANES)],
-        [(2,) + block] * 2 + [block] * 4 + [block[1:]] * 2,
+        [(2, 2) + block] * STEPS + [(2 * STEPS + 1, ROWS, 2 * LANES), (ribbons, 2 * ROWS, LANES)],
+        [(2, 2) + block] + [(2,) + block] * 4 + [(2,) + block[1:]] * 2,
         cost_estimate=pl.CostEstimate(flops=200_000_000, bytes_accessed=8_000_000, transcendentals=0),
     )(*held[:5], strip_a, strip_b)
     edges, sums = call(
@@ -640,13 +630,8 @@
     parts = exchange(sums, "gx")
     rhs, _, friction, ice_mask, grounded, speed = held
     return tuple(
-        call(
-            final_kernel,
-            [adjoint_rhs.shape, adjoint_rhs.shape, friction.shape],
-            [adjoint_rhs.shape] * 2 + [pltpu.SemaphoreType.DMA((4 * PIECES,))],
-            out_specs=[pl.BlockSpec(memory_space=pltpu.HBM)] * 2 + [pl.BlockSpec(memory_space=pltpu.VMEM)],
-        )(
-            rhs, powers, edges, friction, ice_mask, grounded, speed, *parts
+        call(final_kernel, [adjoint_rhs.shape, adjoint_rhs.shape, friction.shape])(
+            rhs, *powers, edges, friction, ice_mask, grounded, speed, *parts
         )
     )
 

time: 36.6 us -> 37.1 us (1.014)
  Pallas kernels: 8.68 us -> 9.13 us
    pallas_call x2, Pallas kernels: 6.56 us -> 7.02 us  [the longest x1 5.19 us: body(): call(main_kernel, [(2, 2) + block] * STEPS + [(2 * STEPS + 1, ROWS, 2 * L...]
  transfers between devices with their start and end apart: 12 -> 12, of which waited for: 5 -> 5; matrix products, arithmetic and copies ran while one was open for 0% -> 0% of each run, Pallas kernels for 12% -> 14%
where the time goes in v11:
time: 37.1 us; the launch traced here: 36.9 us
  starting transfers between devices  19.1 us (51%)
  Pallas kernels  9.13 us (25%)
  waiting for transfers between devices  7.94 us (21%)
  between operations  0.73 us (2%)
    ppermute x6, starting transfers between devices, swapped(): return lax.ppermute(x, axis, pairs)  9.59 us
    ppermute x6, starting transfers between devices, exchange(): parts.append(lax.ppermute(x, axis, pairs))  9.47 us
    ppermute x6, waiting for transfers between devices, exchange(): parts.append(lax.ppermute(x, axis, pairs))  7.43 us
    pallas_call x1, Pallas kernels, body(): call(main_kernel, [(2, 2) + block] * STEPS + [(2 * STEPS + 1, ROWS, 2 * L...  5.19 us
    pallas_call x1, Pallas kernels, body(): call(final_kernel, [adjoint_rhs.shape, adjoint_rhs.shape, friction.shape])  1.82 us
    pallas_call x1, Pallas kernels, body(): call(pack_kernel, [jax.ShapeDtypeStruct(x.shape, x.dtype) for x in inputs...  1.35 us
  transfers between devices with their start and end apart: 12, of which 5 were waited for; matrix products, arithmetic and copies ran while one was open for 0% of the time, Pallas kernels for 14%

profile of v11, /device:TPU:0, one launch (start us, length us, event | category | flops | bytes accessed | tf_op | source)
XLA Modules:
  0.0 36.9 jit_solution(16314654231544011280)
XLA Ops:
  0.6 1.3 %shard_map.85 = (f32[2,20,8,256]{3,2,1,0:T(8,128)S(1)}, f32[20,8,256]{2,1,0:T(8,128)S(1)}, f32[8,256]{1,0:T(8,128)S(1)}, s32[8,256]{1,0:T(8,128)S(1)}, s32[8,256...) custom-call(f32[2,20,8,256]{3,2,1,0:T(8,128)} %refs_0_.1, ...), custom_call_target="tpu_custom_call" | custom-call | tf_op jit(solution)/shard_map/pallas_call | solution.py:606
  2.0 3.1 %collective-permute-start = (f32[62,8,128]{2,1,0:T(8,128)S(1)}, f32[62,8,128]{2,1,0:T(8,128)S(1)}, u32[]{:S(2)}, u32[]{:S(2)}) collective-permute-start(f32[62,8,128]{2,1,0:T(8,128)S(1)} %get-tuple-element.26), channel_id=1, source_target_pairs={{0,4},{4,0},{8,12},{12,8},{1,5},{5,1},{9,13},{13,9},{2,6},{6,2},{1... | collective-permute-start | bytes 761864 | tf_op jit(solution)/shard_map/ppermute | solution.py:43
  5.1 0.7 %collective-permute-start.1 = (f32[62,8,128]{2,1,0:T(8,128)S(1)}, f32[62,8,128]{2,1,0:T(8,128)S(1)}, u32[]{:S(2)}, u32[]{:S(2)}) collective-permute-start(f32[62,8,128]{2,1,0:T(8,128)S(1)} %get-tuple-element.27), channel_id=1, source_target_pairs={{0,0},{4,8},{8,4},{12,12},{1,1},{5,9},{9,5},{13,13},{2,2},{6,10},{... | collective-permute-start | bytes 761864 | tf_op jit(solution)/shard_map/ppermute | solution.py:43
  5.8 0.1 collective-permute-start.2
  5.8 0.7 %collective-permute-start.3 = (f32[3,8,128]{2,1,0:T(8,128)S(1)}, f32[3,8,128]{2,1,0:T(8,128)S(1)}, u32[]{:S(2)}, u32[]{:S(2)}) collective-permute-start(f32[3,8,128]{2,1,0:T(8,128)S(1)} %get-tuple-element.34), channel_id=1, source_target_pairs={{0,0},{1,2},{2,1},{3,3},{4,4},{5,6},{6,5},{7,7},{8,8},{9,10},{10,9... | collective-permute-start | bytes 36872 | tf_op jit(solution)/shard_map/ppermute | solution.py:43
  6.5 0.5 %collective-permute-done.2.from_a = f32[3,8,128]{2,1,0:T(8,128)S(1)} collective-permute-done((f32[3,8,128]{2,1,0:T(8,128)S(1)}, f32[3,8,128]{2,1,0:T(8,128)S(1)}, u32[]{:S(2)}, u32[]{:S(2)}) %collective-permute-start.2) | collective-permute-done | bytes 12320 | tf_op jit(solution)/shard_map/ppermute | solution.py:43
  7.0 0.0 collective-permute-done.3.from_b
  7.0 4.4 %collective-permute-start.4 = (f32[6,8,128]{2,1,0:T(8,128)S(1)}, f32[6,8,128]{2,1,0:T(8,128)S(1)}, u32[]{:S(2)}, u32[]{:S(2)}) collective-permute-start(f32[6,8,128]{2,1,0:T(8,128)S(1)} %shard_map.87.columns), channel_id=1, source_target_pairs={{0,4},{4,0},{8,12},{12,8},{1,5},{5,1},{9,13},{13,9},{2,6},{6,2},{1... | collective-permute-start | bytes 73736 | tf_op jit(solution)/shard_map/ppermute | solution.py:43
  11.5 0.7 %collective-permute-start.5 = (f32[6,8,128]{2,1,0:T(8,128)S(1)}, f32[6,8,128]{2,1,0:T(8,128)S(1)}, u32[]{:S(2)}, u32[]{:S(2)}) collective-permute-start(f32[6,8,128]{2,1,0:T(8,128)S(1)} %shard_map.87.columns), channel_id=1, source_target_pairs={{0,0},{4,8},{8,4},{12,12},{1,1},{5,9},{9,5},{13,13},{2,2},{6,10},{... | collective-permute-start | bytes 73736 | tf_op jit(solution)/shard_map/ppermute | solution.py:43
  12.1 0.0 collective-permute-done.strip_a
  12.1 5.2 %shard_map.86 = (f32[2,2,20,24,128]{4,3,2,1,0:T(8,128)S(1)}, f32[2,2,20,24,128]{4,3,2,1,0:T(8,128)S(1)}, f32[2,2,20,24,128]{4,3,2,1,0:T(8,128)S(1)}, f32[2,2,20,...) custom-call(f32[2,20,8,256]{3,2,1,0:T(8,128)S(1)} %get-tuple-element.21.rhs, ...), custom_call_target="tpu_custom_call" | custom-call | flops 200000000 | bytes 8000000 | tf_op jit(solution)/shard_map/pallas_call | solution.py:617
  17.3 0.0 collective-permute-done.4.columns_a
  17.4 0.7 %shard_map.88 = (f32[4,2,5,8,128]{4,3,2,1,0:T(8,128)S(1)}, f32[2,16,128]{2,1,0:T(8,128)S(1)}) custom-call(f32[17,16,128]{2,1,0:T(8,128)S(1)} %get-tuple-element.32.ribbon, f32[6,8,128]{2,1,0:T(8,128)S(1)} %shard_map.87.columns, f32[6,8,128]{2,1,0:T(8,128)S(1)} %collective-permute-done.4.columns_a, f32[6,8,128]{2,1,0:T(8,128)S(1)} %collective-permute-done.5.columns_b, ...), custom_call_target="tpu_custom_call" | custom-call | tf_op jit(solution)/shard_map/pallas_call | solution.py:623
  18.1 4.3 %collective-permute-start.6 = (f32[2,16,128]{2,1,0:T(8,128)S(1)}, f32[2,16,128]{2,1,0:T(8,128)S(1)}, u32[]{:S(2)}, u32[]{:S(2)}) collective-permute-start(f32[2,16,128]{2,1,0:T(8,128)S(1)} %get-tuple-element.38.refs_0_), channel_id=1, source_target_pairs={{0,1},{1,0},{2,3},{3,2},{4,5},{5,4},{6,7},{7,6},{8,9},{9,8},{10,11... | collective-permute-start | bytes 49160 | tf_op jit(solution)/shard_map/ppermute | solution.py:591
  22.4 1.1 %collective-permute-start.7 = (f32[2,16,128]{2,1,0:T(8,128)S(1)}, f32[2,16,128]{2,1,0:T(8,128)S(1)}, u32[]{:S(2)}, u32[]{:S(2)}) collective-permute-start(f32[2,16,128]{2,1,0:T(8,128)S(1)} %get-tuple-element.38.refs_0_), channel_id=1, source_target_pairs={{0,2},{1,3},{2,0},{3,1},{4,6},{5,7},{6,4},{7,5},{8,10},{9,11},{10,... | collective-permute-start | bytes 49160 | tf_op jit(solution)/shard_map/ppermute | solution.py:591
  23.5 0.4 collective-permute-start.8
  23.9 0.0 collective-permute-done.6.refs_1_
  23.9 2.3 %collective-permute-done.7.refs_2_ = f32[2,16,128]{2,1,0:T(8,128)S(1)} collective-permute-done((f32[2,16,128]{2,1,0:T(8,128)S(1)}, f32[2,16,128]{2,1,0:T(8,128)S(1)}, u32[]{:S(2)}, u32[]{:S(2)}) %collective-permute-start.7) | collective-permute-done | bytes 16416 | tf_op jit(solution)/shard_map/ppermute | solution.py:591
  26.2 0.5 %collective-permute-done.8.refs_3_ = f32[2,16,128]{2,1,0:T(8,128)S(1)} collective-permute-done((f32[2,16,128]{2,1,0:T(8,128)S(1)}, f32[2,16,128]{2,1,0:T(8,128)S(1)}, u32[]{:S(2)}, u32[]{:S(2)}) %collective-permute-start.8) | collective-permute-done | bytes 16416 | tf_op jit(solution)/shard_map/ppermute | solution.py:591
  26.7 2.8 %collective-permute-start.10 = (f32[2,16,128]{2,1,0:T(8,128)S(1)}, f32[2,16,128]{2,1,0:T(8,128)S(1)}, u32[]{:S(2)}, u32[]{:S(2)}) collective-permute-start(f32[2,16,128]{2,1,0:T(8,128)S(1)} %shard_map.89.rest_0_), channel_id=1, source_target_pairs={{0,8},{4,12},{8,0},{12,4},{1,9},{5,13},{9,1},{13,5},{2,10},{6,14},... | collective-permute-start | bytes 49160 | tf_op jit(solution)/shard_map/ppermute | solution.py:591
  29.5 0.9 %collective-permute-start.11 = (f32[2,16,128]{2,1,0:T(8,128)S(1)}, f32[2,16,128]{2,1,0:T(8,128)S(1)}, u32[]{:S(2)}, u32[]{:S(2)}) collective-permute-start(f32[2,16,128]{2,1,0:T(8,128)S(1)} %shard_map.89.rest_0_), channel_id=1, source_target_pairs={{0,12},{4,8},{8,4},{12,0},{1,13},{5,9},{9,5},{13,1},{2,14},{6,10},... | collective-permute-start | bytes 49160 | tf_op jit(solution)/shard_map/ppermute | solution.py:591
  30.4 1.1 %collective-permute-done.10.rest_2_ = f32[2,16,128]{2,1,0:T(8,128)S(1)} collective-permute-done((f32[2,16,128]{2,1,0:T(8,128)S(1)}, f32[2,16,128]{2,1,0:T(8,128)S(1)}, u32[]{:S(2)}, u32[]{:S(2)}) %collective-permute-start.10) | collective-permute-done | bytes 16416 | tf_op jit(solution)/shard_map/ppermute | solution.py:591
  31.5 3.5 %collective-permute-done.11.rest_3_ = f32[2,16,128]{2,1,0:T(8,128)S(1)} collective-permute-done((f32[2,16,128]{2,1,0:T(8,128)S(1)}, f32[2,16,128]{2,1,0:T(8,128)S(1)}, u32[]{:S(2)}, u32[]{:S(2)}) %collective-permute-start.11) | collective-permute-done | bytes 16416 | tf_op jit(solution)/shard_map/ppermute | solution.py:591
  35.0 1.8 %shard_map.90 = (f32[2,20,8,256]{3,2,1,0:T(8,128)}, f32[2,20,8,256]{3,2,1,0:T(8,128)}, f32[8,256]{1,0:T(8,128)}) custom-call(f32[2,20,8,256]{3,2,1,0:T(8,128)S(1)} %get-tuple-element.21.rhs, f32[2,2,20,24,128]{4,3,2,1,0:T(8,128)S(1)} %get-tuple-element.28.power_1, f32[2,2,20,24,128]{4,3,2,1,0:T(8,128)S(1)} %get-tuple-element.29.power_2, ...), custom_call_target="tpu_custom_call" | custom-call | tf_op jit(solution)/shard_map/pallas_call | solution.py:633
  (6 shorter events, 0.0 us)
Async XLA Ops:
  2.0 10.1 %collective-permute-start = (f32[62,8,128]{2,1,0:T(8,128)S(1)}, f32[62,8,128]{2,1,0:T(8,128)S(1)}, u32[]{:S(2)}, u32[]{:S(2)}) collective-permute-start(f32[62,8,128]{2,1,0:T(8,128)S(1)} %get-tuple-element.26), channel_id=1, source_target_pairs={{0,4},{4,0},{8,12},{12,8},{1,5},{5,1},{9,13},{13,9},{2,6},{6,2},{1... | collective-permute-start | bytes 761864 | tf_op jit(solution)/shard_map/ppermute | solution.py:43
  5.1 7.0 %collective-permute-start.1 = (f32[62,8,128]{2,1,0:T(8,128)S(1)}, f32[62,8,128]{2,1,0:T(8,128)S(1)}, u32[]{:S(2)}, u32[]{:S(2)}) collective-permute-start(f32[62,8,128]{2,1,0:T(8,128)S(1)} %get-tuple-element.27), channel_id=1, source_target_pairs={{0,0},{4,8},{8,4},{12,12},{1,1},{5,9},{9,5},{13,13},{2,2},{6,10},{... | collective-permute-start | bytes 761864 | tf_op jit(solution)/shard_map/ppermute | solution.py:43
  5.8 1.2 %collective-permute-start.2 = (f32[3,8,128]{2,1,0:T(8,128)S(1)}, f32[3,8,128]{2,1,0:T(8,128)S(1)}, u32[]{:S(2)}, u32[]{:S(2)}) collective-permute-start(f32[3,8,128]{2,1,0:T(8,128)S(1)} %get-tuple-element.33), channel_id=1, source_target_pairs={{0,1},{1,0},{2,3},{3,2},{4,5},{5,4},{6,7},{7,6},{8,9},{9,8},{10,11... | collective-permute-start | bytes 36872 | tf_op jit(solution)/shard_map/ppermute | solution.py:43
  5.8 1.2 %collective-permute-start.3 = (f32[3,8,128]{2,1,0:T(8,128)S(1)}, f32[3,8,128]{2,1,0:T(8,128)S(1)}, u32[]{:S(2)}, u32[]{:S(2)}) collective-permute-start(f32[3,8,128]{2,1,0:T(8,128)S(1)} %get-tuple-element.34), channel_id=1, source_target_pairs={{0,0},{1,2},{2,1},{3,3},{4,4},{5,6},{6,5},{7,7},{8,8},{9,10},{10,9... | collective-permute-start | bytes 36872 | tf_op jit(solution)/shard_map/ppermute | solution.py:43
  7.0 10.3 %collective-permute-start.4 = (f32[6,8,128]{2,1,0:T(8,128)S(1)}, f32[6,8,128]{2,1,0:T(8,128)S(1)}, u32[]{:S(2)}, u32[]{:S(2)}) collective-permute-start(f32[6,8,128]{2,1,0:T(8,128)S(1)} %shard_map.87.columns), channel_id=1, source_target_pairs={{0,4},{4,0},{8,12},{12,8},{1,5},{5,1},{9,13},{13,9},{2,6},{6,2},{1... | collective-permute-start | bytes 73736 | tf_op jit(solution)/shard_map/ppermute | solution.py:43
  11.5 5.9 %collective-permute-start.5 = (f32[6,8,128]{2,1,0:T(8,128)S(1)}, f32[6,8,128]{2,1,0:T(8,128)S(1)}, u32[]{:S(2)}, u32[]{:S(2)}) collective-permute-start(f32[6,8,128]{2,1,0:T(8,128)S(1)} %shard_map.87.columns), channel_id=1, source_target_pairs={{0,0},{4,8},{8,4},{12,12},{1,1},{5,9},{9,5},{13,13},{2,2},{6,10},{... | collective-permute-start | bytes 73736 | tf_op jit(solution)/shard_map/ppermute | solution.py:43
  18.1 5.8 %collective-permute-start.6 = (f32[2,16,128]{2,1,0:T(8,128)S(1)}, f32[2,16,128]{2,1,0:T(8,128)S(1)}, u32[]{:S(2)}, u32[]{:S(2)}) collective-permute-start(f32[2,16,128]{2,1,0:T(8,128)S(1)} %get-tuple-element.38.refs_0_), channel_id=1, source_target_pairs={{0,1},{1,0},{2,3},{3,2},{4,5},{5,4},{6,7},{7,6},{8,9},{9,8},{10,11... | collective-permute-start | bytes 49160 | tf_op jit(solution)/shard_map/ppermute | solution.py:591
  22.4 3.7 %collective-permute-start.7 = (f32[2,16,128]{2,1,0:T(8,128)S(1)}, f32[2,16,128]{2,1,0:T(8,128)S(1)}, u32[]{:S(2)}, u32[]{:S(2)}) collective-permute-start(f32[2,16,128]{2,1,0:T(8,128)S(1)} %get-tuple-element.38.refs_0_), channel_id=1, source_target_pairs={{0,2},{1,3},{2,0},{3,1},{4,6},{5,7},{6,4},{7,5},{8,10},{9,11},{10,... | collective-permute-start | bytes 49160 | tf_op jit(solution)/shard_map/ppermute | solution.py:591
  23.5 3.2 %collective-permute-start.8 = (f32[2,16,128]{2,1,0:T(8,128)S(1)}, f32[2,16,128]{2,1,0:T(8,128)S(1)}, u32[]{:S(2)}, u32[]{:S(2)}) collective-permute-start(f32[2,16,128]{2,1,0:T(8,128)S(1)} %get-tuple-element.38.refs_0_), channel_id=1, source_target_pairs={{0,3},{1,2},{2,1},{3,0},{4,7},{5,6},{6,5},{7,4},{8,11},{9,10},{10,... | collective-permute-start | bytes 49160 | tf_op jit(solution)/shard_map/ppermute | solution.py:591
  26.7 4.8 %collective-permute-start.10 = (f32[2,16,128]{2,1,0:T(8,128)S(1)}, f32[2,16,128]{2,1,0:T(8,128)S(1)}, u32[]{:S(2)}, u32[]{:S(2)}) collective-permute-start(f32[2,16,128]{2,1,0:T(8,128)S(1)} %shard_map.89.rest_0_), channel_id=1, source_target_pairs={{0,8},{4,12},{8,0},{12,4},{1,9},{5,13},{9,1},{13,5},{2,10},{6,14},... | collective-permute-start | bytes 49160 | tf_op jit(solution)/shard_map/ppermute | solution.py:591
  29.5 5.5 %collective-permute-start.11 = (f32[2,16,128]{2,1,0:T(8,128)S(1)}, f32[2,16,128]{2,1,0:T(8,128)S(1)}, u32[]{:S(2)}, u32[]{:S(2)}) collective-permute-start(f32[2,16,128]{2,1,0:T(8,128)S(1)} %shard_map.89.rest_0_), channel_id=1, source_target_pairs={{0,12},{4,8},{8,4},{12,0},{1,13},{5,9},{9,5},{13,1},{2,14},{6,10},... | collective-permute-start | bytes 49160 | tf_op jit(solution)/shard_map/ppermute | solution.py:591
  30.4 4.6 %collective-permute-start.9 = (f32[2,16,128]{2,1,0:T(8,128)S(1)}, f32[2,16,128]{2,1,0:T(8,128)S(1)}, u32[]{:S(2)}, u32[]{:S(2)}) collective-permute-start(f32[2,16,128]{2,1,0:T(8,128)S(1)} %shard_map.89.rest_0_), channel_id=1, source_target_pairs={{0,4},{4,0},{8,12},{12,8},{1,5},{5,1},{9,13},{13,9},{2,6},{6,2},{1... | collective-permute-start | bytes 49160 | tf_op jit(solution)/shard_map/ppermute | solution.py:591

commit v12 on v10

--- a/solution.py
+++ b/solution.py
@@ -12,7 +12,6 @@
 ROWS = 8
 LANES = 128
 UNROLL = 5
-PIECES = 2
 SLOT = 32
 
 
@@ -286,7 +285,7 @@
 
 
 def main_kernel(
-    rhs, eta, friction, ice, grounded, strip_a, strip_b,
+    rhs, eta, friction, ice, grounded, strip_b, strip_a,
     powers, sums, ribbon,
     field_a, field_b, eta_row, eta_col, eta_half, eta_up, cover, drag,
 ):
@@ -536,7 +535,7 @@
 
 
 def final_kernel(rhs, powers, edges, friction, ice, grounded, speed, *rest):
-    *parts, iterate_out, residual_out, hessian, iterate, residual, gone = rest
+    *parts, iterate, residual, hessian = rest
     layers, tiles = rhs.shape[1], edges.shape[2]
     total = (parts[0][0], parts[0][1])
     for x in parts[1:]:
@@ -556,8 +555,6 @@
             y = y + weights[t] * vectors[t]
         return x, y
 
-    piece = layers // PIECES
-    copies = []
     for c in range(2):
         side = [combined([edges[t, c, n] for t in range(STEPS)], factors) for n in range(tiles)]
         for k in range(layers):
@@ -572,15 +569,8 @@
             x, y = patched
             iterate[c, k] = jnp.where(cover > 0.0, wide[0] * r + x, rest * r)
             residual[c, k] = r - jnp.where(cover > 0.0, y, rest * r)
-            if (k + 1) % piece == 0:
-                for i, (src, dst) in enumerate(((iterate, iterate_out), (residual, residual_out))):
-                    part = (c, pl.ds(k + 1 - piece, piece))
-                    copies.append(pltpu.make_async_copy(src.at[part], dst.at[part], gone.at[len(copies)]))
-                    copies[-1].start()
     weight = cover * (friction[...] * grounded[...].astype(jnp.float32))
     hessian[...] = weight * (speed[0] * iterate[0, 0] + speed[1] * iterate[1, 0])
-    for copy in copies:
-        copy.wait()
 
 
 def exchange(x, axis):
@@ -619,7 +609,7 @@
         [pltpu.SemaphoreType.DMA((len(inputs),))],
         in_specs=[pl.BlockSpec(memory_space=pltpu.HBM)] * len(inputs),
     )(*[pltpu.with_memory_space_constraint(x, pltpu.HBM) for x in inputs])
-    strip_a, strip_b = swapped(strip_a, "gx", 0), swapped(strip_b, "gx", 1)
+    strip_b, strip_a = swapped(strip_b, "gx", 1), swapped(strip_a, "gx", 0)
     beside = ("gy", "gz")
     (columns,) = call(beside_kernel, [both])(swapped(column_a, beside, 0), swapped(column_b, beside, 1))
     columns_a, columns_b = swapped(columns, "gx", 0), swapped(columns, "gx", 1)
@@ -629,7 +619,7 @@
         [(STEPS,) + adjoint_rhs.shape, (2 * STEPS + 1, ROWS, 2 * LANES), (ribbons, 2 * ROWS, LANES)],
         [(2,) + block] * 2 + [block] * 4 + [block[1:]] * 2,
         cost_estimate=pl.CostEstimate(flops=200_000_000, bytes_accessed=8_000_000, transcendentals=0),
-    )(*held[:5], strip_a, strip_b)
+    )(*held[:5], strip_b, strip_a)
     edges, sums = call(
         ribbon_kernel,
         [(STEPS, 2, layers // 4) + tile, (2, 2 * ROWS, LANES)],
@@ -640,12 +630,7 @@
     parts = exchange(sums, "gx")
     rhs, _, friction, ice_mask, grounded, speed = held
     return tuple(
-        call(
-            final_kernel,
-            [adjoint_rhs.shape, adjoint_rhs.shape, friction.shape],
-            [adjoint_rhs.shape] * 2 + [pltpu.SemaphoreType.DMA((4 * PIECES,))],
-            out_specs=[pl.BlockSpec(memory_space=pltpu.HBM)] * 2 + [pl.BlockSpec(memory_space=pltpu.VMEM)],
-        )(
+        call(final_kernel, [adjoint_rhs.shape, adjoint_rhs.shape, friction.shape])(
             rhs, powers, edges, friction, ice_mask, grounded, speed, *parts
         )
     )

time: 36.6 us -> 36.4 us (level)
  waiting for transfers between devices: 7.94 us -> 11.5 us
  starting transfers between devices: 19.1 us -> 15.9 us
  Pallas kernels: 8.68 us -> 8.12 us
    ppermute x6, waiting for transfers between devices: 0.51 us -> 4.37 us  [swapped(): return lax.ppermute(x, axis, pairs)]
    ppermute x6, starting transfers between devices: 9.48 us -> 7.88 us  [exchange(): parts.append(lax.ppermute(x, axis, pairs))]
    ppermute x6, starting transfers between devices: 9.59 us -> 8.02 us  [swapped(): return lax.ppermute(x, axis, pairs)]
    pallas_call x1, Pallas kernels: 2.37 us -> 1.81 us  [body(): call(final_kernel, [adjoint_rhs.shape, adjoint_rhs.shape, friction.shape])]
  transfers between devices with their start and end apart: 12 -> 12, of which waited for: 5 -> 6; matrix products, arithmetic and copies ran while one was open for 0% -> 0% of each run, Pallas kernels for 12% -> 12%
where the time goes in v12:
time: 36.4 us; the launch traced here: 36.2 us
  starting transfers between devices  15.9 us (44%)
  waiting for transfers between devices  11.5 us (32%)
  Pallas kernels  8.12 us (22%)
  between operations  0.72 us (2%)
    ppermute x6, starting transfers between devices, swapped(): return lax.ppermute(x, axis, pairs)  8.02 us
    ppermute x6, starting transfers between devices, exchange(): parts.append(lax.ppermute(x, axis, pairs))  7.88 us
    ppermute x6, waiting for transfers between devices, exchange(): parts.append(lax.ppermute(x, axis, pairs))  7.09 us
    ppermute x6, waiting for transfers between devices, swapped(): return lax.ppermute(x, axis, pairs)  4.37 us
    pallas_call x1, Pallas kernels, body(): call(main_kernel, [(STEPS,) + adjoint_rhs.shape, (2 * STEPS + 1, ROWS, 2...  4.19 us
    pallas_call x1, Pallas kernels, body(): call(final_kernel, [adjoint_rhs.shape, adjoint_rhs.shape, friction.shape])  1.81 us
    pallas_call x1, Pallas kernels, body(): call(pack_kernel, [jax.ShapeDtypeStruct(x.shape, x.dtype) for x in inputs...  1.35 us
    pallas_call x1, Pallas kernels, body(): call(ribbon_kernel, [(STEPS, 2, layers // 4) + tile, (2, 2 * ROWS, LANES)])  0.74 us
  transfers between devices with their start and end apart: 12, of which 6 were waited for; matrix products, arithmetic and copies ran while one was open for 0% of the time, Pallas kernels for 12%

profile of v12, /device:TPU:0, one launch (start us, length us, event | category | flops | bytes accessed | tf_op | source)
XLA Modules:
  0.0 36.2 jit_solution(5859166316858030117)
XLA Ops:
  0.6 1.3 %shard_map.85 = (f32[2,20,8,256]{3,2,1,0:T(8,128)S(1)}, f32[20,8,256]{2,1,0:T(8,128)S(1)}, f32[8,256]{1,0:T(8,128)S(1)}, s32[8,256]{1,0:T(8,128)S(1)}, s32[8,256...) custom-call(f32[2,20,8,256]{3,2,1,0:T(8,128)} %refs_0_.1, ...), custom_call_target="tpu_custom_call" | custom-call | tf_op jit(solution)/shard_map/pallas_call | solution.py:606
  2.0 0.7 %collective-permute-start = (f32[62,8,128]{2,1,0:T(8,128)S(1)}, f32[62,8,128]{2,1,0:T(8,128)S(1)}, u32[]{:S(2)}, u32[]{:S(2)}) collective-permute-start(f32[62,8,128]{2,1,0:T(8,128)S(1)} %get-tuple-element.23), channel_id=1, source_target_pairs={{0,0},{4,8},{8,4},{12,12},{1,1},{5,9},{9,5},{13,13},{2,2},{6,10},{... | collective-permute-start | bytes 761864 | tf_op jit(solution)/shard_map/ppermute | solution.py:42
  2.7 5.9 %collective-permute-start.1 = (f32[62,8,128]{2,1,0:T(8,128)S(1)}, f32[62,8,128]{2,1,0:T(8,128)S(1)}, u32[]{:S(2)}, u32[]{:S(2)}) collective-permute-start(f32[62,8,128]{2,1,0:T(8,128)S(1)} %get-tuple-element.24), channel_id=1, source_target_pairs={{0,4},{4,0},{8,12},{12,8},{1,5},{5,1},{9,13},{13,9},{2,6},{6,2},{1... | collective-permute-start | bytes 761864 | tf_op jit(solution)/shard_map/ppermute | solution.py:42
  8.6 0.0 collective-permute-start.2
  8.6 0.7 %collective-permute-start.3 = (f32[3,8,128]{2,1,0:T(8,128)S(1)}, f32[3,8,128]{2,1,0:T(8,128)S(1)}, u32[]{:S(2)}, u32[]{:S(2)}) collective-permute-start(f32[3,8,128]{2,1,0:T(8,128)S(1)} %get-tuple-element.28), channel_id=1, source_target_pairs={{0,0},{1,2},{2,1},{3,3},{4,4},{5,6},{6,5},{7,7},{8,8},{9,10},{10,9... | collective-permute-start | bytes 36872 | tf_op jit(solution)/shard_map/ppermute | solution.py:42
  9.2 0.5 %collective-permute-done.2.from_a = f32[3,8,128]{2,1,0:T(8,128)S(1)} collective-permute-done((f32[3,8,128]{2,1,0:T(8,128)S(1)}, f32[3,8,128]{2,1,0:T(8,128)S(1)}, u32[]{:S(2)}, u32[]{:S(2)}) %collective-permute-start.2) | collective-permute-done | bytes 12320 | tf_op jit(solution)/shard_map/ppermute | solution.py:42
  9.7 0.0 collective-permute-done.3.from_b
  9.8 0.1 collective-permute-start.4
  9.9 0.7 %collective-permute-start.5 = (f32[6,8,128]{2,1,0:T(8,128)S(1)}, f32[6,8,128]{2,1,0:T(8,128)S(1)}, u32[]{:S(2)}, u32[]{:S(2)}) collective-permute-start(f32[6,8,128]{2,1,0:T(8,128)S(1)} %shard_map.87.columns), channel_id=1, source_target_pairs={{0,0},{4,8},{8,4},{12,12},{1,1},{5,9},{9,5},{13,13},{2,2},{6,10},{... | collective-permute-start | bytes 73736 | tf_op jit(solution)/shard_map/ppermute | solution.py:42
  10.6 3.8 %collective-permute-done.1.strip_a = f32[62,8,128]{2,1,0:T(8,128)S(1)} collective-permute-done((f32[62,8,128]{2,1,0:T(8,128)S(1)}, f32[62,8,128]{2,1,0:T(8,128)S(1)}, u32[]{:S(2)}, u32[]{:S(2)}) %collective-permute-start.1) | collective-permute-done | bytes 253984 | tf_op jit(solution)/shard_map/ppermute | solution.py:42
  14.4 4.2 %shard_map.86 = (f32[4,2,20,8,256]{4,3,2,1,0:T(8,128)S(1)}, f32[9,8,256]{2,1,0:T(8,128)S(1)}, f32[17,16,128]{2,1,0:T(8,128)S(1)}) custom-call(f32[2,20,8,256]{3,2,1,0:T(8,128)S(1)} %get-tuple-element.18.rhs, f32[20,8,256]{2,1,0:T(8,128)S(1)} %get-tuple-element.19.eta, f32[8,256]{1,0:T(8,128)S(1)} %get-tuple-element.20.friction, ...), custom_call_target="tpu_custom_call" | custom-call | flops 200000000 | bytes 8000000 | tf_op jit(solution)/shard_map/pallas_call | solution.py:617
  18.6 0.0 collective-permute-done.4.columns_a
  18.6 0.0 collective-permute-done.5.columns_b
  18.6 0.7 %shard_map.88 = (f32[4,2,5,8,128]{4,3,2,1,0:T(8,128)S(1)}, f32[2,16,128]{2,1,0:T(8,128)S(1)}) custom-call(f32[17,16,128]{2,1,0:T(8,128)S(1)} %get-tuple-element.26.ribbon, f32[6,8,128]{2,1,0:T(8,128)S(1)} %shard_map.87.columns, f32[6,8,128]{2,1,0:T(8,128)S(1)} %collective-permute-done.4.columns_a, f32[6,8,128]{2,1,0:T(8,128)S(1)} %collective-permute-done.5.columns_b, ...), custom_call_target="tpu_custom_call" | custom-call | tf_op jit(solution)/shard_map/pallas_call | solution.py:623
  19.4 0.7 %collective-permute-start.6 = (f32[2,16,128]{2,1,0:T(8,128)S(1)}, f32[2,16,128]{2,1,0:T(8,128)S(1)}, u32[]{:S(2)}, u32[]{:S(2)}) collective-permute-start(f32[2,16,128]{2,1,0:T(8,128)S(1)} %get-tuple-element.32.refs_0_), channel_id=1, source_target_pairs={{0,1},{1,0},{2,3},{3,2},{4,5},{5,4},{6,7},{7,6},{8,9},{9,8},{10,11... | collective-permute-start | bytes 49160 | tf_op jit(solution)/shard_map/ppermute | solution.py:591
  20.1 1.2 %collective-permute-start.7 = (f32[2,16,128]{2,1,0:T(8,128)S(1)}, f32[2,16,128]{2,1,0:T(8,128)S(1)}, u32[]{:S(2)}, u32[]{:S(2)}) collective-permute-start(f32[2,16,128]{2,1,0:T(8,128)S(1)} %get-tuple-element.32.refs_0_), channel_id=1, source_target_pairs={{0,2},{1,3},{2,0},{3,1},{4,6},{5,7},{6,4},{7,5},{8,10},{9,11},{10,... | collective-permute-start | bytes 49160 | tf_op jit(solution)/shard_map/ppermute | solution.py:591
  21.3 0.3 collective-permute-start.8
  21.5 2.3 %collective-permute-done.7.refs_2_ = f32[2,16,128]{2,1,0:T(8,128)S(1)} collective-permute-done((f32[2,16,128]{2,1,0:T(8,128)S(1)}, f32[2,16,128]{2,1,0:T(8,128)S(1)}, u32[]{:S(2)}, u32[]{:S(2)}) %collective-permute-start.7) | collective-permute-done | bytes 16416 | tf_op jit(solution)/shard_map/ppermute | solution.py:591
  23.9 0.6 %collective-permute-done.8.refs_3_ = f32[2,16,128]{2,1,0:T(8,128)S(1)} collective-permute-done((f32[2,16,128]{2,1,0:T(8,128)S(1)}, f32[2,16,128]{2,1,0:T(8,128)S(1)}, u32[]{:S(2)}, u32[]{:S(2)}) %collective-permute-start.8) | collective-permute-done | bytes 16416 | tf_op jit(solution)/shard_map/ppermute | solution.py:591
  24.5 4.4 %collective-permute-start.10 = (f32[2,16,128]{2,1,0:T(8,128)S(1)}, f32[2,16,128]{2,1,0:T(8,128)S(1)}, u32[]{:S(2)}, u32[]{:S(2)}) collective-permute-start(f32[2,16,128]{2,1,0:T(8,128)S(1)} %shard_map.89.rest_0_), channel_id=1, source_target_pairs={{0,8},{4,12},{8,0},{12,4},{1,9},{5,13},{9,1},{13,5},{2,10},{6,14},... | collective-permute-start | bytes 49160 | tf_op jit(solution)/shard_map/ppermute | solution.py:591
  28.9 1.3 %collective-permute-start.11 = (f32[2,16,128]{2,1,0:T(8,128)S(1)}, f32[2,16,128]{2,1,0:T(8,128)S(1)}, u32[]{:S(2)}, u32[]{:S(2)}) collective-permute-start(f32[2,16,128]{2,1,0:T(8,128)S(1)} %shard_map.89.rest_0_), channel_id=1, source_target_pairs={{0,12},{4,8},{8,4},{12,0},{1,13},{5,9},{9,5},{13,1},{2,14},{6,10},... | collective-permute-start | bytes 49160 | tf_op jit(solution)/shard_map/ppermute | solution.py:591
  30.2 0.4 %collective-permute-done.10.rest_2_ = f32[2,16,128]{2,1,0:T(8,128)S(1)} collective-permute-done((f32[2,16,128]{2,1,0:T(8,128)S(1)}, f32[2,16,128]{2,1,0:T(8,128)S(1)}, u32[]{:S(2)}, u32[]{:S(2)}) %collective-permute-start.10) | collective-permute-done | bytes 16416 | tf_op jit(solution)/shard_map/ppermute | solution.py:591
  30.6 3.8 %collective-permute-done.11.rest_3_ = f32[2,16,128]{2,1,0:T(8,128)S(1)} collective-permute-done((f32[2,16,128]{2,1,0:T(8,128)S(1)}, f32[2,16,128]{2,1,0:T(8,128)S(1)}, u32[]{:S(2)}, u32[]{:S(2)}) %collective-permute-start.11) | collective-permute-done | bytes 16416 | tf_op jit(solution)/shard_map/ppermute | solution.py:591
  34.4 1.8 %shard_map.90 = (f32[2,20,8,256]{3,2,1,0:T(8,128)}, f32[2,20,8,256]{3,2,1,0:T(8,128)}, f32[8,256]{1,0:T(8,128)}) custom-call(f32[2,20,8,256]{3,2,1,0:T(8,128)S(1)} %get-tuple-element.18.rhs, f32[4,2,20,8,256]{4,3,2,1,0:T(8,128)S(1)} %get-tuple-element.25.powers, f32[4,2,5,8,128]{4,3,2,1,0:T(8,128)S(1)} %get-tuple-element.30.edges, ...), custom_call_target="tpu_custom_call" | custom-call | tf_op jit(solution)/shard_map/pallas_call | solution.py:633
  (6 shorter events, 0.0 us)
Async XLA Ops:
  2.0 8.6 %collective-permute-start = (f32[62,8,128]{2,1,0:T(8,128)S(1)}, f32[62,8,128]{2,1,0:T(8,128)S(1)}, u32[]{:S(2)}, u32[]{:S(2)}) collective-permute-start(f32[62,8,128]{2,1,0:T(8,128)S(1)} %get-tuple-element.23), channel_id=1, source_target_pairs={{0,0},{4,8},{8,4},{12,12},{1,1},{5,9},{9,5},{13,13},{2,2},{6,10},{... | collective-permute-start | bytes 761864 | tf_op jit(solution)/shard_map/ppermute | solution.py:42
  2.7 11.7 %collective-permute-start.1 = (f32[62,8,128]{2,1,0:T(8,128)S(1)}, f32[62,8,128]{2,1,0:T(8,128)S(1)}, u32[]{:S(2)}, u32[]{:S(2)}) collective-permute-start(f32[62,8,128]{2,1,0:T(8,128)S(1)} %get-tuple-element.24), channel_id=1, source_target_pairs={{0,4},{4,0},{8,12},{12,8},{1,5},{5,1},{9,13},{13,9},{2,6},{6,2},{1... | collective-permute-start | bytes 761864 | tf_op jit(solution)/shard_map/ppermute | solution.py:42
  8.6 1.2 %collective-permute-start.2 = (f32[3,8,128]{2,1,0:T(8,128)S(1)}, f32[3,8,128]{2,1,0:T(8,128)S(1)}, u32[]{:S(2)}, u32[]{:S(2)}) collective-permute-start(f32[3,8,128]{2,1,0:T(8,128)S(1)} %get-tuple-element.27), channel_id=1, source_target_pairs={{0,1},{1,0},{2,3},{3,2},{4,5},{5,4},{6,7},{7,6},{8,9},{9,8},{10,11... | collective-permute-start | bytes 36872 | tf_op jit(solution)/shard_map/ppermute | solution.py:42
  8.6 1.2 %collective-permute-start.3 = (f32[3,8,128]{2,1,0:T(8,128)S(1)}, f32[3,8,128]{2,1,0:T(8,128)S(1)}, u32[]{:S(2)}, u32[]{:S(2)}) collective-permute-start(f32[3,8,128]{2,1,0:T(8,128)S(1)} %get-tuple-element.28), channel_id=1, source_target_pairs={{0,0},{1,2},{2,1},{3,3},{4,4},{5,6},{6,5},{7,7},{8,8},{9,10},{10,9... | collective-permute-start | bytes 36872 | tf_op jit(solution)/shard_map/ppermute | solution.py:42
  9.8 8.9 %collective-permute-start.4 = (f32[6,8,128]{2,1,0:T(8,128)S(1)}, f32[6,8,128]{2,1,0:T(8,128)S(1)}, u32[]{:S(2)}, u32[]{:S(2)}) collective-permute-start(f32[6,8,128]{2,1,0:T(8,128)S(1)} %shard_map.87.columns), channel_id=1, source_target_pairs={{0,4},{4,0},{8,12},{12,8},{1,5},{5,1},{9,13},{13,9},{2,6},{6,2},{1... | collective-permute-start | bytes 73736 | tf_op jit(solution)/shard_map/ppermute | solution.py:42
  9.9 8.7 %collective-permute-start.5 = (f32[6,8,128]{2,1,0:T(8,128)S(1)}, f32[6,8,128]{2,1,0:T(8,128)S(1)}, u32[]{:S(2)}, u32[]{:S(2)}) collective-permute-start(f32[6,8,128]{2,1,0:T(8,128)S(1)} %shard_map.87.columns), channel_id=1, source_target_pairs={{0,0},{4,8},{8,4},{12,12},{1,1},{5,9},{9,5},{13,13},{2,2},{6,10},{... | collective-permute-start | bytes 73736 | tf_op jit(solution)/shard_map/ppermute | solution.py:42
  19.4 2.2 %collective-permute-start.6 = (f32[2,16,128]{2,1,0:T(8,128)S(1)}, f32[2,16,128]{2,1,0:T(8,128)S(1)}, u32[]{:S(2)}, u32[]{:S(2)}) collective-permute-start(f32[2,16,128]{2,1,0:T(8,128)S(1)} %get-tuple-element.32.refs_0_), channel_id=1, source_target_pairs={{0,1},{1,0},{2,3},{3,2},{4,5},{5,4},{6,7},{7,6},{8,9},{9,8},{10,11... | collective-permute-start | bytes 49160 | tf_op jit(solution)/shard_map/ppermute | solution.py:591
  20.1 3.7 %collective-permute-start.7 = (f32[2,16,128]{2,1,0:T(8,128)S(1)}, f32[2,16,128]{2,1,0:T(8,128)S(1)}, u32[]{:S(2)}, u32[]{:S(2)}) collective-permute-start(f32[2,16,128]{2,1,0:T(8,128)S(1)} %get-tuple-element.32.refs_0_), channel_id=1, source_target_pairs={{0,2},{1,3},{2,0},{3,1},{4,6},{5,7},{6,4},{7,5},{8,10},{9,11},{10,... | collective-permute-start | bytes 49160 | tf_op jit(solution)/shard_map/ppermute | solution.py:591
  21.3 3.2 %collective-permute-start.8 = (f32[2,16,128]{2,1,0:T(8,128)S(1)}, f32[2,16,128]{2,1,0:T(8,128)S(1)}, u32[]{:S(2)}, u32[]{:S(2)}) collective-permute-start(f32[2,16,128]{2,1,0:T(8,128)S(1)} %get-tuple-element.32.refs_0_), channel_id=1, source_target_pairs={{0,3},{1,2},{2,1},{3,0},{4,7},{5,6},{6,5},{7,4},{8,11},{9,10},{10,... | collective-permute-start | bytes 49160 | tf_op jit(solution)/shard_map/ppermute | solution.py:591
  24.5 6.1 %collective-permute-start.10 = (f32[2,16,128]{2,1,0:T(8,128)S(1)}, f32[2,16,128]{2,1,0:T(8,128)S(1)}, u32[]{:S(2)}, u32[]{:S(2)}) collective-permute-start(f32[2,16,128]{2,1,0:T(8,128)S(1)} %shard_map.89.rest_0_), channel_id=1, source_target_pairs={{0,8},{4,12},{8,0},{12,4},{1,9},{5,13},{9,1},{13,5},{2,10},{6,14},... | collective-permute-start | bytes 49160 | tf_op jit(solution)/shard_map/ppermute | solution.py:591
  28.9 5.5 %collective-permute-start.11 = (f32[2,16,128]{2,1,0:T(8,128)S(1)}, f32[2,16,128]{2,1,0:T(8,128)S(1)}, u32[]{:S(2)}, u32[]{:S(2)}) collective-permute-start(f32[2,16,128]{2,1,0:T(8,128)S(1)} %shard_map.89.rest_0_), channel_id=1, source_target_pairs={{0,12},{4,8},{8,4},{12,0},{1,13},{5,9},{9,5},{13,1},{2,14},{6,10},... | collective-permute-start | bytes 49160 | tf_op jit(solution)/shard_map/ppermute | solution.py:591
  30.2 4.2 %collective-permute-start.9 = (f32[2,16,128]{2,1,0:T(8,128)S(1)}, f32[2,16,128]{2,1,0:T(8,128)S(1)}, u32[]{:S(2)}, u32[]{:S(2)}) collective-permute-start(f32[2,16,128]{2,1,0:T(8,128)S(1)} %shard_map.89.rest_0_), channel_id=1, source_target_pairs={{0,4},{4,0},{8,12},{12,8},{1,5},{5,1},{9,13},{13,9},{2,6},{6,2},{1... | collective-permute-start | bytes 49160 | tf_op jit(solution)/shard_map/ppermute | solution.py:591

commit v13 on v12

--- a/solution.py
+++ b/solution.py
@@ -91,7 +91,7 @@
 
 
 def pack_kernel(*refs):
-    sources, held, (column_a, column_b, strip_a, strip_b, arrived) = refs[:6], refs[6:12], refs[12:]
+    sources, held, (packs, strip_a, strip_b, arrived) = refs[:6], refs[6:12], refs[12:]
     copies = [pltpu.make_async_copy(a, b, arrived.at[i]) for i, (a, b) in enumerate(zip(sources, held))]
     for copy in copies:
         copy.start()
@@ -103,7 +103,6 @@
     lane = lax.broadcasted_iota(jnp.int32, (ROWS, LANES), 1)
     row = lax.broadcasted_iota(jnp.int32, (ROWS, LANES), 0)
     rows_even, _, _ = place_of("gx")
-    columns_even, _, _ = place_of(("gy", "gz"))
     upper_a = (row < HALO) != rows_even
     count = ribbon_tiles(layers)
     zero = jnp.zeros((ROWS, LANES), jnp.float32)
@@ -123,25 +122,27 @@
                 at = slot * SLOT
                 left[tile] = jnp.where(between(lane, at + 8, 4), turned(v[:, :LANES], at + 8), left[tile])
                 right[tile] = jnp.where(between(lane, at + 16, 4), turned(v[:, LANES:], at + 20), right[tile])
-    to_left, to_right = [zero] * column_a.shape[0], [zero] * column_a.shape[0]
+    groups = packs.shape[0] // 2
+    packed = [zero] * packs.shape[0]
     for tile in range(count):
         group, at = packed_place(tile)
         here = between(lane % SLOT, at, HALO)
-        to_left[group] = jnp.where(here, turned(left[tile], at - 8), to_left[group])
-        to_right[group] = jnp.where(here, turned(right[tile], at - 16), to_right[group])
-    for group in range(column_a.shape[0]):
-        column_a[group] = jnp.where(columns_even, to_right[group], to_left[group])
-        column_b[group] = jnp.where(columns_even, to_left[group], to_right[group])
-
-
-def beside_kernel(from_a, from_b, columns):
-    even, has_a, has_b = place_of(("gy", "gz"))
-    count = from_a.shape[0]
-    for group in range(count):
-        a = jnp.where(has_a, from_a[group], 0.0)
-        b = jnp.where(has_b, from_b[group], 0.0)
-        columns[group] = jnp.where(even, a, b)
-        columns[count + group] = jnp.where(even, b, a)
+        packed[group] = jnp.where(here, turned(left[tile], at - 8), packed[group])
+        packed[groups + group] = jnp.where(here, turned(right[tile], at - 16), packed[groups + group])
+    for group, v in enumerate(packed):
+        packs[group] = v
+
+
+def column_kernel(packs, packs_b, packs_a, column_a, column_b):
+    below_and_above, _ = beyond()
+    even, _, _ = place_of(("gy", "gz"))
+    groups = packs.shape[0] // 2
+    for group in range(groups):
+        to_left, to_right = [
+            jnp.concatenate([packs[i], below_and_above(packs_a[i], packs_b[i])], 0) for i in (group, groups + group)
+        ]
+        column_a[group] = jnp.where(even, to_right, to_left)
+        column_b[group] = jnp.where(even, to_left, to_right)
 
 
 def two_sum(a, b):
@@ -388,21 +389,21 @@
         src, dst = dst, src
 
 
-def ribbon_kernel(ribbon, columns, columns_a, columns_b, sums, edges, moments):
+def ribbon_kernel(ribbon, column_a, column_b, sums, edges, moments):
     tiles = edges.shape[2]
-    below_and_above, _ = beyond()
     lane = lax.broadcasted_iota(jnp.int32, (2 * ROWS, LANES), 1)
-
-    count = columns.shape[0] // 2
-    beside = [
-        jnp.concatenate([columns[i], below_and_above(columns_a[i], columns_b[i])], 0) for i in range(2 * count)
+    even, has_a, has_b = place_of(("gy", "gz"))
+    came = [
+        (jnp.where(has_a, column_a[i], 0.0), jnp.where(has_b, column_b[i], 0.0)) for i in range(column_a.shape[0])
     ]
+    from_right = [jnp.where(even, a, b) for a, b in came]
+    from_left = [jnp.where(even, b, a) for a, b in came]
     spot = lane % SLOT
 
     def whole(tile):
         group, at = packed_place(tile)
-        right = jnp.where(between(spot, 8, HALO), turned(beside[group], 8 - at), ribbon[tile])
-        return jnp.where(between(spot, 16, HALO), turned(beside[count + group], 16 - at), right)
+        right = jnp.where(between(spot, 8, HALO), turned(from_right[group], 8 - at), ribbon[tile])
+        return jnp.where(between(spot, 16, HALO), turned(from_left[group], 16 - at), right)
 
     field = [[whole(c * tiles + n) for n in range(tiles)] for c in range(2)]
     eta = [whole(2 * tiles + n) for n in range(tiles)]
@@ -601,18 +602,21 @@
     tile = (ROWS, LANES)
     strips = (2 * (layers + layers // 2 + 1),) + tile
     ribbons = ribbon_tiles(layers)
-    packed = ((ribbons + 7) // 8,) + tile
-    both = (2 * packed[0],) + tile
-    *held, column_a, column_b, strip_a, strip_b = call(
+    groups = (ribbons + 7) // 8
+    *held, packs, strip_a, strip_b = call(
         pack_kernel,
-        [jax.ShapeDtypeStruct(x.shape, x.dtype) for x in inputs] + [packed, packed, strips, strips],
+        [jax.ShapeDtypeStruct(x.shape, x.dtype) for x in inputs] + [(2 * groups,) + tile, strips, strips],
         [pltpu.SemaphoreType.DMA((len(inputs),))],
         in_specs=[pl.BlockSpec(memory_space=pltpu.HBM)] * len(inputs),
     )(*[pltpu.with_memory_space_constraint(x, pltpu.HBM) for x in inputs])
+    packs_b, packs_a = swapped(packs, "gx", 1), swapped(packs, "gx", 0)
     strip_b, strip_a = swapped(strip_b, "gx", 1), swapped(strip_a, "gx", 0)
-    beside = ("gy", "gz")
-    (columns,) = call(beside_kernel, [both])(swapped(column_a, beside, 0), swapped(column_b, beside, 1))
-    columns_a, columns_b = swapped(columns, "gx", 0), swapped(columns, "gx", 1)
+    column_a, column_b = call(
+        column_kernel,
+        [(groups, 2 * ROWS, LANES)] * 2,
+        cost_estimate=pl.CostEstimate(flops=3_000_000_000, bytes_accessed=200_000, transcendentals=0),
+    )(packs, packs_b, packs_a)
+    column_a, column_b = swapped(column_a, ("gy", "gz"), 0), swapped(column_b, ("gy", "gz"), 1)
     block = (layers, 2 * ROWS, 2 * LANES)
     powers, sums, ribbon = call(
         main_kernel,
@@ -623,7 +627,7 @@
     edges, sums = call(
         ribbon_kernel,
         [(STEPS, 2, layers // 4) + tile, (2, 2 * ROWS, LANES)],
-    )(ribbon, columns, columns_a, columns_b, sums)
+    )(ribbon, column_a, column_b, sums)
     parts = exchange(sums, ("gy", "gz"))
     if len(parts) > 1:
         sums = call(add_kernel, [sums.shape])(*parts)[0]

time: 36.4 us -> 36.8 us (1.011)
  waiting for transfers between devices: 11.5 us -> 11.9 us
    ppermute x6, starting transfers between devices: 7.88 us -> 6.07 us  [exchange(): parts.append(lax.ppermute(x, axis, pairs))]
    ppermute x6, starting transfers between devices: 8.02 us -> 9.74 us  [swapped(): return lax.ppermute(x, axis, pairs)]
    ppermute x6, waiting for transfers between devices: 4.37 us -> 4.82 us  [swapped(): return lax.ppermute(x, axis, pairs)]
  transfers between devices with their start and end apart: 12 -> 12, of which waited for: 6 -> 5; matrix products, arithmetic and copies ran while one was open for 0% -> 0% of each run, Pallas kernels for 12% -> 12%
where the time goes in v13:
time: 36.8 us; the launch traced here: 36.6 us
  starting transfers between devices  15.8 us (43%)
  waiting for transfers between devices  11.9 us (32%)
  Pallas kernels  8.18 us (22%)
  between operations  0.74 us (2%)
    ppermute x6, starting transfers between devices, swapped(): return lax.ppermute(x, axis, pairs)  9.74 us
    ppermute x6, waiting for transfers between devices, exchange(): parts.append(lax.ppermute(x, axis, pairs))  7.04 us
    ppermute x6, starting transfers between devices, exchange(): parts.append(lax.ppermute(x, axis, pairs))  6.07 us
    ppermute x6, waiting for transfers between devices, swapped(): return lax.ppermute(x, axis, pairs)  4.82 us
    pallas_call x1, Pallas kernels, body(): call(main_kernel, [(STEPS,) + adjoint_rhs.shape, (2 * STEPS + 1, ROWS, 2...  4.19 us
    pallas_call x1, Pallas kernels, body(): call(final_kernel, [adjoint_rhs.shape, adjoint_rhs.shape, friction.shape])  1.81 us
    pallas_call x1, Pallas kernels, body(): call(pack_kernel, [jax.ShapeDtypeStruct(x.shape, x.dtype) for x in inputs...  1.35 us
    pallas_call x1, Pallas kernels, body(): call(ribbon_kernel, [(STEPS, 2, layers // 4) + tile, (2, 2 * ROWS, LANES)])  0.78 us
  transfers between devices with their start and end apart: 12, of which 5 were waited for; matrix products, arithmetic and copies ran while one was open for 0% of the time, Pallas kernels for 12%

profile of v13, /device:TPU:0, one launch (start us, length us, event | category | flops | bytes accessed | tf_op | source)
XLA Modules:
  0.0 36.6 jit_solution(11787529304935860927)
XLA Ops:
  0.6 1.3 %shard_map.85 = (f32[2,20,8,256]{3,2,1,0:T(8,128)S(1)}, f32[20,8,256]{2,1,0:T(8,128)S(1)}, f32[8,256]{1,0:T(8,128)S(1)}, s32[8,256]{1,0:T(8,128)S(1)}, s32[8,256...) custom-call(f32[2,20,8,256]{3,2,1,0:T(8,128)} %refs_0_.1, ...), custom_call_target="tpu_custom_call" | custom-call | tf_op jit(solution)/shard_map/pallas_call | solution.py:606
  2.0 0.7 %collective-permute-start.2 = (f32[6,8,128]{2,1,0:T(8,128)S(1)}, f32[6,8,128]{2,1,0:T(8,128)S(1)}, u32[]{:S(2)}, u32[]{:S(2)}) collective-permute-start(f32[6,8,128]{2,1,0:T(8,128)S(1)} %get-tuple-element.28.packs), channel_id=1, source_target_pairs={{0,0},{4,8},{8,4},{12,12},{1,1},{5,9},{9,5},{13,13},{2,2},{6,10},{... | collective-permute-start | bytes 73736 | tf_op jit(solution)/shard_map/ppermute | solution.py:42
  2.7 5.9 %collective-permute-start.3 = (f32[6,8,128]{2,1,0:T(8,128)S(1)}, f32[6,8,128]{2,1,0:T(8,128)S(1)}, u32[]{:S(2)}, u32[]{:S(2)}) collective-permute-start(f32[6,8,128]{2,1,0:T(8,128)S(1)} %get-tuple-element.28.packs), channel_id=1, source_target_pairs={{0,4},{4,0},{8,12},{12,8},{1,5},{5,1},{9,13},{13,9},{2,6},{6,2},{1... | collective-permute-start | bytes 73736 | tf_op jit(solution)/shard_map/ppermute | solution.py:42
  8.6 0.7 %collective-permute-start = (f32[62,8,128]{2,1,0:T(8,128)S(1)}, f32[62,8,128]{2,1,0:T(8,128)S(1)}, u32[]{:S(2)}, u32[]{:S(2)}) collective-permute-start(f32[62,8,128]{2,1,0:T(8,128)S(1)} %get-tuple-element.24), channel_id=1, source_target_pairs={{0,0},{4,8},{8,4},{12,12},{1,1},{5,9},{9,5},{13,13},{2,2},{6,10},{... | collective-permute-start | bytes 761864 | tf_op jit(solution)/shard_map/ppermute | solution.py:42
  9.2 1.8 %collective-permute-start.1 = (f32[62,8,128]{2,1,0:T(8,128)S(1)}, f32[62,8,128]{2,1,0:T(8,128)S(1)}, u32[]{:S(2)}, u32[]{:S(2)}) collective-permute-start(f32[62,8,128]{2,1,0:T(8,128)S(1)} %get-tuple-element.25), channel_id=1, source_target_pairs={{0,4},{4,0},{8,12},{12,8},{1,5},{5,1},{9,13},{13,9},{2,6},{6,2},{1... | collective-permute-start | bytes 761864 | tf_op jit(solution)/shard_map/ppermute | solution.py:42
  11.0 0.0 collective-permute-done.2.packs_b
  11.0 0.0 collective-permute-done.3.packs_a
  11.1 0.1 collective-permute-start.4
  11.1 0.7 %collective-permute-start.5 = (f32[3,16,128]{2,1,0:T(8,128)S(1)}, f32[3,16,128]{2,1,0:T(8,128)S(1)}, u32[]{:S(2)}, u32[]{:S(2)}) collective-permute-start(f32[3,16,128]{2,1,0:T(8,128)S(1)} %get-tuple-element.30), channel_id=1, source_target_pairs={{0,0},{1,2},{2,1},{3,3},{4,4},{5,6},{6,5},{7,7},{8,8},{9,10},{10,9... | collective-permute-start | bytes 73736 | tf_op jit(solution)/shard_map/ppermute | solution.py:42
  11.8 0.0 collective-permute-done.strip_b
  11.8 4.8 %collective-permute-done.1.strip_a = f32[62,8,128]{2,1,0:T(8,128)S(1)} collective-permute-done((f32[62,8,128]{2,1,0:T(8,128)S(1)}, f32[62,8,128]{2,1,0:T(8,128)S(1)}, u32[]{:S(2)}, u32[]{:S(2)}) %collective-permute-start.1) | collective-permute-done | bytes 253984 | tf_op jit(solution)/shard_map/ppermute | solution.py:42
  16.6 4.2 %shard_map.86 = (f32[4,2,20,8,256]{4,3,2,1,0:T(8,128)S(1)}, f32[9,8,256]{2,1,0:T(8,128)S(1)}, f32[17,16,128]{2,1,0:T(8,128)S(1)}) custom-call(f32[2,20,8,256]{3,2,1,0:T(8,128)S(1)} %get-tuple-element.19.rhs, f32[20,8,256]{2,1,0:T(8,128)S(1)} %get-tuple-element.20.eta, f32[8,256]{1,0:T(8,128)S(1)} %get-tuple-element.21.friction, ...), custom_call_target="tpu_custom_call" | custom-call | flops 200000000 | bytes 8000000 | tf_op jit(solution)/shard_map/pallas_call | solution.py:621
  20.8 0.0 collective-permute-done.5.column_b
  20.8 0.8 %shard_map.88 = (f32[4,2,5,8,128]{4,3,2,1,0:T(8,128)S(1)}, f32[2,16,128]{2,1,0:T(8,128)S(1)}) custom-call(f32[17,16,128]{2,1,0:T(8,128)S(1)} %get-tuple-element.27.ribbon, f32[3,16,128]{2,1,0:T(8,128)S(1)} %collective-permute-done.4.column_a, f32[3,16,128]{2,1,0:T(8,128)S(1)} %collective-permute-done.5.column_b, f32[9,8,256]{2,1,0:T(8,128)S(1)} %get-tuple-element.31.sums), custom_call_target="tpu_custom_call" | custom-call | tf_op jit(solution)/shard_map/pallas_call | solution.py:627
  21.6 0.1 collective-permute-start.6
  21.7 1.6 %collective-permute-start.7 = (f32[2,16,128]{2,1,0:T(8,128)S(1)}, f32[2,16,128]{2,1,0:T(8,128)S(1)}, u32[]{:S(2)}, u32[]{:S(2)}) collective-permute-start(f32[2,16,128]{2,1,0:T(8,128)S(1)} %get-tuple-element.34.refs_0_), channel_id=1, source_target_pairs={{0,2},{1,3},{2,0},{3,1},{4,6},{5,7},{6,4},{7,5},{8,10},{9,11},{10,... | collective-permute-start | bytes 49160 | tf_op jit(solution)/shard_map/ppermute | solution.py:592
  23.3 0.3 collective-permute-start.8
  23.6 1.9 %collective-permute-done.7.refs_2_ = f32[2,16,128]{2,1,0:T(8,128)S(1)} collective-permute-done((f32[2,16,128]{2,1,0:T(8,128)S(1)}, f32[2,16,128]{2,1,0:T(8,128)S(1)}, u32[]{:S(2)}, u32[]{:S(2)}) %collective-permute-start.7) | collective-permute-done | bytes 16416 | tf_op jit(solution)/shard_map/ppermute | solution.py:592
  25.5 0.9 %collective-permute-done.8.refs_3_ = f32[2,16,128]{2,1,0:T(8,128)S(1)} collective-permute-done((f32[2,16,128]{2,1,0:T(8,128)S(1)}, f32[2,16,128]{2,1,0:T(8,128)S(1)}, u32[]{:S(2)}, u32[]{:S(2)}) %collective-permute-start.8) | collective-permute-done | bytes 16416 | tf_op jit(solution)/shard_map/ppermute | solution.py:592
  26.5 2.8 %collective-permute-start.10 = (f32[2,16,128]{2,1,0:T(8,128)S(1)}, f32[2,16,128]{2,1,0:T(8,128)S(1)}, u32[]{:S(2)}, u32[]{:S(2)}) collective-permute-start(f32[2,16,128]{2,1,0:T(8,128)S(1)} %shard_map.89.rest_0_), channel_id=1, source_target_pairs={{0,8},{4,12},{8,0},{12,4},{1,9},{5,13},{9,1},{13,5},{2,10},{6,14},... | collective-permute-start | bytes 49160 | tf_op jit(solution)/shard_map/ppermute | solution.py:592
  29.2 1.3 %collective-permute-start.11 = (f32[2,16,128]{2,1,0:T(8,128)S(1)}, f32[2,16,128]{2,1,0:T(8,128)S(1)}, u32[]{:S(2)}, u32[]{:S(2)}) collective-permute-start(f32[2,16,128]{2,1,0:T(8,128)S(1)} %shard_map.89.rest_0_), channel_id=1, source_target_pairs={{0,12},{4,8},{8,4},{12,0},{1,13},{5,9},{9,5},{13,1},{2,14},{6,10},... | collective-permute-start | bytes 49160 | tf_op jit(solution)/shard_map/ppermute | solution.py:592
  30.6 0.6 %collective-permute-done.10.rest_2_ = f32[2,16,128]{2,1,0:T(8,128)S(1)} collective-permute-done((f32[2,16,128]{2,1,0:T(8,128)S(1)}, f32[2,16,128]{2,1,0:T(8,128)S(1)}, u32[]{:S(2)}, u32[]{:S(2)}) %collective-permute-start.10) | collective-permute-done | bytes 16416 | tf_op jit(solution)/shard_map/ppermute | solution.py:592
  31.2 3.6 %collective-permute-done.11.rest_3_ = f32[2,16,128]{2,1,0:T(8,128)S(1)} collective-permute-done((f32[2,16,128]{2,1,0:T(8,128)S(1)}, f32[2,16,128]{2,1,0:T(8,128)S(1)}, u32[]{:S(2)}, u32[]{:S(2)}) %collective-permute-start.11) | collective-permute-done | bytes 16416 | tf_op jit(solution)/shard_map/ppermute | solution.py:592
  34.8 1.8 %shard_map.90 = (f32[2,20,8,256]{3,2,1,0:T(8,128)}, f32[2,20,8,256]{3,2,1,0:T(8,128)}, f32[8,256]{1,0:T(8,128)}) custom-call(f32[2,20,8,256]{3,2,1,0:T(8,128)S(1)} %get-tuple-element.19.rhs, f32[4,2,20,8,256]{4,3,2,1,0:T(8,128)S(1)} %get-tuple-element.26.powers, f32[4,2,5,8,128]{4,3,2,1,0:T(8,128)S(1)} %get-tuple-element.32.edges, ...), custom_call_target="tpu_custom_call" | custom-call | tf_op jit(solution)/shard_map/pallas_call | solution.py:637
  (6 shorter events, 0.1 us)
Async XLA Ops:
  2.0 9.0 %collective-permute-start.2 = (f32[6,8,128]{2,1,0:T(8,128)S(1)}, f32[6,8,128]{2,1,0:T(8,128)S(1)}, u32[]{:S(2)}, u32[]{:S(2)}) collective-permute-start(f32[6,8,128]{2,1,0:T(8,128)S(1)} %get-tuple-element.28.packs), channel_id=1, source_target_pairs={{0,0},{4,8},{8,4},{12,12},{1,1},{5,9},{9,5},{13,13},{2,2},{6,10},{... | collective-permute-start | bytes 73736 | tf_op jit(solution)/shard_map/ppermute | solution.py:42
  2.7 8.4 %collective-permute-start.3 = (f32[6,8,128]{2,1,0:T(8,128)S(1)}, f32[6,8,128]{2,1,0:T(8,128)S(1)}, u32[]{:S(2)}, u32[]{:S(2)}) collective-permute-start(f32[6,8,128]{2,1,0:T(8,128)S(1)} %get-tuple-element.28.packs), channel_id=1, source_target_pairs={{0,4},{4,0},{8,12},{12,8},{1,5},{5,1},{9,13},{13,9},{2,6},{6,2},{1... | collective-permute-start | bytes 73736 | tf_op jit(solution)/shard_map/ppermute | solution.py:42
  8.6 3.2 %collective-permute-start = (f32[62,8,128]{2,1,0:T(8,128)S(1)}, f32[62,8,128]{2,1,0:T(8,128)S(1)}, u32[]{:S(2)}, u32[]{:S(2)}) collective-permute-start(f32[62,8,128]{2,1,0:T(8,128)S(1)} %get-tuple-element.24), channel_id=1, source_target_pairs={{0,0},{4,8},{8,4},{12,12},{1,1},{5,9},{9,5},{13,13},{2,2},{6,10},{... | collective-permute-start | bytes 761864 | tf_op jit(solution)/shard_map/ppermute | solution.py:42
  9.2 7.4 %collective-permute-start.1 = (f32[62,8,128]{2,1,0:T(8,128)S(1)}, f32[62,8,128]{2,1,0:T(8,128)S(1)}, u32[]{:S(2)}, u32[]{:S(2)}) collective-permute-start(f32[62,8,128]{2,1,0:T(8,128)S(1)} %get-tuple-element.25), channel_id=1, source_target_pairs={{0,4},{4,0},{8,12},{12,8},{1,5},{5,1},{9,13},{13,9},{2,6},{6,2},{1... | collective-permute-start | bytes 761864 | tf_op jit(solution)/shard_map/ppermute | solution.py:42
  11.1 9.8 %collective-permute-start.4 = (f32[3,16,128]{2,1,0:T(8,128)S(1)}, f32[3,16,128]{2,1,0:T(8,128)S(1)}, u32[]{:S(2)}, u32[]{:S(2)}) collective-permute-start(f32[3,16,128]{2,1,0:T(8,128)S(1)} %get-tuple-element.29), channel_id=1, source_target_pairs={{0,1},{1,0},{2,3},{3,2},{4,5},{5,4},{6,7},{7,6},{8,9},{9,8},{10,11... | collective-permute-start | bytes 73736 | tf_op jit(solution)/shard_map/ppermute | solution.py:42
  11.1 9.7 %collective-permute-start.5 = (f32[3,16,128]{2,1,0:T(8,128)S(1)}, f32[3,16,128]{2,1,0:T(8,128)S(1)}, u32[]{:S(2)}, u32[]{:S(2)}) collective-permute-start(f32[3,16,128]{2,1,0:T(8,128)S(1)} %get-tuple-element.30), channel_id=1, source_target_pairs={{0,0},{1,2},{2,1},{3,3},{4,4},{5,6},{6,5},{7,7},{8,8},{9,10},{10,9... | collective-permute-start | bytes 73736 | tf_op jit(solution)/shard_map/ppermute | solution.py:42
  21.6 1.9 %collective-permute-start.6 = (f32[2,16,128]{2,1,0:T(8,128)S(1)}, f32[2,16,128]{2,1,0:T(8,128)S(1)}, u32[]{:S(2)}, u32[]{:S(2)}) collective-permute-start(f32[2,16,128]{2,1,0:T(8,128)S(1)} %get-tuple-element.34.refs_0_), channel_id=1, source_target_pairs={{0,1},{1,0},{2,3},{3,2},{4,5},{5,4},{6,7},{7,6},{8,9},{9,8},{10,11... | collective-permute-start | bytes 49160 | tf_op jit(solution)/shard_map/ppermute | solution.py:592
  21.7 3.8 %collective-permute-start.7 = (f32[2,16,128]{2,1,0:T(8,128)S(1)}, f32[2,16,128]{2,1,0:T(8,128)S(1)}, u32[]{:S(2)}, u32[]{:S(2)}) collective-permute-start(f32[2,16,128]{2,1,0:T(8,128)S(1)} %get-tuple-element.34.refs_0_), channel_id=1, source_target_pairs={{0,2},{1,3},{2,0},{3,1},{4,6},{5,7},{6,4},{7,5},{8,10},{9,11},{10,... | collective-permute-start | bytes 49160 | tf_op jit(solution)/shard_map/ppermute | solution.py:592
  23.3 3.2 %collective-permute-start.8 = (f32[2,16,128]{2,1,0:T(8,128)S(1)}, f32[2,16,128]{2,1,0:T(8,128)S(1)}, u32[]{:S(2)}, u32[]{:S(2)}) collective-permute-start(f32[2,16,128]{2,1,0:T(8,128)S(1)} %get-tuple-element.34.refs_0_), channel_id=1, source_target_pairs={{0,3},{1,2},{2,1},{3,0},{4,7},{5,6},{6,5},{7,4},{8,11},{9,10},{10,... | collective-permute-start | bytes 49160 | tf_op jit(solution)/shard_map/ppermute | solution.py:592
  26.5 4.7 %collective-permute-start.10 = (f32[2,16,128]{2,1,0:T(8,128)S(1)}, f32[2,16,128]{2,1,0:T(8,128)S(1)}, u32[]{:S(2)}, u32[]{:S(2)}) collective-permute-start(f32[2,16,128]{2,1,0:T(8,128)S(1)} %shard_map.89.rest_0_), channel_id=1, source_target_pairs={{0,8},{4,12},{8,0},{12,4},{1,9},{5,13},{9,1},{13,5},{2,10},{6,14},... | collective-permute-start | bytes 49160 | tf_op jit(solution)/shard_map/ppermute | solution.py:592
  29.2 5.5 %collective-permute-start.11 = (f32[2,16,128]{2,1,0:T(8,128)S(1)}, f32[2,16,128]{2,1,0:T(8,128)S(1)}, u32[]{:S(2)}, u32[]{:S(2)}) collective-permute-start(f32[2,16,128]{2,1,0:T(8,128)S(1)} %shard_map.89.rest_0_), channel_id=1, source_target_pairs={{0,12},{4,8},{8,4},{12,0},{1,13},{5,9},{9,5},{13,1},{2,14},{6,10},... | collective-permute-start | bytes 49160 | tf_op jit(solution)/shard_map/ppermute | solution.py:592
  30.6 4.2 %collective-permute-start.9 = (f32[2,16,128]{2,1,0:T(8,128)S(1)}, f32[2,16,128]{2,1,0:T(8,128)S(1)}, u32[]{:S(2)}, u32[]{:S(2)}) collective-permute-start(f32[2,16,128]{2,1,0:T(8,128)S(1)} %shard_map.89.rest_0_), channel_id=1, source_target_pairs={{0,4},{4,0},{8,12},{12,8},{1,5},{5,1},{9,13},{13,9},{2,6},{6,2},{1... | collective-permute-start | bytes 49160 | tf_op jit(solution)/shard_map/ppermute | solution.py:592

commit v14 on v12

--- a/solution.py
+++ b/solution.py
@@ -33,13 +33,17 @@
     return even, has_a, has_b
 
 
-def swapped(x, axis, first):
-    count = lax.axis_size(axis)
+def swapped(x, axes, first):
+    count, parts = lax.axis_size(axes), lax.axis_size("parts")
     pairs = []
-    for i in range(count):
-        other = i + 1 if (i - first) % 2 == 0 else i - 1
-        pairs.append((i, other if 0 <= other < count else i))
-    return lax.ppermute(x, axis, pairs)
+    for part in range(parts):
+        for i in range(count):
+            other = i + 1 if (i - first) % 2 == 0 else i - 1
+            at = part
+            if not 0 <= other < count:
+                other, at = i, part ^ 1 if part ^ 1 < parts else part
+            pairs.append((part * count + i, at * count + other))
+    return lax.ppermute(x, ("parts", *axes), pairs)
 
 
 def own_planes(rhs, eta, friction, ice, grounded):
@@ -388,7 +392,7 @@
         src, dst = dst, src
 
 
-def ribbon_kernel(ribbon, columns, columns_a, columns_b, sums, edges, moments):
+def ribbon_kernel(ribbon, columns, columns_b, columns_a, sums, edges, moments):
     tiles = edges.shape[2]
     below_and_above, _ = beyond()
     lane = lax.broadcasted_iota(jnp.int32, (2 * ROWS, LANES), 1)
@@ -609,10 +613,10 @@
         [pltpu.SemaphoreType.DMA((len(inputs),))],
         in_specs=[pl.BlockSpec(memory_space=pltpu.HBM)] * len(inputs),
     )(*[pltpu.with_memory_space_constraint(x, pltpu.HBM) for x in inputs])
-    strip_b, strip_a = swapped(strip_b, "gx", 1), swapped(strip_a, "gx", 0)
+    strip_b, strip_a = swapped(strip_b, ("gx",), 1), swapped(strip_a, ("gx",), 0)
     beside = ("gy", "gz")
     (columns,) = call(beside_kernel, [both])(swapped(column_a, beside, 0), swapped(column_b, beside, 1))
-    columns_a, columns_b = swapped(columns, "gx", 0), swapped(columns, "gx", 1)
+    columns_b, columns_a = swapped(columns, ("gx",), 1), swapped(columns, ("gx",), 0)
     block = (layers, 2 * ROWS, 2 * LANES)
     powers, sums, ribbon = call(
         main_kernel,
@@ -623,7 +627,7 @@
     edges, sums = call(
         ribbon_kernel,
         [(STEPS, 2, layers // 4) + tile, (2, 2 * ROWS, LANES)],
-    )(ribbon, columns, columns_a, columns_b, sums)
+    )(ribbon, columns, columns_b, columns_a, sums)
     parts = exchange(sums, ("gy", "gz"))
     if len(parts) > 1:
         sums = call(add_kernel, [sums.shape])(*parts)[0]

time: 36.4 us -> 33.9 us (0.931)
  starting transfers between devices: 15.9 us -> 14.7 us
  waiting for transfers between devices: 11.5 us -> 10.3 us
    ppermute x6, starting transfers between devices: 7.88 us -> 6.3 us  [exchange(): parts.append(lax.ppermute(x, axis, pairs))]
    ppermute x6, waiting for transfers between devices: 4.37 us -> 3.11 us  [swapped(): return lax.ppermute(x, ('parts', *axes), pairs)]
  transfers between devices with their start and end apart: 12 -> 12, of which waited for: 6 -> 5; matrix products, arithmetic and copies ran while one was open for 0% -> 0% of each run, Pallas kernels for 12% -> 12%
where the time goes in v14:
time: 33.9 us; the launch traced here: 33.8 us
  starting transfers between devices  14.7 us (43%)
  waiting for transfers between devices  10.3 us (30%)
  Pallas kernels  8.12 us (24%)
  between operations  0.69 us (2%)
    ppermute x6, starting transfers between devices, swapped(): return lax.ppermute(x, ('parts', *axes), pairs)  8.35 us
    ppermute x6, waiting for transfers between devices, exchange(): parts.append(lax.ppermute(x, axis, pairs))  7.18 us
    ppermute x6, starting transfers between devices, exchange(): parts.append(lax.ppermute(x, axis, pairs))  6.3 us
    pallas_call x1, Pallas kernels, body(): call(main_kernel, [(STEPS,) + adjoint_rhs.shape, (2 * STEPS + 1, ROWS, 2...  4.19 us
    ppermute x6, waiting for transfers between devices, swapped(): return lax.ppermute(x, ('parts', *axes), pairs)  3.11 us
    pallas_call x1, Pallas kernels, body(): call(final_kernel, [adjoint_rhs.shape, adjoint_rhs.shape, friction.shape])  1.81 us
    pallas_call x1, Pallas kernels, body(): call(pack_kernel, [jax.ShapeDtypeStruct(x.shape, x.dtype) for x in inputs...  1.35 us
    pallas_call x1, Pallas kernels, body(): call(ribbon_kernel, [(STEPS, 2, layers // 4) + tile, (2, 2 * ROWS, LANES)])  0.74 us
  transfers between devices with their start and end apart: 12, of which 5 were waited for; matrix products, arithmetic and copies ran while one was open for 0% of the time, Pallas kernels for 12%

profile of v14, /device:TPU:0, one launch (start us, length us, event | category | flops | bytes accessed | tf_op | source)
XLA Modules:
  0.0 33.8 jit_solution(8005405866441827706)
XLA Ops:
  0.6 1.3 %shard_map.85 = (f32[2,20,8,256]{3,2,1,0:T(8,128)S(1)}, f32[20,8,256]{2,1,0:T(8,128)S(1)}, f32[8,256]{1,0:T(8,128)S(1)}, s32[8,256]{1,0:T(8,128)S(1)}, s32[8,256...) custom-call(f32[2,20,8,256]{3,2,1,0:T(8,128)} %refs_0_.1, ...), custom_call_target="tpu_custom_call" | custom-call | tf_op jit(solution)/shard_map/pallas_call | solution.py:610
  2.0 3.0 %collective-permute-start = (f32[62,8,128]{2,1,0:T(8,128)S(1)}, f32[62,8,128]{2,1,0:T(8,128)S(1)}, u32[]{:S(2)}, u32[]{:S(2)}) collective-permute-start(f32[62,8,128]{2,1,0:T(8,128)S(1)} %get-tuple-element.23), channel_id=1, source_target_pairs={{0,16},{4,8},{8,4},{12,28},{16,0},{20,24},{24,20},{28,12},{1,17},{... | collective-permute-start | bytes 761864 | tf_op jit(solution)/shard_map/ppermute | solution.py:46
  5.0 1.6 %collective-permute-start.1 = (f32[62,8,128]{2,1,0:T(8,128)S(1)}, f32[62,8,128]{2,1,0:T(8,128)S(1)}, u32[]{:S(2)}, u32[]{:S(2)}) collective-permute-start(f32[62,8,128]{2,1,0:T(8,128)S(1)} %get-tuple-element.24), channel_id=1, source_target_pairs={{0,4},{4,0},{8,12},{12,8},{16,20},{20,16},{24,28},{28,24},{1,5},{5... | collective-permute-start | bytes 761864 | tf_op jit(solution)/shard_map/ppermute | solution.py:46
  6.7 1.5 %collective-permute-start.3 = (f32[3,8,128]{2,1,0:T(8,128)S(1)}, f32[3,8,128]{2,1,0:T(8,128)S(1)}, u32[]{:S(2)}, u32[]{:S(2)}) collective-permute-start(f32[3,8,128]{2,1,0:T(8,128)S(1)} %get-tuple-element.28), channel_id=1, source_target_pairs={{0,16},{1,2},{2,1},{3,19},{16,0},{17,18},{18,17},{19,3},{4,20},{5,... | collective-permute-start | bytes 36872 | tf_op jit(solution)/shard_map/ppermute | solution.py:46
  8.2 3.1 %collective-permute-done.3.from_b = f32[3,8,128]{2,1,0:T(8,128)S(1)} collective-permute-done((f32[3,8,128]{2,1,0:T(8,128)S(1)}, f32[3,8,128]{2,1,0:T(8,128)S(1)}, u32[]{:S(2)}, u32[]{:S(2)}) %collective-permute-start.3) | collective-permute-done | bytes 12320 | tf_op jit(solution)/shard_map/ppermute | solution.py:46
  11.3 1.7 %collective-permute-start.4 = (f32[6,8,128]{2,1,0:T(8,128)S(1)}, f32[6,8,128]{2,1,0:T(8,128)S(1)}, u32[]{:S(2)}, u32[]{:S(2)}) collective-permute-start(f32[6,8,128]{2,1,0:T(8,128)S(1)} %shard_map.87.columns), channel_id=1, source_target_pairs={{0,16},{4,8},{8,4},{12,28},{16,0},{20,24},{24,20},{28,12},{1,17},{... | collective-permute-start | bytes 73736 | tf_op jit(solution)/shard_map/ppermute | solution.py:46
  13.0 0.4 %collective-permute-start.5 = (f32[6,8,128]{2,1,0:T(8,128)S(1)}, f32[6,8,128]{2,1,0:T(8,128)S(1)}, u32[]{:S(2)}, u32[]{:S(2)}) collective-permute-start(f32[6,8,128]{2,1,0:T(8,128)S(1)} %shard_map.87.columns), channel_id=1, source_target_pairs={{0,4},{4,0},{8,12},{12,8},{16,20},{20,16},{24,28},{28,24},{1,5},{5... | collective-permute-start | bytes 73736 | tf_op jit(solution)/shard_map/ppermute | solution.py:46
  13.5 0.0 collective-permute-done.strip_b
  13.5 0.0 collective-permute-done.1.strip_a
  13.5 4.2 %shard_map.86 = (f32[4,2,20,8,256]{4,3,2,1,0:T(8,128)S(1)}, f32[9,8,256]{2,1,0:T(8,128)S(1)}, f32[17,16,128]{2,1,0:T(8,128)S(1)}) custom-call(f32[2,20,8,256]{3,2,1,0:T(8,128)S(1)} %get-tuple-element.18.rhs, f32[20,8,256]{2,1,0:T(8,128)S(1)} %get-tuple-element.19.eta, f32[8,256]{1,0:T(8,128)S(1)} %get-tuple-element.20.friction, ...), custom_call_target="tpu_custom_call" | custom-call | flops 200000000 | bytes 8000000 | tf_op jit(solution)/shard_map/pallas_call | solution.py:621
  17.7 0.0 collective-permute-done.4.columns_b
  17.7 0.0 collective-permute-done.5.columns_a
  17.7 0.7 %shard_map.88 = (f32[4,2,5,8,128]{4,3,2,1,0:T(8,128)S(1)}, f32[2,16,128]{2,1,0:T(8,128)S(1)}) custom-call(f32[17,16,128]{2,1,0:T(8,128)S(1)} %get-tuple-element.26.ribbon, f32[6,8,128]{2,1,0:T(8,128)S(1)} %shard_map.87.columns, f32[6,8,128]{2,1,0:T(8,128)S(1)} %collective-permute-done.4.columns_b, f32[6,8,128]{2,1,0:T(8,128)S(1)} %collective-permute-done.5.columns_a, ...), custom_call_target="tpu_custom_call" | custom-call | tf_op jit(solution)/shard_map/pallas_call | solution.py:627
  18.4 0.1 collective-permute-start.6
  18.5 1.0 %collective-permute-start.7 = (f32[2,16,128]{2,1,0:T(8,128)S(1)}, f32[2,16,128]{2,1,0:T(8,128)S(1)}, u32[]{:S(2)}, u32[]{:S(2)}) collective-permute-start(f32[2,16,128]{2,1,0:T(8,128)S(1)} %get-tuple-element.32.refs_0_), channel_id=1, source_target_pairs={{0,2},{1,3},{2,0},{3,1},{4,6},{5,7},{6,4},{7,5},{8,10},{9,11},{10,... | collective-permute-start | bytes 49160 | tf_op jit(solution)/shard_map/ppermute | solution.py:595
  19.5 0.9 %collective-permute-start.8 = (f32[2,16,128]{2,1,0:T(8,128)S(1)}, f32[2,16,128]{2,1,0:T(8,128)S(1)}, u32[]{:S(2)}, u32[]{:S(2)}) collective-permute-start(f32[2,16,128]{2,1,0:T(8,128)S(1)} %get-tuple-element.32.refs_0_), channel_id=1, source_target_pairs={{0,3},{1,2},{2,1},{3,0},{4,7},{5,6},{6,5},{7,4},{8,11},{9,10},{10,... | collective-permute-start | bytes 49160 | tf_op jit(solution)/shard_map/ppermute | solution.py:595
  20.4 1.9 %collective-permute-done.7.refs_2_ = f32[2,16,128]{2,1,0:T(8,128)S(1)} collective-permute-done((f32[2,16,128]{2,1,0:T(8,128)S(1)}, f32[2,16,128]{2,1,0:T(8,128)S(1)}, u32[]{:S(2)}, u32[]{:S(2)}) %collective-permute-start.7) | collective-permute-done | bytes 16416 | tf_op jit(solution)/shard_map/ppermute | solution.py:595
  22.3 0.3 %collective-permute-done.8.refs_3_ = f32[2,16,128]{2,1,0:T(8,128)S(1)} collective-permute-done((f32[2,16,128]{2,1,0:T(8,128)S(1)}, f32[2,16,128]{2,1,0:T(8,128)S(1)}, u32[]{:S(2)}, u32[]{:S(2)}) %collective-permute-start.8) | collective-permute-done | bytes 16416 | tf_op jit(solution)/shard_map/ppermute | solution.py:595
  22.7 3.7 %collective-permute-start.10 = (f32[2,16,128]{2,1,0:T(8,128)S(1)}, f32[2,16,128]{2,1,0:T(8,128)S(1)}, u32[]{:S(2)}, u32[]{:S(2)}) collective-permute-start(f32[2,16,128]{2,1,0:T(8,128)S(1)} %shard_map.89.rest_0_), channel_id=1, source_target_pairs={{0,8},{4,12},{8,0},{12,4},{1,9},{5,13},{9,1},{13,5},{2,10},{6,14},... | collective-permute-start | bytes 49160 | tf_op jit(solution)/shard_map/ppermute | solution.py:595
  26.4 0.1 collective-permute-start.11
  26.5 0.5 %collective-permute-start.9 = (f32[2,16,128]{2,1,0:T(8,128)S(1)}, f32[2,16,128]{2,1,0:T(8,128)S(1)}, u32[]{:S(2)}, u32[]{:S(2)}) collective-permute-start(f32[2,16,128]{2,1,0:T(8,128)S(1)} %shard_map.89.rest_0_), channel_id=1, source_target_pairs={{0,4},{4,0},{8,12},{12,8},{1,5},{5,1},{9,13},{13,9},{2,6},{6,2},{1... | collective-permute-start | bytes 49160 | tf_op jit(solution)/shard_map/ppermute | solution.py:595
  27.1 1.1 %collective-permute-done.10.rest_2_ = f32[2,16,128]{2,1,0:T(8,128)S(1)} collective-permute-done((f32[2,16,128]{2,1,0:T(8,128)S(1)}, f32[2,16,128]{2,1,0:T(8,128)S(1)}, u32[]{:S(2)}, u32[]{:S(2)}) %collective-permute-start.10) | collective-permute-done | bytes 16416 | tf_op jit(solution)/shard_map/ppermute | solution.py:595
  28.1 3.8 %collective-permute-done.11.rest_3_ = f32[2,16,128]{2,1,0:T(8,128)S(1)} collective-permute-done((f32[2,16,128]{2,1,0:T(8,128)S(1)}, f32[2,16,128]{2,1,0:T(8,128)S(1)}, u32[]{:S(2)}, u32[]{:S(2)}) %collective-permute-start.11) | collective-permute-done | bytes 16416 | tf_op jit(solution)/shard_map/ppermute | solution.py:595
  32.0 1.8 %shard_map.90 = (f32[2,20,8,256]{3,2,1,0:T(8,128)}, f32[2,20,8,256]{3,2,1,0:T(8,128)}, f32[8,256]{1,0:T(8,128)}) custom-call(f32[2,20,8,256]{3,2,1,0:T(8,128)S(1)} %get-tuple-element.18.rhs, f32[4,2,20,8,256]{4,3,2,1,0:T(8,128)S(1)} %get-tuple-element.25.powers, f32[4,2,5,8,128]{4,3,2,1,0:T(8,128)S(1)} %get-tuple-element.30.edges, ...), custom_call_target="tpu_custom_call" | custom-call | tf_op jit(solution)/shard_map/pallas_call | solution.py:637
  (6 shorter events, 0.0 us)
Async XLA Ops:
  2.0 11.5 %collective-permute-start = (f32[62,8,128]{2,1,0:T(8,128)S(1)}, f32[62,8,128]{2,1,0:T(8,128)S(1)}, u32[]{:S(2)}, u32[]{:S(2)}) collective-permute-start(f32[62,8,128]{2,1,0:T(8,128)S(1)} %get-tuple-element.23), channel_id=1, source_target_pairs={{0,16},{4,8},{8,4},{12,28},{16,0},{20,24},{24,20},{28,12},{1,17},{... | collective-permute-start | bytes 761864 | tf_op jit(solution)/shard_map/ppermute | solution.py:46
  5.0 8.4 %collective-permute-start.1 = (f32[62,8,128]{2,1,0:T(8,128)S(1)}, f32[62,8,128]{2,1,0:T(8,128)S(1)}, u32[]{:S(2)}, u32[]{:S(2)}) collective-permute-start(f32[62,8,128]{2,1,0:T(8,128)S(1)} %get-tuple-element.24), channel_id=1, source_target_pairs={{0,4},{4,0},{8,12},{12,8},{16,20},{20,16},{24,28},{28,24},{1,5},{5... | collective-permute-start | bytes 761864 | tf_op jit(solution)/shard_map/ppermute | solution.py:46
  6.7 1.5 %collective-permute-start.2 = (f32[3,8,128]{2,1,0:T(8,128)S(1)}, f32[3,8,128]{2,1,0:T(8,128)S(1)}, u32[]{:S(2)}, u32[]{:S(2)}) collective-permute-start(f32[3,8,128]{2,1,0:T(8,128)S(1)} %get-tuple-element.27), channel_id=1, source_target_pairs={{0,1},{1,0},{2,3},{3,2},{16,17},{17,16},{18,19},{19,18},{4,5},{5,4... | collective-permute-start | bytes 36872 | tf_op jit(solution)/shard_map/ppermute | solution.py:46
  6.7 4.6 %collective-permute-start.3 = (f32[3,8,128]{2,1,0:T(8,128)S(1)}, f32[3,8,128]{2,1,0:T(8,128)S(1)}, u32[]{:S(2)}, u32[]{:S(2)}) collective-permute-start(f32[3,8,128]{2,1,0:T(8,128)S(1)} %get-tuple-element.28), channel_id=1, source_target_pairs={{0,16},{1,2},{2,1},{3,19},{16,0},{17,18},{18,17},{19,3},{4,20},{5,... | collective-permute-start | bytes 36872 | tf_op jit(solution)/shard_map/ppermute | solution.py:46
  11.3 6.4 %collective-permute-start.4 = (f32[6,8,128]{2,1,0:T(8,128)S(1)}, f32[6,8,128]{2,1,0:T(8,128)S(1)}, u32[]{:S(2)}, u32[]{:S(2)}) collective-permute-start(f32[6,8,128]{2,1,0:T(8,128)S(1)} %shard_map.87.columns), channel_id=1, source_target_pairs={{0,16},{4,8},{8,4},{12,28},{16,0},{20,24},{24,20},{28,12},{1,17},{... | collective-permute-start | bytes 73736 | tf_op jit(solution)/shard_map/ppermute | solution.py:46
  13.0 4.6 %collective-permute-start.5 = (f32[6,8,128]{2,1,0:T(8,128)S(1)}, f32[6,8,128]{2,1,0:T(8,128)S(1)}, u32[]{:S(2)}, u32[]{:S(2)}) collective-permute-start(f32[6,8,128]{2,1,0:T(8,128)S(1)} %shard_map.87.columns), channel_id=1, source_target_pairs={{0,4},{4,0},{8,12},{12,8},{16,20},{20,16},{24,28},{28,24},{1,5},{5... | collective-permute-start | bytes 73736 | tf_op jit(solution)/shard_map/ppermute | solution.py:46
  18.4 1.9 %collective-permute-start.6 = (f32[2,16,128]{2,1,0:T(8,128)S(1)}, f32[2,16,128]{2,1,0:T(8,128)S(1)}, u32[]{:S(2)}, u32[]{:S(2)}) collective-permute-start(f32[2,16,128]{2,1,0:T(8,128)S(1)} %get-tuple-element.32.refs_0_), channel_id=1, source_target_pairs={{0,1},{1,0},{2,3},{3,2},{4,5},{5,4},{6,7},{7,6},{8,9},{9,8},{10,11... | collective-permute-start | bytes 49160 | tf_op jit(solution)/shard_map/ppermute | solution.py:595
  18.5 3.8 %collective-permute-start.7 = (f32[2,16,128]{2,1,0:T(8,128)S(1)}, f32[2,16,128]{2,1,0:T(8,128)S(1)}, u32[]{:S(2)}, u32[]{:S(2)}) collective-permute-start(f32[2,16,128]{2,1,0:T(8,128)S(1)} %get-tuple-element.32.refs_0_), channel_id=1, source_target_pairs={{0,2},{1,3},{2,0},{3,1},{4,6},{5,7},{6,4},{7,5},{8,10},{9,11},{10,... | collective-permute-start | bytes 49160 | tf_op jit(solution)/shard_map/ppermute | solution.py:595
  19.5 3.2 %collective-permute-start.8 = (f32[2,16,128]{2,1,0:T(8,128)S(1)}, f32[2,16,128]{2,1,0:T(8,128)S(1)}, u32[]{:S(2)}, u32[]{:S(2)}) collective-permute-start(f32[2,16,128]{2,1,0:T(8,128)S(1)} %get-tuple-element.32.refs_0_), channel_id=1, source_target_pairs={{0,3},{1,2},{2,1},{3,0},{4,7},{5,6},{6,5},{7,4},{8,11},{9,10},{10,... | collective-permute-start | bytes 49160 | tf_op jit(solution)/shard_map/ppermute | solution.py:595
  22.7 5.5 %collective-permute-start.10 = (f32[2,16,128]{2,1,0:T(8,128)S(1)}, f32[2,16,128]{2,1,0:T(8,128)S(1)}, u32[]{:S(2)}, u32[]{:S(2)}) collective-permute-start(f32[2,16,128]{2,1,0:T(8,128)S(1)} %shard_map.89.rest_0_), channel_id=1, source_target_pairs={{0,8},{4,12},{8,0},{12,4},{1,9},{5,13},{9,1},{13,5},{2,10},{6,14},... | collective-permute-start | bytes 49160 | tf_op jit(solution)/shard_map/ppermute | solution.py:595
  26.4 5.5 %collective-permute-start.11 = (f32[2,16,128]{2,1,0:T(8,128)S(1)}, f32[2,16,128]{2,1,0:T(8,128)S(1)}, u32[]{:S(2)}, u32[]{:S(2)}) collective-permute-start(f32[2,16,128]{2,1,0:T(8,128)S(1)} %shard_map.89.rest_0_), channel_id=1, source_target_pairs={{0,12},{4,8},{8,4},{12,0},{1,13},{5,9},{9,5},{13,1},{2,14},{6,10},... | collective-permute-start | bytes 49160 | tf_op jit(solution)/shard_map/ppermute | solution.py:595
  26.5 5.4 %collective-permute-start.9 = (f32[2,16,128]{2,1,0:T(8,128)S(1)}, f32[2,16,128]{2,1,0:T(8,128)S(1)}, u32[]{:S(2)}, u32[]{:S(2)}) collective-permute-start(f32[2,16,128]{2,1,0:T(8,128)S(1)} %shard_map.89.rest_0_), channel_id=1, source_target_pairs={{0,4},{4,0},{8,12},{12,8},{1,5},{5,1},{9,13},{13,9},{2,6},{6,2},{1... | collective-permute-start | bytes 49160 | tf_op jit(solution)/shard_map/ppermute | solution.py:595

commit v15 on v14

--- a/solution.py
+++ b/solution.py
@@ -33,17 +33,22 @@
     return even, has_a, has_b
 
 
-def swapped(x, axes, first):
-    count, parts = lax.axis_size(axes), lax.axis_size("parts")
+def swapped(x, axes, first, spare=None):
+    count, others = lax.axis_size(axes), lax.axis_size(spare) if spare else 1
     pairs = []
-    for part in range(parts):
+    for at in range(others):
         for i in range(count):
-            other = i + 1 if (i - first) % 2 == 0 else i - 1
-            at = part
+            other, to = (i + 1 if (i - first) % 2 == 0 else i - 1), at
             if not 0 <= other < count:
-                other, at = i, part ^ 1 if part ^ 1 < parts else part
-            pairs.append((part * count + i, at * count + other))
-    return lax.ppermute(x, ("parts", *axes), pairs)
+                other, to = (i, at ^ 1) if spare else (count - 1 - i, at)
+                if to >= others or count % 2:
+                    other, to = i, at
+            if spare == "parts":
+                pairs.append((at * count + i, to * count + other))
+            else:
+                pairs.append((i * others + at, other * others + to))
+    names = axes if not spare else ("parts", *axes) if spare == "parts" else (*axes, spare)
+    return lax.ppermute(x, names, pairs)
 
 
 def own_planes(rhs, eta, friction, ice, grounded):
@@ -290,8 +295,8 @@
 
 def main_kernel(
     rhs, eta, friction, ice, grounded, strip_b, strip_a,
-    powers, sums, ribbon,
-    field_a, field_b, eta_row, eta_col, eta_half, eta_up, cover, drag,
+    power_1, power_2, power_3, power_4, sums, ribbon,
+    masked, eta_row, eta_col, eta_half, eta_up, cover, drag,
 ):
     layers = eta.shape[0]
     plane = own_planes(rhs, eta, friction, ice, grounded)
@@ -300,7 +305,7 @@
 
     def target(p):
         if p < 2 * layers:
-            return field_a.at[p // layers, p % layers]
+            return masked.at[p // layers, p % layers]
         if p < 3 * layers:
             return eta_half.at[p - 2 * layers]
         return cover if p == 3 * layers else drag
@@ -340,37 +345,36 @@
     eta_half[layers - 1] = 0.5 * eta_half[layers - 1]
 
     def apply(t, src, dst):
-        def layer(k, carry):
-            below0, below1, odd, even = carry
-            g0, g1 = load(src.at[0, k]), load(src.at[1, k])
-            after = jnp.minimum(k + 1, layers - 1)
-            e_up = load(eta_up.at[k])
-            up0 = e_up * (g0 - load(src.at[0, after]))
-            up1 = e_up * (g1 - load(src.at[1, after]))
-            out0, out1 = horizontal(g0, g1, load(eta_row.at[k]), load(eta_col.at[k]), load(eta_half.at[k]), moves)
+        def block(b, carry):
+            g0, g1, below0, below1, odd, even = carry
+            g0, g1, below0, below1 = Tiles(g0), Tiles(g1), Tiles(below0), Tiles(below1)
+            odd, even = list(odd), list(even)
             m = load(cover)
-            out0, out1 = m * (out0 + (up0 - Tiles(below0))), m * (out1 + (up1 - Tiles(below1)))
-            if t < STEPS:
-                out0.store(dst.at[0, k])
-                out1.store(dst.at[1, k])
-            odd, even = list(odd), list(even)
-            for c, g, out in ((0, g0, out0), (1, g1, out1)):
-                for half in range(2):
-                    now = out.tiles[half]
-                    powers[t - 1, c, k, :, half * LANES : (half + 1) * LANES] = now
-                    odd[half] = odd[half] + g.tiles[half] * now
-                    even[half] = even[half] + now * now
-            return up0.tiles, up1.tiles, odd, even
-
-        def block(b, carry):
             for i in range(UNROLL):
-                carry = layer(b * UNROLL + i, carry)
-            return carry
+                k = b * UNROLL + i
+                after = k + 1 if i + 1 < UNROLL else jnp.minimum(k + 1, layers - 1)
+                next0, next1 = load(src.at[0, after]), load(src.at[1, after])
+                e_up = load(eta_up.at[k])
+                up0, up1 = e_up * (g0 - next0), e_up * (g1 - next1)
+                out0, out1 = horizontal(g0, g1, load(eta_row.at[k]), load(eta_col.at[k]), load(eta_half.at[k]), moves)
+                out0, out1 = m * (out0 + (up0 - below0)), m * (out1 + (up1 - below1))
+                for c, g, out in ((0, g0, out0), (1, g1, out1)):
+                    if t < STEPS:
+                        out.store(dst.at[c, k])
+                    for half in range(2):
+                        now = out.tiles[half]
+                        if t == STEPS:
+                            dst[c, k, :, half * LANES : (half + 1) * LANES] = now
+                        odd[half] = odd[half] + g.tiles[half] * now
+                        even[half] = even[half] + now * now
+                g0, g1, below0, below1 = next0, next1, up0, up1
+            return g0.tiles, g1.tiles, below0.tiles, below1.tiles, odd, even
 
         zero = [jnp.zeros((ROWS, LANES), jnp.float32)] * 2
         d = -1.0 * load(drag)
-        start = ((d * load(src.at[0, 0])).tiles, (d * load(src.at[1, 0])).tiles, zero, zero)
-        ends = lax.fori_loop(0, layers // UNROLL, block, start)[2:]
+        g0, g1 = load(src.at[0, 0]), load(src.at[1, 0])
+        start = (g0.tiles, g1.tiles, (d * g0).tiles, (d * g1).tiles, zero, zero)
+        ends = lax.fori_loop(0, layers // UNROLL, block, start)[4:]
         return [jnp.concatenate(v, 1) for v in ends]
 
     bare = 1.0 - ice[...].astype(jnp.float32)
@@ -384,12 +388,11 @@
     sums[0] = whole
     wide = lax.broadcasted_iota(jnp.int32, (ROWS, 2 * LANES), 1)
     inner = between(wide, HALO, 2 * LANES - 2 * HALO)
-    src, dst = field_a, field_b
+    fields = (masked, power_1, power_2, power_3, power_4)
     for t in range(1, STEPS + 1):
-        odd, even = apply(t, src, dst)
+        odd, even = apply(t, fields[t - 1], fields[t])
         sums[2 * t - 1] = jnp.where(inner, odd, 0.0) + outside
         sums[2 * t] = jnp.where(inner, even, 0.0) + outside
-        src, dst = dst, src
 
 
 def ribbon_kernel(ribbon, columns, columns_b, columns_a, sums, edges, moments):
@@ -538,13 +541,14 @@
     return powers
 
 
-def final_kernel(rhs, powers, edges, friction, ice, grounded, speed, *rest):
+def final_kernel(rhs, power_1, power_2, power_3, power_4, edges, friction, ice, grounded, speed, *rest):
     *parts, iterate, residual, hessian = rest
     layers, tiles = rhs.shape[1], edges.shape[2]
     total = (parts[0][0], parts[0][1])
     for x in parts[1:]:
         total = join(total, (x[0], x[1]))
     factors = solve(total)
+    powers = (power_1, power_2, power_3, power_4)
     wide = [jnp.concatenate([c, c], 1) for c in factors]
     rest = sum(wide[1:], wide[0])
     cover = ice[...].astype(jnp.float32)
@@ -563,7 +567,7 @@
         side = [combined([edges[t, c, n] for t in range(STEPS)], factors) for n in range(tiles)]
         for k in range(layers):
             at = k // tiles * SLOT
-            inner = combined([powers[t, c, k] for t in range(STEPS)], wide)
+            inner = combined([p[c, k, :ROWS] for p in powers], wide)
             patched = []
             for v, e in zip(inner, side[k % tiles]):
                 head = jnp.where(lane < HALO, turned(e, -at - 20), v[:, :LANES])
@@ -613,15 +617,15 @@
         [pltpu.SemaphoreType.DMA((len(inputs),))],
         in_specs=[pl.BlockSpec(memory_space=pltpu.HBM)] * len(inputs),
     )(*[pltpu.with_memory_space_constraint(x, pltpu.HBM) for x in inputs])
-    strip_b, strip_a = swapped(strip_b, ("gx",), 1), swapped(strip_a, ("gx",), 0)
+    strip_b, strip_a = swapped(strip_b, ("gx",), 1, "parts"), swapped(strip_a, ("gx",), 0)
     beside = ("gy", "gz")
     (columns,) = call(beside_kernel, [both])(swapped(column_a, beside, 0), swapped(column_b, beside, 1))
-    columns_b, columns_a = swapped(columns, ("gx",), 1), swapped(columns, ("gx",), 0)
+    columns_b, columns_a = swapped(columns, ("gx",), 1, "gy"), swapped(columns, ("gx",), 0)
     block = (layers, 2 * ROWS, 2 * LANES)
-    powers, sums, ribbon = call(
+    *powers, sums, ribbon = call(
         main_kernel,
-        [(STEPS,) + adjoint_rhs.shape, (2 * STEPS + 1, ROWS, 2 * LANES), (ribbons, 2 * ROWS, LANES)],
-        [(2,) + block] * 2 + [block] * 4 + [block[1:]] * 2,
+        [(2,) + block] * (STEPS - 1) + [adjoint_rhs.shape, (2 * STEPS + 1, ROWS, 2 * LANES), (ribbons, 2 * ROWS, LANES)],
+        [(2,) + block] + [block] * 4 + [block[1:]] * 2,
         cost_estimate=pl.CostEstimate(flops=200_000_000, bytes_accessed=8_000_000, transcendentals=0),
     )(*held[:5], strip_b, strip_a)
     edges, sums = call(
@@ -635,7 +639,7 @@
     rhs, _, friction, ice_mask, grounded, speed = held
     return tuple(
         call(final_kernel, [adjoint_rhs.shape, adjoint_rhs.shape, friction.shape])(
-            rhs, powers, edges, friction, ice_mask, grounded, speed, *parts
+            rhs, *powers, edges, friction, ice_mask, grounded, speed, *parts
         )
     )
 

time: 33.9 us -> 32.4 us (0.956)
  waiting for transfers between devices: 10.3 us -> 8.1 us
  starting transfers between devices: 14.7 us -> 15.3 us
    ppermute x6, waiting for transfers between devices: 3.11 us -> 1.53 us  [swapped(): return lax.ppermute(x, names, pairs)]
    ppermute x6, starting transfers between devices: 8.35 us -> 9.37 us  [swapped(): return lax.ppermute(x, names, pairs)]
    ppermute x6, waiting for transfers between devices: 7.18 us -> 6.57 us  [exchange(): parts.append(lax.ppermute(x, axis, pairs))]
  transfers between devices with their start and end apart: 12 -> 12, of which waited for: 5 -> 5; matrix products, arithmetic and copies ran while one was open for 0% -> 0% of each run, Pallas kernels for 12% -> 13%
where the time goes in v15:
time: 32.4 us; the launch traced here: 32.2 us
  starting transfers between devices  15.3 us (47%)
  waiting for transfers between devices  8.1 us (25%)
  Pallas kernels  8.08 us (25%)
  between operations  0.68 us (2%)
    ppermute x6, starting transfers between devices, swapped(): return lax.ppermute(x, names, pairs)  9.37 us
    ppermute x6, waiting for transfers between devices, exchange(): parts.append(lax.ppermute(x, axis, pairs))  6.57 us
    ppermute x6, starting transfers between devices, exchange(): parts.append(lax.ppermute(x, axis, pairs))  5.97 us
    pallas_call x1, Pallas kernels, body(): call(main_kernel, [(2,) + block] * (STEPS - 1) + [adjoint_rhs.shape, (2 *...  4.15 us
    pallas_call x1, Pallas kernels, body(): call(final_kernel, [adjoint_rhs.shape, adjoint_rhs.shape, friction.shape])  1.81 us
    ppermute x6, waiting for transfers between devices, swapped(): return lax.ppermute(x, names, pairs)  1.53 us
    pallas_call x1, Pallas kernels, body(): call(pack_kernel, [jax.ShapeDtypeStruct(x.shape, x.dtype) for x in inputs...  1.35 us
    pallas_call x1, Pallas kernels, body(): call(ribbon_kernel, [(STEPS, 2, layers // 4) + tile, (2, 2 * ROWS, LANES)])  0.74 us
  transfers between devices with their start and end apart: 12, of which 5 were waited for; matrix products, arithmetic and copies ran while one was open for 0% of the time, Pallas kernels for 13%

profile of v15, /device:TPU:0, one launch (start us, length us, event | category | flops | bytes accessed | tf_op | source)
XLA Modules:
  0.0 32.2 jit_solution(10074944316491761778)
XLA Ops:
  0.6 1.3 %shard_map.85 = (f32[2,20,8,256]{3,2,1,0:T(8,128)S(1)}, f32[20,8,256]{2,1,0:T(8,128)S(1)}, f32[8,256]{1,0:T(8,128)S(1)}, s32[8,256]{1,0:T(8,128)S(1)}, s32[8,256...) custom-call(f32[2,20,8,256]{3,2,1,0:T(8,128)} %refs_0_.1, ...), custom_call_target="tpu_custom_call" | custom-call | tf_op jit(solution)/shard_map/pallas_call | solution.py:614
  2.0 3.0 %collective-permute-start = (f32[62,8,128]{2,1,0:T(8,128)S(1)}, f32[62,8,128]{2,1,0:T(8,128)S(1)}, u32[]{:S(2)}, u32[]{:S(2)}) collective-permute-start(f32[62,8,128]{2,1,0:T(8,128)S(1)} %get-tuple-element.26), channel_id=1, source_target_pairs={{0,16},{4,8},{8,4},{12,28},{16,0},{20,24},{24,20},{28,12},{1,17},{... | collective-permute-start | bytes 761864 | tf_op jit(solution)/shard_map/ppermute | solution.py:51
  5.0 1.6 %collective-permute-start.1 = (f32[62,8,128]{2,1,0:T(8,128)S(1)}, f32[62,8,128]{2,1,0:T(8,128)S(1)}, u32[]{:S(2)}, u32[]{:S(2)}) collective-permute-start(f32[62,8,128]{2,1,0:T(8,128)S(1)} %get-tuple-element.27), channel_id=1, source_target_pairs={{0,4},{4,0},{8,12},{12,8},{1,5},{5,1},{9,13},{13,9},{2,6},{6,2},{1... | collective-permute-start | bytes 761864 | tf_op jit(solution)/shard_map/ppermute | solution.py:51
  6.7 0.0 collective-permute-start.2
  6.7 1.6 %collective-permute-start.3 = (f32[3,8,128]{2,1,0:T(8,128)S(1)}, f32[3,8,128]{2,1,0:T(8,128)S(1)}, u32[]{:S(2)}, u32[]{:S(2)}) collective-permute-start(f32[3,8,128]{2,1,0:T(8,128)S(1)} %get-tuple-element.34), channel_id=1, source_target_pairs={{0,3},{1,2},{2,1},{3,0},{4,7},{5,6},{6,5},{7,4},{8,11},{9,10},{10,... | collective-permute-start | bytes 36872 | tf_op jit(solution)/shard_map/ppermute | solution.py:51
  8.3 1.5 %collective-permute-done.3.from_b = f32[3,8,128]{2,1,0:T(8,128)S(1)} collective-permute-done((f32[3,8,128]{2,1,0:T(8,128)S(1)}, f32[3,8,128]{2,1,0:T(8,128)S(1)}, u32[]{:S(2)}, u32[]{:S(2)}) %collective-permute-start.3) | collective-permute-done | bytes 12320 | tf_op jit(solution)/shard_map/ppermute | solution.py:51
  9.8 1.5 %collective-permute-start.4 = (f32[6,8,128]{2,1,0:T(8,128)S(1)}, f32[6,8,128]{2,1,0:T(8,128)S(1)}, u32[]{:S(2)}, u32[]{:S(2)}) collective-permute-start(f32[6,8,128]{2,1,0:T(8,128)S(1)} %shard_map.87.columns), channel_id=1, source_target_pairs={{0,2},{4,8},{8,4},{12,14},{2,0},{6,10},{10,6},{14,12},{1,3},{5,9},... | collective-permute-start | bytes 73736 | tf_op jit(solution)/shard_map/ppermute | solution.py:51
  11.3 1.6 %collective-permute-start.5 = (f32[6,8,128]{2,1,0:T(8,128)S(1)}, f32[6,8,128]{2,1,0:T(8,128)S(1)}, u32[]{:S(2)}, u32[]{:S(2)}) collective-permute-start(f32[6,8,128]{2,1,0:T(8,128)S(1)} %shard_map.87.columns), channel_id=1, source_target_pairs={{0,4},{4,0},{8,12},{12,8},{1,5},{5,1},{9,13},{13,9},{2,6},{6,2},{1... | collective-permute-start | bytes 73736 | tf_op jit(solution)/shard_map/ppermute | solution.py:51
  12.9 0.0 collective-permute-done.strip_b
  12.9 4.2 %shard_map.86 = (f32[2,20,16,256]{3,2,1,0:T(8,128)S(1)}, f32[2,20,16,256]{3,2,1,0:T(8,128)S(1)}, f32[2,20,16,256]{3,2,1,0:T(8,128)S(1)}, f32[2,20,8,256]{3,2,1,0...) custom-call(f32[2,20,8,256]{3,2,1,0:T(8,128)S(1)} %get-tuple-element.21.rhs, ...), custom_call_target="tpu_custom_call" | custom-call | flops 200000000 | bytes 8000000 | tf_op jit(solution)/shard_map/pallas_call | solution.py:625
  17.1 0.0 collective-permute-done.5.columns_a
  17.1 0.7 %shard_map.88 = (f32[4,2,5,8,128]{4,3,2,1,0:T(8,128)S(1)}, f32[2,16,128]{2,1,0:T(8,128)S(1)}) custom-call(f32[17,16,128]{2,1,0:T(8,128)S(1)} %get-tuple-element.32.ribbon, f32[6,8,128]{2,1,0:T(8,128)S(1)} %shard_map.87.columns, f32[6,8,128]{2,1,0:T(8,128)S(1)} %collective-permute-done.4.columns_b, f32[6,8,128]{2,1,0:T(8,128)S(1)} %collective-permute-done.5.columns_a, ...), custom_call_target="tpu_custom_call" | custom-call | tf_op jit(solution)/shard_map/pallas_call | solution.py:631
  17.8 0.3 collective-permute-start.6
  18.1 1.5 %collective-permute-start.7 = (f32[2,16,128]{2,1,0:T(8,128)S(1)}, f32[2,16,128]{2,1,0:T(8,128)S(1)}, u32[]{:S(2)}, u32[]{:S(2)}) collective-permute-start(f32[2,16,128]{2,1,0:T(8,128)S(1)} %get-tuple-element.38.refs_0_), channel_id=1, source_target_pairs={{0,2},{1,3},{2,0},{3,1},{4,6},{5,7},{6,4},{7,5},{8,10},{9,11},{10,... | collective-permute-start | bytes 49160 | tf_op jit(solution)/shard_map/ppermute | solution.py:599
  19.6 0.1 collective-permute-start.8
  19.7 0.0 collective-permute-done.6.refs_1_
  19.7 2.1 %collective-permute-done.7.refs_2_ = f32[2,16,128]{2,1,0:T(8,128)S(1)} collective-permute-done((f32[2,16,128]{2,1,0:T(8,128)S(1)}, f32[2,16,128]{2,1,0:T(8,128)S(1)}, u32[]{:S(2)}, u32[]{:S(2)}) %collective-permute-start.7) | collective-permute-done | bytes 16416 | tf_op jit(solution)/shard_map/ppermute | solution.py:599
  21.9 0.9 %collective-permute-done.8.refs_3_ = f32[2,16,128]{2,1,0:T(8,128)S(1)} collective-permute-done((f32[2,16,128]{2,1,0:T(8,128)S(1)}, f32[2,16,128]{2,1,0:T(8,128)S(1)}, u32[]{:S(2)}, u32[]{:S(2)}) %collective-permute-start.8) | collective-permute-done | bytes 16416 | tf_op jit(solution)/shard_map/ppermute | solution.py:599
  22.8 2.0 %collective-permute-start.10 = (f32[2,16,128]{2,1,0:T(8,128)S(1)}, f32[2,16,128]{2,1,0:T(8,128)S(1)}, u32[]{:S(2)}, u32[]{:S(2)}) collective-permute-start(f32[2,16,128]{2,1,0:T(8,128)S(1)} %shard_map.89.rest_0_), channel_id=1, source_target_pairs={{0,8},{4,12},{8,0},{12,4},{1,9},{5,13},{9,1},{13,5},{2,10},{6,14},... | collective-permute-start | bytes 49160 | tf_op jit(solution)/shard_map/ppermute | solution.py:599
  24.9 1.6 %collective-permute-start.11 = (f32[2,16,128]{2,1,0:T(8,128)S(1)}, f32[2,16,128]{2,1,0:T(8,128)S(1)}, u32[]{:S(2)}, u32[]{:S(2)}) collective-permute-start(f32[2,16,128]{2,1,0:T(8,128)S(1)} %shard_map.89.rest_0_), channel_id=1, source_target_pairs={{0,12},{4,8},{8,4},{12,0},{1,13},{5,9},{9,5},{13,1},{2,14},{6,10},... | collective-permute-start | bytes 49160 | tf_op jit(solution)/shard_map/ppermute | solution.py:599
  26.4 0.4 %collective-permute-start.9 = (f32[2,16,128]{2,1,0:T(8,128)S(1)}, f32[2,16,128]{2,1,0:T(8,128)S(1)}, u32[]{:S(2)}, u32[]{:S(2)}) collective-permute-start(f32[2,16,128]{2,1,0:T(8,128)S(1)} %shard_map.89.rest_0_), channel_id=1, source_target_pairs={{0,4},{4,0},{8,12},{12,8},{1,5},{5,1},{9,13},{13,9},{2,6},{6,2},{1... | collective-permute-start | bytes 49160 | tf_op jit(solution)/shard_map/ppermute | solution.py:599
  26.9 0.8 %collective-permute-done.10.rest_2_ = f32[2,16,128]{2,1,0:T(8,128)S(1)} collective-permute-done((f32[2,16,128]{2,1,0:T(8,128)S(1)}, f32[2,16,128]{2,1,0:T(8,128)S(1)}, u32[]{:S(2)}, u32[]{:S(2)}) %collective-permute-start.10) | collective-permute-done | bytes 16416 | tf_op jit(solution)/shard_map/ppermute | solution.py:599
  27.7 2.7 %collective-permute-done.11.rest_3_ = f32[2,16,128]{2,1,0:T(8,128)S(1)} collective-permute-done((f32[2,16,128]{2,1,0:T(8,128)S(1)}, f32[2,16,128]{2,1,0:T(8,128)S(1)}, u32[]{:S(2)}, u32[]{:S(2)}) %collective-permute-start.11) | collective-permute-done | bytes 16416 | tf_op jit(solution)/shard_map/ppermute | solution.py:599
  30.4 1.8 %shard_map.90 = (f32[2,20,8,256]{3,2,1,0:T(8,128)}, f32[2,20,8,256]{3,2,1,0:T(8,128)}, f32[8,256]{1,0:T(8,128)}) custom-call(f32[2,20,8,256]{3,2,1,0:T(8,128)S(1)} %get-tuple-element.21.rhs, f32[2,20,16,256]{3,2,1,0:T(8,128)S(1)} %get-tuple-element.28.power_1, f32[2,20,16,256]{3,2,1,0:T(8,128)S(1)} %get-tuple-element.29.power_2, ...), custom_call_target="tpu_custom_call" | custom-call | tf_op jit(solution)/shard_map/pallas_call | solution.py:641
  (6 shorter events, 0.0 us)
Async XLA Ops:
  2.0 10.9 %collective-permute-start = (f32[62,8,128]{2,1,0:T(8,128)S(1)}, f32[62,8,128]{2,1,0:T(8,128)S(1)}, u32[]{:S(2)}, u32[]{:S(2)}) collective-permute-start(f32[62,8,128]{2,1,0:T(8,128)S(1)} %get-tuple-element.26), channel_id=1, source_target_pairs={{0,16},{4,8},{8,4},{12,28},{16,0},{20,24},{24,20},{28,12},{1,17},{... | collective-permute-start | bytes 761864 | tf_op jit(solution)/shard_map/ppermute | solution.py:51
  5.0 7.9 %collective-permute-start.1 = (f32[62,8,128]{2,1,0:T(8,128)S(1)}, f32[62,8,128]{2,1,0:T(8,128)S(1)}, u32[]{:S(2)}, u32[]{:S(2)}) collective-permute-start(f32[62,8,128]{2,1,0:T(8,128)S(1)} %get-tuple-element.27), channel_id=1, source_target_pairs={{0,4},{4,0},{8,12},{12,8},{1,5},{5,1},{9,13},{13,9},{2,6},{6,2},{1... | collective-permute-start | bytes 761864 | tf_op jit(solution)/shard_map/ppermute | solution.py:51
  6.7 1.6 %collective-permute-start.2 = (f32[3,8,128]{2,1,0:T(8,128)S(1)}, f32[3,8,128]{2,1,0:T(8,128)S(1)}, u32[]{:S(2)}, u32[]{:S(2)}) collective-permute-start(f32[3,8,128]{2,1,0:T(8,128)S(1)} %get-tuple-element.33), channel_id=1, source_target_pairs={{0,1},{1,0},{2,3},{3,2},{4,5},{5,4},{6,7},{7,6},{8,9},{9,8},{10,11... | collective-permute-start | bytes 36872 | tf_op jit(solution)/shard_map/ppermute | solution.py:51
  6.7 3.1 %collective-permute-start.3 = (f32[3,8,128]{2,1,0:T(8,128)S(1)}, f32[3,8,128]{2,1,0:T(8,128)S(1)}, u32[]{:S(2)}, u32[]{:S(2)}) collective-permute-start(f32[3,8,128]{2,1,0:T(8,128)S(1)} %get-tuple-element.34), channel_id=1, source_target_pairs={{0,3},{1,2},{2,1},{3,0},{4,7},{5,6},{6,5},{7,4},{8,11},{9,10},{10,... | collective-permute-start | bytes 36872 | tf_op jit(solution)/shard_map/ppermute | solution.py:51
  9.8 7.3 %collective-permute-start.4 = (f32[6,8,128]{2,1,0:T(8,128)S(1)}, f32[6,8,128]{2,1,0:T(8,128)S(1)}, u32[]{:S(2)}, u32[]{:S(2)}) collective-permute-start(f32[6,8,128]{2,1,0:T(8,128)S(1)} %shard_map.87.columns), channel_id=1, source_target_pairs={{0,2},{4,8},{8,4},{12,14},{2,0},{6,10},{10,6},{14,12},{1,3},{5,9},... | collective-permute-start | bytes 73736 | tf_op jit(solution)/shard_map/ppermute | solution.py:51
  11.3 5.8 %collective-permute-start.5 = (f32[6,8,128]{2,1,0:T(8,128)S(1)}, f32[6,8,128]{2,1,0:T(8,128)S(1)}, u32[]{:S(2)}, u32[]{:S(2)}) collective-permute-start(f32[6,8,128]{2,1,0:T(8,128)S(1)} %shard_map.87.columns), channel_id=1, source_target_pairs={{0,4},{4,0},{8,12},{12,8},{1,5},{5,1},{9,13},{13,9},{2,6},{6,2},{1... | collective-permute-start | bytes 73736 | tf_op jit(solution)/shard_map/ppermute | solution.py:51
  17.8 1.9 %collective-permute-start.6 = (f32[2,16,128]{2,1,0:T(8,128)S(1)}, f32[2,16,128]{2,1,0:T(8,128)S(1)}, u32[]{:S(2)}, u32[]{:S(2)}) collective-permute-start(f32[2,16,128]{2,1,0:T(8,128)S(1)} %get-tuple-element.38.refs_0_), channel_id=1, source_target_pairs={{0,1},{1,0},{2,3},{3,2},{4,5},{5,4},{6,7},{7,6},{8,9},{9,8},{10,11... | collective-permute-start | bytes 49160 | tf_op jit(solution)/shard_map/ppermute | solution.py:599
  18.1 3.7 %collective-permute-start.7 = (f32[2,16,128]{2,1,0:T(8,128)S(1)}, f32[2,16,128]{2,1,0:T(8,128)S(1)}, u32[]{:S(2)}, u32[]{:S(2)}) collective-permute-start(f32[2,16,128]{2,1,0:T(8,128)S(1)} %get-tuple-element.38.refs_0_), channel_id=1, source_target_pairs={{0,2},{1,3},{2,0},{3,1},{4,6},{5,7},{6,4},{7,5},{8,10},{9,11},{10,... | collective-permute-start | bytes 49160 | tf_op jit(solution)/shard_map/ppermute | solution.py:599
  19.6 3.2 %collective-permute-start.8 = (f32[2,16,128]{2,1,0:T(8,128)S(1)}, f32[2,16,128]{2,1,0:T(8,128)S(1)}, u32[]{:S(2)}, u32[]{:S(2)}) collective-permute-start(f32[2,16,128]{2,1,0:T(8,128)S(1)} %get-tuple-element.38.refs_0_), channel_id=1, source_target_pairs={{0,3},{1,2},{2,1},{3,0},{4,7},{5,6},{6,5},{7,4},{8,11},{9,10},{10,... | collective-permute-start | bytes 49160 | tf_op jit(solution)/shard_map/ppermute | solution.py:599
  22.8 4.9 %collective-permute-start.10 = (f32[2,16,128]{2,1,0:T(8,128)S(1)}, f32[2,16,128]{2,1,0:T(8,128)S(1)}, u32[]{:S(2)}, u32[]{:S(2)}) collective-permute-start(f32[2,16,128]{2,1,0:T(8,128)S(1)} %shard_map.89.rest_0_), channel_id=1, source_target_pairs={{0,8},{4,12},{8,0},{12,4},{1,9},{5,13},{9,1},{13,5},{2,10},{6,14},... | collective-permute-start | bytes 49160 | tf_op jit(solution)/shard_map/ppermute | solution.py:599
  24.9 5.5 %collective-permute-start.11 = (f32[2,16,128]{2,1,0:T(8,128)S(1)}, f32[2,16,128]{2,1,0:T(8,128)S(1)}, u32[]{:S(2)}, u32[]{:S(2)}) collective-permute-start(f32[2,16,128]{2,1,0:T(8,128)S(1)} %shard_map.89.rest_0_), channel_id=1, source_target_pairs={{0,12},{4,8},{8,4},{12,0},{1,13},{5,9},{9,5},{13,1},{2,14},{6,10},... | collective-permute-start | bytes 49160 | tf_op jit(solution)/shard_map/ppermute | solution.py:599
  26.4 4.0 %collective-permute-start.9 = (f32[2,16,128]{2,1,0:T(8,128)S(1)}, f32[2,16,128]{2,1,0:T(8,128)S(1)}, u32[]{:S(2)}, u32[]{:S(2)}) collective-permute-start(f32[2,16,128]{2,1,0:T(8,128)S(1)} %shard_map.89.rest_0_), channel_id=1, source_target_pairs={{0,4},{4,0},{8,12},{12,8},{1,5},{5,1},{9,13},{13,9},{2,6},{6,2},{1... | collective-permute-start | bytes 49160 | tf_op jit(solution)/shard_map/ppermute | solution.py:599

commit v16 on v15

--- a/solution.py
+++ b/solution.py
@@ -12,6 +12,7 @@
 ROWS = 8
 LANES = 128
 UNROLL = 5
+FIRST = 4
 SLOT = 32
 
 
@@ -213,12 +214,20 @@
         self.tiles = tiles
 
     @staticmethod
-    def load(ref):
-        return Tiles([ref[r : r + ROWS, c : c + LANES] for r in (0, ROWS) for c in (0, LANES)])
-
-    def store(self, ref):
-        for v, (r, c) in zip(self.tiles, ((0, 0), (0, LANES), (ROWS, 0), (ROWS, LANES))):
-            ref[r : r + ROWS, c : c + LANES] = v
+    def load(ref, *place):
+        return Tiles([ref[(half, *place, pl.ds(r, ROWS))] for r in (0, ROWS) for half in (0, 1)])
+
+    def store(self, ref, *place):
+        for i, v in enumerate(self.tiles):
+            ref[(i % 2, *place, pl.ds(i // 2 * ROWS, ROWS))] = v
+
+    @staticmethod
+    def gather(ref, *place):
+        return Tiles([ref[(half, *place, pl.ds(FIRST + r, ROWS, stride=2))] for r in (0, 1) for half in (0, 1)])
+
+    def spread(self, ref, *place):
+        for i, v in enumerate(self.tiles):
+            ref[(i % 2, *place, pl.ds(FIRST + i // 2, ROWS, stride=2))] = v
 
     def both(self, other, op):
         if isinstance(other, Tiles):
@@ -239,27 +248,16 @@
 
 class Moves:
     def __init__(self):
-        row = lax.broadcasted_iota(jnp.int32, (ROWS, LANES), 0)
         lane = lax.broadcasted_iota(jnp.int32, (ROWS, LANES), 1)
-        self.first_row, self.last_row = row == 0, row == ROWS - 1
         self.first_lane, self.last_lane = lane == 0, lane == LANES - 1
 
-    def rows(self, v, shift, edge):
-        own0, own1, halo0, halo1 = [pltpu.roll(x, shift, 0) for x in v.tiles]
-        return Tiles(
-            [
-                jnp.where(edge, halo0, own0),
-                jnp.where(edge, halo1, own1),
-                jnp.where(edge, own0, halo0),
-                jnp.where(edge, own1, halo1),
-            ]
-        )
-
     def row_next(self, v):
-        return self.rows(v, ROWS - 1, self.last_row)
+        even0, even1, odd0, odd1 = v.tiles
+        return Tiles([odd0, odd1, pltpu.roll(even0, ROWS - 1, 0), pltpu.roll(even1, ROWS - 1, 0)])
 
     def row_prev(self, v):
-        return self.rows(v, 1, self.first_row)
+        even0, even1, odd0, odd1 = v.tiles
+        return Tiles([pltpu.roll(odd0, 1, 0), pltpu.roll(odd1, 1, 0), even0, even1])
 
     def col_next(self, v):
         own0, own1, halo0, halo1 = [pltpu.roll(x, LANES - 1, 1) for x in v.tiles]
@@ -296,19 +294,12 @@
 def main_kernel(
     rhs, eta, friction, ice, grounded, strip_b, strip_a,
     power_1, power_2, power_3, power_4, sums, ribbon,
-    masked, eta_row, eta_col, eta_half, eta_up, cover, drag,
+    rows, field_a, field_b, eta_row, eta_col, eta_half, eta_up, cover,
 ):
     layers = eta.shape[0]
     plane = own_planes(rhs, eta, friction, ice, grounded)
     below_and_above, above_and_below = beyond()
     lane = lax.broadcasted_iota(jnp.int32, (2 * ROWS, LANES), 1)
-
-    def target(p):
-        if p < 2 * layers:
-            return masked.at[p // layers, p % layers]
-        if p < 3 * layers:
-            return eta_half.at[p - 2 * layers]
-        return cover if p == 3 * layers else drag
 
     strips = [jnp.zeros((2 * ROWS, LANES), jnp.float32) for _ in range(ribbon.shape[0])]
     for q in range(strip_a.shape[0] // 2):
@@ -320,9 +311,10 @@
             halves[1].append(pltpu.roll(above_and_below(from_a, from_b), HALO, 0))
         for p, halo in zip((first, second), halves):
             v = plane(p)
-            dst = target(p)
-            dst[0:ROWS, :] = v
-            dst[ROWS:, 0:LANES], dst[ROWS:, LANES:] = halo
+            for half in range(2):
+                rows[half, p, FIRST + HALO : FIRST + HALO + ROWS] = v[:, half * LANES : (half + 1) * LANES]
+                rows[half, p, FIRST : FIRST + HALO] = halo[half][HALO:]
+                rows[half, p, FIRST + HALO + ROWS : FIRST + 2 * ROWS] = halo[half][:HALO]
             head = jnp.concatenate([v[:, :LANES], halo[0]], 0)
             tail = jnp.concatenate([v[:, LANES:], halo[1]], 0)
             tile, slots = ribbon_places(p, layers)
@@ -335,47 +327,50 @@
 
     moves = Moves()
     load = Tiles.load
+    before = None
     for k in range(layers):
-        e = load(eta_half.at[k])
-        (2.0 * (e + moves.row_next(e))).store(eta_row.at[k])
-        (0.5 * (e + moves.col_next(e))).store(eta_col.at[k])
-        eta_up[k] = eta_half[k] + eta_half[k + 1] if k + 1 < layers else jnp.zeros_like(eta_up[k])
+        for c in range(2):
+            Tiles.gather(rows, c * layers + k).store(field_a, c, k)
+        e = Tiles.gather(rows, 2 * layers + k)
+        (2.0 * (e + moves.row_next(e))).store(eta_row, k)
+        (0.5 * (e + moves.col_next(e))).store(eta_col, k)
+        (0.5 * e).store(eta_half, k)
         if k:
-            eta_half[k - 1] = 0.5 * eta_half[k - 1]
-    eta_half[layers - 1] = 0.5 * eta_half[layers - 1]
-
-    def apply(t, src, dst):
+            (before + e).store(eta_up, k - 1)
+        before = e
+    (0.0 * before).store(eta_up, layers - 1)
+    Tiles.gather(rows, 3 * layers).store(cover)
+    drag = Tiles.gather(rows, 3 * layers + 1)
+
+    def apply(src, dst, power):
         def block(b, carry):
-            g0, g1, below0, below1, odd, even = carry
-            g0, g1, below0, below1 = Tiles(g0), Tiles(g1), Tiles(below0), Tiles(below1)
-            odd, even = list(odd), list(even)
+            g0, g1, below0, below1, odd, even = [Tiles(v) for v in carry]
             m = load(cover)
             for i in range(UNROLL):
                 k = b * UNROLL + i
                 after = k + 1 if i + 1 < UNROLL else jnp.minimum(k + 1, layers - 1)
-                next0, next1 = load(src.at[0, after]), load(src.at[1, after])
-                e_up = load(eta_up.at[k])
+                next0, next1 = load(src, 0, after), load(src, 1, after)
+                e_up = load(eta_up, k)
                 up0, up1 = e_up * (g0 - next0), e_up * (g1 - next1)
-                out0, out1 = horizontal(g0, g1, load(eta_row.at[k]), load(eta_col.at[k]), load(eta_half.at[k]), moves)
+                out0, out1 = horizontal(g0, g1, load(eta_row, k), load(eta_col, k), load(eta_half, k), moves)
                 out0, out1 = m * (out0 + (up0 - below0)), m * (out1 + (up1 - below1))
-                for c, g, out in ((0, g0, out0), (1, g1, out1)):
-                    if t < STEPS:
-                        out.store(dst.at[c, k])
-                    for half in range(2):
-                        now = out.tiles[half]
-                        if t == STEPS:
-                            dst[c, k, :, half * LANES : (half + 1) * LANES] = now
-                        odd[half] = odd[half] + g.tiles[half] * now
-                        even[half] = even[half] + now * now
+                for c, out in ((0, out0), (1, out1)):
+                    if dst is not None:
+                        out.store(dst, c, k)
+                    out.spread(power, c, k)
+                odd = odd + (g0 * out0 + g1 * out1)
+                even = even + (out0 * out0 + out1 * out1)
                 g0, g1, below0, below1 = next0, next1, up0, up1
-            return g0.tiles, g1.tiles, below0.tiles, below1.tiles, odd, even
-
-        zero = [jnp.zeros((ROWS, LANES), jnp.float32)] * 2
-        d = -1.0 * load(drag)
-        g0, g1 = load(src.at[0, 0]), load(src.at[1, 0])
-        start = (g0.tiles, g1.tiles, (d * g0).tiles, (d * g1).tiles, zero, zero)
+            return [v.tiles for v in (g0, g1, below0, below1, odd, even)]
+
+        zero = [jnp.zeros((ROWS, LANES), jnp.float32)] * 4
+        g0, g1 = load(src, 0, 0), load(src, 1, 0)
+        start = [g0.tiles, g1.tiles, (-1.0 * drag * g0).tiles, (-1.0 * drag * g1).tiles, zero, zero]
         ends = lax.fori_loop(0, layers // UNROLL, block, start)[4:]
-        return [jnp.concatenate(v, 1) for v in ends]
+        mine = between(lax.broadcasted_iota(jnp.int32, (ROWS, LANES), 0), HALO // 2, ROWS // 2)
+        return [
+            jnp.concatenate([jnp.where(mine, v[i], 0.0) + jnp.where(mine, v[2 + i], 0.0) for i in (0, 1)], 1) for v in ends
+        ]
 
     bare = 1.0 - ice[...].astype(jnp.float32)
     whole = jnp.zeros((ROWS, 2 * LANES), jnp.float32)
@@ -388,9 +383,9 @@
     sums[0] = whole
     wide = lax.broadcasted_iota(jnp.int32, (ROWS, 2 * LANES), 1)
     inner = between(wide, HALO, 2 * LANES - 2 * HALO)
-    fields = (masked, power_1, power_2, power_3, power_4)
-    for t in range(1, STEPS + 1):
-        odd, even = apply(t, fields[t - 1], fields[t])
+    fields = (field_a, field_b, field_a, field_b, None)
+    for t, power in enumerate((power_1, power_2, power_3, power_4), 1):
+        odd, even = apply(fields[t - 1], fields[t], power)
         sums[2 * t - 1] = jnp.where(inner, odd, 0.0) + outside
         sums[2 * t] = jnp.where(inner, even, 0.0) + outside
 
@@ -567,11 +562,15 @@
         side = [combined([edges[t, c, n] for t in range(STEPS)], factors) for n in range(tiles)]
         for k in range(layers):
             at = k // tiles * SLOT
-            inner = combined([p[c, k, :ROWS] for p in powers], wide)
+            halves = [
+                combined([p[half, c, k, FIRST + HALO : FIRST + HALO + ROWS] for p in powers], factors)
+                for half in (0, 1)
+            ]
+            inner = zip(*halves)
             patched = []
-            for v, e in zip(inner, side[k % tiles]):
-                head = jnp.where(lane < HALO, turned(e, -at - 20), v[:, :LANES])
-                tail = jnp.where(lane >= LANES - HALO, turned(e, 120 - at), v[:, LANES:])
+            for (head, tail), e in zip(inner, side[k % tiles]):
+                head = jnp.where(lane < HALO, turned(e, -at - 20), head)
+                tail = jnp.where(lane >= LANES - HALO, turned(e, 120 - at), tail)
                 patched.append(jnp.concatenate([head, tail], 1))
             r = rhs[c, k]
             x, y = patched
@@ -621,11 +620,12 @@
     beside = ("gy", "gz")
     (columns,) = call(beside_kernel, [both])(swapped(column_a, beside, 0), swapped(column_b, beside, 1))
     columns_b, columns_a = swapped(columns, ("gx",), 1, "gy"), swapped(columns, ("gx",), 0)
-    block = (layers, 2 * ROWS, 2 * LANES)
+    block = (layers, 2 * ROWS, LANES)
+    inorder = (2, 2, layers, 3 * ROWS, LANES)
     *powers, sums, ribbon = call(
         main_kernel,
-        [(2,) + block] * (STEPS - 1) + [adjoint_rhs.shape, (2 * STEPS + 1, ROWS, 2 * LANES), (ribbons, 2 * ROWS, LANES)],
-        [(2,) + block] + [block] * 4 + [block[1:]] * 2,
+        [inorder] * STEPS + [(2 * STEPS + 1, ROWS, 2 * LANES), (ribbons, 2 * ROWS, LANES)],
+        [(2, 3 * layers + 2, 3 * ROWS, LANES)] + [(2, 2) + block] * 2 + [(2,) + block] * 4 + [(2,) + block[1:]],
         cost_estimate=pl.CostEstimate(flops=200_000_000, bytes_accessed=8_000_000, transcendentals=0),
     )(*held[:5], strip_b, strip_a)
     edges, sums = call(

time: 32.4 us -> 32.8 us (1.012)
  Pallas kernels: 8.08 us -> 8.51 us
    pallas_call x1, Pallas kernels: 4.15 us -> 4.56 us  [body(): call(main_kernel, [inorder] * STEPS + [(2 * STEPS + 1, ROWS, 2 * LANES),...]
  transfers between devices with their start and end apart: 12 -> 12, of which waited for: 5 -> 5; matrix products, arithmetic and copies ran while one was open for 0% -> 0% of each run, Pallas kernels for 13% -> 14%
where the time goes in v16:
time: 32.8 us; the launch traced here: 32.6 us
  starting transfers between devices  15.3 us (47%)
  Pallas kernels  8.51 us (26%)
  waiting for transfers between devices  8.1 us (25%)
  between operations  0.68 us (2%)
    ppermute x6, starting transfers between devices, swapped(): return lax.ppermute(x, names, pairs)  9.37 us
    ppermute x6, waiting for transfers between devices, exchange(): parts.append(lax.ppermute(x, axis, pairs))  6.57 us
    ppermute x6, starting transfers between devices, exchange(): parts.append(lax.ppermute(x, axis, pairs))  5.97 us
    pallas_call x1, Pallas kernels, body(): call(main_kernel, [inorder] * STEPS + [(2 * STEPS + 1, ROWS, 2 * LANES),...  4.56 us
    pallas_call x1, Pallas kernels, body(): call(final_kernel, [adjoint_rhs.shape, adjoint_rhs.shape, friction.shape])  1.82 us
    ppermute x6, waiting for transfers between devices, swapped(): return lax.ppermute(x, names, pairs)  1.53 us
    pallas_call x1, Pallas kernels, body(): call(pack_kernel, [jax.ShapeDtypeStruct(x.shape, x.dtype) for x in inputs...  1.35 us
    pallas_call x1, Pallas kernels, body(): call(ribbon_kernel, [(STEPS, 2, layers // 4) + tile, (2, 2 * ROWS, LANES)])  0.74 us
  transfers between devices with their start and end apart: 12, of which 5 were waited for; matrix products, arithmetic and copies ran while one was open for 0% of the time, Pallas kernels for 14%

profile of v16, /device:TPU:0, one launch (start us, length us, event | category | flops | bytes accessed | tf_op | source)
XLA Modules:
  0.0 32.6 jit_solution(12951352263931048499)
XLA Ops:
  0.6 1.3 %shard_map.85 = (f32[2,20,8,256]{3,2,1,0:T(8,128)S(1)}, f32[20,8,256]{2,1,0:T(8,128)S(1)}, f32[8,256]{1,0:T(8,128)S(1)}, s32[8,256]{1,0:T(8,128)S(1)}, s32[8,256...) custom-call(f32[2,20,8,256]{3,2,1,0:T(8,128)} %refs_0_.1, ...), custom_call_target="tpu_custom_call" | custom-call | tf_op jit(solution)/shard_map/pallas_call | solution.py:613
  2.0 3.0 %collective-permute-start = (f32[62,8,128]{2,1,0:T(8,128)S(1)}, f32[62,8,128]{2,1,0:T(8,128)S(1)}, u32[]{:S(2)}, u32[]{:S(2)}) collective-permute-start(f32[62,8,128]{2,1,0:T(8,128)S(1)} %get-tuple-element.26), channel_id=1, source_target_pairs={{0,16},{4,8},{8,4},{12,28},{16,0},{20,24},{24,20},{28,12},{1,17},{... | collective-permute-start | bytes 761864 | tf_op jit(solution)/shard_map/ppermute | solution.py:52
  5.0 1.6 %collective-permute-start.1 = (f32[62,8,128]{2,1,0:T(8,128)S(1)}, f32[62,8,128]{2,1,0:T(8,128)S(1)}, u32[]{:S(2)}, u32[]{:S(2)}) collective-permute-start(f32[62,8,128]{2,1,0:T(8,128)S(1)} %get-tuple-element.27), channel_id=1, source_target_pairs={{0,4},{4,0},{8,12},{12,8},{1,5},{5,1},{9,13},{13,9},{2,6},{6,2},{1... | collective-permute-start | bytes 761864 | tf_op jit(solution)/shard_map/ppermute | solution.py:52
  6.7 0.0 collective-permute-start.2
  6.7 1.6 %collective-permute-start.3 = (f32[3,8,128]{2,1,0:T(8,128)S(1)}, f32[3,8,128]{2,1,0:T(8,128)S(1)}, u32[]{:S(2)}, u32[]{:S(2)}) collective-permute-start(f32[3,8,128]{2,1,0:T(8,128)S(1)} %get-tuple-element.34), channel_id=1, source_target_pairs={{0,3},{1,2},{2,1},{3,0},{4,7},{5,6},{6,5},{7,4},{8,11},{9,10},{10,... | collective-permute-start | bytes 36872 | tf_op jit(solution)/shard_map/ppermute | solution.py:52
  8.3 1.5 %collective-permute-done.3.from_b = f32[3,8,128]{2,1,0:T(8,128)S(1)} collective-permute-done((f32[3,8,128]{2,1,0:T(8,128)S(1)}, f32[3,8,128]{2,1,0:T(8,128)S(1)}, u32[]{:S(2)}, u32[]{:S(2)}) %collective-permute-start.3) | collective-permute-done | bytes 12320 | tf_op jit(solution)/shard_map/ppermute | solution.py:52
  9.8 1.5 %collective-permute-start.4 = (f32[6,8,128]{2,1,0:T(8,128)S(1)}, f32[6,8,128]{2,1,0:T(8,128)S(1)}, u32[]{:S(2)}, u32[]{:S(2)}) collective-permute-start(f32[6,8,128]{2,1,0:T(8,128)S(1)} %shard_map.87.columns), channel_id=1, source_target_pairs={{0,2},{4,8},{8,4},{12,14},{2,0},{6,10},{10,6},{14,12},{1,3},{5,9},... | collective-permute-start | bytes 73736 | tf_op jit(solution)/shard_map/ppermute | solution.py:52
  11.3 1.6 %collective-permute-start.5 = (f32[6,8,128]{2,1,0:T(8,128)S(1)}, f32[6,8,128]{2,1,0:T(8,128)S(1)}, u32[]{:S(2)}, u32[]{:S(2)}) collective-permute-start(f32[6,8,128]{2,1,0:T(8,128)S(1)} %shard_map.87.columns), channel_id=1, source_target_pairs={{0,4},{4,0},{8,12},{12,8},{1,5},{5,1},{9,13},{13,9},{2,6},{6,2},{1... | collective-permute-start | bytes 73736 | tf_op jit(solution)/shard_map/ppermute | solution.py:52
  12.9 0.0 collective-permute-done.strip_b
  12.9 4.6 %shard_map.86 = (f32[2,2,20,24,128]{4,3,2,1,0:T(8,128)S(1)}, f32[2,2,20,24,128]{4,3,2,1,0:T(8,128)S(1)}, f32[2,2,20,24,128]{4,3,2,1,0:T(8,128)S(1)}, f32[2,2,20,...) custom-call(f32[2,20,8,256]{3,2,1,0:T(8,128)S(1)} %get-tuple-element.21.rhs, ...), custom_call_target="tpu_custom_call" | custom-call | flops 200000000 | bytes 8000000 | tf_op jit(solution)/shard_map/pallas_call | solution.py:625
  17.5 0.0 collective-permute-done.4.columns_b
  17.5 0.7 %shard_map.88 = (f32[4,2,5,8,128]{4,3,2,1,0:T(8,128)S(1)}, f32[2,16,128]{2,1,0:T(8,128)S(1)}) custom-call(f32[17,16,128]{2,1,0:T(8,128)S(1)} %get-tuple-element.32.ribbon, f32[6,8,128]{2,1,0:T(8,128)S(1)} %shard_map.87.columns, f32[6,8,128]{2,1,0:T(8,128)S(1)} %collective-permute-done.4.columns_b, f32[6,8,128]{2,1,0:T(8,128)S(1)} %collective-permute-done.5.columns_a, ...), custom_call_target="tpu_custom_call" | custom-call | tf_op jit(solution)/shard_map/pallas_call | solution.py:631
  18.2 0.3 collective-permute-start.6
  18.5 1.5 %collective-permute-start.7 = (f32[2,16,128]{2,1,0:T(8,128)S(1)}, f32[2,16,128]{2,1,0:T(8,128)S(1)}, u32[]{:S(2)}, u32[]{:S(2)}) collective-permute-start(f32[2,16,128]{2,1,0:T(8,128)S(1)} %get-tuple-element.38.refs_0_), channel_id=1, source_target_pairs={{0,2},{1,3},{2,0},{3,1},{4,6},{5,7},{6,4},{7,5},{8,10},{9,11},{10,... | collective-permute-start | bytes 49160 | tf_op jit(solution)/shard_map/ppermute | solution.py:598
  20.0 0.1 collective-permute-start.8
  20.2 2.1 %collective-permute-done.7.refs_2_ = f32[2,16,128]{2,1,0:T(8,128)S(1)} collective-permute-done((f32[2,16,128]{2,1,0:T(8,128)S(1)}, f32[2,16,128]{2,1,0:T(8,128)S(1)}, u32[]{:S(2)}, u32[]{:S(2)}) %collective-permute-start.7) | collective-permute-done | bytes 16416 | tf_op jit(solution)/shard_map/ppermute | solution.py:598
  22.3 0.9 %collective-permute-done.8.refs_3_ = f32[2,16,128]{2,1,0:T(8,128)S(1)} collective-permute-done((f32[2,16,128]{2,1,0:T(8,128)S(1)}, f32[2,16,128]{2,1,0:T(8,128)S(1)}, u32[]{:S(2)}, u32[]{:S(2)}) %collective-permute-start.8) | collective-permute-done | bytes 16416 | tf_op jit(solution)/shard_map/ppermute | solution.py:598
  23.2 2.0 %collective-permute-start.10 = (f32[2,16,128]{2,1,0:T(8,128)S(1)}, f32[2,16,128]{2,1,0:T(8,128)S(1)}, u32[]{:S(2)}, u32[]{:S(2)}) collective-permute-start(f32[2,16,128]{2,1,0:T(8,128)S(1)} %shard_map.89.rest_0_), channel_id=1, source_target_pairs={{0,8},{4,12},{8,0},{12,4},{1,9},{5,13},{9,1},{13,5},{2,10},{6,14},... | collective-permute-start | bytes 49160 | tf_op jit(solution)/shard_map/ppermute | solution.py:598
  25.3 1.6 %collective-permute-start.11 = (f32[2,16,128]{2,1,0:T(8,128)S(1)}, f32[2,16,128]{2,1,0:T(8,128)S(1)}, u32[]{:S(2)}, u32[]{:S(2)}) collective-permute-start(f32[2,16,128]{2,1,0:T(8,128)S(1)} %shard_map.89.rest_0_), channel_id=1, source_target_pairs={{0,12},{4,8},{8,4},{12,0},{1,13},{5,9},{9,5},{13,1},{2,14},{6,10},... | collective-permute-start | bytes 49160 | tf_op jit(solution)/shard_map/ppermute | solution.py:598
  26.8 0.4 %collective-permute-start.9 = (f32[2,16,128]{2,1,0:T(8,128)S(1)}, f32[2,16,128]{2,1,0:T(8,128)S(1)}, u32[]{:S(2)}, u32[]{:S(2)}) collective-permute-start(f32[2,16,128]{2,1,0:T(8,128)S(1)} %shard_map.89.rest_0_), channel_id=1, source_target_pairs={{0,4},{4,0},{8,12},{12,8},{1,5},{5,1},{9,13},{13,9},{2,6},{6,2},{1... | collective-permute-start | bytes 49160 | tf_op jit(solution)/shard_map/ppermute | solution.py:598
  27.3 0.8 %collective-permute-done.10.rest_2_ = f32[2,16,128]{2,1,0:T(8,128)S(1)} collective-permute-done((f32[2,16,128]{2,1,0:T(8,128)S(1)}, f32[2,16,128]{2,1,0:T(8,128)S(1)}, u32[]{:S(2)}, u32[]{:S(2)}) %collective-permute-start.10) | collective-permute-done | bytes 16416 | tf_op jit(solution)/shard_map/ppermute | solution.py:598
  28.1 2.7 %collective-permute-done.11.rest_3_ = f32[2,16,128]{2,1,0:T(8,128)S(1)} collective-permute-done((f32[2,16,128]{2,1,0:T(8,128)S(1)}, f32[2,16,128]{2,1,0:T(8,128)S(1)}, u32[]{:S(2)}, u32[]{:S(2)}) %collective-permute-start.11) | collective-permute-done | bytes 16416 | tf_op jit(solution)/shard_map/ppermute | solution.py:598
  30.8 0.0 collective-permute-done.9.rest_1_
  30.8 1.8 %shard_map.90 = (f32[2,20,8,256]{3,2,1,0:T(8,128)}, f32[2,20,8,256]{3,2,1,0:T(8,128)}, f32[8,256]{1,0:T(8,128)}) custom-call(f32[2,20,8,256]{3,2,1,0:T(8,128)S(1)} %get-tuple-element.21.rhs, f32[2,2,20,24,128]{4,3,2,1,0:T(8,128)S(1)} %get-tuple-element.28.power_1, f32[2,2,20,24,128]{4,3,2,1,0:T(8,128)S(1)} %get-tuple-element.29.power_2, ...), custom_call_target="tpu_custom_call" | custom-call | tf_op jit(solution)/shard_map/pallas_call | solution.py:641
  (6 shorter events, 0.0 us)
Async XLA Ops:
  2.0 10.9 %collective-permute-start = (f32[62,8,128]{2,1,0:T(8,128)S(1)}, f32[62,8,128]{2,1,0:T(8,128)S(1)}, u32[]{:S(2)}, u32[]{:S(2)}) collective-permute-start(f32[62,8,128]{2,1,0:T(8,128)S(1)} %get-tuple-element.26), channel_id=1, source_target_pairs={{0,16},{4,8},{8,4},{12,28},{16,0},{20,24},{24,20},{28,12},{1,17},{... | collective-permute-start | bytes 761864 | tf_op jit(solution)/shard_map/ppermute | solution.py:52
  5.0 7.9 %collective-permute-start.1 = (f32[62,8,128]{2,1,0:T(8,128)S(1)}, f32[62,8,128]{2,1,0:T(8,128)S(1)}, u32[]{:S(2)}, u32[]{:S(2)}) collective-permute-start(f32[62,8,128]{2,1,0:T(8,128)S(1)} %get-tuple-element.27), channel_id=1, source_target_pairs={{0,4},{4,0},{8,12},{12,8},{1,5},{5,1},{9,13},{13,9},{2,6},{6,2},{1... | collective-permute-start | bytes 761864 | tf_op jit(solution)/shard_map/ppermute | solution.py:52
  6.7 1.6 %collective-permute-start.2 = (f32[3,8,128]{2,1,0:T(8,128)S(1)}, f32[3,8,128]{2,1,0:T(8,128)S(1)}, u32[]{:S(2)}, u32[]{:S(2)}) collective-permute-start(f32[3,8,128]{2,1,0:T(8,128)S(1)} %get-tuple-element.33), channel_id=1, source_target_pairs={{0,1},{1,0},{2,3},{3,2},{4,5},{5,4},{6,7},{7,6},{8,9},{9,8},{10,11... | collective-permute-start | bytes 36872 | tf_op jit(solution)/shard_map/ppermute | solution.py:52
  6.7 3.1 %collective-permute-start.3 = (f32[3,8,128]{2,1,0:T(8,128)S(1)}, f32[3,8,128]{2,1,0:T(8,128)S(1)}, u32[]{:S(2)}, u32[]{:S(2)}) collective-permute-start(f32[3,8,128]{2,1,0:T(8,128)S(1)} %get-tuple-element.34), channel_id=1, source_target_pairs={{0,3},{1,2},{2,1},{3,0},{4,7},{5,6},{6,5},{7,4},{8,11},{9,10},{10,... | collective-permute-start | bytes 36872 | tf_op jit(solution)/shard_map/ppermute | solution.py:52
  9.8 7.7 %collective-permute-start.4 = (f32[6,8,128]{2,1,0:T(8,128)S(1)}, f32[6,8,128]{2,1,0:T(8,128)S(1)}, u32[]{:S(2)}, u32[]{:S(2)}) collective-permute-start(f32[6,8,128]{2,1,0:T(8,128)S(1)} %shard_map.87.columns), channel_id=1, source_target_pairs={{0,2},{4,8},{8,4},{12,14},{2,0},{6,10},{10,6},{14,12},{1,3},{5,9},... | collective-permute-start | bytes 73736 | tf_op jit(solution)/shard_map/ppermute | solution.py:52
  11.3 6.2 %collective-permute-start.5 = (f32[6,8,128]{2,1,0:T(8,128)S(1)}, f32[6,8,128]{2,1,0:T(8,128)S(1)}, u32[]{:S(2)}, u32[]{:S(2)}) collective-permute-start(f32[6,8,128]{2,1,0:T(8,128)S(1)} %shard_map.87.columns), channel_id=1, source_target_pairs={{0,4},{4,0},{8,12},{12,8},{1,5},{5,1},{9,13},{13,9},{2,6},{6,2},{1... | collective-permute-start | bytes 73736 | tf_op jit(solution)/shard_map/ppermute | solution.py:52
  18.2 1.9 %collective-permute-start.6 = (f32[2,16,128]{2,1,0:T(8,128)S(1)}, f32[2,16,128]{2,1,0:T(8,128)S(1)}, u32[]{:S(2)}, u32[]{:S(2)}) collective-permute-start(f32[2,16,128]{2,1,0:T(8,128)S(1)} %get-tuple-element.38.refs_0_), channel_id=1, source_target_pairs={{0,1},{1,0},{2,3},{3,2},{4,5},{5,4},{6,7},{7,6},{8,9},{9,8},{10,11... | collective-permute-start | bytes 49160 | tf_op jit(solution)/shard_map/ppermute | solution.py:598
  18.5 3.7 %collective-permute-start.7 = (f32[2,16,128]{2,1,0:T(8,128)S(1)}, f32[2,16,128]{2,1,0:T(8,128)S(1)}, u32[]{:S(2)}, u32[]{:S(2)}) collective-permute-start(f32[2,16,128]{2,1,0:T(8,128)S(1)} %get-tuple-element.38.refs_0_), channel_id=1, source_target_pairs={{0,2},{1,3},{2,0},{3,1},{4,6},{5,7},{6,4},{7,5},{8,10},{9,11},{10,... | collective-permute-start | bytes 49160 | tf_op jit(solution)/shard_map/ppermute | solution.py:598
  20.0 3.2 %collective-permute-start.8 = (f32[2,16,128]{2,1,0:T(8,128)S(1)}, f32[2,16,128]{2,1,0:T(8,128)S(1)}, u32[]{:S(2)}, u32[]{:S(2)}) collective-permute-start(f32[2,16,128]{2,1,0:T(8,128)S(1)} %get-tuple-element.38.refs_0_), channel_id=1, source_target_pairs={{0,3},{1,2},{2,1},{3,0},{4,7},{5,6},{6,5},{7,4},{8,11},{9,10},{10,... | collective-permute-start | bytes 49160 | tf_op jit(solution)/shard_map/ppermute | solution.py:598
  23.2 4.9 %collective-permute-start.10 = (f32[2,16,128]{2,1,0:T(8,128)S(1)}, f32[2,16,128]{2,1,0:T(8,128)S(1)}, u32[]{:S(2)}, u32[]{:S(2)}) collective-permute-start(f32[2,16,128]{2,1,0:T(8,128)S(1)} %shard_map.89.rest_0_), channel_id=1, source_target_pairs={{0,8},{4,12},{8,0},{12,4},{1,9},{5,13},{9,1},{13,5},{2,10},{6,14},... | collective-permute-start | bytes 49160 | tf_op jit(solution)/shard_map/ppermute | solution.py:598
  25.3 5.5 %collective-permute-start.11 = (f32[2,16,128]{2,1,0:T(8,128)S(1)}, f32[2,16,128]{2,1,0:T(8,128)S(1)}, u32[]{:S(2)}, u32[]{:S(2)}) collective-permute-start(f32[2,16,128]{2,1,0:T(8,128)S(1)} %shard_map.89.rest_0_), channel_id=1, source_target_pairs={{0,12},{4,8},{8,4},{12,0},{1,13},{5,9},{9,5},{13,1},{2,14},{6,10},... | collective-permute-start | bytes 49160 | tf_op jit(solution)/shard_map/ppermute | solution.py:598
  26.8 4.0 %collective-permute-start.9 = (f32[2,16,128]{2,1,0:T(8,128)S(1)}, f32[2,16,128]{2,1,0:T(8,128)S(1)}, u32[]{:S(2)}, u32[]{:S(2)}) collective-permute-start(f32[2,16,128]{2,1,0:T(8,128)S(1)} %shard_map.89.rest_0_), channel_id=1, source_target_pairs={{0,4},{4,0},{8,12},{12,8},{1,5},{5,1},{9,13},{13,9},{2,6},{6,2},{1... | collective-permute-start | bytes 49160 | tf_op jit(solution)/shard_map/ppermute | solution.py:598

commit v17 on v15

--- a/solution.py
+++ b/solution.py
@@ -99,8 +99,8 @@
     return pltpu.roll(v, shift, 1) if shift else v
 
 
-def pack_kernel(*refs):
-    sources, held, (column_a, column_b, strip_a, strip_b, arrived) = refs[:6], refs[6:12], refs[12:]
+def strip_kernel(*refs):
+    sources, held, (strip_a, strip_b, arrived) = refs[:6], refs[6:12], refs[12:]
     copies = [pltpu.make_async_copy(a, b, arrived.at[i]) for i, (a, b) in enumerate(zip(sources, held))]
     for copy in copies:
         copy.start()
@@ -109,14 +109,8 @@
     rhs, eta, friction, ice, grounded, _ = held
     layers = eta.shape[0]
     plane = own_planes(rhs, eta, friction, ice, grounded)
-    lane = lax.broadcasted_iota(jnp.int32, (ROWS, LANES), 1)
-    row = lax.broadcasted_iota(jnp.int32, (ROWS, LANES), 0)
-    rows_even, _, _ = place_of("gx")
-    columns_even, _, _ = place_of(("gy", "gz"))
-    upper_a = (row < HALO) != rows_even
-    count = ribbon_tiles(layers)
-    zero = jnp.zeros((ROWS, LANES), jnp.float32)
-    left, right = [zero] * count, [zero] * count
+    even, _, _ = place_of("gx")
+    upper_a = (lax.broadcasted_iota(jnp.int32, (ROWS, LANES), 0) < HALO) != even
     for q in range(strip_a.shape[0] // 2):
         first, second = pair_of(q, layers)
         x, y = plane(first), plane(second)
@@ -126,21 +120,26 @@
             ys = pltpu.roll(ys, HALO, 0)
             strip_a[2 * q + half] = jnp.where(upper_a, xs, ys)
             strip_b[2 * q + half] = jnp.where(upper_a, ys, xs)
-        for p, v in ((first, x), (second, y)):
-            tile, slots = ribbon_places(p, layers)
-            for slot in slots:
-                at = slot * SLOT
-                left[tile] = jnp.where(between(lane, at + 8, 4), turned(v[:, :LANES], at + 8), left[tile])
-                right[tile] = jnp.where(between(lane, at + 16, 4), turned(v[:, LANES:], at + 20), right[tile])
+
+
+def column_kernel(rhs, eta, friction, ice, grounded, column_a, column_b):
+    layers = eta.shape[0]
+    plane = own_planes(rhs, eta, friction, ice, grounded)
+    lane = lax.broadcasted_iota(jnp.int32, (ROWS, LANES), 1)
+    even, _, _ = place_of(("gy", "gz"))
+    zero = jnp.zeros((ROWS, LANES), jnp.float32)
     to_left, to_right = [zero] * column_a.shape[0], [zero] * column_a.shape[0]
-    for tile in range(count):
+    for p in range(3 * layers + 2):
+        v = plane(p)
+        tile, slots = ribbon_places(p, layers)
         group, at = packed_place(tile)
-        here = between(lane % SLOT, at, HALO)
-        to_left[group] = jnp.where(here, turned(left[tile], at - 8), to_left[group])
-        to_right[group] = jnp.where(here, turned(right[tile], at - 16), to_right[group])
+        for slot in slots:
+            here = between(lane, slot * SLOT + at, HALO)
+            to_left[group] = jnp.where(here, turned(v[:, :LANES], slot * SLOT + at), to_left[group])
+            to_right[group] = jnp.where(here, turned(v[:, LANES:], slot * SLOT + at + HALO), to_right[group])
     for group in range(column_a.shape[0]):
-        column_a[group] = jnp.where(columns_even, to_right[group], to_left[group])
-        column_b[group] = jnp.where(columns_even, to_left[group], to_right[group])
+        column_a[group] = jnp.where(even, to_right[group], to_left[group])
+        column_b[group] = jnp.where(even, to_left[group], to_right[group])
 
 
 def beside_kernel(from_a, from_b, columns):
@@ -161,22 +160,18 @@
 
 def join(x, y):
     s, e = two_sum(x[0], y[0])
-    e = e + (x[1] + y[1])
-    h = s + e
-    return h, e - (h - s)
+    return s, e + (x[1] + y[1])
+
+
+def cut(v, bits):
+    t = v * (2.0**bits + 1.0)
+    h = t - (t - v)
+    return h, v - h
 
 
 def times(scalar, x):
-    def cut(v):
-        t = v * 4097.0
-        h = t - (t - v)
-        return h, v - h
-
-    p = scalar * x[0]
-    sh, sl = cut(scalar)
-    xh, xl = cut(x[0])
-    e = ((sh * xh - p) + sh * xl + sl * xh) + sl * xl
-    return p, e + scalar * x[1]
+    high, low = cut(x[0], 12)
+    return scalar * high, scalar * low + scalar * x[1]
 
 
 def beyond():
@@ -277,7 +272,7 @@
     col_prev = staticmethod(col_prev)
 
 
-def horizontal(g0, g1, e_row, e_col, e_half, moves):
+def horizontal(g0, g1, e_row, e_row_1, e_col, e_col_1, e_half, moves):
     row_next, row_prev, col_next, col_prev = moves.row_next, moves.row_prev, moves.col_next, moves.col_prev
     g0n, g1n = row_next(g0), col_next(g1)
     f = e_half * (g1n - col_prev(g1))
@@ -286,15 +281,15 @@
     out0 = flux - row_next(f) - row_prev(flux - f)
     flux = e_col * (g0 - col_next(g0))
     out0 = out0 + (flux - col_prev(flux))
-    flux = (4.0 * e_col) * (g1 - g1n)
+    flux = e_col_1 * (g1 - g1n)
     out1 = flux - col_next(h) - col_prev(flux - h)
-    flux = (0.25 * e_row) * (g1 - row_next(g1))
+    flux = e_row_1 * (g1 - row_next(g1))
     out1 = out1 + (flux - row_prev(flux))
     return out0, out1
 
 
 def main_kernel(
-    rhs, eta, friction, ice, grounded, strip_b, strip_a,
+    rhs, eta, friction, ice, grounded, strip_a, strip_b,
     power_1, power_2, power_3, power_4, sums, ribbon,
     masked, eta_row, eta_col, eta_half, eta_up, cover, drag,
 ):
@@ -337,8 +332,12 @@
     load = Tiles.load
     for k in range(layers):
         e = load(eta_half.at[k])
-        (2.0 * (e + moves.row_next(e))).store(eta_row.at[k])
-        (0.5 * (e + moves.col_next(e))).store(eta_col.at[k])
+        pair = e + moves.row_next(e)
+        (2.0 * pair).store(eta_row.at[0, k])
+        (0.5 * pair).store(eta_row.at[1, k])
+        pair = e + moves.col_next(e)
+        (0.5 * pair).store(eta_col.at[0, k])
+        (2.0 * pair).store(eta_col.at[1, k])
         eta_up[k] = eta_half[k] + eta_half[k + 1] if k + 1 < layers else jnp.zeros_like(eta_up[k])
         if k:
             eta_half[k - 1] = 0.5 * eta_half[k - 1]
@@ -356,7 +355,8 @@
                 next0, next1 = load(src.at[0, after]), load(src.at[1, after])
                 e_up = load(eta_up.at[k])
                 up0, up1 = e_up * (g0 - next0), e_up * (g1 - next1)
-                out0, out1 = horizontal(g0, g1, load(eta_row.at[k]), load(eta_col.at[k]), load(eta_half.at[k]), moves)
+                pairs = [load(ref.at[c, k]) for ref in (eta_row, eta_col) for c in range(2)]
+                out0, out1 = horizontal(g0, g1, *pairs, load(eta_half.at[k]), moves)
                 out0, out1 = m * (out0 + (up0 - below0)), m * (out1 + (up1 - below1))
                 for c, g, out in ((0, g0, out0), (1, g1, out1)):
                     if t < STEPS:
@@ -420,6 +420,7 @@
 
     eta_row = [2.0 * (e + row_next(e)) for e in eta]
     eta_col = [0.5 * (e + col_next(e)) for e in eta]
+    eta_row_1, eta_col_1 = [0.25 * e for e in eta_row], [4.0 * e for e in eta_col]
     eta_half = [0.5 * e for e in eta]
     eta_up = [e + n for e, n in zip(eta, after(eta))]
     eta_up[-1] = jnp.where(lane < LANES - SLOT, eta_up[-1], 0.0)
@@ -431,7 +432,8 @@
         result = ([], [])
         odd = even = jnp.zeros((ROWS, LANES), jnp.float32)
         for n in range(tiles):
-            outs = horizontal(field[0][n], field[1][n], eta_row[n], eta_col[n], eta_half[n], Turns)
+            coefficients = (eta_row[n], eta_row_1[n], eta_col[n], eta_col_1[n], eta_half[n])
+            outs = horizontal(field[0][n], field[1][n], *coefficients, Turns)
             for c in range(2):
                 below = ups[c][n - 1] if n else turned(ups[c][-1], SLOT) - drag * field[c][0]
                 out = cover * (outs[c] + (ups[c][n] - below))
@@ -474,13 +476,13 @@
     def spread(v, j):
         return jnp.broadcast_to(v[j : j + 1], (ROWS, LANES))
 
-    centre = spread(total[0], 1) / spread(total[0], 0)
+    centre, _ = cut(spread(total[0], 1) / spread(total[0], 0), 13)
     wide = jnp.concatenate([centre, centre], 0)
-    mu = [spread(total[0], 0)]
+    mu = [spread(total[0] + total[1], 0)]
     for _ in range(2 * STEPS):
         step = times(wide, total)
         total = join(tuple(pltpu.roll(v, 2 * ROWS - 1, 0) for v in total), (-step[0], -step[1]))
-        mu.append(spread(total[0], 0))
+        mu.append(spread(total[0] + total[1], 0))
 
     def plus(a, b):
         n = max(len(a), len(b))
@@ -611,13 +613,14 @@
     ribbons = ribbon_tiles(layers)
     packed = ((ribbons + 7) // 8,) + tile
     both = (2 * packed[0],) + tile
-    *held, column_a, column_b, strip_a, strip_b = call(
-        pack_kernel,
-        [jax.ShapeDtypeStruct(x.shape, x.dtype) for x in inputs] + [packed, packed, strips, strips],
+    *held, strip_a, strip_b = call(
+        strip_kernel,
+        [jax.ShapeDtypeStruct(x.shape, x.dtype) for x in inputs] + [strips, strips],
         [pltpu.SemaphoreType.DMA((len(inputs),))],
         in_specs=[pl.BlockSpec(memory_space=pltpu.HBM)] * len(inputs),
     )(*[pltpu.with_memory_space_constraint(x, pltpu.HBM) for x in inputs])
-    strip_b, strip_a = swapped(strip_b, ("gx",), 1, "parts"), swapped(strip_a, ("gx",), 0)
+    strip_a, strip_b = swapped(strip_a, ("gx",), 0), swapped(strip_b, ("gx",), 1, "parts")
+    column_a, column_b = call(column_kernel, [packed, packed])(*held[:5])
     beside = ("gy", "gz")
     (columns,) = call(beside_kernel, [both])(swapped(column_a, beside, 0), swapped(column_b, beside, 1))
     columns_b, columns_a = swapped(columns, ("gx",), 1, "gy"), swapped(columns, ("gx",), 0)
@@ -625,9 +628,9 @@
     *powers, sums, ribbon = call(
         main_kernel,
         [(2,) + block] * (STEPS - 1) + [adjoint_rhs.shape, (2 * STEPS + 1, ROWS, 2 * LANES), (ribbons, 2 * ROWS, LANES)],
-        [(2,) + block] + [block] * 4 + [block[1:]] * 2,
+        [(2,) + block] * 3 + [block] * 2 + [block[1:]] * 2,
         cost_estimate=pl.CostEstimate(flops=200_000_000, bytes_accessed=8_000_000, transcendentals=0),
-    )(*held[:5], strip_b, strip_a)
+    )(*held[:5], strip_a, strip_b)
     edges, sums = call(
         ribbon_kernel,
         [(STEPS, 2, layers // 4) + tile, (2, 2 * ROWS, LANES)],

time: 32.4 us -> 32.7 us (level)
  waiting for transfers between devices: 8.1 us -> 9.52 us
  starting transfers between devices: 15.3 us -> 14.4 us
    ppermute x6, starting transfers between devices: 9.37 us -> 7.99 us  [swapped(): return lax.ppermute(x, names, pairs)]
    ppermute x6, waiting for transfers between devices: 1.53 us -> 2.48 us  [swapped(): return lax.ppermute(x, names, pairs)]
    ppermute x6, waiting for transfers between devices: 6.57 us -> 7.04 us  [exchange(): parts.append(lax.ppermute(x, axis, pairs))]
    ppermute x6, starting transfers between devices: 5.97 us -> 6.38 us  [exchange(): parts.append(lax.ppermute(x, axis, pairs))]
    pallas_call x1 -> x2, Pallas kernels: 1.35 us -> 1.33 us  [the longest x1 1.13 us: body(): call(strip_kernel, [jax.ShapeDtypeStruct(x.shape, x.dtype) for x in input...]
  transfers between devices with their start and end apart: 12 -> 12, of which waited for: 5 -> 6; matrix products, arithmetic and copies ran while one was open for 0% -> 0% of each run, Pallas kernels for 13% -> 13%
where the time goes in v17:
time: 32.7 us; the launch traced here: 32.5 us
  starting transfers between devices  14.4 us (44%)
  waiting for transfers between devices  9.52 us (29%)
  Pallas kernels  7.94 us (24%)
  between operations  0.71 us (2%)
    ppermute x6, starting transfers between devices, swapped(): return lax.ppermute(x, names, pairs)  7.99 us
    ppermute x6, waiting for transfers between devices, exchange(): parts.append(lax.ppermute(x, axis, pairs))  7.04 us
    ppermute x6, starting transfers between devices, exchange(): parts.append(lax.ppermute(x, axis, pairs))  6.38 us
    pallas_call x1, Pallas kernels, body(): call(main_kernel, [(2,) + block] * (STEPS - 1) + [adjoint_rhs.shape, (2 *...  4.15 us
    ppermute x6, waiting for transfers between devices, swapped(): return lax.ppermute(x, names, pairs)  2.48 us
    pallas_call x1, Pallas kernels, body(): call(final_kernel, [adjoint_rhs.shape, adjoint_rhs.shape, friction.shape])  1.72 us
    pallas_call x1, Pallas kernels, body(): call(strip_kernel, [jax.ShapeDtypeStruct(x.shape, x.dtype) for x in input...  1.13 us
    pallas_call x1, Pallas kernels, body(): call(ribbon_kernel, [(STEPS, 2, layers // 4) + tile, (2, 2 * ROWS, LANES)])  0.72 us
  transfers between devices with their start and end apart: 12, of which 6 were waited for; matrix products, arithmetic and copies ran while one was open for 0% of the time, Pallas kernels for 13%

profile of v17, /device:TPU:0, one launch (start us, length us, event | category | flops | bytes accessed | tf_op | source)
XLA Modules:
  0.0 32.5 jit_solution(13923095581654333963)
XLA Ops:
  0.6 1.1 %shard_map.85 = (f32[2,20,8,256]{3,2,1,0:T(8,128)S(1)}, f32[20,8,256]{2,1,0:T(8,128)S(1)}, f32[8,256]{1,0:T(8,128)S(1)}, s32[8,256]{1,0:T(8,128)S(1)}, s32[8,256...) custom-call(f32[2,20,8,256]{3,2,1,0:T(8,128)} %refs_0_.1, ...), custom_call_target="tpu_custom_call" | custom-call | tf_op jit(solution)/shard_map/pallas_call | solution.py:616
  1.8 3.1 %collective-permute-start = (f32[62,8,128]{2,1,0:T(8,128)S(1)}, f32[62,8,128]{2,1,0:T(8,128)S(1)}, u32[]{:S(2)}, u32[]{:S(2)}) collective-permute-start(f32[62,8,128]{2,1,0:T(8,128)S(1)} %get-tuple-element.26), channel_id=1, source_target_pairs={{0,4},{4,0},{8,12},{12,8},{1,5},{5,1},{9,13},{13,9},{2,6},{6,2},{1... | collective-permute-start | bytes 761864 | tf_op jit(solution)/shard_map/ppermute | solution.py:51
  4.9 1.5 %collective-permute-start.1 = (f32[62,8,128]{2,1,0:T(8,128)S(1)}, f32[62,8,128]{2,1,0:T(8,128)S(1)}, u32[]{:S(2)}, u32[]{:S(2)}) collective-permute-start(f32[62,8,128]{2,1,0:T(8,128)S(1)} %get-tuple-element.27), channel_id=1, source_target_pairs={{0,16},{4,8},{8,4},{12,28},{16,0},{20,24},{24,20},{28,12},{1,17},{... | collective-permute-start | bytes 761864 | tf_op jit(solution)/shard_map/ppermute | solution.py:51
  6.4 0.2 shard_map.87
  6.6 0.1 collective-permute-start.2
  6.7 1.6 %collective-permute-start.3 = (f32[3,8,128]{2,1,0:T(8,128)S(1)}, f32[3,8,128]{2,1,0:T(8,128)S(1)}, u32[]{:S(2)}, u32[]{:S(2)}) collective-permute-start(f32[3,8,128]{2,1,0:T(8,128)S(1)} %get-tuple-element.34), channel_id=1, source_target_pairs={{0,3},{1,2},{2,1},{3,0},{4,7},{5,6},{6,5},{7,4},{8,11},{9,10},{10,... | collective-permute-start | bytes 36872 | tf_op jit(solution)/shard_map/ppermute | solution.py:51
  8.3 0.0 collective-permute-done.2.from_a
  8.3 1.6 %collective-permute-done.3.from_b = f32[3,8,128]{2,1,0:T(8,128)S(1)} collective-permute-done((f32[3,8,128]{2,1,0:T(8,128)S(1)}, f32[3,8,128]{2,1,0:T(8,128)S(1)}, u32[]{:S(2)}, u32[]{:S(2)}) %collective-permute-start.3) | collective-permute-done | bytes 12320 | tf_op jit(solution)/shard_map/ppermute | solution.py:51
  9.8 1.5 %collective-permute-start.4 = (f32[6,8,128]{2,1,0:T(8,128)S(1)}, f32[6,8,128]{2,1,0:T(8,128)S(1)}, u32[]{:S(2)}, u32[]{:S(2)}) collective-permute-start(f32[6,8,128]{2,1,0:T(8,128)S(1)} %shard_map.88.columns), channel_id=1, source_target_pairs={{0,2},{4,8},{8,4},{12,14},{2,0},{6,10},{10,6},{14,12},{1,3},{5,9},... | collective-permute-start | bytes 73736 | tf_op jit(solution)/shard_map/ppermute | solution.py:51
  11.3 0.2 collective-permute-start.5
  11.6 0.9 %collective-permute-done.1.strip_b = f32[62,8,128]{2,1,0:T(8,128)S(1)} collective-permute-done((f32[62,8,128]{2,1,0:T(8,128)S(1)}, f32[62,8,128]{2,1,0:T(8,128)S(1)}, u32[]{:S(2)}, u32[]{:S(2)}) %collective-permute-start.1) | collective-permute-done | bytes 253984 | tf_op jit(solution)/shard_map/ppermute | solution.py:51
  12.4 4.1 %shard_map.86 = (f32[2,20,16,256]{3,2,1,0:T(8,128)S(1)}, f32[2,20,16,256]{3,2,1,0:T(8,128)S(1)}, f32[2,20,16,256]{3,2,1,0:T(8,128)S(1)}, f32[2,20,8,256]{3,2,1,0...) custom-call(f32[2,20,8,256]{3,2,1,0:T(8,128)S(1)} %get-tuple-element.21.rhs, ...), custom_call_target="tpu_custom_call" | custom-call | flops 200000000 | bytes 8000000 | tf_op jit(solution)/shard_map/pallas_call | solution.py:628
  16.6 0.7 %shard_map.89 = (f32[4,2,5,8,128]{4,3,2,1,0:T(8,128)S(1)}, f32[2,16,128]{2,1,0:T(8,128)S(1)}) custom-call(f32[17,16,128]{2,1,0:T(8,128)S(1)} %get-tuple-element.32.ribbon, f32[6,8,128]{2,1,0:T(8,128)S(1)} %shard_map.88.columns, f32[6,8,128]{2,1,0:T(8,128)S(1)} %collective-permute-done.4.columns_b, f32[6,8,128]{2,1,0:T(8,128)S(1)} %collective-permute-done.5.columns_a, ...), custom_call_target="tpu_custom_call" | custom-call | tf_op jit(solution)/shard_map/pallas_call | solution.py:634
  17.4 0.1 collective-permute-start.6
  17.4 1.6 %collective-permute-start.7 = (f32[2,16,128]{2,1,0:T(8,128)S(1)}, f32[2,16,128]{2,1,0:T(8,128)S(1)}, u32[]{:S(2)}, u32[]{:S(2)}) collective-permute-start(f32[2,16,128]{2,1,0:T(8,128)S(1)} %get-tuple-element.38.refs_0_), channel_id=1, source_target_pairs={{0,2},{1,3},{2,0},{3,1},{4,6},{5,7},{6,4},{7,5},{8,10},{9,11},{10,... | collective-permute-start | bytes 49160 | tf_op jit(solution)/shard_map/ppermute | solution.py:601
  19.0 0.3 collective-permute-start.8
  19.3 1.9 %collective-permute-done.7.refs_2_ = f32[2,16,128]{2,1,0:T(8,128)S(1)} collective-permute-done((f32[2,16,128]{2,1,0:T(8,128)S(1)}, f32[2,16,128]{2,1,0:T(8,128)S(1)}, u32[]{:S(2)}, u32[]{:S(2)}) %collective-permute-start.7) | collective-permute-done | bytes 16416 | tf_op jit(solution)/shard_map/ppermute | solution.py:601
  21.2 0.9 %collective-permute-done.8.refs_3_ = f32[2,16,128]{2,1,0:T(8,128)S(1)} collective-permute-done((f32[2,16,128]{2,1,0:T(8,128)S(1)}, f32[2,16,128]{2,1,0:T(8,128)S(1)}, u32[]{:S(2)}, u32[]{:S(2)}) %collective-permute-start.8) | collective-permute-done | bytes 16416 | tf_op jit(solution)/shard_map/ppermute | solution.py:601
  22.2 1.5 %collective-permute-start.9 = (f32[2,16,128]{2,1,0:T(8,128)S(1)}, f32[2,16,128]{2,1,0:T(8,128)S(1)}, u32[]{:S(2)}, u32[]{:S(2)}) collective-permute-start(f32[2,16,128]{2,1,0:T(8,128)S(1)} %shard_map.90.rest_0_), channel_id=1, source_target_pairs={{0,4},{4,0},{8,12},{12,8},{1,5},{5,1},{9,13},{13,9},{2,6},{6,2},{1... | collective-permute-start | bytes 49160 | tf_op jit(solution)/shard_map/ppermute | solution.py:601
  23.7 1.6 %collective-permute-start.10 = (f32[2,16,128]{2,1,0:T(8,128)S(1)}, f32[2,16,128]{2,1,0:T(8,128)S(1)}, u32[]{:S(2)}, u32[]{:S(2)}) collective-permute-start(f32[2,16,128]{2,1,0:T(8,128)S(1)} %shard_map.90.rest_0_), channel_id=1, source_target_pairs={{0,8},{4,12},{8,0},{12,4},{1,9},{5,13},{9,1},{13,5},{2,10},{6,14},... | collective-permute-start | bytes 49160 | tf_op jit(solution)/shard_map/ppermute | solution.py:601
  25.3 1.3 %collective-permute-start.11 = (f32[2,16,128]{2,1,0:T(8,128)S(1)}, f32[2,16,128]{2,1,0:T(8,128)S(1)}, u32[]{:S(2)}, u32[]{:S(2)}) collective-permute-start(f32[2,16,128]{2,1,0:T(8,128)S(1)} %shard_map.90.rest_0_), channel_id=1, source_target_pairs={{0,12},{4,8},{8,4},{12,0},{1,13},{5,9},{9,5},{13,1},{2,14},{6,10},... | collective-permute-start | bytes 49160 | tf_op jit(solution)/shard_map/ppermute | solution.py:601
  26.6 1.7 %collective-permute-done.10.rest_2_ = f32[2,16,128]{2,1,0:T(8,128)S(1)} collective-permute-done((f32[2,16,128]{2,1,0:T(8,128)S(1)}, f32[2,16,128]{2,1,0:T(8,128)S(1)}, u32[]{:S(2)}, u32[]{:S(2)}) %collective-permute-start.10) | collective-permute-done | bytes 16416 | tf_op jit(solution)/shard_map/ppermute | solution.py:601
  28.3 2.5 %collective-permute-done.11.rest_3_ = f32[2,16,128]{2,1,0:T(8,128)S(1)} collective-permute-done((f32[2,16,128]{2,1,0:T(8,128)S(1)}, f32[2,16,128]{2,1,0:T(8,128)S(1)}, u32[]{:S(2)}, u32[]{:S(2)}) %collective-permute-start.11) | collective-permute-done | bytes 16416 | tf_op jit(solution)/shard_map/ppermute | solution.py:601
  30.8 1.7 %shard_map.91 = (f32[2,20,8,256]{3,2,1,0:T(8,128)}, f32[2,20,8,256]{3,2,1,0:T(8,128)}, f32[8,256]{1,0:T(8,128)}) custom-call(f32[2,20,8,256]{3,2,1,0:T(8,128)S(1)} %get-tuple-element.21.rhs, f32[2,20,16,256]{3,2,1,0:T(8,128)S(1)} %get-tuple-element.28.power_1, f32[2,20,16,256]{3,2,1,0:T(8,128)S(1)} %get-tuple-element.29.power_2, ...), custom_call_target="tpu_custom_call" | custom-call | tf_op jit(solution)/shard_map/pallas_call | solution.py:644
  (7 shorter events, 0.0 us)
Async XLA Ops:
  1.8 9.8 %collective-permute-start = (f32[62,8,128]{2,1,0:T(8,128)S(1)}, f32[62,8,128]{2,1,0:T(8,128)S(1)}, u32[]{:S(2)}, u32[]{:S(2)}) collective-permute-start(f32[62,8,128]{2,1,0:T(8,128)S(1)} %get-tuple-element.26), channel_id=1, source_target_pairs={{0,4},{4,0},{8,12},{12,8},{1,5},{5,1},{9,13},{13,9},{2,6},{6,2},{1... | collective-permute-start | bytes 761864 | tf_op jit(solution)/shard_map/ppermute | solution.py:51
  4.9 7.6 %collective-permute-start.1 = (f32[62,8,128]{2,1,0:T(8,128)S(1)}, f32[62,8,128]{2,1,0:T(8,128)S(1)}, u32[]{:S(2)}, u32[]{:S(2)}) collective-permute-start(f32[62,8,128]{2,1,0:T(8,128)S(1)} %get-tuple-element.27), channel_id=1, source_target_pairs={{0,16},{4,8},{8,4},{12,28},{16,0},{20,24},{24,20},{28,12},{1,17},{... | collective-permute-start | bytes 761864 | tf_op jit(solution)/shard_map/ppermute | solution.py:51
  6.6 1.7 %collective-permute-start.2 = (f32[3,8,128]{2,1,0:T(8,128)S(1)}, f32[3,8,128]{2,1,0:T(8,128)S(1)}, u32[]{:S(2)}, u32[]{:S(2)}) collective-permute-start(f32[3,8,128]{2,1,0:T(8,128)S(1)} %get-tuple-element.33), channel_id=1, source_target_pairs={{0,1},{1,0},{2,3},{3,2},{4,5},{5,4},{6,7},{7,6},{8,9},{9,8},{10,11... | collective-permute-start | bytes 36872 | tf_op jit(solution)/shard_map/ppermute | solution.py:51
  6.7 3.2 %collective-permute-start.3 = (f32[3,8,128]{2,1,0:T(8,128)S(1)}, f32[3,8,128]{2,1,0:T(8,128)S(1)}, u32[]{:S(2)}, u32[]{:S(2)}) collective-permute-start(f32[3,8,128]{2,1,0:T(8,128)S(1)} %get-tuple-element.34), channel_id=1, source_target_pairs={{0,3},{1,2},{2,1},{3,0},{4,7},{5,6},{6,5},{7,4},{8,11},{9,10},{10,... | collective-permute-start | bytes 36872 | tf_op jit(solution)/shard_map/ppermute | solution.py:51
  9.8 6.8 %collective-permute-start.4 = (f32[6,8,128]{2,1,0:T(8,128)S(1)}, f32[6,8,128]{2,1,0:T(8,128)S(1)}, u32[]{:S(2)}, u32[]{:S(2)}) collective-permute-start(f32[6,8,128]{2,1,0:T(8,128)S(1)} %shard_map.88.columns), channel_id=1, source_target_pairs={{0,2},{4,8},{8,4},{12,14},{2,0},{6,10},{10,6},{14,12},{1,3},{5,9},... | collective-permute-start | bytes 73736 | tf_op jit(solution)/shard_map/ppermute | solution.py:51
  11.3 5.3 %collective-permute-start.5 = (f32[6,8,128]{2,1,0:T(8,128)S(1)}, f32[6,8,128]{2,1,0:T(8,128)S(1)}, u32[]{:S(2)}, u32[]{:S(2)}) collective-permute-start(f32[6,8,128]{2,1,0:T(8,128)S(1)} %shard_map.88.columns), channel_id=1, source_target_pairs={{0,4},{4,0},{8,12},{12,8},{1,5},{5,1},{9,13},{13,9},{2,6},{6,2},{1... | collective-permute-start | bytes 73736 | tf_op jit(solution)/shard_map/ppermute | solution.py:51
  17.4 1.9 %collective-permute-start.6 = (f32[2,16,128]{2,1,0:T(8,128)S(1)}, f32[2,16,128]{2,1,0:T(8,128)S(1)}, u32[]{:S(2)}, u32[]{:S(2)}) collective-permute-start(f32[2,16,128]{2,1,0:T(8,128)S(1)} %get-tuple-element.38.refs_0_), channel_id=1, source_target_pairs={{0,1},{1,0},{2,3},{3,2},{4,5},{5,4},{6,7},{7,6},{8,9},{9,8},{10,11... | collective-permute-start | bytes 49160 | tf_op jit(solution)/shard_map/ppermute | solution.py:601
  17.4 3.8 %collective-permute-start.7 = (f32[2,16,128]{2,1,0:T(8,128)S(1)}, f32[2,16,128]{2,1,0:T(8,128)S(1)}, u32[]{:S(2)}, u32[]{:S(2)}) collective-permute-start(f32[2,16,128]{2,1,0:T(8,128)S(1)} %get-tuple-element.38.refs_0_), channel_id=1, source_target_pairs={{0,2},{1,3},{2,0},{3,1},{4,6},{5,7},{6,4},{7,5},{8,10},{9,11},{10,... | collective-permute-start | bytes 49160 | tf_op jit(solution)/shard_map/ppermute | solution.py:601
  19.0 3.2 %collective-permute-start.8 = (f32[2,16,128]{2,1,0:T(8,128)S(1)}, f32[2,16,128]{2,1,0:T(8,128)S(1)}, u32[]{:S(2)}, u32[]{:S(2)}) collective-permute-start(f32[2,16,128]{2,1,0:T(8,128)S(1)} %get-tuple-element.38.refs_0_), channel_id=1, source_target_pairs={{0,3},{1,2},{2,1},{3,0},{4,7},{5,6},{6,5},{7,4},{8,11},{9,10},{10,... | collective-permute-start | bytes 49160 | tf_op jit(solution)/shard_map/ppermute | solution.py:601
  22.2 4.5 %collective-permute-start.9 = (f32[2,16,128]{2,1,0:T(8,128)S(1)}, f32[2,16,128]{2,1,0:T(8,128)S(1)}, u32[]{:S(2)}, u32[]{:S(2)}) collective-permute-start(f32[2,16,128]{2,1,0:T(8,128)S(1)} %shard_map.90.rest_0_), channel_id=1, source_target_pairs={{0,4},{4,0},{8,12},{12,8},{1,5},{5,1},{9,13},{13,9},{2,6},{6,2},{1... | collective-permute-start | bytes 49160 | tf_op jit(solution)/shard_map/ppermute | solution.py:601
  23.7 4.6 %collective-permute-start.10 = (f32[2,16,128]{2,1,0:T(8,128)S(1)}, f32[2,16,128]{2,1,0:T(8,128)S(1)}, u32[]{:S(2)}, u32[]{:S(2)}) collective-permute-start(f32[2,16,128]{2,1,0:T(8,128)S(1)} %shard_map.90.rest_0_), channel_id=1, source_target_pairs={{0,8},{4,12},{8,0},{12,4},{1,9},{5,13},{9,1},{13,5},{2,10},{6,14},... | collective-permute-start | bytes 49160 | tf_op jit(solution)/shard_map/ppermute | solution.py:601
  25.3 5.5 %collective-permute-start.11 = (f32[2,16,128]{2,1,0:T(8,128)S(1)}, f32[2,16,128]{2,1,0:T(8,128)S(1)}, u32[]{:S(2)}, u32[]{:S(2)}) collective-permute-start(f32[2,16,128]{2,1,0:T(8,128)S(1)} %shard_map.90.rest_0_), channel_id=1, source_target_pairs={{0,12},{4,8},{8,4},{12,0},{1,13},{5,9},{9,5},{13,1},{2,14},{6,10},... | collective-permute-start | bytes 49160 | tf_op jit(solution)/shard_map/ppermute | solution.py:601

commit v18 on v17

--- a/solution.py
+++ b/solution.py
@@ -43,12 +43,8 @@
                 other, to = (i, at ^ 1) if spare else (count - 1 - i, at)
                 if to >= others or count % 2:
                     other, to = i, at
-            if spare == "parts":
-                pairs.append((at * count + i, to * count + other))
-            else:
-                pairs.append((i * others + at, other * others + to))
-    names = axes if not spare else ("parts", *axes) if spare == "parts" else (*axes, spare)
-    return lax.ppermute(x, names, pairs)
+            pairs.append((i * others + at, other * others + to))
+    return lax.ppermute(x, (*axes, spare) if spare else axes, pairs)
 
 
 def own_planes(rhs, eta, friction, ice, grounded):
@@ -289,7 +285,7 @@
 
 
 def main_kernel(
-    rhs, eta, friction, ice, grounded, strip_a, strip_b,
+    rhs, eta, friction, ice, grounded, strip_b, strip_a,
     power_1, power_2, power_3, power_4, sums, ribbon,
     masked, eta_row, eta_col, eta_half, eta_up, cover, drag,
 ):
@@ -593,7 +589,7 @@
         stride *= size
     for at, (stride, size) in enumerate(rounds):
         parts = [x]
-        for turn in range(1, size):
+        for turn in range(size - 1, 0, -1):
             pairs = []
             for i in range(count):
                 place = (i // stride) % size
@@ -619,18 +615,18 @@
         [pltpu.SemaphoreType.DMA((len(inputs),))],
         in_specs=[pl.BlockSpec(memory_space=pltpu.HBM)] * len(inputs),
     )(*[pltpu.with_memory_space_constraint(x, pltpu.HBM) for x in inputs])
-    strip_a, strip_b = swapped(strip_a, ("gx",), 0), swapped(strip_b, ("gx",), 1, "parts")
+    strip_b, strip_a = swapped(strip_b, ("gx",), 1, "gz"), swapped(strip_a, ("gx",), 0)
     column_a, column_b = call(column_kernel, [packed, packed])(*held[:5])
     beside = ("gy", "gz")
     (columns,) = call(beside_kernel, [both])(swapped(column_a, beside, 0), swapped(column_b, beside, 1))
-    columns_b, columns_a = swapped(columns, ("gx",), 1, "gy"), swapped(columns, ("gx",), 0)
+    columns_b, columns_a = swapped(columns, ("gx",), 1, "gz"), swapped(columns, ("gx",), 0)
     block = (layers, 2 * ROWS, 2 * LANES)
     *powers, sums, ribbon = call(
         main_kernel,
         [(2,) + block] * (STEPS - 1) + [adjoint_rhs.shape, (2 * STEPS + 1, ROWS, 2 * LANES), (ribbons, 2 * ROWS, LANES)],
         [(2,) + block] * 3 + [block] * 2 + [block[1:]] * 2,
         cost_estimate=pl.CostEstimate(flops=200_000_000, bytes_accessed=8_000_000, transcendentals=0),
-    )(*held[:5], strip_a, strip_b)
+    )(*held[:5], strip_b, strip_a)
     edges, sums = call(
         ribbon_kernel,
         [(STEPS, 2, layers // 4) + tile, (2, 2 * ROWS, LANES)],

time: 32.7 us -> 31.5 us (0.963)
  waiting for transfers between devices: 9.52 us -> 8.27 us
    ppermute x6, waiting for transfers between devices: 7.04 us -> 6.07 us  [exchange(): parts.append(lax.ppermute(x, axis, pairs))]
  transfers between devices with their start and end apart: 12 -> 12, of which waited for: 6 -> 6; matrix products, arithmetic and copies ran while one was open for 0% -> 0% of each run, Pallas kernels for 13% -> 14%
where the time goes in v18:
time: 31.5 us; the launch traced here: 31.4 us
  starting transfers between devices  14.5 us (46%)
  waiting for transfers between devices  8.27 us (26%)
  Pallas kernels  7.94 us (25%)
  between operations  0.7 us (2%)
    ppermute x6, starting transfers between devices, swapped(): return lax.ppermute(x, (*axes, spare) if spare else axes, pairs)  8.1 us
    ppermute x6, starting transfers between devices, exchange(): parts.append(lax.ppermute(x, axis, pairs))  6.38 us
    ppermute x6, waiting for transfers between devices, exchange(): parts.append(lax.ppermute(x, axis, pairs))  6.07 us
    pallas_call x1, Pallas kernels, body(): call(main_kernel, [(2,) + block] * (STEPS - 1) + [adjoint_rhs.shape, (2 *...  4.15 us
    ppermute x6, waiting for transfers between devices, swapped(): return lax.ppermute(x, (*axes, spare) if spare else axes, pairs)  2.2 us
    pallas_call x1, Pallas kernels, body(): call(final_kernel, [adjoint_rhs.shape, adjoint_rhs.shape, friction.shape])  1.73 us
    pallas_call x1, Pallas kernels, body(): call(strip_kernel, [jax.ShapeDtypeStruct(x.shape, x.dtype) for x in input...  1.13 us
    pallas_call x1, Pallas kernels, body(): call(ribbon_kernel, [(STEPS, 2, layers // 4) + tile, (2, 2 * ROWS, LANES)])  0.72 us
  transfers between devices with their start and end apart: 12, of which 6 were waited for; matrix products, arithmetic and copies ran while one was open for 0% of the time, Pallas kernels for 14%

profile of v18, /device:TPU:0, one launch (start us, length us, event | category | flops | bytes accessed | tf_op | source)
XLA Modules:
  0.0 31.4 jit_solution(9363944350141291009)
XLA Ops:
  0.6 1.1 %shard_map.85 = (f32[2,20,8,256]{3,2,1,0:T(8,128)S(1)}, f32[20,8,256]{2,1,0:T(8,128)S(1)}, f32[8,256]{1,0:T(8,128)S(1)}, s32[8,256]{1,0:T(8,128)S(1)}, s32[8,256...) custom-call(f32[2,20,8,256]{3,2,1,0:T(8,128)} %refs_0_.1, ...), custom_call_target="tpu_custom_call" | custom-call | tf_op jit(solution)/shard_map/pallas_call | solution.py:612
  1.8 0.5 %collective-permute-start = (f32[62,8,128]{2,1,0:T(8,128)S(1)}, f32[62,8,128]{2,1,0:T(8,128)S(1)}, u32[]{:S(2)}, u32[]{:S(2)}) collective-permute-start(f32[62,8,128]{2,1,0:T(8,128)S(1)} %get-tuple-element.26), channel_id=1, source_target_pairs={{0,1},{4,8},{8,4},{12,13},{1,0},{5,9},{9,5},{13,12},{2,3},{6,10},{... | collective-permute-start | bytes 761864 | tf_op jit(solution)/shard_map/ppermute | solution.py:47
  2.3 4.1 %collective-permute-start.1 = (f32[62,8,128]{2,1,0:T(8,128)S(1)}, f32[62,8,128]{2,1,0:T(8,128)S(1)}, u32[]{:S(2)}, u32[]{:S(2)}) collective-permute-start(f32[62,8,128]{2,1,0:T(8,128)S(1)} %get-tuple-element.27), channel_id=1, source_target_pairs={{0,4},{4,0},{8,12},{12,8},{1,5},{5,1},{9,13},{13,9},{2,6},{6,2},{1... | collective-permute-start | bytes 761864 | tf_op jit(solution)/shard_map/ppermute | solution.py:47
  6.4 0.2 shard_map.87
  6.6 0.1 collective-permute-start.2
  6.7 1.6 %collective-permute-start.3 = (f32[3,8,128]{2,1,0:T(8,128)S(1)}, f32[3,8,128]{2,1,0:T(8,128)S(1)}, u32[]{:S(2)}, u32[]{:S(2)}) collective-permute-start(f32[3,8,128]{2,1,0:T(8,128)S(1)} %get-tuple-element.34), channel_id=1, source_target_pairs={{0,3},{1,2},{2,1},{3,0},{4,7},{5,6},{6,5},{7,4},{8,11},{9,10},{10,... | collective-permute-start | bytes 36872 | tf_op jit(solution)/shard_map/ppermute | solution.py:47
  8.3 0.0 collective-permute-done.2.from_a
  8.3 1.6 %collective-permute-done.3.from_b = f32[3,8,128]{2,1,0:T(8,128)S(1)} collective-permute-done((f32[3,8,128]{2,1,0:T(8,128)S(1)}, f32[3,8,128]{2,1,0:T(8,128)S(1)}, u32[]{:S(2)}, u32[]{:S(2)}) %collective-permute-start.3) | collective-permute-done | bytes 12320 | tf_op jit(solution)/shard_map/ppermute | solution.py:47
  9.9 0.7 %collective-permute-start.4 = (f32[6,8,128]{2,1,0:T(8,128)S(1)}, f32[6,8,128]{2,1,0:T(8,128)S(1)}, u32[]{:S(2)}, u32[]{:S(2)}) collective-permute-start(f32[6,8,128]{2,1,0:T(8,128)S(1)} %shard_map.88.columns), channel_id=1, source_target_pairs={{0,1},{4,8},{8,4},{12,13},{1,0},{5,9},{9,5},{13,12},{2,3},{6,10},{... | collective-permute-start | bytes 73736 | tf_op jit(solution)/shard_map/ppermute | solution.py:47
  10.6 1.0 %collective-permute-start.5 = (f32[6,8,128]{2,1,0:T(8,128)S(1)}, f32[6,8,128]{2,1,0:T(8,128)S(1)}, u32[]{:S(2)}, u32[]{:S(2)}) collective-permute-start(f32[6,8,128]{2,1,0:T(8,128)S(1)} %shard_map.88.columns), channel_id=1, source_target_pairs={{0,4},{4,0},{8,12},{12,8},{1,5},{5,1},{9,13},{13,9},{2,6},{6,2},{1... | collective-permute-start | bytes 73736 | tf_op jit(solution)/shard_map/ppermute | solution.py:47
  11.7 0.6 %collective-permute-done.1.strip_a = f32[62,8,128]{2,1,0:T(8,128)S(1)} collective-permute-done((f32[62,8,128]{2,1,0:T(8,128)S(1)}, f32[62,8,128]{2,1,0:T(8,128)S(1)}, u32[]{:S(2)}, u32[]{:S(2)}) %collective-permute-start.1) | collective-permute-done | bytes 253984 | tf_op jit(solution)/shard_map/ppermute | solution.py:47
  12.3 4.2 %shard_map.86 = (f32[2,20,16,256]{3,2,1,0:T(8,128)S(1)}, f32[2,20,16,256]{3,2,1,0:T(8,128)S(1)}, f32[2,20,16,256]{3,2,1,0:T(8,128)S(1)}, f32[2,20,8,256]{3,2,1,0...) custom-call(f32[2,20,8,256]{3,2,1,0:T(8,128)S(1)} %get-tuple-element.21.rhs, ...), custom_call_target="tpu_custom_call" | custom-call | flops 200000000 | bytes 8000000 | tf_op jit(solution)/shard_map/pallas_call | solution.py:624
  16.4 0.0 collective-permute-done.5.columns_a
  16.5 0.7 %shard_map.89 = (f32[4,2,5,8,128]{4,3,2,1,0:T(8,128)S(1)}, f32[2,16,128]{2,1,0:T(8,128)S(1)}) custom-call(f32[17,16,128]{2,1,0:T(8,128)S(1)} %get-tuple-element.32.ribbon, f32[6,8,128]{2,1,0:T(8,128)S(1)} %shard_map.88.columns, f32[6,8,128]{2,1,0:T(8,128)S(1)} %collective-permute-done.4.columns_b, f32[6,8,128]{2,1,0:T(8,128)S(1)} %collective-permute-done.5.columns_a, ...), custom_call_target="tpu_custom_call" | custom-call | tf_op jit(solution)/shard_map/pallas_call | solution.py:630
  17.2 0.6 %collective-permute-start.6 = (f32[2,16,128]{2,1,0:T(8,128)S(1)}, f32[2,16,128]{2,1,0:T(8,128)S(1)}, u32[]{:S(2)}, u32[]{:S(2)}) collective-permute-start(f32[2,16,128]{2,1,0:T(8,128)S(1)} %get-tuple-element.38.refs_0_), channel_id=1, source_target_pairs={{0,3},{1,2},{2,1},{3,0},{4,7},{5,6},{6,5},{7,4},{8,11},{9,10},{10,... | collective-permute-start | bytes 49160 | tf_op jit(solution)/shard_map/ppermute | solution.py:597
  17.8 1.0 %collective-permute-start.7 = (f32[2,16,128]{2,1,0:T(8,128)S(1)}, f32[2,16,128]{2,1,0:T(8,128)S(1)}, u32[]{:S(2)}, u32[]{:S(2)}) collective-permute-start(f32[2,16,128]{2,1,0:T(8,128)S(1)} %get-tuple-element.38.refs_0_), channel_id=1, source_target_pairs={{0,2},{1,3},{2,0},{3,1},{4,6},{5,7},{6,4},{7,5},{8,10},{9,11},{10,... | collective-permute-start | bytes 49160 | tf_op jit(solution)/shard_map/ppermute | solution.py:597
  18.8 0.3 collective-permute-start.8
  19.1 1.4 %collective-permute-done.6.refs_1_ = f32[2,16,128]{2,1,0:T(8,128)S(1)} collective-permute-done((f32[2,16,128]{2,1,0:T(8,128)S(1)}, f32[2,16,128]{2,1,0:T(8,128)S(1)}, u32[]{:S(2)}, u32[]{:S(2)}) %collective-permute-start.6) | collective-permute-done | bytes 16416 | tf_op jit(solution)/shard_map/ppermute | solution.py:597
  20.5 1.1 %collective-permute-done.7.refs_2_ = f32[2,16,128]{2,1,0:T(8,128)S(1)} collective-permute-done((f32[2,16,128]{2,1,0:T(8,128)S(1)}, f32[2,16,128]{2,1,0:T(8,128)S(1)}, u32[]{:S(2)}, u32[]{:S(2)}) %collective-permute-start.7) | collective-permute-done | bytes 16416 | tf_op jit(solution)/shard_map/ppermute | solution.py:597
  21.7 3.4 %collective-permute-start.9 = (f32[2,16,128]{2,1,0:T(8,128)S(1)}, f32[2,16,128]{2,1,0:T(8,128)S(1)}, u32[]{:S(2)}, u32[]{:S(2)}) collective-permute-start(f32[2,16,128]{2,1,0:T(8,128)S(1)} %shard_map.90.rest_0_), channel_id=1, source_target_pairs={{0,12},{4,8},{8,4},{12,0},{1,13},{5,9},{9,5},{13,1},{2,14},{6,10},... | collective-permute-start | bytes 49160 | tf_op jit(solution)/shard_map/ppermute | solution.py:597
  25.0 1.1 %collective-permute-start.11 = (f32[2,16,128]{2,1,0:T(8,128)S(1)}, f32[2,16,128]{2,1,0:T(8,128)S(1)}, u32[]{:S(2)}, u32[]{:S(2)}) collective-permute-start(f32[2,16,128]{2,1,0:T(8,128)S(1)} %shard_map.90.rest_0_), channel_id=1, source_target_pairs={{0,4},{4,0},{8,12},{12,8},{1,5},{5,1},{9,13},{13,9},{2,6},{6,2},{1... | collective-permute-start | bytes 49160 | tf_op jit(solution)/shard_map/ppermute | solution.py:597
  26.1 1.1 %collective-permute-done.9.rest_1_ = f32[2,16,128]{2,1,0:T(8,128)S(1)} collective-permute-done((f32[2,16,128]{2,1,0:T(8,128)S(1)}, f32[2,16,128]{2,1,0:T(8,128)S(1)}, u32[]{:S(2)}, u32[]{:S(2)}) %collective-permute-start.9) | collective-permute-done | bytes 16416 | tf_op jit(solution)/shard_map/ppermute | solution.py:597
  27.3 2.4 %collective-permute-done.10.rest_2_ = f32[2,16,128]{2,1,0:T(8,128)S(1)} collective-permute-done((f32[2,16,128]{2,1,0:T(8,128)S(1)}, f32[2,16,128]{2,1,0:T(8,128)S(1)}, u32[]{:S(2)}, u32[]{:S(2)}) %collective-permute-start.10) | collective-permute-done | bytes 16416 | tf_op jit(solution)/shard_map/ppermute | solution.py:597
  29.7 1.7 %shard_map.91 = (f32[2,20,8,256]{3,2,1,0:T(8,128)}, f32[2,20,8,256]{3,2,1,0:T(8,128)}, f32[8,256]{1,0:T(8,128)}) custom-call(f32[2,20,8,256]{3,2,1,0:T(8,128)S(1)} %get-tuple-element.21.rhs, f32[2,20,16,256]{3,2,1,0:T(8,128)S(1)} %get-tuple-element.28.power_1, f32[2,20,16,256]{3,2,1,0:T(8,128)S(1)} %get-tuple-element.29.power_2, ...), custom_call_target="tpu_custom_call" | custom-call | tf_op jit(solution)/shard_map/pallas_call | solution.py:640
  (7 shorter events, 0.0 us)
Async XLA Ops:
  1.8 9.9 %collective-permute-start = (f32[62,8,128]{2,1,0:T(8,128)S(1)}, f32[62,8,128]{2,1,0:T(8,128)S(1)}, u32[]{:S(2)}, u32[]{:S(2)}) collective-permute-start(f32[62,8,128]{2,1,0:T(8,128)S(1)} %get-tuple-element.26), channel_id=1, source_target_pairs={{0,1},{4,8},{8,4},{12,13},{1,0},{5,9},{9,5},{13,12},{2,3},{6,10},{... | collective-permute-start | bytes 761864 | tf_op jit(solution)/shard_map/ppermute | solution.py:47
  2.3 10.0 %collective-permute-start.1 = (f32[62,8,128]{2,1,0:T(8,128)S(1)}, f32[62,8,128]{2,1,0:T(8,128)S(1)}, u32[]{:S(2)}, u32[]{:S(2)}) collective-permute-start(f32[62,8,128]{2,1,0:T(8,128)S(1)} %get-tuple-element.27), channel_id=1, source_target_pairs={{0,4},{4,0},{8,12},{12,8},{1,5},{5,1},{9,13},{13,9},{2,6},{6,2},{1... | collective-permute-start | bytes 761864 | tf_op jit(solution)/shard_map/ppermute | solution.py:47
  6.6 1.7 %collective-permute-start.2 = (f32[3,8,128]{2,1,0:T(8,128)S(1)}, f32[3,8,128]{2,1,0:T(8,128)S(1)}, u32[]{:S(2)}, u32[]{:S(2)}) collective-permute-start(f32[3,8,128]{2,1,0:T(8,128)S(1)} %get-tuple-element.33), channel_id=1, source_target_pairs={{0,1},{1,0},{2,3},{3,2},{4,5},{5,4},{6,7},{7,6},{8,9},{9,8},{10,11... | collective-permute-start | bytes 36872 | tf_op jit(solution)/shard_map/ppermute | solution.py:47
  6.7 3.2 %collective-permute-start.3 = (f32[3,8,128]{2,1,0:T(8,128)S(1)}, f32[3,8,128]{2,1,0:T(8,128)S(1)}, u32[]{:S(2)}, u32[]{:S(2)}) collective-permute-start(f32[3,8,128]{2,1,0:T(8,128)S(1)} %get-tuple-element.34), channel_id=1, source_target_pairs={{0,3},{1,2},{2,1},{3,0},{4,7},{5,6},{6,5},{7,4},{8,11},{9,10},{10,... | collective-permute-start | bytes 36872 | tf_op jit(solution)/shard_map/ppermute | solution.py:47
  9.9 6.5 %collective-permute-start.4 = (f32[6,8,128]{2,1,0:T(8,128)S(1)}, f32[6,8,128]{2,1,0:T(8,128)S(1)}, u32[]{:S(2)}, u32[]{:S(2)}) collective-permute-start(f32[6,8,128]{2,1,0:T(8,128)S(1)} %shard_map.88.columns), channel_id=1, source_target_pairs={{0,1},{4,8},{8,4},{12,13},{1,0},{5,9},{9,5},{13,12},{2,3},{6,10},{... | collective-permute-start | bytes 73736 | tf_op jit(solution)/shard_map/ppermute | solution.py:47
  10.6 5.8 %collective-permute-start.5 = (f32[6,8,128]{2,1,0:T(8,128)S(1)}, f32[6,8,128]{2,1,0:T(8,128)S(1)}, u32[]{:S(2)}, u32[]{:S(2)}) collective-permute-start(f32[6,8,128]{2,1,0:T(8,128)S(1)} %shard_map.88.columns), channel_id=1, source_target_pairs={{0,4},{4,0},{8,12},{12,8},{1,5},{5,1},{9,13},{13,9},{2,6},{6,2},{1... | collective-permute-start | bytes 73736 | tf_op jit(solution)/shard_map/ppermute | solution.py:47
  17.2 3.4 %collective-permute-start.6 = (f32[2,16,128]{2,1,0:T(8,128)S(1)}, f32[2,16,128]{2,1,0:T(8,128)S(1)}, u32[]{:S(2)}, u32[]{:S(2)}) collective-permute-start(f32[2,16,128]{2,1,0:T(8,128)S(1)} %get-tuple-element.38.refs_0_), channel_id=1, source_target_pairs={{0,3},{1,2},{2,1},{3,0},{4,7},{5,6},{6,5},{7,4},{8,11},{9,10},{10,... | collective-permute-start | bytes 49160 | tf_op jit(solution)/shard_map/ppermute | solution.py:597
  17.8 3.8 %collective-permute-start.7 = (f32[2,16,128]{2,1,0:T(8,128)S(1)}, f32[2,16,128]{2,1,0:T(8,128)S(1)}, u32[]{:S(2)}, u32[]{:S(2)}) collective-permute-start(f32[2,16,128]{2,1,0:T(8,128)S(1)} %get-tuple-element.38.refs_0_), channel_id=1, source_target_pairs={{0,2},{1,3},{2,0},{3,1},{4,6},{5,7},{6,4},{7,5},{8,10},{9,11},{10,... | collective-permute-start | bytes 49160 | tf_op jit(solution)/shard_map/ppermute | solution.py:597
  18.8 2.8 %collective-permute-start.8 = (f32[2,16,128]{2,1,0:T(8,128)S(1)}, f32[2,16,128]{2,1,0:T(8,128)S(1)}, u32[]{:S(2)}, u32[]{:S(2)}) collective-permute-start(f32[2,16,128]{2,1,0:T(8,128)S(1)} %get-tuple-element.38.refs_0_), channel_id=1, source_target_pairs={{0,1},{1,0},{2,3},{3,2},{4,5},{5,4},{6,7},{7,6},{8,9},{9,8},{10,11... | collective-permute-start | bytes 49160 | tf_op jit(solution)/shard_map/ppermute | solution.py:597
  21.7 5.6 %collective-permute-start.9 = (f32[2,16,128]{2,1,0:T(8,128)S(1)}, f32[2,16,128]{2,1,0:T(8,128)S(1)}, u32[]{:S(2)}, u32[]{:S(2)}) collective-permute-start(f32[2,16,128]{2,1,0:T(8,128)S(1)} %shard_map.90.rest_0_), channel_id=1, source_target_pairs={{0,12},{4,8},{8,4},{12,0},{1,13},{5,9},{9,5},{13,1},{2,14},{6,10},... | collective-permute-start | bytes 49160 | tf_op jit(solution)/shard_map/ppermute | solution.py:597
  25.0 4.6 %collective-permute-start.10 = (f32[2,16,128]{2,1,0:T(8,128)S(1)}, f32[2,16,128]{2,1,0:T(8,128)S(1)}, u32[]{:S(2)}, u32[]{:S(2)}) collective-permute-start(f32[2,16,128]{2,1,0:T(8,128)S(1)} %shard_map.90.rest_0_), channel_id=1, source_target_pairs={{0,8},{4,12},{8,0},{12,4},{1,9},{5,13},{9,1},{13,5},{2,10},{6,14},... | collective-permute-start | bytes 49160 | tf_op jit(solution)/shard_map/ppermute | solution.py:597
  25.0 4.6 %collective-permute-start.11 = (f32[2,16,128]{2,1,0:T(8,128)S(1)}, f32[2,16,128]{2,1,0:T(8,128)S(1)}, u32[]{:S(2)}, u32[]{:S(2)}) collective-permute-start(f32[2,16,128]{2,1,0:T(8,128)S(1)} %shard_map.90.rest_0_), channel_id=1, source_target_pairs={{0,4},{4,0},{8,12},{12,8},{1,5},{5,1},{9,13},{13,9},{2,6},{6,2},{1... | collective-permute-start | bytes 49160 | tf_op jit(solution)/shard_map/ppermute | solution.py:597

commit v19 on v18

--- a/solution.py
+++ b/solution.py
@@ -173,12 +173,13 @@
 def beyond():
     even, has_a, has_b = place_of("gx")
     upper_a = (lax.broadcasted_iota(jnp.int32, (ROWS, LANES), 0) < HALO) == even
+    lower_a = jnp.logical_not(upper_a)
 
     def below_and_above(from_a, from_b):
-        return jnp.where(upper_a, jnp.where(has_a, from_a, 0.0), jnp.where(has_b, from_b, 0.0))
+        return jnp.where(upper_a & has_a, from_a, jnp.where(lower_a & has_b, from_b, 0.0))
 
     def above_and_below(from_a, from_b):
-        return jnp.where(upper_a, jnp.where(has_b, from_b, 0.0), jnp.where(has_a, from_a, 0.0))
+        return jnp.where(lower_a & has_a, from_a, jnp.where(upper_a & has_b, from_b, 0.0))
 
     return below_and_above, above_and_below
 
@@ -197,6 +198,35 @@
 
 def col_prev(v):
     return pltpu.roll(v, 1, 1)
+
+
+def ribbon_of(p, layers, head, tail, lane, strips):
+    tile, slots = ribbon_places(p, layers)
+    for slot in slots:
+        at = slot * SLOT
+        strips[tile] = jnp.where(between(lane, at, 8), turned(tail, at + 8), strips[tile])
+        strips[tile] = jnp.where(between(lane, at + 20, 8), turned(head, at + 20), strips[tile])
+
+
+def own_kernel(_, rhs, eta, friction, ice, grounded, ribbon, squares):
+    layers = eta.shape[0]
+    plane = own_planes(rhs, eta, friction, ice, grounded)
+    lane = lax.broadcasted_iota(jnp.int32, (ROWS, LANES), 1)
+    strips = [jnp.zeros((ROWS, LANES), jnp.float32)] * ribbon.shape[0]
+    for p in range(3 * layers + 2):
+        v = plane(p)
+        ribbon_of(p, layers, v[:, :LANES], v[:, LANES:], lane, strips)
+    for tile, v in enumerate(strips):
+        ribbon[tile] = v
+    bare = 1.0 - ice[...].astype(jnp.float32)
+    whole = jnp.zeros((ROWS, 2 * LANES), jnp.float32)
+    outside = jnp.zeros((ROWS, 2 * LANES), jnp.float32)
+    for c in range(2):
+        for k in range(layers):
+            square = rhs[c, k] * rhs[c, k]
+            whole = whole + square
+            outside = outside + bare * square
+    squares[0], squares[1] = whole, outside
 
 
 class Tiles:
@@ -285,23 +315,23 @@
 
 
 def main_kernel(
-    rhs, eta, friction, ice, grounded, strip_b, strip_a,
+    rhs, eta, friction, ice, grounded, squares, strip_b, strip_a,
     power_1, power_2, power_3, power_4, sums, ribbon,
     masked, eta_row, eta_col, eta_half, eta_up, cover, drag,
 ):
     layers = eta.shape[0]
     plane = own_planes(rhs, eta, friction, ice, grounded)
     below_and_above, above_and_below = beyond()
-    lane = lax.broadcasted_iota(jnp.int32, (2 * ROWS, LANES), 1)
+    lane = lax.broadcasted_iota(jnp.int32, (ROWS, LANES), 1)
 
     def target(p):
         if p < 2 * layers:
             return masked.at[p // layers, p % layers]
         if p < 3 * layers:
-            return eta_half.at[p - 2 * layers]
+            return eta_up.at[p - 2 * layers]
         return cover if p == 3 * layers else drag
 
-    strips = [jnp.zeros((2 * ROWS, LANES), jnp.float32) for _ in range(ribbon.shape[0])]
+    strips = [jnp.zeros((ROWS, LANES), jnp.float32)] * ribbon.shape[0]
     for q in range(strip_a.shape[0] // 2):
         first, second = pair_of(q, layers)
         halves = ([], [])
@@ -314,30 +344,24 @@
             dst = target(p)
             dst[0:ROWS, :] = v
             dst[ROWS:, 0:LANES], dst[ROWS:, LANES:] = halo
-            head = jnp.concatenate([v[:, :LANES], halo[0]], 0)
-            tail = jnp.concatenate([v[:, LANES:], halo[1]], 0)
-            tile, slots = ribbon_places(p, layers)
-            for slot in slots:
-                at = slot * SLOT
-                strips[tile] = jnp.where(between(lane, at, 8), turned(tail, at + 8), strips[tile])
-                strips[tile] = jnp.where(between(lane, at + 20, 8), turned(head, at + 20), strips[tile])
+            ribbon_of(p, layers, *halo, lane, strips)
     for tile, v in enumerate(strips):
         ribbon[tile] = v
 
     moves = Moves()
     load = Tiles.load
+    e = load(eta_up.at[0])
     for k in range(layers):
-        e = load(eta_half.at[k])
         pair = e + moves.row_next(e)
         (2.0 * pair).store(eta_row.at[0, k])
         (0.5 * pair).store(eta_row.at[1, k])
         pair = e + moves.col_next(e)
         (0.5 * pair).store(eta_col.at[0, k])
         (2.0 * pair).store(eta_col.at[1, k])
-        eta_up[k] = eta_half[k] + eta_half[k + 1] if k + 1 < layers else jnp.zeros_like(eta_up[k])
-        if k:
-            eta_half[k - 1] = 0.5 * eta_half[k - 1]
-    eta_half[layers - 1] = 0.5 * eta_half[layers - 1]
+        (0.5 * e).store(eta_half.at[k])
+        after = load(eta_up.at[k + 1]) if k + 1 < layers else None
+        (e + after if k + 1 < layers else 0.0 * e).store(eta_up.at[k])
+        e = after
 
     def apply(t, src, dst):
         def block(b, carry):
@@ -373,15 +397,8 @@
         ends = lax.fori_loop(0, layers // UNROLL, block, start)[4:]
         return [jnp.concatenate(v, 1) for v in ends]
 
-    bare = 1.0 - ice[...].astype(jnp.float32)
-    whole = jnp.zeros((ROWS, 2 * LANES), jnp.float32)
-    outside = jnp.zeros((ROWS, 2 * LANES), jnp.float32)
-    for c in range(2):
-        for k in range(layers):
-            square = rhs[c, k] * rhs[c, k]
-            whole = whole + square
-            outside = outside + bare * square
-    sums[0] = whole
+    outside = squares[1]
+    sums[0] = squares[0]
     wide = lax.broadcasted_iota(jnp.int32, (ROWS, 2 * LANES), 1)
     inner = between(wide, HALO, 2 * LANES - 2 * HALO)
     fields = (masked, power_1, power_2, power_3, power_4)
@@ -391,7 +408,7 @@
         sums[2 * t] = jnp.where(inner, even, 0.0) + outside
 
 
-def ribbon_kernel(ribbon, columns, columns_b, columns_a, sums, edges, moments):
+def ribbon_kernel(own, halo, columns, columns_b, columns_a, sums, edges, moments):
     tiles = edges.shape[2]
     below_and_above, _ = beyond()
     lane = lax.broadcasted_iota(jnp.int32, (2 * ROWS, LANES), 1)
@@ -404,7 +421,7 @@
 
     def whole(tile):
         group, at = packed_place(tile)
-        right = jnp.where(between(spot, 8, HALO), turned(beside[group], 8 - at), ribbon[tile])
+        right = jnp.where(between(spot, 8, HALO), turned(beside[group], 8 - at), jnp.concatenate([own[tile], halo[tile]], 0))
         return jnp.where(between(spot, 16, HALO), turned(beside[count + group], 16 - at), right)
 
     field = [[whole(c * tiles + n) for n in range(tiles)] for c in range(2)]
@@ -579,7 +596,7 @@
     hessian[...] = weight * (speed[0] * iterate[0, 0] + speed[1] * iterate[1, 0])
 
 
-def exchange(x, axis):
+def exchange(x, axis, order):
     count = lax.axis_size(axis)
     stride = 1
     rounds = []
@@ -589,7 +606,7 @@
         stride *= size
     for at, (stride, size) in enumerate(rounds):
         parts = [x]
-        for turn in range(size - 1, 0, -1):
+        for turn in order if size == 4 else (1,):
             pairs = []
             for i in range(count):
                 place = (i // stride) % size
@@ -621,20 +638,25 @@
     (columns,) = call(beside_kernel, [both])(swapped(column_a, beside, 0), swapped(column_b, beside, 1))
     columns_b, columns_a = swapped(columns, ("gx",), 1, "gz"), swapped(columns, ("gx",), 0)
     block = (layers, 2 * ROWS, 2 * LANES)
-    *powers, sums, ribbon = call(
+    own, squares = call(
+        own_kernel,
+        [(ribbons,) + tile, (2, ROWS, 2 * LANES)],
+        in_specs=[pl.BlockSpec(memory_space=pl.ANY)] + [pl.BlockSpec(memory_space=pltpu.VMEM)] * 5,
+    )(columns, *held[:5])
+    *powers, sums, halo = call(
         main_kernel,
-        [(2,) + block] * (STEPS - 1) + [adjoint_rhs.shape, (2 * STEPS + 1, ROWS, 2 * LANES), (ribbons, 2 * ROWS, LANES)],
+        [(2,) + block] * (STEPS - 1) + [adjoint_rhs.shape, (2 * STEPS + 1, ROWS, 2 * LANES), (ribbons,) + tile],
         [(2,) + block] * 3 + [block] * 2 + [block[1:]] * 2,
         cost_estimate=pl.CostEstimate(flops=200_000_000, bytes_accessed=8_000_000, transcendentals=0),
-    )(*held[:5], strip_b, strip_a)
+    )(*held[:5], squares, strip_b, strip_a)
     edges, sums = call(
         ribbon_kernel,
         [(STEPS, 2, layers // 4) + tile, (2, 2 * ROWS, LANES)],
-    )(ribbon, columns, columns_b, columns_a, sums)
-    parts = exchange(sums, ("gy", "gz"))
+    )(own, halo, columns, columns_b, columns_a, sums)
+    parts = exchange(sums, ("gy", "gz"), (3, 2, 1))
     if len(parts) > 1:
         sums = call(add_kernel, [sums.shape])(*parts)[0]
-    parts = exchange(sums, "gx")
+    parts = exchange(sums, "gx", (1, 2, 3))
     rhs, _, friction, ice_mask, grounded, speed = held
     return tuple(
         call(final_kernel, [adjoint_rhs.shape, adjoint_rhs.shape, friction.shape])(

time: 31.5 us -> 30.7 us (0.975)
  starting transfers between devices: 14.5 us -> 13.8 us
    ppermute x6, starting transfers between devices: 6.38 us -> 5.68 us  [exchange(): parts.append(lax.ppermute(x, axis, pairs))]
  transfers between devices with their start and end apart: 12 -> 12, of which waited for: 6 -> 7; matrix products, arithmetic and copies ran while one was open for 0% -> 0% of each run, Pallas kernels for 14% -> 14%
where the time goes in v19:
time: 30.7 us; the launch traced here: 30.6 us
  starting transfers between devices  13.8 us (45%)
  waiting for transfers between devices  8.07 us (26%)
  Pallas kernels  8.03 us (26%)
  between operations  0.71 us (2%)
    ppermute x6, starting transfers between devices, swapped(): return lax.ppermute(x, (*axes, spare) if spare else axes, pairs)  8.1 us
    ppermute x6, waiting for transfers between devices, exchange(): parts.append(lax.ppermute(x, axis, pairs))  6.13 us
    ppermute x6, starting transfers between devices, exchange(): parts.append(lax.ppermute(x, axis, pairs))  5.68 us
    pallas_call x1, Pallas kernels, body(): call(main_kernel, [(2,) + block] * (STEPS - 1) + [adjoint_rhs.shape, (2 *...  3.97 us
    ppermute x6, waiting for transfers between devices, swapped(): return lax.ppermute(x, (*axes, spare) if spare else axes, pairs)  1.95 us
    pallas_call x1, Pallas kernels, body(): call(final_kernel, [adjoint_rhs.shape, adjoint_rhs.shape, friction.shape])  1.76 us
    pallas_call x1, Pallas kernels, body(): call(strip_kernel, [jax.ShapeDtypeStruct(x.shape, x.dtype) for x in input...  1.13 us
    pallas_call x1, Pallas kernels, body(): call(ribbon_kernel, [(STEPS, 2, layers // 4) + tile, (2, 2 * ROWS, LANES)])  0.72 us
  transfers between devices with their start and end apart: 12, of which 7 were waited for; matrix products, arithmetic and copies ran while one was open for 0% of the time, Pallas kernels for 14%

profile of v19, /device:TPU:0, one launch (start us, length us, event | category | flops | bytes accessed | tf_op | source)
XLA Modules:
  0.0 30.6 jit_solution(18177506695475888181)
XLA Ops:
  0.6 1.1 %shard_map.85 = (f32[2,20,8,256]{3,2,1,0:T(8,128)S(1)}, f32[20,8,256]{2,1,0:T(8,128)S(1)}, f32[8,256]{1,0:T(8,128)S(1)}, s32[8,256]{1,0:T(8,128)S(1)}, s32[8,256...) custom-call(f32[2,20,8,256]{3,2,1,0:T(8,128)} %refs_0_.1, ...), custom_call_target="tpu_custom_call" | custom-call | tf_op jit(solution)/shard_map/pallas_call | solution.py:629
  1.8 0.5 %collective-permute-start.2 = (f32[62,8,128]{2,1,0:T(8,128)S(1)}, f32[62,8,128]{2,1,0:T(8,128)S(1)}, u32[]{:S(2)}, u32[]{:S(2)}) collective-permute-start(f32[62,8,128]{2,1,0:T(8,128)S(1)} %get-tuple-element.31), channel_id=1, source_target_pairs={{0,1},{4,8},{8,4},{12,13},{1,0},{5,9},{9,5},{13,12},{2,3},{6,10},{... | collective-permute-start | bytes 761864 | tf_op jit(solution)/shard_map/ppermute | solution.py:47
  2.3 4.1 %collective-permute-start.3 = (f32[62,8,128]{2,1,0:T(8,128)S(1)}, f32[62,8,128]{2,1,0:T(8,128)S(1)}, u32[]{:S(2)}, u32[]{:S(2)}) collective-permute-start(f32[62,8,128]{2,1,0:T(8,128)S(1)} %get-tuple-element.32), channel_id=1, source_target_pairs={{0,4},{4,0},{8,12},{12,8},{1,5},{5,1},{9,13},{13,9},{2,6},{6,2},{1... | collective-permute-start | bytes 761864 | tf_op jit(solution)/shard_map/ppermute | solution.py:47
  6.4 0.2 shard_map.86
  6.7 1.6 %collective-permute-start.1 = (f32[3,8,128]{2,1,0:T(8,128)S(1)}, f32[3,8,128]{2,1,0:T(8,128)S(1)}, u32[]{:S(2)}, u32[]{:S(2)}) collective-permute-start(f32[3,8,128]{2,1,0:T(8,128)S(1)} %get-tuple-element.29), channel_id=1, source_target_pairs={{0,3},{1,2},{2,1},{3,0},{4,7},{5,6},{6,5},{7,4},{8,11},{9,10},{10,... | collective-permute-start | bytes 36872 | tf_op jit(solution)/shard_map/ppermute | solution.py:47
  8.3 1.6 %collective-permute-done.1.from_b = f32[3,8,128]{2,1,0:T(8,128)S(1)} collective-permute-done((f32[3,8,128]{2,1,0:T(8,128)S(1)}, f32[3,8,128]{2,1,0:T(8,128)S(1)}, u32[]{:S(2)}, u32[]{:S(2)}) %collective-permute-start.1) | collective-permute-done | bytes 12320 | tf_op jit(solution)/shard_map/ppermute | solution.py:47
  9.9 0.7 %collective-permute-start.4 = (f32[6,8,128]{2,1,0:T(8,128)S(1)}, f32[6,8,128]{2,1,0:T(8,128)S(1)}, u32[]{:S(2)}, u32[]{:S(2)}) collective-permute-start(f32[6,8,128]{2,1,0:T(8,128)S(1)} %shard_map.87._.columns), channel_id=1, source_target_pairs={{0,1},{4,8},{8,4},{12,13},{1,0},{5,9},{9,5},{13,12},{2,3},{6,10},{... | collective-permute-start | bytes 73736 | tf_op jit(solution)/shard_map/ppermute | solution.py:47
  10.6 1.0 %collective-permute-start.5 = (f32[6,8,128]{2,1,0:T(8,128)S(1)}, f32[6,8,128]{2,1,0:T(8,128)S(1)}, u32[]{:S(2)}, u32[]{:S(2)}) collective-permute-start(f32[6,8,128]{2,1,0:T(8,128)S(1)} %shard_map.87._.columns), channel_id=1, source_target_pairs={{0,4},{4,0},{8,12},{12,8},{1,5},{5,1},{9,13},{13,9},{2,6},{6,2},{1... | collective-permute-start | bytes 73736 | tf_op jit(solution)/shard_map/ppermute | solution.py:47
  11.7 0.2 shard_map.88
  11.9 0.4 %collective-permute-done.3.strip_a = f32[62,8,128]{2,1,0:T(8,128)S(1)} collective-permute-done((f32[62,8,128]{2,1,0:T(8,128)S(1)}, f32[62,8,128]{2,1,0:T(8,128)S(1)}, u32[]{:S(2)}, u32[]{:S(2)}) %collective-permute-start.3) | collective-permute-done | bytes 253984 | tf_op jit(solution)/shard_map/ppermute | solution.py:47
  12.3 4.0 %shard_map.89 = (f32[2,20,16,256]{3,2,1,0:T(8,128)S(1)}, f32[2,20,16,256]{3,2,1,0:T(8,128)S(1)}, f32[2,20,16,256]{3,2,1,0:T(8,128)S(1)}, f32[2,20,8,256]{3,2,1,0...) custom-call(f32[2,20,8,256]{3,2,1,0:T(8,128)S(1)} %get-tuple-element.23.rhs, ...), custom_call_target="tpu_custom_call" | custom-call | flops 200000000 | bytes 8000000 | tf_op jit(solution)/shard_map/pallas_call | solution.py:646
  16.3 0.7 %shard_map.90 = (f32[4,2,5,8,128]{4,3,2,1,0:T(8,128)S(1)}, f32[2,16,128]{2,1,0:T(8,128)S(1)}) custom-call(f32[17,8,128]{2,1,0:T(8,128)S(1)} %get-tuple-element.37.own, f32[17,8,128]{2,1,0:T(8,128)S(1)} %get-tuple-element.38.halo, f32[6,8,128]{2,1,0:T(8,128)S(1)} %shard_map.87._.columns, f32[6,8,128]{2,1,0:T(8,128)S(1)} %collective-permute-done.4.columns_b, ...), custom_call_target="tpu_custom_call" | custom-call | tf_op jit(solution)/shard_map/pallas_call | solution.py:652
  17.0 0.9 %collective-permute-start.6 = (f32[2,16,128]{2,1,0:T(8,128)S(1)}, f32[2,16,128]{2,1,0:T(8,128)S(1)}, u32[]{:S(2)}, u32[]{:S(2)}) collective-permute-start(f32[2,16,128]{2,1,0:T(8,128)S(1)} %get-tuple-element.42.refs_0_), channel_id=1, source_target_pairs={{0,3},{1,2},{2,1},{3,0},{4,7},{5,6},{6,5},{7,4},{8,11},{9,10},{10,... | collective-permute-start | bytes 49160 | tf_op jit(solution)/shard_map/ppermute | solution.py:614
  17.9 0.7 %collective-permute-start.7 = (f32[2,16,128]{2,1,0:T(8,128)S(1)}, f32[2,16,128]{2,1,0:T(8,128)S(1)}, u32[]{:S(2)}, u32[]{:S(2)}) collective-permute-start(f32[2,16,128]{2,1,0:T(8,128)S(1)} %get-tuple-element.42.refs_0_), channel_id=1, source_target_pairs={{0,2},{1,3},{2,0},{3,1},{4,6},{5,7},{6,4},{7,5},{8,10},{9,11},{10,... | collective-permute-start | bytes 49160 | tf_op jit(solution)/shard_map/ppermute | solution.py:614
  18.6 0.3 collective-permute-start.8
  18.9 1.4 %collective-permute-done.6.refs_1_ = f32[2,16,128]{2,1,0:T(8,128)S(1)} collective-permute-done((f32[2,16,128]{2,1,0:T(8,128)S(1)}, f32[2,16,128]{2,1,0:T(8,128)S(1)}, u32[]{:S(2)}, u32[]{:S(2)}) %collective-permute-start.6) | collective-permute-done | bytes 16416 | tf_op jit(solution)/shard_map/ppermute | solution.py:614
  20.4 1.3 %collective-permute-done.7.refs_2_ = f32[2,16,128]{2,1,0:T(8,128)S(1)} collective-permute-done((f32[2,16,128]{2,1,0:T(8,128)S(1)}, f32[2,16,128]{2,1,0:T(8,128)S(1)}, u32[]{:S(2)}, u32[]{:S(2)}) %collective-permute-start.7) | collective-permute-done | bytes 16416 | tf_op jit(solution)/shard_map/ppermute | solution.py:614
  21.7 1.3 %collective-permute-start.10 = (f32[2,16,128]{2,1,0:T(8,128)S(1)}, f32[2,16,128]{2,1,0:T(8,128)S(1)}, u32[]{:S(2)}, u32[]{:S(2)}) collective-permute-start(f32[2,16,128]{2,1,0:T(8,128)S(1)} %shard_map.91.rest_0_), channel_id=1, source_target_pairs={{0,8},{4,12},{8,0},{12,4},{1,9},{5,13},{9,1},{13,5},{2,10},{6,14},... | collective-permute-start | bytes 49160 | tf_op jit(solution)/shard_map/ppermute | solution.py:614
  23.0 2.1 %collective-permute-start.11 = (f32[2,16,128]{2,1,0:T(8,128)S(1)}, f32[2,16,128]{2,1,0:T(8,128)S(1)}, u32[]{:S(2)}, u32[]{:S(2)}) collective-permute-start(f32[2,16,128]{2,1,0:T(8,128)S(1)} %shard_map.91.rest_0_), channel_id=1, source_target_pairs={{0,12},{4,8},{8,4},{12,0},{1,13},{5,9},{9,5},{13,1},{2,14},{6,10},... | collective-permute-start | bytes 49160 | tf_op jit(solution)/shard_map/ppermute | solution.py:614
  25.1 0.3 %collective-permute-start.9 = (f32[2,16,128]{2,1,0:T(8,128)S(1)}, f32[2,16,128]{2,1,0:T(8,128)S(1)}, u32[]{:S(2)}, u32[]{:S(2)}) collective-permute-start(f32[2,16,128]{2,1,0:T(8,128)S(1)} %shard_map.91.rest_0_), channel_id=1, source_target_pairs={{0,4},{4,0},{8,12},{12,8},{1,5},{5,1},{9,13},{13,9},{2,6},{6,2},{1... | collective-permute-start | bytes 49160 | tf_op jit(solution)/shard_map/ppermute | solution.py:614
  25.4 1.0 %collective-permute-done.10.rest_2_ = f32[2,16,128]{2,1,0:T(8,128)S(1)} collective-permute-done((f32[2,16,128]{2,1,0:T(8,128)S(1)}, f32[2,16,128]{2,1,0:T(8,128)S(1)}, u32[]{:S(2)}, u32[]{:S(2)}) %collective-permute-start.10) | collective-permute-done | bytes 16416 | tf_op jit(solution)/shard_map/ppermute | solution.py:614
  26.4 2.2 %collective-permute-done.11.rest_3_ = f32[2,16,128]{2,1,0:T(8,128)S(1)} collective-permute-done((f32[2,16,128]{2,1,0:T(8,128)S(1)}, f32[2,16,128]{2,1,0:T(8,128)S(1)}, u32[]{:S(2)}, u32[]{:S(2)}) %collective-permute-start.11) | collective-permute-done | bytes 16416 | tf_op jit(solution)/shard_map/ppermute | solution.py:614
  28.6 0.2 collective-permute-done.9.rest_1_
  28.8 1.8 %shard_map.92 = (f32[2,20,8,256]{3,2,1,0:T(8,128)}, f32[2,20,8,256]{3,2,1,0:T(8,128)}, f32[8,256]{1,0:T(8,128)}) custom-call(f32[2,20,8,256]{3,2,1,0:T(8,128)S(1)} %get-tuple-element.23.rhs, f32[2,20,16,256]{3,2,1,0:T(8,128)S(1)} %get-tuple-element.33.power_1, f32[2,20,16,256]{3,2,1,0:T(8,128)S(1)} %get-tuple-element.34.power_2, ...), custom_call_target="tpu_custom_call" | custom-call | tf_op jit(solution)/shard_map/pallas_call | solution.py:662
  (8 shorter events, 0.1 us)
Async XLA Ops:
  1.8 10.1 %collective-permute-start.2 = (f32[62,8,128]{2,1,0:T(8,128)S(1)}, f32[62,8,128]{2,1,0:T(8,128)S(1)}, u32[]{:S(2)}, u32[]{:S(2)}) collective-permute-start(f32[62,8,128]{2,1,0:T(8,128)S(1)} %get-tuple-element.31), channel_id=1, source_target_pairs={{0,1},{4,8},{8,4},{12,13},{1,0},{5,9},{9,5},{13,12},{2,3},{6,10},{... | collective-permute-start | bytes 761864 | tf_op jit(solution)/shard_map/ppermute | solution.py:47
  2.3 10.0 %collective-permute-start.3 = (f32[62,8,128]{2,1,0:T(8,128)S(1)}, f32[62,8,128]{2,1,0:T(8,128)S(1)}, u32[]{:S(2)}, u32[]{:S(2)}) collective-permute-start(f32[62,8,128]{2,1,0:T(8,128)S(1)} %get-tuple-element.32), channel_id=1, source_target_pairs={{0,4},{4,0},{8,12},{12,8},{1,5},{5,1},{9,13},{13,9},{2,6},{6,2},{1... | collective-permute-start | bytes 761864 | tf_op jit(solution)/shard_map/ppermute | solution.py:47
  6.6 1.7 %collective-permute-start = (f32[3,8,128]{2,1,0:T(8,128)S(1)}, f32[3,8,128]{2,1,0:T(8,128)S(1)}, u32[]{:S(2)}, u32[]{:S(2)}) collective-permute-start(f32[3,8,128]{2,1,0:T(8,128)S(1)} %get-tuple-element.28), channel_id=1, source_target_pairs={{0,1},{1,0},{2,3},{3,2},{4,5},{5,4},{6,7},{7,6},{8,9},{9,8},{10,11... | collective-permute-start | bytes 36872 | tf_op jit(solution)/shard_map/ppermute | solution.py:47
  6.7 3.2 %collective-permute-start.1 = (f32[3,8,128]{2,1,0:T(8,128)S(1)}, f32[3,8,128]{2,1,0:T(8,128)S(1)}, u32[]{:S(2)}, u32[]{:S(2)}) collective-permute-start(f32[3,8,128]{2,1,0:T(8,128)S(1)} %get-tuple-element.29), channel_id=1, source_target_pairs={{0,3},{1,2},{2,1},{3,0},{4,7},{5,6},{6,5},{7,4},{8,11},{9,10},{10,... | collective-permute-start | bytes 36872 | tf_op jit(solution)/shard_map/ppermute | solution.py:47
  9.9 6.4 %collective-permute-start.4 = (f32[6,8,128]{2,1,0:T(8,128)S(1)}, f32[6,8,128]{2,1,0:T(8,128)S(1)}, u32[]{:S(2)}, u32[]{:S(2)}) collective-permute-start(f32[6,8,128]{2,1,0:T(8,128)S(1)} %shard_map.87._.columns), channel_id=1, source_target_pairs={{0,1},{4,8},{8,4},{12,13},{1,0},{5,9},{9,5},{13,12},{2,3},{6,10},{... | collective-permute-start | bytes 73736 | tf_op jit(solution)/shard_map/ppermute | solution.py:47
  10.6 5.6 %collective-permute-start.5 = (f32[6,8,128]{2,1,0:T(8,128)S(1)}, f32[6,8,128]{2,1,0:T(8,128)S(1)}, u32[]{:S(2)}, u32[]{:S(2)}) collective-permute-start(f32[6,8,128]{2,1,0:T(8,128)S(1)} %shard_map.87._.columns), channel_id=1, source_target_pairs={{0,4},{4,0},{8,12},{12,8},{1,5},{5,1},{9,13},{13,9},{2,6},{6,2},{1... | collective-permute-start | bytes 73736 | tf_op jit(solution)/shard_map/ppermute | solution.py:47
  17.0 3.4 %collective-permute-start.6 = (f32[2,16,128]{2,1,0:T(8,128)S(1)}, f32[2,16,128]{2,1,0:T(8,128)S(1)}, u32[]{:S(2)}, u32[]{:S(2)}) collective-permute-start(f32[2,16,128]{2,1,0:T(8,128)S(1)} %get-tuple-element.42.refs_0_), channel_id=1, source_target_pairs={{0,3},{1,2},{2,1},{3,0},{4,7},{5,6},{6,5},{7,4},{8,11},{9,10},{10,... | collective-permute-start | bytes 49160 | tf_op jit(solution)/shard_map/ppermute | solution.py:614
  17.9 3.7 %collective-permute-start.7 = (f32[2,16,128]{2,1,0:T(8,128)S(1)}, f32[2,16,128]{2,1,0:T(8,128)S(1)}, u32[]{:S(2)}, u32[]{:S(2)}) collective-permute-start(f32[2,16,128]{2,1,0:T(8,128)S(1)} %get-tuple-element.42.refs_0_), channel_id=1, source_target_pairs={{0,2},{1,3},{2,0},{3,1},{4,6},{5,7},{6,4},{7,5},{8,10},{9,11},{10,... | collective-permute-start | bytes 49160 | tf_op jit(solution)/shard_map/ppermute | solution.py:614
  18.6 3.0 %collective-permute-start.8 = (f32[2,16,128]{2,1,0:T(8,128)S(1)}, f32[2,16,128]{2,1,0:T(8,128)S(1)}, u32[]{:S(2)}, u32[]{:S(2)}) collective-permute-start(f32[2,16,128]{2,1,0:T(8,128)S(1)} %get-tuple-element.42.refs_0_), channel_id=1, source_target_pairs={{0,1},{1,0},{2,3},{3,2},{4,5},{5,4},{6,7},{7,6},{8,9},{9,8},{10,11... | collective-permute-start | bytes 49160 | tf_op jit(solution)/shard_map/ppermute | solution.py:614
  21.7 4.7 %collective-permute-start.10 = (f32[2,16,128]{2,1,0:T(8,128)S(1)}, f32[2,16,128]{2,1,0:T(8,128)S(1)}, u32[]{:S(2)}, u32[]{:S(2)}) collective-permute-start(f32[2,16,128]{2,1,0:T(8,128)S(1)} %shard_map.91.rest_0_), channel_id=1, source_target_pairs={{0,8},{4,12},{8,0},{12,4},{1,9},{5,13},{9,1},{13,5},{2,10},{6,14},... | collective-permute-start | bytes 49160 | tf_op jit(solution)/shard_map/ppermute | solution.py:614
  23.0 5.6 %collective-permute-start.11 = (f32[2,16,128]{2,1,0:T(8,128)S(1)}, f32[2,16,128]{2,1,0:T(8,128)S(1)}, u32[]{:S(2)}, u32[]{:S(2)}) collective-permute-start(f32[2,16,128]{2,1,0:T(8,128)S(1)} %shard_map.91.rest_0_), channel_id=1, source_target_pairs={{0,12},{4,8},{8,4},{12,0},{1,13},{5,9},{9,5},{13,1},{2,14},{6,10},... | collective-permute-start | bytes 49160 | tf_op jit(solution)/shard_map/ppermute | solution.py:614
  25.1 3.7 %collective-permute-start.9 = (f32[2,16,128]{2,1,0:T(8,128)S(1)}, f32[2,16,128]{2,1,0:T(8,128)S(1)}, u32[]{:S(2)}, u32[]{:S(2)}) collective-permute-start(f32[2,16,128]{2,1,0:T(8,128)S(1)} %shard_map.91.rest_0_), channel_id=1, source_target_pairs={{0,4},{4,0},{8,12},{12,8},{1,5},{5,1},{9,13},{13,9},{2,6},{6,2},{1... | collective-permute-start | bytes 49160 | tf_op jit(solution)/shard_map/ppermute | solution.py:614

commit v20 on v19

--- a/solution.py
+++ b/solution.py
@@ -470,21 +470,34 @@
             pair = join(pair, tuple(pltpu.roll(v, step, 0) for v in pair))
         high = jnp.where(tall == j, jnp.concatenate([pair[0]] * 2, 0), high)
         low = jnp.where(tall == j, jnp.concatenate([pair[1]] * 2, 0), low)
-    moments[0] = high
-    moments[1] = low
+    total = (high, low)
+    for step in (64, 32):
+        total = join(total, tuple(pltpu.roll(v, step, 1) for v in total))
+    group = lax.broadcasted_iota(jnp.int32, (ROWS, LANES), 1) // 32
+    parts = [total[0][:ROWS], total[1][:ROWS], total[0][ROWS:], total[1][ROWS:]]
+    moments[...] = jnp.where(
+        group == 0, parts[0], jnp.where(group == 1, parts[1], jnp.where(group == 2, parts[2], parts[3]))
+    )
+
+
+def added(parts):
+    terms = [(v, turned(v, -32)) for v in parts]
+    return join(join(terms[0], terms[1]), join(terms[2], terms[3])) if len(terms) == 4 else join(*terms)
 
 
 def add_kernel(*refs):
     *ins, out = refs
-    total = (ins[0][0], ins[0][1])
-    for x in ins[1:]:
-        total = join(total, (x[0], x[1]))
-    out[0], out[1] = total
+    high, low = added([x[...] for x in ins])
+    lane = lax.broadcasted_iota(jnp.int32, (ROWS, LANES), 1)
+    out[...] = jnp.where(lane % 64 < 32, high, turned(low, 32))
 
 
 def solve(total):
-    for step in (64, 32, 16, 8, 4, 2, 1):
+    for step in (16, 8, 4, 2, 1):
         total = join(total, tuple(pltpu.roll(v, step, 1) for v in total))
+    total = tuple(
+        jnp.concatenate([jnp.broadcast_to(v[:, i : i + 1], (ROWS, LANES)) for i in (31, 95)], 0) for v in total
+    )
 
     def spread(v, j):
         return jnp.broadcast_to(v[j : j + 1], (ROWS, LANES))
@@ -559,10 +572,7 @@
 def final_kernel(rhs, power_1, power_2, power_3, power_4, edges, friction, ice, grounded, speed, *rest):
     *parts, iterate, residual, hessian = rest
     layers, tiles = rhs.shape[1], edges.shape[2]
-    total = (parts[0][0], parts[0][1])
-    for x in parts[1:]:
-        total = join(total, (x[0], x[1]))
-    factors = solve(total)
+    factors = solve(added([x[...] for x in parts]))
     powers = (power_1, power_2, power_3, power_4)
     wide = [jnp.concatenate([c, c], 1) for c in factors]
     rest = sum(wide[1:], wide[0])
@@ -651,7 +661,7 @@
     )(*held[:5], squares, strip_b, strip_a)
     edges, sums = call(
         ribbon_kernel,
-        [(STEPS, 2, layers // 4) + tile, (2, 2 * ROWS, LANES)],
+        [(STEPS, 2, layers // 4) + tile, tile],
     )(own, halo, columns, columns_b, columns_a, sums)
     parts = exchange(sums, ("gy", "gz"), (3, 2, 1))
     if len(parts) > 1:

time: 30.7 us -> 30.7 us (level)
  no operation moved by 1% of the time
where the time goes in v20:
time: 30.7 us; the launch traced here: 30.5 us
  starting transfers between devices  13.7 us (45%)
  Pallas kernels  8.29 us (27%)
  waiting for transfers between devices  7.84 us (26%)
  between operations  0.7 us (2%)
    ppermute x6, starting transfers between devices, swapped(): return lax.ppermute(x, (*axes, spare) if spare else axes, pairs)  8.1 us
    ppermute x6, waiting for transfers between devices, exchange(): parts.append(lax.ppermute(x, axis, pairs))  5.89 us
    ppermute x6, starting transfers between devices, exchange(): parts.append(lax.ppermute(x, axis, pairs))  5.59 us
    pallas_call x1, Pallas kernels, body(): call(main_kernel, [(2,) + block] * (STEPS - 1) + [adjoint_rhs.shape, (2 *...  3.97 us
    ppermute x6, waiting for transfers between devices, swapped(): return lax.ppermute(x, (*axes, spare) if spare else axes, pairs)  1.95 us
    pallas_call x1, Pallas kernels, body(): call(final_kernel, [adjoint_rhs.shape, adjoint_rhs.shape, friction.shape])  1.74 us
    pallas_call x1, Pallas kernels, body(): call(strip_kernel, [jax.ShapeDtypeStruct(x.shape, x.dtype) for x in input...  1.13 us
    pallas_call x1, Pallas kernels, body(): call(ribbon_kernel, [(STEPS, 2, layers // 4) + tile, tile])  0.86 us
  transfers between devices with their start and end apart: 12, of which 7 were waited for; matrix products, arithmetic and copies ran while one was open for 0% of the time, Pallas kernels for 14%

profile of v20, /device:TPU:0, one launch (start us, length us, event | category | flops | bytes accessed | tf_op | source)
XLA Modules:
  0.0 30.5 jit_solution(8892652641200395533)
XLA Ops:
  0.6 1.1 %shard_map.85 = (f32[2,20,8,256]{3,2,1,0:T(8,128)S(1)}, f32[20,8,256]{2,1,0:T(8,128)S(1)}, f32[8,256]{1,0:T(8,128)S(1)}, s32[8,256]{1,0:T(8,128)S(1)}, s32[8,256...) custom-call(f32[2,20,8,256]{3,2,1,0:T(8,128)} %refs_0_.1, ...), custom_call_target="tpu_custom_call" | custom-call | tf_op jit(solution)/shard_map/pallas_call | solution.py:639
  1.8 0.5 %collective-permute-start.2 = (f32[62,8,128]{2,1,0:T(8,128)S(1)}, f32[62,8,128]{2,1,0:T(8,128)S(1)}, u32[]{:S(2)}, u32[]{:S(2)}) collective-permute-start(f32[62,8,128]{2,1,0:T(8,128)S(1)} %get-tuple-element.31), channel_id=1, source_target_pairs={{0,1},{4,8},{8,4},{12,13},{1,0},{5,9},{9,5},{13,12},{2,3},{6,10},{... | collective-permute-start | bytes 761864 | tf_op jit(solution)/shard_map/ppermute | solution.py:47
  2.3 4.1 %collective-permute-start.3 = (f32[62,8,128]{2,1,0:T(8,128)S(1)}, f32[62,8,128]{2,1,0:T(8,128)S(1)}, u32[]{:S(2)}, u32[]{:S(2)}) collective-permute-start(f32[62,8,128]{2,1,0:T(8,128)S(1)} %get-tuple-element.32), channel_id=1, source_target_pairs={{0,4},{4,0},{8,12},{12,8},{1,5},{5,1},{9,13},{13,9},{2,6},{6,2},{1... | collective-permute-start | bytes 761864 | tf_op jit(solution)/shard_map/ppermute | solution.py:47
  6.4 0.2 shard_map.86
  6.7 1.6 %collective-permute-start.1 = (f32[3,8,128]{2,1,0:T(8,128)S(1)}, f32[3,8,128]{2,1,0:T(8,128)S(1)}, u32[]{:S(2)}, u32[]{:S(2)}) collective-permute-start(f32[3,8,128]{2,1,0:T(8,128)S(1)} %get-tuple-element.29), channel_id=1, source_target_pairs={{0,3},{1,2},{2,1},{3,0},{4,7},{5,6},{6,5},{7,4},{8,11},{9,10},{10,... | collective-permute-start | bytes 36872 | tf_op jit(solution)/shard_map/ppermute | solution.py:47
  8.3 1.6 %collective-permute-done.1.from_b = f32[3,8,128]{2,1,0:T(8,128)S(1)} collective-permute-done((f32[3,8,128]{2,1,0:T(8,128)S(1)}, f32[3,8,128]{2,1,0:T(8,128)S(1)}, u32[]{:S(2)}, u32[]{:S(2)}) %collective-permute-start.1) | collective-permute-done | bytes 12320 | tf_op jit(solution)/shard_map/ppermute | solution.py:47
  9.9 0.7 %collective-permute-start.4 = (f32[6,8,128]{2,1,0:T(8,128)S(1)}, f32[6,8,128]{2,1,0:T(8,128)S(1)}, u32[]{:S(2)}, u32[]{:S(2)}) collective-permute-start(f32[6,8,128]{2,1,0:T(8,128)S(1)} %shard_map.87._.columns), channel_id=1, source_target_pairs={{0,1},{4,8},{8,4},{12,13},{1,0},{5,9},{9,5},{13,12},{2,3},{6,10},{... | collective-permute-start | bytes 73736 | tf_op jit(solution)/shard_map/ppermute | solution.py:47
  10.6 1.0 %collective-permute-start.5 = (f32[6,8,128]{2,1,0:T(8,128)S(1)}, f32[6,8,128]{2,1,0:T(8,128)S(1)}, u32[]{:S(2)}, u32[]{:S(2)}) collective-permute-start(f32[6,8,128]{2,1,0:T(8,128)S(1)} %shard_map.87._.columns), channel_id=1, source_target_pairs={{0,4},{4,0},{8,12},{12,8},{1,5},{5,1},{9,13},{13,9},{2,6},{6,2},{1... | collective-permute-start | bytes 73736 | tf_op jit(solution)/shard_map/ppermute | solution.py:47
  11.7 0.2 shard_map.88
  11.9 0.4 %collective-permute-done.3.strip_a = f32[62,8,128]{2,1,0:T(8,128)S(1)} collective-permute-done((f32[62,8,128]{2,1,0:T(8,128)S(1)}, f32[62,8,128]{2,1,0:T(8,128)S(1)}, u32[]{:S(2)}, u32[]{:S(2)}) %collective-permute-start.3) | collective-permute-done | bytes 253984 | tf_op jit(solution)/shard_map/ppermute | solution.py:47
  12.3 4.0 %shard_map.89 = (f32[2,20,16,256]{3,2,1,0:T(8,128)S(1)}, f32[2,20,16,256]{3,2,1,0:T(8,128)S(1)}, f32[2,20,16,256]{3,2,1,0:T(8,128)S(1)}, f32[2,20,8,256]{3,2,1,0...) custom-call(f32[2,20,8,256]{3,2,1,0:T(8,128)S(1)} %get-tuple-element.23.rhs, ...), custom_call_target="tpu_custom_call" | custom-call | flops 200000000 | bytes 8000000 | tf_op jit(solution)/shard_map/pallas_call | solution.py:656
  16.3 0.9 %shard_map.90 = (f32[4,2,5,8,128]{4,3,2,1,0:T(8,128)S(1)}, f32[8,128]{1,0:T(8,128)S(1)}) custom-call(f32[17,8,128]{2,1,0:T(8,128)S(1)} %get-tuple-element.37.own, f32[17,8,128]{2,1,0:T(8,128)S(1)} %get-tuple-element.38.halo, f32[6,8,128]{2,1,0:T(8,128)S(1)} %shard_map.87._.columns, f32[6,8,128]{2,1,0:T(8,128)S(1)} %collective-permute-done.4.columns_b, ...), custom_call_target="tpu_custom_call" | custom-call | tf_op jit(solution)/shard_map/pallas_call | solution.py:662
  17.1 0.9 %collective-permute-start.6 = (f32[8,128]{1,0:T(8,128)S(1)}, f32[8,128]{1,0:T(8,128)S(1)}, u32[]{:S(2)}, u32[]{:S(2)}) collective-permute-start(f32[8,128]{1,0:T(8,128)S(1)} %get-tuple-element.42.refs_0_), channel_id=1, source_target_pairs={{0,3},{1,2},{2,1},{3,0},{4,7},{5,6},{6,5},{7,4},{8,11},{9,10},{10,... | collective-permute-start | bytes 12296 | tf_op jit(solution)/shard_map/ppermute | solution.py:624
  18.0 0.7 %collective-permute-start.7 = (f32[8,128]{1,0:T(8,128)S(1)}, f32[8,128]{1,0:T(8,128)S(1)}, u32[]{:S(2)}, u32[]{:S(2)}) collective-permute-start(f32[8,128]{1,0:T(8,128)S(1)} %get-tuple-element.42.refs_0_), channel_id=1, source_target_pairs={{0,2},{1,3},{2,0},{3,1},{4,6},{5,7},{6,4},{7,5},{8,10},{9,11},{10,... | collective-permute-start | bytes 12296 | tf_op jit(solution)/shard_map/ppermute | solution.py:624
  18.8 0.3 collective-permute-start.8
  19.1 1.2 %collective-permute-done.6.refs_1_ = f32[8,128]{1,0:T(8,128)S(1)} collective-permute-done((f32[8,128]{1,0:T(8,128)S(1)}, f32[8,128]{1,0:T(8,128)S(1)}, u32[]{:S(2)}, u32[]{:S(2)}) %collective-permute-start.6) | collective-permute-done | bytes 4128 | tf_op jit(solution)/shard_map/ppermute | solution.py:624
  20.2 1.4 %collective-permute-done.7.refs_2_ = f32[8,128]{1,0:T(8,128)S(1)} collective-permute-done((f32[8,128]{1,0:T(8,128)S(1)}, f32[8,128]{1,0:T(8,128)S(1)}, u32[]{:S(2)}, u32[]{:S(2)}) %collective-permute-start.7) | collective-permute-done | bytes 4128 | tf_op jit(solution)/shard_map/ppermute | solution.py:624
  21.8 1.3 %collective-permute-start.10 = (f32[8,128]{1,0:T(8,128)S(1)}, f32[8,128]{1,0:T(8,128)S(1)}, u32[]{:S(2)}, u32[]{:S(2)}) collective-permute-start(f32[8,128]{1,0:T(8,128)S(1)} %shard_map.91.rest_0_), channel_id=1, source_target_pairs={{0,8},{4,12},{8,0},{12,4},{1,9},{5,13},{9,1},{13,5},{2,10},{6,14},... | collective-permute-start | bytes 12296 | tf_op jit(solution)/shard_map/ppermute | solution.py:624
  23.0 2.1 %collective-permute-start.11 = (f32[8,128]{1,0:T(8,128)S(1)}, f32[8,128]{1,0:T(8,128)S(1)}, u32[]{:S(2)}, u32[]{:S(2)}) collective-permute-start(f32[8,128]{1,0:T(8,128)S(1)} %shard_map.91.rest_0_), channel_id=1, source_target_pairs={{0,12},{4,8},{8,4},{12,0},{1,13},{5,9},{9,5},{13,1},{2,14},{6,10},... | collective-permute-start | bytes 12296 | tf_op jit(solution)/shard_map/ppermute | solution.py:624
  25.2 0.3 collective-permute-start.9
  25.4 0.8 %collective-permute-done.10.rest_2_ = f32[8,128]{1,0:T(8,128)S(1)} collective-permute-done((f32[8,128]{1,0:T(8,128)S(1)}, f32[8,128]{1,0:T(8,128)S(1)}, u32[]{:S(2)}, u32[]{:S(2)}) %collective-permute-start.10) | collective-permute-done | bytes 4128 | tf_op jit(solution)/shard_map/ppermute | solution.py:624
  26.3 2.2 %collective-permute-done.11.rest_3_ = f32[8,128]{1,0:T(8,128)S(1)} collective-permute-done((f32[8,128]{1,0:T(8,128)S(1)}, f32[8,128]{1,0:T(8,128)S(1)}, u32[]{:S(2)}, u32[]{:S(2)}) %collective-permute-start.11) | collective-permute-done | bytes 4128 | tf_op jit(solution)/shard_map/ppermute | solution.py:624
  28.4 0.3 %collective-permute-done.9.rest_1_ = f32[8,128]{1,0:T(8,128)S(1)} collective-permute-done((f32[8,128]{1,0:T(8,128)S(1)}, f32[8,128]{1,0:T(8,128)S(1)}, u32[]{:S(2)}, u32[]{:S(2)}) %collective-permute-start.9) | collective-permute-done | bytes 4128 | tf_op jit(solution)/shard_map/ppermute | solution.py:624
  28.8 1.7 %shard_map.92 = (f32[2,20,8,256]{3,2,1,0:T(8,128)}, f32[2,20,8,256]{3,2,1,0:T(8,128)}, f32[8,256]{1,0:T(8,128)}) custom-call(f32[2,20,8,256]{3,2,1,0:T(8,128)S(1)} %get-tuple-element.23.rhs, f32[2,20,16,256]{3,2,1,0:T(8,128)S(1)} %get-tuple-element.33.power_1, f32[2,20,16,256]{3,2,1,0:T(8,128)S(1)} %get-tuple-element.34.power_2, ...), custom_call_target="tpu_custom_call" | custom-call | tf_op jit(solution)/shard_map/pallas_call | solution.py:672
  (8 shorter events, 0.2 us)
Async XLA Ops:
  1.8 10.1 %collective-permute-start.2 = (f32[62,8,128]{2,1,0:T(8,128)S(1)}, f32[62,8,128]{2,1,0:T(8,128)S(1)}, u32[]{:S(2)}, u32[]{:S(2)}) collective-permute-start(f32[62,8,128]{2,1,0:T(8,128)S(1)} %get-tuple-element.31), channel_id=1, source_target_pairs={{0,1},{4,8},{8,4},{12,13},{1,0},{5,9},{9,5},{13,12},{2,3},{6,10},{... | collective-permute-start | bytes 761864 | tf_op jit(solution)/shard_map/ppermute | solution.py:47
  2.3 10.0 %collective-permute-start.3 = (f32[62,8,128]{2,1,0:T(8,128)S(1)}, f32[62,8,128]{2,1,0:T(8,128)S(1)}, u32[]{:S(2)}, u32[]{:S(2)}) collective-permute-start(f32[62,8,128]{2,1,0:T(8,128)S(1)} %get-tuple-element.32), channel_id=1, source_target_pairs={{0,4},{4,0},{8,12},{12,8},{1,5},{5,1},{9,13},{13,9},{2,6},{6,2},{1... | collective-permute-start | bytes 761864 | tf_op jit(solution)/shard_map/ppermute | solution.py:47
  6.6 1.7 %collective-permute-start = (f32[3,8,128]{2,1,0:T(8,128)S(1)}, f32[3,8,128]{2,1,0:T(8,128)S(1)}, u32[]{:S(2)}, u32[]{:S(2)}) collective-permute-start(f32[3,8,128]{2,1,0:T(8,128)S(1)} %get-tuple-element.28), channel_id=1, source_target_pairs={{0,1},{1,0},{2,3},{3,2},{4,5},{5,4},{6,7},{7,6},{8,9},{9,8},{10,11... | collective-permute-start | bytes 36872 | tf_op jit(solution)/shard_map/ppermute | solution.py:47
  6.7 3.2 %collective-permute-start.1 = (f32[3,8,128]{2,1,0:T(8,128)S(1)}, f32[3,8,128]{2,1,0:T(8,128)S(1)}, u32[]{:S(2)}, u32[]{:S(2)}) collective-permute-start(f32[3,8,128]{2,1,0:T(8,128)S(1)} %get-tuple-element.29), channel_id=1, source_target_pairs={{0,3},{1,2},{2,1},{3,0},{4,7},{5,6},{6,5},{7,4},{8,11},{9,10},{10,... | collective-permute-start | bytes 36872 | tf_op jit(solution)/shard_map/ppermute | solution.py:47
  9.9 6.4 %collective-permute-start.4 = (f32[6,8,128]{2,1,0:T(8,128)S(1)}, f32[6,8,128]{2,1,0:T(8,128)S(1)}, u32[]{:S(2)}, u32[]{:S(2)}) collective-permute-start(f32[6,8,128]{2,1,0:T(8,128)S(1)} %shard_map.87._.columns), channel_id=1, source_target_pairs={{0,1},{4,8},{8,4},{12,13},{1,0},{5,9},{9,5},{13,12},{2,3},{6,10},{... | collective-permute-start | bytes 73736 | tf_op jit(solution)/shard_map/ppermute | solution.py:47
  10.6 5.6 %collective-permute-start.5 = (f32[6,8,128]{2,1,0:T(8,128)S(1)}, f32[6,8,128]{2,1,0:T(8,128)S(1)}, u32[]{:S(2)}, u32[]{:S(2)}) collective-permute-start(f32[6,8,128]{2,1,0:T(8,128)S(1)} %shard_map.87._.columns), channel_id=1, source_target_pairs={{0,4},{4,0},{8,12},{12,8},{1,5},{5,1},{9,13},{13,9},{2,6},{6,2},{1... | collective-permute-start | bytes 73736 | tf_op jit(solution)/shard_map/ppermute | solution.py:47
  17.1 3.1 %collective-permute-start.6 = (f32[8,128]{1,0:T(8,128)S(1)}, f32[8,128]{1,0:T(8,128)S(1)}, u32[]{:S(2)}, u32[]{:S(2)}) collective-permute-start(f32[8,128]{1,0:T(8,128)S(1)} %get-tuple-element.42.refs_0_), channel_id=1, source_target_pairs={{0,3},{1,2},{2,1},{3,0},{4,7},{5,6},{6,5},{7,4},{8,11},{9,10},{10,... | collective-permute-start | bytes 12296 | tf_op jit(solution)/shard_map/ppermute | solution.py:624
  18.0 3.6 %collective-permute-start.7 = (f32[8,128]{1,0:T(8,128)S(1)}, f32[8,128]{1,0:T(8,128)S(1)}, u32[]{:S(2)}, u32[]{:S(2)}) collective-permute-start(f32[8,128]{1,0:T(8,128)S(1)} %get-tuple-element.42.refs_0_), channel_id=1, source_target_pairs={{0,2},{1,3},{2,0},{3,1},{4,6},{5,7},{6,4},{7,5},{8,10},{9,11},{10,... | collective-permute-start | bytes 12296 | tf_op jit(solution)/shard_map/ppermute | solution.py:624
  18.8 2.9 %collective-permute-start.8 = (f32[8,128]{1,0:T(8,128)S(1)}, f32[8,128]{1,0:T(8,128)S(1)}, u32[]{:S(2)}, u32[]{:S(2)}) collective-permute-start(f32[8,128]{1,0:T(8,128)S(1)} %get-tuple-element.42.refs_0_), channel_id=1, source_target_pairs={{0,1},{1,0},{2,3},{3,2},{4,5},{5,4},{6,7},{7,6},{8,9},{9,8},{10,11... | collective-permute-start | bytes 12296 | tf_op jit(solution)/shard_map/ppermute | solution.py:624
  21.8 4.5 %collective-permute-start.10 = (f32[8,128]{1,0:T(8,128)S(1)}, f32[8,128]{1,0:T(8,128)S(1)}, u32[]{:S(2)}, u32[]{:S(2)}) collective-permute-start(f32[8,128]{1,0:T(8,128)S(1)} %shard_map.91.rest_0_), channel_id=1, source_target_pairs={{0,8},{4,12},{8,0},{12,4},{1,9},{5,13},{9,1},{13,5},{2,10},{6,14},... | collective-permute-start | bytes 12296 | tf_op jit(solution)/shard_map/ppermute | solution.py:624
  23.0 5.4 %collective-permute-start.11 = (f32[8,128]{1,0:T(8,128)S(1)}, f32[8,128]{1,0:T(8,128)S(1)}, u32[]{:S(2)}, u32[]{:S(2)}) collective-permute-start(f32[8,128]{1,0:T(8,128)S(1)} %shard_map.91.rest_0_), channel_id=1, source_target_pairs={{0,12},{4,8},{8,4},{12,0},{1,13},{5,9},{9,5},{13,1},{2,14},{6,10},... | collective-permute-start | bytes 12296 | tf_op jit(solution)/shard_map/ppermute | solution.py:624
  25.2 3.6 %collective-permute-start.9 = (f32[8,128]{1,0:T(8,128)S(1)}, f32[8,128]{1,0:T(8,128)S(1)}, u32[]{:S(2)}, u32[]{:S(2)}) collective-permute-start(f32[8,128]{1,0:T(8,128)S(1)} %shard_map.91.rest_0_), channel_id=1, source_target_pairs={{0,4},{4,0},{8,12},{12,8},{1,5},{5,1},{9,13},{13,9},{2,6},{6,2},{1... | collective-permute-start | bytes 12296 | tf_op jit(solution)/shard_map/ppermute | solution.py:624

commit v21 on v19

--- a/solution.py
+++ b/solution.py
@@ -470,32 +470,38 @@
             pair = join(pair, tuple(pltpu.roll(v, step, 0) for v in pair))
         high = jnp.where(tall == j, jnp.concatenate([pair[0]] * 2, 0), high)
         low = jnp.where(tall == j, jnp.concatenate([pair[1]] * 2, 0), low)
-    moments[0] = high
-    moments[1] = low
+    total = join((high, low), (pltpu.roll(high, 64, 1), pltpu.roll(low, 64, 1)))
+    first = lax.broadcasted_iota(jnp.int32, (ROWS, LANES), 1) < 64
+    for i, v in enumerate(total):
+        moments[i] = jnp.where(first, v[:ROWS], v[ROWS:])
+
+
+def added(terms):
+    while len(terms) > 1:
+        terms = [join(*terms[i : i + 2]) if i + 1 < len(terms) else terms[i] for i in range(0, len(terms), 2)]
+    return terms[0]
 
 
 def add_kernel(*refs):
     *ins, out = refs
-    total = (ins[0][0], ins[0][1])
-    for x in ins[1:]:
-        total = join(total, (x[0], x[1]))
-    out[0], out[1] = total
+    out[0], out[1] = added([(x[0], x[1]) for x in ins])
 
 
 def solve(total):
-    for step in (64, 32, 16, 8, 4, 2, 1):
-        total = join(total, tuple(pltpu.roll(v, step, 1) for v in total))
-
-    def spread(v, j):
-        return jnp.broadcast_to(v[j : j + 1], (ROWS, LANES))
-
-    centre, _ = cut(spread(total[0], 1) / spread(total[0], 0), 13)
-    wide = jnp.concatenate([centre, centre], 0)
-    mu = [spread(total[0] + total[1], 0)]
-    for _ in range(2 * STEPS):
-        step = times(wide, total)
-        total = join(tuple(pltpu.roll(v, 2 * ROWS - 1, 0) for v in total), (-step[0], -step[1]))
-        mu.append(spread(total[0] + total[1], 0))
+    for unit in (8, 1):
+        total = added([tuple(turned(v, unit * i) for v in total) for i in range(8)])
+
+    def spread(j):
+        row, lane = (j, 63) if j < ROWS else (j - ROWS, 127)
+        return tuple(jnp.broadcast_to(v[row : row + 1, lane : lane + 1], (ROWS, LANES)) for v in total)
+
+    table = [spread(j) for j in range(2 * STEPS + 1)]
+    centre, _ = cut(table[1][0] / table[0][0], 13)
+    mu = [sum(table[0])]
+    while len(table) > 1:
+        steps = [times(centre, x) for x in table[:-1]]
+        table = [join(x, (-y[0], -y[1])) for x, y in zip(table[1:], steps)]
+        mu.append(sum(table[0]))
 
     def plus(a, b):
         n = max(len(a), len(b))
@@ -559,10 +565,7 @@
 def final_kernel(rhs, power_1, power_2, power_3, power_4, edges, friction, ice, grounded, speed, *rest):
     *parts, iterate, residual, hessian = rest
     layers, tiles = rhs.shape[1], edges.shape[2]
-    total = (parts[0][0], parts[0][1])
-    for x in parts[1:]:
-        total = join(total, (x[0], x[1]))
-    factors = solve(total)
+    factors = solve(added([(x[0], x[1]) for x in parts]))
     powers = (power_1, power_2, power_3, power_4)
     wide = [jnp.concatenate([c, c], 1) for c in factors]
     rest = sum(wide[1:], wide[0])
@@ -651,7 +654,7 @@
     )(*held[:5], squares, strip_b, strip_a)
     edges, sums = call(
         ribbon_kernel,
-        [(STEPS, 2, layers // 4) + tile, (2, 2 * ROWS, LANES)],
+        [(STEPS, 2, layers // 4) + tile, (2,) + tile],
     )(own, halo, columns, columns_b, columns_a, sums)
     parts = exchange(sums, ("gy", "gz"), (3, 2, 1))
     if len(parts) > 1:

time: 30.7 us -> 30.4 us (level)
  transfers between devices with their start and end apart: 12 -> 12, of which waited for: 7 -> 7; matrix products, arithmetic and copies ran while one was open for 0% -> 0% of each run, Pallas kernels for 14% -> 15%
where the time goes in v21:
time: 30.4 us; the launch traced here: 30.3 us
  starting transfers between devices  13.7 us (45%)
  waiting for transfers between devices  7.93 us (26%)
  Pallas kernels  7.92 us (26%)
  between operations  0.7 us (2%)
    ppermute x6, starting transfers between devices, swapped(): return lax.ppermute(x, (*axes, spare) if spare else axes, pairs)  8.1 us
    ppermute x6, waiting for transfers between devices, exchange(): parts.append(lax.ppermute(x, axis, pairs))  5.98 us
    ppermute x6, starting transfers between devices, exchange(): parts.append(lax.ppermute(x, axis, pairs))  5.62 us
    pallas_call x1, Pallas kernels, body(): call(main_kernel, [(2,) + block] * (STEPS - 1) + [adjoint_rhs.shape, (2 *...  3.97 us
    ppermute x6, waiting for transfers between devices, swapped(): return lax.ppermute(x, (*axes, spare) if spare else axes, pairs)  1.95 us
    pallas_call x1, Pallas kernels, body(): call(final_kernel, [adjoint_rhs.shape, adjoint_rhs.shape, friction.shape])  1.58 us
    pallas_call x1, Pallas kernels, body(): call(strip_kernel, [jax.ShapeDtypeStruct(x.shape, x.dtype) for x in input...  1.13 us
    pallas_call x1, Pallas kernels, body(): call(ribbon_kernel, [(STEPS, 2, layers // 4) + tile, (2,) + tile])  0.79 us
  transfers between devices with their start and end apart: 12, of which 7 were waited for; matrix products, arithmetic and copies ran while one was open for 0% of the time, Pallas kernels for 15%

profile of v21, /device:TPU:0, one launch (start us, length us, event | category | flops | bytes accessed | tf_op | source)
XLA Modules:
  0.0 30.3 jit_solution(1403495662340532854)
XLA Ops:
  0.6 1.1 %shard_map.85 = (f32[2,20,8,256]{3,2,1,0:T(8,128)S(1)}, f32[20,8,256]{2,1,0:T(8,128)S(1)}, f32[8,256]{1,0:T(8,128)S(1)}, s32[8,256]{1,0:T(8,128)S(1)}, s32[8,256...) custom-call(f32[2,20,8,256]{3,2,1,0:T(8,128)} %refs_0_.1, ...), custom_call_target="tpu_custom_call" | custom-call | tf_op jit(solution)/shard_map/pallas_call | solution.py:632
  1.8 0.5 %collective-permute-start.2 = (f32[62,8,128]{2,1,0:T(8,128)S(1)}, f32[62,8,128]{2,1,0:T(8,128)S(1)}, u32[]{:S(2)}, u32[]{:S(2)}) collective-permute-start(f32[62,8,128]{2,1,0:T(8,128)S(1)} %get-tuple-element.31), channel_id=1, source_target_pairs={{0,1},{4,8},{8,4},{12,13},{1,0},{5,9},{9,5},{13,12},{2,3},{6,10},{... | collective-permute-start | bytes 761864 | tf_op jit(solution)/shard_map/ppermute | solution.py:47
  2.3 4.1 %collective-permute-start.3 = (f32[62,8,128]{2,1,0:T(8,128)S(1)}, f32[62,8,128]{2,1,0:T(8,128)S(1)}, u32[]{:S(2)}, u32[]{:S(2)}) collective-permute-start(f32[62,8,128]{2,1,0:T(8,128)S(1)} %get-tuple-element.32), channel_id=1, source_target_pairs={{0,4},{4,0},{8,12},{12,8},{1,5},{5,1},{9,13},{13,9},{2,6},{6,2},{1... | collective-permute-start | bytes 761864 | tf_op jit(solution)/shard_map/ppermute | solution.py:47
  6.4 0.2 shard_map.86
  6.7 1.6 %collective-permute-start.1 = (f32[3,8,128]{2,1,0:T(8,128)S(1)}, f32[3,8,128]{2,1,0:T(8,128)S(1)}, u32[]{:S(2)}, u32[]{:S(2)}) collective-permute-start(f32[3,8,128]{2,1,0:T(8,128)S(1)} %get-tuple-element.29), channel_id=1, source_target_pairs={{0,3},{1,2},{2,1},{3,0},{4,7},{5,6},{6,5},{7,4},{8,11},{9,10},{10,... | collective-permute-start | bytes 36872 | tf_op jit(solution)/shard_map/ppermute | solution.py:47
  8.3 1.6 %collective-permute-done.1.from_b = f32[3,8,128]{2,1,0:T(8,128)S(1)} collective-permute-done((f32[3,8,128]{2,1,0:T(8,128)S(1)}, f32[3,8,128]{2,1,0:T(8,128)S(1)}, u32[]{:S(2)}, u32[]{:S(2)}) %collective-permute-start.1) | collective-permute-done | bytes 12320 | tf_op jit(solution)/shard_map/ppermute | solution.py:47
  9.9 0.7 %collective-permute-start.4 = (f32[6,8,128]{2,1,0:T(8,128)S(1)}, f32[6,8,128]{2,1,0:T(8,128)S(1)}, u32[]{:S(2)}, u32[]{:S(2)}) collective-permute-start(f32[6,8,128]{2,1,0:T(8,128)S(1)} %shard_map.87._.columns), channel_id=1, source_target_pairs={{0,1},{4,8},{8,4},{12,13},{1,0},{5,9},{9,5},{13,12},{2,3},{6,10},{... | collective-permute-start | bytes 73736 | tf_op jit(solution)/shard_map/ppermute | solution.py:47
  10.6 1.0 %collective-permute-start.5 = (f32[6,8,128]{2,1,0:T(8,128)S(1)}, f32[6,8,128]{2,1,0:T(8,128)S(1)}, u32[]{:S(2)}, u32[]{:S(2)}) collective-permute-start(f32[6,8,128]{2,1,0:T(8,128)S(1)} %shard_map.87._.columns), channel_id=1, source_target_pairs={{0,4},{4,0},{8,12},{12,8},{1,5},{5,1},{9,13},{13,9},{2,6},{6,2},{1... | collective-permute-start | bytes 73736 | tf_op jit(solution)/shard_map/ppermute | solution.py:47
  11.7 0.2 shard_map.88
  11.9 0.4 %collective-permute-done.3.strip_a = f32[62,8,128]{2,1,0:T(8,128)S(1)} collective-permute-done((f32[62,8,128]{2,1,0:T(8,128)S(1)}, f32[62,8,128]{2,1,0:T(8,128)S(1)}, u32[]{:S(2)}, u32[]{:S(2)}) %collective-permute-start.3) | collective-permute-done | bytes 253984 | tf_op jit(solution)/shard_map/ppermute | solution.py:47
  12.3 4.0 %shard_map.89 = (f32[2,20,16,256]{3,2,1,0:T(8,128)S(1)}, f32[2,20,16,256]{3,2,1,0:T(8,128)S(1)}, f32[2,20,16,256]{3,2,1,0:T(8,128)S(1)}, f32[2,20,8,256]{3,2,1,0...) custom-call(f32[2,20,8,256]{3,2,1,0:T(8,128)S(1)} %get-tuple-element.23.rhs, ...), custom_call_target="tpu_custom_call" | custom-call | flops 200000000 | bytes 8000000 | tf_op jit(solution)/shard_map/pallas_call | solution.py:649
  16.3 0.8 %shard_map.90 = (f32[4,2,5,8,128]{4,3,2,1,0:T(8,128)S(1)}, f32[2,8,128]{2,1,0:T(8,128)S(1)}) custom-call(f32[17,8,128]{2,1,0:T(8,128)S(1)} %get-tuple-element.37.own, f32[17,8,128]{2,1,0:T(8,128)S(1)} %get-tuple-element.38.halo, f32[6,8,128]{2,1,0:T(8,128)S(1)} %shard_map.87._.columns, f32[6,8,128]{2,1,0:T(8,128)S(1)} %collective-permute-done.4.columns_b, ...), custom_call_target="tpu_custom_call" | custom-call | tf_op jit(solution)/shard_map/pallas_call | solution.py:655
  17.1 0.9 %collective-permute-start.6 = (f32[2,8,128]{2,1,0:T(8,128)S(1)}, f32[2,8,128]{2,1,0:T(8,128)S(1)}, u32[]{:S(2)}, u32[]{:S(2)}) collective-permute-start(f32[2,8,128]{2,1,0:T(8,128)S(1)} %get-tuple-element.42.refs_0_), channel_id=1, source_target_pairs={{0,3},{1,2},{2,1},{3,0},{4,7},{5,6},{6,5},{7,4},{8,11},{9,10},{10,... | collective-permute-start | bytes 24584 | tf_op jit(solution)/shard_map/ppermute | solution.py:617
  17.9 0.7 %collective-permute-start.7 = (f32[2,8,128]{2,1,0:T(8,128)S(1)}, f32[2,8,128]{2,1,0:T(8,128)S(1)}, u32[]{:S(2)}, u32[]{:S(2)}) collective-permute-start(f32[2,8,128]{2,1,0:T(8,128)S(1)} %get-tuple-element.42.refs_0_), channel_id=1, source_target_pairs={{0,2},{1,3},{2,0},{3,1},{4,6},{5,7},{6,4},{7,5},{8,10},{9,11},{10,... | collective-permute-start | bytes 24584 | tf_op jit(solution)/shard_map/ppermute | solution.py:617
  18.7 0.3 collective-permute-start.8
  19.0 1.3 %collective-permute-done.6.refs_1_ = f32[2,8,128]{2,1,0:T(8,128)S(1)} collective-permute-done((f32[2,8,128]{2,1,0:T(8,128)S(1)}, f32[2,8,128]{2,1,0:T(8,128)S(1)}, u32[]{:S(2)}, u32[]{:S(2)}) %collective-permute-start.6) | collective-permute-done | bytes 8224 | tf_op jit(solution)/shard_map/ppermute | solution.py:617
  20.2 1.4 %collective-permute-done.7.refs_2_ = f32[2,8,128]{2,1,0:T(8,128)S(1)} collective-permute-done((f32[2,8,128]{2,1,0:T(8,128)S(1)}, f32[2,8,128]{2,1,0:T(8,128)S(1)}, u32[]{:S(2)}, u32[]{:S(2)}) %collective-permute-start.7) | collective-permute-done | bytes 8224 | tf_op jit(solution)/shard_map/ppermute | solution.py:617
  21.6 1.3 %collective-permute-start.10 = (f32[2,8,128]{2,1,0:T(8,128)S(1)}, f32[2,8,128]{2,1,0:T(8,128)S(1)}, u32[]{:S(2)}, u32[]{:S(2)}) collective-permute-start(f32[2,8,128]{2,1,0:T(8,128)S(1)} %shard_map.91.rest_0_), channel_id=1, source_target_pairs={{0,8},{4,12},{8,0},{12,4},{1,9},{5,13},{9,1},{13,5},{2,10},{6,14},... | collective-permute-start | bytes 24584 | tf_op jit(solution)/shard_map/ppermute | solution.py:617
  22.9 2.1 %collective-permute-start.11 = (f32[2,8,128]{2,1,0:T(8,128)S(1)}, f32[2,8,128]{2,1,0:T(8,128)S(1)}, u32[]{:S(2)}, u32[]{:S(2)}) collective-permute-start(f32[2,8,128]{2,1,0:T(8,128)S(1)} %shard_map.91.rest_0_), channel_id=1, source_target_pairs={{0,12},{4,8},{8,4},{12,0},{1,13},{5,9},{9,5},{13,1},{2,14},{6,10},... | collective-permute-start | bytes 24584 | tf_op jit(solution)/shard_map/ppermute | solution.py:617
  25.0 0.3 collective-permute-start.9
  25.3 0.9 %collective-permute-done.10.rest_2_ = f32[2,8,128]{2,1,0:T(8,128)S(1)} collective-permute-done((f32[2,8,128]{2,1,0:T(8,128)S(1)}, f32[2,8,128]{2,1,0:T(8,128)S(1)}, u32[]{:S(2)}, u32[]{:S(2)}) %collective-permute-start.10) | collective-permute-done | bytes 8224 | tf_op jit(solution)/shard_map/ppermute | solution.py:617
  26.2 2.2 %collective-permute-done.11.rest_3_ = f32[2,8,128]{2,1,0:T(8,128)S(1)} collective-permute-done((f32[2,8,128]{2,1,0:T(8,128)S(1)}, f32[2,8,128]{2,1,0:T(8,128)S(1)}, u32[]{:S(2)}, u32[]{:S(2)}) %collective-permute-start.11) | collective-permute-done | bytes 8224 | tf_op jit(solution)/shard_map/ppermute | solution.py:617
  28.4 0.3 %collective-permute-done.9.rest_1_ = f32[2,8,128]{2,1,0:T(8,128)S(1)} collective-permute-done((f32[2,8,128]{2,1,0:T(8,128)S(1)}, f32[2,8,128]{2,1,0:T(8,128)S(1)}, u32[]{:S(2)}, u32[]{:S(2)}) %collective-permute-start.9) | collective-permute-done | bytes 8224 | tf_op jit(solution)/shard_map/ppermute | solution.py:617
  28.7 1.6 %shard_map.92 = (f32[2,20,8,256]{3,2,1,0:T(8,128)}, f32[2,20,8,256]{3,2,1,0:T(8,128)}, f32[8,256]{1,0:T(8,128)}) custom-call(f32[2,20,8,256]{3,2,1,0:T(8,128)S(1)} %get-tuple-element.23.rhs, f32[2,20,16,256]{3,2,1,0:T(8,128)S(1)} %get-tuple-element.33.power_1, f32[2,20,16,256]{3,2,1,0:T(8,128)S(1)} %get-tuple-element.34.power_2, ...), custom_call_target="tpu_custom_call" | custom-call | tf_op jit(solution)/shard_map/pallas_call | solution.py:665
  (8 shorter events, 0.1 us)
Async XLA Ops:
  1.8 10.1 %collective-permute-start.2 = (f32[62,8,128]{2,1,0:T(8,128)S(1)}, f32[62,8,128]{2,1,0:T(8,128)S(1)}, u32[]{:S(2)}, u32[]{:S(2)}) collective-permute-start(f32[62,8,128]{2,1,0:T(8,128)S(1)} %get-tuple-element.31), channel_id=1, source_target_pairs={{0,1},{4,8},{8,4},{12,13},{1,0},{5,9},{9,5},{13,12},{2,3},{6,10},{... | collective-permute-start | bytes 761864 | tf_op jit(solution)/shard_map/ppermute | solution.py:47
  2.3 10.0 %collective-permute-start.3 = (f32[62,8,128]{2,1,0:T(8,128)S(1)}, f32[62,8,128]{2,1,0:T(8,128)S(1)}, u32[]{:S(2)}, u32[]{:S(2)}) collective-permute-start(f32[62,8,128]{2,1,0:T(8,128)S(1)} %get-tuple-element.32), channel_id=1, source_target_pairs={{0,4},{4,0},{8,12},{12,8},{1,5},{5,1},{9,13},{13,9},{2,6},{6,2},{1... | collective-permute-start | bytes 761864 | tf_op jit(solution)/shard_map/ppermute | solution.py:47
  6.6 1.7 %collective-permute-start = (f32[3,8,128]{2,1,0:T(8,128)S(1)}, f32[3,8,128]{2,1,0:T(8,128)S(1)}, u32[]{:S(2)}, u32[]{:S(2)}) collective-permute-start(f32[3,8,128]{2,1,0:T(8,128)S(1)} %get-tuple-element.28), channel_id=1, source_target_pairs={{0,1},{1,0},{2,3},{3,2},{4,5},{5,4},{6,7},{7,6},{8,9},{9,8},{10,11... | collective-permute-start | bytes 36872 | tf_op jit(solution)/shard_map/ppermute | solution.py:47
  6.7 3.2 %collective-permute-start.1 = (f32[3,8,128]{2,1,0:T(8,128)S(1)}, f32[3,8,128]{2,1,0:T(8,128)S(1)}, u32[]{:S(2)}, u32[]{:S(2)}) collective-permute-start(f32[3,8,128]{2,1,0:T(8,128)S(1)} %get-tuple-element.29), channel_id=1, source_target_pairs={{0,3},{1,2},{2,1},{3,0},{4,7},{5,6},{6,5},{7,4},{8,11},{9,10},{10,... | collective-permute-start | bytes 36872 | tf_op jit(solution)/shard_map/ppermute | solution.py:47
  9.9 6.4 %collective-permute-start.4 = (f32[6,8,128]{2,1,0:T(8,128)S(1)}, f32[6,8,128]{2,1,0:T(8,128)S(1)}, u32[]{:S(2)}, u32[]{:S(2)}) collective-permute-start(f32[6,8,128]{2,1,0:T(8,128)S(1)} %shard_map.87._.columns), channel_id=1, source_target_pairs={{0,1},{4,8},{8,4},{12,13},{1,0},{5,9},{9,5},{13,12},{2,3},{6,10},{... | collective-permute-start | bytes 73736 | tf_op jit(solution)/shard_map/ppermute | solution.py:47
  10.6 5.6 %collective-permute-start.5 = (f32[6,8,128]{2,1,0:T(8,128)S(1)}, f32[6,8,128]{2,1,0:T(8,128)S(1)}, u32[]{:S(2)}, u32[]{:S(2)}) collective-permute-start(f32[6,8,128]{2,1,0:T(8,128)S(1)} %shard_map.87._.columns), channel_id=1, source_target_pairs={{0,4},{4,0},{8,12},{12,8},{1,5},{5,1},{9,13},{13,9},{2,6},{6,2},{1... | collective-permute-start | bytes 73736 | tf_op jit(solution)/shard_map/ppermute | solution.py:47
  17.1 3.1 %collective-permute-start.6 = (f32[2,8,128]{2,1,0:T(8,128)S(1)}, f32[2,8,128]{2,1,0:T(8,128)S(1)}, u32[]{:S(2)}, u32[]{:S(2)}) collective-permute-start(f32[2,8,128]{2,1,0:T(8,128)S(1)} %get-tuple-element.42.refs_0_), channel_id=1, source_target_pairs={{0,3},{1,2},{2,1},{3,0},{4,7},{5,6},{6,5},{7,4},{8,11},{9,10},{10,... | collective-permute-start | bytes 24584 | tf_op jit(solution)/shard_map/ppermute | solution.py:617
  17.9 3.7 %collective-permute-start.7 = (f32[2,8,128]{2,1,0:T(8,128)S(1)}, f32[2,8,128]{2,1,0:T(8,128)S(1)}, u32[]{:S(2)}, u32[]{:S(2)}) collective-permute-start(f32[2,8,128]{2,1,0:T(8,128)S(1)} %get-tuple-element.42.refs_0_), channel_id=1, source_target_pairs={{0,2},{1,3},{2,0},{3,1},{4,6},{5,7},{6,4},{7,5},{8,10},{9,11},{10,... | collective-permute-start | bytes 24584 | tf_op jit(solution)/shard_map/ppermute | solution.py:617
  18.7 2.9 %collective-permute-start.8 = (f32[2,8,128]{2,1,0:T(8,128)S(1)}, f32[2,8,128]{2,1,0:T(8,128)S(1)}, u32[]{:S(2)}, u32[]{:S(2)}) collective-permute-start(f32[2,8,128]{2,1,0:T(8,128)S(1)} %get-tuple-element.42.refs_0_), channel_id=1, source_target_pairs={{0,1},{1,0},{2,3},{3,2},{4,5},{5,4},{6,7},{7,6},{8,9},{9,8},{10,11... | collective-permute-start | bytes 24584 | tf_op jit(solution)/shard_map/ppermute | solution.py:617
  21.6 4.6 %collective-permute-start.10 = (f32[2,8,128]{2,1,0:T(8,128)S(1)}, f32[2,8,128]{2,1,0:T(8,128)S(1)}, u32[]{:S(2)}, u32[]{:S(2)}) collective-permute-start(f32[2,8,128]{2,1,0:T(8,128)S(1)} %shard_map.91.rest_0_), channel_id=1, source_target_pairs={{0,8},{4,12},{8,0},{12,4},{1,9},{5,13},{9,1},{13,5},{2,10},{6,14},... | collective-permute-start | bytes 24584 | tf_op jit(solution)/shard_map/ppermute | solution.py:617
  22.9 5.5 %collective-permute-start.11 = (f32[2,8,128]{2,1,0:T(8,128)S(1)}, f32[2,8,128]{2,1,0:T(8,128)S(1)}, u32[]{:S(2)}, u32[]{:S(2)}) collective-permute-start(f32[2,8,128]{2,1,0:T(8,128)S(1)} %shard_map.91.rest_0_), channel_id=1, source_target_pairs={{0,12},{4,8},{8,4},{12,0},{1,13},{5,9},{9,5},{13,1},{2,14},{6,10},... | collective-permute-start | bytes 24584 | tf_op jit(solution)/shard_map/ppermute | solution.py:617
  25.0 3.7 %collective-permute-start.9 = (f32[2,8,128]{2,1,0:T(8,128)S(1)}, f32[2,8,128]{2,1,0:T(8,128)S(1)}, u32[]{:S(2)}, u32[]{:S(2)}) collective-permute-start(f32[2,8,128]{2,1,0:T(8,128)S(1)} %shard_map.91.rest_0_), channel_id=1, source_target_pairs={{0,4},{4,0},{8,12},{12,8},{1,5},{5,1},{9,13},{13,9},{2,6},{6,2},{1... | collective-permute-start | bytes 24584 | tf_op jit(solution)/shard_map/ppermute | solution.py:617

commit v22 on v21

--- a/solution.py
+++ b/solution.py
@@ -408,7 +408,7 @@
         sums[2 * t] = jnp.where(inner, even, 0.0) + outside
 
 
-def ribbon_kernel(own, halo, columns, columns_b, columns_a, sums, edges, moments):
+def ribbon_kernel(own, halo, columns, columns_a, columns_b, sums, edges, moments):
     tiles = edges.shape[2]
     below_and_above, _ = beyond()
     lane = lax.broadcasted_iota(jnp.int32, (2 * ROWS, LANES), 1)
@@ -562,40 +562,36 @@
     return powers
 
 
-def final_kernel(rhs, power_1, power_2, power_3, power_4, edges, friction, ice, grounded, speed, *rest):
-    *parts, iterate, residual, hessian = rest
+def patch_kernel(_, rhs, ice, power_1, power_2, power_3, power_4, edges, vectors):
     layers, tiles = rhs.shape[1], edges.shape[2]
-    factors = solve(added([(x[0], x[1]) for x in parts]))
-    powers = (power_1, power_2, power_3, power_4)
-    wide = [jnp.concatenate([c, c], 1) for c in factors]
-    rest = sum(wide[1:], wide[0])
-    cover = ice[...].astype(jnp.float32)
+    covered = ice[...] > 0
     lane = lax.broadcasted_iota(jnp.int32, (ROWS, LANES), 1)
-
-    def combined(vectors, weights):
-        x = weights[1] * vectors[0]
-        y = weights[0] * vectors[0]
-        for t in range(1, STEPS):
-            if t + 1 < STEPS:
-                x = x + weights[t + 1] * vectors[t]
-            y = y + weights[t] * vectors[t]
-        return x, y
-
-    for c in range(2):
-        side = [combined([edges[t, c, n] for t in range(STEPS)], factors) for n in range(tiles)]
-        for k in range(layers):
-            at = k // tiles * SLOT
-            inner = combined([p[c, k, :ROWS] for p in powers], wide)
-            patched = []
-            for v, e in zip(inner, side[k % tiles]):
+    for t, power in enumerate((power_1, power_2, power_3, power_4)):
+        for c in range(2):
+            for k in range(layers):
+                e, at = edges[t, c, k % tiles], k // tiles * SLOT
+                v = power[c, k, :ROWS]
                 head = jnp.where(lane < HALO, turned(e, -at - 20), v[:, :LANES])
                 tail = jnp.where(lane >= LANES - HALO, turned(e, 120 - at), v[:, LANES:])
-                patched.append(jnp.concatenate([head, tail], 1))
+                vectors[t, c, k] = jnp.where(covered, jnp.concatenate([head, tail], 1), rhs[c, k])
+
+
+def final_kernel(rhs, vectors, friction, ice, grounded, speed, *rest):
+    *parts, iterate, residual, hessian = rest
+    layers = rhs.shape[1]
+    wide = [jnp.concatenate([c, c], 1) for c in solve(added([(x[0], x[1]) for x in parts]))]
+    for c in range(2):
+        for k in range(layers):
             r = rhs[c, k]
-            x, y = patched
-            iterate[c, k] = jnp.where(cover > 0.0, wide[0] * r + x, rest * r)
-            residual[c, k] = r - jnp.where(cover > 0.0, y, rest * r)
-    weight = cover * (friction[...] * grounded[...].astype(jnp.float32))
+            x, y = wide[0] * r, r
+            for t in range(STEPS):
+                v = vectors[t, c, k]
+                if t + 1 < STEPS:
+                    x = x + wide[t + 1] * v
+                y = y - wide[t] * v
+            iterate[c, k] = x
+            residual[c, k] = y
+    weight = ice[...].astype(jnp.float32) * (friction[...] * grounded[...].astype(jnp.float32))
     hessian[...] = weight * (speed[0] * iterate[0, 0] + speed[1] * iterate[1, 0])
 
 
@@ -639,7 +635,7 @@
     column_a, column_b = call(column_kernel, [packed, packed])(*held[:5])
     beside = ("gy", "gz")
     (columns,) = call(beside_kernel, [both])(swapped(column_a, beside, 0), swapped(column_b, beside, 1))
-    columns_b, columns_a = swapped(columns, ("gx",), 1, "gz"), swapped(columns, ("gx",), 0)
+    columns_a, columns_b = swapped(columns, ("gx",), 0), swapped(columns, ("gx",), 1, "gz")
     block = (layers, 2 * ROWS, 2 * LANES)
     own, squares = call(
         own_kernel,
@@ -655,15 +651,20 @@
     edges, sums = call(
         ribbon_kernel,
         [(STEPS, 2, layers // 4) + tile, (2,) + tile],
-    )(own, halo, columns, columns_b, columns_a, sums)
-    parts = exchange(sums, ("gy", "gz"), (3, 2, 1))
+    )(own, halo, columns, columns_a, columns_b, sums)
+    parts = exchange(sums, ("gy", "gz"), (1, 2, 3))
     if len(parts) > 1:
         sums = call(add_kernel, [sums.shape])(*parts)[0]
-    parts = exchange(sums, "gx", (1, 2, 3))
+    parts = exchange(sums, "gx", (1, 3, 2))
     rhs, _, friction, ice_mask, grounded, speed = held
+    (vectors,) = call(
+        patch_kernel,
+        [(STEPS,) + adjoint_rhs.shape],
+        in_specs=[pl.BlockSpec(memory_space=pl.ANY)] + [pl.BlockSpec(memory_space=pltpu.VMEM)] * 7,
+    )(sums, rhs, ice_mask, *powers, edges)
     return tuple(
         call(final_kernel, [adjoint_rhs.shape, adjoint_rhs.shape, friction.shape])(
-            rhs, *powers, edges, friction, ice_mask, grounded, speed, *parts
+            rhs, vectors, friction, ice_mask, grounded, speed, *parts
         )
     )
 

time: 30.4 us -> 30.1 us (level)
  waiting for transfers between devices: 7.93 us -> 7.51 us
    ppermute x6, waiting for transfers between devices: 5.98 us -> 5.56 us  [exchange(): parts.append(lax.ppermute(x, axis, pairs))]
    pallas_call x0 -> x1, Pallas kernels: none -> 0.41 us  [body(): call(patch_kernel, [(STEPS,) + adjoint_rhs.shape], in_specs=[pl.BlockSpec...]
  transfers between devices with their start and end apart: 12 -> 12, of which waited for: 7 -> 7; matrix products, arithmetic and copies ran while one was open for 0% -> 0% of each run, Pallas kernels for 15% -> 16%
where the time goes in v22:
time: 30.1 us; the launch traced here: 30 us
  starting transfers between devices  13.7 us (46%)
  Pallas kernels  8.04 us (27%)
  waiting for transfers between devices  7.51 us (25%)
  between operations  0.71 us (2%)
    ppermute x6, starting transfers between devices, swapped(): return lax.ppermute(x, (*axes, spare) if spare else axes, pairs)  8.1 us
    ppermute x6, starting transfers between devices, exchange(): parts.append(lax.ppermute(x, axis, pairs))  5.62 us
    ppermute x6, waiting for transfers between devices, exchange(): parts.append(lax.ppermute(x, axis, pairs))  5.56 us
    pallas_call x1, Pallas kernels, body(): call(main_kernel, [(2,) + block] * (STEPS - 1) + [adjoint_rhs.shape, (2 *...  3.91 us
    ppermute x6, waiting for transfers between devices, swapped(): return lax.ppermute(x, (*axes, spare) if spare else axes, pairs)  1.95 us
    pallas_call x1, Pallas kernels, body(): call(final_kernel, [adjoint_rhs.shape, adjoint_rhs.shape, friction.shape])  1.34 us
    pallas_call x1, Pallas kernels, body(): call(strip_kernel, [jax.ShapeDtypeStruct(x.shape, x.dtype) for x in input...  1.13 us
    pallas_call x1, Pallas kernels, body(): call(ribbon_kernel, [(STEPS, 2, layers // 4) + tile, (2,) + tile])  0.79 us
  transfers between devices with their start and end apart: 12, of which 7 were waited for; matrix products, arithmetic and copies ran while one was open for 0% of the time, Pallas kernels for 16%

profile of v22, /device:TPU:0, one launch (start us, length us, event | category | flops | bytes accessed | tf_op | source)
XLA Modules:
  0.0 30.0 jit_solution(9972269562302807464)
XLA Ops:
  0.6 1.1 %shard_map.85 = (f32[2,20,8,256]{3,2,1,0:T(8,128)S(1)}, f32[20,8,256]{2,1,0:T(8,128)S(1)}, f32[8,256]{1,0:T(8,128)S(1)}, s32[8,256]{1,0:T(8,128)S(1)}, s32[8,256...) custom-call(f32[2,20,8,256]{3,2,1,0:T(8,128)} %refs_0_.1, ...), custom_call_target="tpu_custom_call" | custom-call | tf_op jit(solution)/shard_map/pallas_call | solution.py:628
  1.8 0.5 %collective-permute-start.2 = (f32[62,8,128]{2,1,0:T(8,128)S(1)}, f32[62,8,128]{2,1,0:T(8,128)S(1)}, u32[]{:S(2)}, u32[]{:S(2)}) collective-permute-start(f32[62,8,128]{2,1,0:T(8,128)S(1)} %get-tuple-element.32), channel_id=1, source_target_pairs={{0,1},{4,8},{8,4},{12,13},{1,0},{5,9},{9,5},{13,12},{2,3},{6,10},{... | collective-permute-start | bytes 761864 | tf_op jit(solution)/shard_map/ppermute | solution.py:47
  2.3 4.1 %collective-permute-start.3 = (f32[62,8,128]{2,1,0:T(8,128)S(1)}, f32[62,8,128]{2,1,0:T(8,128)S(1)}, u32[]{:S(2)}, u32[]{:S(2)}) collective-permute-start(f32[62,8,128]{2,1,0:T(8,128)S(1)} %get-tuple-element.33), channel_id=1, source_target_pairs={{0,4},{4,0},{8,12},{12,8},{1,5},{5,1},{9,13},{13,9},{2,6},{6,2},{1... | collective-permute-start | bytes 761864 | tf_op jit(solution)/shard_map/ppermute | solution.py:47
  6.7 1.6 %collective-permute-start.1 = (f32[3,8,128]{2,1,0:T(8,128)S(1)}, f32[3,8,128]{2,1,0:T(8,128)S(1)}, u32[]{:S(2)}, u32[]{:S(2)}) collective-permute-start(f32[3,8,128]{2,1,0:T(8,128)S(1)} %get-tuple-element.29), channel_id=1, source_target_pairs={{0,3},{1,2},{2,1},{3,0},{4,7},{5,6},{6,5},{7,4},{8,11},{9,10},{10,... | collective-permute-start | bytes 36872 | tf_op jit(solution)/shard_map/ppermute | solution.py:47
  8.3 1.6 %collective-permute-done.1.from_b = f32[3,8,128]{2,1,0:T(8,128)S(1)} collective-permute-done((f32[3,8,128]{2,1,0:T(8,128)S(1)}, f32[3,8,128]{2,1,0:T(8,128)S(1)}, u32[]{:S(2)}, u32[]{:S(2)}) %collective-permute-start.1) | collective-permute-done | bytes 12320 | tf_op jit(solution)/shard_map/ppermute | solution.py:47
  9.9 0.7 %collective-permute-start.5 = (f32[6,8,128]{2,1,0:T(8,128)S(1)}, f32[6,8,128]{2,1,0:T(8,128)S(1)}, u32[]{:S(2)}, u32[]{:S(2)}) collective-permute-start(f32[6,8,128]{2,1,0:T(8,128)S(1)} %shard_map.87._.columns), channel_id=1, source_target_pairs={{0,1},{4,8},{8,4},{12,13},{1,0},{5,9},{9,5},{13,12},{2,3},{6,10},{... | collective-permute-start | bytes 73736 | tf_op jit(solution)/shard_map/ppermute | solution.py:47
  10.6 1.0 %collective-permute-start.4 = (f32[6,8,128]{2,1,0:T(8,128)S(1)}, f32[6,8,128]{2,1,0:T(8,128)S(1)}, u32[]{:S(2)}, u32[]{:S(2)}) collective-permute-start(f32[6,8,128]{2,1,0:T(8,128)S(1)} %shard_map.87._.columns), channel_id=1, source_target_pairs={{0,4},{4,0},{8,12},{12,8},{1,5},{5,1},{9,13},{13,9},{2,6},{6,2},{1... | collective-permute-start | bytes 73736 | tf_op jit(solution)/shard_map/ppermute | solution.py:47
  11.7 0.2 shard_map.88
  11.9 0.4 %collective-permute-done.3.strip_a = f32[62,8,128]{2,1,0:T(8,128)S(1)} collective-permute-done((f32[62,8,128]{2,1,0:T(8,128)S(1)}, f32[62,8,128]{2,1,0:T(8,128)S(1)}, u32[]{:S(2)}, u32[]{:S(2)}) %collective-permute-start.3) | collective-permute-done | bytes 253984 | tf_op jit(solution)/shard_map/ppermute | solution.py:47
  12.3 3.9 %shard_map.89 = (f32[2,20,16,256]{3,2,1,0:T(8,128)S(1)}, f32[2,20,16,256]{3,2,1,0:T(8,128)S(1)}, f32[2,20,16,256]{3,2,1,0:T(8,128)S(1)}, f32[2,20,8,256]{3,2,1,0...) custom-call(f32[2,20,8,256]{3,2,1,0:T(8,128)S(1)} %get-tuple-element.23.rhs, ...), custom_call_target="tpu_custom_call" | custom-call | flops 200000000 | bytes 8000000 | tf_op jit(solution)/shard_map/pallas_call | solution.py:645
  16.2 0.8 %shard_map.90 = (f32[4,2,5,8,128]{4,3,2,1,0:T(8,128)S(1)}, f32[2,8,128]{2,1,0:T(8,128)S(1)}) custom-call(f32[17,8,128]{2,1,0:T(8,128)S(1)} %get-tuple-element.30.own, f32[17,8,128]{2,1,0:T(8,128)S(1)} %get-tuple-element.34.halo, f32[6,8,128]{2,1,0:T(8,128)S(1)} %shard_map.87._.columns, f32[6,8,128]{2,1,0:T(8,128)S(1)} %collective-permute-done.4.columns_a, ...), custom_call_target="tpu_custom_call" | custom-call | tf_op jit(solution)/shard_map/pallas_call | solution.py:651
  17.0 0.9 %collective-permute-start.8 = (f32[2,8,128]{2,1,0:T(8,128)S(1)}, f32[2,8,128]{2,1,0:T(8,128)S(1)}, u32[]{:S(2)}, u32[]{:S(2)}) collective-permute-start(f32[2,8,128]{2,1,0:T(8,128)S(1)} %get-tuple-element.36.refs_0_), channel_id=1, source_target_pairs={{0,3},{1,2},{2,1},{3,0},{4,7},{5,6},{6,5},{7,4},{8,11},{9,10},{10,... | collective-permute-start | bytes 24584 | tf_op jit(solution)/shard_map/ppermute | solution.py:613
  17.9 0.7 %collective-permute-start.7 = (f32[2,8,128]{2,1,0:T(8,128)S(1)}, f32[2,8,128]{2,1,0:T(8,128)S(1)}, u32[]{:S(2)}, u32[]{:S(2)}) collective-permute-start(f32[2,8,128]{2,1,0:T(8,128)S(1)} %get-tuple-element.36.refs_0_), channel_id=1, source_target_pairs={{0,2},{1,3},{2,0},{3,1},{4,6},{5,7},{6,4},{7,5},{8,10},{9,11},{10,... | collective-permute-start | bytes 24584 | tf_op jit(solution)/shard_map/ppermute | solution.py:613
  18.6 0.3 collective-permute-start.6
  18.9 1.3 %collective-permute-done.8.refs_3_ = f32[2,8,128]{2,1,0:T(8,128)S(1)} collective-permute-done((f32[2,8,128]{2,1,0:T(8,128)S(1)}, f32[2,8,128]{2,1,0:T(8,128)S(1)}, u32[]{:S(2)}, u32[]{:S(2)}) %collective-permute-start.8) | collective-permute-done | bytes 8224 | tf_op jit(solution)/shard_map/ppermute | solution.py:613
  20.2 1.4 %collective-permute-done.7.refs_2_ = f32[2,8,128]{2,1,0:T(8,128)S(1)} collective-permute-done((f32[2,8,128]{2,1,0:T(8,128)S(1)}, f32[2,8,128]{2,1,0:T(8,128)S(1)}, u32[]{:S(2)}, u32[]{:S(2)}) %collective-permute-start.7) | collective-permute-done | bytes 8224 | tf_op jit(solution)/shard_map/ppermute | solution.py:613
  21.5 1.3 %collective-permute-start.11 = (f32[2,8,128]{2,1,0:T(8,128)S(1)}, f32[2,8,128]{2,1,0:T(8,128)S(1)}, u32[]{:S(2)}, u32[]{:S(2)}) collective-permute-start(f32[2,8,128]{2,1,0:T(8,128)S(1)} %shard_map.91._.rest_0_), channel_id=1, source_target_pairs={{0,8},{4,12},{8,0},{12,4},{1,9},{5,13},{9,1},{13,5},{2,10},{6,14},... | collective-permute-start | bytes 24584 | tf_op jit(solution)/shard_map/ppermute | solution.py:613
  22.9 2.1 %collective-permute-start.10 = (f32[2,8,128]{2,1,0:T(8,128)S(1)}, f32[2,8,128]{2,1,0:T(8,128)S(1)}, u32[]{:S(2)}, u32[]{:S(2)}) collective-permute-start(f32[2,8,128]{2,1,0:T(8,128)S(1)} %shard_map.91._.rest_0_), channel_id=1, source_target_pairs={{0,12},{4,8},{8,4},{12,0},{1,13},{5,9},{9,5},{13,1},{2,14},{6,10},... | collective-permute-start | bytes 24584 | tf_op jit(solution)/shard_map/ppermute | solution.py:613
  25.0 0.3 collective-permute-start.9
  25.3 0.4 %shard_map.92.vectors = f32[4,2,20,8,256]{4,3,2,1,0:T(8,128)S(1)} custom-call(f32[2,8,128]{2,1,0:T(8,128)S(1)} %shard_map.91._.rest_0_, f32[2,20,8,256]{3,2,1,0:T(8,128)S(1)} %get-tuple-element.23.rhs, s32[8,256]{1,0:T(8,128)S(1)} %get-tuple-element.26.ice, f32[2,20,16,256]{3,2,1,0:T(8,128)S(1)} %get-tuple-element.37.power_1, ...), custom_call_target="tpu_custom_call" | custom-call | tf_op jit(solution)/shard_map/pallas_call | solution.py:660
  25.7 0.5 %collective-permute-done.11.rest_3_ = f32[2,8,128]{2,1,0:T(8,128)S(1)} collective-permute-done((f32[2,8,128]{2,1,0:T(8,128)S(1)}, f32[2,8,128]{2,1,0:T(8,128)S(1)}, u32[]{:S(2)}, u32[]{:S(2)}) %collective-permute-start.11) | collective-permute-done | bytes 8224 | tf_op jit(solution)/shard_map/ppermute | solution.py:613
  26.2 2.2 %collective-permute-done.10.rest_2_ = f32[2,8,128]{2,1,0:T(8,128)S(1)} collective-permute-done((f32[2,8,128]{2,1,0:T(8,128)S(1)}, f32[2,8,128]{2,1,0:T(8,128)S(1)}, u32[]{:S(2)}, u32[]{:S(2)}) %collective-permute-start.10) | collective-permute-done | bytes 8224 | tf_op jit(solution)/shard_map/ppermute | solution.py:613
  28.3 0.3 %collective-permute-done.9.rest_1_ = f32[2,8,128]{2,1,0:T(8,128)S(1)} collective-permute-done((f32[2,8,128]{2,1,0:T(8,128)S(1)}, f32[2,8,128]{2,1,0:T(8,128)S(1)}, u32[]{:S(2)}, u32[]{:S(2)}) %collective-permute-start.9) | collective-permute-done | bytes 8224 | tf_op jit(solution)/shard_map/ppermute | solution.py:613
  28.6 1.3 %shard_map.93 = (f32[2,20,8,256]{3,2,1,0:T(8,128)}, f32[2,20,8,256]{3,2,1,0:T(8,128)}, f32[8,256]{1,0:T(8,128)}) custom-call(f32[2,20,8,256]{3,2,1,0:T(8,128)S(1)} %get-tuple-element.23.rhs, f32[4,2,20,8,256]{4,3,2,1,0:T(8,128)S(1)} %shard_map.92.vectors, f32[8,256]{1,0:T(8,128)S(1)} %get-tuple-element.25.friction, s32[8,256]{1,0:T(8,128)S(1)} %get-tuple-element.26.ice, ...), custom_call_target="tpu_custom_call" | custom-call | tf_op jit(solution)/shard_map/pallas_call | solution.py:666
  (9 shorter events, 0.3 us)
Async XLA Ops:
  1.8 10.1 %collective-permute-start.2 = (f32[62,8,128]{2,1,0:T(8,128)S(1)}, f32[62,8,128]{2,1,0:T(8,128)S(1)}, u32[]{:S(2)}, u32[]{:S(2)}) collective-permute-start(f32[62,8,128]{2,1,0:T(8,128)S(1)} %get-tuple-element.32), channel_id=1, source_target_pairs={{0,1},{4,8},{8,4},{12,13},{1,0},{5,9},{9,5},{13,12},{2,3},{6,10},{... | collective-permute-start | bytes 761864 | tf_op jit(solution)/shard_map/ppermute | solution.py:47
  2.3 10.0 %collective-permute-start.3 = (f32[62,8,128]{2,1,0:T(8,128)S(1)}, f32[62,8,128]{2,1,0:T(8,128)S(1)}, u32[]{:S(2)}, u32[]{:S(2)}) collective-permute-start(f32[62,8,128]{2,1,0:T(8,128)S(1)} %get-tuple-element.33), channel_id=1, source_target_pairs={{0,4},{4,0},{8,12},{12,8},{1,5},{5,1},{9,13},{13,9},{2,6},{6,2},{1... | collective-permute-start | bytes 761864 | tf_op jit(solution)/shard_map/ppermute | solution.py:47
  6.6 1.7 %collective-permute-start = (f32[3,8,128]{2,1,0:T(8,128)S(1)}, f32[3,8,128]{2,1,0:T(8,128)S(1)}, u32[]{:S(2)}, u32[]{:S(2)}) collective-permute-start(f32[3,8,128]{2,1,0:T(8,128)S(1)} %get-tuple-element.28), channel_id=1, source_target_pairs={{0,1},{1,0},{2,3},{3,2},{4,5},{5,4},{6,7},{7,6},{8,9},{9,8},{10,11... | collective-permute-start | bytes 36872 | tf_op jit(solution)/shard_map/ppermute | solution.py:47
  6.7 3.2 %collective-permute-start.1 = (f32[3,8,128]{2,1,0:T(8,128)S(1)}, f32[3,8,128]{2,1,0:T(8,128)S(1)}, u32[]{:S(2)}, u32[]{:S(2)}) collective-permute-start(f32[3,8,128]{2,1,0:T(8,128)S(1)} %get-tuple-element.29), channel_id=1, source_target_pairs={{0,3},{1,2},{2,1},{3,0},{4,7},{5,6},{6,5},{7,4},{8,11},{9,10},{10,... | collective-permute-start | bytes 36872 | tf_op jit(solution)/shard_map/ppermute | solution.py:47
  9.9 6.3 %collective-permute-start.5 = (f32[6,8,128]{2,1,0:T(8,128)S(1)}, f32[6,8,128]{2,1,0:T(8,128)S(1)}, u32[]{:S(2)}, u32[]{:S(2)}) collective-permute-start(f32[6,8,128]{2,1,0:T(8,128)S(1)} %shard_map.87._.columns), channel_id=1, source_target_pairs={{0,1},{4,8},{8,4},{12,13},{1,0},{5,9},{9,5},{13,12},{2,3},{6,10},{... | collective-permute-start | bytes 73736 | tf_op jit(solution)/shard_map/ppermute | solution.py:47
  10.6 5.6 %collective-permute-start.4 = (f32[6,8,128]{2,1,0:T(8,128)S(1)}, f32[6,8,128]{2,1,0:T(8,128)S(1)}, u32[]{:S(2)}, u32[]{:S(2)}) collective-permute-start(f32[6,8,128]{2,1,0:T(8,128)S(1)} %shard_map.87._.columns), channel_id=1, source_target_pairs={{0,4},{4,0},{8,12},{12,8},{1,5},{5,1},{9,13},{13,9},{2,6},{6,2},{1... | collective-permute-start | bytes 73736 | tf_op jit(solution)/shard_map/ppermute | solution.py:47
  17.0 3.1 %collective-permute-start.8 = (f32[2,8,128]{2,1,0:T(8,128)S(1)}, f32[2,8,128]{2,1,0:T(8,128)S(1)}, u32[]{:S(2)}, u32[]{:S(2)}) collective-permute-start(f32[2,8,128]{2,1,0:T(8,128)S(1)} %get-tuple-element.36.refs_0_), channel_id=1, source_target_pairs={{0,3},{1,2},{2,1},{3,0},{4,7},{5,6},{6,5},{7,4},{8,11},{9,10},{10,... | collective-permute-start | bytes 24584 | tf_op jit(solution)/shard_map/ppermute | solution.py:613
  17.9 3.7 %collective-permute-start.7 = (f32[2,8,128]{2,1,0:T(8,128)S(1)}, f32[2,8,128]{2,1,0:T(8,128)S(1)}, u32[]{:S(2)}, u32[]{:S(2)}) collective-permute-start(f32[2,8,128]{2,1,0:T(8,128)S(1)} %get-tuple-element.36.refs_0_), channel_id=1, source_target_pairs={{0,2},{1,3},{2,0},{3,1},{4,6},{5,7},{6,4},{7,5},{8,10},{9,11},{10,... | collective-permute-start | bytes 24584 | tf_op jit(solution)/shard_map/ppermute | solution.py:613
  18.6 2.9 %collective-permute-start.6 = (f32[2,8,128]{2,1,0:T(8,128)S(1)}, f32[2,8,128]{2,1,0:T(8,128)S(1)}, u32[]{:S(2)}, u32[]{:S(2)}) collective-permute-start(f32[2,8,128]{2,1,0:T(8,128)S(1)} %get-tuple-element.36.refs_0_), channel_id=1, source_target_pairs={{0,1},{1,0},{2,3},{3,2},{4,5},{5,4},{6,7},{7,6},{8,9},{9,8},{10,11... | collective-permute-start | bytes 24584 | tf_op jit(solution)/shard_map/ppermute | solution.py:613
  21.5 4.6 %collective-permute-start.11 = (f32[2,8,128]{2,1,0:T(8,128)S(1)}, f32[2,8,128]{2,1,0:T(8,128)S(1)}, u32[]{:S(2)}, u32[]{:S(2)}) collective-permute-start(f32[2,8,128]{2,1,0:T(8,128)S(1)} %shard_map.91._.rest_0_), channel_id=1, source_target_pairs={{0,8},{4,12},{8,0},{12,4},{1,9},{5,13},{9,1},{13,5},{2,10},{6,14},... | collective-permute-start | bytes 24584 | tf_op jit(solution)/shard_map/ppermute | solution.py:613
  22.9 5.5 %collective-permute-start.10 = (f32[2,8,128]{2,1,0:T(8,128)S(1)}, f32[2,8,128]{2,1,0:T(8,128)S(1)}, u32[]{:S(2)}, u32[]{:S(2)}) collective-permute-start(f32[2,8,128]{2,1,0:T(8,128)S(1)} %shard_map.91._.rest_0_), channel_id=1, source_target_pairs={{0,12},{4,8},{8,4},{12,0},{1,13},{5,9},{9,5},{13,1},{2,14},{6,10},... | collective-permute-start | bytes 24584 | tf_op jit(solution)/shard_map/ppermute | solution.py:613
  25.0 3.7 %collective-permute-start.9 = (f32[2,8,128]{2,1,0:T(8,128)S(1)}, f32[2,8,128]{2,1,0:T(8,128)S(1)}, u32[]{:S(2)}, u32[]{:S(2)}) collective-permute-start(f32[2,8,128]{2,1,0:T(8,128)S(1)} %shard_map.91._.rest_0_), channel_id=1, source_target_pairs={{0,4},{4,0},{8,12},{12,8},{1,5},{5,1},{9,13},{13,9},{2,6},{6,2},{1... | collective-permute-start | bytes 24584 | tf_op jit(solution)/shard_map/ppermute | solution.py:613

commit v23 on v22

--- a/solution.py
+++ b/solution.py
@@ -11,7 +11,7 @@
 HALO = 4
 ROWS = 8
 LANES = 128
-UNROLL = 5
+UNROLL = 4
 SLOT = 32
 
 

time: 30.1 us -> 30.4 us (level)
  transfers between devices with their start and end apart: 12 -> 12, of which waited for: 7 -> 7; matrix products, arithmetic and copies ran while one was open for 0% -> 0% of each run, Pallas kernels for 16% -> 17%
where the time goes in v23:
time: 30.4 us; the launch traced here: 30.2 us
  starting transfers between devices  13.7 us (45%)
  Pallas kernels  8.31 us (27%)
  waiting for transfers between devices  7.51 us (25%)
  between operations  0.71 us (2%)
    ppermute x6, starting transfers between devices, swapped(): return lax.ppermute(x, (*axes, spare) if spare else axes, pairs)  8.1 us
    ppermute x6, starting transfers between devices, exchange(): parts.append(lax.ppermute(x, axis, pairs))  5.62 us
    ppermute x6, waiting for transfers between devices, exchange(): parts.append(lax.ppermute(x, axis, pairs))  5.56 us
    pallas_call x1, Pallas kernels, body(): call(main_kernel, [(2,) + block] * (STEPS - 1) + [adjoint_rhs.shape, (2 *...  4.18 us
    ppermute x6, waiting for transfers between devices, swapped(): return lax.ppermute(x, (*axes, spare) if spare else axes, pairs)  1.95 us
    pallas_call x1, Pallas kernels, body(): call(final_kernel, [adjoint_rhs.shape, adjoint_rhs.shape, friction.shape])  1.34 us
    pallas_call x1, Pallas kernels, body(): call(strip_kernel, [jax.ShapeDtypeStruct(x.shape, x.dtype) for x in input...  1.13 us
    pallas_call x1, Pallas kernels, body(): call(ribbon_kernel, [(STEPS, 2, layers // 4) + tile, (2,) + tile])  0.79 us
  transfers between devices with their start and end apart: 12, of which 7 were waited for; matrix products, arithmetic and copies ran while one was open for 0% of the time, Pallas kernels for 17%

profile of v23, /device:TPU:0, one launch (start us, length us, event | category | flops | bytes accessed | tf_op | source)
XLA Modules:
  0.0 30.2 jit_solution(16333990786662384062)
XLA Ops:
  0.6 1.1 %shard_map.85 = (f32[2,20,8,256]{3,2,1,0:T(8,128)S(1)}, f32[20,8,256]{2,1,0:T(8,128)S(1)}, f32[8,256]{1,0:T(8,128)S(1)}, s32[8,256]{1,0:T(8,128)S(1)}, s32[8,256...) custom-call(f32[2,20,8,256]{3,2,1,0:T(8,128)} %refs_0_.1, ...), custom_call_target="tpu_custom_call" | custom-call | tf_op jit(solution)/shard_map/pallas_call | solution.py:628
  1.8 0.5 %collective-permute-start.2 = (f32[62,8,128]{2,1,0:T(8,128)S(1)}, f32[62,8,128]{2,1,0:T(8,128)S(1)}, u32[]{:S(2)}, u32[]{:S(2)}) collective-permute-start(f32[62,8,128]{2,1,0:T(8,128)S(1)} %get-tuple-element.32), channel_id=1, source_target_pairs={{0,1},{4,8},{8,4},{12,13},{1,0},{5,9},{9,5},{13,12},{2,3},{6,10},{... | collective-permute-start | bytes 761864 | tf_op jit(solution)/shard_map/ppermute | solution.py:47
  2.3 4.1 %collective-permute-start.3 = (f32[62,8,128]{2,1,0:T(8,128)S(1)}, f32[62,8,128]{2,1,0:T(8,128)S(1)}, u32[]{:S(2)}, u32[]{:S(2)}) collective-permute-start(f32[62,8,128]{2,1,0:T(8,128)S(1)} %get-tuple-element.33), channel_id=1, source_target_pairs={{0,4},{4,0},{8,12},{12,8},{1,5},{5,1},{9,13},{13,9},{2,6},{6,2},{1... | collective-permute-start | bytes 761864 | tf_op jit(solution)/shard_map/ppermute | solution.py:47
  6.7 1.6 %collective-permute-start.1 = (f32[3,8,128]{2,1,0:T(8,128)S(1)}, f32[3,8,128]{2,1,0:T(8,128)S(1)}, u32[]{:S(2)}, u32[]{:S(2)}) collective-permute-start(f32[3,8,128]{2,1,0:T(8,128)S(1)} %get-tuple-element.29), channel_id=1, source_target_pairs={{0,3},{1,2},{2,1},{3,0},{4,7},{5,6},{6,5},{7,4},{8,11},{9,10},{10,... | collective-permute-start | bytes 36872 | tf_op jit(solution)/shard_map/ppermute | solution.py:47
  8.3 1.6 %collective-permute-done.1.from_b = f32[3,8,128]{2,1,0:T(8,128)S(1)} collective-permute-done((f32[3,8,128]{2,1,0:T(8,128)S(1)}, f32[3,8,128]{2,1,0:T(8,128)S(1)}, u32[]{:S(2)}, u32[]{:S(2)}) %collective-permute-start.1) | collective-permute-done | bytes 12320 | tf_op jit(solution)/shard_map/ppermute | solution.py:47
  9.9 0.7 %collective-permute-start.5 = (f32[6,8,128]{2,1,0:T(8,128)S(1)}, f32[6,8,128]{2,1,0:T(8,128)S(1)}, u32[]{:S(2)}, u32[]{:S(2)}) collective-permute-start(f32[6,8,128]{2,1,0:T(8,128)S(1)} %shard_map.87._.columns), channel_id=1, source_target_pairs={{0,1},{4,8},{8,4},{12,13},{1,0},{5,9},{9,5},{13,12},{2,3},{6,10},{... | collective-permute-start | bytes 73736 | tf_op jit(solution)/shard_map/ppermute | solution.py:47
  10.6 1.0 %collective-permute-start.4 = (f32[6,8,128]{2,1,0:T(8,128)S(1)}, f32[6,8,128]{2,1,0:T(8,128)S(1)}, u32[]{:S(2)}, u32[]{:S(2)}) collective-permute-start(f32[6,8,128]{2,1,0:T(8,128)S(1)} %shard_map.87._.columns), channel_id=1, source_target_pairs={{0,4},{4,0},{8,12},{12,8},{1,5},{5,1},{9,13},{13,9},{2,6},{6,2},{1... | collective-permute-start | bytes 73736 | tf_op jit(solution)/shard_map/ppermute | solution.py:47
  11.7 0.2 shard_map.88
  11.9 0.4 %collective-permute-done.3.strip_a = f32[62,8,128]{2,1,0:T(8,128)S(1)} collective-permute-done((f32[62,8,128]{2,1,0:T(8,128)S(1)}, f32[62,8,128]{2,1,0:T(8,128)S(1)}, u32[]{:S(2)}, u32[]{:S(2)}) %collective-permute-start.3) | collective-permute-done | bytes 253984 | tf_op jit(solution)/shard_map/ppermute | solution.py:47
  12.3 4.2 %shard_map.89 = (f32[2,20,16,256]{3,2,1,0:T(8,128)S(1)}, f32[2,20,16,256]{3,2,1,0:T(8,128)S(1)}, f32[2,20,16,256]{3,2,1,0:T(8,128)S(1)}, f32[2,20,8,256]{3,2,1,0...) custom-call(f32[2,20,8,256]{3,2,1,0:T(8,128)S(1)} %get-tuple-element.23.rhs, ...), custom_call_target="tpu_custom_call" | custom-call | flops 200000000 | bytes 8000000 | tf_op jit(solution)/shard_map/pallas_call | solution.py:645
  16.5 0.8 %shard_map.90 = (f32[4,2,5,8,128]{4,3,2,1,0:T(8,128)S(1)}, f32[2,8,128]{2,1,0:T(8,128)S(1)}) custom-call(f32[17,8,128]{2,1,0:T(8,128)S(1)} %get-tuple-element.30.own, f32[17,8,128]{2,1,0:T(8,128)S(1)} %get-tuple-element.34.halo, f32[6,8,128]{2,1,0:T(8,128)S(1)} %shard_map.87._.columns, f32[6,8,128]{2,1,0:T(8,128)S(1)} %collective-permute-done.4.columns_a, ...), custom_call_target="tpu_custom_call" | custom-call | tf_op jit(solution)/shard_map/pallas_call | solution.py:651
  17.3 0.9 %collective-permute-start.8 = (f32[2,8,128]{2,1,0:T(8,128)S(1)}, f32[2,8,128]{2,1,0:T(8,128)S(1)}, u32[]{:S(2)}, u32[]{:S(2)}) collective-permute-start(f32[2,8,128]{2,1,0:T(8,128)S(1)} %get-tuple-element.36.refs_0_), channel_id=1, source_target_pairs={{0,3},{1,2},{2,1},{3,0},{4,7},{5,6},{6,5},{7,4},{8,11},{9,10},{10,... | collective-permute-start | bytes 24584 | tf_op jit(solution)/shard_map/ppermute | solution.py:613
  18.1 0.7 %collective-permute-start.7 = (f32[2,8,128]{2,1,0:T(8,128)S(1)}, f32[2,8,128]{2,1,0:T(8,128)S(1)}, u32[]{:S(2)}, u32[]{:S(2)}) collective-permute-start(f32[2,8,128]{2,1,0:T(8,128)S(1)} %get-tuple-element.36.refs_0_), channel_id=1, source_target_pairs={{0,2},{1,3},{2,0},{3,1},{4,6},{5,7},{6,4},{7,5},{8,10},{9,11},{10,... | collective-permute-start | bytes 24584 | tf_op jit(solution)/shard_map/ppermute | solution.py:613
  18.9 0.3 collective-permute-start.6
  19.2 1.3 %collective-permute-done.8.refs_3_ = f32[2,8,128]{2,1,0:T(8,128)S(1)} collective-permute-done((f32[2,8,128]{2,1,0:T(8,128)S(1)}, f32[2,8,128]{2,1,0:T(8,128)S(1)}, u32[]{:S(2)}, u32[]{:S(2)}) %collective-permute-start.8) | collective-permute-done | bytes 8224 | tf_op jit(solution)/shard_map/ppermute | solution.py:613
  20.4 1.4 %collective-permute-done.7.refs_2_ = f32[2,8,128]{2,1,0:T(8,128)S(1)} collective-permute-done((f32[2,8,128]{2,1,0:T(8,128)S(1)}, f32[2,8,128]{2,1,0:T(8,128)S(1)}, u32[]{:S(2)}, u32[]{:S(2)}) %collective-permute-start.7) | collective-permute-done | bytes 8224 | tf_op jit(solution)/shard_map/ppermute | solution.py:613
  21.8 1.3 %collective-permute-start.11 = (f32[2,8,128]{2,1,0:T(8,128)S(1)}, f32[2,8,128]{2,1,0:T(8,128)S(1)}, u32[]{:S(2)}, u32[]{:S(2)}) collective-permute-start(f32[2,8,128]{2,1,0:T(8,128)S(1)} %shard_map.91._.rest_0_), channel_id=1, source_target_pairs={{0,8},{4,12},{8,0},{12,4},{1,9},{5,13},{9,1},{13,5},{2,10},{6,14},... | collective-permute-start | bytes 24584 | tf_op jit(solution)/shard_map/ppermute | solution.py:613
  23.1 2.1 %collective-permute-start.10 = (f32[2,8,128]{2,1,0:T(8,128)S(1)}, f32[2,8,128]{2,1,0:T(8,128)S(1)}, u32[]{:S(2)}, u32[]{:S(2)}) collective-permute-start(f32[2,8,128]{2,1,0:T(8,128)S(1)} %shard_map.91._.rest_0_), channel_id=1, source_target_pairs={{0,12},{4,8},{8,4},{12,0},{1,13},{5,9},{9,5},{13,1},{2,14},{6,10},... | collective-permute-start | bytes 24584 | tf_op jit(solution)/shard_map/ppermute | solution.py:613
  25.2 0.3 collective-permute-start.9
  25.5 0.4 %shard_map.92.vectors = f32[4,2,20,8,256]{4,3,2,1,0:T(8,128)S(1)} custom-call(f32[2,8,128]{2,1,0:T(8,128)S(1)} %shard_map.91._.rest_0_, f32[2,20,8,256]{3,2,1,0:T(8,128)S(1)} %get-tuple-element.23.rhs, s32[8,256]{1,0:T(8,128)S(1)} %get-tuple-element.26.ice, f32[2,20,16,256]{3,2,1,0:T(8,128)S(1)} %get-tuple-element.37.power_1, ...), custom_call_target="tpu_custom_call" | custom-call | tf_op jit(solution)/shard_map/pallas_call | solution.py:660
  26.0 0.5 %collective-permute-done.11.rest_3_ = f32[2,8,128]{2,1,0:T(8,128)S(1)} collective-permute-done((f32[2,8,128]{2,1,0:T(8,128)S(1)}, f32[2,8,128]{2,1,0:T(8,128)S(1)}, u32[]{:S(2)}, u32[]{:S(2)}) %collective-permute-start.11) | collective-permute-done | bytes 8224 | tf_op jit(solution)/shard_map/ppermute | solution.py:613
  26.4 2.2 %collective-permute-done.10.rest_2_ = f32[2,8,128]{2,1,0:T(8,128)S(1)} collective-permute-done((f32[2,8,128]{2,1,0:T(8,128)S(1)}, f32[2,8,128]{2,1,0:T(8,128)S(1)}, u32[]{:S(2)}, u32[]{:S(2)}) %collective-permute-start.10) | collective-permute-done | bytes 8224 | tf_op jit(solution)/shard_map/ppermute | solution.py:613
  28.6 0.3 %collective-permute-done.9.rest_1_ = f32[2,8,128]{2,1,0:T(8,128)S(1)} collective-permute-done((f32[2,8,128]{2,1,0:T(8,128)S(1)}, f32[2,8,128]{2,1,0:T(8,128)S(1)}, u32[]{:S(2)}, u32[]{:S(2)}) %collective-permute-start.9) | collective-permute-done | bytes 8224 | tf_op jit(solution)/shard_map/ppermute | solution.py:613
  28.9 1.3 %shard_map.93 = (f32[2,20,8,256]{3,2,1,0:T(8,128)}, f32[2,20,8,256]{3,2,1,0:T(8,128)}, f32[8,256]{1,0:T(8,128)}) custom-call(f32[2,20,8,256]{3,2,1,0:T(8,128)S(1)} %get-tuple-element.23.rhs, f32[4,2,20,8,256]{4,3,2,1,0:T(8,128)S(1)} %shard_map.92.vectors, f32[8,256]{1,0:T(8,128)S(1)} %get-tuple-element.25.friction, s32[8,256]{1,0:T(8,128)S(1)} %get-tuple-element.26.ice, ...), custom_call_target="tpu_custom_call" | custom-call | tf_op jit(solution)/shard_map/pallas_call | solution.py:666
  (9 shorter events, 0.3 us)
Async XLA Ops:
  1.8 10.1 %collective-permute-start.2 = (f32[62,8,128]{2,1,0:T(8,128)S(1)}, f32[62,8,128]{2,1,0:T(8,128)S(1)}, u32[]{:S(2)}, u32[]{:S(2)}) collective-permute-start(f32[62,8,128]{2,1,0:T(8,128)S(1)} %get-tuple-element.32), channel_id=1, source_target_pairs={{0,1},{4,8},{8,4},{12,13},{1,0},{5,9},{9,5},{13,12},{2,3},{6,10},{... | collective-permute-start | bytes 761864 | tf_op jit(solution)/shard_map/ppermute | solution.py:47
  2.3 10.0 %collective-permute-start.3 = (f32[62,8,128]{2,1,0:T(8,128)S(1)}, f32[62,8,128]{2,1,0:T(8,128)S(1)}, u32[]{:S(2)}, u32[]{:S(2)}) collective-permute-start(f32[62,8,128]{2,1,0:T(8,128)S(1)} %get-tuple-element.33), channel_id=1, source_target_pairs={{0,4},{4,0},{8,12},{12,8},{1,5},{5,1},{9,13},{13,9},{2,6},{6,2},{1... | collective-permute-start | bytes 761864 | tf_op jit(solution)/shard_map/ppermute | solution.py:47
  6.6 1.7 %collective-permute-start = (f32[3,8,128]{2,1,0:T(8,128)S(1)}, f32[3,8,128]{2,1,0:T(8,128)S(1)}, u32[]{:S(2)}, u32[]{:S(2)}) collective-permute-start(f32[3,8,128]{2,1,0:T(8,128)S(1)} %get-tuple-element.28), channel_id=1, source_target_pairs={{0,1},{1,0},{2,3},{3,2},{4,5},{5,4},{6,7},{7,6},{8,9},{9,8},{10,11... | collective-permute-start | bytes 36872 | tf_op jit(solution)/shard_map/ppermute | solution.py:47
  6.7 3.2 %collective-permute-start.1 = (f32[3,8,128]{2,1,0:T(8,128)S(1)}, f32[3,8,128]{2,1,0:T(8,128)S(1)}, u32[]{:S(2)}, u32[]{:S(2)}) collective-permute-start(f32[3,8,128]{2,1,0:T(8,128)S(1)} %get-tuple-element.29), channel_id=1, source_target_pairs={{0,3},{1,2},{2,1},{3,0},{4,7},{5,6},{6,5},{7,4},{8,11},{9,10},{10,... | collective-permute-start | bytes 36872 | tf_op jit(solution)/shard_map/ppermute | solution.py:47
  9.9 6.6 %collective-permute-start.5 = (f32[6,8,128]{2,1,0:T(8,128)S(1)}, f32[6,8,128]{2,1,0:T(8,128)S(1)}, u32[]{:S(2)}, u32[]{:S(2)}) collective-permute-start(f32[6,8,128]{2,1,0:T(8,128)S(1)} %shard_map.87._.columns), channel_id=1, source_target_pairs={{0,1},{4,8},{8,4},{12,13},{1,0},{5,9},{9,5},{13,12},{2,3},{6,10},{... | collective-permute-start | bytes 73736 | tf_op jit(solution)/shard_map/ppermute | solution.py:47
  10.6 5.8 %collective-permute-start.4 = (f32[6,8,128]{2,1,0:T(8,128)S(1)}, f32[6,8,128]{2,1,0:T(8,128)S(1)}, u32[]{:S(2)}, u32[]{:S(2)}) collective-permute-start(f32[6,8,128]{2,1,0:T(8,128)S(1)} %shard_map.87._.columns), channel_id=1, source_target_pairs={{0,4},{4,0},{8,12},{12,8},{1,5},{5,1},{9,13},{13,9},{2,6},{6,2},{1... | collective-permute-start | bytes 73736 | tf_op jit(solution)/shard_map/ppermute | solution.py:47
  17.3 3.1 %collective-permute-start.8 = (f32[2,8,128]{2,1,0:T(8,128)S(1)}, f32[2,8,128]{2,1,0:T(8,128)S(1)}, u32[]{:S(2)}, u32[]{:S(2)}) collective-permute-start(f32[2,8,128]{2,1,0:T(8,128)S(1)} %get-tuple-element.36.refs_0_), channel_id=1, source_target_pairs={{0,3},{1,2},{2,1},{3,0},{4,7},{5,6},{6,5},{7,4},{8,11},{9,10},{10,... | collective-permute-start | bytes 24584 | tf_op jit(solution)/shard_map/ppermute | solution.py:613
  18.1 3.7 %collective-permute-start.7 = (f32[2,8,128]{2,1,0:T(8,128)S(1)}, f32[2,8,128]{2,1,0:T(8,128)S(1)}, u32[]{:S(2)}, u32[]{:S(2)}) collective-permute-start(f32[2,8,128]{2,1,0:T(8,128)S(1)} %get-tuple-element.36.refs_0_), channel_id=1, source_target_pairs={{0,2},{1,3},{2,0},{3,1},{4,6},{5,7},{6,4},{7,5},{8,10},{9,11},{10,... | collective-permute-start | bytes 24584 | tf_op jit(solution)/shard_map/ppermute | solution.py:613
  18.9 2.9 %collective-permute-start.6 = (f32[2,8,128]{2,1,0:T(8,128)S(1)}, f32[2,8,128]{2,1,0:T(8,128)S(1)}, u32[]{:S(2)}, u32[]{:S(2)}) collective-permute-start(f32[2,8,128]{2,1,0:T(8,128)S(1)} %get-tuple-element.36.refs_0_), channel_id=1, source_target_pairs={{0,1},{1,0},{2,3},{3,2},{4,5},{5,4},{6,7},{7,6},{8,9},{9,8},{10,11... | collective-permute-start | bytes 24584 | tf_op jit(solution)/shard_map/ppermute | solution.py:613
  21.8 4.6 %collective-permute-start.11 = (f32[2,8,128]{2,1,0:T(8,128)S(1)}, f32[2,8,128]{2,1,0:T(8,128)S(1)}, u32[]{:S(2)}, u32[]{:S(2)}) collective-permute-start(f32[2,8,128]{2,1,0:T(8,128)S(1)} %shard_map.91._.rest_0_), channel_id=1, source_target_pairs={{0,8},{4,12},{8,0},{12,4},{1,9},{5,13},{9,1},{13,5},{2,10},{6,14},... | collective-permute-start | bytes 24584 | tf_op jit(solution)/shard_map/ppermute | solution.py:613
  23.1 5.5 %collective-permute-start.10 = (f32[2,8,128]{2,1,0:T(8,128)S(1)}, f32[2,8,128]{2,1,0:T(8,128)S(1)}, u32[]{:S(2)}, u32[]{:S(2)}) collective-permute-start(f32[2,8,128]{2,1,0:T(8,128)S(1)} %shard_map.91._.rest_0_), channel_id=1, source_target_pairs={{0,12},{4,8},{8,4},{12,0},{1,13},{5,9},{9,5},{13,1},{2,14},{6,10},... | collective-permute-start | bytes 24584 | tf_op jit(solution)/shard_map/ppermute | solution.py:613
  25.2 3.7 %collective-permute-start.9 = (f32[2,8,128]{2,1,0:T(8,128)S(1)}, f32[2,8,128]{2,1,0:T(8,128)S(1)}, u32[]{:S(2)}, u32[]{:S(2)}) collective-permute-start(f32[2,8,128]{2,1,0:T(8,128)S(1)} %shard_map.91._.rest_0_), channel_id=1, source_target_pairs={{0,4},{4,0},{8,12},{12,8},{1,5},{5,1},{9,13},{13,9},{2,6},{6,2},{1... | collective-permute-start | bytes 24584 | tf_op jit(solution)/shard_map/ppermute | solution.py:613

commit v24 on v23

--- a/solution.py
+++ b/solution.py
@@ -11,7 +11,7 @@
 HALO = 4
 ROWS = 8
 LANES = 128
-UNROLL = 4
+UNROLL = 10
 SLOT = 32
 
 

time: 30.4 us -> 31.4 us (1.033)
  Pallas kernels: 8.31 us -> 9.3 us
    pallas_call x1, Pallas kernels: 4.18 us -> 5.17 us  [body(): call(main_kernel, [(2,) + block] * (STEPS - 1) + [adjoint_rhs.shape, (2 *...]
  transfers between devices with their start and end apart: 12 -> 12, of which waited for: 7 -> 7; matrix products, arithmetic and copies ran while one was open for 0% -> 0% of each run, Pallas kernels for 17% -> 19%
where the time goes in v24:
time: 31.4 us; the launch traced here: 31.2 us
  starting transfers between devices  13.7 us (44%)
  Pallas kernels  9.3 us (30%)
  waiting for transfers between devices  7.51 us (24%)
  between operations  0.71 us (2%)
    ppermute x6, starting transfers between devices, swapped(): return lax.ppermute(x, (*axes, spare) if spare else axes, pairs)  8.1 us
    ppermute x6, starting transfers between devices, exchange(): parts.append(lax.ppermute(x, axis, pairs))  5.62 us
    ppermute x6, waiting for transfers between devices, exchange(): parts.append(lax.ppermute(x, axis, pairs))  5.56 us
    pallas_call x1, Pallas kernels, body(): call(main_kernel, [(2,) + block] * (STEPS - 1) + [adjoint_rhs.shape, (2 *...  5.17 us
    ppermute x6, waiting for transfers between devices, swapped(): return lax.ppermute(x, (*axes, spare) if spare else axes, pairs)  1.95 us
    pallas_call x1, Pallas kernels, body(): call(final_kernel, [adjoint_rhs.shape, adjoint_rhs.shape, friction.shape])  1.34 us
    pallas_call x1, Pallas kernels, body(): call(strip_kernel, [jax.ShapeDtypeStruct(x.shape, x.dtype) for x in input...  1.13 us
    pallas_call x1, Pallas kernels, body(): call(ribbon_kernel, [(STEPS, 2, layers // 4) + tile, (2,) + tile])  0.79 us
  transfers between devices with their start and end apart: 12, of which 7 were waited for; matrix products, arithmetic and copies ran while one was open for 0% of the time, Pallas kernels for 19%

profile of v24, /device:TPU:0, one launch (start us, length us, event | category | flops | bytes accessed | tf_op | source)
XLA Modules:
  0.0 31.2 jit_solution(17942554407296482093)
XLA Ops:
  0.6 1.1 %shard_map.85 = (f32[2,20,8,256]{3,2,1,0:T(8,128)S(1)}, f32[20,8,256]{2,1,0:T(8,128)S(1)}, f32[8,256]{1,0:T(8,128)S(1)}, s32[8,256]{1,0:T(8,128)S(1)}, s32[8,256...) custom-call(f32[2,20,8,256]{3,2,1,0:T(8,128)} %refs_0_.1, ...), custom_call_target="tpu_custom_call" | custom-call | tf_op jit(solution)/shard_map/pallas_call | solution.py:628
  1.8 0.5 %collective-permute-start.2 = (f32[62,8,128]{2,1,0:T(8,128)S(1)}, f32[62,8,128]{2,1,0:T(8,128)S(1)}, u32[]{:S(2)}, u32[]{:S(2)}) collective-permute-start(f32[62,8,128]{2,1,0:T(8,128)S(1)} %get-tuple-element.32), channel_id=1, source_target_pairs={{0,1},{4,8},{8,4},{12,13},{1,0},{5,9},{9,5},{13,12},{2,3},{6,10},{... | collective-permute-start | bytes 761864 | tf_op jit(solution)/shard_map/ppermute | solution.py:47
  2.3 4.1 %collective-permute-start.3 = (f32[62,8,128]{2,1,0:T(8,128)S(1)}, f32[62,8,128]{2,1,0:T(8,128)S(1)}, u32[]{:S(2)}, u32[]{:S(2)}) collective-permute-start(f32[62,8,128]{2,1,0:T(8,128)S(1)} %get-tuple-element.33), channel_id=1, source_target_pairs={{0,4},{4,0},{8,12},{12,8},{1,5},{5,1},{9,13},{13,9},{2,6},{6,2},{1... | collective-permute-start | bytes 761864 | tf_op jit(solution)/shard_map/ppermute | solution.py:47
  6.7 1.6 %collective-permute-start.1 = (f32[3,8,128]{2,1,0:T(8,128)S(1)}, f32[3,8,128]{2,1,0:T(8,128)S(1)}, u32[]{:S(2)}, u32[]{:S(2)}) collective-permute-start(f32[3,8,128]{2,1,0:T(8,128)S(1)} %get-tuple-element.29), channel_id=1, source_target_pairs={{0,3},{1,2},{2,1},{3,0},{4,7},{5,6},{6,5},{7,4},{8,11},{9,10},{10,... | collective-permute-start | bytes 36872 | tf_op jit(solution)/shard_map/ppermute | solution.py:47
  8.3 1.6 %collective-permute-done.1.from_b = f32[3,8,128]{2,1,0:T(8,128)S(1)} collective-permute-done((f32[3,8,128]{2,1,0:T(8,128)S(1)}, f32[3,8,128]{2,1,0:T(8,128)S(1)}, u32[]{:S(2)}, u32[]{:S(2)}) %collective-permute-start.1) | collective-permute-done | bytes 12320 | tf_op jit(solution)/shard_map/ppermute | solution.py:47
  9.9 0.7 %collective-permute-start.5 = (f32[6,8,128]{2,1,0:T(8,128)S(1)}, f32[6,8,128]{2,1,0:T(8,128)S(1)}, u32[]{:S(2)}, u32[]{:S(2)}) collective-permute-start(f32[6,8,128]{2,1,0:T(8,128)S(1)} %shard_map.87._.columns), channel_id=1, source_target_pairs={{0,1},{4,8},{8,4},{12,13},{1,0},{5,9},{9,5},{13,12},{2,3},{6,10},{... | collective-permute-start | bytes 73736 | tf_op jit(solution)/shard_map/ppermute | solution.py:47
  10.6 1.0 %collective-permute-start.4 = (f32[6,8,128]{2,1,0:T(8,128)S(1)}, f32[6,8,128]{2,1,0:T(8,128)S(1)}, u32[]{:S(2)}, u32[]{:S(2)}) collective-permute-start(f32[6,8,128]{2,1,0:T(8,128)S(1)} %shard_map.87._.columns), channel_id=1, source_target_pairs={{0,4},{4,0},{8,12},{12,8},{1,5},{5,1},{9,13},{13,9},{2,6},{6,2},{1... | collective-permute-start | bytes 73736 | tf_op jit(solution)/shard_map/ppermute | solution.py:47
  11.7 0.2 shard_map.88
  11.9 0.4 %collective-permute-done.3.strip_a = f32[62,8,128]{2,1,0:T(8,128)S(1)} collective-permute-done((f32[62,8,128]{2,1,0:T(8,128)S(1)}, f32[62,8,128]{2,1,0:T(8,128)S(1)}, u32[]{:S(2)}, u32[]{:S(2)}) %collective-permute-start.3) | collective-permute-done | bytes 253984 | tf_op jit(solution)/shard_map/ppermute | solution.py:47
  12.3 5.2 %shard_map.89 = (f32[2,20,16,256]{3,2,1,0:T(8,128)S(1)}, f32[2,20,16,256]{3,2,1,0:T(8,128)S(1)}, f32[2,20,16,256]{3,2,1,0:T(8,128)S(1)}, f32[2,20,8,256]{3,2,1,0...) custom-call(f32[2,20,8,256]{3,2,1,0:T(8,128)S(1)} %get-tuple-element.23.rhs, ...), custom_call_target="tpu_custom_call" | custom-call | flops 200000000 | bytes 8000000 | tf_op jit(solution)/shard_map/pallas_call | solution.py:645
  17.5 0.8 %shard_map.90 = (f32[4,2,5,8,128]{4,3,2,1,0:T(8,128)S(1)}, f32[2,8,128]{2,1,0:T(8,128)S(1)}) custom-call(f32[17,8,128]{2,1,0:T(8,128)S(1)} %get-tuple-element.30.own, f32[17,8,128]{2,1,0:T(8,128)S(1)} %get-tuple-element.34.halo, f32[6,8,128]{2,1,0:T(8,128)S(1)} %shard_map.87._.columns, f32[6,8,128]{2,1,0:T(8,128)S(1)} %collective-permute-done.4.columns_a, ...), custom_call_target="tpu_custom_call" | custom-call | tf_op jit(solution)/shard_map/pallas_call | solution.py:651
  18.3 0.9 %collective-permute-start.8 = (f32[2,8,128]{2,1,0:T(8,128)S(1)}, f32[2,8,128]{2,1,0:T(8,128)S(1)}, u32[]{:S(2)}, u32[]{:S(2)}) collective-permute-start(f32[2,8,128]{2,1,0:T(8,128)S(1)} %get-tuple-element.36.refs_0_), channel_id=1, source_target_pairs={{0,3},{1,2},{2,1},{3,0},{4,7},{5,6},{6,5},{7,4},{8,11},{9,10},{10,... | collective-permute-start | bytes 24584 | tf_op jit(solution)/shard_map/ppermute | solution.py:613
  19.1 0.7 %collective-permute-start.7 = (f32[2,8,128]{2,1,0:T(8,128)S(1)}, f32[2,8,128]{2,1,0:T(8,128)S(1)}, u32[]{:S(2)}, u32[]{:S(2)}) collective-permute-start(f32[2,8,128]{2,1,0:T(8,128)S(1)} %get-tuple-element.36.refs_0_), channel_id=1, source_target_pairs={{0,2},{1,3},{2,0},{3,1},{4,6},{5,7},{6,4},{7,5},{8,10},{9,11},{10,... | collective-permute-start | bytes 24584 | tf_op jit(solution)/shard_map/ppermute | solution.py:613
  19.9 0.3 collective-permute-start.6
  20.2 1.3 %collective-permute-done.8.refs_3_ = f32[2,8,128]{2,1,0:T(8,128)S(1)} collective-permute-done((f32[2,8,128]{2,1,0:T(8,128)S(1)}, f32[2,8,128]{2,1,0:T(8,128)S(1)}, u32[]{:S(2)}, u32[]{:S(2)}) %collective-permute-start.8) | collective-permute-done | bytes 8224 | tf_op jit(solution)/shard_map/ppermute | solution.py:613
  21.4 1.4 %collective-permute-done.7.refs_2_ = f32[2,8,128]{2,1,0:T(8,128)S(1)} collective-permute-done((f32[2,8,128]{2,1,0:T(8,128)S(1)}, f32[2,8,128]{2,1,0:T(8,128)S(1)}, u32[]{:S(2)}, u32[]{:S(2)}) %collective-permute-start.7) | collective-permute-done | bytes 8224 | tf_op jit(solution)/shard_map/ppermute | solution.py:613
  22.8 1.3 %collective-permute-start.11 = (f32[2,8,128]{2,1,0:T(8,128)S(1)}, f32[2,8,128]{2,1,0:T(8,128)S(1)}, u32[]{:S(2)}, u32[]{:S(2)}) collective-permute-start(f32[2,8,128]{2,1,0:T(8,128)S(1)} %shard_map.91._.rest_0_), channel_id=1, source_target_pairs={{0,8},{4,12},{8,0},{12,4},{1,9},{5,13},{9,1},{13,5},{2,10},{6,14},... | collective-permute-start | bytes 24584 | tf_op jit(solution)/shard_map/ppermute | solution.py:613
  24.1 2.1 %collective-permute-start.10 = (f32[2,8,128]{2,1,0:T(8,128)S(1)}, f32[2,8,128]{2,1,0:T(8,128)S(1)}, u32[]{:S(2)}, u32[]{:S(2)}) collective-permute-start(f32[2,8,128]{2,1,0:T(8,128)S(1)} %shard_map.91._.rest_0_), channel_id=1, source_target_pairs={{0,12},{4,8},{8,4},{12,0},{1,13},{5,9},{9,5},{13,1},{2,14},{6,10},... | collective-permute-start | bytes 24584 | tf_op jit(solution)/shard_map/ppermute | solution.py:613
  26.2 0.3 collective-permute-start.9
  26.5 0.4 %shard_map.92.vectors = f32[4,2,20,8,256]{4,3,2,1,0:T(8,128)S(1)} custom-call(f32[2,8,128]{2,1,0:T(8,128)S(1)} %shard_map.91._.rest_0_, f32[2,20,8,256]{3,2,1,0:T(8,128)S(1)} %get-tuple-element.23.rhs, s32[8,256]{1,0:T(8,128)S(1)} %get-tuple-element.26.ice, f32[2,20,16,256]{3,2,1,0:T(8,128)S(1)} %get-tuple-element.37.power_1, ...), custom_call_target="tpu_custom_call" | custom-call | tf_op jit(solution)/shard_map/pallas_call | solution.py:660
  26.9 0.5 %collective-permute-done.11.rest_3_ = f32[2,8,128]{2,1,0:T(8,128)S(1)} collective-permute-done((f32[2,8,128]{2,1,0:T(8,128)S(1)}, f32[2,8,128]{2,1,0:T(8,128)S(1)}, u32[]{:S(2)}, u32[]{:S(2)}) %collective-permute-start.11) | collective-permute-done | bytes 8224 | tf_op jit(solution)/shard_map/ppermute | solution.py:613
  27.4 2.2 %collective-permute-done.10.rest_2_ = f32[2,8,128]{2,1,0:T(8,128)S(1)} collective-permute-done((f32[2,8,128]{2,1,0:T(8,128)S(1)}, f32[2,8,128]{2,1,0:T(8,128)S(1)}, u32[]{:S(2)}, u32[]{:S(2)}) %collective-permute-start.10) | collective-permute-done | bytes 8224 | tf_op jit(solution)/shard_map/ppermute | solution.py:613
  29.6 0.3 collective-permute-done.9.rest_1_
  29.9 1.3 %shard_map.93 = (f32[2,20,8,256]{3,2,1,0:T(8,128)}, f32[2,20,8,256]{3,2,1,0:T(8,128)}, f32[8,256]{1,0:T(8,128)}) custom-call(f32[2,20,8,256]{3,2,1,0:T(8,128)S(1)} %get-tuple-element.23.rhs, f32[4,2,20,8,256]{4,3,2,1,0:T(8,128)S(1)} %shard_map.92.vectors, f32[8,256]{1,0:T(8,128)S(1)} %get-tuple-element.25.friction, s32[8,256]{1,0:T(8,128)S(1)} %get-tuple-element.26.ice, ...), custom_call_target="tpu_custom_call" | custom-call | tf_op jit(solution)/shard_map/pallas_call | solution.py:666
  (9 shorter events, 0.3 us)
Async XLA Ops:
  1.8 10.1 %collective-permute-start.2 = (f32[62,8,128]{2,1,0:T(8,128)S(1)}, f32[62,8,128]{2,1,0:T(8,128)S(1)}, u32[]{:S(2)}, u32[]{:S(2)}) collective-permute-start(f32[62,8,128]{2,1,0:T(8,128)S(1)} %get-tuple-element.32), channel_id=1, source_target_pairs={{0,1},{4,8},{8,4},{12,13},{1,0},{5,9},{9,5},{13,12},{2,3},{6,10},{... | collective-permute-start | bytes 761864 | tf_op jit(solution)/shard_map/ppermute | solution.py:47
  2.3 10.0 %collective-permute-start.3 = (f32[62,8,128]{2,1,0:T(8,128)S(1)}, f32[62,8,128]{2,1,0:T(8,128)S(1)}, u32[]{:S(2)}, u32[]{:S(2)}) collective-permute-start(f32[62,8,128]{2,1,0:T(8,128)S(1)} %get-tuple-element.33), channel_id=1, source_target_pairs={{0,4},{4,0},{8,12},{12,8},{1,5},{5,1},{9,13},{13,9},{2,6},{6,2},{1... | collective-permute-start | bytes 761864 | tf_op jit(solution)/shard_map/ppermute | solution.py:47
  6.6 1.7 %collective-permute-start = (f32[3,8,128]{2,1,0:T(8,128)S(1)}, f32[3,8,128]{2,1,0:T(8,128)S(1)}, u32[]{:S(2)}, u32[]{:S(2)}) collective-permute-start(f32[3,8,128]{2,1,0:T(8,128)S(1)} %get-tuple-element.28), channel_id=1, source_target_pairs={{0,1},{1,0},{2,3},{3,2},{4,5},{5,4},{6,7},{7,6},{8,9},{9,8},{10,11... | collective-permute-start | bytes 36872 | tf_op jit(solution)/shard_map/ppermute | solution.py:47
  6.7 3.2 %collective-permute-start.1 = (f32[3,8,128]{2,1,0:T(8,128)S(1)}, f32[3,8,128]{2,1,0:T(8,128)S(1)}, u32[]{:S(2)}, u32[]{:S(2)}) collective-permute-start(f32[3,8,128]{2,1,0:T(8,128)S(1)} %get-tuple-element.29), channel_id=1, source_target_pairs={{0,3},{1,2},{2,1},{3,0},{4,7},{5,6},{6,5},{7,4},{8,11},{9,10},{10,... | collective-permute-start | bytes 36872 | tf_op jit(solution)/shard_map/ppermute | solution.py:47
  9.9 7.6 %collective-permute-start.5 = (f32[6,8,128]{2,1,0:T(8,128)S(1)}, f32[6,8,128]{2,1,0:T(8,128)S(1)}, u32[]{:S(2)}, u32[]{:S(2)}) collective-permute-start(f32[6,8,128]{2,1,0:T(8,128)S(1)} %shard_map.87._.columns), channel_id=1, source_target_pairs={{0,1},{4,8},{8,4},{12,13},{1,0},{5,9},{9,5},{13,12},{2,3},{6,10},{... | collective-permute-start | bytes 73736 | tf_op jit(solution)/shard_map/ppermute | solution.py:47
  10.6 6.8 %collective-permute-start.4 = (f32[6,8,128]{2,1,0:T(8,128)S(1)}, f32[6,8,128]{2,1,0:T(8,128)S(1)}, u32[]{:S(2)}, u32[]{:S(2)}) collective-permute-start(f32[6,8,128]{2,1,0:T(8,128)S(1)} %shard_map.87._.columns), channel_id=1, source_target_pairs={{0,4},{4,0},{8,12},{12,8},{1,5},{5,1},{9,13},{13,9},{2,6},{6,2},{1... | collective-permute-start | bytes 73736 | tf_op jit(solution)/shard_map/ppermute | solution.py:47
  18.3 3.1 %collective-permute-start.8 = (f32[2,8,128]{2,1,0:T(8,128)S(1)}, f32[2,8,128]{2,1,0:T(8,128)S(1)}, u32[]{:S(2)}, u32[]{:S(2)}) collective-permute-start(f32[2,8,128]{2,1,0:T(8,128)S(1)} %get-tuple-element.36.refs_0_), channel_id=1, source_target_pairs={{0,3},{1,2},{2,1},{3,0},{4,7},{5,6},{6,5},{7,4},{8,11},{9,10},{10,... | collective-permute-start | bytes 24584 | tf_op jit(solution)/shard_map/ppermute | solution.py:613
  19.1 3.7 %collective-permute-start.7 = (f32[2,8,128]{2,1,0:T(8,128)S(1)}, f32[2,8,128]{2,1,0:T(8,128)S(1)}, u32[]{:S(2)}, u32[]{:S(2)}) collective-permute-start(f32[2,8,128]{2,1,0:T(8,128)S(1)} %get-tuple-element.36.refs_0_), channel_id=1, source_target_pairs={{0,2},{1,3},{2,0},{3,1},{4,6},{5,7},{6,4},{7,5},{8,10},{9,11},{10,... | collective-permute-start | bytes 24584 | tf_op jit(solution)/shard_map/ppermute | solution.py:613
  19.9 2.9 %collective-permute-start.6 = (f32[2,8,128]{2,1,0:T(8,128)S(1)}, f32[2,8,128]{2,1,0:T(8,128)S(1)}, u32[]{:S(2)}, u32[]{:S(2)}) collective-permute-start(f32[2,8,128]{2,1,0:T(8,128)S(1)} %get-tuple-element.36.refs_0_), channel_id=1, source_target_pairs={{0,1},{1,0},{2,3},{3,2},{4,5},{5,4},{6,7},{7,6},{8,9},{9,8},{10,11... | collective-permute-start | bytes 24584 | tf_op jit(solution)/shard_map/ppermute | solution.py:613
  22.8 4.6 %collective-permute-start.11 = (f32[2,8,128]{2,1,0:T(8,128)S(1)}, f32[2,8,128]{2,1,0:T(8,128)S(1)}, u32[]{:S(2)}, u32[]{:S(2)}) collective-permute-start(f32[2,8,128]{2,1,0:T(8,128)S(1)} %shard_map.91._.rest_0_), channel_id=1, source_target_pairs={{0,8},{4,12},{8,0},{12,4},{1,9},{5,13},{9,1},{13,5},{2,10},{6,14},... | collective-permute-start | bytes 24584 | tf_op jit(solution)/shard_map/ppermute | solution.py:613
  24.1 5.5 %collective-permute-start.10 = (f32[2,8,128]{2,1,0:T(8,128)S(1)}, f32[2,8,128]{2,1,0:T(8,128)S(1)}, u32[]{:S(2)}, u32[]{:S(2)}) collective-permute-start(f32[2,8,128]{2,1,0:T(8,128)S(1)} %shard_map.91._.rest_0_), channel_id=1, source_target_pairs={{0,12},{4,8},{8,4},{12,0},{1,13},{5,9},{9,5},{13,1},{2,14},{6,10},... | collective-permute-start | bytes 24584 | tf_op jit(solution)/shard_map/ppermute | solution.py:613
  26.2 3.7 %collective-permute-start.9 = (f32[2,8,128]{2,1,0:T(8,128)S(1)}, f32[2,8,128]{2,1,0:T(8,128)S(1)}, u32[]{:S(2)}, u32[]{:S(2)}) collective-permute-start(f32[2,8,128]{2,1,0:T(8,128)S(1)} %shard_map.91._.rest_0_), channel_id=1, source_target_pairs={{0,4},{4,0},{8,12},{12,8},{1,5},{5,1},{9,13},{13,9},{2,6},{6,2},{1... | collective-permute-start | bytes 24584 | tf_op jit(solution)/shard_map/ppermute | solution.py:613

commit v25 on v22

--- a/solution.py
+++ b/solution.py
@@ -298,20 +298,20 @@
     col_prev = staticmethod(col_prev)
 
 
-def horizontal(g0, g1, e_row, e_row_1, e_col, e_col_1, e_half, moves):
-    row_next, row_prev, col_next, col_prev = moves.row_next, moves.row_prev, moves.col_next, moves.col_prev
-    g0n, g1n = row_next(g0), col_next(g1)
-    f = e_half * (g1n - col_prev(g1))
-    h = e_half * (g0n - row_prev(g0))
-    flux = e_row * (g0 - g0n)
-    out0 = flux - row_next(f) - row_prev(flux - f)
-    flux = e_col * (g0 - col_next(g0))
-    out0 = out0 + (flux - col_prev(flux))
-    flux = e_col_1 * (g1 - g1n)
-    out1 = flux - col_next(h) - col_prev(flux - h)
-    flux = e_row_1 * (g1 - row_next(g1))
-    out1 = out1 + (flux - row_prev(flux))
-    return out0, out1
+def along(g0, g1, e_row, e_col, e_half, moves):
+    f = e_half * (moves.col_next(g1) - moves.col_prev(g1))
+    flux = e_row * (g0 - moves.row_next(g0))
+    out = flux - moves.row_next(f) - moves.row_prev(flux - f)
+    flux = e_col * (g0 - moves.col_next(g0))
+    return out + (flux - moves.col_prev(flux))
+
+
+def across(g0, g1, e_row, e_col, e_half, moves):
+    h = e_half * (moves.row_next(g0) - moves.row_prev(g0))
+    flux = e_col * (g1 - moves.col_next(g1))
+    out = flux - moves.col_next(h) - moves.col_prev(flux - h)
+    flux = e_row * (g1 - moves.row_next(g1))
+    return out + (flux - moves.row_prev(flux))
 
 
 def main_kernel(
@@ -373,12 +373,12 @@
                 k = b * UNROLL + i
                 after = k + 1 if i + 1 < UNROLL else jnp.minimum(k + 1, layers - 1)
                 next0, next1 = load(src.at[0, after]), load(src.at[1, after])
-                e_up = load(eta_up.at[k])
-                up0, up1 = e_up * (g0 - next0), e_up * (g1 - next1)
-                pairs = [load(ref.at[c, k]) for ref in (eta_row, eta_col) for c in range(2)]
-                out0, out1 = horizontal(g0, g1, *pairs, load(eta_half.at[k]), moves)
-                out0, out1 = m * (out0 + (up0 - below0)), m * (out1 + (up1 - below1))
-                for c, g, out in ((0, g0, out0), (1, g1, out1)):
+                e_up, e_half = load(eta_up.at[k]), load(eta_half.at[k])
+                ups = []
+                for c, g, following, below, part in ((0, g0, next0, below0, along), (1, g1, next1, below1, across)):
+                    up = e_up * (g - following)
+                    out = part(g0, g1, load(eta_row.at[c, k]), load(eta_col.at[c, k]), e_half, moves)
+                    out = m * (out + (up - below))
                     if t < STEPS:
                         out.store(dst.at[c, k])
                     for half in range(2):
@@ -387,6 +387,8 @@
                             dst[c, k, :, half * LANES : (half + 1) * LANES] = now
                         odd[half] = odd[half] + g.tiles[half] * now
                         even[half] = even[half] + now * now
+                    ups.append(up)
+                up0, up1 = ups
                 g0, g1, below0, below1 = next0, next1, up0, up1
             return g0.tiles, g1.tiles, below0.tiles, below1.tiles, odd, even
 
@@ -445,8 +447,10 @@
         result = ([], [])
         odd = even = jnp.zeros((ROWS, LANES), jnp.float32)
         for n in range(tiles):
-            coefficients = (eta_row[n], eta_row_1[n], eta_col[n], eta_col_1[n], eta_half[n])
-            outs = horizontal(field[0][n], field[1][n], *coefficients, Turns)
+            outs = (
+                along(field[0][n], field[1][n], eta_row[n], eta_col[n], eta_half[n], Turns),
+                across(field[0][n], field[1][n], eta_row_1[n], eta_col_1[n], eta_half[n], Turns),
+            )
             for c in range(2):
                 below = ups[c][n - 1] if n else turned(ups[c][-1], SLOT) - drag * field[c][0]
                 out = cover * (outs[c] + (ups[c][n] - below))

time: 30.1 us -> 30.1 us (level)
  no operation moved by 1% of the time
where the time goes in v25:
time: 30.1 us; the launch traced here: 30 us
  starting transfers between devices  13.7 us (46%)
  Pallas kernels  8.04 us (27%)
  waiting for transfers between devices  7.51 us (25%)
  between operations  0.71 us (2%)
    ppermute x6, starting transfers between devices, swapped(): return lax.ppermute(x, (*axes, spare) if spare else axes, pairs)  8.1 us
    ppermute x6, starting transfers between devices, exchange(): parts.append(lax.ppermute(x, axis, pairs))  5.62 us
    ppermute x6, waiting for transfers between devices, exchange(): parts.append(lax.ppermute(x, axis, pairs))  5.56 us
    pallas_call x1, Pallas kernels, body(): call(main_kernel, [(2,) + block] * (STEPS - 1) + [adjoint_rhs.shape, (2 *...  3.91 us
    ppermute x6, waiting for transfers between devices, swapped(): return lax.ppermute(x, (*axes, spare) if spare else axes, pairs)  1.95 us
    pallas_call x1, Pallas kernels, body(): call(final_kernel, [adjoint_rhs.shape, adjoint_rhs.shape, friction.shape])  1.34 us
    pallas_call x1, Pallas kernels, body(): call(strip_kernel, [jax.ShapeDtypeStruct(x.shape, x.dtype) for x in input...  1.13 us
    pallas_call x1, Pallas kernels, body(): call(ribbon_kernel, [(STEPS, 2, layers // 4) + tile, (2,) + tile])  0.79 us
  transfers between devices with their start and end apart: 12, of which 7 were waited for; matrix products, arithmetic and copies ran while one was open for 0% of the time, Pallas kernels for 16%

profile of v25, /device:TPU:0, one launch (start us, length us, event | category | flops | bytes accessed | tf_op | source)
XLA Modules:
  0.0 30.0 jit_solution(14980222378225661126)
XLA Ops:
  0.6 1.1 %shard_map.85 = (f32[2,20,8,256]{3,2,1,0:T(8,128)S(1)}, f32[20,8,256]{2,1,0:T(8,128)S(1)}, f32[8,256]{1,0:T(8,128)S(1)}, s32[8,256]{1,0:T(8,128)S(1)}, s32[8,256...) custom-call(f32[2,20,8,256]{3,2,1,0:T(8,128)} %refs_0_.1, ...), custom_call_target="tpu_custom_call" | custom-call | tf_op jit(solution)/shard_map/pallas_call | solution.py:632
  1.8 0.5 %collective-permute-start.2 = (f32[62,8,128]{2,1,0:T(8,128)S(1)}, f32[62,8,128]{2,1,0:T(8,128)S(1)}, u32[]{:S(2)}, u32[]{:S(2)}) collective-permute-start(f32[62,8,128]{2,1,0:T(8,128)S(1)} %get-tuple-element.32), channel_id=1, source_target_pairs={{0,1},{4,8},{8,4},{12,13},{1,0},{5,9},{9,5},{13,12},{2,3},{6,10},{... | collective-permute-start | bytes 761864 | tf_op jit(solution)/shard_map/ppermute | solution.py:47
  2.3 4.1 %collective-permute-start.3 = (f32[62,8,128]{2,1,0:T(8,128)S(1)}, f32[62,8,128]{2,1,0:T(8,128)S(1)}, u32[]{:S(2)}, u32[]{:S(2)}) collective-permute-start(f32[62,8,128]{2,1,0:T(8,128)S(1)} %get-tuple-element.33), channel_id=1, source_target_pairs={{0,4},{4,0},{8,12},{12,8},{1,5},{5,1},{9,13},{13,9},{2,6},{6,2},{1... | collective-permute-start | bytes 761864 | tf_op jit(solution)/shard_map/ppermute | solution.py:47
  6.7 1.6 %collective-permute-start.1 = (f32[3,8,128]{2,1,0:T(8,128)S(1)}, f32[3,8,128]{2,1,0:T(8,128)S(1)}, u32[]{:S(2)}, u32[]{:S(2)}) collective-permute-start(f32[3,8,128]{2,1,0:T(8,128)S(1)} %get-tuple-element.29), channel_id=1, source_target_pairs={{0,3},{1,2},{2,1},{3,0},{4,7},{5,6},{6,5},{7,4},{8,11},{9,10},{10,... | collective-permute-start | bytes 36872 | tf_op jit(solution)/shard_map/ppermute | solution.py:47
  8.3 1.6 %collective-permute-done.1.from_b = f32[3,8,128]{2,1,0:T(8,128)S(1)} collective-permute-done((f32[3,8,128]{2,1,0:T(8,128)S(1)}, f32[3,8,128]{2,1,0:T(8,128)S(1)}, u32[]{:S(2)}, u32[]{:S(2)}) %collective-permute-start.1) | collective-permute-done | bytes 12320 | tf_op jit(solution)/shard_map/ppermute | solution.py:47
  9.9 0.7 %collective-permute-start.5 = (f32[6,8,128]{2,1,0:T(8,128)S(1)}, f32[6,8,128]{2,1,0:T(8,128)S(1)}, u32[]{:S(2)}, u32[]{:S(2)}) collective-permute-start(f32[6,8,128]{2,1,0:T(8,128)S(1)} %shard_map.87._.columns), channel_id=1, source_target_pairs={{0,1},{4,8},{8,4},{12,13},{1,0},{5,9},{9,5},{13,12},{2,3},{6,10},{... | collective-permute-start | bytes 73736 | tf_op jit(solution)/shard_map/ppermute | solution.py:47
  10.6 1.0 %collective-permute-start.4 = (f32[6,8,128]{2,1,0:T(8,128)S(1)}, f32[6,8,128]{2,1,0:T(8,128)S(1)}, u32[]{:S(2)}, u32[]{:S(2)}) collective-permute-start(f32[6,8,128]{2,1,0:T(8,128)S(1)} %shard_map.87._.columns), channel_id=1, source_target_pairs={{0,4},{4,0},{8,12},{12,8},{1,5},{5,1},{9,13},{13,9},{2,6},{6,2},{1... | collective-permute-start | bytes 73736 | tf_op jit(solution)/shard_map/ppermute | solution.py:47
  11.7 0.2 shard_map.88
  11.9 0.4 %collective-permute-done.3.strip_a = f32[62,8,128]{2,1,0:T(8,128)S(1)} collective-permute-done((f32[62,8,128]{2,1,0:T(8,128)S(1)}, f32[62,8,128]{2,1,0:T(8,128)S(1)}, u32[]{:S(2)}, u32[]{:S(2)}) %collective-permute-start.3) | collective-permute-done | bytes 253984 | tf_op jit(solution)/shard_map/ppermute | solution.py:47
  12.3 3.9 %shard_map.89 = (f32[2,20,16,256]{3,2,1,0:T(8,128)S(1)}, f32[2,20,16,256]{3,2,1,0:T(8,128)S(1)}, f32[2,20,16,256]{3,2,1,0:T(8,128)S(1)}, f32[2,20,8,256]{3,2,1,0...) custom-call(f32[2,20,8,256]{3,2,1,0:T(8,128)S(1)} %get-tuple-element.23.rhs, ...), custom_call_target="tpu_custom_call" | custom-call | flops 200000000 | bytes 8000000 | tf_op jit(solution)/shard_map/pallas_call | solution.py:649
  16.2 0.8 %shard_map.90 = (f32[4,2,5,8,128]{4,3,2,1,0:T(8,128)S(1)}, f32[2,8,128]{2,1,0:T(8,128)S(1)}) custom-call(f32[17,8,128]{2,1,0:T(8,128)S(1)} %get-tuple-element.30.own, f32[17,8,128]{2,1,0:T(8,128)S(1)} %get-tuple-element.34.halo, f32[6,8,128]{2,1,0:T(8,128)S(1)} %shard_map.87._.columns, f32[6,8,128]{2,1,0:T(8,128)S(1)} %collective-permute-done.4.columns_a, ...), custom_call_target="tpu_custom_call" | custom-call | tf_op jit(solution)/shard_map/pallas_call | solution.py:655
  17.0 0.9 %collective-permute-start.8 = (f32[2,8,128]{2,1,0:T(8,128)S(1)}, f32[2,8,128]{2,1,0:T(8,128)S(1)}, u32[]{:S(2)}, u32[]{:S(2)}) collective-permute-start(f32[2,8,128]{2,1,0:T(8,128)S(1)} %get-tuple-element.36.refs_0_), channel_id=1, source_target_pairs={{0,3},{1,2},{2,1},{3,0},{4,7},{5,6},{6,5},{7,4},{8,11},{9,10},{10,... | collective-permute-start | bytes 24584 | tf_op jit(solution)/shard_map/ppermute | solution.py:617
  17.9 0.7 %collective-permute-start.7 = (f32[2,8,128]{2,1,0:T(8,128)S(1)}, f32[2,8,128]{2,1,0:T(8,128)S(1)}, u32[]{:S(2)}, u32[]{:S(2)}) collective-permute-start(f32[2,8,128]{2,1,0:T(8,128)S(1)} %get-tuple-element.36.refs_0_), channel_id=1, source_target_pairs={{0,2},{1,3},{2,0},{3,1},{4,6},{5,7},{6,4},{7,5},{8,10},{9,11},{10,... | collective-permute-start | bytes 24584 | tf_op jit(solution)/shard_map/ppermute | solution.py:617
  18.6 0.3 collective-permute-start.6
  18.9 1.3 %collective-permute-done.8.refs_3_ = f32[2,8,128]{2,1,0:T(8,128)S(1)} collective-permute-done((f32[2,8,128]{2,1,0:T(8,128)S(1)}, f32[2,8,128]{2,1,0:T(8,128)S(1)}, u32[]{:S(2)}, u32[]{:S(2)}) %collective-permute-start.8) | collective-permute-done | bytes 8224 | tf_op jit(solution)/shard_map/ppermute | solution.py:617
  20.2 1.4 %collective-permute-done.7.refs_2_ = f32[2,8,128]{2,1,0:T(8,128)S(1)} collective-permute-done((f32[2,8,128]{2,1,0:T(8,128)S(1)}, f32[2,8,128]{2,1,0:T(8,128)S(1)}, u32[]{:S(2)}, u32[]{:S(2)}) %collective-permute-start.7) | collective-permute-done | bytes 8224 | tf_op jit(solution)/shard_map/ppermute | solution.py:617
  21.5 1.3 %collective-permute-start.11 = (f32[2,8,128]{2,1,0:T(8,128)S(1)}, f32[2,8,128]{2,1,0:T(8,128)S(1)}, u32[]{:S(2)}, u32[]{:S(2)}) collective-permute-start(f32[2,8,128]{2,1,0:T(8,128)S(1)} %shard_map.91._.rest_0_), channel_id=1, source_target_pairs={{0,8},{4,12},{8,0},{12,4},{1,9},{5,13},{9,1},{13,5},{2,10},{6,14},... | collective-permute-start | bytes 24584 | tf_op jit(solution)/shard_map/ppermute | solution.py:617
  22.9 2.1 %collective-permute-start.10 = (f32[2,8,128]{2,1,0:T(8,128)S(1)}, f32[2,8,128]{2,1,0:T(8,128)S(1)}, u32[]{:S(2)}, u32[]{:S(2)}) collective-permute-start(f32[2,8,128]{2,1,0:T(8,128)S(1)} %shard_map.91._.rest_0_), channel_id=1, source_target_pairs={{0,12},{4,8},{8,4},{12,0},{1,13},{5,9},{9,5},{13,1},{2,14},{6,10},... | collective-permute-start | bytes 24584 | tf_op jit(solution)/shard_map/ppermute | solution.py:617
  25.0 0.3 collective-permute-start.9
  25.3 0.4 %shard_map.92.vectors = f32[4,2,20,8,256]{4,3,2,1,0:T(8,128)S(1)} custom-call(f32[2,8,128]{2,1,0:T(8,128)S(1)} %shard_map.91._.rest_0_, f32[2,20,8,256]{3,2,1,0:T(8,128)S(1)} %get-tuple-element.23.rhs, s32[8,256]{1,0:T(8,128)S(1)} %get-tuple-element.26.ice, f32[2,20,16,256]{3,2,1,0:T(8,128)S(1)} %get-tuple-element.37.power_1, ...), custom_call_target="tpu_custom_call" | custom-call | tf_op jit(solution)/shard_map/pallas_call | solution.py:664
  25.7 0.5 %collective-permute-done.11.rest_3_ = f32[2,8,128]{2,1,0:T(8,128)S(1)} collective-permute-done((f32[2,8,128]{2,1,0:T(8,128)S(1)}, f32[2,8,128]{2,1,0:T(8,128)S(1)}, u32[]{:S(2)}, u32[]{:S(2)}) %collective-permute-start.11) | collective-permute-done | bytes 8224 | tf_op jit(solution)/shard_map/ppermute | solution.py:617
  26.2 2.2 %collective-permute-done.10.rest_2_ = f32[2,8,128]{2,1,0:T(8,128)S(1)} collective-permute-done((f32[2,8,128]{2,1,0:T(8,128)S(1)}, f32[2,8,128]{2,1,0:T(8,128)S(1)}, u32[]{:S(2)}, u32[]{:S(2)}) %collective-permute-start.10) | collective-permute-done | bytes 8224 | tf_op jit(solution)/shard_map/ppermute | solution.py:617
  28.3 0.3 %collective-permute-done.9.rest_1_ = f32[2,8,128]{2,1,0:T(8,128)S(1)} collective-permute-done((f32[2,8,128]{2,1,0:T(8,128)S(1)}, f32[2,8,128]{2,1,0:T(8,128)S(1)}, u32[]{:S(2)}, u32[]{:S(2)}) %collective-permute-start.9) | collective-permute-done | bytes 8224 | tf_op jit(solution)/shard_map/ppermute | solution.py:617
  28.6 1.3 %shard_map.93 = (f32[2,20,8,256]{3,2,1,0:T(8,128)}, f32[2,20,8,256]{3,2,1,0:T(8,128)}, f32[8,256]{1,0:T(8,128)}) custom-call(f32[2,20,8,256]{3,2,1,0:T(8,128)S(1)} %get-tuple-element.23.rhs, f32[4,2,20,8,256]{4,3,2,1,0:T(8,128)S(1)} %shard_map.92.vectors, f32[8,256]{1,0:T(8,128)S(1)} %get-tuple-element.25.friction, s32[8,256]{1,0:T(8,128)S(1)} %get-tuple-element.26.ice, ...), custom_call_target="tpu_custom_call" | custom-call | tf_op jit(solution)/shard_map/pallas_call | solution.py:670
  (9 shorter events, 0.3 us)
Async XLA Ops:
  1.8 10.1 %collective-permute-start.2 = (f32[62,8,128]{2,1,0:T(8,128)S(1)}, f32[62,8,128]{2,1,0:T(8,128)S(1)}, u32[]{:S(2)}, u32[]{:S(2)}) collective-permute-start(f32[62,8,128]{2,1,0:T(8,128)S(1)} %get-tuple-element.32), channel_id=1, source_target_pairs={{0,1},{4,8},{8,4},{12,13},{1,0},{5,9},{9,5},{13,12},{2,3},{6,10},{... | collective-permute-start | bytes 761864 | tf_op jit(solution)/shard_map/ppermute | solution.py:47
  2.3 10.0 %collective-permute-start.3 = (f32[62,8,128]{2,1,0:T(8,128)S(1)}, f32[62,8,128]{2,1,0:T(8,128)S(1)}, u32[]{:S(2)}, u32[]{:S(2)}) collective-permute-start(f32[62,8,128]{2,1,0:T(8,128)S(1)} %get-tuple-element.33), channel_id=1, source_target_pairs={{0,4},{4,0},{8,12},{12,8},{1,5},{5,1},{9,13},{13,9},{2,6},{6,2},{1... | collective-permute-start | bytes 761864 | tf_op jit(solution)/shard_map/ppermute | solution.py:47
  6.6 1.7 %collective-permute-start = (f32[3,8,128]{2,1,0:T(8,128)S(1)}, f32[3,8,128]{2,1,0:T(8,128)S(1)}, u32[]{:S(2)}, u32[]{:S(2)}) collective-permute-start(f32[3,8,128]{2,1,0:T(8,128)S(1)} %get-tuple-element.28), channel_id=1, source_target_pairs={{0,1},{1,0},{2,3},{3,2},{4,5},{5,4},{6,7},{7,6},{8,9},{9,8},{10,11... | collective-permute-start | bytes 36872 | tf_op jit(solution)/shard_map/ppermute | solution.py:47
  6.7 3.2 %collective-permute-start.1 = (f32[3,8,128]{2,1,0:T(8,128)S(1)}, f32[3,8,128]{2,1,0:T(8,128)S(1)}, u32[]{:S(2)}, u32[]{:S(2)}) collective-permute-start(f32[3,8,128]{2,1,0:T(8,128)S(1)} %get-tuple-element.29), channel_id=1, source_target_pairs={{0,3},{1,2},{2,1},{3,0},{4,7},{5,6},{6,5},{7,4},{8,11},{9,10},{10,... | collective-permute-start | bytes 36872 | tf_op jit(solution)/shard_map/ppermute | solution.py:47
  9.9 6.3 %collective-permute-start.5 = (f32[6,8,128]{2,1,0:T(8,128)S(1)}, f32[6,8,128]{2,1,0:T(8,128)S(1)}, u32[]{:S(2)}, u32[]{:S(2)}) collective-permute-start(f32[6,8,128]{2,1,0:T(8,128)S(1)} %shard_map.87._.columns), channel_id=1, source_target_pairs={{0,1},{4,8},{8,4},{12,13},{1,0},{5,9},{9,5},{13,12},{2,3},{6,10},{... | collective-permute-start | bytes 73736 | tf_op jit(solution)/shard_map/ppermute | solution.py:47
  10.6 5.6 %collective-permute-start.4 = (f32[6,8,128]{2,1,0:T(8,128)S(1)}, f32[6,8,128]{2,1,0:T(8,128)S(1)}, u32[]{:S(2)}, u32[]{:S(2)}) collective-permute-start(f32[6,8,128]{2,1,0:T(8,128)S(1)} %shard_map.87._.columns), channel_id=1, source_target_pairs={{0,4},{4,0},{8,12},{12,8},{1,5},{5,1},{9,13},{13,9},{2,6},{6,2},{1... | collective-permute-start | bytes 73736 | tf_op jit(solution)/shard_map/ppermute | solution.py:47
  17.0 3.1 %collective-permute-start.8 = (f32[2,8,128]{2,1,0:T(8,128)S(1)}, f32[2,8,128]{2,1,0:T(8,128)S(1)}, u32[]{:S(2)}, u32[]{:S(2)}) collective-permute-start(f32[2,8,128]{2,1,0:T(8,128)S(1)} %get-tuple-element.36.refs_0_), channel_id=1, source_target_pairs={{0,3},{1,2},{2,1},{3,0},{4,7},{5,6},{6,5},{7,4},{8,11},{9,10},{10,... | collective-permute-start | bytes 24584 | tf_op jit(solution)/shard_map/ppermute | solution.py:617
  17.9 3.7 %collective-permute-start.7 = (f32[2,8,128]{2,1,0:T(8,128)S(1)}, f32[2,8,128]{2,1,0:T(8,128)S(1)}, u32[]{:S(2)}, u32[]{:S(2)}) collective-permute-start(f32[2,8,128]{2,1,0:T(8,128)S(1)} %get-tuple-element.36.refs_0_), channel_id=1, source_target_pairs={{0,2},{1,3},{2,0},{3,1},{4,6},{5,7},{6,4},{7,5},{8,10},{9,11},{10,... | collective-permute-start | bytes 24584 | tf_op jit(solution)/shard_map/ppermute | solution.py:617
  18.6 2.9 %collective-permute-start.6 = (f32[2,8,128]{2,1,0:T(8,128)S(1)}, f32[2,8,128]{2,1,0:T(8,128)S(1)}, u32[]{:S(2)}, u32[]{:S(2)}) collective-permute-start(f32[2,8,128]{2,1,0:T(8,128)S(1)} %get-tuple-element.36.refs_0_), channel_id=1, source_target_pairs={{0,1},{1,0},{2,3},{3,2},{4,5},{5,4},{6,7},{7,6},{8,9},{9,8},{10,11... | collective-permute-start | bytes 24584 | tf_op jit(solution)/shard_map/ppermute | solution.py:617
  21.5 4.6 %collective-permute-start.11 = (f32[2,8,128]{2,1,0:T(8,128)S(1)}, f32[2,8,128]{2,1,0:T(8,128)S(1)}, u32[]{:S(2)}, u32[]{:S(2)}) collective-permute-start(f32[2,8,128]{2,1,0:T(8,128)S(1)} %shard_map.91._.rest_0_), channel_id=1, source_target_pairs={{0,8},{4,12},{8,0},{12,4},{1,9},{5,13},{9,1},{13,5},{2,10},{6,14},... | collective-permute-start | bytes 24584 | tf_op jit(solution)/shard_map/ppermute | solution.py:617
  22.9 5.5 %collective-permute-start.10 = (f32[2,8,128]{2,1,0:T(8,128)S(1)}, f32[2,8,128]{2,1,0:T(8,128)S(1)}, u32[]{:S(2)}, u32[]{:S(2)}) collective-permute-start(f32[2,8,128]{2,1,0:T(8,128)S(1)} %shard_map.91._.rest_0_), channel_id=1, source_target_pairs={{0,12},{4,8},{8,4},{12,0},{1,13},{5,9},{9,5},{13,1},{2,14},{6,10},... | collective-permute-start | bytes 24584 | tf_op jit(solution)/shard_map/ppermute | solution.py:617
  25.0 3.7 %collective-permute-start.9 = (f32[2,8,128]{2,1,0:T(8,128)S(1)}, f32[2,8,128]{2,1,0:T(8,128)S(1)}, u32[]{:S(2)}, u32[]{:S(2)}) collective-permute-start(f32[2,8,128]{2,1,0:T(8,128)S(1)} %shard_map.91._.rest_0_), channel_id=1, source_target_pairs={{0,4},{4,0},{8,12},{12,8},{1,5},{5,1},{9,13},{13,9},{2,6},{6,2},{1... | collective-permute-start | bytes 24584 | tf_op jit(solution)/shard_map/ppermute | solution.py:617

commit v26 on v22

--- a/solution.py
+++ b/solution.py
@@ -97,9 +97,14 @@
 
 def strip_kernel(*refs):
     sources, held, (strip_a, strip_b, arrived) = refs[:6], refs[6:12], refs[12:]
-    copies = [pltpu.make_async_copy(a, b, arrived.at[i]) for i, (a, b) in enumerate(zip(sources, held))]
-    for copy in copies:
-        copy.start()
+    half = held[1].shape[0] // 2
+    pieces = [[(c, pl.ds(h, half)) for c in range(2) for h in (0, half)], [(pl.ds(h, half),) for h in (0, half)]]
+    copies = []
+    for i, (a, b) in enumerate(zip(sources, held)):
+        for at in pieces[i] if i < 2 else [()]:
+            src, dst = (a.at[at], b.at[at]) if at else (a, b)
+            copies.append(pltpu.make_async_copy(src, dst, arrived.at[len(copies)]))
+            copies[-1].start()
     for copy in copies:
         copy.wait()
     rhs, eta, friction, ice, grounded, _ = held
@@ -628,7 +633,7 @@
     *held, strip_a, strip_b = call(
         strip_kernel,
         [jax.ShapeDtypeStruct(x.shape, x.dtype) for x in inputs] + [strips, strips],
-        [pltpu.SemaphoreType.DMA((len(inputs),))],
+        [pltpu.SemaphoreType.DMA((len(inputs) + 4,))],
         in_specs=[pl.BlockSpec(memory_space=pltpu.HBM)] * len(inputs),
     )(*[pltpu.with_memory_space_constraint(x, pltpu.HBM) for x in inputs])
     strip_b, strip_a = swapped(strip_b, ("gx",), 1, "gz"), swapped(strip_a, ("gx",), 0)

time: 30.1 us -> 30.2 us (level)
  no operation moved by 1% of the time
where the time goes in v26:
time: 30.2 us; the launch traced here: 30.1 us
  starting transfers between devices  13.7 us (45%)
  Pallas kernels  8.14 us (27%)
  waiting for transfers between devices  7.51 us (25%)
  between operations  0.71 us (2%)
    ppermute x6, starting transfers between devices, swapped(): return lax.ppermute(x, (*axes, spare) if spare else axes, pairs)  8.1 us
    ppermute x6, starting transfers between devices, exchange(): parts.append(lax.ppermute(x, axis, pairs))  5.62 us
    ppermute x6, waiting for transfers between devices, exchange(): parts.append(lax.ppermute(x, axis, pairs))  5.56 us
    pallas_call x1, Pallas kernels, body(): call(main_kernel, [(2,) + block] * (STEPS - 1) + [adjoint_rhs.shape, (2 *...  3.91 us
    ppermute x6, waiting for transfers between devices, swapped(): return lax.ppermute(x, (*axes, spare) if spare else axes, pairs)  1.95 us
    pallas_call x1, Pallas kernels, body(): call(final_kernel, [adjoint_rhs.shape, adjoint_rhs.shape, friction.shape])  1.34 us
    pallas_call x1, Pallas kernels, body(): call(strip_kernel, [jax.ShapeDtypeStruct(x.shape, x.dtype) for x in input...  1.23 us
    pallas_call x1, Pallas kernels, body(): call(ribbon_kernel, [(STEPS, 2, layers // 4) + tile, (2,) + tile])  0.79 us
  transfers between devices with their start and end apart: 12, of which 7 were waited for; matrix products, arithmetic and copies ran while one was open for 0% of the time, Pallas kernels for 16%

profile of v26, /device:TPU:0, one launch (start us, length us, event | category | flops | bytes accessed | tf_op | source)
XLA Modules:
  0.0 30.1 jit_solution(17103245501723322694)
XLA Ops:
  0.6 1.2 %shard_map.85 = (f32[2,20,8,256]{3,2,1,0:T(8,128)S(1)}, f32[20,8,256]{2,1,0:T(8,128)S(1)}, f32[8,256]{1,0:T(8,128)S(1)}, s32[8,256]{1,0:T(8,128)S(1)}, s32[8,256...) custom-call(f32[2,20,8,256]{3,2,1,0:T(8,128)} %refs_0_.1, ...), custom_call_target="tpu_custom_call" | custom-call | tf_op jit(solution)/shard_map/pallas_call | solution.py:633
  1.9 0.5 %collective-permute-start.2 = (f32[62,8,128]{2,1,0:T(8,128)S(1)}, f32[62,8,128]{2,1,0:T(8,128)S(1)}, u32[]{:S(2)}, u32[]{:S(2)}) collective-permute-start(f32[62,8,128]{2,1,0:T(8,128)S(1)} %get-tuple-element.32), channel_id=1, source_target_pairs={{0,1},{4,8},{8,4},{12,13},{1,0},{5,9},{9,5},{13,12},{2,3},{6,10},{... | collective-permute-start | bytes 761864 | tf_op jit(solution)/shard_map/ppermute | solution.py:47
  2.4 4.1 %collective-permute-start.3 = (f32[62,8,128]{2,1,0:T(8,128)S(1)}, f32[62,8,128]{2,1,0:T(8,128)S(1)}, u32[]{:S(2)}, u32[]{:S(2)}) collective-permute-start(f32[62,8,128]{2,1,0:T(8,128)S(1)} %get-tuple-element.33), channel_id=1, source_target_pairs={{0,4},{4,0},{8,12},{12,8},{1,5},{5,1},{9,13},{13,9},{2,6},{6,2},{1... | collective-permute-start | bytes 761864 | tf_op jit(solution)/shard_map/ppermute | solution.py:47
  6.8 1.6 %collective-permute-start.1 = (f32[3,8,128]{2,1,0:T(8,128)S(1)}, f32[3,8,128]{2,1,0:T(8,128)S(1)}, u32[]{:S(2)}, u32[]{:S(2)}) collective-permute-start(f32[3,8,128]{2,1,0:T(8,128)S(1)} %get-tuple-element.29), channel_id=1, source_target_pairs={{0,3},{1,2},{2,1},{3,0},{4,7},{5,6},{6,5},{7,4},{8,11},{9,10},{10,... | collective-permute-start | bytes 36872 | tf_op jit(solution)/shard_map/ppermute | solution.py:47
  8.4 1.6 %collective-permute-done.1.from_b = f32[3,8,128]{2,1,0:T(8,128)S(1)} collective-permute-done((f32[3,8,128]{2,1,0:T(8,128)S(1)}, f32[3,8,128]{2,1,0:T(8,128)S(1)}, u32[]{:S(2)}, u32[]{:S(2)}) %collective-permute-start.1) | collective-permute-done | bytes 12320 | tf_op jit(solution)/shard_map/ppermute | solution.py:47
  10.0 0.7 %collective-permute-start.5 = (f32[6,8,128]{2,1,0:T(8,128)S(1)}, f32[6,8,128]{2,1,0:T(8,128)S(1)}, u32[]{:S(2)}, u32[]{:S(2)}) collective-permute-start(f32[6,8,128]{2,1,0:T(8,128)S(1)} %shard_map.87._.columns), channel_id=1, source_target_pairs={{0,1},{4,8},{8,4},{12,13},{1,0},{5,9},{9,5},{13,12},{2,3},{6,10},{... | collective-permute-start | bytes 73736 | tf_op jit(solution)/shard_map/ppermute | solution.py:47
  10.8 1.0 %collective-permute-start.4 = (f32[6,8,128]{2,1,0:T(8,128)S(1)}, f32[6,8,128]{2,1,0:T(8,128)S(1)}, u32[]{:S(2)}, u32[]{:S(2)}) collective-permute-start(f32[6,8,128]{2,1,0:T(8,128)S(1)} %shard_map.87._.columns), channel_id=1, source_target_pairs={{0,4},{4,0},{8,12},{12,8},{1,5},{5,1},{9,13},{13,9},{2,6},{6,2},{1... | collective-permute-start | bytes 73736 | tf_op jit(solution)/shard_map/ppermute | solution.py:47
  11.8 0.2 shard_map.88
  12.0 0.4 %collective-permute-done.3.strip_a = f32[62,8,128]{2,1,0:T(8,128)S(1)} collective-permute-done((f32[62,8,128]{2,1,0:T(8,128)S(1)}, f32[62,8,128]{2,1,0:T(8,128)S(1)}, u32[]{:S(2)}, u32[]{:S(2)}) %collective-permute-start.3) | collective-permute-done | bytes 253984 | tf_op jit(solution)/shard_map/ppermute | solution.py:47
  12.4 3.9 %shard_map.89 = (f32[2,20,16,256]{3,2,1,0:T(8,128)S(1)}, f32[2,20,16,256]{3,2,1,0:T(8,128)S(1)}, f32[2,20,16,256]{3,2,1,0:T(8,128)S(1)}, f32[2,20,8,256]{3,2,1,0...) custom-call(f32[2,20,8,256]{3,2,1,0:T(8,128)S(1)} %get-tuple-element.23.rhs, ...), custom_call_target="tpu_custom_call" | custom-call | flops 200000000 | bytes 8000000 | tf_op jit(solution)/shard_map/pallas_call | solution.py:650
  16.3 0.8 %shard_map.90 = (f32[4,2,5,8,128]{4,3,2,1,0:T(8,128)S(1)}, f32[2,8,128]{2,1,0:T(8,128)S(1)}) custom-call(f32[17,8,128]{2,1,0:T(8,128)S(1)} %get-tuple-element.30.own, f32[17,8,128]{2,1,0:T(8,128)S(1)} %get-tuple-element.34.halo, f32[6,8,128]{2,1,0:T(8,128)S(1)} %shard_map.87._.columns, f32[6,8,128]{2,1,0:T(8,128)S(1)} %collective-permute-done.4.columns_a, ...), custom_call_target="tpu_custom_call" | custom-call | tf_op jit(solution)/shard_map/pallas_call | solution.py:656
  17.1 0.9 %collective-permute-start.8 = (f32[2,8,128]{2,1,0:T(8,128)S(1)}, f32[2,8,128]{2,1,0:T(8,128)S(1)}, u32[]{:S(2)}, u32[]{:S(2)}) collective-permute-start(f32[2,8,128]{2,1,0:T(8,128)S(1)} %get-tuple-element.36.refs_0_), channel_id=1, source_target_pairs={{0,3},{1,2},{2,1},{3,0},{4,7},{5,6},{6,5},{7,4},{8,11},{9,10},{10,... | collective-permute-start | bytes 24584 | tf_op jit(solution)/shard_map/ppermute | solution.py:618
  18.0 0.7 %collective-permute-start.7 = (f32[2,8,128]{2,1,0:T(8,128)S(1)}, f32[2,8,128]{2,1,0:T(8,128)S(1)}, u32[]{:S(2)}, u32[]{:S(2)}) collective-permute-start(f32[2,8,128]{2,1,0:T(8,128)S(1)} %get-tuple-element.36.refs_0_), channel_id=1, source_target_pairs={{0,2},{1,3},{2,0},{3,1},{4,6},{5,7},{6,4},{7,5},{8,10},{9,11},{10,... | collective-permute-start | bytes 24584 | tf_op jit(solution)/shard_map/ppermute | solution.py:618
  18.7 0.3 collective-permute-start.6
  19.0 1.3 %collective-permute-done.8.refs_3_ = f32[2,8,128]{2,1,0:T(8,128)S(1)} collective-permute-done((f32[2,8,128]{2,1,0:T(8,128)S(1)}, f32[2,8,128]{2,1,0:T(8,128)S(1)}, u32[]{:S(2)}, u32[]{:S(2)}) %collective-permute-start.8) | collective-permute-done | bytes 8224 | tf_op jit(solution)/shard_map/ppermute | solution.py:618
  20.3 1.4 %collective-permute-done.7.refs_2_ = f32[2,8,128]{2,1,0:T(8,128)S(1)} collective-permute-done((f32[2,8,128]{2,1,0:T(8,128)S(1)}, f32[2,8,128]{2,1,0:T(8,128)S(1)}, u32[]{:S(2)}, u32[]{:S(2)}) %collective-permute-start.7) | collective-permute-done | bytes 8224 | tf_op jit(solution)/shard_map/ppermute | solution.py:618
  21.6 1.3 %collective-permute-start.11 = (f32[2,8,128]{2,1,0:T(8,128)S(1)}, f32[2,8,128]{2,1,0:T(8,128)S(1)}, u32[]{:S(2)}, u32[]{:S(2)}) collective-permute-start(f32[2,8,128]{2,1,0:T(8,128)S(1)} %shard_map.91._.rest_0_), channel_id=1, source_target_pairs={{0,8},{4,12},{8,0},{12,4},{1,9},{5,13},{9,1},{13,5},{2,10},{6,14},... | collective-permute-start | bytes 24584 | tf_op jit(solution)/shard_map/ppermute | solution.py:618
  23.0 2.1 %collective-permute-start.10 = (f32[2,8,128]{2,1,0:T(8,128)S(1)}, f32[2,8,128]{2,1,0:T(8,128)S(1)}, u32[]{:S(2)}, u32[]{:S(2)}) collective-permute-start(f32[2,8,128]{2,1,0:T(8,128)S(1)} %shard_map.91._.rest_0_), channel_id=1, source_target_pairs={{0,12},{4,8},{8,4},{12,0},{1,13},{5,9},{9,5},{13,1},{2,14},{6,10},... | collective-permute-start | bytes 24584 | tf_op jit(solution)/shard_map/ppermute | solution.py:618
  25.1 0.3 collective-permute-start.9
  25.4 0.4 %shard_map.92.vectors = f32[4,2,20,8,256]{4,3,2,1,0:T(8,128)S(1)} custom-call(f32[2,8,128]{2,1,0:T(8,128)S(1)} %shard_map.91._.rest_0_, f32[2,20,8,256]{3,2,1,0:T(8,128)S(1)} %get-tuple-element.23.rhs, s32[8,256]{1,0:T(8,128)S(1)} %get-tuple-element.26.ice, f32[2,20,16,256]{3,2,1,0:T(8,128)S(1)} %get-tuple-element.37.power_1, ...), custom_call_target="tpu_custom_call" | custom-call | tf_op jit(solution)/shard_map/pallas_call | solution.py:665
  25.8 0.5 %collective-permute-done.11.rest_3_ = f32[2,8,128]{2,1,0:T(8,128)S(1)} collective-permute-done((f32[2,8,128]{2,1,0:T(8,128)S(1)}, f32[2,8,128]{2,1,0:T(8,128)S(1)}, u32[]{:S(2)}, u32[]{:S(2)}) %collective-permute-start.11) | collective-permute-done | bytes 8224 | tf_op jit(solution)/shard_map/ppermute | solution.py:618
  26.3 2.2 %collective-permute-done.10.rest_2_ = f32[2,8,128]{2,1,0:T(8,128)S(1)} collective-permute-done((f32[2,8,128]{2,1,0:T(8,128)S(1)}, f32[2,8,128]{2,1,0:T(8,128)S(1)}, u32[]{:S(2)}, u32[]{:S(2)}) %collective-permute-start.10) | collective-permute-done | bytes 8224 | tf_op jit(solution)/shard_map/ppermute | solution.py:618
  28.4 0.3 %collective-permute-done.9.rest_1_ = f32[2,8,128]{2,1,0:T(8,128)S(1)} collective-permute-done((f32[2,8,128]{2,1,0:T(8,128)S(1)}, f32[2,8,128]{2,1,0:T(8,128)S(1)}, u32[]{:S(2)}, u32[]{:S(2)}) %collective-permute-start.9) | collective-permute-done | bytes 8224 | tf_op jit(solution)/shard_map/ppermute | solution.py:618
  28.7 1.3 %shard_map.93 = (f32[2,20,8,256]{3,2,1,0:T(8,128)}, f32[2,20,8,256]{3,2,1,0:T(8,128)}, f32[8,256]{1,0:T(8,128)}) custom-call(f32[2,20,8,256]{3,2,1,0:T(8,128)S(1)} %get-tuple-element.23.rhs, f32[4,2,20,8,256]{4,3,2,1,0:T(8,128)S(1)} %shard_map.92.vectors, f32[8,256]{1,0:T(8,128)S(1)} %get-tuple-element.25.friction, s32[8,256]{1,0:T(8,128)S(1)} %get-tuple-element.26.ice, ...), custom_call_target="tpu_custom_call" | custom-call | tf_op jit(solution)/shard_map/pallas_call | solution.py:671
  (9 shorter events, 0.3 us)
Async XLA Ops:
  1.9 10.1 %collective-permute-start.2 = (f32[62,8,128]{2,1,0:T(8,128)S(1)}, f32[62,8,128]{2,1,0:T(8,128)S(1)}, u32[]{:S(2)}, u32[]{:S(2)}) collective-permute-start(f32[62,8,128]{2,1,0:T(8,128)S(1)} %get-tuple-element.32), channel_id=1, source_target_pairs={{0,1},{4,8},{8,4},{12,13},{1,0},{5,9},{9,5},{13,12},{2,3},{6,10},{... | collective-permute-start | bytes 761864 | tf_op jit(solution)/shard_map/ppermute | solution.py:47
  2.4 10.0 %collective-permute-start.3 = (f32[62,8,128]{2,1,0:T(8,128)S(1)}, f32[62,8,128]{2,1,0:T(8,128)S(1)}, u32[]{:S(2)}, u32[]{:S(2)}) collective-permute-start(f32[62,8,128]{2,1,0:T(8,128)S(1)} %get-tuple-element.33), channel_id=1, source_target_pairs={{0,4},{4,0},{8,12},{12,8},{1,5},{5,1},{9,13},{13,9},{2,6},{6,2},{1... | collective-permute-start | bytes 761864 | tf_op jit(solution)/shard_map/ppermute | solution.py:47
  6.7 1.7 %collective-permute-start = (f32[3,8,128]{2,1,0:T(8,128)S(1)}, f32[3,8,128]{2,1,0:T(8,128)S(1)}, u32[]{:S(2)}, u32[]{:S(2)}) collective-permute-start(f32[3,8,128]{2,1,0:T(8,128)S(1)} %get-tuple-element.28), channel_id=1, source_target_pairs={{0,1},{1,0},{2,3},{3,2},{4,5},{5,4},{6,7},{7,6},{8,9},{9,8},{10,11... | collective-permute-start | bytes 36872 | tf_op jit(solution)/shard_map/ppermute | solution.py:47
  6.8 3.2 %collective-permute-start.1 = (f32[3,8,128]{2,1,0:T(8,128)S(1)}, f32[3,8,128]{2,1,0:T(8,128)S(1)}, u32[]{:S(2)}, u32[]{:S(2)}) collective-permute-start(f32[3,8,128]{2,1,0:T(8,128)S(1)} %get-tuple-element.29), channel_id=1, source_target_pairs={{0,3},{1,2},{2,1},{3,0},{4,7},{5,6},{6,5},{7,4},{8,11},{9,10},{10,... | collective-permute-start | bytes 36872 | tf_op jit(solution)/shard_map/ppermute | solution.py:47
  10.0 6.3 %collective-permute-start.5 = (f32[6,8,128]{2,1,0:T(8,128)S(1)}, f32[6,8,128]{2,1,0:T(8,128)S(1)}, u32[]{:S(2)}, u32[]{:S(2)}) collective-permute-start(f32[6,8,128]{2,1,0:T(8,128)S(1)} %shard_map.87._.columns), channel_id=1, source_target_pairs={{0,1},{4,8},{8,4},{12,13},{1,0},{5,9},{9,5},{13,12},{2,3},{6,10},{... | collective-permute-start | bytes 73736 | tf_op jit(solution)/shard_map/ppermute | solution.py:47
  10.8 5.6 %collective-permute-start.4 = (f32[6,8,128]{2,1,0:T(8,128)S(1)}, f32[6,8,128]{2,1,0:T(8,128)S(1)}, u32[]{:S(2)}, u32[]{:S(2)}) collective-permute-start(f32[6,8,128]{2,1,0:T(8,128)S(1)} %shard_map.87._.columns), channel_id=1, source_target_pairs={{0,4},{4,0},{8,12},{12,8},{1,5},{5,1},{9,13},{13,9},{2,6},{6,2},{1... | collective-permute-start | bytes 73736 | tf_op jit(solution)/shard_map/ppermute | solution.py:47
  17.1 3.1 %collective-permute-start.8 = (f32[2,8,128]{2,1,0:T(8,128)S(1)}, f32[2,8,128]{2,1,0:T(8,128)S(1)}, u32[]{:S(2)}, u32[]{:S(2)}) collective-permute-start(f32[2,8,128]{2,1,0:T(8,128)S(1)} %get-tuple-element.36.refs_0_), channel_id=1, source_target_pairs={{0,3},{1,2},{2,1},{3,0},{4,7},{5,6},{6,5},{7,4},{8,11},{9,10},{10,... | collective-permute-start | bytes 24584 | tf_op jit(solution)/shard_map/ppermute | solution.py:618
  18.0 3.7 %collective-permute-start.7 = (f32[2,8,128]{2,1,0:T(8,128)S(1)}, f32[2,8,128]{2,1,0:T(8,128)S(1)}, u32[]{:S(2)}, u32[]{:S(2)}) collective-permute-start(f32[2,8,128]{2,1,0:T(8,128)S(1)} %get-tuple-element.36.refs_0_), channel_id=1, source_target_pairs={{0,2},{1,3},{2,0},{3,1},{4,6},{5,7},{6,4},{7,5},{8,10},{9,11},{10,... | collective-permute-start | bytes 24584 | tf_op jit(solution)/shard_map/ppermute | solution.py:618
  18.7 2.9 %collective-permute-start.6 = (f32[2,8,128]{2,1,0:T(8,128)S(1)}, f32[2,8,128]{2,1,0:T(8,128)S(1)}, u32[]{:S(2)}, u32[]{:S(2)}) collective-permute-start(f32[2,8,128]{2,1,0:T(8,128)S(1)} %get-tuple-element.36.refs_0_), channel_id=1, source_target_pairs={{0,1},{1,0},{2,3},{3,2},{4,5},{5,4},{6,7},{7,6},{8,9},{9,8},{10,11... | collective-permute-start | bytes 24584 | tf_op jit(solution)/shard_map/ppermute | solution.py:618
  21.6 4.6 %collective-permute-start.11 = (f32[2,8,128]{2,1,0:T(8,128)S(1)}, f32[2,8,128]{2,1,0:T(8,128)S(1)}, u32[]{:S(2)}, u32[]{:S(2)}) collective-permute-start(f32[2,8,128]{2,1,0:T(8,128)S(1)} %shard_map.91._.rest_0_), channel_id=1, source_target_pairs={{0,8},{4,12},{8,0},{12,4},{1,9},{5,13},{9,1},{13,5},{2,10},{6,14},... | collective-permute-start | bytes 24584 | tf_op jit(solution)/shard_map/ppermute | solution.py:618
  23.0 5.5 %collective-permute-start.10 = (f32[2,8,128]{2,1,0:T(8,128)S(1)}, f32[2,8,128]{2,1,0:T(8,128)S(1)}, u32[]{:S(2)}, u32[]{:S(2)}) collective-permute-start(f32[2,8,128]{2,1,0:T(8,128)S(1)} %shard_map.91._.rest_0_), channel_id=1, source_target_pairs={{0,12},{4,8},{8,4},{12,0},{1,13},{5,9},{9,5},{13,1},{2,14},{6,10},... | collective-permute-start | bytes 24584 | tf_op jit(solution)/shard_map/ppermute | solution.py:618
  25.1 3.7 %collective-permute-start.9 = (f32[2,8,128]{2,1,0:T(8,128)S(1)}, f32[2,8,128]{2,1,0:T(8,128)S(1)}, u32[]{:S(2)}, u32[]{:S(2)}) collective-permute-start(f32[2,8,128]{2,1,0:T(8,128)S(1)} %shard_map.91._.rest_0_), channel_id=1, source_target_pairs={{0,4},{4,0},{8,12},{12,8},{1,5},{5,1},{9,13},{13,9},{2,6},{6,2},{1... | collective-permute-start | bytes 24584 | tf_op jit(solution)/shard_map/ppermute | solution.py:618

commit v27 on v22

--- a/solution.py
+++ b/solution.py
@@ -364,6 +364,8 @@
         e = after
 
     def apply(t, src, dst):
+        used = 4 if t < STEPS else 2
+
         def block(b, carry):
             g0, g1, below0, below1, odd, even = carry
             g0, g1, below0, below1 = Tiles(g0), Tiles(g1), Tiles(below0), Tiles(below1)
@@ -373,7 +375,7 @@
                 k = b * UNROLL + i
                 after = k + 1 if i + 1 < UNROLL else jnp.minimum(k + 1, layers - 1)
                 next0, next1 = load(src.at[0, after]), load(src.at[1, after])
-                e_up = load(eta_up.at[k])
+                e_up = Tiles(load(eta_up.at[k]).tiles[:used])
                 up0, up1 = e_up * (g0 - next0), e_up * (g1 - next1)
                 pairs = [load(ref.at[c, k]) for ref in (eta_row, eta_col) for c in range(2)]
                 out0, out1 = horizontal(g0, g1, *pairs, load(eta_half.at[k]), moves)
@@ -393,7 +395,7 @@
         zero = [jnp.zeros((ROWS, LANES), jnp.float32)] * 2
         d = -1.0 * load(drag)
         g0, g1 = load(src.at[0, 0]), load(src.at[1, 0])
-        start = (g0.tiles, g1.tiles, (d * g0).tiles, (d * g1).tiles, zero, zero)
+        start = (g0.tiles, g1.tiles, (d * g0).tiles[:used], (d * g1).tiles[:used], zero, zero)
         ends = lax.fori_loop(0, layers // UNROLL, block, start)[4:]
         return [jnp.concatenate(v, 1) for v in ends]
 

time: 30.1 us -> 30.1 us (level)
  no operation moved by 1% of the time
where the time goes in v27:
time: 30.1 us; the launch traced here: 30 us
  starting transfers between devices  13.7 us (46%)
  Pallas kernels  8.04 us (27%)
  waiting for transfers between devices  7.51 us (25%)
  between operations  0.71 us (2%)
    ppermute x6, starting transfers between devices, swapped(): return lax.ppermute(x, (*axes, spare) if spare else axes, pairs)  8.1 us
    ppermute x6, starting transfers between devices, exchange(): parts.append(lax.ppermute(x, axis, pairs))  5.62 us
    ppermute x6, waiting for transfers between devices, exchange(): parts.append(lax.ppermute(x, axis, pairs))  5.56 us
    pallas_call x1, Pallas kernels, body(): call(main_kernel, [(2,) + block] * (STEPS - 1) + [adjoint_rhs.shape, (2 *...  3.91 us
    ppermute x6, waiting for transfers between devices, swapped(): return lax.ppermute(x, (*axes, spare) if spare else axes, pairs)  1.95 us
    pallas_call x1, Pallas kernels, body(): call(final_kernel, [adjoint_rhs.shape, adjoint_rhs.shape, friction.shape])  1.34 us
    pallas_call x1, Pallas kernels, body(): call(strip_kernel, [jax.ShapeDtypeStruct(x.shape, x.dtype) for x in input...  1.13 us
    pallas_call x1, Pallas kernels, body(): call(ribbon_kernel, [(STEPS, 2, layers // 4) + tile, (2,) + tile])  0.79 us
  transfers between devices with their start and end apart: 12, of which 7 were waited for; matrix products, arithmetic and copies ran while one was open for 0% of the time, Pallas kernels for 16%

profile of v27, /device:TPU:0, one launch (start us, length us, event | category | flops | bytes accessed | tf_op | source)
XLA Modules:
  0.0 30.0 jit_solution(9972269562302807464)
XLA Ops:
  0.6 1.1 %shard_map.85 = (f32[2,20,8,256]{3,2,1,0:T(8,128)S(1)}, f32[20,8,256]{2,1,0:T(8,128)S(1)}, f32[8,256]{1,0:T(8,128)S(1)}, s32[8,256]{1,0:T(8,128)S(1)}, s32[8,256...) custom-call(f32[2,20,8,256]{3,2,1,0:T(8,128)} %refs_0_.1, ...), custom_call_target="tpu_custom_call" | custom-call | tf_op jit(solution)/shard_map/pallas_call | solution.py:630
  1.8 0.5 %collective-permute-start.2 = (f32[62,8,128]{2,1,0:T(8,128)S(1)}, f32[62,8,128]{2,1,0:T(8,128)S(1)}, u32[]{:S(2)}, u32[]{:S(2)}) collective-permute-start(f32[62,8,128]{2,1,0:T(8,128)S(1)} %get-tuple-element.32), channel_id=1, source_target_pairs={{0,1},{4,8},{8,4},{12,13},{1,0},{5,9},{9,5},{13,12},{2,3},{6,10},{... | collective-permute-start | bytes 761864 | tf_op jit(solution)/shard_map/ppermute | solution.py:47
  2.3 4.1 %collective-permute-start.3 = (f32[62,8,128]{2,1,0:T(8,128)S(1)}, f32[62,8,128]{2,1,0:T(8,128)S(1)}, u32[]{:S(2)}, u32[]{:S(2)}) collective-permute-start(f32[62,8,128]{2,1,0:T(8,128)S(1)} %get-tuple-element.33), channel_id=1, source_target_pairs={{0,4},{4,0},{8,12},{12,8},{1,5},{5,1},{9,13},{13,9},{2,6},{6,2},{1... | collective-permute-start | bytes 761864 | tf_op jit(solution)/shard_map/ppermute | solution.py:47
  6.7 1.6 %collective-permute-start.1 = (f32[3,8,128]{2,1,0:T(8,128)S(1)}, f32[3,8,128]{2,1,0:T(8,128)S(1)}, u32[]{:S(2)}, u32[]{:S(2)}) collective-permute-start(f32[3,8,128]{2,1,0:T(8,128)S(1)} %get-tuple-element.29), channel_id=1, source_target_pairs={{0,3},{1,2},{2,1},{3,0},{4,7},{5,6},{6,5},{7,4},{8,11},{9,10},{10,... | collective-permute-start | bytes 36872 | tf_op jit(solution)/shard_map/ppermute | solution.py:47
  8.3 1.6 %collective-permute-done.1.from_b = f32[3,8,128]{2,1,0:T(8,128)S(1)} collective-permute-done((f32[3,8,128]{2,1,0:T(8,128)S(1)}, f32[3,8,128]{2,1,0:T(8,128)S(1)}, u32[]{:S(2)}, u32[]{:S(2)}) %collective-permute-start.1) | collective-permute-done | bytes 12320 | tf_op jit(solution)/shard_map/ppermute | solution.py:47
  9.9 0.7 %collective-permute-start.5 = (f32[6,8,128]{2,1,0:T(8,128)S(1)}, f32[6,8,128]{2,1,0:T(8,128)S(1)}, u32[]{:S(2)}, u32[]{:S(2)}) collective-permute-start(f32[6,8,128]{2,1,0:T(8,128)S(1)} %shard_map.87._.columns), channel_id=1, source_target_pairs={{0,1},{4,8},{8,4},{12,13},{1,0},{5,9},{9,5},{13,12},{2,3},{6,10},{... | collective-permute-start | bytes 73736 | tf_op jit(solution)/shard_map/ppermute | solution.py:47
  10.6 1.0 %collective-permute-start.4 = (f32[6,8,128]{2,1,0:T(8,128)S(1)}, f32[6,8,128]{2,1,0:T(8,128)S(1)}, u32[]{:S(2)}, u32[]{:S(2)}) collective-permute-start(f32[6,8,128]{2,1,0:T(8,128)S(1)} %shard_map.87._.columns), channel_id=1, source_target_pairs={{0,4},{4,0},{8,12},{12,8},{1,5},{5,1},{9,13},{13,9},{2,6},{6,2},{1... | collective-permute-start | bytes 73736 | tf_op jit(solution)/shard_map/ppermute | solution.py:47
  11.7 0.2 shard_map.88
  11.9 0.4 %collective-permute-done.3.strip_a = f32[62,8,128]{2,1,0:T(8,128)S(1)} collective-permute-done((f32[62,8,128]{2,1,0:T(8,128)S(1)}, f32[62,8,128]{2,1,0:T(8,128)S(1)}, u32[]{:S(2)}, u32[]{:S(2)}) %collective-permute-start.3) | collective-permute-done | bytes 253984 | tf_op jit(solution)/shard_map/ppermute | solution.py:47
  12.3 3.9 %shard_map.89 = (f32[2,20,16,256]{3,2,1,0:T(8,128)S(1)}, f32[2,20,16,256]{3,2,1,0:T(8,128)S(1)}, f32[2,20,16,256]{3,2,1,0:T(8,128)S(1)}, f32[2,20,8,256]{3,2,1,0...) custom-call(f32[2,20,8,256]{3,2,1,0:T(8,128)S(1)} %get-tuple-element.23.rhs, ...), custom_call_target="tpu_custom_call" | custom-call | flops 200000000 | bytes 8000000 | tf_op jit(solution)/shard_map/pallas_call | solution.py:647
  16.2 0.8 %shard_map.90 = (f32[4,2,5,8,128]{4,3,2,1,0:T(8,128)S(1)}, f32[2,8,128]{2,1,0:T(8,128)S(1)}) custom-call(f32[17,8,128]{2,1,0:T(8,128)S(1)} %get-tuple-element.30.own, f32[17,8,128]{2,1,0:T(8,128)S(1)} %get-tuple-element.34.halo, f32[6,8,128]{2,1,0:T(8,128)S(1)} %shard_map.87._.columns, f32[6,8,128]{2,1,0:T(8,128)S(1)} %collective-permute-done.4.columns_a, ...), custom_call_target="tpu_custom_call" | custom-call | tf_op jit(solution)/shard_map/pallas_call | solution.py:653
  17.0 0.9 %collective-permute-start.8 = (f32[2,8,128]{2,1,0:T(8,128)S(1)}, f32[2,8,128]{2,1,0:T(8,128)S(1)}, u32[]{:S(2)}, u32[]{:S(2)}) collective-permute-start(f32[2,8,128]{2,1,0:T(8,128)S(1)} %get-tuple-element.36.refs_0_), channel_id=1, source_target_pairs={{0,3},{1,2},{2,1},{3,0},{4,7},{5,6},{6,5},{7,4},{8,11},{9,10},{10,... | collective-permute-start | bytes 24584 | tf_op jit(solution)/shard_map/ppermute | solution.py:615
  17.9 0.7 %collective-permute-start.7 = (f32[2,8,128]{2,1,0:T(8,128)S(1)}, f32[2,8,128]{2,1,0:T(8,128)S(1)}, u32[]{:S(2)}, u32[]{:S(2)}) collective-permute-start(f32[2,8,128]{2,1,0:T(8,128)S(1)} %get-tuple-element.36.refs_0_), channel_id=1, source_target_pairs={{0,2},{1,3},{2,0},{3,1},{4,6},{5,7},{6,4},{7,5},{8,10},{9,11},{10,... | collective-permute-start | bytes 24584 | tf_op jit(solution)/shard_map/ppermute | solution.py:615
  18.6 0.3 collective-permute-start.6
  18.9 1.3 %collective-permute-done.8.refs_3_ = f32[2,8,128]{2,1,0:T(8,128)S(1)} collective-permute-done((f32[2,8,128]{2,1,0:T(8,128)S(1)}, f32[2,8,128]{2,1,0:T(8,128)S(1)}, u32[]{:S(2)}, u32[]{:S(2)}) %collective-permute-start.8) | collective-permute-done | bytes 8224 | tf_op jit(solution)/shard_map/ppermute | solution.py:615
  20.2 1.4 %collective-permute-done.7.refs_2_ = f32[2,8,128]{2,1,0:T(8,128)S(1)} collective-permute-done((f32[2,8,128]{2,1,0:T(8,128)S(1)}, f32[2,8,128]{2,1,0:T(8,128)S(1)}, u32[]{:S(2)}, u32[]{:S(2)}) %collective-permute-start.7) | collective-permute-done | bytes 8224 | tf_op jit(solution)/shard_map/ppermute | solution.py:615
  21.5 1.3 %collective-permute-start.11 = (f32[2,8,128]{2,1,0:T(8,128)S(1)}, f32[2,8,128]{2,1,0:T(8,128)S(1)}, u32[]{:S(2)}, u32[]{:S(2)}) collective-permute-start(f32[2,8,128]{2,1,0:T(8,128)S(1)} %shard_map.91._.rest_0_), channel_id=1, source_target_pairs={{0,8},{4,12},{8,0},{12,4},{1,9},{5,13},{9,1},{13,5},{2,10},{6,14},... | collective-permute-start | bytes 24584 | tf_op jit(solution)/shard_map/ppermute | solution.py:615
  22.9 2.1 %collective-permute-start.10 = (f32[2,8,128]{2,1,0:T(8,128)S(1)}, f32[2,8,128]{2,1,0:T(8,128)S(1)}, u32[]{:S(2)}, u32[]{:S(2)}) collective-permute-start(f32[2,8,128]{2,1,0:T(8,128)S(1)} %shard_map.91._.rest_0_), channel_id=1, source_target_pairs={{0,12},{4,8},{8,4},{12,0},{1,13},{5,9},{9,5},{13,1},{2,14},{6,10},... | collective-permute-start | bytes 24584 | tf_op jit(solution)/shard_map/ppermute | solution.py:615
  25.0 0.3 collective-permute-start.9
  25.3 0.4 %shard_map.92.vectors = f32[4,2,20,8,256]{4,3,2,1,0:T(8,128)S(1)} custom-call(f32[2,8,128]{2,1,0:T(8,128)S(1)} %shard_map.91._.rest_0_, f32[2,20,8,256]{3,2,1,0:T(8,128)S(1)} %get-tuple-element.23.rhs, s32[8,256]{1,0:T(8,128)S(1)} %get-tuple-element.26.ice, f32[2,20,16,256]{3,2,1,0:T(8,128)S(1)} %get-tuple-element.37.power_1, ...), custom_call_target="tpu_custom_call" | custom-call | tf_op jit(solution)/shard_map/pallas_call | solution.py:662
  25.7 0.5 %collective-permute-done.11.rest_3_ = f32[2,8,128]{2,1,0:T(8,128)S(1)} collective-permute-done((f32[2,8,128]{2,1,0:T(8,128)S(1)}, f32[2,8,128]{2,1,0:T(8,128)S(1)}, u32[]{:S(2)}, u32[]{:S(2)}) %collective-permute-start.11) | collective-permute-done | bytes 8224 | tf_op jit(solution)/shard_map/ppermute | solution.py:615
  26.2 2.2 %collective-permute-done.10.rest_2_ = f32[2,8,128]{2,1,0:T(8,128)S(1)} collective-permute-done((f32[2,8,128]{2,1,0:T(8,128)S(1)}, f32[2,8,128]{2,1,0:T(8,128)S(1)}, u32[]{:S(2)}, u32[]{:S(2)}) %collective-permute-start.10) | collective-permute-done | bytes 8224 | tf_op jit(solution)/shard_map/ppermute | solution.py:615
  28.3 0.3 %collective-permute-done.9.rest_1_ = f32[2,8,128]{2,1,0:T(8,128)S(1)} collective-permute-done((f32[2,8,128]{2,1,0:T(8,128)S(1)}, f32[2,8,128]{2,1,0:T(8,128)S(1)}, u32[]{:S(2)}, u32[]{:S(2)}) %collective-permute-start.9) | collective-permute-done | bytes 8224 | tf_op jit(solution)/shard_map/ppermute | solution.py:615
  28.6 1.3 %shard_map.93 = (f32[2,20,8,256]{3,2,1,0:T(8,128)}, f32[2,20,8,256]{3,2,1,0:T(8,128)}, f32[8,256]{1,0:T(8,128)}) custom-call(f32[2,20,8,256]{3,2,1,0:T(8,128)S(1)} %get-tuple-element.23.rhs, f32[4,2,20,8,256]{4,3,2,1,0:T(8,128)S(1)} %shard_map.92.vectors, f32[8,256]{1,0:T(8,128)S(1)} %get-tuple-element.25.friction, s32[8,256]{1,0:T(8,128)S(1)} %get-tuple-element.26.ice, ...), custom_call_target="tpu_custom_call" | custom-call | tf_op jit(solution)/shard_map/pallas_call | solution.py:668
  (9 shorter events, 0.3 us)
Async XLA Ops:
  1.8 10.1 %collective-permute-start.2 = (f32[62,8,128]{2,1,0:T(8,128)S(1)}, f32[62,8,128]{2,1,0:T(8,128)S(1)}, u32[]{:S(2)}, u32[]{:S(2)}) collective-permute-start(f32[62,8,128]{2,1,0:T(8,128)S(1)} %get-tuple-element.32), channel_id=1, source_target_pairs={{0,1},{4,8},{8,4},{12,13},{1,0},{5,9},{9,5},{13,12},{2,3},{6,10},{... | collective-permute-start | bytes 761864 | tf_op jit(solution)/shard_map/ppermute | solution.py:47
  2.3 10.0 %collective-permute-start.3 = (f32[62,8,128]{2,1,0:T(8,128)S(1)}, f32[62,8,128]{2,1,0:T(8,128)S(1)}, u32[]{:S(2)}, u32[]{:S(2)}) collective-permute-start(f32[62,8,128]{2,1,0:T(8,128)S(1)} %get-tuple-element.33), channel_id=1, source_target_pairs={{0,4},{4,0},{8,12},{12,8},{1,5},{5,1},{9,13},{13,9},{2,6},{6,2},{1... | collective-permute-start | bytes 761864 | tf_op jit(solution)/shard_map/ppermute | solution.py:47
  6.6 1.7 %collective-permute-start = (f32[3,8,128]{2,1,0:T(8,128)S(1)}, f32[3,8,128]{2,1,0:T(8,128)S(1)}, u32[]{:S(2)}, u32[]{:S(2)}) collective-permute-start(f32[3,8,128]{2,1,0:T(8,128)S(1)} %get-tuple-element.28), channel_id=1, source_target_pairs={{0,1},{1,0},{2,3},{3,2},{4,5},{5,4},{6,7},{7,6},{8,9},{9,8},{10,11... | collective-permute-start | bytes 36872 | tf_op jit(solution)/shard_map/ppermute | solution.py:47
  6.7 3.2 %collective-permute-start.1 = (f32[3,8,128]{2,1,0:T(8,128)S(1)}, f32[3,8,128]{2,1,0:T(8,128)S(1)}, u32[]{:S(2)}, u32[]{:S(2)}) collective-permute-start(f32[3,8,128]{2,1,0:T(8,128)S(1)} %get-tuple-element.29), channel_id=1, source_target_pairs={{0,3},{1,2},{2,1},{3,0},{4,7},{5,6},{6,5},{7,4},{8,11},{9,10},{10,... | collective-permute-start | bytes 36872 | tf_op jit(solution)/shard_map/ppermute | solution.py:47
  9.9 6.3 %collective-permute-start.5 = (f32[6,8,128]{2,1,0:T(8,128)S(1)}, f32[6,8,128]{2,1,0:T(8,128)S(1)}, u32[]{:S(2)}, u32[]{:S(2)}) collective-permute-start(f32[6,8,128]{2,1,0:T(8,128)S(1)} %shard_map.87._.columns), channel_id=1, source_target_pairs={{0,1},{4,8},{8,4},{12,13},{1,0},{5,9},{9,5},{13,12},{2,3},{6,10},{... | collective-permute-start | bytes 73736 | tf_op jit(solution)/shard_map/ppermute | solution.py:47
  10.6 5.6 %collective-permute-start.4 = (f32[6,8,128]{2,1,0:T(8,128)S(1)}, f32[6,8,128]{2,1,0:T(8,128)S(1)}, u32[]{:S(2)}, u32[]{:S(2)}) collective-permute-start(f32[6,8,128]{2,1,0:T(8,128)S(1)} %shard_map.87._.columns), channel_id=1, source_target_pairs={{0,4},{4,0},{8,12},{12,8},{1,5},{5,1},{9,13},{13,9},{2,6},{6,2},{1... | collective-permute-start | bytes 73736 | tf_op jit(solution)/shard_map/ppermute | solution.py:47
  17.0 3.1 %collective-permute-start.8 = (f32[2,8,128]{2,1,0:T(8,128)S(1)}, f32[2,8,128]{2,1,0:T(8,128)S(1)}, u32[]{:S(2)}, u32[]{:S(2)}) collective-permute-start(f32[2,8,128]{2,1,0:T(8,128)S(1)} %get-tuple-element.36.refs_0_), channel_id=1, source_target_pairs={{0,3},{1,2},{2,1},{3,0},{4,7},{5,6},{6,5},{7,4},{8,11},{9,10},{10,... | collective-permute-start | bytes 24584 | tf_op jit(solution)/shard_map/ppermute | solution.py:615
  17.9 3.7 %collective-permute-start.7 = (f32[2,8,128]{2,1,0:T(8,128)S(1)}, f32[2,8,128]{2,1,0:T(8,128)S(1)}, u32[]{:S(2)}, u32[]{:S(2)}) collective-permute-start(f32[2,8,128]{2,1,0:T(8,128)S(1)} %get-tuple-element.36.refs_0_), channel_id=1, source_target_pairs={{0,2},{1,3},{2,0},{3,1},{4,6},{5,7},{6,4},{7,5},{8,10},{9,11},{10,... | collective-permute-start | bytes 24584 | tf_op jit(solution)/shard_map/ppermute | solution.py:615
  18.6 2.9 %collective-permute-start.6 = (f32[2,8,128]{2,1,0:T(8,128)S(1)}, f32[2,8,128]{2,1,0:T(8,128)S(1)}, u32[]{:S(2)}, u32[]{:S(2)}) collective-permute-start(f32[2,8,128]{2,1,0:T(8,128)S(1)} %get-tuple-element.36.refs_0_), channel_id=1, source_target_pairs={{0,1},{1,0},{2,3},{3,2},{4,5},{5,4},{6,7},{7,6},{8,9},{9,8},{10,11... | collective-permute-start | bytes 24584 | tf_op jit(solution)/shard_map/ppermute | solution.py:615
  21.5 4.6 %collective-permute-start.11 = (f32[2,8,128]{2,1,0:T(8,128)S(1)}, f32[2,8,128]{2,1,0:T(8,128)S(1)}, u32[]{:S(2)}, u32[]{:S(2)}) collective-permute-start(f32[2,8,128]{2,1,0:T(8,128)S(1)} %shard_map.91._.rest_0_), channel_id=1, source_target_pairs={{0,8},{4,12},{8,0},{12,4},{1,9},{5,13},{9,1},{13,5},{2,10},{6,14},... | collective-permute-start | bytes 24584 | tf_op jit(solution)/shard_map/ppermute | solution.py:615
  22.9 5.5 %collective-permute-start.10 = (f32[2,8,128]{2,1,0:T(8,128)S(1)}, f32[2,8,128]{2,1,0:T(8,128)S(1)}, u32[]{:S(2)}, u32[]{:S(2)}) collective-permute-start(f32[2,8,128]{2,1,0:T(8,128)S(1)} %shard_map.91._.rest_0_), channel_id=1, source_target_pairs={{0,12},{4,8},{8,4},{12,0},{1,13},{5,9},{9,5},{13,1},{2,14},{6,10},... | collective-permute-start | bytes 24584 | tf_op jit(solution)/shard_map/ppermute | solution.py:615
  25.0 3.7 %collective-permute-start.9 = (f32[2,8,128]{2,1,0:T(8,128)S(1)}, f32[2,8,128]{2,1,0:T(8,128)S(1)}, u32[]{:S(2)}, u32[]{:S(2)}) collective-permute-start(f32[2,8,128]{2,1,0:T(8,128)S(1)} %shard_map.91._.rest_0_), channel_id=1, source_target_pairs={{0,4},{4,0},{8,12},{12,8},{1,5},{5,1},{9,13},{13,9},{2,6},{6,2},{1... | collective-permute-start | bytes 24584 | tf_op jit(solution)/shard_map/ppermute | solution.py:615

commit v28 on v22

--- a/solution.py
+++ b/solution.py
@@ -466,8 +466,8 @@
         pair = two_sum(total[:, :LANES], total[:, LANES:])
         if more is not None:
             pair = join(pair, (more, jnp.zeros_like(more)))
-        for step in (4, 2, 1):
-            pair = join(pair, tuple(pltpu.roll(v, step, 0) for v in pair))
+        pair = added([pair] + [tuple(pltpu.roll(v, step, 0) for v in pair) for step in (2, 4, 6)])
+        pair = join(pair, tuple(pltpu.roll(v, 1, 0) for v in pair))
         high = jnp.where(tall == j, jnp.concatenate([pair[0]] * 2, 0), high)
         low = jnp.where(tall == j, jnp.concatenate([pair[1]] * 2, 0), low)
     total = join((high, low), (pltpu.roll(high, 64, 1), pltpu.roll(low, 64, 1)))

time: 30.1 us -> 30.2 us (level)
  no operation moved by 1% of the time
where the time goes in v28:
time: 30.2 us; the launch traced here: 30 us
  starting transfers between devices  13.8 us (46%)
  Pallas kernels  8.05 us (27%)
  waiting for transfers between devices  7.51 us (25%)
  between operations  0.71 us (2%)
    ppermute x6, starting transfers between devices, swapped(): return lax.ppermute(x, (*axes, spare) if spare else axes, pairs)  8.1 us
    ppermute x6, starting transfers between devices, exchange(): parts.append(lax.ppermute(x, axis, pairs))  5.65 us
    ppermute x6, waiting for transfers between devices, exchange(): parts.append(lax.ppermute(x, axis, pairs))  5.56 us
    pallas_call x1, Pallas kernels, body(): call(main_kernel, [(2,) + block] * (STEPS - 1) + [adjoint_rhs.shape, (2 *...  3.91 us
    ppermute x6, waiting for transfers between devices, swapped(): return lax.ppermute(x, (*axes, spare) if spare else axes, pairs)  1.95 us
    pallas_call x1, Pallas kernels, body(): call(final_kernel, [adjoint_rhs.shape, adjoint_rhs.shape, friction.shape])  1.34 us
    pallas_call x1, Pallas kernels, body(): call(strip_kernel, [jax.ShapeDtypeStruct(x.shape, x.dtype) for x in input...  1.13 us
    pallas_call x1, Pallas kernels, body(): call(ribbon_kernel, [(STEPS, 2, layers // 4) + tile, (2,) + tile])  0.8 us
  transfers between devices with their start and end apart: 12, of which 7 were waited for; matrix products, arithmetic and copies ran while one was open for 0% of the time, Pallas kernels for 16%

profile of v28, /device:TPU:0, one launch (start us, length us, event | category | flops | bytes accessed | tf_op | source)
XLA Modules:
  0.0 30.0 jit_solution(2838083277717640492)
XLA Ops:
  0.6 1.1 %shard_map.85 = (f32[2,20,8,256]{3,2,1,0:T(8,128)S(1)}, f32[20,8,256]{2,1,0:T(8,128)S(1)}, f32[8,256]{1,0:T(8,128)S(1)}, s32[8,256]{1,0:T(8,128)S(1)}, s32[8,256...) custom-call(f32[2,20,8,256]{3,2,1,0:T(8,128)} %refs_0_.1, ...), custom_call_target="tpu_custom_call" | custom-call | tf_op jit(solution)/shard_map/pallas_call | solution.py:628
  1.8 0.5 %collective-permute-start.2 = (f32[62,8,128]{2,1,0:T(8,128)S(1)}, f32[62,8,128]{2,1,0:T(8,128)S(1)}, u32[]{:S(2)}, u32[]{:S(2)}) collective-permute-start(f32[62,8,128]{2,1,0:T(8,128)S(1)} %get-tuple-element.32), channel_id=1, source_target_pairs={{0,1},{4,8},{8,4},{12,13},{1,0},{5,9},{9,5},{13,12},{2,3},{6,10},{... | collective-permute-start | bytes 761864 | tf_op jit(solution)/shard_map/ppermute | solution.py:47
  2.3 4.1 %collective-permute-start.3 = (f32[62,8,128]{2,1,0:T(8,128)S(1)}, f32[62,8,128]{2,1,0:T(8,128)S(1)}, u32[]{:S(2)}, u32[]{:S(2)}) collective-permute-start(f32[62,8,128]{2,1,0:T(8,128)S(1)} %get-tuple-element.33), channel_id=1, source_target_pairs={{0,4},{4,0},{8,12},{12,8},{1,5},{5,1},{9,13},{13,9},{2,6},{6,2},{1... | collective-permute-start | bytes 761864 | tf_op jit(solution)/shard_map/ppermute | solution.py:47
  6.7 1.6 %collective-permute-start.1 = (f32[3,8,128]{2,1,0:T(8,128)S(1)}, f32[3,8,128]{2,1,0:T(8,128)S(1)}, u32[]{:S(2)}, u32[]{:S(2)}) collective-permute-start(f32[3,8,128]{2,1,0:T(8,128)S(1)} %get-tuple-element.29), channel_id=1, source_target_pairs={{0,3},{1,2},{2,1},{3,0},{4,7},{5,6},{6,5},{7,4},{8,11},{9,10},{10,... | collective-permute-start | bytes 36872 | tf_op jit(solution)/shard_map/ppermute | solution.py:47
  8.3 1.6 %collective-permute-done.1.from_b = f32[3,8,128]{2,1,0:T(8,128)S(1)} collective-permute-done((f32[3,8,128]{2,1,0:T(8,128)S(1)}, f32[3,8,128]{2,1,0:T(8,128)S(1)}, u32[]{:S(2)}, u32[]{:S(2)}) %collective-permute-start.1) | collective-permute-done | bytes 12320 | tf_op jit(solution)/shard_map/ppermute | solution.py:47
  9.9 0.7 %collective-permute-start.5 = (f32[6,8,128]{2,1,0:T(8,128)S(1)}, f32[6,8,128]{2,1,0:T(8,128)S(1)}, u32[]{:S(2)}, u32[]{:S(2)}) collective-permute-start(f32[6,8,128]{2,1,0:T(8,128)S(1)} %shard_map.87._.columns), channel_id=1, source_target_pairs={{0,1},{4,8},{8,4},{12,13},{1,0},{5,9},{9,5},{13,12},{2,3},{6,10},{... | collective-permute-start | bytes 73736 | tf_op jit(solution)/shard_map/ppermute | solution.py:47
  10.6 1.0 %collective-permute-start.4 = (f32[6,8,128]{2,1,0:T(8,128)S(1)}, f32[6,8,128]{2,1,0:T(8,128)S(1)}, u32[]{:S(2)}, u32[]{:S(2)}) collective-permute-start(f32[6,8,128]{2,1,0:T(8,128)S(1)} %shard_map.87._.columns), channel_id=1, source_target_pairs={{0,4},{4,0},{8,12},{12,8},{1,5},{5,1},{9,13},{13,9},{2,6},{6,2},{1... | collective-permute-start | bytes 73736 | tf_op jit(solution)/shard_map/ppermute | solution.py:47
  11.7 0.2 shard_map.88
  11.9 0.4 %collective-permute-done.3.strip_a = f32[62,8,128]{2,1,0:T(8,128)S(1)} collective-permute-done((f32[62,8,128]{2,1,0:T(8,128)S(1)}, f32[62,8,128]{2,1,0:T(8,128)S(1)}, u32[]{:S(2)}, u32[]{:S(2)}) %collective-permute-start.3) | collective-permute-done | bytes 253984 | tf_op jit(solution)/shard_map/ppermute | solution.py:47
  12.3 3.9 %shard_map.89 = (f32[2,20,16,256]{3,2,1,0:T(8,128)S(1)}, f32[2,20,16,256]{3,2,1,0:T(8,128)S(1)}, f32[2,20,16,256]{3,2,1,0:T(8,128)S(1)}, f32[2,20,8,256]{3,2,1,0...) custom-call(f32[2,20,8,256]{3,2,1,0:T(8,128)S(1)} %get-tuple-element.23.rhs, ...), custom_call_target="tpu_custom_call" | custom-call | flops 200000000 | bytes 8000000 | tf_op jit(solution)/shard_map/pallas_call | solution.py:645
  16.2 0.8 %shard_map.90 = (f32[4,2,5,8,128]{4,3,2,1,0:T(8,128)S(1)}, f32[2,8,128]{2,1,0:T(8,128)S(1)}) custom-call(f32[17,8,128]{2,1,0:T(8,128)S(1)} %get-tuple-element.30.own, f32[17,8,128]{2,1,0:T(8,128)S(1)} %get-tuple-element.34.halo, f32[6,8,128]{2,1,0:T(8,128)S(1)} %shard_map.87._.columns, f32[6,8,128]{2,1,0:T(8,128)S(1)} %collective-permute-done.4.columns_a, ...), custom_call_target="tpu_custom_call" | custom-call | tf_op jit(solution)/shard_map/pallas_call | solution.py:651
  17.0 0.9 %collective-permute-start.8 = (f32[2,8,128]{2,1,0:T(8,128)S(1)}, f32[2,8,128]{2,1,0:T(8,128)S(1)}, u32[]{:S(2)}, u32[]{:S(2)}) collective-permute-start(f32[2,8,128]{2,1,0:T(8,128)S(1)} %get-tuple-element.36.refs_0_), channel_id=1, source_target_pairs={{0,3},{1,2},{2,1},{3,0},{4,7},{5,6},{6,5},{7,4},{8,11},{9,10},{10,... | collective-permute-start | bytes 24584 | tf_op jit(solution)/shard_map/ppermute | solution.py:613
  17.9 0.7 %collective-permute-start.7 = (f32[2,8,128]{2,1,0:T(8,128)S(1)}, f32[2,8,128]{2,1,0:T(8,128)S(1)}, u32[]{:S(2)}, u32[]{:S(2)}) collective-permute-start(f32[2,8,128]{2,1,0:T(8,128)S(1)} %get-tuple-element.36.refs_0_), channel_id=1, source_target_pairs={{0,2},{1,3},{2,0},{3,1},{4,6},{5,7},{6,4},{7,5},{8,10},{9,11},{10,... | collective-permute-start | bytes 24584 | tf_op jit(solution)/shard_map/ppermute | solution.py:613
  18.7 0.3 collective-permute-start.6
  18.9 1.3 %collective-permute-done.8.refs_3_ = f32[2,8,128]{2,1,0:T(8,128)S(1)} collective-permute-done((f32[2,8,128]{2,1,0:T(8,128)S(1)}, f32[2,8,128]{2,1,0:T(8,128)S(1)}, u32[]{:S(2)}, u32[]{:S(2)}) %collective-permute-start.8) | collective-permute-done | bytes 8224 | tf_op jit(solution)/shard_map/ppermute | solution.py:613
  20.2 1.4 %collective-permute-done.7.refs_2_ = f32[2,8,128]{2,1,0:T(8,128)S(1)} collective-permute-done((f32[2,8,128]{2,1,0:T(8,128)S(1)}, f32[2,8,128]{2,1,0:T(8,128)S(1)}, u32[]{:S(2)}, u32[]{:S(2)}) %collective-permute-start.7) | collective-permute-done | bytes 8224 | tf_op jit(solution)/shard_map/ppermute | solution.py:613
  21.6 1.3 %collective-permute-start.11 = (f32[2,8,128]{2,1,0:T(8,128)S(1)}, f32[2,8,128]{2,1,0:T(8,128)S(1)}, u32[]{:S(2)}, u32[]{:S(2)}) collective-permute-start(f32[2,8,128]{2,1,0:T(8,128)S(1)} %shard_map.91._.rest_0_), channel_id=1, source_target_pairs={{0,8},{4,12},{8,0},{12,4},{1,9},{5,13},{9,1},{13,5},{2,10},{6,14},... | collective-permute-start | bytes 24584 | tf_op jit(solution)/shard_map/ppermute | solution.py:613
  22.9 2.1 %collective-permute-start.10 = (f32[2,8,128]{2,1,0:T(8,128)S(1)}, f32[2,8,128]{2,1,0:T(8,128)S(1)}, u32[]{:S(2)}, u32[]{:S(2)}) collective-permute-start(f32[2,8,128]{2,1,0:T(8,128)S(1)} %shard_map.91._.rest_0_), channel_id=1, source_target_pairs={{0,12},{4,8},{8,4},{12,0},{1,13},{5,9},{9,5},{13,1},{2,14},{6,10},... | collective-permute-start | bytes 24584 | tf_op jit(solution)/shard_map/ppermute | solution.py:613
  25.0 0.3 collective-permute-start.9
  25.3 0.4 %shard_map.92.vectors = f32[4,2,20,8,256]{4,3,2,1,0:T(8,128)S(1)} custom-call(f32[2,8,128]{2,1,0:T(8,128)S(1)} %shard_map.91._.rest_0_, f32[2,20,8,256]{3,2,1,0:T(8,128)S(1)} %get-tuple-element.23.rhs, s32[8,256]{1,0:T(8,128)S(1)} %get-tuple-element.26.ice, f32[2,20,16,256]{3,2,1,0:T(8,128)S(1)} %get-tuple-element.37.power_1, ...), custom_call_target="tpu_custom_call" | custom-call | tf_op jit(solution)/shard_map/pallas_call | solution.py:660
  25.7 0.5 %collective-permute-done.11.rest_3_ = f32[2,8,128]{2,1,0:T(8,128)S(1)} collective-permute-done((f32[2,8,128]{2,1,0:T(8,128)S(1)}, f32[2,8,128]{2,1,0:T(8,128)S(1)}, u32[]{:S(2)}, u32[]{:S(2)}) %collective-permute-start.11) | collective-permute-done | bytes 8224 | tf_op jit(solution)/shard_map/ppermute | solution.py:613
  26.2 2.2 %collective-permute-done.10.rest_2_ = f32[2,8,128]{2,1,0:T(8,128)S(1)} collective-permute-done((f32[2,8,128]{2,1,0:T(8,128)S(1)}, f32[2,8,128]{2,1,0:T(8,128)S(1)}, u32[]{:S(2)}, u32[]{:S(2)}) %collective-permute-start.10) | collective-permute-done | bytes 8224 | tf_op jit(solution)/shard_map/ppermute | solution.py:613
  28.4 0.3 %collective-permute-done.9.rest_1_ = f32[2,8,128]{2,1,0:T(8,128)S(1)} collective-permute-done((f32[2,8,128]{2,1,0:T(8,128)S(1)}, f32[2,8,128]{2,1,0:T(8,128)S(1)}, u32[]{:S(2)}, u32[]{:S(2)}) %collective-permute-start.9) | collective-permute-done | bytes 8224 | tf_op jit(solution)/shard_map/ppermute | solution.py:613
  28.7 1.3 %shard_map.93 = (f32[2,20,8,256]{3,2,1,0:T(8,128)}, f32[2,20,8,256]{3,2,1,0:T(8,128)}, f32[8,256]{1,0:T(8,128)}) custom-call(f32[2,20,8,256]{3,2,1,0:T(8,128)S(1)} %get-tuple-element.23.rhs, f32[4,2,20,8,256]{4,3,2,1,0:T(8,128)S(1)} %shard_map.92.vectors, f32[8,256]{1,0:T(8,128)S(1)} %get-tuple-element.25.friction, s32[8,256]{1,0:T(8,128)S(1)} %get-tuple-element.26.ice, ...), custom_call_target="tpu_custom_call" | custom-call | tf_op jit(solution)/shard_map/pallas_call | solution.py:666
  (9 shorter events, 0.3 us)
Async XLA Ops:
  1.8 10.1 %collective-permute-start.2 = (f32[62,8,128]{2,1,0:T(8,128)S(1)}, f32[62,8,128]{2,1,0:T(8,128)S(1)}, u32[]{:S(2)}, u32[]{:S(2)}) collective-permute-start(f32[62,8,128]{2,1,0:T(8,128)S(1)} %get-tuple-element.32), channel_id=1, source_target_pairs={{0,1},{4,8},{8,4},{12,13},{1,0},{5,9},{9,5},{13,12},{2,3},{6,10},{... | collective-permute-start | bytes 761864 | tf_op jit(solution)/shard_map/ppermute | solution.py:47
  2.3 10.0 %collective-permute-start.3 = (f32[62,8,128]{2,1,0:T(8,128)S(1)}, f32[62,8,128]{2,1,0:T(8,128)S(1)}, u32[]{:S(2)}, u32[]{:S(2)}) collective-permute-start(f32[62,8,128]{2,1,0:T(8,128)S(1)} %get-tuple-element.33), channel_id=1, source_target_pairs={{0,4},{4,0},{8,12},{12,8},{1,5},{5,1},{9,13},{13,9},{2,6},{6,2},{1... | collective-permute-start | bytes 761864 | tf_op jit(solution)/shard_map/ppermute | solution.py:47
  6.6 1.7 %collective-permute-start = (f32[3,8,128]{2,1,0:T(8,128)S(1)}, f32[3,8,128]{2,1,0:T(8,128)S(1)}, u32[]{:S(2)}, u32[]{:S(2)}) collective-permute-start(f32[3,8,128]{2,1,0:T(8,128)S(1)} %get-tuple-element.28), channel_id=1, source_target_pairs={{0,1},{1,0},{2,3},{3,2},{4,5},{5,4},{6,7},{7,6},{8,9},{9,8},{10,11... | collective-permute-start | bytes 36872 | tf_op jit(solution)/shard_map/ppermute | solution.py:47
  6.7 3.2 %collective-permute-start.1 = (f32[3,8,128]{2,1,0:T(8,128)S(1)}, f32[3,8,128]{2,1,0:T(8,128)S(1)}, u32[]{:S(2)}, u32[]{:S(2)}) collective-permute-start(f32[3,8,128]{2,1,0:T(8,128)S(1)} %get-tuple-element.29), channel_id=1, source_target_pairs={{0,3},{1,2},{2,1},{3,0},{4,7},{5,6},{6,5},{7,4},{8,11},{9,10},{10,... | collective-permute-start | bytes 36872 | tf_op jit(solution)/shard_map/ppermute | solution.py:47
  9.9 6.3 %collective-permute-start.5 = (f32[6,8,128]{2,1,0:T(8,128)S(1)}, f32[6,8,128]{2,1,0:T(8,128)S(1)}, u32[]{:S(2)}, u32[]{:S(2)}) collective-permute-start(f32[6,8,128]{2,1,0:T(8,128)S(1)} %shard_map.87._.columns), channel_id=1, source_target_pairs={{0,1},{4,8},{8,4},{12,13},{1,0},{5,9},{9,5},{13,12},{2,3},{6,10},{... | collective-permute-start | bytes 73736 | tf_op jit(solution)/shard_map/ppermute | solution.py:47
  10.6 5.6 %collective-permute-start.4 = (f32[6,8,128]{2,1,0:T(8,128)S(1)}, f32[6,8,128]{2,1,0:T(8,128)S(1)}, u32[]{:S(2)}, u32[]{:S(2)}) collective-permute-start(f32[6,8,128]{2,1,0:T(8,128)S(1)} %shard_map.87._.columns), channel_id=1, source_target_pairs={{0,4},{4,0},{8,12},{12,8},{1,5},{5,1},{9,13},{13,9},{2,6},{6,2},{1... | collective-permute-start | bytes 73736 | tf_op jit(solution)/shard_map/ppermute | solution.py:47
  17.0 3.2 %collective-permute-start.8 = (f32[2,8,128]{2,1,0:T(8,128)S(1)}, f32[2,8,128]{2,1,0:T(8,128)S(1)}, u32[]{:S(2)}, u32[]{:S(2)}) collective-permute-start(f32[2,8,128]{2,1,0:T(8,128)S(1)} %get-tuple-element.36.refs_0_), channel_id=1, source_target_pairs={{0,3},{1,2},{2,1},{3,0},{4,7},{5,6},{6,5},{7,4},{8,11},{9,10},{10,... | collective-permute-start | bytes 24584 | tf_op jit(solution)/shard_map/ppermute | solution.py:613
  17.9 3.7 %collective-permute-start.7 = (f32[2,8,128]{2,1,0:T(8,128)S(1)}, f32[2,8,128]{2,1,0:T(8,128)S(1)}, u32[]{:S(2)}, u32[]{:S(2)}) collective-permute-start(f32[2,8,128]{2,1,0:T(8,128)S(1)} %get-tuple-element.36.refs_0_), channel_id=1, source_target_pairs={{0,2},{1,3},{2,0},{3,1},{4,6},{5,7},{6,4},{7,5},{8,10},{9,11},{10,... | collective-permute-start | bytes 24584 | tf_op jit(solution)/shard_map/ppermute | solution.py:613
  18.7 2.9 %collective-permute-start.6 = (f32[2,8,128]{2,1,0:T(8,128)S(1)}, f32[2,8,128]{2,1,0:T(8,128)S(1)}, u32[]{:S(2)}, u32[]{:S(2)}) collective-permute-start(f32[2,8,128]{2,1,0:T(8,128)S(1)} %get-tuple-element.36.refs_0_), channel_id=1, source_target_pairs={{0,1},{1,0},{2,3},{3,2},{4,5},{5,4},{6,7},{7,6},{8,9},{9,8},{10,11... | collective-permute-start | bytes 24584 | tf_op jit(solution)/shard_map/ppermute | solution.py:613
  21.6 4.6 %collective-permute-start.11 = (f32[2,8,128]{2,1,0:T(8,128)S(1)}, f32[2,8,128]{2,1,0:T(8,128)S(1)}, u32[]{:S(2)}, u32[]{:S(2)}) collective-permute-start(f32[2,8,128]{2,1,0:T(8,128)S(1)} %shard_map.91._.rest_0_), channel_id=1, source_target_pairs={{0,8},{4,12},{8,0},{12,4},{1,9},{5,13},{9,1},{13,5},{2,10},{6,14},... | collective-permute-start | bytes 24584 | tf_op jit(solution)/shard_map/ppermute | solution.py:613
  22.9 5.5 %collective-permute-start.10 = (f32[2,8,128]{2,1,0:T(8,128)S(1)}, f32[2,8,128]{2,1,0:T(8,128)S(1)}, u32[]{:S(2)}, u32[]{:S(2)}) collective-permute-start(f32[2,8,128]{2,1,0:T(8,128)S(1)} %shard_map.91._.rest_0_), channel_id=1, source_target_pairs={{0,12},{4,8},{8,4},{12,0},{1,13},{5,9},{9,5},{13,1},{2,14},{6,10},... | collective-permute-start | bytes 24584 | tf_op jit(solution)/shard_map/ppermute | solution.py:613
  25.0 3.7 %collective-permute-start.9 = (f32[2,8,128]{2,1,0:T(8,128)S(1)}, f32[2,8,128]{2,1,0:T(8,128)S(1)}, u32[]{:S(2)}, u32[]{:S(2)}) collective-permute-start(f32[2,8,128]{2,1,0:T(8,128)S(1)} %shard_map.91._.rest_0_), channel_id=1, source_target_pairs={{0,4},{4,0},{8,12},{12,8},{1,5},{5,1},{9,13},{13,9},{2,6},{6,2},{1... | collective-permute-start | bytes 24584 | tf_op jit(solution)/shard_map/ppermute | solution.py:613
